TPU v7x, 32 devices: a whole 2x2x4 slice. The times are simulated.
32 devices in a mesh: blk: 16 (over z, x, core), fsdp: 2 (over y).
Axes of the slice: x: 2, y: 2, z: 4, core: 2. Of those that a mesh axis runs over, the one named last changes fastest.
Arguments:
- params: float32 [16, 4096, 1024], P('blk', 'fsdp'), may hold values from -6 to 6
- inputs: bfloat16 [16, 1792, 4096], P('blk', 'fsdp'), may hold values from -6 to 6
- cotangent: bfloat16 [16, 1792, 1024], P('blk', 'fsdp'), may hold values from -6 to 6
- mix: int32 [16, 3], replicated, may hold values from 8 to 48, as said below
Outputs:
- new_params: float32 [16, 4096, 1024], P('blk', 'fsdp')
Inputs may be any that keep to these rules, and one draw needn't show every extreme that they name: `mix`: each row holds three positive numerators that sum to 64.
All inputs are finite; a program needn't handle non-finite values.
Results may differ from a plain program's by a relative error of at most 0.0003.
Values may be sent and summed in bfloat16 or wider, within the bound.
No kernel may reach another device: no remote copies, remote signals or barrier semaphores. Data moves between devices by JAX's collectives and lax.ppermute only.
A program may use at most 128 MiB of HBM per device.

v0:
```python
import jax
import jax.numpy as jnp
from jax import lax
from jax.sharding import PartitionSpec as P

MIX_DENOM = 64


RATE = 0.03


def from_behind(value, axis, steps):
    count = lax.axis_size(axis)
    pairs = [(source, (source + steps) % count) for source in range(count)]
    return lax.ppermute(value, axis, pairs)


def on_device(params, inputs, cotangent, mix):
    weights = params[0]
    features = inputs[0]
    cot_local = cotangent[0]
    replica = lax.axis_index("blk")
    pick = (jnp.arange(lax.axis_size("blk")) == replica).astype(jnp.float32)
    coeff = jnp.dot(pick, mix.astype(jnp.float32), precision=lax.Precision.HIGHEST) / MIX_DENOM
    c_left = coeff[0]
    c_self = coeff[1]
    c_right = coeff[2]
    left_weights = from_behind(weights, "blk", 1)
    right_weights = from_behind(weights, "blk", -1)
    gradient = lax.psum_scatter(
        lax.dot_general(
            features, cot_local, (((0,), (0,)), ((), ())), preferred_element_type=jnp.float32
        ),
        "fsdp",
        scatter_dimension=0,
        tiled=True,
    )
    left_grads = from_behind(gradient, "blk", 1)
    right_grads = from_behind(gradient, "blk", -1)
    mixed_params = c_left * left_weights + c_self * weights + c_right * right_weights
    mixed_grads = c_left * left_grads + c_self * gradient + c_right * right_grads
    updated = mixed_params - RATE * mixed_grads
    return updated[None]


def solution(mesh):
    return jax.shard_map(
        on_device,
        mesh=mesh,
        in_specs=(P("blk", "fsdp", None), P("blk", "fsdp", None), P("blk", "fsdp", None), P()),
        out_specs=P("blk", "fsdp", None),
        check_vma=False,
    )
```

profile of v0, /device:TPU:1, one launch (start us, length us, event | category | flops | bytes accessed | tf_op | source)
XLA Modules:
  0.0 428.3 jit_solution(14746283124913501972)
XLA Ops:
  6.5 0.0 copy-start
  6.5 0.0 reduce-scatter.2.cloned.1.call-start
  6.5 1.5 copy-done
  8.0 14.4 %fusion = f32[4096,1024]{1,0:T(8,128)} fusion(bf16[1,896,4096]{2,1,0:T(8,128)(2,1)} %param.5, bf16[1,896,1024]{2,1,0:T(8,128)(2,1)S(1)} %copy-done), kind=kOutput, calls=%fused_computation.1 | convolution fusion | flops 7516192768 | bytes 25952256 | tf_op jit(solution)/shard_map/dot_general | solution.py:31
  22.5 0.0 copy-start.2
  22.5 0.0 reduce-scatter.2.cloned.1.call-update
  22.5 0.1 collective-permute-start.1
  22.6 2.6 collective-permute-start
  25.2 188.6 %reduce-scatter.2.cloned.1.call-done = f32[2048,1024]{1,0:T(8,128)} async-done(((f32[4096,1024]{1,0:T(8,128)}), f32[2048,1024]{1,0:T(8,128)}) %reduce-scatter.2.cloned.1.call-update) | async-done | bytes 8388624 | tf_op jit(solution)/shard_map/reduce_scatter | solution.py:30
  213.9 0.7 collective-permute-start.3
  214.5 1.1 collective-permute-start.2
  215.6 0.0 copy-done.2
  215.6 0.1 fusion.3
  215.7 0.6 fusion.9
  216.4 0.0 collective-permute-done.1
  216.4 0.0 collective-permute-done
  216.4 180.6 %collective-permute-done.3 = f32[2048,1024]{1,0:T(8,128)} collective-permute-done((f32[2048,1024]{1,0:T(8,128)}, f32[2048,1024]{1,0:T(8,128)}, u32[]{:S(2)}, u32[]{:S(2)}) %collective-permute-start.3) | collective-permute-done | bytes 8388640 | tf_op jit(solution)/shard_map/ppermute | solution.py:15
  396.9 0.0 collective-permute-done.2
  396.9 0.0 copy-start.1
  396.9 24.6 %subtract_bitcast_fusion = f32[1,2048,1024]{2,1,0:T(8,128)} fusion(f32[2048,1024]{1,0:T(8,128)} %collective-permute-done.3, f32[2048,1024]{1,0:T(8,128)} %reduce-scatter.2.cloned.1.call-done, f32[2048,1024]{1,0:T(8,128)} %collective-permute-done.2, f32[2048,1024]{1,0:T(8,128)} %collective-permute-done.1, f32[2048,1024]{1,0:T(8,128)} %collective-permute-done, ...), kind=kLoop, calls=%fused_computation | loop fusion | flops 25165824 | bytes 58720268 | tf_op jit(solution)/shard_map/broadcast_in_dim | solution.py:43
  421.5 0.0 copy-done.1
Async XLA Ops:
  6.5 1.5 copy-start
  6.5 207.3 %reduce-scatter.2.cloned.1.call-start = ((), (), s32[]{:S(2)}) async-start(), calls=%async_computation.1 | async-start | bytes 25165824 | tf_op jit(solution)/shard_map/reduce_scatter | solution.py:30
  22.5 193.1 %copy-start.2 = (s32[16,3]{0,1:T(4,128)S(1)}, s32[16,3]{0,1:T(4,128)}, u32[]{:S(2)}) copy-start(s32[16,3]{0,1:T(4,128)} %param.7) | copy-start | bytes 580
  22.5 193.9 %collective-permute-start.1 = (f32[2048,1024]{1,0:T(8,128)}, f32[2048,1024]{1,0:T(8,128)}, u32[]{:S(2)}, u32[]{:S(2)}) collective-permute-start(f32[2048,1024]{1,0:T(8,128)} %bitcast.20), channel_id=1, source_target_pairs={{0,30},{2,0},{4,2},{6,4},{8,6},{10,8},{12,10},{14,12},{16,14},{18,... | collective-permute-start | bytes 25165832 | tf_op jit(solution)/shard_map/ppermute | solution.py:15
  22.6 193.8 %collective-permute-start = (f32[2048,1024]{1,0:T(8,128)}, f32[2048,1024]{1,0:T(8,128)}, u32[]{:S(2)}, u32[]{:S(2)}) collective-permute-start(f32[2048,1024]{1,0:T(8,128)} %bitcast.21), channel_id=1, source_target_pairs={{0,2},{2,4},{4,6},{6,8},{8,10},{10,12},{12,14},{14,16},{16,18},{18... | collective-permute-start | bytes 25165832 | tf_op jit(solution)/shard_map/ppermute | solution.py:15
  213.9 183.1 %collective-permute-start.3 = (f32[2048,1024]{1,0:T(8,128)}, f32[2048,1024]{1,0:T(8,128)}, u32[]{:S(2)}, u32[]{:S(2)}) collective-permute-start(f32[2048,1024]{1,0:T(8,128)} %reduce-scatter.2.cloned.1.call-done), channel_id=1, source_target_pairs={{0,30},{2,0},{4,2},{6,4},{8,6},{10,8},{12,10},{14,12},{16,14},{18,... | collective-permute-start | bytes 25165832 | tf_op jit(solution)/shard_map/ppermute | solution.py:15
  214.5 182.4 %collective-permute-start.2 = (f32[2048,1024]{1,0:T(8,128)}, f32[2048,1024]{1,0:T(8,128)}, u32[]{:S(2)}, u32[]{:S(2)}) collective-permute-start(f32[2048,1024]{1,0:T(8,128)} %reduce-scatter.2.cloned.1.call-done), channel_id=1, source_target_pairs={{0,2},{2,4},{4,6},{6,8},{8,10},{10,12},{12,14},{14,16},{16,18},{18... | collective-permute-start | bytes 25165832 | tf_op jit(solution)/shard_map/ppermute | solution.py:15
  396.9 24.6 %copy-start.1 = (bf16[1,896,1024]{2,1,0:T(8,128)(2,1)S(1)}, bf16[1,896,1024]{2,1,0:T(8,128)(2,1)}, u32[]{:S(2)}) copy-start(bf16[1,896,1024]{2,1,0:T(8,128)(2,1)} %param.6) | copy-start | bytes 5505028
Sparse Core Ops, SparseCore 0:
  22.6 191.2 reduce-scatter.1
where the time goes:
time: 429 us; the launch traced here: 428 us
  waiting for transfers between devices  369 us (86%)
  other arithmetic  24.6 us (6%)
  matrix products  14.5 us (3%)
  between operations  13.4 us (3%)
  starting transfers between devices  4.47 us (1%)
    reduce_scatter x1, waiting for transfers between devices, on_device(): lax.psum_scatter(lax.dot_general(features, cot_local, (((0,), (0,)), ((),...  189 us
    ppermute x4, waiting for transfers between devices, from_behind(): return lax.ppermute(value, axis, pairs)  181 us
    broadcast_in_dim x1, other arithmetic, on_device(): return updated[None]  24.6 us
    dot_general x1, matrix products, on_device(): lax.dot_general(features, cot_local, (((0,), (0,)), ((), ())), preferred_...  14.4 us
  transfers between devices with their start and end apart: 5, of which 2 were waited for; matrix products, arithmetic and copies ran while one was open for 0% of the time, Pallas kernels for 0%

commit v1 on v0

v1 whole, which is shorter than its diff:
```python
import math

import jax
import jax.numpy as jnp
from jax import lax
from jax.sharding import PartitionSpec as P

MIX_DENOM = 64
RATE = 0.03
LARGEST = 6.0
WIRE = jnp.float16
CHUNKS = 8
AHEAD = 2
LAG = 2


def from_behind(value, axis, steps):
    count = lax.axis_size(axis)
    pairs = [(source, (source + steps) % count) for source in range(count)]
    return lax.ppermute(value, axis, pairs)


def wire_scale(tokens):
    bound = LARGEST + RATE * LARGEST * LARGEST * tokens
    return 2.0 ** math.floor(math.log2(float(jnp.finfo(WIRE).max) / bound))


def on_device(params, inputs, cotangent, mix):
    weights = params[0]
    features = inputs[0]
    cot_local = cotangent[0]
    rows = weights.shape[0]
    shards = lax.axis_size("fsdp")
    scale = wire_scale(features.shape[0] * shards)
    replica = lax.axis_index("blk")
    shard = lax.axis_index("fsdp")
    pick = (jnp.arange(lax.axis_size("blk")) == replica).astype(jnp.float32)
    coeff = jnp.dot(pick, mix.astype(jnp.float32), precision=lax.Precision.HIGHEST) / MIX_DENOM
    c_left = coeff[0] / scale
    c_self = coeff[1]
    c_right = coeff[2] / scale
    step = rows // CHUNKS

    def partial(owner, chunk):
        block = lax.dynamic_slice_in_dim(features, owner * rows + chunk * step, step, axis=1)
        return lax.dot_general(
            block, cot_local, (((0,), (0,)), ((), ())), preferred_element_type=jnp.float32
        )

    def others(chunk):
        return [
            (partial(lax.rem(shard + away, shards), chunk) * (RATE * scale)).astype(WIRE)
            for away in range(1, shards)
        ]

    arrived = {}
    mine = {}
    sides = {}
    out = jnp.zeros_like(weights)

    def send_terms(chunk):
        terms = others(chunk)
        if chunk >= AHEAD:
            terms, arrived[chunk - AHEAD] = lax.optimization_barrier((terms, arrived[chunk - AHEAD]))
        arrived[chunk] = [
            from_behind(term, "fsdp", away) for away, term in zip(range(1, shards), terms)
        ]

    def finish(chunk, out):
        left, right = sides[chunk]
        mixed = c_left * left.astype(jnp.float32) + c_self * mine[chunk] + c_right * right.astype(jnp.float32)
        return lax.dynamic_update_slice_in_dim(out, mixed, chunk * step, axis=0)

    for chunk in range(AHEAD):
        send_terms(chunk)
    for chunk in range(CHUNKS):
        if chunk + AHEAD < CHUNKS:
            send_terms(chunk + AHEAD)
        before = weights[chunk * step:(chunk + 1) * step]
        total = partial(shard, chunk)
        if chunk >= 1:
            before, total, sent = lax.optimization_barrier((before, total, sent))
        total = RATE * total
        for term in arrived[chunk]:
            total = total + term.astype(jnp.float32) / scale
        own = before - total
        mine[chunk], sent = lax.optimization_barrier((own, (own * scale).astype(WIRE)))
        sides[chunk] = (from_behind(sent, "blk", 1), from_behind(sent, "blk", -1))
        if chunk >= LAG:
            sides[chunk - LAG], mine[chunk] = lax.optimization_barrier((sides[chunk - LAG], mine[chunk]))
            out = finish(chunk - LAG, out)
    for chunk in range(CHUNKS - LAG, CHUNKS):
        out = finish(chunk, out)
    return out[None]


def solution(mesh):
    return jax.shard_map(
        on_device,
        mesh=mesh,
        in_specs=(P("blk", "fsdp", None), P("blk", "fsdp", None), P("blk", "fsdp", None), P()),
        out_specs=P("blk", "fsdp", None),
        check_vma=False,
    )
```

time: 429 us -> 170 us (0.40)
  waiting for transfers between devices: 369 us -> 76.7 us
  matrix products: 14.5 us -> 40.3 us
  starting transfers between devices: 4.47 us -> 26.2 us
  between operations: 13.4 us -> 1.57 us
  other arithmetic: 24.6 us -> 14.2 us
  local copies, waits for them, and re-layouts: 2.14 us -> 9.41 us
    reduce_scatter x1 -> x0, waiting for transfers between devices: 189 us -> none  [on_device(): lax.psum_scatter(lax.dot_general(features, cot_local, (((0,), (0,)), ((),...]
    ppermute x4 -> x24, waiting for transfers between devices: 181 us -> 76.7 us  [from_behind(): return lax.ppermute(value, axis, pairs)]
    dot_general x1 -> x16, matrix products: 14.4 us -> 40.1 us  [partial(): lax.dot_general(block, cot_local, (((0,), (0,)), ((), ())), preferred_ele...]
    broadcast_in_dim x1 -> x0, other arithmetic: 24.6 us -> none  [on_device(): return updated[None]]
    ppermute x4 -> x24, starting transfers between devices: 4.47 us -> 26.2 us  [from_behind(): return lax.ppermute(value, axis, pairs)]
    dynamic_update_slice x0 -> x7, other arithmetic: none -> 7.69 us  [finish(): return lax.dynamic_update_slice_in_dim(out, mixed, chunk * step, axis=0)]
    slice x1 -> x2, local copies, waits for them, and re-layouts: 0.64 us -> 6.78 us  [the longest x1 6.12 us: on_device(): before = weights[chunk * step:(chunk + 1) * step]]
    convert_element_type x0 -> x8, other arithmetic: none -> 5.4 us  [on_device(): (own * scale).astype(WIRE)]
  transfers between devices with their start and end apart: 5 -> 24, of which waited for: 2 -> 14; matrix products, arithmetic and copies ran while one was open for 0% -> 34% of each run, Pallas kernels for 0% -> 0%
where the time goes in v1:
time: 170 us; the launch traced here: 168 us
  waiting for transfers between devices  76.7 us (45%)
  matrix products  40.3 us (24%)
  starting transfers between devices  26.2 us (15%)
  other arithmetic  14.2 us (8%)
  local copies, waits for them, and re-layouts  9.41 us (6%)
    ppermute x24, waiting for transfers between devices, from_behind(): return lax.ppermute(value, axis, pairs)  76.7 us
    dot_general x16, matrix products, partial(): lax.dot_general(block, cot_local, (((0,), (0,)), ((), ())), preferred_ele...  40.1 us
    ppermute x24, starting transfers between devices, from_behind(): return lax.ppermute(value, axis, pairs)  26.2 us
    dynamic_update_slice x7, other arithmetic, finish(): return lax.dynamic_update_slice_in_dim(out, mixed, chunk * step, axis=0)  7.69 us
    slice x1, local copies, waits for them, and re-layouts, on_device(): before = weights[chunk * step:(chunk + 1) * step]  6.12 us
    convert_element_type x8, other arithmetic, on_device(): (own * scale).astype(WIRE)  5.4 us
  transfers between devices with their start and end apart: 24, of which 14 were waited for; matrix products, arithmetic and copies ran while one was open for 34% of the time, Pallas kernels for 0%

profile of v1, /device:TPU:1, one launch (start us, length us, event | category | flops | bytes accessed | tf_op | source)
XLA Modules:
  0.0 168.4 jit_solution(11655465099464992801)
XLA Ops:
  0.0 1.5 copy-done
  1.5 2.6 %fusion.77 = f16[256,1024]{1,0:T(8,128)(2,1)} fusion(bf16[1,896,1024]{2,1,0:T(8,128)(2,1)S(1)} %copy-done, bf16[1,896,4096]{2,1,0:T(8,128)(2,1)} %param.5, s32[]{:T(128)S(6)} %select_n.50), kind=kOutput, calls=%fused_computation.48 | convolution fusion | flops 470286336 | bytes 2818052 | tf_op jit(solution)/shard_map/dot_general | solution.py:46
  4.1 2.1 %collective-permute-start = (f16[256,1024]{1,0:T(8,128)(2,1)}, f16[256,1024]{1,0:T(8,128)(2,1)}, u32[]{:S(2)}, u32[]{:S(2)}) collective-permute-start(f16[256,1024]{1,0:T(8,128)(2,1)} %fusion.77), channel_id=1, source_target_pairs={{0,1},{1,0},{2,3},{3,2},{4,5},{5,4},{6,7},{7,6},{8,9},{9,8},{10,11... | collective-permute-start | bytes 1572872 | tf_op jit(solution)/shard_map/ppermute | solution.py:20
  6.1 1.7 %fusion.71 = f16[256,1024]{1,0:T(8,128)(2,1)S(1)} fusion(bf16[1,896,1024]{2,1,0:T(8,128)(2,1)S(1)} %copy-done, bf16[1,896,4096]{2,1,0:T(8,128)(2,1)} %param.5, s32[]{:T(128)S(6)} %select_n.54), kind=kOutput, calls=%fused_computation.46 | convolution fusion | flops 470286336 | bytes 2818052 | tf_op jit(solution)/shard_map/dot_general | solution.py:46
  8.0 2.7 %fusion.32 = f32[256,1024]{1,0:T(8,128)} fusion(bf16[1,896,1024]{2,1,0:T(8,128)(2,1)S(1)} %copy-done, bf16[1,896,4096]{2,1,0:T(8,128)(2,1)} %param.5, s32[]{:T(128)S(6)} %select_n.48), kind=kOutput, calls=%fused_computation.33 | convolution fusion | flops 470024192 | bytes 3342340 | tf_op jit(solution)/shard_map/dot_general | solution.py:46
  10.7 2.5 %fusion.80 = f16[256,1024]{1,0:T(8,128)(2,1)} fusion(bf16[1,896,1024]{2,1,0:T(8,128)(2,1)S(1)} %copy-done, bf16[1,896,4096]{2,1,0:T(8,128)(2,1)} %param.5, s32[]{:T(128)S(6)} %select_n.49), kind=kOutput, calls=%fused_computation.49 | convolution fusion | flops 470286336 | bytes 2818052 | tf_op jit(solution)/shard_map/dot_general | solution.py:46
  13.2 6.1 %slice_bitcast_fusion = (f32[256,1024]{1,0:T(8,128)S(1)}, f32[256,1024]{1,0:T(8,128)}, f32[256,1024]{1,0:T(8,128)}, f32[256,1024]{1,0:T(8,128)}, f32[256,1024]{1...) fusion(f32[1,2048,1024]{2,1,0:T(8,128)} %param.4), kind=kLoop, calls=%fused_computation.62 | loop fusion | bytes 14680064 | tf_op jit(solution)/shard_map/slice | solution.py:79
  19.4 2.7 %fusion.24 = f32[256,1024]{1,0:T(8,128)} fusion(bf16[1,896,1024]{2,1,0:T(8,128)(2,1)S(1)} %copy-done, bf16[1,896,4096]{2,1,0:T(8,128)(2,1)} %param.5, s32[]{:T(128)S(6)} %select_n.51), kind=kOutput, calls=%fused_computation.25 | convolution fusion | flops 469762048 | bytes 3342340 | tf_op jit(solution)/shard_map/dot_general | solution.py:46
  22.1 2.8 %fusion.22 = f32[256,1024]{1,0:T(8,128)} fusion(bf16[1,896,1024]{2,1,0:T(8,128)(2,1)S(1)} %copy-done, bf16[1,896,4096]{2,1,0:T(8,128)(2,1)} %param.5, s32[]{:T(128)S(6)} %select_n.52), kind=kOutput, calls=%fused_computation.23 | convolution fusion | flops 469762048 | bytes 3342340 | tf_op jit(solution)/shard_map/dot_general | solution.py:46
  24.9 2.6 %fusion.74 = f16[256,1024]{1,0:T(8,128)(2,1)} fusion(bf16[1,896,1024]{2,1,0:T(8,128)(2,1)S(1)} %copy-done, bf16[1,896,4096]{2,1,0:T(8,128)(2,1)} %param.5, s32[]{:T(128)S(6)} %select_n.53), kind=kOutput, calls=%fused_computation.47 | convolution fusion | flops 470286336 | bytes 2818052 | tf_op jit(solution)/shard_map/dot_general | solution.py:46
  27.4 2.5 %fusion.68 = f16[256,1024]{1,0:T(8,128)(2,1)} fusion(bf16[1,896,1024]{2,1,0:T(8,128)(2,1)S(1)} %copy-done, bf16[1,896,4096]{2,1,0:T(8,128)(2,1)} %param.5, s32[]{:T(128)S(6)} %select_n.55), kind=kOutput, calls=%fused_computation.45 | convolution fusion | flops 470286336 | bytes 2818052 | tf_op jit(solution)/shard_map/dot_general | solution.py:46
  30.1 0.7 fusion.137
  32.0 2.7 %fusion.14 = f32[256,1024]{1,0:T(8,128)} fusion(bf16[1,896,1024]{2,1,0:T(8,128)(2,1)S(1)} %copy-done, bf16[1,896,4096]{2,1,0:T(8,128)(2,1)} %param.5, s32[]{:T(128)S(6)} %select_n.56), kind=kOutput, calls=%fused_computation.15 | convolution fusion | flops 469762048 | bytes 3342340 | tf_op jit(solution)/shard_map/dot_general | solution.py:46
  34.7 2.5 %fusion.65 = f16[256,1024]{1,0:T(8,128)(2,1)} fusion(bf16[1,896,1024]{2,1,0:T(8,128)(2,1)S(1)} %copy-done, bf16[1,896,4096]{2,1,0:T(8,128)(2,1)} %param.5, s32[]{:T(128)S(6)} %select_n.57), kind=kOutput, calls=%fused_computation.44 | convolution fusion | flops 470286336 | bytes 2818052 | tf_op jit(solution)/shard_map/dot_general | solution.py:46
  37.3 2.8 %fusion.10 = f32[256,1024]{1,0:T(8,128)} fusion(bf16[1,896,1024]{2,1,0:T(8,128)(2,1)S(1)} %copy-done, bf16[1,896,4096]{2,1,0:T(8,128)(2,1)} %param.5, s32[]{:T(128)S(6)} %select_n.58), kind=kOutput, calls=%fused_computation.11 | convolution fusion | flops 469762048 | bytes 3342340 | tf_op jit(solution)/shard_map/dot_general | solution.py:46
  40.1 2.7 %fusion.6 = f32[256,1024]{1,0:T(8,128)} fusion(bf16[1,896,1024]{2,1,0:T(8,128)(2,1)S(1)} %copy-done, bf16[1,896,4096]{2,1,0:T(8,128)(2,1)} %param.5, s32[]{:T(128)S(6)} %select_n.60), kind=kOutput, calls=%fused_computation.7 | convolution fusion | flops 469762048 | bytes 3342340 | tf_op jit(solution)/shard_map/dot_general | solution.py:46
  42.8 2.7 %fusion.2 = f32[256,1024]{1,0:T(8,128)} fusion(bf16[1,896,1024]{2,1,0:T(8,128)(2,1)S(1)} %copy-done, bf16[1,896,4096]{2,1,0:T(8,128)(2,1)} %param.5, s32[]{:T(128)S(6)} %select_n.62), kind=kOutput, calls=%fused_computation.3 | convolution fusion | flops 469762048 | bytes 3342340 | tf_op jit(solution)/shard_map/dot_general | solution.py:46
  45.5 2.7 %fusion = f32[256,1024]{1,0:T(8,128)} fusion(bf16[1,896,1024]{2,1,0:T(8,128)(2,1)S(1)} %copy-done, bf16[1,896,4096]{2,1,0:T(8,128)(2,1)} %param.5, s32[]{:T(128)S(6)} %select_n.63), kind=kOutput, calls=%fused_computation.1 | convolution fusion | flops 469762048 | bytes 3342340 | tf_op jit(solution)/shard_map/dot_general | solution.py:46
  48.2 1.9 %fusion.62 = f16[256,1024]{1,0:T(8,128)(2,1)S(1)} fusion(bf16[1,896,1024]{2,1,0:T(8,128)(2,1)S(1)} %copy-done, bf16[1,896,4096]{2,1,0:T(8,128)(2,1)} %param.5, s32[]{:T(128)S(6)} %select_n.59), kind=kOutput, calls=%fused_computation.43 | convolution fusion | flops 470286336 | bytes 2818052 | tf_op jit(solution)/shard_map/dot_general | solution.py:46
  50.1 1.9 %fusion.59 = f16[256,1024]{1,0:T(8,128)(2,1)S(1)} fusion(bf16[1,896,1024]{2,1,0:T(8,128)(2,1)S(1)} %copy-done, bf16[1,896,4096]{2,1,0:T(8,128)(2,1)} %param.5, s32[]{:T(128)S(6)} %select_n.61), kind=kOutput, calls=%fused_computation.42 | convolution fusion | flops 470286336 | bytes 2818052 | tf_op jit(solution)/shard_map/dot_general | solution.py:46
  52.0 1.5 collective-permute-start.4
  53.5 2.1 %multiply_convert_fusion.7 = (f16[256,1024]{1,0:T(8,128)(2,1)S(1)}, f32[256,1024]{1,0:T(8,128)S(1)}) fusion(f32[256,1024]{1,0:T(8,128)} %fusion.32, f16[256,1024]{1,0:T(8,128)(2,1)} %collective-permute-done, f32[1,2048,1024]{2,1,0:T(8,128)} %param.4), kind=kLoop, calls=%fused_computation.82 | loop fusion | flops 1572864 | bytes 4194304 | tf_op jit(solution)/shard_map/convert_element_type | solution.py:87
  55.6 2.7 %collective-permute-start.1 = (f16[256,1024]{1,0:T(8,128)(2,1)S(1)}, f16[256,1024]{1,0:T(8,128)(2,1)S(1)}, u32[]{:S(2)}, u32[]{:S(2)}) collective-permute-start(f16[256,1024]{1,0:T(8,128)(2,1)S(1)} %get-tuple-element.66), channel_id=1, source_target_pairs={{0,2},{2,4},{4,6},{6,8},{8,10},{10,12},{12,14},{14,16},{16,18},{18... | collective-permute-start | bytes 1572872 | tf_op jit(solution)/shard_map/ppermute | solution.py:20
  58.3 0.3 collective-permute-start.7
  58.6 1.4 multiply_convert_fusion.6
  60.0 2.0 %collective-permute-start.5 = (f16[256,1024]{1,0:T(8,128)(2,1)S(1)}, f16[256,1024]{1,0:T(8,128)(2,1)S(1)}, u32[]{:S(2)}, u32[]{:S(2)}) collective-permute-start(f16[256,1024]{1,0:T(8,128)(2,1)S(1)} %get-tuple-element.70), channel_id=1, source_target_pairs={{0,2},{2,4},{4,6},{6,8},{8,10},{10,12},{12,14},{14,16},{16,18},{18... | collective-permute-start | bytes 1572872 | tf_op jit(solution)/shard_map/ppermute | solution.py:20
  62.0 2.8 %collective-permute-done.4 = f16[256,1024]{1,0:T(8,128)(2,1)S(1)} collective-permute-done((f16[256,1024]{1,0:T(8,128)(2,1)}, f16[256,1024]{1,0:T(8,128)(2,1)S(1)}, u32[]{:S(2)}, u32[]{:S(2)}) %collective-permute-start.4) | collective-permute-done | bytes 524320 | tf_op jit(solution)/shard_map/ppermute | solution.py:20
  64.8 3.3 %collective-permute-start.6 = (f16[256,1024]{1,0:T(8,128)(2,1)S(1)}, f16[256,1024]{1,0:T(8,128)(2,1)S(1)}, u32[]{:S(2)}, u32[]{:S(2)}) collective-permute-start(f16[256,1024]{1,0:T(8,128)(2,1)S(1)} %get-tuple-element.70), channel_id=1, source_target_pairs={{0,30},{2,0},{4,2},{6,4},{8,6},{10,8},{12,10},{14,12},{16,14},{18,... | collective-permute-start | bytes 1572872 | tf_op jit(solution)/shard_map/ppermute | solution.py:20
  68.1 0.4 multiply_convert_fusion.5
  68.5 1.6 collective-permute-done.1
  70.0 2.5 %collective-permute-start.8 = (f16[256,1024]{1,0:T(8,128)(2,1)S(1)}, f16[256,1024]{1,0:T(8,128)(2,1)S(1)}, u32[]{:S(2)}, u32[]{:S(2)}) collective-permute-start(f16[256,1024]{1,0:T(8,128)(2,1)S(1)} %get-tuple-element.79), channel_id=1, source_target_pairs={{0,2},{2,4},{4,6},{6,8},{8,10},{10,12},{12,14},{14,16},{16,18},{18... | collective-permute-start | bytes 1572872 | tf_op jit(solution)/shard_map/ppermute | solution.py:20
  72.5 11.2 %collective-permute-done.2 = f16[256,1024]{1,0:T(8,128)(2,1)S(1)} collective-permute-done((f16[256,1024]{1,0:T(8,128)(2,1)S(1)}, f16[256,1024]{1,0:T(8,128)(2,1)S(1)}, u32[]{:S(2)}, u32[]{:S(2)}) %collective-permute-start.2) | collective-permute-done | bytes 524320 | tf_op jit(solution)/shard_map/ppermute | solution.py:20
  83.8 0.4 multiply_convert_fusion.4
  84.2 2.7 %collective-permute-done.5 = f16[256,1024]{1,0:T(8,128)(2,1)S(1)} collective-permute-done((f16[256,1024]{1,0:T(8,128)(2,1)S(1)}, f16[256,1024]{1,0:T(8,128)(2,1)S(1)}, u32[]{:S(2)}, u32[]{:S(2)}) %collective-permute-start.5) | collective-permute-done | bytes 524320 | tf_op jit(solution)/shard_map/ppermute | solution.py:20
  86.9 8.1 %collective-permute-done.6 = f16[256,1024]{1,0:T(8,128)(2,1)S(1)} collective-permute-done((f16[256,1024]{1,0:T(8,128)(2,1)S(1)}, f16[256,1024]{1,0:T(8,128)(2,1)S(1)}, u32[]{:S(2)}, u32[]{:S(2)}) %collective-permute-start.6) | collective-permute-done | bytes 524320 | tf_op jit(solution)/shard_map/ppermute | solution.py:20
  95.2 1.2 collective-permute-start.13
  96.5 1.1 multiply_add_fusion
  97.6 1.1 pad_bitcast_fusion
  98.7 0.9 bitcast_dynamic-update-slice_fusion.6
  99.6 8.4 %collective-permute-done.10 = f16[256,1024]{1,0:T(8,128)(2,1)S(1)} collective-permute-done((f16[256,1024]{1,0:T(8,128)(2,1)S(1)}, f16[256,1024]{1,0:T(8,128)(2,1)S(1)}, u32[]{:S(2)}, u32[]{:S(2)}) %collective-permute-start.10) | collective-permute-done | bytes 524320 | tf_op jit(solution)/shard_map/ppermute | solution.py:20
  108.0 2.3 %collective-permute-start.12 = (f16[256,1024]{1,0:T(8,128)(2,1)S(1)}, f16[256,1024]{1,0:T(8,128)(2,1)S(1)}, u32[]{:S(2)}, u32[]{:S(2)}) collective-permute-start(f16[256,1024]{1,0:T(8,128)(2,1)S(1)} %get-tuple-element.88), channel_id=1, source_target_pairs={{0,30},{2,0},{4,2},{6,4},{8,6},{10,8},{12,10},{14,12},{16,14},{18,... | collective-permute-start | bytes 1572872 | tf_op jit(solution)/shard_map/ppermute | solution.py:20
  110.3 0.3 multiply_convert_fusion.3
  110.7 0.5 collective-permute-start.15
  111.2 8.0 %collective-permute-done.13 = f16[256,1024]{1,0:T(8,128)(2,1)S(1)} collective-permute-done((f16[256,1024]{1,0:T(8,128)(2,1)S(1)}, f16[256,1024]{1,0:T(8,128)(2,1)S(1)}, u32[]{:S(2)}, u32[]{:S(2)}) %collective-permute-start.13) | collective-permute-done | bytes 524320 | tf_op jit(solution)/shard_map/ppermute | solution.py:20
  119.2 0.3 multiply_convert_fusion.2
  119.5 2.7 %collective-permute-done.12 = f16[256,1024]{1,0:T(8,128)(2,1)S(1)} collective-permute-done((f16[256,1024]{1,0:T(8,128)(2,1)S(1)}, f16[256,1024]{1,0:T(8,128)(2,1)S(1)}, u32[]{:S(2)}, u32[]{:S(2)}) %collective-permute-start.12) | collective-permute-done | bytes 524320 | tf_op jit(solution)/shard_map/ppermute | solution.py:20
  122.4 1.2 collective-permute-start.19
  123.7 0.9 bitcast_dynamic-update-slice_fusion.5
  124.6 1.0 bitcast_dynamic-update-slice_fusion.4
  125.6 9.6 %collective-permute-done.16 = f16[256,1024]{1,0:T(8,128)(2,1)S(1)} collective-permute-done((f16[256,1024]{1,0:T(8,128)(2,1)S(1)}, f16[256,1024]{1,0:T(8,128)(2,1)S(1)}, u32[]{:S(2)}, u32[]{:S(2)}) %collective-permute-start.16) | collective-permute-done | bytes 524320 | tf_op jit(solution)/shard_map/ppermute | solution.py:20
  135.2 2.3 %collective-permute-start.18 = (f16[256,1024]{1,0:T(8,128)(2,1)S(1)}, f16[256,1024]{1,0:T(8,128)(2,1)S(1)}, u32[]{:S(2)}, u32[]{:S(2)}) collective-permute-start(f16[256,1024]{1,0:T(8,128)(2,1)S(1)} %get-tuple-element.106), channel_id=1, source_target_pairs={{0,30},{2,0},{4,2},{6,4},{8,6},{10,8},{12,10},{14,12},{16,14},{18,... | collective-permute-start | bytes 1572872 | tf_op jit(solution)/shard_map/ppermute | solution.py:20
  137.5 0.3 multiply_convert_fusion.1
  137.9 1.9 %collective-permute-start.21 = (f16[256,1024]{1,0:T(8,128)(2,1)S(1)}, f16[256,1024]{1,0:T(8,128)(2,1)S(1)}, u32[]{:S(2)}, u32[]{:S(2)}) collective-permute-start(f16[256,1024]{1,0:T(8,128)(2,1)S(1)} %get-tuple-element.114), channel_id=1, source_target_pairs={{0,30},{2,0},{4,2},{6,4},{8,6},{10,8},{12,10},{14,12},{16,14},{18,... | collective-permute-start | bytes 1572872 | tf_op jit(solution)/shard_map/ppermute | solution.py:20
  139.7 6.7 %collective-permute-done.19 = f16[256,1024]{1,0:T(8,128)(2,1)S(1)} collective-permute-done((f16[256,1024]{1,0:T(8,128)(2,1)S(1)}, f16[256,1024]{1,0:T(8,128)(2,1)S(1)}, u32[]{:S(2)}, u32[]{:S(2)}) %collective-permute-start.19) | collective-permute-done | bytes 524320 | tf_op jit(solution)/shard_map/ppermute | solution.py:20
  146.4 0.3 multiply_convert_fusion
  146.7 1.4 collective-permute-start.23
  148.2 0.4 collective-permute-start.22
  148.6 1.0 bitcast_dynamic-update-slice_fusion.3
  149.5 1.0 bitcast_dynamic-update-slice_fusion.2
  150.5 4.6 %collective-permute-done.21 = f16[256,1024]{1,0:T(8,128)(2,1)S(1)} collective-permute-done((f16[256,1024]{1,0:T(8,128)(2,1)S(1)}, f16[256,1024]{1,0:T(8,128)(2,1)S(1)}, u32[]{:S(2)}, u32[]{:S(2)}) %collective-permute-start.21) | collective-permute-done | bytes 524320 | tf_op jit(solution)/shard_map/ppermute | solution.py:20
  155.0 5.8 %collective-permute-done.20 = f16[256,1024]{1,0:T(8,128)(2,1)S(1)} collective-permute-done((f16[256,1024]{1,0:T(8,128)(2,1)S(1)}, f16[256,1024]{1,0:T(8,128)(2,1)S(1)}, u32[]{:S(2)}, u32[]{:S(2)}) %collective-permute-start.20) | collective-permute-done | bytes 524320 | tf_op jit(solution)/shard_map/ppermute | solution.py:20
  160.8 1.0 bitcast_dynamic-update-slice_fusion.1
  161.8 4.5 %collective-permute-done.23 = f16[256,1024]{1,0:T(8,128)(2,1)S(1)} collective-permute-done((f16[256,1024]{1,0:T(8,128)(2,1)S(1)}, f16[256,1024]{1,0:T(8,128)(2,1)S(1)}, u32[]{:S(2)}, u32[]{:S(2)}) %collective-permute-start.23) | collective-permute-done | bytes 524320 | tf_op jit(solution)/shard_map/ppermute | solution.py:20
  166.4 1.9 %bitcast_dynamic-update-slice_fusion = f32[1,2048,1024]{2,1,0:T(8,128)} fusion(f32[1,2048,1024]{2,1,0:T(8,128)} %copy-done.2, f16[256,1024]{1,0:T(8,128)(2,1)S(1)} %collective-permute-done.23, f32[256,1024]{1,0:T(8,128)S(1)} %get-tuple-element.124, f16[256,1024]{1,0:T(8,128)(2,1)S(1)} %collective-permute-done.22, f32[]{:T(128)} %bitcast.16, f32[]{:T(128)} %bitcast.15, ...), kind=kLoop, calls=%fused_computation.52 | loop fusion | flops 1835008 | bytes 3147264 | tf_op jit(solution)/shard_map/dynamic_update_slice | solution.py:72
  (60 shorter events, 1.0 us)
Async XLA Ops:
  0.0 1.5 copy-start
  4.1 48.0 %collective-permute-start = (f16[256,1024]{1,0:T(8,128)(2,1)}, f16[256,1024]{1,0:T(8,128)(2,1)}, u32[]{:S(2)}, u32[]{:S(2)}) collective-permute-start(f16[256,1024]{1,0:T(8,128)(2,1)} %fusion.77), channel_id=1, source_target_pairs={{0,1},{1,0},{2,3},{3,2},{4,5},{5,4},{6,7},{7,6},{8,9},{9,8},{10,11... | collective-permute-start | bytes 1572872 | tf_op jit(solution)/shard_map/ppermute | solution.py:20
  7.9 50.4 %collective-permute-start.3 = (f16[256,1024]{1,0:T(8,128)(2,1)S(1)}, f16[256,1024]{1,0:T(8,128)(2,1)}, u32[]{:S(2)}, u32[]{:S(2)}) collective-permute-start(f16[256,1024]{1,0:T(8,128)(2,1)S(1)} %fusion.71), channel_id=1, source_target_pairs={{0,1},{1,0},{2,3},{3,2},{4,5},{5,4},{6,7},{7,6},{8,9},{9,8},{10,11... | collective-permute-start | bytes 1572872 | tf_op jit(solution)/shard_map/ppermute | solution.py:20
  19.4 10.6 %copy-start.19 = (s32[16,3]{0,1:T(4,128)S(1)}, s32[16,3]{0,1:T(4,128)}, u32[]{:S(2)}) copy-start(s32[16,3]{0,1:T(4,128)} %param.7) | copy-start | bytes 580
  48.2 10.1 %copy-start.18 = (f16[256,1024]{1,0:T(8,128)(2,1)S(1)}, f16[256,1024]{1,0:T(8,128)(2,1)}, u32[]{:S(2)}) copy-start(f16[256,1024]{1,0:T(8,128)(2,1)} %fusion.74) | copy-start | bytes 1572868
  48.2 10.4 %copy-start.8 = (f32[256,1024]{1,0:T(8,128)S(1)}, f32[256,1024]{1,0:T(8,128)}, u32[]{:S(2)}) copy-start(f32[256,1024]{1,0:T(8,128)} %get-tuple-element.67) | copy-start | bytes 3145732
  48.2 10.4 %copy-start.15 = (f32[256,1024]{1,0:T(8,128)S(1)}, f32[256,1024]{1,0:T(8,128)}, u32[]{:S(2)}) copy-start(f32[256,1024]{1,0:T(8,128)} %fusion.22) | copy-start | bytes 3145732
  48.2 19.9 %copy-start.7 = (f32[256,1024]{1,0:T(8,128)S(1)}, f32[256,1024]{1,0:T(8,128)}, u32[]{:S(2)}) copy-start(f32[256,1024]{1,0:T(8,128)} %get-tuple-element.71) | copy-start | bytes 3145732
  48.2 19.9 %copy-start.13 = (f32[256,1024]{1,0:T(8,128)S(1)}, f32[256,1024]{1,0:T(8,128)}, u32[]{:S(2)}) copy-start(f32[256,1024]{1,0:T(8,128)} %fusion.24) | copy-start | bytes 3145732
  50.1 33.7 %copy-start.6 = (f32[256,1024]{1,0:T(8,128)S(1)}, f32[256,1024]{1,0:T(8,128)}, u32[]{:S(2)}) copy-start(f32[256,1024]{1,0:T(8,128)} %get-tuple-element.80) | copy-start | bytes 3145732
  50.1 33.7 %copy-start.14 = (f32[256,1024]{1,0:T(8,128)S(1)}, f32[256,1024]{1,0:T(8,128)}, u32[]{:S(2)}) copy-start(f32[256,1024]{1,0:T(8,128)} %fusion.14) | copy-start | bytes 3145732
  52.0 12.7 %collective-permute-start.4 = (f16[256,1024]{1,0:T(8,128)(2,1)}, f16[256,1024]{1,0:T(8,128)(2,1)S(1)}, u32[]{:S(2)}, u32[]{:S(2)}) collective-permute-start(f16[256,1024]{1,0:T(8,128)(2,1)} %fusion.80), channel_id=1, source_target_pairs={{0,1},{1,0},{2,3},{3,2},{4,5},{5,4},{6,7},{7,6},{8,9},{9,8},{10,11... | collective-permute-start | bytes 1572872 | tf_op jit(solution)/shard_map/ppermute | solution.py:20
  55.6 39.4 %copy-start.16 = (f16[256,1024]{1,0:T(8,128)(2,1)S(1)}, f16[256,1024]{1,0:T(8,128)(2,1)}, u32[]{:S(2)}) copy-start(f16[256,1024]{1,0:T(8,128)(2,1)} %fusion.68) | copy-start | bytes 1572868
  55.6 39.6 %copy-start.17 = (f16[256,1024]{1,0:T(8,128)(2,1)S(1)}, f16[256,1024]{1,0:T(8,128)(2,1)}, u32[]{:S(2)}) copy-start(f16[256,1024]{1,0:T(8,128)(2,1)} %fusion.65) | copy-start | bytes 1572868
  55.6 14.4 %collective-permute-start.1 = (f16[256,1024]{1,0:T(8,128)(2,1)S(1)}, f16[256,1024]{1,0:T(8,128)(2,1)S(1)}, u32[]{:S(2)}, u32[]{:S(2)}) collective-permute-start(f16[256,1024]{1,0:T(8,128)(2,1)S(1)} %get-tuple-element.66), channel_id=1, source_target_pairs={{0,2},{2,4},{4,6},{6,8},{8,10},{10,12},{12,14},{14,16},{16,18},{18... | collective-permute-start | bytes 1572872 | tf_op jit(solution)/shard_map/ppermute | solution.py:20
  58.3 25.5 %collective-permute-start.2 = (f16[256,1024]{1,0:T(8,128)(2,1)S(1)}, f16[256,1024]{1,0:T(8,128)(2,1)S(1)}, u32[]{:S(2)}, u32[]{:S(2)}) collective-permute-start(f16[256,1024]{1,0:T(8,128)(2,1)S(1)} %get-tuple-element.66), channel_id=1, source_target_pairs={{0,30},{2,0},{4,2},{6,4},{8,6},{10,8},{12,10},{14,12},{16,14},{18,... | collective-permute-start | bytes 1572872 | tf_op jit(solution)/shard_map/ppermute | solution.py:20
  58.3 25.5 %collective-permute-start.7 = (f16[256,1024]{1,0:T(8,128)(2,1)S(1)}, f16[256,1024]{1,0:T(8,128)(2,1)S(1)}, u32[]{:S(2)}, u32[]{:S(2)}) collective-permute-start(f16[256,1024]{1,0:T(8,128)(2,1)S(1)} %copy-done.18), channel_id=1, source_target_pairs={{0,1},{1,0},{2,3},{3,2},{4,5},{5,4},{6,7},{7,6},{8,9},{9,8},{10,11... | collective-permute-start | bytes 1572872 | tf_op jit(solution)/shard_map/ppermute | solution.py:20
  60.0 26.9 %collective-permute-start.5 = (f16[256,1024]{1,0:T(8,128)(2,1)S(1)}, f16[256,1024]{1,0:T(8,128)(2,1)S(1)}, u32[]{:S(2)}, u32[]{:S(2)}) collective-permute-start(f16[256,1024]{1,0:T(8,128)(2,1)S(1)} %get-tuple-element.70), channel_id=1, source_target_pairs={{0,2},{2,4},{4,6},{6,8},{8,10},{10,12},{12,14},{14,16},{16,18},{18... | collective-permute-start | bytes 1572872 | tf_op jit(solution)/shard_map/ppermute | solution.py:20
  64.8 30.2 %collective-permute-start.6 = (f16[256,1024]{1,0:T(8,128)(2,1)S(1)}, f16[256,1024]{1,0:T(8,128)(2,1)S(1)}, u32[]{:S(2)}, u32[]{:S(2)}) collective-permute-start(f16[256,1024]{1,0:T(8,128)(2,1)S(1)} %get-tuple-element.70), channel_id=1, source_target_pairs={{0,30},{2,0},{4,2},{6,4},{8,6},{10,8},{12,10},{14,12},{16,14},{18,... | collective-permute-start | bytes 1572872 | tf_op jit(solution)/shard_map/ppermute | solution.py:20
  70.0 40.6 %collective-permute-start.8 = (f16[256,1024]{1,0:T(8,128)(2,1)S(1)}, f16[256,1024]{1,0:T(8,128)(2,1)S(1)}, u32[]{:S(2)}, u32[]{:S(2)}) collective-permute-start(f16[256,1024]{1,0:T(8,128)(2,1)S(1)} %get-tuple-element.79), channel_id=1, source_target_pairs={{0,2},{2,4},{4,6},{6,8},{8,10},{10,12},{12,14},{14,16},{16,18},{18... | collective-permute-start | bytes 1572872 | tf_op jit(solution)/shard_map/ppermute | solution.py:20
  83.8 26.9 %collective-permute-start.9 = (f16[256,1024]{1,0:T(8,128)(2,1)S(1)}, f16[256,1024]{1,0:T(8,128)(2,1)S(1)}, u32[]{:S(2)}, u32[]{:S(2)}) collective-permute-start(f16[256,1024]{1,0:T(8,128)(2,1)S(1)} %get-tuple-element.79), channel_id=1, source_target_pairs={{0,30},{2,0},{4,2},{6,4},{8,6},{10,8},{12,10},{14,12},{16,14},{18,... | collective-permute-start | bytes 1572872 | tf_op jit(solution)/shard_map/ppermute | solution.py:20
  95.0 24.5 %collective-permute-start.11 = (f16[256,1024]{1,0:T(8,128)(2,1)S(1)}, f16[256,1024]{1,0:T(8,128)(2,1)S(1)}, u32[]{:S(2)}, u32[]{:S(2)}) collective-permute-start(f16[256,1024]{1,0:T(8,128)(2,1)S(1)} %get-tuple-element.88), channel_id=1, source_target_pairs={{0,2},{2,4},{4,6},{6,8},{8,10},{10,12},{12,14},{14,16},{16,18},{18... | collective-permute-start | bytes 1572872 | tf_op jit(solution)/shard_map/ppermute | solution.py:20
  95.0 13.0 %collective-permute-start.10 = (f16[256,1024]{1,0:T(8,128)(2,1)S(1)}, f16[256,1024]{1,0:T(8,128)(2,1)S(1)}, u32[]{:S(2)}, u32[]{:S(2)}) collective-permute-start(f16[256,1024]{1,0:T(8,128)(2,1)S(1)} %copy-done.16), channel_id=1, source_target_pairs={{0,1},{1,0},{2,3},{3,2},{4,5},{5,4},{6,7},{7,6},{8,9},{9,8},{10,11... | collective-permute-start | bytes 1572872 | tf_op jit(solution)/shard_map/ppermute | solution.py:20
  95.2 24.0 %collective-permute-start.13 = (f16[256,1024]{1,0:T(8,128)(2,1)S(1)}, f16[256,1024]{1,0:T(8,128)(2,1)S(1)}, u32[]{:S(2)}, u32[]{:S(2)}) collective-permute-start(f16[256,1024]{1,0:T(8,128)(2,1)S(1)} %copy-done.17), channel_id=1, source_target_pairs={{0,1},{1,0},{2,3},{3,2},{4,5},{5,4},{6,7},{7,6},{8,9},{9,8},{10,11... | collective-permute-start | bytes 1572872 | tf_op jit(solution)/shard_map/ppermute | solution.py:20
  96.5 13.8 %copy-start.5 = (f32[256,1024]{1,0:T(8,128)S(1)}, f32[256,1024]{1,0:T(8,128)}, u32[]{:S(2)}) copy-start(f32[256,1024]{1,0:T(8,128)} %get-tuple-element.89) | copy-start | bytes 3145732
  96.5 13.8 %copy-start.12 = (f32[256,1024]{1,0:T(8,128)S(1)}, f32[256,1024]{1,0:T(8,128)}, u32[]{:S(2)}) copy-start(f32[256,1024]{1,0:T(8,128)} %fusion.10) | copy-start | bytes 3145732
  97.6 21.6 %copy-start.4 = (f32[256,1024]{1,0:T(8,128)S(1)}, f32[256,1024]{1,0:T(8,128)}, u32[]{:S(2)}) copy-start(f32[256,1024]{1,0:T(8,128)} %get-tuple-element.98) | copy-start | bytes 3145732
  97.6 21.6 %copy-start.11 = (f32[256,1024]{1,0:T(8,128)S(1)}, f32[256,1024]{1,0:T(8,128)}, u32[]{:S(2)}) copy-start(f32[256,1024]{1,0:T(8,128)} %fusion.6) | copy-start | bytes 3145732
  99.6 37.9 %copy-start.3 = (f32[256,1024]{1,0:T(8,128)S(1)}, f32[256,1024]{1,0:T(8,128)}, u32[]{:S(2)}) copy-start(f32[256,1024]{1,0:T(8,128)} %get-tuple-element.107) | copy-start | bytes 3145732
  99.6 37.9 %copy-start.10 = (f32[256,1024]{1,0:T(8,128)S(1)}, f32[256,1024]{1,0:T(8,128)}, u32[]{:S(2)}) copy-start(f32[256,1024]{1,0:T(8,128)} %fusion.2) | copy-start | bytes 3145732
  108.0 14.2 %collective-permute-start.12 = (f16[256,1024]{1,0:T(8,128)(2,1)S(1)}, f16[256,1024]{1,0:T(8,128)(2,1)S(1)}, u32[]{:S(2)}, u32[]{:S(2)}) collective-permute-start(f16[256,1024]{1,0:T(8,128)(2,1)S(1)} %get-tuple-element.88), channel_id=1, source_target_pairs={{0,30},{2,0},{4,2},{6,4},{8,6},{10,8},{12,10},{14,12},{16,14},{18,... | collective-permute-start | bytes 1572872 | tf_op jit(solution)/shard_map/ppermute | solution.py:20
  110.6 27.2 %collective-permute-start.14 = (f16[256,1024]{1,0:T(8,128)(2,1)S(1)}, f16[256,1024]{1,0:T(8,128)(2,1)S(1)}, u32[]{:S(2)}, u32[]{:S(2)}) collective-permute-start(f16[256,1024]{1,0:T(8,128)(2,1)S(1)} %get-tuple-element.97), channel_id=1, source_target_pairs={{0,2},{2,4},{4,6},{6,8},{8,10},{10,12},{12,14},{14,16},{16,18},{18... | collective-permute-start | bytes 1572872 | tf_op jit(solution)/shard_map/ppermute | solution.py:20
  110.7 29.0 %collective-permute-start.15 = (f16[256,1024]{1,0:T(8,128)(2,1)S(1)}, f16[256,1024]{1,0:T(8,128)(2,1)S(1)}, u32[]{:S(2)}, u32[]{:S(2)}) collective-permute-start(f16[256,1024]{1,0:T(8,128)(2,1)S(1)} %get-tuple-element.97), channel_id=1, source_target_pairs={{0,30},{2,0},{4,2},{6,4},{8,6},{10,8},{12,10},{14,12},{16,14},{18,... | collective-permute-start | bytes 1572872 | tf_op jit(solution)/shard_map/ppermute | solution.py:20
  111.2 35.2 %copy-start.9 = (f32[256,1024]{1,0:T(8,128)S(1)}, f32[256,1024]{1,0:T(8,128)}, u32[]{:S(2)}) copy-start(f32[256,1024]{1,0:T(8,128)} %fusion) | copy-start | bytes 3145732
  122.2 26.0 %collective-permute-start.17 = (f16[256,1024]{1,0:T(8,128)(2,1)S(1)}, f16[256,1024]{1,0:T(8,128)(2,1)S(1)}, u32[]{:S(2)}, u32[]{:S(2)}) collective-permute-start(f16[256,1024]{1,0:T(8,128)(2,1)S(1)} %get-tuple-element.106), channel_id=1, source_target_pairs={{0,2},{2,4},{4,6},{6,8},{8,10},{10,12},{12,14},{14,16},{16,18},{18... | collective-permute-start | bytes 1572872 | tf_op jit(solution)/shard_map/ppermute | solution.py:20
  122.2 13.0 %collective-permute-start.16 = (f16[256,1024]{1,0:T(8,128)(2,1)S(1)}, f16[256,1024]{1,0:T(8,128)(2,1)S(1)}, u32[]{:S(2)}, u32[]{:S(2)}) collective-permute-start(f16[256,1024]{1,0:T(8,128)(2,1)S(1)} %fusion.62), channel_id=1, source_target_pairs={{0,1},{1,0},{2,3},{3,2},{4,5},{5,4},{6,7},{7,6},{8,9},{9,8},{10,11... | collective-permute-start | bytes 1572872 | tf_op jit(solution)/shard_map/ppermute | solution.py:20
  122.4 24.0 %collective-permute-start.19 = (f16[256,1024]{1,0:T(8,128)(2,1)S(1)}, f16[256,1024]{1,0:T(8,128)(2,1)S(1)}, u32[]{:S(2)}, u32[]{:S(2)}) collective-permute-start(f16[256,1024]{1,0:T(8,128)(2,1)S(1)} %fusion.59), channel_id=1, source_target_pairs={{0,1},{1,0},{2,3},{3,2},{4,5},{5,4},{6,7},{7,6},{8,9},{9,8},{10,11... | collective-permute-start | bytes 1572872 | tf_op jit(solution)/shard_map/ppermute | solution.py:20
  135.2 13.4 %collective-permute-start.18 = (f16[256,1024]{1,0:T(8,128)(2,1)S(1)}, f16[256,1024]{1,0:T(8,128)(2,1)S(1)}, u32[]{:S(2)}, u32[]{:S(2)}) collective-permute-start(f16[256,1024]{1,0:T(8,128)(2,1)S(1)} %get-tuple-element.106), channel_id=1, source_target_pairs={{0,30},{2,0},{4,2},{6,4},{8,6},{10,8},{12,10},{14,12},{16,14},{18,... | collective-permute-start | bytes 1572872 | tf_op jit(solution)/shard_map/ppermute | solution.py:20
  137.9 17.2 %collective-permute-start.21 = (f16[256,1024]{1,0:T(8,128)(2,1)S(1)}, f16[256,1024]{1,0:T(8,128)(2,1)S(1)}, u32[]{:S(2)}, u32[]{:S(2)}) collective-permute-start(f16[256,1024]{1,0:T(8,128)(2,1)S(1)} %get-tuple-element.114), channel_id=1, source_target_pairs={{0,30},{2,0},{4,2},{6,4},{8,6},{10,8},{12,10},{14,12},{16,14},{18,... | collective-permute-start | bytes 1572872 | tf_op jit(solution)/shard_map/ppermute | solution.py:20
  139.7 21.1 %collective-permute-start.20 = (f16[256,1024]{1,0:T(8,128)(2,1)S(1)}, f16[256,1024]{1,0:T(8,128)(2,1)S(1)}, u32[]{:S(2)}, u32[]{:S(2)}) collective-permute-start(f16[256,1024]{1,0:T(8,128)(2,1)S(1)} %get-tuple-element.114), channel_id=1, source_target_pairs={{0,2},{2,4},{4,6},{6,8},{8,10},{10,12},{12,14},{14,16},{16,18},{18... | collective-permute-start | bytes 1572872 | tf_op jit(solution)/shard_map/ppermute | solution.py:20
  146.4 21.9 %copy-start.1 = (bf16[1,896,1024]{2,1,0:T(8,128)(2,1)S(1)}, bf16[1,896,1024]{2,1,0:T(8,128)(2,1)}, u32[]{:S(2)}) copy-start(bf16[1,896,1024]{2,1,0:T(8,128)(2,1)} %param.6) | copy-start | bytes 5505028
  146.7 19.5 %collective-permute-start.23 = (f16[256,1024]{1,0:T(8,128)(2,1)S(1)}, f16[256,1024]{1,0:T(8,128)(2,1)S(1)}, u32[]{:S(2)}, u32[]{:S(2)}) collective-permute-start(f16[256,1024]{1,0:T(8,128)(2,1)S(1)} %get-tuple-element.123), channel_id=1, source_target_pairs={{0,30},{2,0},{4,2},{6,4},{8,6},{10,8},{12,10},{14,12},{16,14},{18,... | collective-permute-start | bytes 1572872 | tf_op jit(solution)/shard_map/ppermute | solution.py:20
  148.2 18.3 %collective-permute-start.22 = (f16[256,1024]{1,0:T(8,128)(2,1)S(1)}, f16[256,1024]{1,0:T(8,128)(2,1)S(1)}, u32[]{:S(2)}, u32[]{:S(2)}) collective-permute-start(f16[256,1024]{1,0:T(8,128)(2,1)S(1)} %get-tuple-element.123), channel_id=1, source_target_pairs={{0,2},{2,4},{4,6},{6,8},{8,10},{10,12},{12,14},{14,16},{16,18},{18... | collective-permute-start | bytes 1572872 | tf_op jit(solution)/shard_map/ppermute | solution.py:20
  161.8 4.6 %copy-start.2 = (f32[1,2048,1024]{2,1,0:T(8,128)}, f32[1,2048,1024]{2,1,0:T(8,128)S(1)}, u32[]{:S(2)}) copy-start(f32[1,2048,1024]{2,1,0:T(8,128)S(1)} %bitcast_dynamic-update-slice_fusion.1) | copy-start | bytes 25165828

commit v2 on v1

v2 whole, which is shorter than its diff:
```python
import math

import jax
import jax.numpy as jnp
from jax import lax
from jax.sharding import PartitionSpec as P

MIX_DENOM = 64
RATE = 0.03
LARGEST = 6.0
WIRE = jnp.float16
CHUNKS = 8
AHEAD = 2


def from_behind(value, axis, steps):
    count = lax.axis_size(axis)
    pairs = [(source, (source + steps) % count) for source in range(count)]
    return lax.ppermute(value, axis, pairs)


def swapped(value, axis, first):
    count = lax.axis_size(axis)
    pairs = []
    for source in range(first, count, 2):
        partner = (source + 1) % count
        pairs += [(source, partner), (partner, source)]
    return lax.ppermute(value, axis, pairs)


def wire_scale(tokens):
    bound = LARGEST + RATE * LARGEST * LARGEST * tokens
    return 2.0 ** math.floor(math.log2(float(jnp.finfo(WIRE).max) / bound))


def on_device(params, inputs, cotangent, mix):
    weights = params[0]
    features = inputs[0]
    cot_local = cotangent[0]
    rows = weights.shape[0]
    shards = lax.axis_size("fsdp")
    scale = wire_scale(features.shape[0] * shards)
    replica = lax.axis_index("blk")
    shard = lax.axis_index("fsdp")
    pick = (jnp.arange(lax.axis_size("blk")) == replica).astype(jnp.float32)
    coeff = jnp.dot(pick, mix.astype(jnp.float32), precision=lax.Precision.HIGHEST) / MIX_DENOM
    even = replica % 2 == 0
    c_self = coeff[1]
    c_near = jnp.where(even, coeff[2], coeff[0]) / scale
    c_far = jnp.where(even, coeff[0], coeff[2]) / scale
    step = rows // CHUNKS

    def partial(owner, first, count):
        block = lax.dynamic_slice_in_dim(features, owner * rows + first, count, axis=1)
        return lax.dot_general(
            block, cot_local, (((0,), (0,)), ((), ())), preferred_element_type=jnp.float32
        )

    def for_others(first, count):
        return [
            (partial(lax.rem(shard + away, shards), first, count) * (RATE * scale)).astype(WIRE)
            for away in range(1, shards)
        ]

    def send_terms(terms):
        return [from_behind(term, "fsdp", away) for away, term in zip(range(1, shards), terms)]

    def rows_of(value, chunk):
        return value[chunk * step:(chunk + 1) * step]

    terms = {chunk: for_others(chunk * step, step) for chunk in range(AHEAD)}
    arrived = {chunk: send_terms(terms[chunk]) for chunk in range(AHEAD)}
    gradient = partial(shard, 0, rows)
    rest = for_others(AHEAD * step, rows - AHEAD * step)
    mine = {}
    near = {}
    far = {}
    out = jnp.zeros_like(weights)

    def finish(chunk, out):
        mixed = (
            c_near * near[chunk].astype(jnp.float32)
            + c_self * mine[chunk]
            + c_far * far[chunk].astype(jnp.float32)
        )
        return lax.dynamic_update_slice_in_dim(out, mixed, chunk * step, axis=0)

    for chunk in range(CHUNKS):
        if chunk >= 1:
            arrived[chunk], mine[chunk - 1], out = lax.optimization_barrier(
                (arrived[chunk], mine[chunk - 1], out)
            )
        total = RATE * rows_of(gradient, chunk)
        for term in arrived[chunk]:
            total = total + term.astype(jnp.float32) / scale
        own = rows_of(weights, chunk) - total
        mine[chunk], sent = lax.optimization_barrier((own, (own * scale).astype(WIRE)))
        if chunk + AHEAD < CHUNKS:
            rest, sent = lax.optimization_barrier((rest, sent))
            arrived[chunk + AHEAD] = send_terms([rows_of(term, chunk) for term in rest])
        far[chunk] = swapped(sent, "blk", 1)
        near[chunk] = swapped(sent, "blk", 0)
        if chunk >= 1:
            out = finish(chunk - 1, out)
    out = finish(CHUNKS - 1, out)
    return out[None]


def solution(mesh):
    return jax.shard_map(
        on_device,
        mesh=mesh,
        in_specs=(P("blk", "fsdp", None), P("blk", "fsdp", None), P("blk", "fsdp", None), P()),
        out_specs=P("blk", "fsdp", None),
        check_vma=False,
    )
```

time: 170 us -> 127 us (0.75)
  waiting for transfers between devices: 76.7 us -> 45.1 us
  matrix products: 40.3 us -> 20 us
  starting transfers between devices: 26.2 us -> 36.5 us
  local copies, waits for them, and re-layouts: 9.41 us -> 5.89 us
  other arithmetic: 14.2 us -> 16.4 us
    ppermute x24 -> x8, waiting for transfers between devices: 76.7 us -> 16.1 us  [from_behind(): return lax.ppermute(value, axis, pairs)]
    ppermute x0 -> x16, starting transfers between devices: none -> 30.3 us  [swapped(): return lax.ppermute(value, axis, pairs)]
    ppermute x0 -> x16, waiting for transfers between devices: none -> 29 us  [swapped(): return lax.ppermute(value, axis, pairs)]
    dot_general x16 -> x4, matrix products: 40.1 us -> 19.9 us  [partial(): lax.dot_general(block, cot_local, (((0,), (0,)), ((), ())), preferred_ele...]
    ppermute x24 -> x8, starting transfers between devices: 26.2 us -> 6.22 us  [from_behind(): return lax.ppermute(value, axis, pairs)]
    slice x2 -> x7, local copies, waits for them, and re-layouts: 6.78 us -> 3.3 us  [the longest x6 2.62 us: rows_of(): return value[chunk * step:(chunk + 1) * step]]
    dynamic_update_slice x7 -> x8, other arithmetic: 7.69 us -> 9.34 us  [finish(): return lax.dynamic_update_slice_in_dim(out, mixed, chunk * step, axis=0)]
  transfers between devices with their start and end apart: 24 -> 24, of which waited for: 14 -> 10; matrix products, arithmetic and copies ran while one was open for 34% -> 29% of each run, Pallas kernels for 0% -> 0%
where the time goes in v2:
time: 127 us
  waiting for transfers between devices  45.1 us (36%)
  starting transfers between devices  36.5 us (29%)
  matrix products  20 us (16%)
  other arithmetic  16.4 us (13%)
  local copies, waits for them, and re-layouts  5.89 us (5%)
  between operations  2.97 us (2%)
    ppermute x16, starting transfers between devices, swapped(): return lax.ppermute(value, axis, pairs)  30.3 us
    ppermute x16, waiting for transfers between devices, swapped(): return lax.ppermute(value, axis, pairs)  29 us
    dot_general x4, matrix products, partial(): lax.dot_general(block, cot_local, (((0,), (0,)), ((), ())), preferred_ele...  19.9 us
    ppermute x8, waiting for transfers between devices, from_behind(): return lax.ppermute(value, axis, pairs)  16.1 us
    dynamic_update_slice x8, other arithmetic, finish(): return lax.dynamic_update_slice_in_dim(out, mixed, chunk * step, axis=0)  9.34 us
    convert_element_type x8, other arithmetic, on_device(): (own * scale).astype(WIRE)  7.06 us
    ppermute x8, starting transfers between devices, from_behind(): return lax.ppermute(value, axis, pairs)  6.22 us
    slice x6, local copies, waits for them, and re-layouts, rows_of(): return value[chunk * step:(chunk + 1) * step]  2.62 us
  transfers between devices with their start and end apart: 24, of which 10 were waited for; matrix products, arithmetic and copies ran while one was open for 29% of the time, Pallas kernels for 0%

profile of v2, /device:TPU:1, one launch (start us, length us, event | category | flops | bytes accessed | tf_op | source)
XLA Modules:
  0.0 126.9 jit_solution(12957337609541689881)
XLA Ops:
  0.0 1.5 %copy-done = bf16[1,896,1024]{2,1,0:T(8,128)(2,1)S(1)} copy-done((bf16[1,896,1024]{2,1,0:T(8,128)(2,1)S(1)}, bf16[1,896,1024]{2,1,0:T(8,128)(2,1)}, u32[]{:S(2)}) %copy-start) | copy-done | bytes 1835032
  1.5 1.7 %fusion.20 = f16[256,1024]{1,0:T(8,128)(2,1)S(1)} fusion(bf16[1,896,1024]{2,1,0:T(8,128)(2,1)S(1)} %copy-done, bf16[1,896,4096]{2,1,0:T(8,128)(2,1)} %param.5, s32[]{:T(128)S(6)} %select_n.28), kind=kOutput, calls=%fused_computation.15 | convolution fusion | flops 470286336 | bytes 2818052 | tf_op jit(solution)/shard_map/dot_general | solution.py:55
  3.3 2.1 %collective-permute-start = (f16[256,1024]{1,0:T(8,128)(2,1)S(1)}, f16[256,1024]{1,0:T(8,128)(2,1)S(1)}, u32[]{:S(2)}, u32[]{:S(2)}) collective-permute-start(f16[256,1024]{1,0:T(8,128)(2,1)S(1)} %fusion.20), channel_id=1, source_target_pairs={{0,1},{1,0},{2,3},{3,2},{4,5},{5,4},{6,7},{7,6},{8,9},{9,8},{10,11... | collective-permute-start | bytes 1572872 | tf_op jit(solution)/shard_map/ppermute | solution.py:19
  5.4 2.5 %fusion.17 = f16[256,1024]{1,0:T(8,128)(2,1)} fusion(bf16[1,896,1024]{2,1,0:T(8,128)(2,1)S(1)} %copy-done, bf16[1,896,4096]{2,1,0:T(8,128)(2,1)} %param.5, s32[]{:T(128)S(6)} %select_n.29), kind=kOutput, calls=%fused_computation.14 | convolution fusion | flops 470286336 | bytes 2818052 | tf_op jit(solution)/shard_map/dot_general | solution.py:55
  7.9 0.0 collective-permute-start.1
  8.0 8.8 %fusion = f32[2048,1024]{1,0:T(8,128)} fusion(bf16[1,896,4096]{2,1,0:T(8,128)(2,1)} %param.5, s32[]{:T(128)S(6)} %select_n.27, bf16[1,896,1024]{2,1,0:T(8,128)(2,1)S(1)} %copy-done), kind=kOutput, calls=%fused_computation.1 | convolution fusion | flops 3758096384 | bytes 13893636 | tf_op jit(solution)/shard_map/dot_general | solution.py:55
  16.8 6.7 %multiply_convert_fusion = f16[1536,1024]{1,0:T(8,128)(2,1)} fusion(bf16[1,896,4096]{2,1,0:T(8,128)(2,1)} %param.5, s32[]{:T(128)S(6)} %select_n.26, bf16[1,896,1024]{2,1,0:T(8,128)(2,1)S(1)} %copy-done), kind=kOutput, calls=%fused_computation | convolution fusion | flops 2821718016 | bytes 7733252 | tf_op jit(solution)/shard_map/dot_general | solution.py:55
  23.5 2.6 %multiply_convert_fusion.8 = (f16[256,1024]{1,0:T(8,128)(2,1)}, f32[256,1024]{1,0:T(8,128)S(1)}) fusion(f16[256,1024]{1,0:T(8,128)(2,1)S(1)} %collective-permute-done, f32[2048,1024]{1,0:T(8,128)} %fusion, f32[1,2048,1024]{2,1,0:T(8,128)} %param.4), kind=kLoop, calls=%fused_computation.57 | loop fusion | flops 1835008 | bytes 4194304 | tf_op jit(solution)/shard_map/convert_element_type | solution.py:97
  26.2 1.0 collective-permute-start.3
  27.1 1.6 %collective-permute-start.4 = (f16[256,1024]{1,0:T(8,128)(2,1)}, f16[256,1024]{1,0:T(8,128)(2,1)}, u32[]{:S(2)}, u32[]{:S(2)}) collective-permute-start(f16[256,1024]{1,0:T(8,128)(2,1)} %get-tuple-element.62), channel_id=1, source_target_pairs={{2,4},{4,2},{6,8},{8,6},{10,12},{12,10},{14,16},{16,14},{18,20},{2... | collective-permute-start | bytes 1572872 | tf_op jit(solution)/shard_map/ppermute | solution.py:28
  28.7 0.1 fusion.23
  28.8 0.7 fusion.61
  32.2 1.1 slice.110
  33.3 1.3 %collective-permute-start.2 = (f16[256,1024]{1,0:T(8,128)(2,1)S(1)}, f16[256,1024]{1,0:T(8,128)(2,1)S(1)}, u32[]{:S(2)}, u32[]{:S(2)}) collective-permute-start(f16[256,1024]{1,0:T(8,128)(2,1)S(1)} %slice.110), channel_id=1, source_target_pairs={{0,1},{1,0},{2,3},{3,2},{4,5},{5,4},{6,7},{7,6},{8,9},{9,8},{10,11... | collective-permute-start | bytes 1572872 | tf_op jit(solution)/shard_map/ppermute | solution.py:19
  34.6 2.6 %multiply_convert_fusion.7 = (f16[256,1024]{1,0:T(8,128)(2,1)S(1)}, f32[256,1024]{1,0:T(8,128)S(1)}) fusion(f16[256,1024]{1,0:T(8,128)(2,1)} %collective-permute-done.1, f32[2048,1024]{1,0:T(8,128)} %fusion, f32[1,2048,1024]{2,1,0:T(8,128)} %param.4), kind=kLoop, calls=%fused_computation.56 | loop fusion | flops 1835008 | bytes 4194304 | tf_op jit(solution)/shard_map/convert_element_type | solution.py:97
  37.2 4.0 %collective-permute-start.6 = (f16[256,1024]{1,0:T(8,128)(2,1)S(1)}, f16[256,1024]{1,0:T(8,128)(2,1)S(1)}, u32[]{:S(2)}, u32[]{:S(2)}) collective-permute-start(f16[256,1024]{1,0:T(8,128)(2,1)S(1)} %get-tuple-element.69), channel_id=1, source_target_pairs={{0,2},{2,0},{4,6},{6,4},{8,10},{10,8},{12,14},{14,12},{16,18},{18,... | collective-permute-start | bytes 1572872 | tf_op jit(solution)/shard_map/ppermute | solution.py:28
  41.3 1.1 slice.117
  42.4 0.1 collective-permute-start.5
  42.5 0.0 slice-start.1
  42.5 1.1 broadcast_in_dim.10
  43.6 2.4 %add_dynamic-update-slice_fusion.5 = f32[2048,1024]{1,0:T(8,128)S(1)} fusion(f32[2048,1024]{1,0:T(8,128)S(1)} %broadcast_in_dim.10, f16[256,1024]{1,0:T(8,128)(2,1)} %collective-permute-done.4, f32[256,1024]{1,0:T(8,128)S(1)} %get-tuple-element.63, f16[256,1024]{1,0:T(8,128)(2,1)S(1)} %collective-permute-done.3, f32[]{:T(128)S(6)} %div.37, f32[]{:T(128)} %bitcast.12, ...), kind=kLoop, calls=%fused_computation.55 | loop fusion | flops 1835008 | bytes 3145740 | tf_op jit(solution)/shard_map/dynamic_update_slice | solution.py:86
  46.0 0.3 multiply_convert_fusion.6
  46.3 1.9 %collective-permute-start.10 = (f16[256,1024]{1,0:T(8,128)(2,1)S(1)}, f16[256,1024]{1,0:T(8,128)(2,1)S(1)}, u32[]{:S(2)}, u32[]{:S(2)}) collective-permute-start(f16[256,1024]{1,0:T(8,128)(2,1)S(1)} %get-tuple-element.76), channel_id=1, source_target_pairs={{2,4},{4,2},{6,8},{8,6},{10,12},{12,10},{14,16},{16,14},{18,20},{2... | collective-permute-start | bytes 1572872 | tf_op jit(solution)/shard_map/ppermute | solution.py:28
  48.3 2.6 %collective-permute-start.9 = (f16[256,1024]{1,0:T(8,128)(2,1)S(1)}, f16[256,1024]{1,0:T(8,128)(2,1)S(1)}, u32[]{:S(2)}, u32[]{:S(2)}) collective-permute-start(f16[256,1024]{1,0:T(8,128)(2,1)S(1)} %get-tuple-element.76), channel_id=1, source_target_pairs={{0,2},{2,0},{4,6},{6,4},{8,10},{10,8},{12,14},{14,12},{16,18},{18,... | collective-permute-start | bytes 1572872 | tf_op jit(solution)/shard_map/ppermute | solution.py:28
  50.9 6.6 %collective-permute-done.7 = f16[256,1024]{1,0:T(8,128)(2,1)S(1)} collective-permute-done((f16[256,1024]{1,0:T(8,128)(2,1)S(1)}, f16[256,1024]{1,0:T(8,128)(2,1)S(1)}, u32[]{:S(2)}, u32[]{:S(2)}) %collective-permute-start.7) | collective-permute-done | bytes 524320 | tf_op jit(solution)/shard_map/ppermute | solution.py:28
  57.5 0.8 add_dynamic-update-slice_fusion.4
  58.4 0.1 slice.121
  58.5 1.3 %collective-permute-start.8 = (f16[256,1024]{1,0:T(8,128)(2,1)S(1)}, f16[256,1024]{1,0:T(8,128)(2,1)S(1)}, u32[]{:S(2)}, u32[]{:S(2)}) collective-permute-start(f16[256,1024]{1,0:T(8,128)(2,1)S(1)} %slice.121), channel_id=1, source_target_pairs={{0,1},{1,0},{2,3},{3,2},{4,5},{5,4},{6,7},{7,6},{8,9},{9,8},{10,11... | collective-permute-start | bytes 1572872 | tf_op jit(solution)/shard_map/ppermute | solution.py:19
  59.8 0.3 multiply_convert_fusion.5
  60.1 0.9 collective-permute-start.12
  61.0 2.0 %collective-permute-start.13 = (f16[256,1024]{1,0:T(8,128)(2,1)S(1)}, f16[256,1024]{1,0:T(8,128)(2,1)S(1)}, u32[]{:S(2)}, u32[]{:S(2)}) collective-permute-start(f16[256,1024]{1,0:T(8,128)(2,1)S(1)} %get-tuple-element.83), channel_id=1, source_target_pairs={{2,4},{4,2},{6,8},{8,6},{10,12},{12,10},{14,16},{16,14},{18,20},{2... | collective-permute-start | bytes 1572872 | tf_op jit(solution)/shard_map/ppermute | solution.py:28
  63.0 0.1 slice.125
  63.1 3.9 %collective-permute-done.10 = f16[256,1024]{1,0:T(8,128)(2,1)S(1)} collective-permute-done((f16[256,1024]{1,0:T(8,128)(2,1)S(1)}, f16[256,1024]{1,0:T(8,128)(2,1)S(1)}, u32[]{:S(2)}, u32[]{:S(2)}) %collective-permute-start.10) | collective-permute-done | bytes 524320 | tf_op jit(solution)/shard_map/ppermute | solution.py:28
  67.0 0.8 add_dynamic-update-slice_fusion.3
  67.9 3.6 %collective-permute-done.8 = f16[256,1024]{1,0:T(8,128)(2,1)S(1)} collective-permute-done((f16[256,1024]{1,0:T(8,128)(2,1)S(1)}, f16[256,1024]{1,0:T(8,128)(2,1)S(1)}, u32[]{:S(2)}, u32[]{:S(2)}) %collective-permute-start.8) | collective-permute-done | bytes 524320 | tf_op jit(solution)/shard_map/ppermute | solution.py:19
  71.4 0.3 multiply_convert_fusion.4
  71.7 2.6 %collective-permute-start.16 = (f16[256,1024]{1,0:T(8,128)(2,1)S(1)}, f16[256,1024]{1,0:T(8,128)(2,1)S(1)}, u32[]{:S(2)}, u32[]{:S(2)}) collective-permute-start(f16[256,1024]{1,0:T(8,128)(2,1)S(1)} %get-tuple-element.90), channel_id=1, source_target_pairs={{0,2},{2,0},{4,6},{6,4},{8,10},{10,8},{12,14},{14,12},{16,18},{18,... | collective-permute-start | bytes 1572872 | tf_op jit(solution)/shard_map/ppermute | solution.py:28
  74.3 2.0 %collective-permute-start.17 = (f16[256,1024]{1,0:T(8,128)(2,1)S(1)}, f16[256,1024]{1,0:T(8,128)(2,1)S(1)}, u32[]{:S(2)}, u32[]{:S(2)}) collective-permute-start(f16[256,1024]{1,0:T(8,128)(2,1)S(1)} %get-tuple-element.90), channel_id=1, source_target_pairs={{2,4},{4,2},{6,8},{8,6},{10,12},{12,10},{14,16},{16,14},{18,20},{2... | collective-permute-start | bytes 1572872 | tf_op jit(solution)/shard_map/ppermute | solution.py:28
  76.3 1.9 %collective-permute-done.13 = f16[256,1024]{1,0:T(8,128)(2,1)S(1)} collective-permute-done((f16[256,1024]{1,0:T(8,128)(2,1)S(1)}, f16[256,1024]{1,0:T(8,128)(2,1)S(1)}, u32[]{:S(2)}, u32[]{:S(2)}) %collective-permute-start.13) | collective-permute-done | bytes 524320 | tf_op jit(solution)/shard_map/ppermute | solution.py:28
  78.3 0.8 add_dynamic-update-slice_fusion.2
  79.1 3.6 %collective-permute-done.11 = f16[256,1024]{1,0:T(8,128)(2,1)S(1)} collective-permute-done((f16[256,1024]{1,0:T(8,128)(2,1)S(1)}, f16[256,1024]{1,0:T(8,128)(2,1)S(1)}, u32[]{:S(2)}, u32[]{:S(2)}) %collective-permute-start.11) | collective-permute-done | bytes 524320 | tf_op jit(solution)/shard_map/ppermute | solution.py:19
  82.7 0.1 slice.130
  82.8 1.3 %collective-permute-start.15 = (f16[256,1024]{1,0:T(8,128)(2,1)S(1)}, f16[256,1024]{1,0:T(8,128)(2,1)S(1)}, u32[]{:S(2)}, u32[]{:S(2)}) collective-permute-start(f16[256,1024]{1,0:T(8,128)(2,1)S(1)} %slice.130), channel_id=1, source_target_pairs={{0,1},{1,0},{2,3},{3,2},{4,5},{5,4},{6,7},{7,6},{8,9},{9,8},{10,11... | collective-permute-start | bytes 1572872 | tf_op jit(solution)/shard_map/ppermute | solution.py:19
  84.1 0.3 multiply_convert_fusion.3
  84.4 1.8 %collective-permute-start.18 = (f16[256,1024]{1,0:T(8,128)(2,1)S(1)}, f16[256,1024]{1,0:T(8,128)(2,1)S(1)}, u32[]{:S(2)}, u32[]{:S(2)}) collective-permute-start(f16[256,1024]{1,0:T(8,128)(2,1)S(1)} %get-tuple-element.95), channel_id=1, source_target_pairs={{0,2},{2,0},{4,6},{6,4},{8,10},{10,8},{12,14},{14,12},{16,18},{18,... | collective-permute-start | bytes 1572872 | tf_op jit(solution)/shard_map/ppermute | solution.py:28
  86.2 1.4 %collective-permute-start.19 = (f16[256,1024]{1,0:T(8,128)(2,1)S(1)}, f16[256,1024]{1,0:T(8,128)(2,1)S(1)}, u32[]{:S(2)}, u32[]{:S(2)}) collective-permute-start(f16[256,1024]{1,0:T(8,128)(2,1)S(1)} %get-tuple-element.95), channel_id=1, source_target_pairs={{2,4},{4,2},{6,8},{8,6},{10,12},{12,10},{14,16},{16,14},{18,20},{2... | collective-permute-start | bytes 1572872 | tf_op jit(solution)/shard_map/ppermute | solution.py:28
  87.6 0.1 slice.126
  87.7 0.1 collective-permute-start.14
  87.8 1.7 %collective-permute-done.17 = f16[256,1024]{1,0:T(8,128)(2,1)S(1)} collective-permute-done((f16[256,1024]{1,0:T(8,128)(2,1)S(1)}, f16[256,1024]{1,0:T(8,128)(2,1)S(1)}, u32[]{:S(2)}, u32[]{:S(2)}) %collective-permute-start.17) | collective-permute-done | bytes 524320 | tf_op jit(solution)/shard_map/ppermute | solution.py:28
  89.5 0.8 add_dynamic-update-slice_fusion.1
  90.3 4.5 %collective-permute-done.15 = f16[256,1024]{1,0:T(8,128)(2,1)S(1)} collective-permute-done((f16[256,1024]{1,0:T(8,128)(2,1)S(1)}, f16[256,1024]{1,0:T(8,128)(2,1)S(1)}, u32[]{:S(2)}, u32[]{:S(2)}) %collective-permute-start.15) | collective-permute-done | bytes 524320 | tf_op jit(solution)/shard_map/ppermute | solution.py:19
  94.8 0.3 multiply_convert_fusion.2
  95.1 4.4 %collective-permute-start.20 = (f16[256,1024]{1,0:T(8,128)(2,1)S(1)}, f16[256,1024]{1,0:T(8,128)(2,1)S(1)}, u32[]{:S(2)}, u32[]{:S(2)}) collective-permute-start(f16[256,1024]{1,0:T(8,128)(2,1)S(1)} %get-tuple-element.98), channel_id=1, source_target_pairs={{0,2},{2,0},{4,6},{6,4},{8,10},{10,8},{12,14},{14,12},{16,18},{18,... | collective-permute-start | bytes 1572872 | tf_op jit(solution)/shard_map/ppermute | solution.py:28
  99.5 1.1 collective-permute-start.21
  100.7 0.0 collective-permute-done.19
  100.7 0.8 add_dynamic-update-slice_fusion
  101.6 4.5 %collective-permute-done.14 = f16[256,1024]{1,0:T(8,128)(2,1)S(1)} collective-permute-done((f16[256,1024]{1,0:T(8,128)(2,1)S(1)}, f16[256,1024]{1,0:T(8,128)(2,1)S(1)}, u32[]{:S(2)}, u32[]{:S(2)}) %collective-permute-start.14) | collective-permute-done | bytes 524320 | tf_op jit(solution)/shard_map/ppermute | solution.py:19
  106.0 0.3 multiply_convert_fusion.1
  106.4 2.4 %collective-permute-start.22 = (f16[256,1024]{1,0:T(8,128)(2,1)S(1)}, f16[256,1024]{1,0:T(8,128)(2,1)S(1)}, u32[]{:S(2)}, u32[]{:S(2)}) collective-permute-start(f16[256,1024]{1,0:T(8,128)(2,1)S(1)} %get-tuple-element.101), channel_id=1, source_target_pairs={{0,2},{2,0},{4,6},{6,4},{8,10},{10,8},{12,14},{14,12},{16,18},{18,... | collective-permute-start | bytes 1572872 | tf_op jit(solution)/shard_map/ppermute | solution.py:28
  108.8 0.5 collective-permute-start.23
  109.3 4.5 %collective-permute-done.21 = f16[256,1024]{1,0:T(8,128)(2,1)S(1)} collective-permute-done((f16[256,1024]{1,0:T(8,128)(2,1)S(1)}, f16[256,1024]{1,0:T(8,128)(2,1)S(1)}, u32[]{:S(2)}, u32[]{:S(2)}) %collective-permute-start.21) | collective-permute-done | bytes 524320 | tf_op jit(solution)/shard_map/ppermute | solution.py:28
  113.8 0.8 bitcast_dynamic-update-slice_fusion.1
  114.6 10.4 %collective-permute-done.23 = f16[256,1024]{1,0:T(8,128)(2,1)S(1)} collective-permute-done((f16[256,1024]{1,0:T(8,128)(2,1)S(1)}, f16[256,1024]{1,0:T(8,128)(2,1)S(1)}, u32[]{:S(2)}, u32[]{:S(2)}) %collective-permute-start.23) | collective-permute-done | bytes 524320 | tf_op jit(solution)/shard_map/ppermute | solution.py:28
  125.0 1.9 %bitcast_dynamic-update-slice_fusion = f32[1,2048,1024]{2,1,0:T(8,128)} fusion(f32[1,2048,1024]{2,1,0:T(8,128)} %copy-done.1, f16[256,1024]{1,0:T(8,128)(2,1)S(1)} %collective-permute-done.23, f32[256,1024]{1,0:T(8,128)S(1)} %get-tuple-element.102, f16[256,1024]{1,0:T(8,128)(2,1)S(1)} %collective-permute-done.22, f32[]{:T(128)S(6)} %div.37, f32[]{:T(128)} %bitcast.12, ...), kind=kLoop, calls=%fused_computation.42 | loop fusion | flops 1835008 | bytes 3146248 | tf_op jit(solution)/shard_map/dynamic_update_slice | solution.py:86
  (28 shorter events, 0.1 us)
Async XLA Ops:
  0.0 1.5 %copy-start = (bf16[1,896,1024]{2,1,0:T(8,128)(2,1)S(1)}, bf16[1,896,1024]{2,1,0:T(8,128)(2,1)}, u32[]{:S(2)}) copy-start(bf16[1,896,1024]{2,1,0:T(8,128)(2,1)} %param.6) | copy-start | bytes 5505028
  3.3 20.3 %collective-permute-start = (f16[256,1024]{1,0:T(8,128)(2,1)S(1)}, f16[256,1024]{1,0:T(8,128)(2,1)S(1)}, u32[]{:S(2)}, u32[]{:S(2)}) collective-permute-start(f16[256,1024]{1,0:T(8,128)(2,1)S(1)} %fusion.20), channel_id=1, source_target_pairs={{0,1},{1,0},{2,3},{3,2},{4,5},{5,4},{6,7},{7,6},{8,9},{9,8},{10,11... | collective-permute-start | bytes 1572872 | tf_op jit(solution)/shard_map/ppermute | solution.py:19
  7.9 24.2 %collective-permute-start.1 = (f16[256,1024]{1,0:T(8,128)(2,1)}, f16[256,1024]{1,0:T(8,128)(2,1)}, u32[]{:S(2)}, u32[]{:S(2)}) collective-permute-start(f16[256,1024]{1,0:T(8,128)(2,1)} %fusion.17), channel_id=1, source_target_pairs={{0,1},{1,0},{2,3},{3,2},{4,5},{5,4},{6,7},{7,6},{8,9},{9,8},{10,11... | collective-permute-start | bytes 1572872 | tf_op jit(solution)/shard_map/ppermute | solution.py:19
  16.8 11.9 %copy-start.4 = (s32[16,3]{0,1:T(4,128)S(1)}, s32[16,3]{0,1:T(4,128)}, u32[]{:S(2)}) copy-start(s32[16,3]{0,1:T(4,128)} %param.7) | copy-start | bytes 580
  26.2 16.2 %collective-permute-start.3 = (f16[256,1024]{1,0:T(8,128)(2,1)}, f16[256,1024]{1,0:T(8,128)(2,1)S(1)}, u32[]{:S(2)}, u32[]{:S(2)}) collective-permute-start(f16[256,1024]{1,0:T(8,128)(2,1)} %get-tuple-element.62), channel_id=1, source_target_pairs={{0,2},{2,0},{4,6},{6,4},{8,10},{10,8},{12,14},{14,12},{16,18},{18,... | collective-permute-start | bytes 1572872 | tf_op jit(solution)/shard_map/ppermute | solution.py:28
  27.1 15.4 %collective-permute-start.4 = (f16[256,1024]{1,0:T(8,128)(2,1)}, f16[256,1024]{1,0:T(8,128)(2,1)}, u32[]{:S(2)}, u32[]{:S(2)}) collective-permute-start(f16[256,1024]{1,0:T(8,128)(2,1)} %get-tuple-element.62), channel_id=1, source_target_pairs={{2,4},{4,2},{6,8},{8,6},{10,12},{12,10},{14,16},{16,14},{18,20},{2... | collective-permute-start | bytes 1572872 | tf_op jit(solution)/shard_map/ppermute | solution.py:28
  33.3 12.7 %slice-start = ((s8[8388608]{0:T(1024)(128)(4,1)}), s8[4194304]{0:T(1024)(128)(4,1)S(1)}, s32[]{:S(2)}) async-start(s8[8388608]{0:T(1024)(128)(4,1)} %bitcast.69), calls=%async_computation | async-start | bytes 8388608
  33.3 12.7 %copy-start.2 = (f32[2048,1024]{1,0:T(8,128)S(1)}, f32[2048,1024]{1,0:T(8,128)}, u32[]{:S(2)}) copy-start(f32[2048,1024]{1,0:T(8,128)} %fusion) | copy-start | bytes 25165828
  33.3 12.7 %collective-permute-start.2 = (f16[256,1024]{1,0:T(8,128)(2,1)S(1)}, f16[256,1024]{1,0:T(8,128)(2,1)S(1)}, u32[]{:S(2)}, u32[]{:S(2)}) collective-permute-start(f16[256,1024]{1,0:T(8,128)(2,1)S(1)} %slice.110), channel_id=1, source_target_pairs={{0,1},{1,0},{2,3},{3,2},{4,5},{5,4},{6,7},{7,6},{8,9},{9,8},{10,11... | collective-permute-start | bytes 1572872 | tf_op jit(solution)/shard_map/ppermute | solution.py:19
  37.2 13.7 %collective-permute-start.6 = (f16[256,1024]{1,0:T(8,128)(2,1)S(1)}, f16[256,1024]{1,0:T(8,128)(2,1)S(1)}, u32[]{:S(2)}, u32[]{:S(2)}) collective-permute-start(f16[256,1024]{1,0:T(8,128)(2,1)S(1)} %get-tuple-element.69), channel_id=1, source_target_pairs={{0,2},{2,0},{4,6},{6,4},{8,10},{10,8},{12,14},{14,12},{16,18},{18,... | collective-permute-start | bytes 1572872 | tf_op jit(solution)/shard_map/ppermute | solution.py:28
  41.3 16.3 %collective-permute-start.7 = (f16[256,1024]{1,0:T(8,128)(2,1)S(1)}, f16[256,1024]{1,0:T(8,128)(2,1)S(1)}, u32[]{:S(2)}, u32[]{:S(2)}) collective-permute-start(f16[256,1024]{1,0:T(8,128)(2,1)S(1)} %get-tuple-element.69), channel_id=1, source_target_pairs={{2,4},{4,2},{6,8},{8,6},{10,12},{12,10},{14,16},{16,14},{18,20},{2... | collective-permute-start | bytes 1572872 | tf_op jit(solution)/shard_map/ppermute | solution.py:28
  42.4 16.0 %collective-permute-start.5 = (f16[256,1024]{1,0:T(8,128)(2,1)S(1)}, f16[256,1024]{1,0:T(8,128)(2,1)S(1)}, u32[]{:S(2)}, u32[]{:S(2)}) collective-permute-start(f16[256,1024]{1,0:T(8,128)(2,1)S(1)} %slice.117), channel_id=1, source_target_pairs={{0,1},{1,0},{2,3},{3,2},{4,5},{5,4},{6,7},{7,6},{8,9},{9,8},{10,11... | collective-permute-start | bytes 1572872 | tf_op jit(solution)/shard_map/ppermute | solution.py:19
  42.5 3.5 %slice-start.1 = ((s8[8388608]{0:T(1024)(128)(4,1)}), s8[4194304]{0:T(1024)(128)(4,1)S(1)}, s32[]{:S(2)}) async-start(s8[8388608]{0:T(1024)(128)(4,1)} %bitcast.69), calls=%async_computation.1 | async-start | bytes 8388608
  42.5 15.9 %copy-start.3 = (f16[1536,1024]{1,0:T(8,128)(2,1)S(1)}, f16[1536,1024]{1,0:T(8,128)(2,1)}, u32[]{:S(2)}) copy-start(f16[1536,1024]{1,0:T(8,128)(2,1)} %multiply_convert_fusion) | copy-start | bytes 9437188
  46.3 20.7 %collective-permute-start.10 = (f16[256,1024]{1,0:T(8,128)(2,1)S(1)}, f16[256,1024]{1,0:T(8,128)(2,1)S(1)}, u32[]{:S(2)}, u32[]{:S(2)}) collective-permute-start(f16[256,1024]{1,0:T(8,128)(2,1)S(1)} %get-tuple-element.76), channel_id=1, source_target_pairs={{2,4},{4,2},{6,8},{8,6},{10,12},{12,10},{14,16},{16,14},{18,20},{2... | collective-permute-start | bytes 1572872 | tf_op jit(solution)/shard_map/ppermute | solution.py:28
  48.3 18.7 %collective-permute-start.9 = (f16[256,1024]{1,0:T(8,128)(2,1)S(1)}, f16[256,1024]{1,0:T(8,128)(2,1)S(1)}, u32[]{:S(2)}, u32[]{:S(2)}) collective-permute-start(f16[256,1024]{1,0:T(8,128)(2,1)S(1)} %get-tuple-element.76), channel_id=1, source_target_pairs={{0,2},{2,0},{4,6},{6,4},{8,10},{10,8},{12,14},{14,12},{16,18},{18,... | collective-permute-start | bytes 1572872 | tf_op jit(solution)/shard_map/ppermute | solution.py:28
  58.5 13.0 %collective-permute-start.8 = (f16[256,1024]{1,0:T(8,128)(2,1)S(1)}, f16[256,1024]{1,0:T(8,128)(2,1)S(1)}, u32[]{:S(2)}, u32[]{:S(2)}) collective-permute-start(f16[256,1024]{1,0:T(8,128)(2,1)S(1)} %slice.121), channel_id=1, source_target_pairs={{0,1},{1,0},{2,3},{3,2},{4,5},{5,4},{6,7},{7,6},{8,9},{9,8},{10,11... | collective-permute-start | bytes 1572872 | tf_op jit(solution)/shard_map/ppermute | solution.py:19
  60.1 16.3 %collective-permute-start.12 = (f16[256,1024]{1,0:T(8,128)(2,1)S(1)}, f16[256,1024]{1,0:T(8,128)(2,1)S(1)}, u32[]{:S(2)}, u32[]{:S(2)}) collective-permute-start(f16[256,1024]{1,0:T(8,128)(2,1)S(1)} %get-tuple-element.83), channel_id=1, source_target_pairs={{0,2},{2,0},{4,6},{6,4},{8,10},{10,8},{12,14},{14,12},{16,18},{18,... | collective-permute-start | bytes 1572872 | tf_op jit(solution)/shard_map/ppermute | solution.py:28
  61.0 17.2 %collective-permute-start.13 = (f16[256,1024]{1,0:T(8,128)(2,1)S(1)}, f16[256,1024]{1,0:T(8,128)(2,1)S(1)}, u32[]{:S(2)}, u32[]{:S(2)}) collective-permute-start(f16[256,1024]{1,0:T(8,128)(2,1)S(1)} %get-tuple-element.83), channel_id=1, source_target_pairs={{2,4},{4,2},{6,8},{8,6},{10,12},{12,10},{14,16},{16,14},{18,20},{2... | collective-permute-start | bytes 1572872 | tf_op jit(solution)/shard_map/ppermute | solution.py:28
  67.0 15.7 %collective-permute-start.11 = (f16[256,1024]{1,0:T(8,128)(2,1)S(1)}, f16[256,1024]{1,0:T(8,128)(2,1)S(1)}, u32[]{:S(2)}, u32[]{:S(2)}) collective-permute-start(f16[256,1024]{1,0:T(8,128)(2,1)S(1)} %slice.125), channel_id=1, source_target_pairs={{0,1},{1,0},{2,3},{3,2},{4,5},{5,4},{6,7},{7,6},{8,9},{9,8},{10,11... | collective-permute-start | bytes 1572872 | tf_op jit(solution)/shard_map/ppermute | solution.py:19
  71.7 15.9 %collective-permute-start.16 = (f16[256,1024]{1,0:T(8,128)(2,1)S(1)}, f16[256,1024]{1,0:T(8,128)(2,1)S(1)}, u32[]{:S(2)}, u32[]{:S(2)}) collective-permute-start(f16[256,1024]{1,0:T(8,128)(2,1)S(1)} %get-tuple-element.90), channel_id=1, source_target_pairs={{0,2},{2,0},{4,6},{6,4},{8,10},{10,8},{12,14},{14,12},{16,18},{18,... | collective-permute-start | bytes 1572872 | tf_op jit(solution)/shard_map/ppermute | solution.py:28
  74.3 15.2 %collective-permute-start.17 = (f16[256,1024]{1,0:T(8,128)(2,1)S(1)}, f16[256,1024]{1,0:T(8,128)(2,1)S(1)}, u32[]{:S(2)}, u32[]{:S(2)}) collective-permute-start(f16[256,1024]{1,0:T(8,128)(2,1)S(1)} %get-tuple-element.90), channel_id=1, source_target_pairs={{2,4},{4,2},{6,8},{8,6},{10,12},{12,10},{14,16},{16,14},{18,20},{2... | collective-permute-start | bytes 1572872 | tf_op jit(solution)/shard_map/ppermute | solution.py:28
  82.8 12.0 %collective-permute-start.15 = (f16[256,1024]{1,0:T(8,128)(2,1)S(1)}, f16[256,1024]{1,0:T(8,128)(2,1)S(1)}, u32[]{:S(2)}, u32[]{:S(2)}) collective-permute-start(f16[256,1024]{1,0:T(8,128)(2,1)S(1)} %slice.130), channel_id=1, source_target_pairs={{0,1},{1,0},{2,3},{3,2},{4,5},{5,4},{6,7},{7,6},{8,9},{9,8},{10,11... | collective-permute-start | bytes 1572872 | tf_op jit(solution)/shard_map/ppermute | solution.py:19
  84.4 16.3 %collective-permute-start.18 = (f16[256,1024]{1,0:T(8,128)(2,1)S(1)}, f16[256,1024]{1,0:T(8,128)(2,1)S(1)}, u32[]{:S(2)}, u32[]{:S(2)}) collective-permute-start(f16[256,1024]{1,0:T(8,128)(2,1)S(1)} %get-tuple-element.95), channel_id=1, source_target_pairs={{0,2},{2,0},{4,6},{6,4},{8,10},{10,8},{12,14},{14,12},{16,18},{18,... | collective-permute-start | bytes 1572872 | tf_op jit(solution)/shard_map/ppermute | solution.py:28
  86.2 14.5 %collective-permute-start.19 = (f16[256,1024]{1,0:T(8,128)(2,1)S(1)}, f16[256,1024]{1,0:T(8,128)(2,1)S(1)}, u32[]{:S(2)}, u32[]{:S(2)}) collective-permute-start(f16[256,1024]{1,0:T(8,128)(2,1)S(1)} %get-tuple-element.95), channel_id=1, source_target_pairs={{2,4},{4,2},{6,8},{8,6},{10,12},{12,10},{14,16},{16,14},{18,20},{2... | collective-permute-start | bytes 1572872 | tf_op jit(solution)/shard_map/ppermute | solution.py:28
  87.7 18.4 %collective-permute-start.14 = (f16[256,1024]{1,0:T(8,128)(2,1)S(1)}, f16[256,1024]{1,0:T(8,128)(2,1)S(1)}, u32[]{:S(2)}, u32[]{:S(2)}) collective-permute-start(f16[256,1024]{1,0:T(8,128)(2,1)S(1)} %slice.126), channel_id=1, source_target_pairs={{0,1},{1,0},{2,3},{3,2},{4,5},{5,4},{6,7},{7,6},{8,9},{9,8},{10,11... | collective-permute-start | bytes 1572872 | tf_op jit(solution)/shard_map/ppermute | solution.py:19
  95.1 14.2 %collective-permute-start.20 = (f16[256,1024]{1,0:T(8,128)(2,1)S(1)}, f16[256,1024]{1,0:T(8,128)(2,1)S(1)}, u32[]{:S(2)}, u32[]{:S(2)}) collective-permute-start(f16[256,1024]{1,0:T(8,128)(2,1)S(1)} %get-tuple-element.98), channel_id=1, source_target_pairs={{0,2},{2,0},{4,6},{6,4},{8,10},{10,8},{12,14},{14,12},{16,18},{18,... | collective-permute-start | bytes 1572872 | tf_op jit(solution)/shard_map/ppermute | solution.py:28
  99.5 14.2 %collective-permute-start.21 = (f16[256,1024]{1,0:T(8,128)(2,1)S(1)}, f16[256,1024]{1,0:T(8,128)(2,1)S(1)}, u32[]{:S(2)}, u32[]{:S(2)}) collective-permute-start(f16[256,1024]{1,0:T(8,128)(2,1)S(1)} %get-tuple-element.98), channel_id=1, source_target_pairs={{2,4},{4,2},{6,8},{8,6},{10,12},{12,10},{14,16},{16,14},{18,20},{2... | collective-permute-start | bytes 1572872 | tf_op jit(solution)/shard_map/ppermute | solution.py:28
  106.4 8.3 %collective-permute-start.22 = (f16[256,1024]{1,0:T(8,128)(2,1)S(1)}, f16[256,1024]{1,0:T(8,128)(2,1)S(1)}, u32[]{:S(2)}, u32[]{:S(2)}) collective-permute-start(f16[256,1024]{1,0:T(8,128)(2,1)S(1)} %get-tuple-element.101), channel_id=1, source_target_pairs={{0,2},{2,0},{4,6},{6,4},{8,10},{10,8},{12,14},{14,12},{16,18},{18,... | collective-permute-start | bytes 1572872 | tf_op jit(solution)/shard_map/ppermute | solution.py:28
  108.8 16.2 %collective-permute-start.23 = (f16[256,1024]{1,0:T(8,128)(2,1)S(1)}, f16[256,1024]{1,0:T(8,128)(2,1)S(1)}, u32[]{:S(2)}, u32[]{:S(2)}) collective-permute-start(f16[256,1024]{1,0:T(8,128)(2,1)S(1)} %get-tuple-element.101), channel_id=1, source_target_pairs={{2,4},{4,2},{6,8},{8,6},{10,12},{12,10},{14,16},{16,14},{18,20},{2... | collective-permute-start | bytes 1572872 | tf_op jit(solution)/shard_map/ppermute | solution.py:28
  114.6 10.4 %copy-start.1 = (f32[1,2048,1024]{2,1,0:T(8,128)}, f32[1,2048,1024]{2,1,0:T(8,128)S(1)}, u32[]{:S(2)}) copy-start(f32[1,2048,1024]{2,1,0:T(8,128)S(1)} %bitcast_dynamic-update-slice_fusion.1) | copy-start | bytes 25165828

commit v3 on v2

--- a/solution.py
+++ b/solution.py
@@ -56,7 +56,7 @@
             block, cot_local, (((0,), (0,)), ((), ())), preferred_element_type=jnp.float32
         )
 
-    def for_others(first, count):
+    def for_others(shard, first, count):
         return [
             (partial(lax.rem(shard + away, shards), first, count) * (RATE * scale)).astype(WIRE)
             for away in range(1, shards)
@@ -68,41 +68,55 @@
     def rows_of(value, chunk):
         return value[chunk * step:(chunk + 1) * step]
 
-    terms = {chunk: for_others(chunk * step, step) for chunk in range(AHEAD)}
-    arrived = {chunk: send_terms(terms[chunk]) for chunk in range(AHEAD)}
-    gradient = partial(shard, 0, rows)
-    rest = for_others(AHEAD * step, rows - AHEAD * step)
+    arrived = {}
+    for chunk in range(AHEAD):
+        arrived[chunk] = send_terms(for_others(shard, chunk * step, step))
+    first = AHEAD * step
+    gradient = {"first": partial(shard, 0, first)}
+    rest = for_others(shard, first, rows - first)
+    terms = {
+        chunk: [rows_of(term, chunk - AHEAD) for term in rest] for chunk in range(AHEAD, CHUNKS)
+    }
     mine = {}
     near = {}
     far = {}
+
+    arrived[0], terms, gradient = lax.optimization_barrier((arrived[0], terms, gradient))
+    for chunk in range(CHUNKS):
+        if chunk == 1:
+            arrived[1], gradient["rest"] = lax.optimization_barrier((arrived[1], gradient["rest"]))
+        if chunk >= 1:
+            arrived[chunk], mine[chunk - 1] = lax.optimization_barrier((arrived[chunk], mine[chunk - 1]))
+        if chunk >= 2:
+            arrived[chunk], far[chunk - 2], near[chunk - 2] = lax.optimization_barrier(
+                (arrived[chunk], far[chunk - 2], near[chunk - 2])
+            )
+        if chunk < AHEAD:
+            total = RATE * rows_of(gradient["first"], chunk)
+        else:
+            total = RATE * rows_of(gradient["rest"], chunk - AHEAD)
+        for term in arrived[chunk]:
+            total = total + term.astype(jnp.float32) / scale
+        own = rows_of(weights, chunk) - total
+        mine[chunk], sent = lax.optimization_barrier((own, (own * scale).astype(WIRE)))
+        if chunk == 0:
+            later, sent = lax.optimization_barrier((shard, sent))
+            gradient["rest"] = partial(later, first, rows - first)
+        after = chunk + AHEAD
+        if after < CHUNKS:
+            terms[after], sent = lax.optimization_barrier((terms[after], sent))
+            arrived[after] = send_terms(terms[after])
+        far[chunk] = swapped(sent, "blk", 1)
+        near[chunk] = swapped(sent, "blk", 0)
+
     out = jnp.zeros_like(weights)
-
-    def finish(chunk, out):
+    for chunk in range(CHUNKS):
         mixed = (
             c_near * near[chunk].astype(jnp.float32)
             + c_self * mine[chunk]
             + c_far * far[chunk].astype(jnp.float32)
         )
-        return lax.dynamic_update_slice_in_dim(out, mixed, chunk * step, axis=0)
-
-    for chunk in range(CHUNKS):
-        if chunk >= 1:
-            arrived[chunk], mine[chunk - 1], out = lax.optimization_barrier(
-                (arrived[chunk], mine[chunk - 1], out)
-            )
-        total = RATE * rows_of(gradient, chunk)
-        for term in arrived[chunk]:
-            total = total + term.astype(jnp.float32) / scale
-        own = rows_of(weights, chunk) - total
-        mine[chunk], sent = lax.optimization_barrier((own, (own * scale).astype(WIRE)))
-        if chunk + AHEAD < CHUNKS:
-            rest, sent = lax.optimization_barrier((rest, sent))
-            arrived[chunk + AHEAD] = send_terms([rows_of(term, chunk) for term in rest])
-        far[chunk] = swapped(sent, "blk", 1)
-        near[chunk] = swapped(sent, "blk", 0)
-        if chunk >= 1:
-            out = finish(chunk - 1, out)
-    out = finish(CHUNKS - 1, out)
+        out = lax.dynamic_update_slice_in_dim(out, mixed, chunk * step, axis=0)
     return out[None]
 
 

time: 127 us -> 132 us (1.039)
  other arithmetic: 16.4 us -> 21.7 us
  starting transfers between devices: 36.5 us -> 33.5 us
  local copies, waits for them, and re-layouts: 5.89 us -> 8.54 us
    ppermute x16, waiting for transfers between devices: 29 us -> 13 us  [swapped(): return lax.ppermute(value, axis, pairs)]
    ppermute x8, waiting for transfers between devices: 16.1 us -> 31.2 us  [from_behind(): return lax.ppermute(value, axis, pairs)]
    convert_element_type x8, other arithmetic: 7.06 us -> 10.9 us  [on_device(): (own * scale).astype(WIRE)]
    add x0 -> x1, other arithmetic: none -> 2.55 us  [on_device(): c_near * near[chunk].astype(jnp.float32) + c_self * mine[chunk]]
    ppermute x16, starting transfers between devices: 30.3 us -> 27.8 us  [swapped(): return lax.ppermute(value, axis, pairs)]
    unnamed x14 -> x28, local copies, waits for them, and re-layouts: 1.54 us -> 3.02 us
    slice x6 -> x1, local copies, waits for them, and re-layouts: 2.62 us -> 3.78 us  [rows_of(): return value[chunk * step:(chunk + 1) * step]]
    dynamic_update_slice x8 -> x7, other arithmetic: 9.34 us -> 8.2 us  [on_device(): out = lax.dynamic_update_slice_in_dim(out, mixed, chunk * step, axis=0)]
  transfers between devices with their start and end apart: 24 -> 24, of which waited for: 10 -> 9; matrix products, arithmetic and copies ran while one was open for 29% -> 34% of each run, Pallas kernels for 0% -> 0%
where the time goes in v3:
time: 132 us
  waiting for transfers between devices  44.2 us (33%)
  starting transfers between devices  33.5 us (25%)
  other arithmetic  21.7 us (16%)
  matrix products  20.8 us (16%)
  local copies, waits for them, and re-layouts  8.54 us (6%)
  between operations  3.04 us (2%)
    ppermute x8, waiting for transfers between devices, from_behind(): return lax.ppermute(value, axis, pairs)  31.2 us
    ppermute x16, starting transfers between devices, swapped(): return lax.ppermute(value, axis, pairs)  27.8 us
    dot_general x5, matrix products, partial(): lax.dot_general(block, cot_local, (((0,), (0,)), ((), ())), preferred_ele...  20.7 us
    ppermute x16, waiting for transfers between devices, swapped(): return lax.ppermute(value, axis, pairs)  13 us
    convert_element_type x8, other arithmetic, on_device(): (own * scale).astype(WIRE)  10.9 us
    dynamic_update_slice x7, other arithmetic, on_device(): out = lax.dynamic_update_slice_in_dim(out, mixed, chunk * step, axis=0)  8.2 us
    ppermute x8, starting transfers between devices, from_behind(): return lax.ppermute(value, axis, pairs)  5.61 us
    slice x1, local copies, waits for them, and re-layouts, rows_of(): return value[chunk * step:(chunk + 1) * step]  3.78 us
  transfers between devices with their start and end apart: 24, of which 9 were waited for; matrix products, arithmetic and copies ran while one was open for 34% of the time, Pallas kernels for 0%

profile of v3, /device:TPU:1, one launch (start us, length us, event | category | flops | bytes accessed | tf_op | source)
XLA Modules:
  0.0 131.7 jit_solution(7473929095116922471)
XLA Ops:
  0.0 1.5 %copy-done = bf16[1,896,1024]{2,1,0:T(8,128)(2,1)S(1)} copy-done((bf16[1,896,1024]{2,1,0:T(8,128)(2,1)S(1)}, bf16[1,896,1024]{2,1,0:T(8,128)(2,1)}, u32[]{:S(2)}) %copy-start) | copy-done | bytes 1835032
  1.5 1.7 %fusion.22 = f16[256,1024]{1,0:T(8,128)(2,1)S(1)} fusion(bf16[1,896,1024]{2,1,0:T(8,128)(2,1)S(1)} %copy-done, bf16[1,896,4096]{2,1,0:T(8,128)(2,1)} %param.5, s32[]{:T(128)S(6)} %select_n.31), kind=kOutput, calls=%fused_computation.18 | convolution fusion | flops 470286336 | bytes 2818052 | tf_op jit(solution)/shard_map/dot_general | solution.py:55
  3.3 2.1 %collective-permute-start = (f16[256,1024]{1,0:T(8,128)(2,1)S(1)}, f16[256,1024]{1,0:T(8,128)(2,1)S(1)}, u32[]{:S(2)}, u32[]{:S(2)}) collective-permute-start(f16[256,1024]{1,0:T(8,128)(2,1)S(1)} %fusion.22), channel_id=1, source_target_pairs={{0,1},{1,0},{2,3},{3,2},{4,5},{5,4},{6,7},{7,6},{8,9},{9,8},{10,11... | collective-permute-start | bytes 1572872 | tf_op jit(solution)/shard_map/ppermute | solution.py:19
  5.4 2.6 %fusion.19 = f16[256,1024]{1,0:T(8,128)(2,1)} fusion(bf16[1,896,1024]{2,1,0:T(8,128)(2,1)S(1)} %copy-done, bf16[1,896,4096]{2,1,0:T(8,128)(2,1)} %param.5, s32[]{:T(128)S(6)} %select_n.34), kind=kOutput, calls=%fused_computation.17 | convolution fusion | flops 470286336 | bytes 2818052 | tf_op jit(solution)/shard_map/dot_general | solution.py:55
  8.0 0.0 collective-permute-start.2
  8.0 6.6 %multiply_convert_fusion = f16[1536,1024]{1,0:T(8,128)(2,1)} fusion(bf16[1,896,4096]{2,1,0:T(8,128)(2,1)} %param.5, s32[]{:T(128)S(6)} %select_n.32, bf16[1,896,1024]{2,1,0:T(8,128)(2,1)S(1)} %copy-done), kind=kOutput, calls=%fused_computation.1 | convolution fusion | flops 2821718016 | bytes 7733252 | tf_op jit(solution)/shard_map/dot_general | solution.py:55
  14.6 3.8 %fusion.42 = (f16[256,1024]{1,0:T(8,128)(2,1)S(1)}, f16[256,1024]{1,0:T(8,128)(2,1)}, f16[256,1024]{1,0:T(8,128)(2,1)}, f16[256,1024]{1,0:T(8,128)(2,1)}, f16[256,1024]{1,0:T(8,128)(2,1)}, /*index=5*/f16[256,1024]{1,0:T(8,128)(2,1)}) fusion(f16[1536,1024]{1,0:T(8,128)(2,1)} %multiply_convert_fusion), kind=kLoop, calls=%fused_computation.61 | loop fusion | bytes 6291456 | tf_op jit(solution)/shard_map/slice | solution.py:69
  18.4 2.4 %fusion.8 = f32[512,1024]{1,0:T(8,128)S(1)} fusion(bf16[1,896,1024]{2,1,0:T(8,128)(2,1)S(1)} %copy-done, bf16[1,896,4096]{2,1,0:T(8,128)(2,1)} %param.5, s32[]{:T(128)S(6)} %select_n.33), kind=kOutput, calls=%fused_computation.10 | convolution fusion | flops 939524096 | bytes 4849668 | tf_op jit(solution)/shard_map/dot_general | solution.py:55
  20.9 0.0 collective-permute-done
  20.9 0.0 copy-start.10
  20.9 0.8 copy-done.10
  21.7 0.6 copy-done.3
  22.3 2.5 %multiply_convert_fusion.8 = (f16[256,1024]{1,0:T(8,128)(2,1)}, f32[256,1024]{1,0:T(8,128)S(1)}) fusion(f16[256,1024]{1,0:T(8,128)(2,1)} %copy-done.10, f32[512,1024]{1,0:T(8,128)S(1)} %fusion.8, f32[1,2048,1024]{2,1,0:T(8,128)} %param.4), kind=kLoop, calls=%fused_computation.44 | loop fusion | flops 1835008 | bytes 4194304 | tf_op jit(solution)/shard_map/convert_element_type | solution.py:101
  24.9 2.5 %collective-permute-start.3 = (f16[256,1024]{1,0:T(8,128)(2,1)}, f16[256,1024]{1,0:T(8,128)(2,1)}, u32[]{:S(2)}, u32[]{:S(2)}) collective-permute-start(f16[256,1024]{1,0:T(8,128)(2,1)} %get-tuple-element.89), channel_id=1, source_target_pairs={{2,4},{4,2},{6,8},{8,6},{10,12},{12,10},{14,16},{16,14},{18,20},{2... | collective-permute-start | bytes 1572872 | tf_op jit(solution)/shard_map/ppermute | solution.py:28
  27.4 2.3 %collective-permute-start.4 = (f16[256,1024]{1,0:T(8,128)(2,1)}, f16[256,1024]{1,0:T(8,128)(2,1)}, u32[]{:S(2)}, u32[]{:S(2)}) collective-permute-start(f16[256,1024]{1,0:T(8,128)(2,1)} %get-tuple-element.89), channel_id=1, source_target_pairs={{0,2},{2,0},{4,6},{6,4},{8,10},{10,8},{12,14},{14,12},{16,18},{18,... | collective-permute-start | bytes 1572872 | tf_op jit(solution)/shard_map/ppermute | solution.py:28
  29.7 1.2 collective-permute-start.1
  30.9 7.3 %fusion = f32[1536,1024]{1,0:T(8,128)} fusion(bf16[1,896,4096]{2,1,0:T(8,128)(2,1)} %param.5, s32[]{:T(128)S(6)} %select_n.35, bf16[1,896,1024]{2,1,0:T(8,128)(2,1)S(1)} %copy-done), kind=kOutput, calls=%fused_computation.2 | convolution fusion | flops 2818572288 | bytes 10878980 | tf_op jit(solution)/shard_map/dot_general | solution.py:55
  38.2 0.0 collective-permute-done.2
  38.2 2.9 %multiply_convert_fusion.7 = (f16[256,1024]{1,0:T(8,128)(2,1)}, f32[256,1024]{1,0:T(8,128)}) fusion(f16[256,1024]{1,0:T(8,128)(2,1)} %collective-permute-done.2, f32[512,1024]{1,0:T(8,128)S(1)} %copy-done.4, f32[1,2048,1024]{2,1,0:T(8,128)} %param.4), kind=kLoop, calls=%fused_computation.43 | loop fusion | flops 1835008 | bytes 4194304 | tf_op jit(solution)/shard_map/convert_element_type | solution.py:101
  41.1 1.2 collective-permute-start.7
  42.3 1.2 collective-permute-done.1
  43.6 1.2 collective-permute-start.5
  44.8 0.1 fusion.25
  44.9 0.7 fusion.43
  48.4 2.1 %multiply_convert_fusion.6 = (f16[256,1024]{1,0:T(8,128)(2,1)S(1)}, f32[256,1024]{1,0:T(8,128)S(1)}) fusion(f16[256,1024]{1,0:T(8,128)(2,1)} %collective-permute-done.1, f32[1536,1024]{1,0:T(8,128)} %fusion, f32[1,2048,1024]{2,1,0:T(8,128)} %param.4), kind=kLoop, calls=%fused_computation.41 | loop fusion | flops 1835008 | bytes 4194304 | tf_op jit(solution)/shard_map/convert_element_type | solution.py:101
  50.5 0.1 collective-permute-start.9
  50.6 1.2 collective-permute-start.10
  51.8 4.8 %collective-permute-done.5 = f16[256,1024]{1,0:T(8,128)(2,1)} collective-permute-done((f16[256,1024]{1,0:T(8,128)(2,1)}, f16[256,1024]{1,0:T(8,128)(2,1)}, u32[]{:S(2)}, u32[]{:S(2)}) %collective-permute-start.5) | collective-permute-done | bytes 524320 | tf_op jit(solution)/shard_map/ppermute | solution.py:19
  56.6 2.2 %collective-permute-done.6 = f16[256,1024]{1,0:T(8,128)(2,1)S(1)} collective-permute-done((f16[256,1024]{1,0:T(8,128)(2,1)}, f16[256,1024]{1,0:T(8,128)(2,1)S(1)}, u32[]{:S(2)}, u32[]{:S(2)}) %collective-permute-start.6) | collective-permute-done | bytes 524320 | tf_op jit(solution)/shard_map/ppermute | solution.py:28
  58.8 0.0 collective-permute-done.7
  58.8 2.3 %multiply_convert_fusion.5 = (f16[256,1024]{1,0:T(8,128)(2,1)S(1)}, f32[256,1024]{1,0:T(8,128)S(1)}) fusion(f16[256,1024]{1,0:T(8,128)(2,1)} %collective-permute-done.5, f32[1536,1024]{1,0:T(8,128)} %fusion, f32[1,2048,1024]{2,1,0:T(8,128)} %param.4), kind=kLoop, calls=%fused_computation.40 | loop fusion | flops 1835008 | bytes 4194304 | tf_op jit(solution)/shard_map/convert_element_type | solution.py:101
  61.1 2.4 %collective-permute-start.12 = (f16[256,1024]{1,0:T(8,128)(2,1)S(1)}, f16[256,1024]{1,0:T(8,128)(2,1)S(1)}, u32[]{:S(2)}, u32[]{:S(2)}) collective-permute-start(f16[256,1024]{1,0:T(8,128)(2,1)S(1)} %get-tuple-element.120), channel_id=1, source_target_pairs={{2,4},{4,2},{6,8},{8,6},{10,12},{12,10},{14,16},{16,14},{18,20},{2... | collective-permute-start | bytes 1572872 | tf_op jit(solution)/shard_map/ppermute | solution.py:28
  63.5 0.2 collective-permute-start.8
  63.7 2.5 %multiply_add_fusion = f32[256,1024]{1,0:T(8,128)S(1)} fusion(f16[256,1024]{1,0:T(8,128)(2,1)} %collective-permute-done.3, f32[256,1024]{1,0:T(8,128)S(1)} %get-tuple-element.91, f16[256,1024]{1,0:T(8,128)(2,1)} %collective-permute-done.4, f32[]{:T(128)S(6)} %div.37, f32[]{:T(128)} %bitcast.12, f32[]{:T(128)S(6)} %div.34), kind=kLoop, calls=%fused_computation.42 | loop fusion | flops 1835008 | bytes 3145740 | tf_op jit(solution)/shard_map/add | solution.py:115
  66.3 0.0 slice-start.1
  66.3 1.1 pad_bitcast_fusion
  67.4 9.3 %collective-permute-done.8 = f16[256,1024]{1,0:T(8,128)(2,1)S(1)} collective-permute-done((f16[256,1024]{1,0:T(8,128)(2,1)}, f16[256,1024]{1,0:T(8,128)(2,1)S(1)}, u32[]{:S(2)}, u32[]{:S(2)}) %collective-permute-start.8) | collective-permute-done | bytes 524320 | tf_op jit(solution)/shard_map/ppermute | solution.py:19
  76.7 0.2 collective-permute-start.11
  76.9 2.0 %bitcast_dynamic-update-slice_fusion.6 = f32[1,2048,1024]{2,1,0:T(8,128)S(1)} fusion(f32[1,2048,1024]{2,1,0:T(8,128)S(1)} %pad_bitcast_fusion, f16[256,1024]{1,0:T(8,128)(2,1)} %copy-done.9, f32[256,1024]{1,0:T(8,128)S(1)} %copy-done.6, f16[256,1024]{1,0:T(8,128)(2,1)} %collective-permute-done.7, f32[]{:T(128)S(6)} %div.37, f32[]{:T(128)} %bitcast.12, ...), kind=kLoop, calls=%fused_computation.32 | loop fusion | flops 1835008 | bytes 3145740 | tf_op jit(solution)/shard_map/dynamic_update_slice | solution.py:119
  79.0 0.0 collective-permute-done.10
  79.0 0.3 multiply_convert_fusion.4
  79.3 1.8 %collective-permute-start.15 = (f16[256,1024]{1,0:T(8,128)(2,1)S(1)}, f16[256,1024]{1,0:T(8,128)(2,1)S(1)}, u32[]{:S(2)}, u32[]{:S(2)}) collective-permute-start(f16[256,1024]{1,0:T(8,128)(2,1)S(1)} %get-tuple-element.130), channel_id=1, source_target_pairs={{2,4},{4,2},{6,8},{8,6},{10,12},{12,10},{14,16},{16,14},{18,20},{2... | collective-permute-start | bytes 1572872 | tf_op jit(solution)/shard_map/ppermute | solution.py:28
  81.1 1.8 %collective-permute-start.16 = (f16[256,1024]{1,0:T(8,128)(2,1)S(1)}, f16[256,1024]{1,0:T(8,128)(2,1)S(1)}, u32[]{:S(2)}, u32[]{:S(2)}) collective-permute-start(f16[256,1024]{1,0:T(8,128)(2,1)S(1)} %get-tuple-element.130), channel_id=1, source_target_pairs={{0,2},{2,0},{4,6},{6,4},{8,10},{10,8},{12,14},{14,12},{16,18},{18,... | collective-permute-start | bytes 1572872 | tf_op jit(solution)/shard_map/ppermute | solution.py:28
  82.9 5.9 %collective-permute-done.11 = f16[256,1024]{1,0:T(8,128)(2,1)S(1)} collective-permute-done((f16[256,1024]{1,0:T(8,128)(2,1)S(1)}, f16[256,1024]{1,0:T(8,128)(2,1)S(1)}, u32[]{:S(2)}, u32[]{:S(2)}) %collective-permute-start.11) | collective-permute-done | bytes 524320 | tf_op jit(solution)/shard_map/ppermute | solution.py:19
  88.8 0.3 collective-permute-start.14
  89.1 0.3 multiply_convert_fusion.3
  89.4 3.2 %collective-permute-start.18 = (f16[256,1024]{1,0:T(8,128)(2,1)S(1)}, f16[256,1024]{1,0:T(8,128)(2,1)S(1)}, u32[]{:S(2)}, u32[]{:S(2)}) collective-permute-start(f16[256,1024]{1,0:T(8,128)(2,1)S(1)} %get-tuple-element.140), channel_id=1, source_target_pairs={{2,4},{4,2},{6,8},{8,6},{10,12},{12,10},{14,16},{16,14},{18,20},{2... | collective-permute-start | bytes 1572872 | tf_op jit(solution)/shard_map/ppermute | solution.py:28
  92.6 0.8 collective-permute-start.19
  93.4 0.8 bitcast_dynamic-update-slice_fusion.5
  94.3 5.7 %collective-permute-done.14 = f16[256,1024]{1,0:T(8,128)(2,1)S(1)} collective-permute-done((f16[256,1024]{1,0:T(8,128)(2,1)S(1)}, f16[256,1024]{1,0:T(8,128)(2,1)S(1)}, u32[]{:S(2)}, u32[]{:S(2)}) %collective-permute-start.14) | collective-permute-done | bytes 524320 | tf_op jit(solution)/shard_map/ppermute | solution.py:19
  100.0 0.2 collective-permute-start.17
  100.2 0.8 bitcast_dynamic-update-slice_fusion.4
  101.1 0.3 multiply_convert_fusion.2
  101.4 4.7 %collective-permute-start.21 = (f16[256,1024]{1,0:T(8,128)(2,1)S(1)}, f16[256,1024]{1,0:T(8,128)(2,1)S(1)}, u32[]{:S(2)}, u32[]{:S(2)}) collective-permute-start(f16[256,1024]{1,0:T(8,128)(2,1)S(1)} %get-tuple-element.144), channel_id=1, source_target_pairs={{2,4},{4,2},{6,8},{8,6},{10,12},{12,10},{14,16},{16,14},{18,20},{2... | collective-permute-start | bytes 1572872 | tf_op jit(solution)/shard_map/ppermute | solution.py:28
  106.1 4.3 %collective-permute-done.17 = f16[256,1024]{1,0:T(8,128)(2,1)S(1)} collective-permute-done((f16[256,1024]{1,0:T(8,128)(2,1)S(1)}, f16[256,1024]{1,0:T(8,128)(2,1)S(1)}, u32[]{:S(2)}, u32[]{:S(2)}) %collective-permute-start.17) | collective-permute-done | bytes 524320 | tf_op jit(solution)/shard_map/ppermute | solution.py:19
  110.4 0.3 multiply_convert_fusion.1
  110.7 5.7 %collective-permute-start.23 = (f16[256,1024]{1,0:T(8,128)(2,1)S(1)}, f16[256,1024]{1,0:T(8,128)(2,1)S(1)}, u32[]{:S(2)}, u32[]{:S(2)}) collective-permute-start(f16[256,1024]{1,0:T(8,128)(2,1)S(1)} %get-tuple-element.147), channel_id=1, source_target_pairs={{2,4},{4,2},{6,8},{8,6},{10,12},{12,10},{14,16},{16,14},{18,20},{2... | collective-permute-start | bytes 1572872 | tf_op jit(solution)/shard_map/ppermute | solution.py:28
  116.4 0.9 bitcast_dynamic-update-slice_fusion.3
  117.2 0.9 bitcast_dynamic-update-slice_fusion.2
  118.1 5.1 %collective-permute-done.21 = f16[256,1024]{1,0:T(8,128)(2,1)S(1)} collective-permute-done((f16[256,1024]{1,0:T(8,128)(2,1)S(1)}, f16[256,1024]{1,0:T(8,128)(2,1)S(1)}, u32[]{:S(2)}, u32[]{:S(2)}) %collective-permute-start.21) | collective-permute-done | bytes 524320 | tf_op jit(solution)/shard_map/ppermute | solution.py:28
  123.2 0.9 bitcast_dynamic-update-slice_fusion.1
  124.1 0.0 copy-start.2
  124.1 5.7 %collective-permute-done.23 = f16[256,1024]{1,0:T(8,128)(2,1)S(1)} collective-permute-done((f16[256,1024]{1,0:T(8,128)(2,1)S(1)}, f16[256,1024]{1,0:T(8,128)(2,1)S(1)}, u32[]{:S(2)}, u32[]{:S(2)}) %collective-permute-start.23) | collective-permute-done | bytes 524320 | tf_op jit(solution)/shard_map/ppermute | solution.py:28
  129.8 1.8 %bitcast_dynamic-update-slice_fusion = f32[1,2048,1024]{2,1,0:T(8,128)} fusion(f32[1,2048,1024]{2,1,0:T(8,128)} %copy-done.2, f16[256,1024]{1,0:T(8,128)(2,1)S(1)} %collective-permute-done.23, f32[256,1024]{1,0:T(8,128)S(1)} %get-tuple-element.148, f16[256,1024]{1,0:T(8,128)(2,1)S(1)} %collective-permute-done.22, f32[]{:T(128)S(6)} %div.37, f32[]{:T(128)} %bitcast.12, ...), kind=kLoop, calls=%fused_computation.21 | loop fusion | flops 1835008 | bytes 3146248 | tf_op jit(solution)/shard_map/dynamic_update_slice | solution.py:119
  (38 shorter events, 0.1 us)
Async XLA Ops:
  0.0 1.5 %copy-start = (bf16[1,896,1024]{2,1,0:T(8,128)(2,1)S(1)}, bf16[1,896,1024]{2,1,0:T(8,128)(2,1)}, u32[]{:S(2)}) copy-start(bf16[1,896,1024]{2,1,0:T(8,128)(2,1)} %param.6) | copy-start | bytes 5505028
  3.3 17.6 %collective-permute-start = (f16[256,1024]{1,0:T(8,128)(2,1)S(1)}, f16[256,1024]{1,0:T(8,128)(2,1)S(1)}, u32[]{:S(2)}, u32[]{:S(2)}) collective-permute-start(f16[256,1024]{1,0:T(8,128)(2,1)S(1)} %fusion.22), channel_id=1, source_target_pairs={{0,1},{1,0},{2,3},{3,2},{4,5},{5,4},{6,7},{7,6},{8,9},{9,8},{10,11... | collective-permute-start | bytes 1572872 | tf_op jit(solution)/shard_map/ppermute | solution.py:19
  8.0 30.2 %collective-permute-start.2 = (f16[256,1024]{1,0:T(8,128)(2,1)}, f16[256,1024]{1,0:T(8,128)(2,1)}, u32[]{:S(2)}, u32[]{:S(2)}) collective-permute-start(f16[256,1024]{1,0:T(8,128)(2,1)} %fusion.19), channel_id=1, source_target_pairs={{0,1},{1,0},{2,3},{3,2},{4,5},{5,4},{6,7},{7,6},{8,9},{9,8},{10,11... | collective-permute-start | bytes 1572872 | tf_op jit(solution)/shard_map/ppermute | solution.py:19
  20.8 1.5 %copy-start.3 = (f32[512,1024]{1,0:T(8,128)}, f32[512,1024]{1,0:T(8,128)S(1)}, u32[]{:S(2)}) copy-start(f32[512,1024]{1,0:T(8,128)S(1)} %fusion.8) | copy-start | bytes 6291460
  20.9 0.8 copy-start.10
  24.9 23.5 %collective-permute-start.3 = (f16[256,1024]{1,0:T(8,128)(2,1)}, f16[256,1024]{1,0:T(8,128)(2,1)}, u32[]{:S(2)}, u32[]{:S(2)}) collective-permute-start(f16[256,1024]{1,0:T(8,128)(2,1)} %get-tuple-element.89), channel_id=1, source_target_pairs={{2,4},{4,2},{6,8},{8,6},{10,12},{12,10},{14,16},{16,14},{18,20},{2... | collective-permute-start | bytes 1572872 | tf_op jit(solution)/shard_map/ppermute | solution.py:28
  27.4 21.0 %collective-permute-start.4 = (f16[256,1024]{1,0:T(8,128)(2,1)}, f16[256,1024]{1,0:T(8,128)(2,1)}, u32[]{:S(2)}, u32[]{:S(2)}) collective-permute-start(f16[256,1024]{1,0:T(8,128)(2,1)} %get-tuple-element.89), channel_id=1, source_target_pairs={{0,2},{2,0},{4,6},{6,4},{8,10},{10,8},{12,14},{14,12},{16,18},{18,... | collective-permute-start | bytes 1572872 | tf_op jit(solution)/shard_map/ppermute | solution.py:28
  29.7 13.9 %collective-permute-start.1 = (f16[256,1024]{1,0:T(8,128)(2,1)}, f16[256,1024]{1,0:T(8,128)(2,1)}, u32[]{:S(2)}, u32[]{:S(2)}) collective-permute-start(f16[256,1024]{1,0:T(8,128)(2,1)} %get-tuple-element.82), channel_id=1, source_target_pairs={{0,1},{1,0},{2,3},{3,2},{4,5},{5,4},{6,7},{7,6},{8,9},{9,8},{10,11... | collective-permute-start | bytes 1572872 | tf_op jit(solution)/shard_map/ppermute | solution.py:19
  30.9 7.3 %copy-start.4 = (f32[512,1024]{1,0:T(8,128)S(1)}, f32[512,1024]{1,0:T(8,128)}, u32[]{:S(2)}) copy-start(f32[512,1024]{1,0:T(8,128)} %copy-done.3) | copy-start | bytes 6291460
  30.9 13.9 %copy-start.11 = (s32[16,3]{0,1:T(4,128)S(1)}, s32[16,3]{0,1:T(4,128)}, u32[]{:S(2)}) copy-start(s32[16,3]{0,1:T(4,128)} %param.7) | copy-start | bytes 580
  41.1 17.7 %collective-permute-start.6 = (f16[256,1024]{1,0:T(8,128)(2,1)}, f16[256,1024]{1,0:T(8,128)(2,1)S(1)}, u32[]{:S(2)}, u32[]{:S(2)}) collective-permute-start(f16[256,1024]{1,0:T(8,128)(2,1)} %get-tuple-element.100), channel_id=1, source_target_pairs={{2,4},{4,2},{6,8},{8,6},{10,12},{12,10},{14,16},{16,14},{18,20},{2... | collective-permute-start | bytes 1572872 | tf_op jit(solution)/shard_map/ppermute | solution.py:28
  41.1 17.7 %collective-permute-start.7 = (f16[256,1024]{1,0:T(8,128)(2,1)}, f16[256,1024]{1,0:T(8,128)(2,1)}, u32[]{:S(2)}, u32[]{:S(2)}) collective-permute-start(f16[256,1024]{1,0:T(8,128)(2,1)} %get-tuple-element.100), channel_id=1, source_target_pairs={{0,2},{2,0},{4,6},{6,4},{8,10},{10,8},{12,14},{14,12},{16,18},{18,... | collective-permute-start | bytes 1572872 | tf_op jit(solution)/shard_map/ppermute | solution.py:28
  43.6 13.0 %collective-permute-start.5 = (f16[256,1024]{1,0:T(8,128)(2,1)}, f16[256,1024]{1,0:T(8,128)(2,1)}, u32[]{:S(2)}, u32[]{:S(2)}) collective-permute-start(f16[256,1024]{1,0:T(8,128)(2,1)} %get-tuple-element.95), channel_id=1, source_target_pairs={{0,1},{1,0},{2,3},{3,2},{4,5},{5,4},{6,7},{7,6},{8,9},{9,8},{10,11... | collective-permute-start | bytes 1572872 | tf_op jit(solution)/shard_map/ppermute | solution.py:19
  50.5 28.5 %collective-permute-start.9 = (f16[256,1024]{1,0:T(8,128)(2,1)S(1)}, f16[256,1024]{1,0:T(8,128)(2,1)S(1)}, u32[]{:S(2)}, u32[]{:S(2)}) collective-permute-start(f16[256,1024]{1,0:T(8,128)(2,1)S(1)} %get-tuple-element.110), channel_id=1, source_target_pairs={{2,4},{4,2},{6,8},{8,6},{10,12},{12,10},{14,16},{16,14},{18,20},{2... | collective-permute-start | bytes 1572872 | tf_op jit(solution)/shard_map/ppermute | solution.py:28
  50.6 28.4 %collective-permute-start.10 = (f16[256,1024]{1,0:T(8,128)(2,1)S(1)}, f16[256,1024]{1,0:T(8,128)(2,1)S(1)}, u32[]{:S(2)}, u32[]{:S(2)}) collective-permute-start(f16[256,1024]{1,0:T(8,128)(2,1)S(1)} %get-tuple-element.110), channel_id=1, source_target_pairs={{0,2},{2,0},{4,6},{6,4},{8,10},{10,8},{12,14},{14,12},{16,18},{18,... | collective-permute-start | bytes 1572872 | tf_op jit(solution)/shard_map/ppermute | solution.py:28
  58.8 5.0 %copy-start.9 = (f16[256,1024]{1,0:T(8,128)(2,1)}, f16[256,1024]{1,0:T(8,128)(2,1)S(1)}, u32[]{:S(2)}) copy-start(f16[256,1024]{1,0:T(8,128)(2,1)S(1)} %collective-permute-done.6) | copy-start | bytes 1572868
  58.8 17.9 %copy-start.8 = (f16[256,1024]{1,0:T(8,128)(2,1)S(1)}, f16[256,1024]{1,0:T(8,128)(2,1)}, u32[]{:S(2)}) copy-start(f16[256,1024]{1,0:T(8,128)(2,1)} %get-tuple-element.116) | copy-start | bytes 1572868
  61.1 15.9 %copy-start.6 = (f32[256,1024]{1,0:T(8,128)S(1)}, f32[256,1024]{1,0:T(8,128)}, u32[]{:S(2)}) copy-start(f32[256,1024]{1,0:T(8,128)} %get-tuple-element.102) | copy-start | bytes 3145732
  61.1 27.7 %collective-permute-start.12 = (f16[256,1024]{1,0:T(8,128)(2,1)S(1)}, f16[256,1024]{1,0:T(8,128)(2,1)S(1)}, u32[]{:S(2)}, u32[]{:S(2)}) collective-permute-start(f16[256,1024]{1,0:T(8,128)(2,1)S(1)} %get-tuple-element.120), channel_id=1, source_target_pairs={{2,4},{4,2},{6,8},{8,6},{10,12},{12,10},{14,16},{16,14},{18,20},{2... | collective-permute-start | bytes 1572872 | tf_op jit(solution)/shard_map/ppermute | solution.py:28
  63.5 25.3 %collective-permute-start.13 = (f16[256,1024]{1,0:T(8,128)(2,1)S(1)}, f16[256,1024]{1,0:T(8,128)(2,1)S(1)}, u32[]{:S(2)}, u32[]{:S(2)}) collective-permute-start(f16[256,1024]{1,0:T(8,128)(2,1)S(1)} %get-tuple-element.120), channel_id=1, source_target_pairs={{0,2},{2,0},{4,6},{6,4},{8,10},{10,8},{12,14},{14,12},{16,18},{18,... | collective-permute-start | bytes 1572872 | tf_op jit(solution)/shard_map/ppermute | solution.py:28
  63.5 13.2 %collective-permute-start.8 = (f16[256,1024]{1,0:T(8,128)(2,1)}, f16[256,1024]{1,0:T(8,128)(2,1)S(1)}, u32[]{:S(2)}, u32[]{:S(2)}) collective-permute-start(f16[256,1024]{1,0:T(8,128)(2,1)} %get-tuple-element.106), channel_id=1, source_target_pairs={{0,1},{1,0},{2,3},{3,2},{4,5},{5,4},{6,7},{7,6},{8,9},{9,8},{10,11... | collective-permute-start | bytes 1572872 | tf_op jit(solution)/shard_map/ppermute | solution.py:19
  63.7 15.3 %slice-start = ((s8[8388608]{0:T(1024)(128)(4,1)}), s8[4194304]{0:T(1024)(128)(4,1)S(1)}, s32[]{:S(2)}) async-start(s8[8388608]{0:T(1024)(128)(4,1)} %bitcast.84), calls=%async_computation | async-start | bytes 8388608
  63.7 15.3 %copy-start.5 = (f32[1536,1024]{1,0:T(8,128)S(1)}, f32[1536,1024]{1,0:T(8,128)}, u32[]{:S(2)}) copy-start(f32[1536,1024]{1,0:T(8,128)} %fusion) | copy-start | bytes 18874372
  66.3 12.7 %slice-start.1 = ((s8[8388608]{0:T(1024)(128)(4,1)}), s8[4194304]{0:T(1024)(128)(4,1)S(1)}, s32[]{:S(2)}) async-start(s8[8388608]{0:T(1024)(128)(4,1)} %bitcast.84), calls=%async_computation.1 | async-start | bytes 8388608
  66.3 22.5 %copy-start.7 = (f16[256,1024]{1,0:T(8,128)(2,1)S(1)}, f16[256,1024]{1,0:T(8,128)(2,1)}, u32[]{:S(2)}) copy-start(f16[256,1024]{1,0:T(8,128)(2,1)} %get-tuple-element.126) | copy-start | bytes 1572868
  76.7 12.1 %collective-permute-start.11 = (f16[256,1024]{1,0:T(8,128)(2,1)S(1)}, f16[256,1024]{1,0:T(8,128)(2,1)S(1)}, u32[]{:S(2)}, u32[]{:S(2)}) collective-permute-start(f16[256,1024]{1,0:T(8,128)(2,1)S(1)} %copy-done.8), channel_id=1, source_target_pairs={{0,1},{1,0},{2,3},{3,2},{4,5},{5,4},{6,7},{7,6},{8,9},{9,8},{10,11... | collective-permute-start | bytes 1572872 | tf_op jit(solution)/shard_map/ppermute | solution.py:19
  79.3 21.7 %collective-permute-start.15 = (f16[256,1024]{1,0:T(8,128)(2,1)S(1)}, f16[256,1024]{1,0:T(8,128)(2,1)S(1)}, u32[]{:S(2)}, u32[]{:S(2)}) collective-permute-start(f16[256,1024]{1,0:T(8,128)(2,1)S(1)} %get-tuple-element.130), channel_id=1, source_target_pairs={{2,4},{4,2},{6,8},{8,6},{10,12},{12,10},{14,16},{16,14},{18,20},{2... | collective-permute-start | bytes 1572872 | tf_op jit(solution)/shard_map/ppermute | solution.py:28
  81.1 19.9 %collective-permute-start.16 = (f16[256,1024]{1,0:T(8,128)(2,1)S(1)}, f16[256,1024]{1,0:T(8,128)(2,1)S(1)}, u32[]{:S(2)}, u32[]{:S(2)}) collective-permute-start(f16[256,1024]{1,0:T(8,128)(2,1)S(1)} %get-tuple-element.130), channel_id=1, source_target_pairs={{0,2},{2,0},{4,6},{6,4},{8,10},{10,8},{12,14},{14,12},{16,18},{18,... | collective-permute-start | bytes 1572872 | tf_op jit(solution)/shard_map/ppermute | solution.py:28
  88.8 11.2 %collective-permute-start.14 = (f16[256,1024]{1,0:T(8,128)(2,1)S(1)}, f16[256,1024]{1,0:T(8,128)(2,1)S(1)}, u32[]{:S(2)}, u32[]{:S(2)}) collective-permute-start(f16[256,1024]{1,0:T(8,128)(2,1)S(1)} %copy-done.7), channel_id=1, source_target_pairs={{0,1},{1,0},{2,3},{3,2},{4,5},{5,4},{6,7},{7,6},{8,9},{9,8},{10,11... | collective-permute-start | bytes 1572872 | tf_op jit(solution)/shard_map/ppermute | solution.py:19
  89.4 21.0 %collective-permute-start.18 = (f16[256,1024]{1,0:T(8,128)(2,1)S(1)}, f16[256,1024]{1,0:T(8,128)(2,1)S(1)}, u32[]{:S(2)}, u32[]{:S(2)}) collective-permute-start(f16[256,1024]{1,0:T(8,128)(2,1)S(1)} %get-tuple-element.140), channel_id=1, source_target_pairs={{2,4},{4,2},{6,8},{8,6},{10,12},{12,10},{14,16},{16,14},{18,20},{2... | collective-permute-start | bytes 1572872 | tf_op jit(solution)/shard_map/ppermute | solution.py:28
  92.6 17.8 %collective-permute-start.19 = (f16[256,1024]{1,0:T(8,128)(2,1)S(1)}, f16[256,1024]{1,0:T(8,128)(2,1)S(1)}, u32[]{:S(2)}, u32[]{:S(2)}) collective-permute-start(f16[256,1024]{1,0:T(8,128)(2,1)S(1)} %get-tuple-element.140), channel_id=1, source_target_pairs={{0,2},{2,0},{4,6},{6,4},{8,10},{10,8},{12,14},{14,12},{16,18},{18,... | collective-permute-start | bytes 1572872 | tf_op jit(solution)/shard_map/ppermute | solution.py:28
  100.0 10.4 %collective-permute-start.17 = (f16[256,1024]{1,0:T(8,128)(2,1)S(1)}, f16[256,1024]{1,0:T(8,128)(2,1)S(1)}, u32[]{:S(2)}, u32[]{:S(2)}) collective-permute-start(f16[256,1024]{1,0:T(8,128)(2,1)S(1)} %get-tuple-element.136), channel_id=1, source_target_pairs={{0,1},{1,0},{2,3},{3,2},{4,5},{5,4},{6,7},{7,6},{8,9},{9,8},{10,11... | collective-permute-start | bytes 1572872 | tf_op jit(solution)/shard_map/ppermute | solution.py:19
  101.4 21.8 %collective-permute-start.21 = (f16[256,1024]{1,0:T(8,128)(2,1)S(1)}, f16[256,1024]{1,0:T(8,128)(2,1)S(1)}, u32[]{:S(2)}, u32[]{:S(2)}) collective-permute-start(f16[256,1024]{1,0:T(8,128)(2,1)S(1)} %get-tuple-element.144), channel_id=1, source_target_pairs={{2,4},{4,2},{6,8},{8,6},{10,12},{12,10},{14,16},{16,14},{18,20},{2... | collective-permute-start | bytes 1572872 | tf_op jit(solution)/shard_map/ppermute | solution.py:28
  106.1 17.1 %collective-permute-start.20 = (f16[256,1024]{1,0:T(8,128)(2,1)S(1)}, f16[256,1024]{1,0:T(8,128)(2,1)S(1)}, u32[]{:S(2)}, u32[]{:S(2)}) collective-permute-start(f16[256,1024]{1,0:T(8,128)(2,1)S(1)} %get-tuple-element.144), channel_id=1, source_target_pairs={{0,2},{2,0},{4,6},{6,4},{8,10},{10,8},{12,14},{14,12},{16,18},{18,... | collective-permute-start | bytes 1572872 | tf_op jit(solution)/shard_map/ppermute | solution.py:28
  110.4 21.3 %copy-start.1 = (bf16[1,896,1024]{2,1,0:T(8,128)(2,1)S(1)}, bf16[1,896,1024]{2,1,0:T(8,128)(2,1)}, u32[]{:S(2)}) copy-start(bf16[1,896,1024]{2,1,0:T(8,128)(2,1)} %param.6) | copy-start | bytes 5505028
  110.7 19.1 %collective-permute-start.23 = (f16[256,1024]{1,0:T(8,128)(2,1)S(1)}, f16[256,1024]{1,0:T(8,128)(2,1)S(1)}, u32[]{:S(2)}, u32[]{:S(2)}) collective-permute-start(f16[256,1024]{1,0:T(8,128)(2,1)S(1)} %get-tuple-element.147), channel_id=1, source_target_pairs={{2,4},{4,2},{6,8},{8,6},{10,12},{12,10},{14,16},{16,14},{18,20},{2... | collective-permute-start | bytes 1572872 | tf_op jit(solution)/shard_map/ppermute | solution.py:28
  116.4 13.4 %collective-permute-start.22 = (f16[256,1024]{1,0:T(8,128)(2,1)S(1)}, f16[256,1024]{1,0:T(8,128)(2,1)S(1)}, u32[]{:S(2)}, u32[]{:S(2)}) collective-permute-start(f16[256,1024]{1,0:T(8,128)(2,1)S(1)} %get-tuple-element.147), channel_id=1, source_target_pairs={{0,2},{2,0},{4,6},{6,4},{8,10},{10,8},{12,14},{14,12},{16,18},{18,... | collective-permute-start | bytes 1572872 | tf_op jit(solution)/shard_map/ppermute | solution.py:28
  124.1 5.8 %copy-start.2 = (f32[1,2048,1024]{2,1,0:T(8,128)}, f32[1,2048,1024]{2,1,0:T(8,128)S(1)}, u32[]{:S(2)}) copy-start(f32[1,2048,1024]{2,1,0:T(8,128)S(1)} %bitcast_dynamic-update-slice_fusion.1) | copy-start | bytes 25165828

commit v4 on v3

--- a/solution.py
+++ b/solution.py
@@ -106,6 +106,8 @@
         if after < CHUNKS:
             terms[after], sent = lax.optimization_barrier((terms[after], sent))
             arrived[after] = send_terms(terms[after])
+        if chunk == CHUNKS - 1:
+            far[0], near[0], sent = lax.optimization_barrier((far[0], near[0], sent))
         far[chunk] = swapped(sent, "blk", 1)
         near[chunk] = swapped(sent, "blk", 0)
 

time: 132 us -> 125 us (0.947)
  starting transfers between devices: 33.5 us -> 17.3 us
  other arithmetic: 21.7 us -> 36 us
  waiting for transfers between devices: 44.2 us -> 40.5 us
  matrix products: 20.8 us -> 18.9 us
    ppermute x16, starting transfers between devices: 27.8 us -> 8.58 us  [swapped(): return lax.ppermute(value, axis, pairs)]
    ppermute x8, waiting for transfers between devices: 31.2 us -> 19.6 us  [from_behind(): return lax.ppermute(value, axis, pairs)]
    convert_element_type x8, other arithmetic: 10.9 us -> 22.4 us  [on_device(): (own * scale).astype(WIRE)]
    ppermute x16, waiting for transfers between devices: 13 us -> 20.9 us  [swapped(): return lax.ppermute(value, axis, pairs)]
    dynamic_update_slice x7, other arithmetic: 8.2 us -> 11.5 us  [on_device(): out = lax.dynamic_update_slice_in_dim(out, mixed, chunk * step, axis=0)]
    ppermute x8, starting transfers between devices: 5.61 us -> 8.71 us  [from_behind(): return lax.ppermute(value, axis, pairs)]
    dot_general x5, matrix products: 20.7 us -> 18.8 us  [partial(): lax.dot_general(block, cot_local, (((0,), (0,)), ((), ())), preferred_ele...]
    unnamed x28 -> x42, local copies, waits for them, and re-layouts: 3.02 us -> 2.91 us
  transfers between devices with their start and end apart: 24 -> 24, of which waited for: 9 -> 11; matrix products, arithmetic and copies ran while one was open for 34% -> 46% of each run, Pallas kernels for 0% -> 0%
where the time goes in v4:
time: 125 us; the launch traced here: 124 us
  waiting for transfers between devices  40.5 us (32%)
  other arithmetic  36 us (29%)
  matrix products  18.9 us (15%)
  starting transfers between devices  17.3 us (14%)
  local copies, waits for them, and re-layouts  8.64 us (7%)
  between operations  2.78 us (2%)
    convert_element_type x8, other arithmetic, on_device(): (own * scale).astype(WIRE)  22.4 us
    ppermute x16, waiting for transfers between devices, swapped(): return lax.ppermute(value, axis, pairs)  20.9 us
    ppermute x8, waiting for transfers between devices, from_behind(): return lax.ppermute(value, axis, pairs)  19.6 us
    dot_general x5, matrix products, partial(): lax.dot_general(block, cot_local, (((0,), (0,)), ((), ())), preferred_ele...  18.8 us
    dynamic_update_slice x7, other arithmetic, on_device(): out = lax.dynamic_update_slice_in_dim(out, mixed, chunk * step, axis=0)  11.5 us
    ppermute x8, starting transfers between devices, from_behind(): return lax.ppermute(value, axis, pairs)  8.71 us
    ppermute x16, starting transfers between devices, swapped(): return lax.ppermute(value, axis, pairs)  8.58 us
    slice x1, local copies, waits for them, and re-layouts, rows_of(): return value[chunk * step:(chunk + 1) * step]  4.01 us
  transfers between devices with their start and end apart: 24, of which 11 were waited for; matrix products, arithmetic and copies ran while one was open for 46% of the time, Pallas kernels for 0%

profile of v4, /device:TPU:1, one launch (start us, length us, event | category | flops | bytes accessed | tf_op | source)
XLA Modules:
  0.0 124.1 jit_solution(15403250532712688523)
XLA Ops:
  0.0 1.5 %copy-done = bf16[1,896,1024]{2,1,0:T(8,128)(2,1)S(1)} copy-done((bf16[1,896,1024]{2,1,0:T(8,128)(2,1)S(1)}, bf16[1,896,1024]{2,1,0:T(8,128)(2,1)}, u32[]{:S(2)}) %copy-start) | copy-done | bytes 1835032
  1.5 1.7 %fusion.22 = f16[256,1024]{1,0:T(8,128)(2,1)S(1)} fusion(bf16[1,896,1024]{2,1,0:T(8,128)(2,1)S(1)} %copy-done, bf16[1,896,4096]{2,1,0:T(8,128)(2,1)} %param.5, s32[]{:T(128)S(6)} %select_n.31), kind=kOutput, calls=%fused_computation.18 | convolution fusion | flops 470286336 | bytes 2818052 | tf_op jit(solution)/shard_map/dot_general | solution.py:55
  3.3 2.1 %collective-permute-start = (f16[256,1024]{1,0:T(8,128)(2,1)S(1)}, f16[256,1024]{1,0:T(8,128)(2,1)S(1)}, u32[]{:S(2)}, u32[]{:S(2)}) collective-permute-start(f16[256,1024]{1,0:T(8,128)(2,1)S(1)} %fusion.22), channel_id=1, source_target_pairs={{0,1},{1,0},{2,3},{3,2},{4,5},{5,4},{6,7},{7,6},{8,9},{9,8},{10,11... | collective-permute-start | bytes 1572872 | tf_op jit(solution)/shard_map/ppermute | solution.py:19
  5.4 2.6 %fusion.19 = f16[256,1024]{1,0:T(8,128)(2,1)} fusion(bf16[1,896,1024]{2,1,0:T(8,128)(2,1)S(1)} %copy-done, bf16[1,896,4096]{2,1,0:T(8,128)(2,1)} %param.5, s32[]{:T(128)S(6)} %select_n.34), kind=kOutput, calls=%fused_computation.17 | convolution fusion | flops 470286336 | bytes 2818052 | tf_op jit(solution)/shard_map/dot_general | solution.py:55
  7.9 0.0 collective-permute-start.2
  8.0 6.6 %multiply_convert_fusion = f16[1536,1024]{1,0:T(8,128)(2,1)} fusion(bf16[1,896,4096]{2,1,0:T(8,128)(2,1)} %param.5, s32[]{:T(128)S(6)} %select_n.32, bf16[1,896,1024]{2,1,0:T(8,128)(2,1)S(1)} %copy-done), kind=kOutput, calls=%fused_computation.1 | convolution fusion | flops 2821718016 | bytes 7733252 | tf_op jit(solution)/shard_map/dot_general | solution.py:55
  14.6 4.0 %fusion.42 = (f16[256,1024]{1,0:T(8,128)(2,1)}, f16[256,1024]{1,0:T(8,128)(2,1)}, f16[256,1024]{1,0:T(8,128)(2,1)}, f16[256,1024]{1,0:T(8,128)(2,1)}, f16[256,1024]{1,0:T(8,128)(2,1)}, /*index=5*/f16[256,1024]{1,0:T(8,128)(2,1)}) fusion(f16[1536,1024]{1,0:T(8,128)(2,1)} %multiply_convert_fusion), kind=kLoop, calls=%fused_computation.61 | loop fusion | bytes 6291456 | tf_op jit(solution)/shard_map/slice | solution.py:69
  18.6 2.4 %fusion.8 = f32[512,1024]{1,0:T(8,128)S(1)} fusion(bf16[1,896,1024]{2,1,0:T(8,128)(2,1)S(1)} %copy-done, bf16[1,896,4096]{2,1,0:T(8,128)(2,1)} %param.5, s32[]{:T(128)S(6)} %select_n.33), kind=kOutput, calls=%fused_computation.10 | convolution fusion | flops 939524096 | bytes 4849668 | tf_op jit(solution)/shard_map/dot_general | solution.py:55
  21.1 0.0 collective-permute-done
  21.1 1.3 %copy-done.3 = f32[512,1024]{1,0:T(8,128)} copy-done((f32[512,1024]{1,0:T(8,128)}, f32[512,1024]{1,0:T(8,128)S(1)}, u32[]{:S(2)}) %copy-start.3) | copy-done | bytes 2097176
  22.4 2.3 %multiply_convert_fusion.8 = (f16[256,1024]{1,0:T(8,128)(2,1)}, f32[256,1024]{1,0:T(8,128)S(1)}) fusion(f16[256,1024]{1,0:T(8,128)(2,1)S(1)} %collective-permute-done, f32[512,1024]{1,0:T(8,128)S(1)} %fusion.8, f32[1,2048,1024]{2,1,0:T(8,128)} %param.4), kind=kLoop, calls=%fused_computation.44 | loop fusion | flops 1835008 | bytes 4194304 | tf_op jit(solution)/shard_map/convert_element_type | solution.py:101
  24.7 2.5 %collective-permute-start.3 = (f16[256,1024]{1,0:T(8,128)(2,1)}, f16[256,1024]{1,0:T(8,128)(2,1)S(1)}, u32[]{:S(2)}, u32[]{:S(2)}) collective-permute-start(f16[256,1024]{1,0:T(8,128)(2,1)} %get-tuple-element.92), channel_id=1, source_target_pairs={{2,4},{4,2},{6,8},{8,6},{10,12},{12,10},{14,16},{16,14},{18,20},{2... | collective-permute-start | bytes 1572872 | tf_op jit(solution)/shard_map/ppermute | solution.py:28
  27.3 2.3 %collective-permute-start.4 = (f16[256,1024]{1,0:T(8,128)(2,1)}, f16[256,1024]{1,0:T(8,128)(2,1)}, u32[]{:S(2)}, u32[]{:S(2)}) collective-permute-start(f16[256,1024]{1,0:T(8,128)(2,1)} %get-tuple-element.92), channel_id=1, source_target_pairs={{0,2},{2,0},{4,6},{6,4},{8,10},{10,8},{12,14},{14,12},{16,18},{18,... | collective-permute-start | bytes 1572872 | tf_op jit(solution)/shard_map/ppermute | solution.py:28
  29.6 1.2 collective-permute-start.1
  30.8 5.4 %fusion = f32[1536,1024]{1,0:T(8,128)S(1)} fusion(bf16[1,896,4096]{2,1,0:T(8,128)(2,1)} %param.5, s32[]{:T(128)S(6)} %select_n.35, bf16[1,896,1024]{2,1,0:T(8,128)(2,1)S(1)} %copy-done), kind=kOutput, calls=%fused_computation.2 | convolution fusion | flops 2818572288 | bytes 10878980 | tf_op jit(solution)/shard_map/dot_general | solution.py:55
  36.3 0.0 copy-start.5
  36.3 0.0 collective-permute-done.2
  36.3 4.0 %multiply_convert_fusion.7 = (f16[256,1024]{1,0:T(8,128)(2,1)S(1)}, f32[256,1024]{1,0:T(8,128)}) fusion(f16[256,1024]{1,0:T(8,128)(2,1)} %collective-permute-done.2, f32[512,1024]{1,0:T(8,128)S(1)} %copy-done.4, f32[1,2048,1024]{2,1,0:T(8,128)} %param.4), kind=kLoop, calls=%fused_computation.43 | loop fusion | flops 1835008 | bytes 4194304 | tf_op jit(solution)/shard_map/convert_element_type | solution.py:101
  40.3 0.2 collective-permute-start.5
  40.5 0.0 collective-permute-start.6
  40.5 2.9 %collective-permute-done.1 = f16[256,1024]{1,0:T(8,128)(2,1)} collective-permute-done((f16[256,1024]{1,0:T(8,128)(2,1)}, f16[256,1024]{1,0:T(8,128)(2,1)}, u32[]{:S(2)}, u32[]{:S(2)}) %collective-permute-start.1) | collective-permute-done | bytes 524320 | tf_op jit(solution)/shard_map/ppermute | solution.py:19
  43.4 1.2 collective-permute-start.7
  44.6 2.7 %multiply_convert_fusion.6 = (f16[256,1024]{1,0:T(8,128)(2,1)S(1)}, f32[256,1024]{1,0:T(8,128)}) fusion(f16[256,1024]{1,0:T(8,128)(2,1)} %collective-permute-done.1, f32[1536,1024]{1,0:T(8,128)S(1)} %fusion, f32[1,2048,1024]{2,1,0:T(8,128)} %param.4), kind=kLoop, calls=%fused_computation.42 | loop fusion | flops 1835008 | bytes 4194304 | tf_op jit(solution)/shard_map/convert_element_type | solution.py:101
  47.3 1.3 %collective-permute-start.9 = (f16[256,1024]{1,0:T(8,128)(2,1)S(1)}, f16[256,1024]{1,0:T(8,128)(2,1)S(1)}, u32[]{:S(2)}, u32[]{:S(2)}) collective-permute-start(f16[256,1024]{1,0:T(8,128)(2,1)S(1)} %copy-done.18), channel_id=1, source_target_pairs={{0,1},{1,0},{2,3},{3,2},{4,5},{5,4},{6,7},{7,6},{8,9},{9,8},{10,11... | collective-permute-start | bytes 1572872 | tf_op jit(solution)/shard_map/ppermute | solution.py:19
  48.6 0.0 collective-permute-start.10
  48.6 6.0 %collective-permute-done.5 = f16[256,1024]{1,0:T(8,128)(2,1)S(1)} collective-permute-done((f16[256,1024]{1,0:T(8,128)(2,1)S(1)}, f16[256,1024]{1,0:T(8,128)(2,1)S(1)}, u32[]{:S(2)}, u32[]{:S(2)}) %collective-permute-start.5) | collective-permute-done | bytes 524320 | tf_op jit(solution)/shard_map/ppermute | solution.py:19
  54.6 1.2 collective-permute-start.11
  55.7 5.0 %collective-permute-done.6 = f16[256,1024]{1,0:T(8,128)(2,1)S(1)} collective-permute-done((f16[256,1024]{1,0:T(8,128)(2,1)S(1)}, f16[256,1024]{1,0:T(8,128)(2,1)S(1)}, u32[]{:S(2)}, u32[]{:S(2)}) %collective-permute-start.6) | collective-permute-done | bytes 524320 | tf_op jit(solution)/shard_map/ppermute | solution.py:28
  60.7 0.0 collective-permute-done.7
  60.7 2.9 %multiply_convert_fusion.5 = (f16[256,1024]{1,0:T(8,128)(2,1)}, f32[256,1024]{1,0:T(8,128)}) fusion(f16[256,1024]{1,0:T(8,128)(2,1)S(1)} %collective-permute-done.5, f32[1536,1024]{1,0:T(8,128)S(1)} %fusion, f32[1,2048,1024]{2,1,0:T(8,128)} %param.4), kind=kLoop, calls=%fused_computation.41 | loop fusion | flops 1835008 | bytes 4194304 | tf_op jit(solution)/shard_map/convert_element_type | solution.py:101
  63.6 1.2 collective-permute-start.8
  64.8 0.0 collective-permute-start.12
  64.8 1.1 collective-permute-done.9
  65.9 0.7 collective-permute-start.13
  66.6 5.4 %collective-permute-done.10 = f16[256,1024]{1,0:T(8,128)(2,1)S(1)} collective-permute-done((f16[256,1024]{1,0:T(8,128)(2,1)S(1)}, f16[256,1024]{1,0:T(8,128)(2,1)S(1)}, u32[]{:S(2)}, u32[]{:S(2)}) %collective-permute-start.10) | collective-permute-done | bytes 524320 | tf_op jit(solution)/shard_map/ppermute | solution.py:28
  72.0 0.0 collective-permute-done.11
  72.0 3.1 %multiply_convert_fusion.4 = (f16[256,1024]{1,0:T(8,128)(2,1)}, f32[256,1024]{1,0:T(8,128)}) fusion(f16[256,1024]{1,0:T(8,128)(2,1)S(1)} %collective-permute-done.9, f32[1536,1024]{1,0:T(8,128)S(1)} %fusion, f32[1,2048,1024]{2,1,0:T(8,128)} %param.4), kind=kLoop, calls=%fused_computation.40 | loop fusion | flops 1835008 | bytes 4194304 | tf_op jit(solution)/shard_map/convert_element_type | solution.py:101
  75.1 1.3 %collective-permute-start.15 = (f16[256,1024]{1,0:T(8,128)(2,1)}, f16[256,1024]{1,0:T(8,128)(2,1)}, u32[]{:S(2)}, u32[]{:S(2)}) collective-permute-start(f16[256,1024]{1,0:T(8,128)(2,1)} %get-tuple-element.123), channel_id=1, source_target_pairs={{0,1},{1,0},{2,3},{3,2},{4,5},{5,4},{6,7},{7,6},{8,9},{9,8},{10,11... | collective-permute-start | bytes 1572872 | tf_op jit(solution)/shard_map/ppermute | solution.py:19
  76.4 1.5 %collective-permute-done.8 = f16[256,1024]{1,0:T(8,128)(2,1)} collective-permute-done((f16[256,1024]{1,0:T(8,128)(2,1)}, f16[256,1024]{1,0:T(8,128)(2,1)}, u32[]{:S(2)}, u32[]{:S(2)}) %collective-permute-start.8) | collective-permute-done | bytes 524320 | tf_op jit(solution)/shard_map/ppermute | solution.py:19
  77.9 5.3 %collective-permute-done.12 = f16[256,1024]{1,0:T(8,128)(2,1)} collective-permute-done((f16[256,1024]{1,0:T(8,128)(2,1)}, f16[256,1024]{1,0:T(8,128)(2,1)}, u32[]{:S(2)}, u32[]{:S(2)}) %collective-permute-start.12) | collective-permute-done | bytes 524320 | tf_op jit(solution)/shard_map/ppermute | solution.py:28
  83.3 3.3 %multiply_convert_fusion.3 = (f16[256,1024]{1,0:T(8,128)(2,1)}, f32[256,1024]{1,0:T(8,128)}) fusion(f16[256,1024]{1,0:T(8,128)(2,1)} %collective-permute-done.8, f32[1536,1024]{1,0:T(8,128)} %copy-done.5, f32[1,2048,1024]{2,1,0:T(8,128)} %param.4), kind=kLoop, calls=%fused_computation.39 | loop fusion | flops 1835008 | bytes 4194304 | tf_op jit(solution)/shard_map/convert_element_type | solution.py:101
  86.5 2.2 %collective-permute-done.15 = f16[256,1024]{1,0:T(8,128)(2,1)} collective-permute-done((f16[256,1024]{1,0:T(8,128)(2,1)}, f16[256,1024]{1,0:T(8,128)(2,1)}, u32[]{:S(2)}, u32[]{:S(2)}) %collective-permute-start.15) | collective-permute-done | bytes 524320 | tf_op jit(solution)/shard_map/ppermute | solution.py:19
  88.8 1.2 collective-permute-start.14
  90.0 0.1 fusion.25
  90.1 0.7 fusion.43
  93.2 1.2 %collective-permute-done.16 = f16[256,1024]{1,0:T(8,128)(2,1)} collective-permute-done((f16[256,1024]{1,0:T(8,128)(2,1)}, f16[256,1024]{1,0:T(8,128)(2,1)}, u32[]{:S(2)}, u32[]{:S(2)}) %collective-permute-start.16) | collective-permute-done | bytes 524320 | tf_op jit(solution)/shard_map/ppermute | solution.py:28
  94.5 2.1 %multiply_convert_fusion.2 = (f16[256,1024]{1,0:T(8,128)(2,1)S(1)}, f32[256,1024]{1,0:T(8,128)S(1)}) fusion(f16[256,1024]{1,0:T(8,128)(2,1)} %collective-permute-done.15, f32[1536,1024]{1,0:T(8,128)} %copy-done.5, f32[1,2048,1024]{2,1,0:T(8,128)} %param.4), kind=kLoop, calls=%fused_computation.38 | loop fusion | flops 1835008 | bytes 4194304 | tf_op jit(solution)/shard_map/convert_element_type | solution.py:101
  96.6 0.1 collective-permute-start.20
  96.7 0.1 collective-permute-start.21
  96.7 6.0 %collective-permute-done.14 = f16[256,1024]{1,0:T(8,128)(2,1)} collective-permute-done((f16[256,1024]{1,0:T(8,128)(2,1)S(1)}, f16[256,1024]{1,0:T(8,128)(2,1)}, u32[]{:S(2)}, u32[]{:S(2)}) %collective-permute-start.14) | collective-permute-done | bytes 524320 | tf_op jit(solution)/shard_map/ppermute | solution.py:19
  102.7 2.1 %multiply_convert_fusion.1 = (f16[256,1024]{1,0:T(8,128)(2,1)S(1)}, f32[256,1024]{1,0:T(8,128)S(1)}) fusion(f16[256,1024]{1,0:T(8,128)(2,1)} %collective-permute-done.14, f32[1536,1024]{1,0:T(8,128)} %copy-done.5, f32[1,2048,1024]{2,1,0:T(8,128)} %param.4), kind=kLoop, calls=%fused_computation.37 | loop fusion | flops 1835008 | bytes 4194304 | tf_op jit(solution)/shard_map/convert_element_type | solution.py:101
  104.8 0.6 collective-permute-start.22
  105.4 2.1 %multiply_add_fusion = f32[256,1024]{1,0:T(8,128)S(1)} fusion(f16[256,1024]{1,0:T(8,128)(2,1)S(1)} %collective-permute-done.3, f32[256,1024]{1,0:T(8,128)S(1)} %get-tuple-element.134, f16[256,1024]{1,0:T(8,128)(2,1)} %collective-permute-done.4, f32[]{:T(128)S(6)} %div.43, f32[]{:T(128)} %bitcast.18, f32[]{:T(128)S(6)} %div.34), kind=kLoop, calls=%fused_computation.36 | loop fusion | flops 1835008 | bytes 3145740 | tf_op jit(solution)/shard_map/add | solution.py:117
  107.5 1.1 pad_bitcast_fusion
  108.6 1.0 bitcast_dynamic-update-slice_fusion.6
  109.7 0.0 copy-start.1
  109.7 1.1 bitcast_dynamic-update-slice_fusion.5
  110.8 2.2 %bitcast_dynamic-update-slice_fusion.4 = f32[1,2048,1024]{2,1,0:T(8,128)S(1)} fusion(f32[1,2048,1024]{2,1,0:T(8,128)S(1)} %bitcast_dynamic-update-slice_fusion.5, f16[256,1024]{1,0:T(8,128)(2,1)} %collective-permute-done.12, f32[256,1024]{1,0:T(8,128)S(1)} %copy-done.8, f16[256,1024]{1,0:T(8,128)(2,1)} %collective-permute-done.13, f32[]{:T(128)S(6)} %div.43, ...), kind=kLoop, calls=%fused_computation.25 | loop fusion | flops 1835008 | bytes 3145740 | tf_op jit(solution)/shard_map/dynamic_update_slice | solution.py:121
  113.0 2.2 %bitcast_dynamic-update-slice_fusion.3 = f32[1,2048,1024]{2,1,0:T(8,128)S(1)} fusion(f32[1,2048,1024]{2,1,0:T(8,128)S(1)} %bitcast_dynamic-update-slice_fusion.4, f16[256,1024]{1,0:T(8,128)(2,1)} %collective-permute-done.16, f32[256,1024]{1,0:T(8,128)S(1)} %copy-done.9, f16[256,1024]{1,0:T(8,128)(2,1)} %collective-permute-done.17, f32[]{:T(128)S(6)} %div.43, ...), kind=kLoop, calls=%fused_computation.24 | loop fusion | flops 1835008 | bytes 3145740 | tf_op jit(solution)/shard_map/dynamic_update_slice | solution.py:121
  115.2 2.2 %bitcast_dynamic-update-slice_fusion.2 = f32[1,2048,1024]{2,1,0:T(8,128)S(1)} fusion(f32[1,2048,1024]{2,1,0:T(8,128)S(1)} %bitcast_dynamic-update-slice_fusion.3, f16[256,1024]{1,0:T(8,128)(2,1)} %collective-permute-done.18, f32[256,1024]{1,0:T(8,128)S(1)} %copy-done.10, f16[256,1024]{1,0:T(8,128)(2,1)} %collective-permute-done.19, f32[]{:T(128)S(6)} %div.43, ...), kind=kLoop, calls=%fused_computation.23 | loop fusion | flops 1835008 | bytes 3145740 | tf_op jit(solution)/shard_map/dynamic_update_slice | solution.py:121
  117.3 1.0 bitcast_dynamic-update-slice_fusion.1
  118.3 0.0 copy-start.2
  118.3 3.9 %collective-permute-done.23 = f16[256,1024]{1,0:T(8,128)(2,1)S(1)} collective-permute-done((f16[256,1024]{1,0:T(8,128)(2,1)S(1)}, f16[256,1024]{1,0:T(8,128)(2,1)S(1)}, u32[]{:S(2)}, u32[]{:S(2)}) %collective-permute-start.23) | collective-permute-done | bytes 524320 | tf_op jit(solution)/shard_map/ppermute | solution.py:28
  122.2 1.9 %bitcast_dynamic-update-slice_fusion = f32[1,2048,1024]{2,1,0:T(8,128)} fusion(f32[1,2048,1024]{2,1,0:T(8,128)} %copy-done.2, f16[256,1024]{1,0:T(8,128)(2,1)S(1)} %collective-permute-done.23, f32[256,1024]{1,0:T(8,128)S(1)} %get-tuple-element.154, f16[256,1024]{1,0:T(8,128)(2,1)S(1)} %collective-permute-done.22, f32[]{:T(128)S(6)} %div.43, f32[]{:T(128)} %bitcast.18, ...), kind=kLoop, calls=%fused_computation.21 | loop fusion | flops 1835008 | bytes 3146248 | tf_op jit(solution)/shard_map/dynamic_update_slice | solution.py:121
  (51 shorter events, 0.1 us)
Async XLA Ops:
  0.0 1.5 %copy-start = (bf16[1,896,1024]{2,1,0:T(8,128)(2,1)S(1)}, bf16[1,896,1024]{2,1,0:T(8,128)(2,1)}, u32[]{:S(2)}) copy-start(bf16[1,896,1024]{2,1,0:T(8,128)(2,1)} %param.6) | copy-start | bytes 5505028
  3.3 17.8 %collective-permute-start = (f16[256,1024]{1,0:T(8,128)(2,1)S(1)}, f16[256,1024]{1,0:T(8,128)(2,1)S(1)}, u32[]{:S(2)}, u32[]{:S(2)}) collective-permute-start(f16[256,1024]{1,0:T(8,128)(2,1)S(1)} %fusion.22), channel_id=1, source_target_pairs={{0,1},{1,0},{2,3},{3,2},{4,5},{5,4},{6,7},{7,6},{8,9},{9,8},{10,11... | collective-permute-start | bytes 1572872 | tf_op jit(solution)/shard_map/ppermute | solution.py:19
  7.9 28.3 %collective-permute-start.2 = (f16[256,1024]{1,0:T(8,128)(2,1)}, f16[256,1024]{1,0:T(8,128)(2,1)}, u32[]{:S(2)}, u32[]{:S(2)}) collective-permute-start(f16[256,1024]{1,0:T(8,128)(2,1)} %fusion.19), channel_id=1, source_target_pairs={{0,1},{1,0},{2,3},{3,2},{4,5},{5,4},{6,7},{7,6},{8,9},{9,8},{10,11... | collective-permute-start | bytes 1572872 | tf_op jit(solution)/shard_map/ppermute | solution.py:19
  21.0 1.3 %copy-start.3 = (f32[512,1024]{1,0:T(8,128)}, f32[512,1024]{1,0:T(8,128)S(1)}, u32[]{:S(2)}) copy-start(f32[512,1024]{1,0:T(8,128)S(1)} %fusion.8) | copy-start | bytes 6291460
  24.7 19.9 %collective-permute-start.3 = (f16[256,1024]{1,0:T(8,128)(2,1)}, f16[256,1024]{1,0:T(8,128)(2,1)S(1)}, u32[]{:S(2)}, u32[]{:S(2)}) collective-permute-start(f16[256,1024]{1,0:T(8,128)(2,1)} %get-tuple-element.92), channel_id=1, source_target_pairs={{2,4},{4,2},{6,8},{8,6},{10,12},{12,10},{14,16},{16,14},{18,20},{2... | collective-permute-start | bytes 1572872 | tf_op jit(solution)/shard_map/ppermute | solution.py:28
  27.3 17.4 %collective-permute-start.4 = (f16[256,1024]{1,0:T(8,128)(2,1)}, f16[256,1024]{1,0:T(8,128)(2,1)}, u32[]{:S(2)}, u32[]{:S(2)}) collective-permute-start(f16[256,1024]{1,0:T(8,128)(2,1)} %get-tuple-element.92), channel_id=1, source_target_pairs={{0,2},{2,0},{4,6},{6,4},{8,10},{10,8},{12,14},{14,12},{16,18},{18,... | collective-permute-start | bytes 1572872 | tf_op jit(solution)/shard_map/ppermute | solution.py:28
  29.6 13.9 %collective-permute-start.1 = (f16[256,1024]{1,0:T(8,128)(2,1)}, f16[256,1024]{1,0:T(8,128)(2,1)}, u32[]{:S(2)}, u32[]{:S(2)}) collective-permute-start(f16[256,1024]{1,0:T(8,128)(2,1)} %get-tuple-element.85), channel_id=1, source_target_pairs={{0,1},{1,0},{2,3},{3,2},{4,5},{5,4},{6,7},{7,6},{8,9},{9,8},{10,11... | collective-permute-start | bytes 1572872 | tf_op jit(solution)/shard_map/ppermute | solution.py:19
  30.8 5.5 %copy-start.4 = (f32[512,1024]{1,0:T(8,128)S(1)}, f32[512,1024]{1,0:T(8,128)}, u32[]{:S(2)}) copy-start(f32[512,1024]{1,0:T(8,128)} %copy-done.3) | copy-start | bytes 6291460
  30.8 9.5 %copy-start.19 = (f16[256,1024]{1,0:T(8,128)(2,1)S(1)}, f16[256,1024]{1,0:T(8,128)(2,1)}, u32[]{:S(2)}) copy-start(f16[256,1024]{1,0:T(8,128)(2,1)} %get-tuple-element.100) | copy-start | bytes 1572868
  36.3 38.9 %copy-start.5 = (f32[1536,1024]{1,0:T(8,128)}, f32[1536,1024]{1,0:T(8,128)S(1)}, u32[]{:S(2)}) copy-start(f32[1536,1024]{1,0:T(8,128)S(1)} %fusion) | copy-start | bytes 18874372
  36.3 11.0 %copy-start.18 = (f16[256,1024]{1,0:T(8,128)(2,1)S(1)}, f16[256,1024]{1,0:T(8,128)(2,1)}, u32[]{:S(2)}) copy-start(f16[256,1024]{1,0:T(8,128)(2,1)} %get-tuple-element.110) | copy-start | bytes 1572868
  40.3 14.2 %collective-permute-start.5 = (f16[256,1024]{1,0:T(8,128)(2,1)S(1)}, f16[256,1024]{1,0:T(8,128)(2,1)S(1)}, u32[]{:S(2)}, u32[]{:S(2)}) collective-permute-start(f16[256,1024]{1,0:T(8,128)(2,1)S(1)} %copy-done.19), channel_id=1, source_target_pairs={{0,1},{1,0},{2,3},{3,2},{4,5},{5,4},{6,7},{7,6},{8,9},{9,8},{10,11... | collective-permute-start | bytes 1572872 | tf_op jit(solution)/shard_map/ppermute | solution.py:19
  40.5 20.1 %collective-permute-start.6 = (f16[256,1024]{1,0:T(8,128)(2,1)S(1)}, f16[256,1024]{1,0:T(8,128)(2,1)S(1)}, u32[]{:S(2)}, u32[]{:S(2)}) collective-permute-start(f16[256,1024]{1,0:T(8,128)(2,1)S(1)} %get-tuple-element.104), channel_id=1, source_target_pairs={{2,4},{4,2},{6,8},{8,6},{10,12},{12,10},{14,16},{16,14},{18,20},{2... | collective-permute-start | bytes 1572872 | tf_op jit(solution)/shard_map/ppermute | solution.py:28
  43.4 17.3 %collective-permute-start.7 = (f16[256,1024]{1,0:T(8,128)(2,1)S(1)}, f16[256,1024]{1,0:T(8,128)(2,1)S(1)}, u32[]{:S(2)}, u32[]{:S(2)}) collective-permute-start(f16[256,1024]{1,0:T(8,128)(2,1)S(1)} %get-tuple-element.104), channel_id=1, source_target_pairs={{0,2},{2,0},{4,6},{6,4},{8,10},{10,8},{12,14},{14,12},{16,18},{18,... | collective-permute-start | bytes 1572872 | tf_op jit(solution)/shard_map/ppermute | solution.py:28
  47.3 41.5 %copy-start.11 = (f16[256,1024]{1,0:T(8,128)(2,1)S(1)}, f16[256,1024]{1,0:T(8,128)(2,1)}, u32[]{:S(2)}) copy-start(f16[256,1024]{1,0:T(8,128)(2,1)} %get-tuple-element.120) | copy-start | bytes 1572868
  47.3 42.7 %copy-start.20 = (s32[16,3]{0,1:T(4,128)S(1)}, s32[16,3]{0,1:T(4,128)}, u32[]{:S(2)}) copy-start(s32[16,3]{0,1:T(4,128)} %param.7) | copy-start | bytes 580
  47.3 18.6 %collective-permute-start.9 = (f16[256,1024]{1,0:T(8,128)(2,1)S(1)}, f16[256,1024]{1,0:T(8,128)(2,1)S(1)}, u32[]{:S(2)}, u32[]{:S(2)}) collective-permute-start(f16[256,1024]{1,0:T(8,128)(2,1)S(1)} %copy-done.18), channel_id=1, source_target_pairs={{0,1},{1,0},{2,3},{3,2},{4,5},{5,4},{6,7},{7,6},{8,9},{9,8},{10,11... | collective-permute-start | bytes 1572872 | tf_op jit(solution)/shard_map/ppermute | solution.py:19
  48.6 23.4 %collective-permute-start.10 = (f16[256,1024]{1,0:T(8,128)(2,1)S(1)}, f16[256,1024]{1,0:T(8,128)(2,1)S(1)}, u32[]{:S(2)}, u32[]{:S(2)}) collective-permute-start(f16[256,1024]{1,0:T(8,128)(2,1)S(1)} %get-tuple-element.113), channel_id=1, source_target_pairs={{2,4},{4,2},{6,8},{8,6},{10,12},{12,10},{14,16},{16,14},{18,20},{2... | collective-permute-start | bytes 1572872 | tf_op jit(solution)/shard_map/ppermute | solution.py:28
  54.6 17.5 %collective-permute-start.11 = (f16[256,1024]{1,0:T(8,128)(2,1)S(1)}, f16[256,1024]{1,0:T(8,128)(2,1)S(1)}, u32[]{:S(2)}, u32[]{:S(2)}) collective-permute-start(f16[256,1024]{1,0:T(8,128)(2,1)S(1)} %get-tuple-element.113), channel_id=1, source_target_pairs={{0,2},{2,0},{4,6},{6,4},{8,10},{10,8},{12,14},{14,12},{16,18},{18,... | collective-permute-start | bytes 1572872 | tf_op jit(solution)/shard_map/ppermute | solution.py:28
  60.7 35.9 %copy-start.12 = (f16[256,1024]{1,0:T(8,128)(2,1)}, f16[256,1024]{1,0:T(8,128)(2,1)S(1)}, u32[]{:S(2)}) copy-start(f16[256,1024]{1,0:T(8,128)(2,1)S(1)} %collective-permute-done.7) | copy-start | bytes 1572868
  63.6 14.3 %collective-permute-start.8 = (f16[256,1024]{1,0:T(8,128)(2,1)}, f16[256,1024]{1,0:T(8,128)(2,1)}, u32[]{:S(2)}, u32[]{:S(2)}) collective-permute-start(f16[256,1024]{1,0:T(8,128)(2,1)} %get-tuple-element.107), channel_id=1, source_target_pairs={{0,1},{1,0},{2,3},{3,2},{4,5},{5,4},{6,7},{7,6},{8,9},{9,8},{10,11... | collective-permute-start | bytes 1572872 | tf_op jit(solution)/shard_map/ppermute | solution.py:19
  64.8 18.4 %collective-permute-start.12 = (f16[256,1024]{1,0:T(8,128)(2,1)}, f16[256,1024]{1,0:T(8,128)(2,1)}, u32[]{:S(2)}, u32[]{:S(2)}) collective-permute-start(f16[256,1024]{1,0:T(8,128)(2,1)} %get-tuple-element.117), channel_id=1, source_target_pairs={{2,4},{4,2},{6,8},{8,6},{10,12},{12,10},{14,16},{16,14},{18,20},{2... | collective-permute-start | bytes 1572872 | tf_op jit(solution)/shard_map/ppermute | solution.py:28
  65.9 17.4 %collective-permute-start.13 = (f16[256,1024]{1,0:T(8,128)(2,1)}, f16[256,1024]{1,0:T(8,128)(2,1)}, u32[]{:S(2)}, u32[]{:S(2)}) collective-permute-start(f16[256,1024]{1,0:T(8,128)(2,1)} %get-tuple-element.117), channel_id=1, source_target_pairs={{0,2},{2,0},{4,6},{6,4},{8,10},{10,8},{12,14},{14,12},{16,18},{18,... | collective-permute-start | bytes 1572872 | tf_op jit(solution)/shard_map/ppermute | solution.py:28
  72.0 3.1 %copy-start.14 = (f16[256,1024]{1,0:T(8,128)(2,1)}, f16[256,1024]{1,0:T(8,128)(2,1)S(1)}, u32[]{:S(2)}) copy-start(f16[256,1024]{1,0:T(8,128)(2,1)S(1)} %collective-permute-done.10) | copy-start | bytes 1572868
  72.0 3.1 %copy-start.16 = (f16[256,1024]{1,0:T(8,128)(2,1)}, f16[256,1024]{1,0:T(8,128)(2,1)S(1)}, u32[]{:S(2)}) copy-start(f16[256,1024]{1,0:T(8,128)(2,1)S(1)} %collective-permute-done.11) | copy-start | bytes 1572868
  75.1 13.6 %collective-permute-start.15 = (f16[256,1024]{1,0:T(8,128)(2,1)}, f16[256,1024]{1,0:T(8,128)(2,1)}, u32[]{:S(2)}, u32[]{:S(2)}) collective-permute-start(f16[256,1024]{1,0:T(8,128)(2,1)} %get-tuple-element.123), channel_id=1, source_target_pairs={{0,1},{1,0},{2,3},{3,2},{4,5},{5,4},{6,7},{7,6},{8,9},{9,8},{10,11... | collective-permute-start | bytes 1572872 | tf_op jit(solution)/shard_map/ppermute | solution.py:19
  76.4 18.1 %collective-permute-start.16 = (f16[256,1024]{1,0:T(8,128)(2,1)}, f16[256,1024]{1,0:T(8,128)(2,1)}, u32[]{:S(2)}, u32[]{:S(2)}) collective-permute-start(f16[256,1024]{1,0:T(8,128)(2,1)} %get-tuple-element.126), channel_id=1, source_target_pairs={{2,4},{4,2},{6,8},{8,6},{10,12},{12,10},{14,16},{16,14},{18,20},{2... | collective-permute-start | bytes 1572872 | tf_op jit(solution)/shard_map/ppermute | solution.py:28
  77.9 16.6 %collective-permute-start.17 = (f16[256,1024]{1,0:T(8,128)(2,1)}, f16[256,1024]{1,0:T(8,128)(2,1)}, u32[]{:S(2)}, u32[]{:S(2)}) collective-permute-start(f16[256,1024]{1,0:T(8,128)(2,1)} %get-tuple-element.126), channel_id=1, source_target_pairs={{0,2},{2,0},{4,6},{6,4},{8,10},{10,8},{12,14},{14,12},{16,18},{18,... | collective-permute-start | bytes 1572872 | tf_op jit(solution)/shard_map/ppermute | solution.py:28
  86.5 16.2 %collective-permute-start.18 = (f16[256,1024]{1,0:T(8,128)(2,1)}, f16[256,1024]{1,0:T(8,128)(2,1)}, u32[]{:S(2)}, u32[]{:S(2)}) collective-permute-start(f16[256,1024]{1,0:T(8,128)(2,1)} %get-tuple-element.130), channel_id=1, source_target_pairs={{2,4},{4,2},{6,8},{8,6},{10,12},{12,10},{14,16},{16,14},{18,20},{2... | collective-permute-start | bytes 1572872 | tf_op jit(solution)/shard_map/ppermute | solution.py:28
  86.5 16.2 %collective-permute-start.19 = (f16[256,1024]{1,0:T(8,128)(2,1)}, f16[256,1024]{1,0:T(8,128)(2,1)}, u32[]{:S(2)}, u32[]{:S(2)}) collective-permute-start(f16[256,1024]{1,0:T(8,128)(2,1)} %get-tuple-element.130), channel_id=1, source_target_pairs={{0,2},{2,0},{4,6},{6,4},{8,10},{10,8},{12,14},{14,12},{16,18},{18,... | collective-permute-start | bytes 1572872 | tf_op jit(solution)/shard_map/ppermute | solution.py:28
  88.8 13.9 %collective-permute-start.14 = (f16[256,1024]{1,0:T(8,128)(2,1)S(1)}, f16[256,1024]{1,0:T(8,128)(2,1)}, u32[]{:S(2)}, u32[]{:S(2)}) collective-permute-start(f16[256,1024]{1,0:T(8,128)(2,1)S(1)} %copy-done.11), channel_id=1, source_target_pairs={{0,1},{1,0},{2,3},{3,2},{4,5},{5,4},{6,7},{7,6},{8,9},{9,8},{10,11... | collective-permute-start | bytes 1572872 | tf_op jit(solution)/shard_map/ppermute | solution.py:19
  96.6 20.7 %collective-permute-start.20 = (f16[256,1024]{1,0:T(8,128)(2,1)S(1)}, f16[256,1024]{1,0:T(8,128)(2,1)S(1)}, u32[]{:S(2)}, u32[]{:S(2)}) collective-permute-start(f16[256,1024]{1,0:T(8,128)(2,1)S(1)} %get-tuple-element.151), channel_id=1, source_target_pairs={{0,2},{2,0},{4,6},{6,4},{8,10},{10,8},{12,14},{14,12},{16,18},{18,... | collective-permute-start | bytes 1572872 | tf_op jit(solution)/shard_map/ppermute | solution.py:28
  96.7 20.7 %collective-permute-start.21 = (f16[256,1024]{1,0:T(8,128)(2,1)S(1)}, f16[256,1024]{1,0:T(8,128)(2,1)S(1)}, u32[]{:S(2)}, u32[]{:S(2)}) collective-permute-start(f16[256,1024]{1,0:T(8,128)(2,1)S(1)} %get-tuple-element.151), channel_id=1, source_target_pairs={{2,4},{4,2},{6,8},{8,6},{10,12},{12,10},{14,16},{16,14},{18,20},{2... | collective-permute-start | bytes 1572872 | tf_op jit(solution)/shard_map/ppermute | solution.py:28
  104.8 3.8 %copy-start.6 = (f32[256,1024]{1,0:T(8,128)S(1)}, f32[256,1024]{1,0:T(8,128)}, u32[]{:S(2)}) copy-start(f32[256,1024]{1,0:T(8,128)} %get-tuple-element.137) | copy-start | bytes 3145732
  104.8 3.8 %copy-start.13 = (f16[256,1024]{1,0:T(8,128)(2,1)S(1)}, f16[256,1024]{1,0:T(8,128)(2,1)}, u32[]{:S(2)}) copy-start(f16[256,1024]{1,0:T(8,128)(2,1)} %copy-done.12) | copy-start | bytes 1572868
  104.8 13.5 %collective-permute-start.22 = (f16[256,1024]{1,0:T(8,128)(2,1)S(1)}, f16[256,1024]{1,0:T(8,128)(2,1)S(1)}, u32[]{:S(2)}, u32[]{:S(2)}) collective-permute-start(f16[256,1024]{1,0:T(8,128)(2,1)S(1)} %get-tuple-element.153), channel_id=1, source_target_pairs={{0,2},{2,0},{4,6},{6,4},{8,10},{10,8},{12,14},{14,12},{16,18},{18,... | collective-permute-start | bytes 1572872 | tf_op jit(solution)/shard_map/ppermute | solution.py:28
  105.4 16.8 %collective-permute-start.23 = (f16[256,1024]{1,0:T(8,128)(2,1)S(1)}, f16[256,1024]{1,0:T(8,128)(2,1)S(1)}, u32[]{:S(2)}, u32[]{:S(2)}) collective-permute-start(f16[256,1024]{1,0:T(8,128)(2,1)S(1)} %get-tuple-element.153), channel_id=1, source_target_pairs={{2,4},{4,2},{6,8},{8,6},{10,12},{12,10},{14,16},{16,14},{18,20},{2... | collective-permute-start | bytes 1572872 | tf_op jit(solution)/shard_map/ppermute | solution.py:28
  105.4 4.3 %copy-start.7 = (f32[256,1024]{1,0:T(8,128)S(1)}, f32[256,1024]{1,0:T(8,128)}, u32[]{:S(2)}) copy-start(f32[256,1024]{1,0:T(8,128)} %get-tuple-element.140) | copy-start | bytes 3145732
  105.4 4.3 %copy-start.15 = (f16[256,1024]{1,0:T(8,128)(2,1)S(1)}, f16[256,1024]{1,0:T(8,128)(2,1)}, u32[]{:S(2)}) copy-start(f16[256,1024]{1,0:T(8,128)(2,1)} %copy-done.14) | copy-start | bytes 1572868
  105.4 4.3 %copy-start.17 = (f16[256,1024]{1,0:T(8,128)(2,1)S(1)}, f16[256,1024]{1,0:T(8,128)(2,1)}, u32[]{:S(2)}) copy-start(f16[256,1024]{1,0:T(8,128)(2,1)} %copy-done.16) | copy-start | bytes 1572868
  107.5 3.3 %copy-start.8 = (f32[256,1024]{1,0:T(8,128)S(1)}, f32[256,1024]{1,0:T(8,128)}, u32[]{:S(2)}) copy-start(f32[256,1024]{1,0:T(8,128)} %get-tuple-element.143) | copy-start | bytes 3145732
  107.5 5.4 %copy-start.9 = (f32[256,1024]{1,0:T(8,128)S(1)}, f32[256,1024]{1,0:T(8,128)}, u32[]{:S(2)}) copy-start(f32[256,1024]{1,0:T(8,128)} %get-tuple-element.146) | copy-start | bytes 3145732
  108.6 6.5 %copy-start.10 = (f32[256,1024]{1,0:T(8,128)S(1)}, f32[256,1024]{1,0:T(8,128)}, u32[]{:S(2)}) copy-start(f32[256,1024]{1,0:T(8,128)} %get-tuple-element.149) | copy-start | bytes 3145732
  109.7 14.4 %copy-start.1 = (bf16[1,896,1024]{2,1,0:T(8,128)(2,1)S(1)}, bf16[1,896,1024]{2,1,0:T(8,128)(2,1)}, u32[]{:S(2)}) copy-start(bf16[1,896,1024]{2,1,0:T(8,128)(2,1)} %param.6) | copy-start | bytes 5505028
  118.3 3.9 %copy-start.2 = (f32[1,2048,1024]{2,1,0:T(8,128)}, f32[1,2048,1024]{2,1,0:T(8,128)S(1)}, u32[]{:S(2)}) copy-start(f32[1,2048,1024]{2,1,0:T(8,128)S(1)} %bitcast_dynamic-update-slice_fusion.1) | copy-start | bytes 25165828

commit v5 on v2

v5 whole, which is shorter than its diff:
```python
import functools
import math

import jax
import jax.numpy as jnp
from jax import lax
from jax.experimental import pallas as pl
from jax.experimental.pallas import tpu as pltpu
from jax.sharding import PartitionSpec as P

MIX_DENOM = 64
RATE = 0.03
LARGEST = 6.0
WIRE = jnp.float16
STEP = 256
TILE = 256
AHEAD = 2
EARLY = 3


def from_behind(value, axis, steps):
    count = lax.axis_size(axis)
    pairs = [(source, (source + steps) % count) for source in range(count)]
    return lax.ppermute(value, axis, pairs)


def swapped(value, axis, first):
    count = lax.axis_size(axis)
    pairs = []
    for source in range(first, count, 2):
        partner = (source + 1) % count
        pairs += [(source, partner), (partner, source)]
    return lax.ppermute(value, axis, pairs)


def wire_scale(tokens):
    bound = LARGEST + RATE * LARGEST * LARGEST * tokens
    return 2.0 ** math.floor(math.log2(float(jnp.finfo(WIRE).max) / bound))


def product_kernel(factor, offset_ref, features_ref, cot_ref, *rest):
    product = factor * lax.dot_general(
        features_ref[...], cot_ref[...], (((0,), (0,)), ((), ())), preferred_element_type=jnp.float32
    )
    out_ref = rest[-1]
    out_ref[...] = product if len(rest) == 1 else rest[0][...] + product


def product(features, cot, start, size, factor, added=None):
    tokens, width = cot.shape
    tile = math.gcd(size, TILE)
    by_rows = pl.BlockSpec((tile, width), lambda i, offset: (i, 0))
    specs = [
        pl.BlockSpec((tokens, tile), lambda i, offset: (0, offset[0] + i)),
        pl.BlockSpec((tokens, width), lambda i, offset: (0, 0)),
    ]
    operands = [features, cot]
    if added is not None:
        specs.append(by_rows)
        operands.append(added)
    return pl.pallas_call(
        functools.partial(product_kernel, factor),
        grid_spec=pltpu.PrefetchScalarGridSpec(
            num_scalar_prefetch=1, grid=(size // tile,), in_specs=specs, out_specs=by_rows
        ),
        out_shape=jax.ShapeDtypeStruct((size, width), jnp.float32),
        compiler_params=pltpu.CompilerParams(vmem_limit_bytes=24 * 2**20),
        cost_estimate=pl.CostEstimate(flops=0, bytes_accessed=0, transcendentals=0),
    )(jnp.reshape(start // tile, (1,)), *operands)


def on_device(params, inputs, cotangent, mix):
    weights = params[0]
    features = inputs[0]
    cot_local = cotangent[0]
    rows = weights.shape[0]
    shards = lax.axis_size("fsdp")
    scale = wire_scale(features.shape[0] * shards)
    replica = lax.axis_index("blk")
    shard = lax.axis_index("fsdp")
    pick = (jnp.arange(lax.axis_size("blk")) == replica).astype(jnp.float32)
    coeff = jnp.dot(pick, mix.astype(jnp.float32), precision=lax.Precision.HIGHEST) / MIX_DENOM
    even = replica % 2 == 0
    c_self = coeff[1]
    c_near = jnp.where(even, coeff[2], coeff[0]) / scale
    c_far = jnp.where(even, coeff[0], coeff[2]) / scale
    step = math.gcd(rows, STEP)
    chunks = rows // step
    early = min(EARLY, chunks)

    def rows_of(value, chunk):
        return value[chunk * step:(chunk + 1) * step]

    def for_others(shard, first, count):
        return [
            product(
                features, cot_local, lax.rem(shard + away, shards) * rows + first * step,
                count * step, RATE * scale,
            )
            for away in range(1, shards)
        ]

    def send_terms(made, place):
        return [
            from_behind(rows_of(term, place).astype(WIRE), "fsdp", away)
            for away, term in zip(range(1, shards), made)
        ]

    def u_of(chunk):
        total = rows_of(base, chunk)
        for term in arrived[chunk]:
            total = total - term.astype(jnp.float32) / scale
        return total

    def mix_into(out, chunk):
        mixed = (
            c_near * near[chunk].astype(jnp.float32)
            + c_self * u_of(chunk)
            + c_far * far[chunk].astype(jnp.float32)
        )
        return lax.dynamic_update_slice_in_dim(out, mixed, chunk * step, axis=0)

    near = {}
    far = {}
    made = for_others(shard, 0, early)
    arrived = {chunk: send_terms(made, chunk) for chunk in range(min(AHEAD, chunks))}
    made, later = lax.optimization_barrier((made, shard))
    base = product(features, cot_local, later * rows, rows, -RATE, weights)

    arrived[0], base = lax.optimization_barrier((arrived[0], base))
    for chunk in range(chunks):
        if chunk == 1 and early < chunks:
            arrived[1], rest = lax.optimization_barrier((arrived[1], rest))
        if chunk >= 2:
            arrived[chunk], far[chunk - 2], near[chunk - 2] = lax.optimization_barrier(
                (arrived[chunk], far[chunk - 2], near[chunk - 2])
            )
        sent = (u_of(chunk) * scale).astype(WIRE)
        sent, base, made, later = lax.optimization_barrier((sent, base, made, shard))
        if chunk == 0 and early < chunks:
            rest = for_others(later, early, chunks - early)
        after = chunk + AHEAD
        if after < early:
            arrived[after] = send_terms(made, after)
        elif after < chunks:
            rest, sent = lax.optimization_barrier((rest, sent))
            arrived[after] = send_terms(rest, after - early)
        if chunk == chunks - 1:
            far[0], near[0], sent = lax.optimization_barrier((far[0], near[0], sent))
        far[chunk] = swapped(sent, "blk", 1)
        near[chunk] = swapped(sent, "blk", 0)

    out = jnp.zeros_like(weights)
    for chunk in range(chunks):
        out = mix_into(out, chunk)
    return out[None]


def solution(mesh):
    return jax.shard_map(
        on_device,
        mesh=mesh,
        in_specs=(P("blk", "fsdp", None), P("blk", "fsdp", None), P("blk", "fsdp", None), P()),
        out_specs=P("blk", "fsdp", None),
        check_vma=False,
    )
```

time: 127 us -> 144 us (1.13)
  matrix products: 20 us -> 0.12 us
  local copies, waits for them, and re-layouts: 5.89 us -> 25.1 us
  Pallas kernels: 0 us -> 13.1 us
  other arithmetic: 16.4 us -> 24.6 us
  waiting for transfers between devices: 45.1 us -> 41.7 us
    ppermute x16, waiting for transfers between devices: 29 us -> 5.82 us  [swapped(): return lax.ppermute(value, axis, pairs)]
    unnamed x14 -> x52, local copies, waits for them, and re-layouts: 1.54 us -> 22.2 us
    dot_general x4 -> x0, matrix products: 19.9 us -> none  [partial(): lax.dot_general(block, cot_local, (((0,), (0,)), ((), ())), preferred_ele...]
    ppermute x8, waiting for transfers between devices: 16.1 us -> 35.9 us  [from_behind(): return lax.ppermute(value, axis, pairs)]
    pallas_call x0 -> x3, Pallas kernels: none -> 13.1 us  [product(): pl.pallas_call(functools.partial(product_kernel, factor), grid_spec=pltpu...]
    ppermute x16, starting transfers between devices: 30.3 us -> 25.6 us  [swapped(): return lax.ppermute(value, axis, pairs)]
    ppermute x8, starting transfers between devices: 6.22 us -> 9.82 us  [from_behind(): return lax.ppermute(value, axis, pairs)]
    add x0 -> x1, other arithmetic: none -> 2.74 us  [mix_into(): c_near * near[chunk].astype(jnp.float32) + c_self * u_of(chunk)]
  transfers between devices with their start and end apart: 24 -> 24, of which waited for: 10 -> 7; matrix products, arithmetic and copies ran while one was open for 29% -> 17% of each run, Pallas kernels for 0% -> 7%
where the time goes in v5:
time: 144 us; the launch traced here: 143 us
  waiting for transfers between devices  41.7 us (29%)
  starting transfers between devices  35.4 us (25%)
  local copies, waits for them, and re-layouts  25.1 us (17%)
  other arithmetic  24.6 us (17%)
  Pallas kernels  13.1 us (9%)
  between operations  2.94 us (2%)
    ppermute x8, waiting for transfers between devices, from_behind(): return lax.ppermute(value, axis, pairs)  35.9 us
    ppermute x16, starting transfers between devices, swapped(): return lax.ppermute(value, axis, pairs)  25.6 us
    unnamed x52, local copies, waits for them, and re-layouts  22.2 us
    pallas_call x3, Pallas kernels, product(): pl.pallas_call(functools.partial(product_kernel, factor), grid_spec=pltpu...  13.1 us
    dynamic_update_slice x7, other arithmetic, mix_into(): return lax.dynamic_update_slice_in_dim(out, mixed, chunk * step, axis=0)  11.2 us
    ppermute x8, starting transfers between devices, from_behind(): return lax.ppermute(value, axis, pairs)  9.82 us
    convert_element_type x8, other arithmetic, on_device(): sent = (u_of(chunk) * scale).astype(WIRE)  9.05 us
    ppermute x16, waiting for transfers between devices, swapped(): return lax.ppermute(value, axis, pairs)  5.82 us
  transfers between devices with their start and end apart: 24, of which 7 were waited for; matrix products, arithmetic and copies ran while one was open for 17% of the time, Pallas kernels for 7%

profile of v5, /device:TPU:1, one launch (start us, length us, event | category | flops | bytes accessed | tf_op | source)
XLA Modules:
  0.0 143.0 jit_solution(10481595711212587871)
XLA Ops:
  0.0 3.1 %copy-done.1 = bf16[1,896,4096]{2,1,0:T(8,128)(2,1)S(1)} copy-done((bf16[1,896,4096]{2,1,0:T(8,128)(2,1)S(1)}, bf16[1,896,4096]{2,1,0:T(8,128)(2,1)}, u32[]{:S(2)}) %copy-start.1) | copy-done | bytes 7340056
  3.1 1.5 %copy-done.4 = bf16[1,896,1024]{2,1,0:T(8,128)(2,1)S(1)} copy-done((bf16[1,896,1024]{2,1,0:T(8,128)(2,1)S(1)}, bf16[1,896,1024]{2,1,0:T(8,128)(2,1)}, u32[]{:S(2)}) %copy-start.4) | copy-done | bytes 1835032
  4.6 2.5 %shard_map.46 = f32[768,1024]{1,0:T(8,128)S(1)} custom-call(s32[1]{0:T(128)} %bitcast.4.offset_ref, bf16[896,4096]{1,0:T(8,128)(2,1)S(1)} %bitcast.36, bf16[896,1024]{1,0:T(8,128)(2,1)S(1)} %bitcast.39), custom_call_target="tpu_custom_call" | custom-call | tf_op jit(solution)/shard_map/pallas_call | solution.py:61
  7.0 0.3 convert.22
  7.4 1.2 fusion.6
  8.6 2.1 %collective-permute-start = (f16[256,1024]{1,0:T(8,128)(2,1)}, f16[256,1024]{1,0:T(8,128)(2,1)}, u32[]{:S(2)}, u32[]{:S(2)}) collective-permute-start(f16[256,1024]{1,0:T(8,128)(2,1)} %get-tuple-element.116), channel_id=1, source_target_pairs={{0,1},{1,0},{2,3},{3,2},{4,5},{5,4},{6,7},{7,6},{8,9},{9,8},{10,11... | collective-permute-start | bytes 1572872 | tf_op jit(solution)/shard_map/ppermute | solution.py:24
  10.7 3.1 %copy-done.2 = bf16[1,896,4096]{2,1,0:T(8,128)(2,1)S(1)} copy-done((bf16[1,896,4096]{2,1,0:T(8,128)(2,1)S(1)}, bf16[1,896,4096]{2,1,0:T(8,128)(2,1)}, u32[]{:S(2)}) %copy-start.2) | copy-done | bytes 7340056
  13.8 1.5 %copy-done.5 = bf16[1,896,1024]{2,1,0:T(8,128)(2,1)S(1)} copy-done((bf16[1,896,1024]{2,1,0:T(8,128)(2,1)S(1)}, bf16[1,896,1024]{2,1,0:T(8,128)(2,1)}, u32[]{:S(2)}) %copy-start.5) | copy-done | bytes 1835032
  15.3 3.4 %copy-done.7 = f32[1,2048,1024]{2,1,0:T(8,128)S(1)} copy-done((f32[1,2048,1024]{2,1,0:T(8,128)S(1)}, f32[1,2048,1024]{2,1,0:T(8,128)}, u32[]{:S(2)}) %copy-start.7) | copy-done | bytes 8388632
  18.7 6.5 %shard_map.47 = f32[2048,1024]{1,0:T(8,128)S(1)} custom-call(s32[1]{0:T(128)} %bitcast.7.offset_ref, bf16[896,4096]{1,0:T(8,128)(2,1)S(1)} %bitcast.37, bf16[896,1024]{1,0:T(8,128)(2,1)S(1)} %bitcast.40, f32[2048,1024]{1,0:T(8,128)S(1)} %bitcast.42), custom_call_target="tpu_custom_call" | custom-call | tf_op jit(solution)/shard_map/pallas_call | solution.py:61
  25.3 3.4 %copy-done = f32[2048,1024]{1,0:T(8,128)} copy-done((f32[2048,1024]{1,0:T(8,128)}, f32[2048,1024]{1,0:T(8,128)S(1)}, u32[]{:S(2)}) %copy-start) | copy-done | bytes 8388632
  28.6 2.0 %multiply_convert_fusion.7 = f16[256,1024]{1,0:T(8,128)(2,1)} fusion(f16[256,1024]{1,0:T(8,128)(2,1)} %collective-permute-done, f32[2048,1024]{1,0:T(8,128)S(1)} %shard_map.47), kind=kLoop, calls=%fused_computation.31 | loop fusion | flops 1310720 | bytes 2097152 | tf_op jit(solution)/shard_map/convert_element_type | solution.py:138
  30.7 2.5 %collective-permute-start.2 = (f16[256,1024]{1,0:T(8,128)(2,1)}, f16[256,1024]{1,0:T(8,128)(2,1)}, u32[]{:S(2)}, u32[]{:S(2)}) collective-permute-start(f16[256,1024]{1,0:T(8,128)(2,1)} %multiply_convert_fusion.7), channel_id=1, source_target_pairs={{2,4},{4,2},{6,8},{8,6},{10,12},{12,10},{14,16},{16,14},{18,20},{2... | collective-permute-start | bytes 1572872 | tf_op jit(solution)/shard_map/ppermute | solution.py:33
  33.2 2.3 %collective-permute-start.3 = (f16[256,1024]{1,0:T(8,128)(2,1)}, f16[256,1024]{1,0:T(8,128)(2,1)}, u32[]{:S(2)}, u32[]{:S(2)}) collective-permute-start(f16[256,1024]{1,0:T(8,128)(2,1)} %multiply_convert_fusion.7), channel_id=1, source_target_pairs={{0,2},{2,0},{4,6},{6,4},{8,10},{10,8},{12,14},{14,12},{16,18},{18,... | collective-permute-start | bytes 1572872 | tf_op jit(solution)/shard_map/ppermute | solution.py:33
  35.5 3.2 %copy-done.3 = bf16[1,896,4096]{2,1,0:T(8,128)(2,1)S(1)} copy-done((bf16[1,896,4096]{2,1,0:T(8,128)(2,1)S(1)}, bf16[1,896,4096]{2,1,0:T(8,128)(2,1)}, u32[]{:S(2)}) %copy-start.3) | copy-done | bytes 7340056
  38.7 1.6 %copy-done.6 = bf16[1,896,1024]{2,1,0:T(8,128)(2,1)S(1)} copy-done((bf16[1,896,1024]{2,1,0:T(8,128)(2,1)S(1)}, bf16[1,896,1024]{2,1,0:T(8,128)(2,1)}, u32[]{:S(2)}) %copy-start.6) | copy-done | bytes 1835032
  40.4 4.1 %shard_map.48 = f32[1280,1024]{1,0:T(8,128)S(1)} custom-call(s32[1]{0:T(128)} %bitcast.9.offset_ref, bf16[896,4096]{1,0:T(8,128)(2,1)S(1)} %bitcast.38, bf16[896,1024]{1,0:T(8,128)(2,1)S(1)} %bitcast.41), custom_call_target="tpu_custom_call" | custom-call | tf_op jit(solution)/shard_map/pallas_call | solution.py:61
  44.5 0.1 slice_convert_fusion.5
  44.5 1.3 collective-permute-start.1
  45.8 1.2 multiply_convert_fusion.6
  47.2 1.2 collective-permute-start.7
  48.4 0.1 slice_convert_fusion.4
  48.5 9.7 %collective-permute-done.1 = f16[256,1024]{1,0:T(8,128)(2,1)S(1)} collective-permute-done((f16[256,1024]{1,0:T(8,128)(2,1)S(1)}, f16[256,1024]{1,0:T(8,128)(2,1)S(1)}, u32[]{:S(2)}, u32[]{:S(2)}) %collective-permute-start.1) | collective-permute-done | bytes 524320 | tf_op jit(solution)/shard_map/ppermute | solution.py:24
  58.2 1.2 collective-permute-start.5
  59.4 0.2 multiply_convert_fusion.5
  59.6 1.1 collective-permute-start.10
  60.7 0.1 slice_convert_fusion.3
  60.8 10.0 %collective-permute-done.5 = f16[256,1024]{1,0:T(8,128)(2,1)S(1)} collective-permute-done((f16[256,1024]{1,0:T(8,128)(2,1)S(1)}, f16[256,1024]{1,0:T(8,128)(2,1)S(1)}, u32[]{:S(2)}, u32[]{:S(2)}) %collective-permute-start.5) | collective-permute-done | bytes 524320 | tf_op jit(solution)/shard_map/ppermute | solution.py:24
  70.8 1.2 collective-permute-start.8
  72.1 0.2 multiply_convert_fusion.4
  72.3 0.3 collective-permute-start.12
  72.6 0.3 copy-done.9
  72.9 1.9 %collective-permute-start.13 = (f16[256,1024]{1,0:T(8,128)(2,1)S(1)}, f16[256,1024]{1,0:T(8,128)(2,1)S(1)}, u32[]{:S(2)}, u32[]{:S(2)}) collective-permute-start(f16[256,1024]{1,0:T(8,128)(2,1)S(1)} %multiply_convert_fusion.4), channel_id=1, source_target_pairs={{0,2},{2,0},{4,6},{6,4},{8,10},{10,8},{12,14},{14,12},{16,18},{18,... | collective-permute-start | bytes 1572872 | tf_op jit(solution)/shard_map/ppermute | solution.py:33
  74.9 7.7 %collective-permute-done.8 = f16[256,1024]{1,0:T(8,128)(2,1)S(1)} collective-permute-done((f16[256,1024]{1,0:T(8,128)(2,1)S(1)}, f16[256,1024]{1,0:T(8,128)(2,1)S(1)}, u32[]{:S(2)}, u32[]{:S(2)}) %collective-permute-start.8) | collective-permute-done | bytes 524320 | tf_op jit(solution)/shard_map/ppermute | solution.py:24
  82.6 1.2 collective-permute-start.11
  83.8 1.2 multiply_convert_fusion.3
  85.1 0.5 collective-permute-start.15
  85.6 2.3 %collective-permute-start.16 = (f16[256,1024]{1,0:T(8,128)(2,1)}, f16[256,1024]{1,0:T(8,128)(2,1)}, u32[]{:S(2)}, u32[]{:S(2)}) collective-permute-start(f16[256,1024]{1,0:T(8,128)(2,1)} %multiply_convert_fusion.3), channel_id=1, source_target_pairs={{0,2},{2,0},{4,6},{6,4},{8,10},{10,8},{12,14},{14,12},{16,18},{18,... | collective-permute-start | bytes 1572872 | tf_op jit(solution)/shard_map/ppermute | solution.py:33
  88.0 5.4 %collective-permute-done.11 = f16[256,1024]{1,0:T(8,128)(2,1)S(1)} collective-permute-done((f16[256,1024]{1,0:T(8,128)(2,1)S(1)}, f16[256,1024]{1,0:T(8,128)(2,1)S(1)}, u32[]{:S(2)}, u32[]{:S(2)}) %collective-permute-start.11) | collective-permute-done | bytes 524320 | tf_op jit(solution)/shard_map/ppermute | solution.py:24
  93.4 1.3 collective-permute-start.14
  94.8 1.2 multiply_convert_fusion.2
  95.9 1.6 %collective-permute-start.18 = (f16[256,1024]{1,0:T(8,128)(2,1)}, f16[256,1024]{1,0:T(8,128)(2,1)}, u32[]{:S(2)}, u32[]{:S(2)}) collective-permute-start(f16[256,1024]{1,0:T(8,128)(2,1)} %multiply_convert_fusion.2), channel_id=1, source_target_pairs={{2,4},{4,2},{6,8},{8,6},{10,12},{12,10},{14,16},{16,14},{18,20},{2... | collective-permute-start | bytes 1572872 | tf_op jit(solution)/shard_map/ppermute | solution.py:33
  97.5 2.3 %collective-permute-start.19 = (f16[256,1024]{1,0:T(8,128)(2,1)}, f16[256,1024]{1,0:T(8,128)(2,1)}, u32[]{:S(2)}, u32[]{:S(2)}) collective-permute-start(f16[256,1024]{1,0:T(8,128)(2,1)} %multiply_convert_fusion.2), channel_id=1, source_target_pairs={{0,2},{2,0},{4,6},{6,4},{8,10},{10,8},{12,14},{14,12},{16,18},{18,... | collective-permute-start | bytes 1572872 | tf_op jit(solution)/shard_map/ppermute | solution.py:33
  99.9 0.9 slice_convert_fusion
  100.7 3.1 %collective-permute-done.14 = f16[256,1024]{1,0:T(8,128)(2,1)S(1)} collective-permute-done((f16[256,1024]{1,0:T(8,128)(2,1)S(1)}, f16[256,1024]{1,0:T(8,128)(2,1)S(1)}, u32[]{:S(2)}, u32[]{:S(2)}) %collective-permute-start.14) | collective-permute-done | bytes 524320 | tf_op jit(solution)/shard_map/ppermute | solution.py:24
  103.8 1.3 collective-permute-start.17
  105.2 0.1 fusion
  105.3 0.6 fusion.7
  108.5 1.6 %multiply_convert_fusion.1 = f16[256,1024]{1,0:T(8,128)(2,1)S(1)} fusion(f16[256,1024]{1,0:T(8,128)(2,1)S(1)} %collective-permute-done.14, f32[2048,1024]{1,0:T(8,128)} %copy-done), kind=kLoop, calls=%fused_computation.19 | loop fusion | flops 1310720 | bytes 2097152 | tf_op jit(solution)/shard_map/convert_element_type | solution.py:138
  110.1 5.5 %collective-permute-start.20 = (f16[256,1024]{1,0:T(8,128)(2,1)S(1)}, f16[256,1024]{1,0:T(8,128)(2,1)S(1)}, u32[]{:S(2)}, u32[]{:S(2)}) collective-permute-start(f16[256,1024]{1,0:T(8,128)(2,1)S(1)} %multiply_convert_fusion.1), channel_id=1, source_target_pairs={{0,2},{2,0},{4,6},{6,4},{8,10},{10,8},{12,14},{14,12},{16,18},{18,... | collective-permute-start | bytes 1572872 | tf_op jit(solution)/shard_map/ppermute | solution.py:33
  115.6 1.4 %multiply_convert_fusion = f16[256,1024]{1,0:T(8,128)(2,1)S(1)} fusion(f16[256,1024]{1,0:T(8,128)(2,1)S(1)} %collective-permute-done.17, f32[2048,1024]{1,0:T(8,128)} %copy-done), kind=kLoop, calls=%fused_computation.17 | loop fusion | flops 1310720 | bytes 2097152 | tf_op jit(solution)/shard_map/convert_element_type | solution.py:138
  117.0 3.9 %collective-permute-start.22 = (f16[256,1024]{1,0:T(8,128)(2,1)S(1)}, f16[256,1024]{1,0:T(8,128)(2,1)S(1)}, u32[]{:S(2)}, u32[]{:S(2)}) collective-permute-start(f16[256,1024]{1,0:T(8,128)(2,1)S(1)} %multiply_convert_fusion), channel_id=1, source_target_pairs={{0,2},{2,0},{4,6},{6,4},{8,10},{10,8},{12,14},{14,12},{16,18},{18,... | collective-permute-start | bytes 1572872 | tf_op jit(solution)/shard_map/ppermute | solution.py:33
  120.9 2.7 %multiply_add_fusion = f32[256,1024]{1,0:T(8,128)S(1)} fusion(f16[256,1024]{1,0:T(8,128)(2,1)} %collective-permute-done.2, f32[2048,1024]{1,0:T(8,128)} %copy-done, f16[256,1024]{1,0:T(8,128)(2,1)} %collective-permute-done.3, f16[256,1024]{1,0:T(8,128)(2,1)} %collective-permute-done, f32[]{:T(128)S(6)} %div.82, f32[]{:T(128)} %bitcast.10, f32[]{:T(128)S(6)} %div.64), kind=kLoop, calls=%fused_computation.16 | loop fusion | flops 2621440 | bytes 3670028 | tf_op jit(solution)/shard_map/add | solution.py:117
  123.7 1.1 pad_bitcast_fusion
  124.8 1.1 slice-done.3
  125.8 2.0 %bitcast_dynamic-update-slice_fusion.6 = f32[1,2048,1024]{2,1,0:T(8,128)S(1)} fusion(f32[1,2048,1024]{2,1,0:T(8,128)S(1)} %pad_bitcast_fusion, f16[256,1024]{1,0:T(8,128)(2,1)S(1)} %copy-done.10, f32[2048,1024]{1,0:T(8,128)S(1)} %bitcast.35, f16[256,1024]{1,0:T(8,128)(2,1)S(1)} %copy-done.12, f16[256,1024]{1,0:T(8,128)(2,1)} %collective-permute-done.4, ...), kind=kLoop, calls=%fused_computation.15 | loop fusion | flops 2621440 | bytes 3670028 | tf_op jit(solution)/shard_map/dynamic_update_slice | solution.py:121
  127.9 1.0 bitcast_dynamic-update-slice_fusion.5
  128.9 1.0 bitcast_dynamic-update-slice_fusion.4
  129.9 2.2 %bitcast_dynamic-update-slice_fusion.3 = f32[1,2048,1024]{2,1,0:T(8,128)S(1)} fusion(f32[1,2048,1024]{2,1,0:T(8,128)S(1)} %bitcast_dynamic-update-slice_fusion.4, f16[256,1024]{1,0:T(8,128)(2,1)} %collective-permute-done.15, f32[2048,1024]{1,0:T(8,128)S(1)} %bitcast.35, f16[256,1024]{1,0:T(8,128)(2,1)} %collective-permute-done.16, ...), kind=kLoop, calls=%fused_computation.12 | loop fusion | flops 2621440 | bytes 3670028 | tf_op jit(solution)/shard_map/dynamic_update_slice | solution.py:121
  132.0 2.2 %bitcast_dynamic-update-slice_fusion.2 = f32[1,2048,1024]{2,1,0:T(8,128)S(1)} fusion(f32[1,2048,1024]{2,1,0:T(8,128)S(1)} %bitcast_dynamic-update-slice_fusion.3, f16[256,1024]{1,0:T(8,128)(2,1)} %collective-permute-done.18, f32[2048,1024]{1,0:T(8,128)S(1)} %bitcast.35, f16[256,1024]{1,0:T(8,128)(2,1)} %collective-permute-done.19, ...), kind=kLoop, calls=%fused_computation.11 | loop fusion | flops 2621440 | bytes 3670028 | tf_op jit(solution)/shard_map/dynamic_update_slice | solution.py:121
  134.2 1.2 collective-permute-done.21
  135.4 1.0 bitcast_dynamic-update-slice_fusion.1
  136.4 4.6 %collective-permute-done.23 = f16[256,1024]{1,0:T(8,128)(2,1)S(1)} collective-permute-done((f16[256,1024]{1,0:T(8,128)(2,1)S(1)}, f16[256,1024]{1,0:T(8,128)(2,1)S(1)}, u32[]{:S(2)}, u32[]{:S(2)}) %collective-permute-start.23) | collective-permute-done | bytes 524320 | tf_op jit(solution)/shard_map/ppermute | solution.py:33
  141.0 1.9 %bitcast_dynamic-update-slice_fusion = f32[1,2048,1024]{2,1,0:T(8,128)} fusion(f32[1,2048,1024]{2,1,0:T(8,128)} %copy-done.8, f16[256,1024]{1,0:T(8,128)(2,1)S(1)} %collective-permute-done.23, f32[2048,1024]{1,0:T(8,128)S(1)} %bitcast.35, f16[256,1024]{1,0:T(8,128)(2,1)S(1)} %collective-permute-done.22, f16[256,1024]{1,0:T(8,128)(2,1)S(1)} %collective-permute-done.17, ...), kind=kLoop, calls=%fused_computation.9 | loop fusion | flops 2621440 | bytes 3670536 | tf_op jit(solution)/shard_map/dynamic_update_slice | solution.py:121
  (68 shorter events, 0.4 us)
Async XLA Ops:
  0.0 3.1 %copy-start.1 = (bf16[1,896,4096]{2,1,0:T(8,128)(2,1)S(1)}, bf16[1,896,4096]{2,1,0:T(8,128)(2,1)}, u32[]{:S(2)}) copy-start(bf16[1,896,4096]{2,1,0:T(8,128)(2,1)} %param.5) | copy-start | bytes 22020100
  3.1 1.5 %copy-start.4 = (bf16[1,896,1024]{2,1,0:T(8,128)(2,1)S(1)}, bf16[1,896,1024]{2,1,0:T(8,128)(2,1)}, u32[]{:S(2)}) copy-start(bf16[1,896,1024]{2,1,0:T(8,128)(2,1)} %param.6) | copy-start | bytes 5505028
  8.6 16.6 %collective-permute-start = (f16[256,1024]{1,0:T(8,128)(2,1)}, f16[256,1024]{1,0:T(8,128)(2,1)}, u32[]{:S(2)}, u32[]{:S(2)}) collective-permute-start(f16[256,1024]{1,0:T(8,128)(2,1)} %get-tuple-element.116), channel_id=1, source_target_pairs={{0,1},{1,0},{2,3},{3,2},{4,5},{5,4},{6,7},{7,6},{8,9},{9,8},{10,11... | collective-permute-start | bytes 1572872 | tf_op jit(solution)/shard_map/ppermute | solution.py:24
  10.7 33.8 %collective-permute-start.4 = (f16[256,1024]{1,0:T(8,128)(2,1)}, f16[256,1024]{1,0:T(8,128)(2,1)}, u32[]{:S(2)}, u32[]{:S(2)}) collective-permute-start(f16[256,1024]{1,0:T(8,128)(2,1)} %get-tuple-element.115), channel_id=1, source_target_pairs={{0,1},{1,0},{2,3},{3,2},{4,5},{5,4},{6,7},{7,6},{8,9},{9,8},{10,11... | collective-permute-start | bytes 1572872 | tf_op jit(solution)/shard_map/ppermute | solution.py:24
  10.7 3.1 %copy-start.2 = (bf16[1,896,4096]{2,1,0:T(8,128)(2,1)S(1)}, bf16[1,896,4096]{2,1,0:T(8,128)(2,1)}, u32[]{:S(2)}) copy-start(bf16[1,896,4096]{2,1,0:T(8,128)(2,1)} %param.5) | copy-start | bytes 22020100
  13.8 1.5 %copy-start.5 = (bf16[1,896,1024]{2,1,0:T(8,128)(2,1)S(1)}, bf16[1,896,1024]{2,1,0:T(8,128)(2,1)}, u32[]{:S(2)}) copy-start(bf16[1,896,1024]{2,1,0:T(8,128)(2,1)} %param.6) | copy-start | bytes 5505028
  15.3 3.4 %copy-start.7 = (f32[1,2048,1024]{2,1,0:T(8,128)S(1)}, f32[1,2048,1024]{2,1,0:T(8,128)}, u32[]{:S(2)}) copy-start(f32[1,2048,1024]{2,1,0:T(8,128)} %param.4) | copy-start | bytes 25165828
  25.2 3.4 %copy-start = (f32[2048,1024]{1,0:T(8,128)}, f32[2048,1024]{1,0:T(8,128)S(1)}, u32[]{:S(2)}) copy-start(f32[2048,1024]{1,0:T(8,128)S(1)} %shard_map.47) | copy-start | bytes 25165828
  30.7 28.8 %collective-permute-start.2 = (f16[256,1024]{1,0:T(8,128)(2,1)}, f16[256,1024]{1,0:T(8,128)(2,1)}, u32[]{:S(2)}, u32[]{:S(2)}) collective-permute-start(f16[256,1024]{1,0:T(8,128)(2,1)} %multiply_convert_fusion.7), channel_id=1, source_target_pairs={{2,4},{4,2},{6,8},{8,6},{10,12},{12,10},{14,16},{16,14},{18,20},{2... | collective-permute-start | bytes 1572872 | tf_op jit(solution)/shard_map/ppermute | solution.py:33
  33.2 26.2 %collective-permute-start.3 = (f16[256,1024]{1,0:T(8,128)(2,1)}, f16[256,1024]{1,0:T(8,128)(2,1)}, u32[]{:S(2)}, u32[]{:S(2)}) collective-permute-start(f16[256,1024]{1,0:T(8,128)(2,1)} %multiply_convert_fusion.7), channel_id=1, source_target_pairs={{0,2},{2,0},{4,6},{6,4},{8,10},{10,8},{12,14},{14,12},{16,18},{18,... | collective-permute-start | bytes 1572872 | tf_op jit(solution)/shard_map/ppermute | solution.py:33
  35.5 10.3 %slice-start = ((s8[8388608]{0:T(1024)(128)(4,1)}), s8[4194304]{0:T(1024)(128)(4,1)S(1)}, s32[]{:S(2)}) async-start(s8[8388608]{0:T(1024)(128)(4,1)} %bitcast.32), calls=%async_computation | async-start | bytes 8388608
  35.5 3.2 %copy-start.3 = (bf16[1,896,4096]{2,1,0:T(8,128)(2,1)S(1)}, bf16[1,896,4096]{2,1,0:T(8,128)(2,1)}, u32[]{:S(2)}) copy-start(bf16[1,896,4096]{2,1,0:T(8,128)(2,1)} %param.5) | copy-start | bytes 22020100
  38.7 1.6 %copy-start.6 = (bf16[1,896,1024]{2,1,0:T(8,128)(2,1)S(1)}, bf16[1,896,1024]{2,1,0:T(8,128)(2,1)}, u32[]{:S(2)}) copy-start(bf16[1,896,1024]{2,1,0:T(8,128)(2,1)} %param.6) | copy-start | bytes 5505028
  40.4 5.5 %slice-start.1 = ((s8[8388608]{0:T(1024)(128)(4,1)}), s8[4194304]{0:T(1024)(128)(4,1)S(1)}, s32[]{:S(2)}) async-start(s8[8388608]{0:T(1024)(128)(4,1)} %bitcast.32), calls=%async_computation.1 | async-start | bytes 8388608
  44.5 13.6 %collective-permute-start.1 = (f16[256,1024]{1,0:T(8,128)(2,1)S(1)}, f16[256,1024]{1,0:T(8,128)(2,1)S(1)}, u32[]{:S(2)}, u32[]{:S(2)}) collective-permute-start(f16[256,1024]{1,0:T(8,128)(2,1)S(1)} %slice_convert_fusion.5), channel_id=1, source_target_pairs={{0,1},{1,0},{2,3},{3,2},{4,5},{5,4},{6,7},{7,6},{8,9},{9,8},{10,11... | collective-permute-start | bytes 1572872 | tf_op jit(solution)/shard_map/ppermute | solution.py:24
  47.1 58.1 %copy-start.21 = (s32[16,3]{0,1:T(4,128)S(1)}, s32[16,3]{0,1:T(4,128)}, u32[]{:S(2)}) copy-start(s32[16,3]{0,1:T(4,128)} %param.7) | copy-start | bytes 580
  47.1 25.0 %collective-permute-start.6 = (f16[256,1024]{1,0:T(8,128)(2,1)S(1)}, f16[256,1024]{1,0:T(8,128)(2,1)S(1)}, u32[]{:S(2)}, u32[]{:S(2)}) collective-permute-start(f16[256,1024]{1,0:T(8,128)(2,1)S(1)} %multiply_convert_fusion.6), channel_id=1, source_target_pairs={{2,4},{4,2},{6,8},{8,6},{10,12},{12,10},{14,16},{16,14},{18,20},{2... | collective-permute-start | bytes 1572872 | tf_op jit(solution)/shard_map/ppermute | solution.py:33
  47.2 24.9 %collective-permute-start.7 = (f16[256,1024]{1,0:T(8,128)(2,1)S(1)}, f16[256,1024]{1,0:T(8,128)(2,1)S(1)}, u32[]{:S(2)}, u32[]{:S(2)}) collective-permute-start(f16[256,1024]{1,0:T(8,128)(2,1)S(1)} %multiply_convert_fusion.6), channel_id=1, source_target_pairs={{0,2},{2,0},{4,6},{6,4},{8,10},{10,8},{12,14},{14,12},{16,18},{18,... | collective-permute-start | bytes 1572872 | tf_op jit(solution)/shard_map/ppermute | solution.py:33
  58.2 12.7 %collective-permute-start.5 = (f16[256,1024]{1,0:T(8,128)(2,1)S(1)}, f16[256,1024]{1,0:T(8,128)(2,1)S(1)}, u32[]{:S(2)}, u32[]{:S(2)}) collective-permute-start(f16[256,1024]{1,0:T(8,128)(2,1)S(1)} %slice_convert_fusion.4), channel_id=1, source_target_pairs={{0,1},{1,0},{2,3},{3,2},{4,5},{5,4},{6,7},{7,6},{8,9},{9,8},{10,11... | collective-permute-start | bytes 1572872 | tf_op jit(solution)/shard_map/ppermute | solution.py:24
  59.6 24.2 %collective-permute-start.10 = (f16[256,1024]{1,0:T(8,128)(2,1)S(1)}, f16[256,1024]{1,0:T(8,128)(2,1)S(1)}, u32[]{:S(2)}, u32[]{:S(2)}) collective-permute-start(f16[256,1024]{1,0:T(8,128)(2,1)S(1)} %multiply_convert_fusion.5), channel_id=1, source_target_pairs={{0,2},{2,0},{4,6},{6,4},{8,10},{10,8},{12,14},{14,12},{16,18},{18,... | collective-permute-start | bytes 1572872 | tf_op jit(solution)/shard_map/ppermute | solution.py:33
  60.7 23.1 %collective-permute-start.9 = (f16[256,1024]{1,0:T(8,128)(2,1)S(1)}, f16[256,1024]{1,0:T(8,128)(2,1)S(1)}, u32[]{:S(2)}, u32[]{:S(2)}) collective-permute-start(f16[256,1024]{1,0:T(8,128)(2,1)S(1)} %multiply_convert_fusion.5), channel_id=1, source_target_pairs={{2,4},{4,2},{6,8},{8,6},{10,12},{12,10},{14,16},{16,14},{18,20},{2... | collective-permute-start | bytes 1572872 | tf_op jit(solution)/shard_map/ppermute | solution.py:33
  70.8 11.7 %collective-permute-start.8 = (f16[256,1024]{1,0:T(8,128)(2,1)S(1)}, f16[256,1024]{1,0:T(8,128)(2,1)S(1)}, u32[]{:S(2)}, u32[]{:S(2)}) collective-permute-start(f16[256,1024]{1,0:T(8,128)(2,1)S(1)} %slice_convert_fusion.3), channel_id=1, source_target_pairs={{0,1},{1,0},{2,3},{3,2},{4,5},{5,4},{6,7},{7,6},{8,9},{9,8},{10,11... | collective-permute-start | bytes 1572872 | tf_op jit(solution)/shard_map/ppermute | solution.py:24
  72.1 0.8 copy-start.9
  72.1 31.7 %copy-start.11 = (f16[256,1024]{1,0:T(8,128)(2,1)}, f16[256,1024]{1,0:T(8,128)(2,1)S(1)}, u32[]{:S(2)}) copy-start(f16[256,1024]{1,0:T(8,128)(2,1)S(1)} %collective-permute-done.7) | copy-start | bytes 1572868
  72.3 22.5 %collective-permute-start.12 = (f16[256,1024]{1,0:T(8,128)(2,1)S(1)}, f16[256,1024]{1,0:T(8,128)(2,1)S(1)}, u32[]{:S(2)}, u32[]{:S(2)}) collective-permute-start(f16[256,1024]{1,0:T(8,128)(2,1)S(1)} %multiply_convert_fusion.4), channel_id=1, source_target_pairs={{2,4},{4,2},{6,8},{8,6},{10,12},{12,10},{14,16},{16,14},{18,20},{2... | collective-permute-start | bytes 1572872 | tf_op jit(solution)/shard_map/ppermute | solution.py:33
  72.9 21.9 %collective-permute-start.13 = (f16[256,1024]{1,0:T(8,128)(2,1)S(1)}, f16[256,1024]{1,0:T(8,128)(2,1)S(1)}, u32[]{:S(2)}, u32[]{:S(2)}) collective-permute-start(f16[256,1024]{1,0:T(8,128)(2,1)S(1)} %multiply_convert_fusion.4), channel_id=1, source_target_pairs={{0,2},{2,0},{4,6},{6,4},{8,10},{10,8},{12,14},{14,12},{16,18},{18,... | collective-permute-start | bytes 1572872 | tf_op jit(solution)/shard_map/ppermute | solution.py:33
  82.6 10.8 %collective-permute-start.11 = (f16[256,1024]{1,0:T(8,128)(2,1)S(1)}, f16[256,1024]{1,0:T(8,128)(2,1)S(1)}, u32[]{:S(2)}, u32[]{:S(2)}) collective-permute-start(f16[256,1024]{1,0:T(8,128)(2,1)S(1)} %slice_convert_fusion.2), channel_id=1, source_target_pairs={{0,1},{1,0},{2,3},{3,2},{4,5},{5,4},{6,7},{7,6},{8,9},{9,8},{10,11... | collective-permute-start | bytes 1572872 | tf_op jit(solution)/shard_map/ppermute | solution.py:24
  83.8 21.3 %copy-start.13 = (f16[256,1024]{1,0:T(8,128)(2,1)}, f16[256,1024]{1,0:T(8,128)(2,1)S(1)}, u32[]{:S(2)}) copy-start(f16[256,1024]{1,0:T(8,128)(2,1)S(1)} %collective-permute-done.10) | copy-start | bytes 1572868
  83.8 21.4 %copy-start.15 = (f16[256,1024]{1,0:T(8,128)(2,1)}, f16[256,1024]{1,0:T(8,128)(2,1)S(1)}, u32[]{:S(2)}) copy-start(f16[256,1024]{1,0:T(8,128)(2,1)S(1)} %collective-permute-done.9) | copy-start | bytes 1572868
  85.1 23.4 %collective-permute-start.15 = (f16[256,1024]{1,0:T(8,128)(2,1)}, f16[256,1024]{1,0:T(8,128)(2,1)}, u32[]{:S(2)}, u32[]{:S(2)}) collective-permute-start(f16[256,1024]{1,0:T(8,128)(2,1)} %multiply_convert_fusion.3), channel_id=1, source_target_pairs={{2,4},{4,2},{6,8},{8,6},{10,12},{12,10},{14,16},{16,14},{18,20},{2... | collective-permute-start | bytes 1572872 | tf_op jit(solution)/shard_map/ppermute | solution.py:33
  85.6 22.9 %collective-permute-start.16 = (f16[256,1024]{1,0:T(8,128)(2,1)}, f16[256,1024]{1,0:T(8,128)(2,1)}, u32[]{:S(2)}, u32[]{:S(2)}) collective-permute-start(f16[256,1024]{1,0:T(8,128)(2,1)} %multiply_convert_fusion.3), channel_id=1, source_target_pairs={{0,2},{2,0},{4,6},{6,4},{8,10},{10,8},{12,14},{14,12},{16,18},{18,... | collective-permute-start | bytes 1572872 | tf_op jit(solution)/shard_map/ppermute | solution.py:33
  93.4 10.4 %collective-permute-start.14 = (f16[256,1024]{1,0:T(8,128)(2,1)S(1)}, f16[256,1024]{1,0:T(8,128)(2,1)S(1)}, u32[]{:S(2)}, u32[]{:S(2)}) collective-permute-start(f16[256,1024]{1,0:T(8,128)(2,1)S(1)} %slice_convert_fusion.1), channel_id=1, source_target_pairs={{0,1},{1,0},{2,3},{3,2},{4,5},{5,4},{6,7},{7,6},{8,9},{9,8},{10,11... | collective-permute-start | bytes 1572872 | tf_op jit(solution)/shard_map/ppermute | solution.py:24
  94.8 11.1 %copy-start.17 = (f16[256,1024]{1,0:T(8,128)(2,1)}, f16[256,1024]{1,0:T(8,128)(2,1)S(1)}, u32[]{:S(2)}) copy-start(f16[256,1024]{1,0:T(8,128)(2,1)S(1)} %collective-permute-done.12) | copy-start | bytes 1572868
  94.8 11.1 %copy-start.19 = (f16[256,1024]{1,0:T(8,128)(2,1)}, f16[256,1024]{1,0:T(8,128)(2,1)S(1)}, u32[]{:S(2)}) copy-start(f16[256,1024]{1,0:T(8,128)(2,1)S(1)} %collective-permute-done.13) | copy-start | bytes 1572868
  95.9 19.6 %collective-permute-start.18 = (f16[256,1024]{1,0:T(8,128)(2,1)}, f16[256,1024]{1,0:T(8,128)(2,1)}, u32[]{:S(2)}, u32[]{:S(2)}) collective-permute-start(f16[256,1024]{1,0:T(8,128)(2,1)} %multiply_convert_fusion.2), channel_id=1, source_target_pairs={{2,4},{4,2},{6,8},{8,6},{10,12},{12,10},{14,16},{16,14},{18,20},{2... | collective-permute-start | bytes 1572872 | tf_op jit(solution)/shard_map/ppermute | solution.py:33
  97.5 18.0 %collective-permute-start.19 = (f16[256,1024]{1,0:T(8,128)(2,1)}, f16[256,1024]{1,0:T(8,128)(2,1)}, u32[]{:S(2)}, u32[]{:S(2)}) collective-permute-start(f16[256,1024]{1,0:T(8,128)(2,1)} %multiply_convert_fusion.2), channel_id=1, source_target_pairs={{0,2},{2,0},{4,6},{6,4},{8,10},{10,8},{12,14},{14,12},{16,18},{18,... | collective-permute-start | bytes 1572872 | tf_op jit(solution)/shard_map/ppermute | solution.py:33
  103.8 11.8 %collective-permute-start.17 = (f16[256,1024]{1,0:T(8,128)(2,1)}, f16[256,1024]{1,0:T(8,128)(2,1)S(1)}, u32[]{:S(2)}, u32[]{:S(2)}) collective-permute-start(f16[256,1024]{1,0:T(8,128)(2,1)} %slice_convert_fusion), channel_id=1, source_target_pairs={{0,1},{1,0},{2,3},{3,2},{4,5},{5,4},{6,7},{7,6},{8,9},{9,8},{10,11... | collective-permute-start | bytes 1572872 | tf_op jit(solution)/shard_map/ppermute | solution.py:24
  108.4 16.3 %slice-start.2 = ((s8[8388608]{0:T(1024)(128)(4,1)}), s8[4194304]{0:T(1024)(128)(4,1)S(1)}, s32[]{:S(2)}) async-start(s8[8388608]{0:T(1024)(128)(4,1)} %bitcast.34), calls=%async_computation.2 | async-start | bytes 8388608
  108.5 16.3 %copy-start.10 = (f16[256,1024]{1,0:T(8,128)(2,1)S(1)}, f16[256,1024]{1,0:T(8,128)(2,1)}, u32[]{:S(2)}) copy-start(f16[256,1024]{1,0:T(8,128)(2,1)} %copy-done.9) | copy-start | bytes 1572868
  108.5 16.3 %copy-start.12 = (f16[256,1024]{1,0:T(8,128)(2,1)S(1)}, f16[256,1024]{1,0:T(8,128)(2,1)}, u32[]{:S(2)}) copy-start(f16[256,1024]{1,0:T(8,128)(2,1)} %copy-done.11) | copy-start | bytes 1572868
  110.1 24.1 %collective-permute-start.20 = (f16[256,1024]{1,0:T(8,128)(2,1)S(1)}, f16[256,1024]{1,0:T(8,128)(2,1)S(1)}, u32[]{:S(2)}, u32[]{:S(2)}) collective-permute-start(f16[256,1024]{1,0:T(8,128)(2,1)S(1)} %multiply_convert_fusion.1), channel_id=1, source_target_pairs={{0,2},{2,0},{4,6},{6,4},{8,10},{10,8},{12,14},{14,12},{16,18},{18,... | collective-permute-start | bytes 1572872 | tf_op jit(solution)/shard_map/ppermute | solution.py:33
  115.6 19.8 %collective-permute-start.21 = (f16[256,1024]{1,0:T(8,128)(2,1)S(1)}, f16[256,1024]{1,0:T(8,128)(2,1)S(1)}, u32[]{:S(2)}, u32[]{:S(2)}) collective-permute-start(f16[256,1024]{1,0:T(8,128)(2,1)S(1)} %multiply_convert_fusion.1), channel_id=1, source_target_pairs={{2,4},{4,2},{6,8},{8,6},{10,12},{12,10},{14,16},{16,14},{18,20},{2... | collective-permute-start | bytes 1572872 | tf_op jit(solution)/shard_map/ppermute | solution.py:33
  117.0 19.4 %collective-permute-start.22 = (f16[256,1024]{1,0:T(8,128)(2,1)S(1)}, f16[256,1024]{1,0:T(8,128)(2,1)S(1)}, u32[]{:S(2)}, u32[]{:S(2)}) collective-permute-start(f16[256,1024]{1,0:T(8,128)(2,1)S(1)} %multiply_convert_fusion), channel_id=1, source_target_pairs={{0,2},{2,0},{4,6},{6,4},{8,10},{10,8},{12,14},{14,12},{16,18},{18,... | collective-permute-start | bytes 1572872 | tf_op jit(solution)/shard_map/ppermute | solution.py:33
  120.9 20.1 %collective-permute-start.23 = (f16[256,1024]{1,0:T(8,128)(2,1)S(1)}, f16[256,1024]{1,0:T(8,128)(2,1)S(1)}, u32[]{:S(2)}, u32[]{:S(2)}) collective-permute-start(f16[256,1024]{1,0:T(8,128)(2,1)S(1)} %multiply_convert_fusion), channel_id=1, source_target_pairs={{2,4},{4,2},{6,8},{8,6},{10,12},{12,10},{14,16},{16,14},{18,20},{2... | collective-permute-start | bytes 1572872 | tf_op jit(solution)/shard_map/ppermute | solution.py:33
  120.9 7.0 %copy-start.14 = (f16[256,1024]{1,0:T(8,128)(2,1)S(1)}, f16[256,1024]{1,0:T(8,128)(2,1)}, u32[]{:S(2)}) copy-start(f16[256,1024]{1,0:T(8,128)(2,1)} %copy-done.13) | copy-start | bytes 1572868
  120.9 7.0 %copy-start.16 = (f16[256,1024]{1,0:T(8,128)(2,1)S(1)}, f16[256,1024]{1,0:T(8,128)(2,1)}, u32[]{:S(2)}) copy-start(f16[256,1024]{1,0:T(8,128)(2,1)} %copy-done.15) | copy-start | bytes 1572868
  123.7 2.2 %slice-start.3 = ((s8[8388608]{0:T(1024)(128)(4,1)}), s8[4194304]{0:T(1024)(128)(4,1)S(1)}, s32[]{:S(2)}) async-start(s8[8388608]{0:T(1024)(128)(4,1)} %bitcast.34), calls=%async_computation.3 | async-start | bytes 8388608
  123.7 5.2 %copy-start.18 = (f16[256,1024]{1,0:T(8,128)(2,1)S(1)}, f16[256,1024]{1,0:T(8,128)(2,1)}, u32[]{:S(2)}) copy-start(f16[256,1024]{1,0:T(8,128)(2,1)} %copy-done.17) | copy-start | bytes 1572868
  123.7 5.2 %copy-start.20 = (f16[256,1024]{1,0:T(8,128)(2,1)S(1)}, f16[256,1024]{1,0:T(8,128)(2,1)}, u32[]{:S(2)}) copy-start(f16[256,1024]{1,0:T(8,128)(2,1)} %copy-done.19) | copy-start | bytes 1572868
  136.4 4.6 %copy-start.8 = (f32[1,2048,1024]{2,1,0:T(8,128)}, f32[1,2048,1024]{2,1,0:T(8,128)S(1)}, u32[]{:S(2)}) copy-start(f32[1,2048,1024]{2,1,0:T(8,128)S(1)} %bitcast_dynamic-update-slice_fusion.1) | copy-start | bytes 25165828

commit v6 on v5

--- a/solution.py
+++ b/solution.py
@@ -15,7 +15,6 @@
 STEP = 256
 TILE = 256
 AHEAD = 2
-EARLY = 3
 
 
 def from_behind(value, axis, steps):
@@ -64,7 +63,7 @@
             num_scalar_prefetch=1, grid=(size // tile,), in_specs=specs, out_specs=by_rows
         ),
         out_shape=jax.ShapeDtypeStruct((size, width), jnp.float32),
-        compiler_params=pltpu.CompilerParams(vmem_limit_bytes=24 * 2**20),
+        compiler_params=pltpu.CompilerParams(vmem_limit_bytes=56 * 2**20),
         cost_estimate=pl.CostEstimate(flops=0, bytes_accessed=0, transcendentals=0),
     )(jnp.reshape(start // tile, (1,)), *operands)
 
@@ -86,25 +85,30 @@
     c_far = jnp.where(even, coeff[0], coeff[2]) / scale
     step = math.gcd(rows, STEP)
     chunks = rows // step
-    early = min(EARLY, chunks)
+    early = min(AHEAD, chunks)
 
     def rows_of(value, chunk):
         return value[chunk * step:(chunk + 1) * step]
 
+    def owner(shard, away):
+        other = shard + away
+        return jnp.where(other < shards, other, other - shards)
+
     def for_others(shard, first, count):
-        return [
+        made = count and [
             product(
-                features, cot_local, lax.rem(shard + away, shards) * rows + first * step,
+                features, cot_local, owner(shard, away) * rows + first * step,
                 count * step, RATE * scale,
             )
             for away in range(1, shards)
         ]
+        return {
+            first + place: [rows_of(term, place).astype(WIRE) for term in made]
+            for place in range(count)
+        }
 
-    def send_terms(made, place):
-        return [
-            from_behind(rows_of(term, place).astype(WIRE), "fsdp", away)
-            for away, term in zip(range(1, shards), made)
-        ]
+    def send_terms(terms):
+        return [from_behind(term, "fsdp", away) for away, term in zip(range(1, shards), terms)]
 
     def u_of(chunk):
         total = rows_of(base, chunk)
@@ -122,29 +126,25 @@
 
     near = {}
     far = {}
-    made = for_others(shard, 0, early)
-    arrived = {chunk: send_terms(made, chunk) for chunk in range(min(AHEAD, chunks))}
-    made, later = lax.optimization_barrier((made, shard))
+    terms = for_others(shard, 0, early)
+    arrived = {chunk: send_terms(terms[chunk]) for chunk in range(early)}
+    terms, later = lax.optimization_barrier((terms, shard))
     base = product(features, cot_local, later * rows, rows, -RATE, weights)
 
-    arrived[0], base = lax.optimization_barrier((arrived[0], base))
+    base, later = lax.optimization_barrier((base, shard))
+    terms = for_others(later, early, chunks - early)
+    arrived[0], base, terms = lax.optimization_barrier((arrived[0], base, terms))
     for chunk in range(chunks):
-        if chunk == 1 and early < chunks:
-            arrived[1], rest = lax.optimization_barrier((arrived[1], rest))
         if chunk >= 2:
             arrived[chunk], far[chunk - 2], near[chunk - 2] = lax.optimization_barrier(
                 (arrived[chunk], far[chunk - 2], near[chunk - 2])
             )
         sent = (u_of(chunk) * scale).astype(WIRE)
-        sent, base, made, later = lax.optimization_barrier((sent, base, made, shard))
-        if chunk == 0 and early < chunks:
-            rest = for_others(later, early, chunks - early)
-        after = chunk + AHEAD
-        if after < early:
-            arrived[after] = send_terms(made, after)
-        elif after < chunks:
-            rest, sent = lax.optimization_barrier((rest, sent))
-            arrived[after] = send_terms(rest, after - early)
+        sent, base = lax.optimization_barrier((sent, base))
+        after = chunk + early
+        if after < chunks:
+            terms[after], sent = lax.optimization_barrier((terms[after], sent))
+            arrived[after] = send_terms(terms[after])
         if chunk == chunks - 1:
             far[0], near[0], sent = lax.optimization_barrier((far[0], near[0], sent))
         far[chunk] = swapped(sent, "blk", 1)

time: 144 us -> 139 us (0.965)
  the two profiles are of different devices: /device:TPU:1 before, /device:TPU:0 now
where the time goes in v6:
time: 139 us; the launch traced here: 138 us
  starting transfers between devices  49.5 us (36%)
  other arithmetic  30.3 us (22%)
  Pallas kernels  25.3 us (18%)
  waiting for transfers between devices  21.9 us (16%)
  local copies, waits for them, and re-layouts  8.32 us (6%)
  between operations  2.95 us (2%)
    ppermute x16, starting transfers between devices, swapped(): return lax.ppermute(value, axis, pairs)  38.8 us
    pallas_call x3, Pallas kernels, product(): pl.pallas_call(functools.partial(product_kernel, factor), grid_spec=pltpu...  25.3 us
    ppermute x8, waiting for transfers between devices, from_behind(): return lax.ppermute(value, axis, pairs)  21.8 us
    dynamic_update_slice x7, other arithmetic, mix_into(): return lax.dynamic_update_slice_in_dim(out, mixed, chunk * step, axis=0)  13.9 us
    ppermute x8, starting transfers between devices, from_behind(): return lax.ppermute(value, axis, pairs)  10.7 us
    convert_element_type x8, other arithmetic, on_device(): sent = (u_of(chunk) * scale).astype(WIRE)  8.34 us
    another operation x2, other arithmetic  5.41 us
    unnamed x32, local copies, waits for them, and re-layouts  4.52 us
  transfers between devices with their start and end apart: 24, of which 5 were waited for; matrix products, arithmetic and copies ran while one was open for 21% of the time, Pallas kernels for 15%

profile of v6, /device:TPU:0, one launch (start us, length us, event | category | flops | bytes accessed | tf_op | source)
XLA Modules:
  0.0 138.3 jit_solution(14436679503602384264)
XLA Ops:
  0.0 4.1 %shard_map.46 = f32[512,1024]{1,0:T(8,128)} custom-call(s32[1]{0:T(128)} %bitcast.4.offset_ref, bf16[896,4096]{1,0:T(8,128)(2,1)} %bitcast.36, bf16[896,1024]{1,0:T(8,128)(2,1)} %bitcast.39), custom_call_target="tpu_custom_call" | custom-call | tf_op jit(solution)/shard_map/pallas_call | solution.py:60
  4.1 1.8 %convert.12 = f16[512,1024]{1,0:T(8,128)(2,1)S(1)} convert(f32[512,1024]{1,0:T(8,128)} %shard_map.46) | non-fusion elementwise | flops 524288 | bytes 3145728 | tf_op jit(solution)/shard_map/convert.7
  5.9 0.3 fusion.7
  6.2 3.0 %collective-permute-start = (f16[256,1024]{1,0:T(8,128)(2,1)S(1)}, f16[256,1024]{1,0:T(8,128)(2,1)S(1)}, u32[]{:S(2)}, u32[]{:S(2)}) collective-permute-start(f16[256,1024]{1,0:T(8,128)(2,1)S(1)} %get-tuple-element.132), channel_id=1, source_target_pairs={{0,1},{1,0},{2,3},{3,2},{4,5},{5,4},{6,7},{7,6},{8,9},{9,8},{10,11... | collective-permute-start | bytes 1572872 | tf_op jit(solution)/shard_map/ppermute | solution.py:23
  9.2 0.1 collective-permute-start.4
  9.3 12.5 %shard_map.47 = f32[2048,1024]{1,0:T(8,128)} custom-call(s32[1]{0:T(128)} %bitcast.7.offset_ref, bf16[896,4096]{1,0:T(8,128)(2,1)} %bitcast.37, bf16[896,1024]{1,0:T(8,128)(2,1)} %bitcast.40, f32[2048,1024]{1,0:T(8,128)} %bitcast.42), custom_call_target="tpu_custom_call" | custom-call | tf_op jit(solution)/shard_map/pallas_call | solution.py:60
  21.8 8.7 %shard_map.48 = f32[1536,1024]{1,0:T(8,128)} custom-call(s32[1]{0:T(128)} %bitcast.9.offset_ref, bf16[896,4096]{1,0:T(8,128)(2,1)} %bitcast.38, bf16[896,1024]{1,0:T(8,128)(2,1)} %bitcast.41), custom_call_target="tpu_custom_call" | custom-call | tf_op jit(solution)/shard_map/pallas_call | solution.py:60
  30.5 3.6 %convert.13 = f16[1536,1024]{1,0:T(8,128)(2,1)S(1)} convert(f32[1536,1024]{1,0:T(8,128)} %shard_map.48) | non-fusion elementwise | flops 1572864 | bytes 9437184 | tf_op jit(solution)/shard_map/convert.5
  34.1 0.0 copy-start.11
  34.1 1.8 %fusion.6 = (f16[256,1024]{1,0:T(8,128)(2,1)}, f16[256,1024]{1,0:T(8,128)(2,1)}, f16[256,1024]{1,0:T(8,128)(2,1)}, f16[256,1024]{1,0:T(8,128)(2,1)S(1)}, f16[256...) fusion(f16[1536,1024]{1,0:T(8,128)(2,1)S(1)} %convert.13), kind=kLoop, calls=%fused_computation.32 | loop fusion | bytes 6291456 | tf_op jit(solution)/shard_map/slice | solution.py:91
  35.9 0.0 collective-permute-done
  36.0 0.2 multiply_convert_fusion.7
  36.2 2.0 %collective-permute-start.1 = (f16[256,1024]{1,0:T(8,128)(2,1)S(1)}, f16[256,1024]{1,0:T(8,128)(2,1)S(1)}, u32[]{:S(2)}, u32[]{:S(2)}) collective-permute-start(f16[256,1024]{1,0:T(8,128)(2,1)S(1)} %get-tuple-element.72), channel_id=1, source_target_pairs={{0,1},{1,0},{2,3},{3,2},{4,5},{5,4},{6,7},{7,6},{8,9},{9,8},{10,11... | collective-permute-start | bytes 1572872 | tf_op jit(solution)/shard_map/ppermute | solution.py:23
  38.2 3.1 %collective-permute-start.2 = (f16[256,1024]{1,0:T(8,128)(2,1)S(1)}, f16[256,1024]{1,0:T(8,128)(2,1)S(1)}, u32[]{:S(2)}, u32[]{:S(2)}) collective-permute-start(f16[256,1024]{1,0:T(8,128)(2,1)S(1)} %multiply_convert_fusion.7), channel_id=1, source_target_pairs={{2,4},{4,2},{6,8},{8,6},{10,12},{12,10},{14,16},{16,14},{18,20},{2... | collective-permute-start | bytes 1572872 | tf_op jit(solution)/shard_map/ppermute | solution.py:32
  41.3 0.2 multiply_convert_fusion.6
  41.5 0.6 collective-permute-start.5
  42.1 1.2 collective-permute-start.6
  43.3 7.8 %collective-permute-done.1 = f16[256,1024]{1,0:T(8,128)(2,1)S(1)} collective-permute-done((f16[256,1024]{1,0:T(8,128)(2,1)S(1)}, f16[256,1024]{1,0:T(8,128)(2,1)S(1)}, u32[]{:S(2)}, u32[]{:S(2)}) %collective-permute-start.1) | collective-permute-done | bytes 524320 | tf_op jit(solution)/shard_map/ppermute | solution.py:23
  51.1 0.0 collective-permute-start.7
  51.1 0.2 multiply_convert_fusion.5
  51.3 7.1 %collective-permute-start.10 = (f16[256,1024]{1,0:T(8,128)(2,1)S(1)}, f16[256,1024]{1,0:T(8,128)(2,1)S(1)}, u32[]{:S(2)}, u32[]{:S(2)}) collective-permute-start(f16[256,1024]{1,0:T(8,128)(2,1)S(1)} %multiply_convert_fusion.5), channel_id=1, source_target_pairs={{0,2},{2,0},{4,6},{6,4},{8,10},{10,8},{12,14},{14,12},{16,18},{18,... | collective-permute-start | bytes 1572872 | tf_op jit(solution)/shard_map/ppermute | solution.py:32
  58.5 0.5 collective-permute-start.8
  59.0 1.9 %collective-permute-done.5 = f16[256,1024]{1,0:T(8,128)(2,1)S(1)} collective-permute-done((f16[256,1024]{1,0:T(8,128)(2,1)S(1)}, f16[256,1024]{1,0:T(8,128)(2,1)S(1)}, u32[]{:S(2)}, u32[]{:S(2)}) %collective-permute-start.5) | collective-permute-done | bytes 524320 | tf_op jit(solution)/shard_map/ppermute | solution.py:23
  60.9 2.6 %collective-permute-start.9 = (f16[256,1024]{1,0:T(8,128)(2,1)S(1)}, f16[256,1024]{1,0:T(8,128)(2,1)S(1)}, u32[]{:S(2)}, u32[]{:S(2)}) collective-permute-start(f16[256,1024]{1,0:T(8,128)(2,1)S(1)} %multiply_convert_fusion.5), channel_id=1, source_target_pairs={{2,4},{4,2},{6,8},{8,6},{10,12},{12,10},{14,16},{16,14},{18,20},{2... | collective-permute-start | bytes 1572872 | tf_op jit(solution)/shard_map/ppermute | solution.py:32
  63.5 0.0 collective-permute-done.6
  63.5 0.0 collective-permute-done.7
  63.5 1.1 multiply_convert_fusion.4
  64.6 1.5 %collective-permute-start.11 = (f16[256,1024]{1,0:T(8,128)(2,1)}, f16[256,1024]{1,0:T(8,128)(2,1)S(1)}, u32[]{:S(2)}, u32[]{:S(2)}) collective-permute-start(f16[256,1024]{1,0:T(8,128)(2,1)} %get-tuple-element.94), channel_id=1, source_target_pairs={{0,1},{1,0},{2,3},{3,2},{4,5},{5,4},{6,7},{7,6},{8,9},{9,8},{10,11... | collective-permute-start | bytes 1572872 | tf_op jit(solution)/shard_map/ppermute | solution.py:23
  66.2 2.5 %collective-permute-start.12 = (f16[256,1024]{1,0:T(8,128)(2,1)}, f16[256,1024]{1,0:T(8,128)(2,1)}, u32[]{:S(2)}, u32[]{:S(2)}) collective-permute-start(f16[256,1024]{1,0:T(8,128)(2,1)} %multiply_convert_fusion.4), channel_id=1, source_target_pairs={{2,4},{4,2},{6,8},{8,6},{10,12},{12,10},{14,16},{16,14},{18,20},{2... | collective-permute-start | bytes 1572872 | tf_op jit(solution)/shard_map/ppermute | solution.py:32
  68.6 0.0 collective-permute-done.10
  68.7 0.0 collective-permute-start.13
  68.7 4.6 %collective-permute-done.8 = f16[256,1024]{1,0:T(8,128)(2,1)S(1)} collective-permute-done((f16[256,1024]{1,0:T(8,128)(2,1)S(1)}, f16[256,1024]{1,0:T(8,128)(2,1)S(1)}, u32[]{:S(2)}, u32[]{:S(2)}) %collective-permute-start.8) | collective-permute-done | bytes 524320 | tf_op jit(solution)/shard_map/ppermute | solution.py:23
  73.2 0.0 collective-permute-done.9
  73.3 1.0 multiply_convert_fusion.3
  74.3 1.6 %collective-permute-start.14 = (f16[256,1024]{1,0:T(8,128)(2,1)}, f16[256,1024]{1,0:T(8,128)(2,1)}, u32[]{:S(2)}, u32[]{:S(2)}) collective-permute-start(f16[256,1024]{1,0:T(8,128)(2,1)} %get-tuple-element.100), channel_id=1, source_target_pairs={{0,1},{1,0},{2,3},{3,2},{4,5},{5,4},{6,7},{7,6},{8,9},{9,8},{10,11... | collective-permute-start | bytes 1572872 | tf_op jit(solution)/shard_map/ppermute | solution.py:23
  75.9 2.5 %collective-permute-start.15 = (f16[256,1024]{1,0:T(8,128)(2,1)}, f16[256,1024]{1,0:T(8,128)(2,1)}, u32[]{:S(2)}, u32[]{:S(2)}) collective-permute-start(f16[256,1024]{1,0:T(8,128)(2,1)} %multiply_convert_fusion.3), channel_id=1, source_target_pairs={{2,4},{4,2},{6,8},{8,6},{10,12},{12,10},{14,16},{16,14},{18,20},{2... | collective-permute-start | bytes 1572872 | tf_op jit(solution)/shard_map/ppermute | solution.py:32
  78.3 5.3 %collective-permute-done.11 = f16[256,1024]{1,0:T(8,128)(2,1)S(1)} collective-permute-done((f16[256,1024]{1,0:T(8,128)(2,1)}, f16[256,1024]{1,0:T(8,128)(2,1)S(1)}, u32[]{:S(2)}, u32[]{:S(2)}) %collective-permute-start.11) | collective-permute-done | bytes 524320 | tf_op jit(solution)/shard_map/ppermute | solution.py:23
  83.6 7.7 %collective-permute-start.16 = (f16[256,1024]{1,0:T(8,128)(2,1)}, f16[256,1024]{1,0:T(8,128)(2,1)}, u32[]{:S(2)}, u32[]{:S(2)}) collective-permute-start(f16[256,1024]{1,0:T(8,128)(2,1)} %multiply_convert_fusion.3), channel_id=1, source_target_pairs={{0,2},{2,0},{4,6},{6,4},{8,10},{10,8},{12,14},{14,12},{16,18},{18,... | collective-permute-start | bytes 1572872 | tf_op jit(solution)/shard_map/ppermute | solution.py:32
  91.3 2.3 %multiply_convert_fusion.2 = f16[256,1024]{1,0:T(8,128)(2,1)} fusion(f16[256,1024]{1,0:T(8,128)(2,1)S(1)} %collective-permute-done.11, f32[2048,1024]{1,0:T(8,128)} %shard_map.47), kind=kLoop, calls=%fused_computation.15 | loop fusion | flops 1310720 | bytes 2097152 | tf_op jit(solution)/shard_map/convert_element_type | solution.py:142
  93.5 3.1 %collective-permute-start.18 = (f16[256,1024]{1,0:T(8,128)(2,1)}, f16[256,1024]{1,0:T(8,128)(2,1)}, u32[]{:S(2)}, u32[]{:S(2)}) collective-permute-start(f16[256,1024]{1,0:T(8,128)(2,1)} %multiply_convert_fusion.2), channel_id=1, source_target_pairs={{2,4},{4,2},{6,8},{8,6},{10,12},{12,10},{14,16},{16,14},{18,20},{2... | collective-permute-start | bytes 1572872 | tf_op jit(solution)/shard_map/ppermute | solution.py:32
  96.7 1.4 %collective-permute-start.17 = (f16[256,1024]{1,0:T(8,128)(2,1)}, f16[256,1024]{1,0:T(8,128)(2,1)}, u32[]{:S(2)}, u32[]{:S(2)}) collective-permute-start(f16[256,1024]{1,0:T(8,128)(2,1)} %get-tuple-element.106), channel_id=1, source_target_pairs={{0,1},{1,0},{2,3},{3,2},{4,5},{5,4},{6,7},{7,6},{8,9},{9,8},{10,11... | collective-permute-start | bytes 1572872 | tf_op jit(solution)/shard_map/ppermute | solution.py:23
  98.1 0.1 fusion
  98.2 0.7 fusion.8
  101.5 0.0 slice-start.2
  101.6 1.7 %multiply_convert_fusion.1 = f16[256,1024]{1,0:T(8,128)(2,1)S(1)} fusion(f16[256,1024]{1,0:T(8,128)(2,1)} %collective-permute-done.14, f32[2048,1024]{1,0:T(8,128)} %shard_map.47), kind=kLoop, calls=%fused_computation.13 | loop fusion | flops 1310720 | bytes 2097152 | tf_op jit(solution)/shard_map/convert_element_type | solution.py:142
  103.3 1.7 %collective-permute-start.20 = (f16[256,1024]{1,0:T(8,128)(2,1)S(1)}, f16[256,1024]{1,0:T(8,128)(2,1)S(1)}, u32[]{:S(2)}, u32[]{:S(2)}) collective-permute-start(f16[256,1024]{1,0:T(8,128)(2,1)S(1)} %multiply_convert_fusion.1), channel_id=1, source_target_pairs={{0,2},{2,0},{4,6},{6,4},{8,10},{10,8},{12,14},{14,12},{16,18},{18,... | collective-permute-start | bytes 1572872 | tf_op jit(solution)/shard_map/ppermute | solution.py:32
  105.0 4.1 %collective-permute-start.21 = (f16[256,1024]{1,0:T(8,128)(2,1)S(1)}, f16[256,1024]{1,0:T(8,128)(2,1)S(1)}, u32[]{:S(2)}, u32[]{:S(2)}) collective-permute-start(f16[256,1024]{1,0:T(8,128)(2,1)S(1)} %multiply_convert_fusion.1), channel_id=1, source_target_pairs={{2,4},{4,2},{6,8},{8,6},{10,12},{12,10},{14,16},{16,14},{18,20},{2... | collective-permute-start | bytes 1572872 | tf_op jit(solution)/shard_map/ppermute | solution.py:32
  109.0 2.3 %collective-permute-done.17 = f16[256,1024]{1,0:T(8,128)(2,1)} collective-permute-done((f16[256,1024]{1,0:T(8,128)(2,1)}, f16[256,1024]{1,0:T(8,128)(2,1)}, u32[]{:S(2)}, u32[]{:S(2)}) %collective-permute-start.17) | collective-permute-done | bytes 524320 | tf_op jit(solution)/shard_map/ppermute | solution.py:23
  111.3 1.6 %multiply_convert_fusion = f16[256,1024]{1,0:T(8,128)(2,1)S(1)} fusion(f16[256,1024]{1,0:T(8,128)(2,1)} %collective-permute-done.17, f32[2048,1024]{1,0:T(8,128)} %shard_map.47), kind=kLoop, calls=%fused_computation.11 | loop fusion | flops 1310720 | bytes 2097152 | tf_op jit(solution)/shard_map/convert_element_type | solution.py:142
  112.9 0.1 collective-permute-start.22
  113.0 3.1 %collective-permute-start.23 = (f16[256,1024]{1,0:T(8,128)(2,1)S(1)}, f16[256,1024]{1,0:T(8,128)(2,1)S(1)}, u32[]{:S(2)}, u32[]{:S(2)}) collective-permute-start(f16[256,1024]{1,0:T(8,128)(2,1)S(1)} %multiply_convert_fusion), channel_id=1, source_target_pairs={{2,4},{4,2},{6,8},{8,6},{10,12},{12,10},{14,16},{16,14},{18,20},{2... | collective-permute-start | bytes 1572872 | tf_op jit(solution)/shard_map/ppermute | solution.py:32
  116.1 2.6 %multiply_add_fusion = f32[256,1024]{1,0:T(8,128)S(1)} fusion(f16[256,1024]{1,0:T(8,128)(2,1)} %copy-done.1, f32[2048,1024]{1,0:T(8,128)} %shard_map.47, f16[256,1024]{1,0:T(8,128)(2,1)} %copy-done.2, f16[256,1024]{1,0:T(8,128)(2,1)S(1)} %collective-permute-done, f32[]{:T(128)S(6)} %div.82, f32[]{:T(128)} %bitcast.10, f32[]{:T(128)S(6)} %div.64), kind=kLoop, calls=%fused_computation.10 | loop fusion | flops 2621440 | bytes 3670028 | tf_op jit(solution)/shard_map/add | solution.py:121
  118.8 0.0 slice-start.3
  118.8 1.1 pad_bitcast_fusion
  119.9 1.1 slice-done.3
  120.9 1.0 bitcast_dynamic-update-slice_fusion.6
  122.0 1.0 bitcast_dynamic-update-slice_fusion.5
  123.1 2.2 %bitcast_dynamic-update-slice_fusion.4 = f32[1,2048,1024]{2,1,0:T(8,128)S(1)} fusion(f32[1,2048,1024]{2,1,0:T(8,128)S(1)} %bitcast_dynamic-update-slice_fusion.5, f16[256,1024]{1,0:T(8,128)(2,1)} %collective-permute-done.12, f32[2048,1024]{1,0:T(8,128)S(1)} %bitcast.35, f16[256,1024]{1,0:T(8,128)(2,1)} %collective-permute-done.13, ...), kind=kLoop, calls=%fused_computation.7 | loop fusion | flops 2621440 | bytes 3670028 | tf_op jit(solution)/shard_map/dynamic_update_slice | solution.py:125
  125.3 2.2 %bitcast_dynamic-update-slice_fusion.3 = f32[1,2048,1024]{2,1,0:T(8,128)S(1)} fusion(f32[1,2048,1024]{2,1,0:T(8,128)S(1)} %bitcast_dynamic-update-slice_fusion.4, f16[256,1024]{1,0:T(8,128)(2,1)} %collective-permute-done.15, f32[2048,1024]{1,0:T(8,128)S(1)} %bitcast.35, f16[256,1024]{1,0:T(8,128)(2,1)} %collective-permute-done.16, ...), kind=kLoop, calls=%fused_computation.6 | loop fusion | flops 2621440 | bytes 3670028 | tf_op jit(solution)/shard_map/dynamic_update_slice | solution.py:125
  127.5 2.2 %bitcast_dynamic-update-slice_fusion.2 = f32[1,2048,1024]{2,1,0:T(8,128)S(1)} fusion(f32[1,2048,1024]{2,1,0:T(8,128)S(1)} %bitcast_dynamic-update-slice_fusion.3, f16[256,1024]{1,0:T(8,128)(2,1)} %collective-permute-done.18, f32[2048,1024]{1,0:T(8,128)S(1)} %bitcast.35, f16[256,1024]{1,0:T(8,128)(2,1)} %collective-permute-done.19, ...), kind=kLoop, calls=%fused_computation.5 | loop fusion | flops 2621440 | bytes 3670028 | tf_op jit(solution)/shard_map/dynamic_update_slice | solution.py:125
  129.8 2.1 %bitcast_dynamic-update-slice_fusion.1 = f32[1,2048,1024]{2,1,0:T(8,128)S(1)} fusion(f32[1,2048,1024]{2,1,0:T(8,128)S(1)} %bitcast_dynamic-update-slice_fusion.2, f16[256,1024]{1,0:T(8,128)(2,1)S(1)} %collective-permute-done.21, f32[2048,1024]{1,0:T(8,128)S(1)} %bitcast.35, f16[256,1024]{1,0:T(8,128)(2,1)S(1)} %collective-permute-done.20, ...), kind=kLoop, calls=%fused_computation.4 | loop fusion | flops 2621440 | bytes 3670028 | tf_op jit(solution)/shard_map/dynamic_update_slice | solution.py:125
  131.9 0.0 copy-start
  131.9 3.4 %copy-done = f32[1,2048,1024]{2,1,0:T(8,128)} copy-done((f32[1,2048,1024]{2,1,0:T(8,128)}, f32[1,2048,1024]{2,1,0:T(8,128)S(1)}, u32[]{:S(2)}) %copy-start) | copy-done | bytes 8388632
  135.3 3.0 %bitcast_dynamic-update-slice_fusion = f32[1,2048,1024]{2,1,0:T(8,128)} fusion(f32[1,2048,1024]{2,1,0:T(8,128)} %copy-done, f16[256,1024]{1,0:T(8,128)(2,1)S(1)} %collective-permute-done.23, f32[2048,1024]{1,0:T(8,128)S(1)} %bitcast.35, f16[256,1024]{1,0:T(8,128)(2,1)S(1)} %collective-permute-done.22, f16[256,1024]{1,0:T(8,128)(2,1)} %collective-permute-done.17, ...), kind=kLoop, calls=%fused_computation.3 | loop fusion | flops 2621440 | bytes 3670536 | tf_op jit(solution)/shard_map/dynamic_update_slice | solution.py:125
  (44 shorter events, 0.1 us)
Async XLA Ops:
  6.2 29.7 %collective-permute-start = (f16[256,1024]{1,0:T(8,128)(2,1)S(1)}, f16[256,1024]{1,0:T(8,128)(2,1)S(1)}, u32[]{:S(2)}, u32[]{:S(2)}) collective-permute-start(f16[256,1024]{1,0:T(8,128)(2,1)S(1)} %get-tuple-element.132), channel_id=1, source_target_pairs={{0,1},{1,0},{2,3},{3,2},{4,5},{5,4},{6,7},{7,6},{8,9},{9,8},{10,11... | collective-permute-start | bytes 1572872 | tf_op jit(solution)/shard_map/ppermute | solution.py:23
  9.2 32.1 %collective-permute-start.4 = (f16[256,1024]{1,0:T(8,128)(2,1)S(1)}, f16[256,1024]{1,0:T(8,128)(2,1)S(1)}, u32[]{:S(2)}, u32[]{:S(2)}) collective-permute-start(f16[256,1024]{1,0:T(8,128)(2,1)S(1)} %get-tuple-element.131), channel_id=1, source_target_pairs={{0,1},{1,0},{2,3},{3,2},{4,5},{5,4},{6,7},{7,6},{8,9},{9,8},{10,11... | collective-permute-start | bytes 1572872 | tf_op jit(solution)/shard_map/ppermute | solution.py:23
  21.8 14.1 %slice-start = ((s8[8388608]{0:T(1024)(128)(4,1)}), s8[4194304]{0:T(1024)(128)(4,1)S(1)}, s32[]{:S(2)}) async-start(s8[8388608]{0:T(1024)(128)(4,1)} %bitcast.32), calls=%async_computation | async-start | bytes 8388608
  30.5 5.5 %slice-start.1 = ((s8[8388608]{0:T(1024)(128)(4,1)}), s8[4194304]{0:T(1024)(128)(4,1)S(1)}, s32[]{:S(2)}) async-start(s8[8388608]{0:T(1024)(128)(4,1)} %bitcast.32), calls=%async_computation.1 | async-start | bytes 8388608
  34.1 64.0 %copy-start.11 = (s32[16,3]{0,1:T(4,128)S(1)}, s32[16,3]{0,1:T(4,128)}, u32[]{:S(2)}) copy-start(s32[16,3]{0,1:T(4,128)} %param.7) | copy-start | bytes 580
  36.2 14.9 %collective-permute-start.1 = (f16[256,1024]{1,0:T(8,128)(2,1)S(1)}, f16[256,1024]{1,0:T(8,128)(2,1)S(1)}, u32[]{:S(2)}, u32[]{:S(2)}) collective-permute-start(f16[256,1024]{1,0:T(8,128)(2,1)S(1)} %get-tuple-element.72), channel_id=1, source_target_pairs={{0,1},{1,0},{2,3},{3,2},{4,5},{5,4},{6,7},{7,6},{8,9},{9,8},{10,11... | collective-permute-start | bytes 1572872 | tf_op jit(solution)/shard_map/ppermute | solution.py:23
  38.2 12.9 %collective-permute-start.2 = (f16[256,1024]{1,0:T(8,128)(2,1)S(1)}, f16[256,1024]{1,0:T(8,128)(2,1)S(1)}, u32[]{:S(2)}, u32[]{:S(2)}) collective-permute-start(f16[256,1024]{1,0:T(8,128)(2,1)S(1)} %multiply_convert_fusion.7), channel_id=1, source_target_pairs={{2,4},{4,2},{6,8},{8,6},{10,12},{12,10},{14,16},{16,14},{18,20},{2... | collective-permute-start | bytes 1572872 | tf_op jit(solution)/shard_map/ppermute | solution.py:32
  41.3 9.8 %collective-permute-start.3 = (f16[256,1024]{1,0:T(8,128)(2,1)S(1)}, f16[256,1024]{1,0:T(8,128)(2,1)S(1)}, u32[]{:S(2)}, u32[]{:S(2)}) collective-permute-start(f16[256,1024]{1,0:T(8,128)(2,1)S(1)} %multiply_convert_fusion.7), channel_id=1, source_target_pairs={{0,2},{2,0},{4,6},{6,4},{8,10},{10,8},{12,14},{14,12},{16,18},{18,... | collective-permute-start | bytes 1572872 | tf_op jit(solution)/shard_map/ppermute | solution.py:32
  41.5 19.3 %collective-permute-start.5 = (f16[256,1024]{1,0:T(8,128)(2,1)S(1)}, f16[256,1024]{1,0:T(8,128)(2,1)S(1)}, u32[]{:S(2)}, u32[]{:S(2)}) collective-permute-start(f16[256,1024]{1,0:T(8,128)(2,1)S(1)} %get-tuple-element.82), channel_id=1, source_target_pairs={{0,1},{1,0},{2,3},{3,2},{4,5},{5,4},{6,7},{7,6},{8,9},{9,8},{10,11... | collective-permute-start | bytes 1572872 | tf_op jit(solution)/shard_map/ppermute | solution.py:23
  42.1 21.4 %collective-permute-start.6 = (f16[256,1024]{1,0:T(8,128)(2,1)S(1)}, f16[256,1024]{1,0:T(8,128)(2,1)S(1)}, u32[]{:S(2)}, u32[]{:S(2)}) collective-permute-start(f16[256,1024]{1,0:T(8,128)(2,1)S(1)} %multiply_convert_fusion.6), channel_id=1, source_target_pairs={{2,4},{4,2},{6,8},{8,6},{10,12},{12,10},{14,16},{16,14},{18,20},{2... | collective-permute-start | bytes 1572872 | tf_op jit(solution)/shard_map/ppermute | solution.py:32
  51.1 12.4 %collective-permute-start.7 = (f16[256,1024]{1,0:T(8,128)(2,1)S(1)}, f16[256,1024]{1,0:T(8,128)(2,1)S(1)}, u32[]{:S(2)}, u32[]{:S(2)}) collective-permute-start(f16[256,1024]{1,0:T(8,128)(2,1)S(1)} %multiply_convert_fusion.6), channel_id=1, source_target_pairs={{0,2},{2,0},{4,6},{6,4},{8,10},{10,8},{12,14},{14,12},{16,18},{18,... | collective-permute-start | bytes 1572872 | tf_op jit(solution)/shard_map/ppermute | solution.py:32
  51.1 23.2 %copy-start.1 = (f16[256,1024]{1,0:T(8,128)(2,1)}, f16[256,1024]{1,0:T(8,128)(2,1)S(1)}, u32[]{:S(2)}) copy-start(f16[256,1024]{1,0:T(8,128)(2,1)S(1)} %collective-permute-done.2) | copy-start | bytes 1572868
  51.1 23.2 %copy-start.2 = (f16[256,1024]{1,0:T(8,128)(2,1)}, f16[256,1024]{1,0:T(8,128)(2,1)S(1)}, u32[]{:S(2)}) copy-start(f16[256,1024]{1,0:T(8,128)(2,1)S(1)} %collective-permute-done.3) | copy-start | bytes 1572868
  51.3 17.3 %collective-permute-start.10 = (f16[256,1024]{1,0:T(8,128)(2,1)S(1)}, f16[256,1024]{1,0:T(8,128)(2,1)S(1)}, u32[]{:S(2)}, u32[]{:S(2)}) collective-permute-start(f16[256,1024]{1,0:T(8,128)(2,1)S(1)} %multiply_convert_fusion.5), channel_id=1, source_target_pairs={{0,2},{2,0},{4,6},{6,4},{8,10},{10,8},{12,14},{14,12},{16,18},{18,... | collective-permute-start | bytes 1572872 | tf_op jit(solution)/shard_map/ppermute | solution.py:32
  58.5 14.8 %collective-permute-start.8 = (f16[256,1024]{1,0:T(8,128)(2,1)S(1)}, f16[256,1024]{1,0:T(8,128)(2,1)S(1)}, u32[]{:S(2)}, u32[]{:S(2)}) collective-permute-start(f16[256,1024]{1,0:T(8,128)(2,1)S(1)} %get-tuple-element.88), channel_id=1, source_target_pairs={{0,1},{1,0},{2,3},{3,2},{4,5},{5,4},{6,7},{7,6},{8,9},{9,8},{10,11... | collective-permute-start | bytes 1572872 | tf_op jit(solution)/shard_map/ppermute | solution.py:23
  60.9 12.4 %collective-permute-start.9 = (f16[256,1024]{1,0:T(8,128)(2,1)S(1)}, f16[256,1024]{1,0:T(8,128)(2,1)S(1)}, u32[]{:S(2)}, u32[]{:S(2)}) collective-permute-start(f16[256,1024]{1,0:T(8,128)(2,1)S(1)} %multiply_convert_fusion.5), channel_id=1, source_target_pairs={{2,4},{4,2},{6,8},{8,6},{10,12},{12,10},{14,16},{16,14},{18,20},{2... | collective-permute-start | bytes 1572872 | tf_op jit(solution)/shard_map/ppermute | solution.py:32
  63.5 10.8 %copy-start.3 = (f16[256,1024]{1,0:T(8,128)(2,1)}, f16[256,1024]{1,0:T(8,128)(2,1)S(1)}, u32[]{:S(2)}) copy-start(f16[256,1024]{1,0:T(8,128)(2,1)S(1)} %collective-permute-done.6) | copy-start | bytes 1572868
  63.5 10.8 %copy-start.5 = (f16[256,1024]{1,0:T(8,128)(2,1)}, f16[256,1024]{1,0:T(8,128)(2,1)S(1)}, u32[]{:S(2)}) copy-start(f16[256,1024]{1,0:T(8,128)(2,1)S(1)} %collective-permute-done.7) | copy-start | bytes 1572868
  64.6 19.0 %collective-permute-start.11 = (f16[256,1024]{1,0:T(8,128)(2,1)}, f16[256,1024]{1,0:T(8,128)(2,1)S(1)}, u32[]{:S(2)}, u32[]{:S(2)}) collective-permute-start(f16[256,1024]{1,0:T(8,128)(2,1)} %get-tuple-element.94), channel_id=1, source_target_pairs={{0,1},{1,0},{2,3},{3,2},{4,5},{5,4},{6,7},{7,6},{8,9},{9,8},{10,11... | collective-permute-start | bytes 1572872 | tf_op jit(solution)/shard_map/ppermute | solution.py:23
  66.2 25.1 %collective-permute-start.12 = (f16[256,1024]{1,0:T(8,128)(2,1)}, f16[256,1024]{1,0:T(8,128)(2,1)}, u32[]{:S(2)}, u32[]{:S(2)}) collective-permute-start(f16[256,1024]{1,0:T(8,128)(2,1)} %multiply_convert_fusion.4), channel_id=1, source_target_pairs={{2,4},{4,2},{6,8},{8,6},{10,12},{12,10},{14,16},{16,14},{18,20},{2... | collective-permute-start | bytes 1572872 | tf_op jit(solution)/shard_map/ppermute | solution.py:32
  68.7 5.6 %copy-start.7 = (f16[256,1024]{1,0:T(8,128)(2,1)}, f16[256,1024]{1,0:T(8,128)(2,1)S(1)}, u32[]{:S(2)}) copy-start(f16[256,1024]{1,0:T(8,128)(2,1)S(1)} %collective-permute-done.10) | copy-start | bytes 1572868
  68.7 22.6 %collective-permute-start.13 = (f16[256,1024]{1,0:T(8,128)(2,1)}, f16[256,1024]{1,0:T(8,128)(2,1)}, u32[]{:S(2)}, u32[]{:S(2)}) collective-permute-start(f16[256,1024]{1,0:T(8,128)(2,1)} %multiply_convert_fusion.4), channel_id=1, source_target_pairs={{0,2},{2,0},{4,6},{6,4},{8,10},{10,8},{12,14},{14,12},{16,18},{18,... | collective-permute-start | bytes 1572872 | tf_op jit(solution)/shard_map/ppermute | solution.py:32
  73.2 1.1 copy-start.9
  74.3 22.4 %collective-permute-start.14 = (f16[256,1024]{1,0:T(8,128)(2,1)}, f16[256,1024]{1,0:T(8,128)(2,1)}, u32[]{:S(2)}, u32[]{:S(2)}) collective-permute-start(f16[256,1024]{1,0:T(8,128)(2,1)} %get-tuple-element.100), channel_id=1, source_target_pairs={{0,1},{1,0},{2,3},{3,2},{4,5},{5,4},{6,7},{7,6},{8,9},{9,8},{10,11... | collective-permute-start | bytes 1572872 | tf_op jit(solution)/shard_map/ppermute | solution.py:23
  75.9 25.7 %collective-permute-start.15 = (f16[256,1024]{1,0:T(8,128)(2,1)}, f16[256,1024]{1,0:T(8,128)(2,1)}, u32[]{:S(2)}, u32[]{:S(2)}) collective-permute-start(f16[256,1024]{1,0:T(8,128)(2,1)} %multiply_convert_fusion.3), channel_id=1, source_target_pairs={{2,4},{4,2},{6,8},{8,6},{10,12},{12,10},{14,16},{16,14},{18,20},{2... | collective-permute-start | bytes 1572872 | tf_op jit(solution)/shard_map/ppermute | solution.py:32
  83.6 18.0 %collective-permute-start.16 = (f16[256,1024]{1,0:T(8,128)(2,1)}, f16[256,1024]{1,0:T(8,128)(2,1)}, u32[]{:S(2)}, u32[]{:S(2)}) collective-permute-start(f16[256,1024]{1,0:T(8,128)(2,1)} %multiply_convert_fusion.3), channel_id=1, source_target_pairs={{0,2},{2,0},{4,6},{6,4},{8,10},{10,8},{12,14},{14,12},{16,18},{18,... | collective-permute-start | bytes 1572872 | tf_op jit(solution)/shard_map/ppermute | solution.py:32
  93.5 17.8 %collective-permute-start.18 = (f16[256,1024]{1,0:T(8,128)(2,1)}, f16[256,1024]{1,0:T(8,128)(2,1)}, u32[]{:S(2)}, u32[]{:S(2)}) collective-permute-start(f16[256,1024]{1,0:T(8,128)(2,1)} %multiply_convert_fusion.2), channel_id=1, source_target_pairs={{2,4},{4,2},{6,8},{8,6},{10,12},{12,10},{14,16},{16,14},{18,20},{2... | collective-permute-start | bytes 1572872 | tf_op jit(solution)/shard_map/ppermute | solution.py:32
  96.7 14.7 %collective-permute-start.19 = (f16[256,1024]{1,0:T(8,128)(2,1)}, f16[256,1024]{1,0:T(8,128)(2,1)}, u32[]{:S(2)}, u32[]{:S(2)}) collective-permute-start(f16[256,1024]{1,0:T(8,128)(2,1)} %multiply_convert_fusion.2), channel_id=1, source_target_pairs={{0,2},{2,0},{4,6},{6,4},{8,10},{10,8},{12,14},{14,12},{16,18},{18,... | collective-permute-start | bytes 1572872 | tf_op jit(solution)/shard_map/ppermute | solution.py:32
  96.7 14.7 %collective-permute-start.17 = (f16[256,1024]{1,0:T(8,128)(2,1)}, f16[256,1024]{1,0:T(8,128)(2,1)}, u32[]{:S(2)}, u32[]{:S(2)}) collective-permute-start(f16[256,1024]{1,0:T(8,128)(2,1)} %get-tuple-element.106), channel_id=1, source_target_pairs={{0,1},{1,0},{2,3},{3,2},{4,5},{5,4},{6,7},{7,6},{8,9},{9,8},{10,11... | collective-permute-start | bytes 1572872 | tf_op jit(solution)/shard_map/ppermute | solution.py:23
  101.5 18.3 %slice-start.2 = ((s8[8388608]{0:T(1024)(128)(4,1)}), s8[4194304]{0:T(1024)(128)(4,1)S(1)}, s32[]{:S(2)}) async-start(s8[8388608]{0:T(1024)(128)(4,1)} %bitcast.34), calls=%async_computation.2 | async-start | bytes 8388608
  101.5 18.3 %copy-start.4 = (f16[256,1024]{1,0:T(8,128)(2,1)S(1)}, f16[256,1024]{1,0:T(8,128)(2,1)}, u32[]{:S(2)}) copy-start(f16[256,1024]{1,0:T(8,128)(2,1)} %copy-done.3) | copy-start | bytes 1572868
  101.5 18.3 %copy-start.6 = (f16[256,1024]{1,0:T(8,128)(2,1)S(1)}, f16[256,1024]{1,0:T(8,128)(2,1)}, u32[]{:S(2)}) copy-start(f16[256,1024]{1,0:T(8,128)(2,1)} %copy-done.5) | copy-start | bytes 1572868
  103.3 26.5 %collective-permute-start.20 = (f16[256,1024]{1,0:T(8,128)(2,1)S(1)}, f16[256,1024]{1,0:T(8,128)(2,1)S(1)}, u32[]{:S(2)}, u32[]{:S(2)}) collective-permute-start(f16[256,1024]{1,0:T(8,128)(2,1)S(1)} %multiply_convert_fusion.1), channel_id=1, source_target_pairs={{0,2},{2,0},{4,6},{6,4},{8,10},{10,8},{12,14},{14,12},{16,18},{18,... | collective-permute-start | bytes 1572872 | tf_op jit(solution)/shard_map/ppermute | solution.py:32
  105.0 24.8 %collective-permute-start.21 = (f16[256,1024]{1,0:T(8,128)(2,1)S(1)}, f16[256,1024]{1,0:T(8,128)(2,1)S(1)}, u32[]{:S(2)}, u32[]{:S(2)}) collective-permute-start(f16[256,1024]{1,0:T(8,128)(2,1)S(1)} %multiply_convert_fusion.1), channel_id=1, source_target_pairs={{2,4},{4,2},{6,8},{8,6},{10,12},{12,10},{14,16},{16,14},{18,20},{2... | collective-permute-start | bytes 1572872 | tf_op jit(solution)/shard_map/ppermute | solution.py:32
  112.9 19.0 %collective-permute-start.22 = (f16[256,1024]{1,0:T(8,128)(2,1)S(1)}, f16[256,1024]{1,0:T(8,128)(2,1)S(1)}, u32[]{:S(2)}, u32[]{:S(2)}) collective-permute-start(f16[256,1024]{1,0:T(8,128)(2,1)S(1)} %multiply_convert_fusion), channel_id=1, source_target_pairs={{0,2},{2,0},{4,6},{6,4},{8,10},{10,8},{12,14},{14,12},{16,18},{18,... | collective-permute-start | bytes 1572872 | tf_op jit(solution)/shard_map/ppermute | solution.py:32
  113.0 18.9 %collective-permute-start.23 = (f16[256,1024]{1,0:T(8,128)(2,1)S(1)}, f16[256,1024]{1,0:T(8,128)(2,1)S(1)}, u32[]{:S(2)}, u32[]{:S(2)}) collective-permute-start(f16[256,1024]{1,0:T(8,128)(2,1)S(1)} %multiply_convert_fusion), channel_id=1, source_target_pairs={{2,4},{4,2},{6,8},{8,6},{10,12},{12,10},{14,16},{16,14},{18,20},{2... | collective-permute-start | bytes 1572872 | tf_op jit(solution)/shard_map/ppermute | solution.py:32
  116.1 5.9 %copy-start.8 = (f16[256,1024]{1,0:T(8,128)(2,1)S(1)}, f16[256,1024]{1,0:T(8,128)(2,1)}, u32[]{:S(2)}) copy-start(f16[256,1024]{1,0:T(8,128)(2,1)} %copy-done.7) | copy-start | bytes 1572868
  116.1 5.9 %copy-start.10 = (f16[256,1024]{1,0:T(8,128)(2,1)S(1)}, f16[256,1024]{1,0:T(8,128)(2,1)}, u32[]{:S(2)}) copy-start(f16[256,1024]{1,0:T(8,128)(2,1)} %copy-done.9) | copy-start | bytes 1572868
  118.8 2.2 %slice-start.3 = ((s8[8388608]{0:T(1024)(128)(4,1)}), s8[4194304]{0:T(1024)(128)(4,1)S(1)}, s32[]{:S(2)}) async-start(s8[8388608]{0:T(1024)(128)(4,1)} %bitcast.34), calls=%async_computation.3 | async-start | bytes 8388608
  131.9 3.4 %copy-start = (f32[1,2048,1024]{2,1,0:T(8,128)}, f32[1,2048,1024]{2,1,0:T(8,128)S(1)}, u32[]{:S(2)}) copy-start(f32[1,2048,1024]{2,1,0:T(8,128)S(1)} %bitcast_dynamic-update-slice_fusion.1) | copy-start | bytes 25165828

commit v7 on v4

v7 whole, which is shorter than its diff:
```python
import math

import jax
import jax.numpy as jnp
from jax import lax
from jax.sharding import PartitionSpec as P

MIX_DENOM = 64
RATE = 0.03
LARGEST = 6.0
WIRE = jnp.float16
STEP = 256
AHEAD = 2


def from_behind(value, axis, steps):
    count = lax.axis_size(axis)
    pairs = [(source, (source + steps) % count) for source in range(count)]
    return lax.ppermute(value, axis, pairs)


def swapped(value, axis, first):
    count = lax.axis_size(axis)
    pairs = []
    for source in range(first, count, 2):
        partner = (source + 1) % count
        pairs += [(source, partner), (partner, source)]
    return lax.ppermute(value, axis, pairs)


def wire_scale(tokens):
    bound = LARGEST + RATE * LARGEST * LARGEST * tokens
    return 2.0 ** math.floor(math.log2(float(jnp.finfo(WIRE).max) / bound))


def on_device(params, inputs, cotangent, mix):
    weights = params[0]
    features = inputs[0]
    cot_local = cotangent[0]
    rows = weights.shape[0]
    shards = lax.axis_size("fsdp")
    scale = wire_scale(features.shape[0] * shards)
    replica = lax.axis_index("blk")
    shard = lax.axis_index("fsdp")
    pick = (jnp.arange(lax.axis_size("blk")) == replica).astype(jnp.float32)
    coeff = jnp.dot(pick, mix.astype(jnp.float32), precision=lax.Precision.HIGHEST) / MIX_DENOM
    even = replica % 2 == 0
    c_self = coeff[1]
    c_near = jnp.where(even, coeff[2], coeff[0]) / scale
    c_far = jnp.where(even, coeff[0], coeff[2]) / scale
    step = math.gcd(rows, STEP)
    chunks = rows // step

    def partial(owner, first, count):
        block = lax.dynamic_slice_in_dim(features, owner * rows + first, count, axis=1)
        return lax.dot_general(
            block, cot_local, (((0,), (0,)), ((), ())), preferred_element_type=jnp.float32
        )

    def owner(shard, away):
        other = shard + away
        return jnp.where(other < shards, other, other - shards)

    def for_others(shard, first, count):
        return [
            (partial(owner(shard, away), first, count) * (RATE * scale)).astype(WIRE)
            for away in range(1, shards)
        ]

    def send_terms(terms):
        return [from_behind(term, "fsdp", away) for away, term in zip(range(1, shards), terms)]

    def rows_of(value, chunk):
        return value[chunk * step:(chunk + 1) * step]

    def own_part(shard, first, count):
        return rows_from(weights, first, count) - RATE * partial(shard, first * step, count * step)

    def rows_from(value, first, count):
        return value[first * step:(first + count) * step]

    def u_of(chunk):
        total = rows_of(base[0], chunk) if chunk < split else rows_of(base[1], chunk - split)
        for term in arrived[chunk]:
            total = total - term.astype(jnp.float32) / scale
        return total

    split = min(2, chunks)
    early = min(AHEAD + 1, chunks)
    near = {}
    far = {}
    terms = {chunk: for_others(shard, chunk * step, step) for chunk in range(early)}
    arrived = {chunk: send_terms(terms[chunk]) for chunk in range(min(AHEAD, chunks))}
    base = [own_part(shard, 0, split)]

    arrived[0], base, terms = lax.optimization_barrier((arrived[0], base, terms))
    for chunk in range(chunks):
        if chunk in (1, 2):
            arrived[chunk], base, terms = lax.optimization_barrier((arrived[chunk], base, terms))
        if chunk == 1:
            arrived[1], far[0] = lax.optimization_barrier((arrived[1], far[0]))
        if chunk >= 2:
            arrived[chunk], far[chunk - 2], near[chunk - 2] = lax.optimization_barrier(
                (arrived[chunk], far[chunk - 2], near[chunk - 2])
            )
        sent = (u_of(chunk) * scale).astype(WIRE)
        sent, base, later = lax.optimization_barrier((sent, base, shard))
        if chunk == 0 and early < chunks:
            rest = for_others(later, early * step, rows - early * step)
            for after in range(early, chunks):
                terms[after] = [rows_of(term, after - early) for term in rest]
        if chunk == 1 and split < chunks:
            base.append(own_part(later, split, chunks - split))
        after = chunk + AHEAD
        if after < chunks:
            terms[after], sent = lax.optimization_barrier((terms[after], sent))
            arrived[after] = send_terms(terms[after])
        if chunk == chunks - 1:
            far[0], near[0], sent = lax.optimization_barrier((far[0], near[0], sent))
        far[chunk] = swapped(sent, "blk", 1)
        near[chunk] = swapped(sent, "blk", 0)

    out = jnp.zeros_like(weights)
    for chunk in range(chunks):
        mixed = (
            c_near * near[chunk].astype(jnp.float32)
            + c_self * u_of(chunk)
            + c_far * far[chunk].astype(jnp.float32)
        )
        out = lax.dynamic_update_slice_in_dim(out, mixed, chunk * step, axis=0)
    return out[None]


def solution(mesh):
    return jax.shard_map(
        on_device,
        mesh=mesh,
        in_specs=(P("blk", "fsdp", None), P("blk", "fsdp", None), P("blk", "fsdp", None), P()),
        out_specs=P("blk", "fsdp", None),
        check_vma=False,
    )
```

time: 125 us -> 134 us (1.072); the launches traced: 124 us -> 131 us
  starting transfers between devices: 17.3 us -> 36.8 us
  waiting for transfers between devices: 40.5 us -> 33.2 us
  other arithmetic: 36 us -> 29.5 us
  matrix products: 18.9 us -> 22.7 us
  local copies, waits for them, and re-layouts: 8.64 us -> 6.4 us
    ppermute x16, starting transfers between devices: 8.58 us -> 21.4 us  [swapped(): return lax.ppermute(value, axis, pairs)]
    convert_element_type x8, other arithmetic: 22.4 us -> 11 us  [on_device(): sent = (u_of(chunk) * scale).astype(WIRE)]
    ppermute x8, waiting for transfers between devices: 19.6 us -> 10.4 us  [from_behind(): return lax.ppermute(value, axis, pairs)]
    ppermute x8, starting transfers between devices: 8.71 us -> 15.4 us  [from_behind(): return lax.ppermute(value, axis, pairs)]
    dynamic_update_slice x7, other arithmetic: 11.5 us -> 15.5 us  [on_device(): out = lax.dynamic_update_slice_in_dim(out, mixed, chunk * step, axis=0)]
    dot_general x5 -> x6, matrix products: 18.8 us -> 22.6 us  [partial(): lax.dot_general(block, cot_local, (((0,), (0,)), ((), ())), preferred_ele...]
    slice x1, local copies, waits for them, and re-layouts: 4.01 us -> 1.79 us  [rows_of(): return value[chunk * step:(chunk + 1) * step]]
    ppermute x16, waiting for transfers between devices: 20.9 us -> 22.8 us  [swapped(): return lax.ppermute(value, axis, pairs)]
  transfers between devices with their start and end apart: 24 -> 24, of which waited for: 11 -> 9; matrix products, arithmetic and copies ran while one was open for 46% -> 39% of each run, Pallas kernels for 0% -> 0%
where the time goes in v7:
time: 134 us; the launch traced here: 131 us
  starting transfers between devices  36.8 us (27%)
  waiting for transfers between devices  33.2 us (25%)
  other arithmetic  29.5 us (22%)
  matrix products  22.7 us (17%)
  local copies, waits for them, and re-layouts  6.4 us (5%)
  between operations  2.67 us (2%)
    ppermute x16, waiting for transfers between devices, swapped(): return lax.ppermute(value, axis, pairs)  22.8 us
    dot_general x6, matrix products, partial(): lax.dot_general(block, cot_local, (((0,), (0,)), ((), ())), preferred_ele...  22.6 us
    ppermute x16, starting transfers between devices, swapped(): return lax.ppermute(value, axis, pairs)  21.4 us
    dynamic_update_slice x7, other arithmetic, on_device(): out = lax.dynamic_update_slice_in_dim(out, mixed, chunk * step, axis=0)  15.5 us
    ppermute x8, starting transfers between devices, from_behind(): return lax.ppermute(value, axis, pairs)  15.4 us
    convert_element_type x8, other arithmetic, on_device(): sent = (u_of(chunk) * scale).astype(WIRE)  11 us
    ppermute x8, waiting for transfers between devices, from_behind(): return lax.ppermute(value, axis, pairs)  10.4 us
    add x1, other arithmetic, on_device(): c_near * near[chunk].astype(jnp.float32) + c_self * u_of(chunk)  3.06 us
  transfers between devices with their start and end apart: 24, of which 9 were waited for; matrix products, arithmetic and copies ran while one was open for 39% of the time, Pallas kernels for 0%

profile of v7, /device:TPU:1, one launch (start us, length us, event | category | flops | bytes accessed | tf_op | source)
XLA Modules:
  0.0 131.3 jit_solution(2246205865967357643)
XLA Ops:
  0.0 1.5 %copy-done = bf16[1,896,1024]{2,1,0:T(8,128)(2,1)S(1)} copy-done((bf16[1,896,1024]{2,1,0:T(8,128)(2,1)S(1)}, bf16[1,896,1024]{2,1,0:T(8,128)(2,1)}, u32[]{:S(2)}) %copy-start) | copy-done | bytes 1835032
  1.5 1.7 %fusion.31 = f16[256,1024]{1,0:T(8,128)(2,1)S(1)} fusion(bf16[1,896,1024]{2,1,0:T(8,128)(2,1)S(1)} %copy-done, bf16[1,896,4096]{2,1,0:T(8,128)(2,1)} %param.5, s32[]{:T(128)S(6)} %select_n.43), kind=kOutput, calls=%fused_computation.23 | convolution fusion | flops 470286336 | bytes 2818052 | tf_op jit(solution)/shard_map/dot_general | solution.py:56
  3.3 2.1 %collective-permute-start = (f16[256,1024]{1,0:T(8,128)(2,1)S(1)}, f16[256,1024]{1,0:T(8,128)(2,1)S(1)}, u32[]{:S(2)}, u32[]{:S(2)}) collective-permute-start(f16[256,1024]{1,0:T(8,128)(2,1)S(1)} %fusion.31), channel_id=1, source_target_pairs={{0,1},{1,0},{2,3},{3,2},{4,5},{5,4},{6,7},{7,6},{8,9},{9,8},{10,11... | collective-permute-start | bytes 1572872 | tf_op jit(solution)/shard_map/ppermute | solution.py:19
  5.4 2.5 %fusion.28 = f16[256,1024]{1,0:T(8,128)(2,1)} fusion(bf16[1,896,1024]{2,1,0:T(8,128)(2,1)S(1)} %copy-done, bf16[1,896,4096]{2,1,0:T(8,128)(2,1)} %param.5, s32[]{:T(128)S(6)} %select_n.45), kind=kOutput, calls=%fused_computation.22 | convolution fusion | flops 470286336 | bytes 2818052 | tf_op jit(solution)/shard_map/dot_general | solution.py:56
  7.9 0.0 collective-permute-start.2
  8.0 2.5 %fusion.25 = f16[256,1024]{1,0:T(8,128)(2,1)} fusion(bf16[1,896,1024]{2,1,0:T(8,128)(2,1)S(1)} %copy-done, bf16[1,896,4096]{2,1,0:T(8,128)(2,1)} %param.5, s32[]{:T(128)S(6)} %select_n.46), kind=kOutput, calls=%fused_computation.21 | convolution fusion | flops 470286336 | bytes 2818052 | tf_op jit(solution)/shard_map/dot_general | solution.py:56
  10.5 3.2 %bitcast_subtract_fusion.1 = f32[512,1024]{1,0:T(8,128)S(1)} fusion(f32[1,2048,1024]{2,1,0:T(8,128)} %param.4, bf16[1,896,1024]{2,1,0:T(8,128)(2,1)S(1)} %copy-done, bf16[1,896,4096]{2,1,0:T(8,128)(2,1)} %param.5, s32[]{:T(128)S(6)} %select_n.44), kind=kOutput, calls=%fused_computation.7 | convolution fusion | flops 940572672 | bytes 6946820 | tf_op jit(solution)/shard_map/dot_general | solution.py:56
  13.7 3.4 %collective-permute-done = f16[256,1024]{1,0:T(8,128)(2,1)S(1)} collective-permute-done((f16[256,1024]{1,0:T(8,128)(2,1)S(1)}, f16[256,1024]{1,0:T(8,128)(2,1)S(1)}, u32[]{:S(2)}, u32[]{:S(2)}) %collective-permute-start) | collective-permute-done | bytes 524320 | tf_op jit(solution)/shard_map/ppermute | solution.py:19
  17.0 1.0 multiply_convert_fusion.8
  18.1 3.7 %collective-permute-start.3 = (f16[256,1024]{1,0:T(8,128)(2,1)}, f16[256,1024]{1,0:T(8,128)(2,1)}, u32[]{:S(2)}, u32[]{:S(2)}) collective-permute-start(f16[256,1024]{1,0:T(8,128)(2,1)} %multiply_convert_fusion.8), channel_id=1, source_target_pairs={{2,4},{4,2},{6,8},{8,6},{10,12},{12,10},{14,16},{16,14},{18,20},{2... | collective-permute-start | bytes 1572872 | tf_op jit(solution)/shard_map/ppermute | solution.py:28
  21.8 0.8 collective-permute-start.4
  22.6 4.9 %multiply_convert_fusion = f16[1280,1024]{1,0:T(8,128)(2,1)S(1)} fusion(bf16[1,896,4096]{2,1,0:T(8,128)(2,1)} %param.5, s32[]{:T(128)S(6)} %select_n.48, bf16[1,896,1024]{2,1,0:T(8,128)(2,1)S(1)} %copy-done), kind=kOutput, calls=%fused_computation.2 | convolution fusion | flops 2351431680 | bytes 6750212 | tf_op jit(solution)/shard_map/dot_general | solution.py:56
  27.6 1.3 collective-permute-start.1
  28.9 1.8 %fusion.54 = (f16[256,1024]{1,0:T(8,128)(2,1)}, f16[256,1024]{1,0:T(8,128)(2,1)}, f16[256,1024]{1,0:T(8,128)(2,1)}, f16[256,1024]{1,0:T(8,128)(2,1)}, f16[256,1024]{1,0:T(8,128)(2,1)}) fusion(f16[1280,1024]{1,0:T(8,128)(2,1)S(1)} %multiply_convert_fusion), kind=kLoop, calls=%fused_computation.69 | loop fusion | bytes 5242880 | tf_op jit(solution)/shard_map/slice | solution.py:74
  30.7 4.1 %collective-permute-done.3 = f16[256,1024]{1,0:T(8,128)(2,1)} collective-permute-done((f16[256,1024]{1,0:T(8,128)(2,1)}, f16[256,1024]{1,0:T(8,128)(2,1)}, u32[]{:S(2)}, u32[]{:S(2)}) %collective-permute-start.3) | collective-permute-done | bytes 524320 | tf_op jit(solution)/shard_map/ppermute | solution.py:28
  34.8 1.1 multiply_convert_fusion.7
  35.8 1.6 %collective-permute-start.6 = (f16[256,1024]{1,0:T(8,128)(2,1)}, f16[256,1024]{1,0:T(8,128)(2,1)}, u32[]{:S(2)}, u32[]{:S(2)}) collective-permute-start(f16[256,1024]{1,0:T(8,128)(2,1)} %multiply_convert_fusion.7), channel_id=1, source_target_pairs={{2,4},{4,2},{6,8},{8,6},{10,12},{12,10},{14,16},{16,14},{18,20},{2... | collective-permute-start | bytes 1572872 | tf_op jit(solution)/shard_map/ppermute | solution.py:28
  37.4 6.9 %collective-permute-start.5 = (f16[256,1024]{1,0:T(8,128)(2,1)}, f16[256,1024]{1,0:T(8,128)(2,1)}, u32[]{:S(2)}, u32[]{:S(2)}) collective-permute-start(f16[256,1024]{1,0:T(8,128)(2,1)} %get-tuple-element.96), channel_id=1, source_target_pairs={{0,1},{1,0},{2,3},{3,2},{4,5},{5,4},{6,7},{7,6},{8,9},{9,8},{10,11... | collective-permute-start | bytes 1572872 | tf_op jit(solution)/shard_map/ppermute | solution.py:19
  44.3 7.6 %bitcast_subtract_fusion = f32[1536,1024]{1,0:T(8,128)S(1)} fusion(f32[1,2048,1024]{2,1,0:T(8,128)} %param.4, bf16[1,896,4096]{2,1,0:T(8,128)(2,1)} %param.5, s32[]{:T(128)S(6)} %select_n.49, bf16[1,896,1024]{2,1,0:T(8,128)(2,1)S(1)} %copy-done), kind=kOutput, calls=%fused_computation.1 | convolution fusion | flops 2821718016 | bytes 17170436 | tf_op jit(solution)/shard_map/dot_general | solution.py:56
  51.9 0.0 copy-start.1
  51.9 0.0 copy-start.13
  51.9 0.0 collective-permute-done.4
  52.0 0.2 multiply_convert_fusion.6
  52.2 0.9 collective-permute-start.10
  53.0 0.0 collective-permute-start.8
  53.0 3.4 %collective-permute-done.5 = f16[256,1024]{1,0:T(8,128)(2,1)} collective-permute-done((f16[256,1024]{1,0:T(8,128)(2,1)}, f16[256,1024]{1,0:T(8,128)(2,1)}, u32[]{:S(2)}, u32[]{:S(2)}) %collective-permute-start.5) | collective-permute-done | bytes 524320 | tf_op jit(solution)/shard_map/ppermute | solution.py:19
  56.4 1.2 collective-permute-start.9
  57.6 2.0 %multiply_convert_fusion.5 = f16[256,1024]{1,0:T(8,128)(2,1)} fusion(f16[256,1024]{1,0:T(8,128)(2,1)} %collective-permute-done.5, f32[1536,1024]{1,0:T(8,128)S(1)} %bitcast_subtract_fusion), kind=kLoop, calls=%fused_computation.42 | loop fusion | flops 1310720 | bytes 2097152 | tf_op jit(solution)/shard_map/convert_element_type | solution.py:106
  59.7 1.7 %collective-permute-start.11 = (f16[256,1024]{1,0:T(8,128)(2,1)}, f16[256,1024]{1,0:T(8,128)(2,1)}, u32[]{:S(2)}, u32[]{:S(2)}) collective-permute-start(f16[256,1024]{1,0:T(8,128)(2,1)} %get-tuple-element.122), channel_id=1, source_target_pairs={{0,1},{1,0},{2,3},{3,2},{4,5},{5,4},{6,7},{7,6},{8,9},{9,8},{10,11... | collective-permute-start | bytes 1572872 | tf_op jit(solution)/shard_map/ppermute | solution.py:19
  61.4 0.3 collective-permute-start.12
  61.6 0.0 collective-permute-done.10
  61.6 4.7 %collective-permute-start.13 = (f16[256,1024]{1,0:T(8,128)(2,1)}, f16[256,1024]{1,0:T(8,128)(2,1)}, u32[]{:S(2)}, u32[]{:S(2)}) collective-permute-start(f16[256,1024]{1,0:T(8,128)(2,1)} %multiply_convert_fusion.5), channel_id=1, source_target_pairs={{0,2},{2,0},{4,6},{6,4},{8,10},{10,8},{12,14},{14,12},{16,18},{18,... | collective-permute-start | bytes 1572872 | tf_op jit(solution)/shard_map/ppermute | solution.py:28
  66.4 1.2 collective-permute-done.8
  67.5 13.1 %collective-permute-done.9 = f16[256,1024]{1,0:T(8,128)(2,1)S(1)} collective-permute-done((f16[256,1024]{1,0:T(8,128)(2,1)S(1)}, f16[256,1024]{1,0:T(8,128)(2,1)S(1)}, u32[]{:S(2)}, u32[]{:S(2)}) %collective-permute-start.9) | collective-permute-done | bytes 524320 | tf_op jit(solution)/shard_map/ppermute | solution.py:28
  80.6 1.0 multiply_convert_fusion.4
  81.7 1.7 %collective-permute-start.14 = (f16[256,1024]{1,0:T(8,128)(2,1)}, f16[256,1024]{1,0:T(8,128)(2,1)}, u32[]{:S(2)}, u32[]{:S(2)}) collective-permute-start(f16[256,1024]{1,0:T(8,128)(2,1)} %get-tuple-element.129), channel_id=1, source_target_pairs={{0,1},{1,0},{2,3},{3,2},{4,5},{5,4},{6,7},{7,6},{8,9},{9,8},{10,11... | collective-permute-start | bytes 1572872 | tf_op jit(solution)/shard_map/ppermute | solution.py:19
  83.4 2.8 %collective-permute-start.15 = (f16[256,1024]{1,0:T(8,128)(2,1)}, f16[256,1024]{1,0:T(8,128)(2,1)}, u32[]{:S(2)}, u32[]{:S(2)}) collective-permute-start(f16[256,1024]{1,0:T(8,128)(2,1)} %multiply_convert_fusion.4), channel_id=1, source_target_pairs={{2,4},{4,2},{6,8},{8,6},{10,12},{12,10},{14,16},{16,14},{18,20},{2... | collective-permute-start | bytes 1572872 | tf_op jit(solution)/shard_map/ppermute | solution.py:28
  86.2 1.4 %collective-permute-done.12 = f16[256,1024]{1,0:T(8,128)(2,1)} collective-permute-done((f16[256,1024]{1,0:T(8,128)(2,1)}, f16[256,1024]{1,0:T(8,128)(2,1)}, u32[]{:S(2)}, u32[]{:S(2)}) %collective-permute-start.12) | collective-permute-done | bytes 524320 | tf_op jit(solution)/shard_map/ppermute | solution.py:28
  87.6 2.4 %multiply_convert_fusion.3 = f16[256,1024]{1,0:T(8,128)(2,1)} fusion(f16[256,1024]{1,0:T(8,128)(2,1)} %collective-permute-done.11, f32[1536,1024]{1,0:T(8,128)} %copy-done.1), kind=kLoop, calls=%fused_computation.38 | loop fusion | flops 1310720 | bytes 2097152 | tf_op jit(solution)/shard_map/convert_element_type | solution.py:106
  90.0 1.2 collective-permute-start.18
  91.2 1.7 %collective-permute-start.17 = (f16[256,1024]{1,0:T(8,128)(2,1)}, f16[256,1024]{1,0:T(8,128)(2,1)}, u32[]{:S(2)}, u32[]{:S(2)}) collective-permute-start(f16[256,1024]{1,0:T(8,128)(2,1)} %get-tuple-element.136), channel_id=1, source_target_pairs={{0,1},{1,0},{2,3},{3,2},{4,5},{5,4},{6,7},{7,6},{8,9},{9,8},{10,11... | collective-permute-start | bytes 1572872 | tf_op jit(solution)/shard_map/ppermute | solution.py:19
  92.9 0.1 fusion.34
  93.0 0.7 fusion.55
  96.1 2.1 %collective-permute-done.15 = f16[256,1024]{1,0:T(8,128)(2,1)} collective-permute-done((f16[256,1024]{1,0:T(8,128)(2,1)}, f16[256,1024]{1,0:T(8,128)(2,1)}, u32[]{:S(2)}, u32[]{:S(2)}) %collective-permute-start.15) | collective-permute-done | bytes 524320 | tf_op jit(solution)/shard_map/ppermute | solution.py:28
  98.2 1.6 %multiply_convert_fusion.2 = f16[256,1024]{1,0:T(8,128)(2,1)S(1)} fusion(f16[256,1024]{1,0:T(8,128)(2,1)} %collective-permute-done.14, f32[1536,1024]{1,0:T(8,128)} %copy-done.1), kind=kLoop, calls=%fused_computation.36 | loop fusion | flops 1310720 | bytes 2097152 | tf_op jit(solution)/shard_map/convert_element_type | solution.py:106
  99.8 0.1 collective-permute-start.20
  99.9 2.5 %collective-permute-start.21 = (f16[256,1024]{1,0:T(8,128)(2,1)S(1)}, f16[256,1024]{1,0:T(8,128)(2,1)S(1)}, u32[]{:S(2)}, u32[]{:S(2)}) collective-permute-start(f16[256,1024]{1,0:T(8,128)(2,1)S(1)} %multiply_convert_fusion.2), channel_id=1, source_target_pairs={{2,4},{4,2},{6,8},{8,6},{10,12},{12,10},{14,16},{16,14},{18,20},{2... | collective-permute-start | bytes 1572872 | tf_op jit(solution)/shard_map/ppermute | solution.py:28
  102.4 2.5 %collective-permute-done.17 = f16[256,1024]{1,0:T(8,128)(2,1)} collective-permute-done((f16[256,1024]{1,0:T(8,128)(2,1)}, f16[256,1024]{1,0:T(8,128)(2,1)}, u32[]{:S(2)}, u32[]{:S(2)}) %collective-permute-start.17) | collective-permute-done | bytes 524320 | tf_op jit(solution)/shard_map/ppermute | solution.py:19
  105.0 1.6 %multiply_convert_fusion.1 = f16[256,1024]{1,0:T(8,128)(2,1)S(1)} fusion(f16[256,1024]{1,0:T(8,128)(2,1)} %collective-permute-done.17, f32[1536,1024]{1,0:T(8,128)} %copy-done.1), kind=kLoop, calls=%fused_computation.34 | loop fusion | flops 1310720 | bytes 2097152 | tf_op jit(solution)/shard_map/convert_element_type | solution.py:106
  106.6 1.2 collective-permute-start.22
  107.8 0.4 collective-permute-start.23
  108.2 3.1 %multiply_add_fusion = f32[256,1024]{1,0:T(8,128)S(1)} fusion(f16[256,1024]{1,0:T(8,128)(2,1)} %collective-permute-done.3, f32[512,1024]{1,0:T(8,128)} %copy-done.2, f16[256,1024]{1,0:T(8,128)(2,1)} %collective-permute-done.4, f16[256,1024]{1,0:T(8,128)(2,1)S(1)} %collective-permute-done, f32[]{:T(128)S(6)} %div.51, f32[]{:T(128)} %bitcast.13, f32[]{:T(128)S(6)} %div.42), kind=kLoop, calls=%fused_computation.33 | loop fusion | flops 2621440 | bytes 3670028 | tf_op jit(solution)/shard_map/add | solution.py:126
  111.2 0.0 slice-start.1
  111.3 1.1 pad_bitcast_fusion
  112.3 2.3 %bitcast_dynamic-update-slice_fusion.6 = f32[1,2048,1024]{2,1,0:T(8,128)S(1)} fusion(f32[1,2048,1024]{2,1,0:T(8,128)S(1)} %pad_bitcast_fusion, f16[256,1024]{1,0:T(8,128)(2,1)} %collective-permute-done.6, f32[512,1024]{1,0:T(8,128)S(1)} %copy-done.4, f16[256,1024]{1,0:T(8,128)(2,1)} %collective-permute-done.7, ...), kind=kLoop, calls=%fused_computation.32 | loop fusion | flops 2621440 | bytes 3670028 | tf_op jit(solution)/shard_map/dynamic_update_slice | solution.py:130
  114.7 1.0 bitcast_dynamic-update-slice_fusion.5
  115.7 2.4 %bitcast_dynamic-update-slice_fusion.4 = f32[1,2048,1024]{2,1,0:T(8,128)S(1)} fusion(f32[1,2048,1024]{2,1,0:T(8,128)S(1)} %bitcast_dynamic-update-slice_fusion.5, f16[256,1024]{1,0:T(8,128)(2,1)} %collective-permute-done.12, f32[1536,1024]{1,0:T(8,128)S(1)} %bitcast.76, f16[256,1024]{1,0:T(8,128)(2,1)} %collective-permute-done.13, ...), kind=kLoop, calls=%fused_computation.30 | loop fusion | flops 2621440 | bytes 3670028 | tf_op jit(solution)/shard_map/dynamic_update_slice | solution.py:130
  118.1 2.2 %bitcast_dynamic-update-slice_fusion.3 = f32[1,2048,1024]{2,1,0:T(8,128)S(1)} fusion(f32[1,2048,1024]{2,1,0:T(8,128)S(1)} %bitcast_dynamic-update-slice_fusion.4, f16[256,1024]{1,0:T(8,128)(2,1)} %collective-permute-done.15, f32[1536,1024]{1,0:T(8,128)S(1)} %bitcast.76, f16[256,1024]{1,0:T(8,128)(2,1)} %collective-permute-done.16, ...), kind=kLoop, calls=%fused_computation.29 | loop fusion | flops 2621440 | bytes 3670028 | tf_op jit(solution)/shard_map/dynamic_update_slice | solution.py:130
  120.4 2.4 %bitcast_dynamic-update-slice_fusion.2 = f32[1,2048,1024]{2,1,0:T(8,128)S(1)} fusion(f32[1,2048,1024]{2,1,0:T(8,128)S(1)} %bitcast_dynamic-update-slice_fusion.3, f16[256,1024]{1,0:T(8,128)(2,1)} %collective-permute-done.18, f32[1536,1024]{1,0:T(8,128)S(1)} %bitcast.76, f16[256,1024]{1,0:T(8,128)(2,1)} %collective-permute-done.19, ...), kind=kLoop, calls=%fused_computation.28 | loop fusion | flops 2621440 | bytes 3670028 | tf_op jit(solution)/shard_map/dynamic_update_slice | solution.py:130
  122.8 2.1 %bitcast_dynamic-update-slice_fusion.1 = f32[1,2048,1024]{2,1,0:T(8,128)S(1)} fusion(f32[1,2048,1024]{2,1,0:T(8,128)S(1)} %bitcast_dynamic-update-slice_fusion.2, f16[256,1024]{1,0:T(8,128)(2,1)S(1)} %collective-permute-done.21, f32[1536,1024]{1,0:T(8,128)S(1)} %bitcast.76, f16[256,1024]{1,0:T(8,128)(2,1)S(1)} %collective-permute-done.20, ...), kind=kLoop, calls=%fused_computation.27 | loop fusion | flops 2621440 | bytes 3670028 | tf_op jit(solution)/shard_map/dynamic_update_slice | solution.py:130
  124.9 0.0 copy-start.5
  124.9 2.0 %collective-permute-done.23 = f16[256,1024]{1,0:T(8,128)(2,1)S(1)} collective-permute-done((f16[256,1024]{1,0:T(8,128)(2,1)S(1)}, f16[256,1024]{1,0:T(8,128)(2,1)S(1)}, u32[]{:S(2)}, u32[]{:S(2)}) %collective-permute-start.23) | collective-permute-done | bytes 524320 | tf_op jit(solution)/shard_map/ppermute | solution.py:28
  126.9 1.3 %copy-done.5 = f32[1,2048,1024]{2,1,0:T(8,128)} copy-done((f32[1,2048,1024]{2,1,0:T(8,128)}, f32[1,2048,1024]{2,1,0:T(8,128)S(1)}, u32[]{:S(2)}) %copy-start.5) | copy-done | bytes 8388632
  128.3 3.0 %bitcast_dynamic-update-slice_fusion = f32[1,2048,1024]{2,1,0:T(8,128)} fusion(f32[1,2048,1024]{2,1,0:T(8,128)} %copy-done.5, f16[256,1024]{1,0:T(8,128)(2,1)S(1)} %collective-permute-done.23, f32[1536,1024]{1,0:T(8,128)S(1)} %bitcast.76, f16[256,1024]{1,0:T(8,128)(2,1)S(1)} %collective-permute-done.22, f16[256,1024]{1,0:T(8,128)(2,1)} %collective-permute-done.17, ...), kind=kLoop, calls=%fused_computation.26 | loop fusion | flops 2621440 | bytes 3670536 | tf_op jit(solution)/shard_map/dynamic_update_slice | solution.py:130
  (43 shorter events, 0.1 us)
Async XLA Ops:
  0.0 1.5 %copy-start = (bf16[1,896,1024]{2,1,0:T(8,128)(2,1)S(1)}, bf16[1,896,1024]{2,1,0:T(8,128)(2,1)}, u32[]{:S(2)}) copy-start(bf16[1,896,1024]{2,1,0:T(8,128)(2,1)} %param.6) | copy-start | bytes 5505028
  3.3 13.8 %collective-permute-start = (f16[256,1024]{1,0:T(8,128)(2,1)S(1)}, f16[256,1024]{1,0:T(8,128)(2,1)S(1)}, u32[]{:S(2)}, u32[]{:S(2)}) collective-permute-start(f16[256,1024]{1,0:T(8,128)(2,1)S(1)} %fusion.31), channel_id=1, source_target_pairs={{0,1},{1,0},{2,3},{3,2},{4,5},{5,4},{6,7},{7,6},{8,9},{9,8},{10,11... | collective-permute-start | bytes 1572872 | tf_op jit(solution)/shard_map/ppermute | solution.py:19
  7.9 22.7 %collective-permute-start.2 = (f16[256,1024]{1,0:T(8,128)(2,1)}, f16[256,1024]{1,0:T(8,128)(2,1)S(1)}, u32[]{:S(2)}, u32[]{:S(2)}) collective-permute-start(f16[256,1024]{1,0:T(8,128)(2,1)} %fusion.28), channel_id=1, source_target_pairs={{0,1},{1,0},{2,3},{3,2},{4,5},{5,4},{6,7},{7,6},{8,9},{9,8},{10,11... | collective-permute-start | bytes 1572872 | tf_op jit(solution)/shard_map/ppermute | solution.py:19
  13.7 3.4 %copy-start.2 = (f32[512,1024]{1,0:T(8,128)}, f32[512,1024]{1,0:T(8,128)S(1)}, u32[]{:S(2)}) copy-start(f32[512,1024]{1,0:T(8,128)S(1)} %bitcast_subtract_fusion.1) | copy-start | bytes 6291460
  18.1 16.7 %collective-permute-start.3 = (f16[256,1024]{1,0:T(8,128)(2,1)}, f16[256,1024]{1,0:T(8,128)(2,1)}, u32[]{:S(2)}, u32[]{:S(2)}) collective-permute-start(f16[256,1024]{1,0:T(8,128)(2,1)} %multiply_convert_fusion.8), channel_id=1, source_target_pairs={{2,4},{4,2},{6,8},{8,6},{10,12},{12,10},{14,16},{16,14},{18,20},{2... | collective-permute-start | bytes 1572872 | tf_op jit(solution)/shard_map/ppermute | solution.py:28
  21.8 30.2 %collective-permute-start.4 = (f16[256,1024]{1,0:T(8,128)(2,1)}, f16[256,1024]{1,0:T(8,128)(2,1)}, u32[]{:S(2)}, u32[]{:S(2)}) collective-permute-start(f16[256,1024]{1,0:T(8,128)(2,1)} %multiply_convert_fusion.8), channel_id=1, source_target_pairs={{0,2},{2,0},{4,6},{6,4},{8,10},{10,8},{12,14},{14,12},{16,18},{18,... | collective-permute-start | bytes 1572872 | tf_op jit(solution)/shard_map/ppermute | solution.py:28
  22.6 12.1 %copy-start.3 = (f32[512,1024]{1,0:T(8,128)S(1)}, f32[512,1024]{1,0:T(8,128)}, u32[]{:S(2)}) copy-start(f32[512,1024]{1,0:T(8,128)} %copy-done.2) | copy-start | bytes 6291460
  27.6 24.4 %collective-permute-start.1 = (f16[256,1024]{1,0:T(8,128)(2,1)}, f16[256,1024]{1,0:T(8,128)(2,1)S(1)}, u32[]{:S(2)}, u32[]{:S(2)}) collective-permute-start(f16[256,1024]{1,0:T(8,128)(2,1)} %fusion.25), channel_id=1, source_target_pairs={{0,1},{1,0},{2,3},{3,2},{4,5},{5,4},{6,7},{7,6},{8,9},{9,8},{10,11... | collective-permute-start | bytes 1572872 | tf_op jit(solution)/shard_map/ppermute | solution.py:19
  35.8 21.8 %collective-permute-start.6 = (f16[256,1024]{1,0:T(8,128)(2,1)}, f16[256,1024]{1,0:T(8,128)(2,1)}, u32[]{:S(2)}, u32[]{:S(2)}) collective-permute-start(f16[256,1024]{1,0:T(8,128)(2,1)} %multiply_convert_fusion.7), channel_id=1, source_target_pairs={{2,4},{4,2},{6,8},{8,6},{10,12},{12,10},{14,16},{16,14},{18,20},{2... | collective-permute-start | bytes 1572872 | tf_op jit(solution)/shard_map/ppermute | solution.py:28
  37.4 20.2 %collective-permute-start.7 = (f16[256,1024]{1,0:T(8,128)(2,1)}, f16[256,1024]{1,0:T(8,128)(2,1)}, u32[]{:S(2)}, u32[]{:S(2)}) collective-permute-start(f16[256,1024]{1,0:T(8,128)(2,1)} %multiply_convert_fusion.7), channel_id=1, source_target_pairs={{0,2},{2,0},{4,6},{6,4},{8,10},{10,8},{12,14},{14,12},{16,18},{18,... | collective-permute-start | bytes 1572872 | tf_op jit(solution)/shard_map/ppermute | solution.py:28
  37.4 19.0 %collective-permute-start.5 = (f16[256,1024]{1,0:T(8,128)(2,1)}, f16[256,1024]{1,0:T(8,128)(2,1)}, u32[]{:S(2)}, u32[]{:S(2)}) collective-permute-start(f16[256,1024]{1,0:T(8,128)(2,1)} %get-tuple-element.96), channel_id=1, source_target_pairs={{0,1},{1,0},{2,3},{3,2},{4,5},{5,4},{6,7},{7,6},{8,9},{9,8},{10,11... | collective-permute-start | bytes 1572872 | tf_op jit(solution)/shard_map/ppermute | solution.py:19
  44.3 8.8 %copy-start.8 = (f16[256,1024]{1,0:T(8,128)(2,1)S(1)}, f16[256,1024]{1,0:T(8,128)(2,1)}, u32[]{:S(2)}) copy-start(f16[256,1024]{1,0:T(8,128)(2,1)} %get-tuple-element.115) | copy-start | bytes 1572868
  51.9 28.7 %copy-start.1 = (f32[1536,1024]{1,0:T(8,128)}, f32[1536,1024]{1,0:T(8,128)S(1)}, u32[]{:S(2)}) copy-start(f32[1536,1024]{1,0:T(8,128)S(1)} %bitcast_subtract_fusion) | copy-start | bytes 18874372
  51.9 41.0 %copy-start.13 = (s32[16,3]{0,1:T(4,128)S(1)}, s32[16,3]{0,1:T(4,128)}, u32[]{:S(2)}) copy-start(s32[16,3]{0,1:T(4,128)} %param.7) | copy-start | bytes 580
  52.2 9.5 %collective-permute-start.10 = (f16[256,1024]{1,0:T(8,128)(2,1)S(1)}, f16[256,1024]{1,0:T(8,128)(2,1)S(1)}, u32[]{:S(2)}, u32[]{:S(2)}) collective-permute-start(f16[256,1024]{1,0:T(8,128)(2,1)S(1)} %multiply_convert_fusion.6), channel_id=1, source_target_pairs={{0,2},{2,0},{4,6},{6,4},{8,10},{10,8},{12,14},{14,12},{16,18},{18,... | collective-permute-start | bytes 1572872 | tf_op jit(solution)/shard_map/ppermute | solution.py:28
  53.0 14.5 %collective-permute-start.8 = (f16[256,1024]{1,0:T(8,128)(2,1)S(1)}, f16[256,1024]{1,0:T(8,128)(2,1)S(1)}, u32[]{:S(2)}, u32[]{:S(2)}) collective-permute-start(f16[256,1024]{1,0:T(8,128)(2,1)S(1)} %copy-done.8), channel_id=1, source_target_pairs={{0,1},{1,0},{2,3},{3,2},{4,5},{5,4},{6,7},{7,6},{8,9},{9,8},{10,11... | collective-permute-start | bytes 1572872 | tf_op jit(solution)/shard_map/ppermute | solution.py:19
  56.4 24.2 %collective-permute-start.9 = (f16[256,1024]{1,0:T(8,128)(2,1)S(1)}, f16[256,1024]{1,0:T(8,128)(2,1)S(1)}, u32[]{:S(2)}, u32[]{:S(2)}) collective-permute-start(f16[256,1024]{1,0:T(8,128)(2,1)S(1)} %multiply_convert_fusion.6), channel_id=1, source_target_pairs={{2,4},{4,2},{6,8},{8,6},{10,12},{12,10},{14,16},{16,14},{18,20},{2... | collective-permute-start | bytes 1572872 | tf_op jit(solution)/shard_map/ppermute | solution.py:28
  59.7 26.5 %collective-permute-start.11 = (f16[256,1024]{1,0:T(8,128)(2,1)}, f16[256,1024]{1,0:T(8,128)(2,1)}, u32[]{:S(2)}, u32[]{:S(2)}) collective-permute-start(f16[256,1024]{1,0:T(8,128)(2,1)} %get-tuple-element.122), channel_id=1, source_target_pairs={{0,1},{1,0},{2,3},{3,2},{4,5},{5,4},{6,7},{7,6},{8,9},{9,8},{10,11... | collective-permute-start | bytes 1572872 | tf_op jit(solution)/shard_map/ppermute | solution.py:19
  61.4 26.2 %collective-permute-start.12 = (f16[256,1024]{1,0:T(8,128)(2,1)}, f16[256,1024]{1,0:T(8,128)(2,1)}, u32[]{:S(2)}, u32[]{:S(2)}) collective-permute-start(f16[256,1024]{1,0:T(8,128)(2,1)} %multiply_convert_fusion.5), channel_id=1, source_target_pairs={{2,4},{4,2},{6,8},{8,6},{10,12},{12,10},{14,16},{16,14},{18,20},{2... | collective-permute-start | bytes 1572872 | tf_op jit(solution)/shard_map/ppermute | solution.py:28
  61.6 20.0 %copy-start.9 = (f16[256,1024]{1,0:T(8,128)(2,1)}, f16[256,1024]{1,0:T(8,128)(2,1)S(1)}, u32[]{:S(2)}) copy-start(f16[256,1024]{1,0:T(8,128)(2,1)S(1)} %collective-permute-done.10) | copy-start | bytes 1572868
  61.6 25.9 %collective-permute-start.13 = (f16[256,1024]{1,0:T(8,128)(2,1)}, f16[256,1024]{1,0:T(8,128)(2,1)}, u32[]{:S(2)}, u32[]{:S(2)}) collective-permute-start(f16[256,1024]{1,0:T(8,128)(2,1)} %multiply_convert_fusion.5), channel_id=1, source_target_pairs={{0,2},{2,0},{4,6},{6,4},{8,10},{10,8},{12,14},{14,12},{16,18},{18,... | collective-permute-start | bytes 1572872 | tf_op jit(solution)/shard_map/ppermute | solution.py:28
  67.5 14.1 %copy-start.6 = (f16[256,1024]{1,0:T(8,128)(2,1)}, f16[256,1024]{1,0:T(8,128)(2,1)S(1)}, u32[]{:S(2)}) copy-start(f16[256,1024]{1,0:T(8,128)(2,1)S(1)} %collective-permute-done.8) | copy-start | bytes 1572868
  80.6 1.0 copy-start.11
  81.7 9.6 %collective-permute-start.14 = (f16[256,1024]{1,0:T(8,128)(2,1)}, f16[256,1024]{1,0:T(8,128)(2,1)}, u32[]{:S(2)}, u32[]{:S(2)}) collective-permute-start(f16[256,1024]{1,0:T(8,128)(2,1)} %get-tuple-element.129), channel_id=1, source_target_pairs={{0,1},{1,0},{2,3},{3,2},{4,5},{5,4},{6,7},{7,6},{8,9},{9,8},{10,11... | collective-permute-start | bytes 1572872 | tf_op jit(solution)/shard_map/ppermute | solution.py:19
  83.4 14.8 %collective-permute-start.15 = (f16[256,1024]{1,0:T(8,128)(2,1)}, f16[256,1024]{1,0:T(8,128)(2,1)}, u32[]{:S(2)}, u32[]{:S(2)}) collective-permute-start(f16[256,1024]{1,0:T(8,128)(2,1)} %multiply_convert_fusion.4), channel_id=1, source_target_pairs={{2,4},{4,2},{6,8},{8,6},{10,12},{12,10},{14,16},{16,14},{18,20},{2... | collective-permute-start | bytes 1572872 | tf_op jit(solution)/shard_map/ppermute | solution.py:28
  86.1 12.1 %collective-permute-start.16 = (f16[256,1024]{1,0:T(8,128)(2,1)}, f16[256,1024]{1,0:T(8,128)(2,1)}, u32[]{:S(2)}, u32[]{:S(2)}) collective-permute-start(f16[256,1024]{1,0:T(8,128)(2,1)} %multiply_convert_fusion.4), channel_id=1, source_target_pairs={{0,2},{2,0},{4,6},{6,4},{8,10},{10,8},{12,14},{14,12},{16,18},{18,... | collective-permute-start | bytes 1572872 | tf_op jit(solution)/shard_map/ppermute | solution.py:28
  90.0 15.0 %collective-permute-start.18 = (f16[256,1024]{1,0:T(8,128)(2,1)}, f16[256,1024]{1,0:T(8,128)(2,1)}, u32[]{:S(2)}, u32[]{:S(2)}) collective-permute-start(f16[256,1024]{1,0:T(8,128)(2,1)} %multiply_convert_fusion.3), channel_id=1, source_target_pairs={{2,4},{4,2},{6,8},{8,6},{10,12},{12,10},{14,16},{16,14},{18,20},{2... | collective-permute-start | bytes 1572872 | tf_op jit(solution)/shard_map/ppermute | solution.py:28
  91.2 13.7 %collective-permute-start.19 = (f16[256,1024]{1,0:T(8,128)(2,1)}, f16[256,1024]{1,0:T(8,128)(2,1)}, u32[]{:S(2)}, u32[]{:S(2)}) collective-permute-start(f16[256,1024]{1,0:T(8,128)(2,1)} %multiply_convert_fusion.3), channel_id=1, source_target_pairs={{0,2},{2,0},{4,6},{6,4},{8,10},{10,8},{12,14},{14,12},{16,18},{18,... | collective-permute-start | bytes 1572872 | tf_op jit(solution)/shard_map/ppermute | solution.py:28
  91.2 13.7 %collective-permute-start.17 = (f16[256,1024]{1,0:T(8,128)(2,1)}, f16[256,1024]{1,0:T(8,128)(2,1)}, u32[]{:S(2)}, u32[]{:S(2)}) collective-permute-start(f16[256,1024]{1,0:T(8,128)(2,1)} %get-tuple-element.136), channel_id=1, source_target_pairs={{0,1},{1,0},{2,3},{3,2},{4,5},{5,4},{6,7},{7,6},{8,9},{9,8},{10,11... | collective-permute-start | bytes 1572872 | tf_op jit(solution)/shard_map/ppermute | solution.py:19
  99.8 23.0 %collective-permute-start.20 = (f16[256,1024]{1,0:T(8,128)(2,1)S(1)}, f16[256,1024]{1,0:T(8,128)(2,1)S(1)}, u32[]{:S(2)}, u32[]{:S(2)}) collective-permute-start(f16[256,1024]{1,0:T(8,128)(2,1)S(1)} %multiply_convert_fusion.2), channel_id=1, source_target_pairs={{0,2},{2,0},{4,6},{6,4},{8,10},{10,8},{12,14},{14,12},{16,18},{18,... | collective-permute-start | bytes 1572872 | tf_op jit(solution)/shard_map/ppermute | solution.py:28
  99.9 22.9 %collective-permute-start.21 = (f16[256,1024]{1,0:T(8,128)(2,1)S(1)}, f16[256,1024]{1,0:T(8,128)(2,1)S(1)}, u32[]{:S(2)}, u32[]{:S(2)}) collective-permute-start(f16[256,1024]{1,0:T(8,128)(2,1)S(1)} %multiply_convert_fusion.2), channel_id=1, source_target_pairs={{2,4},{4,2},{6,8},{8,6},{10,12},{12,10},{14,16},{16,14},{18,20},{2... | collective-permute-start | bytes 1572872 | tf_op jit(solution)/shard_map/ppermute | solution.py:28
  106.6 18.3 %collective-permute-start.22 = (f16[256,1024]{1,0:T(8,128)(2,1)S(1)}, f16[256,1024]{1,0:T(8,128)(2,1)S(1)}, u32[]{:S(2)}, u32[]{:S(2)}) collective-permute-start(f16[256,1024]{1,0:T(8,128)(2,1)S(1)} %multiply_convert_fusion.1), channel_id=1, source_target_pairs={{0,2},{2,0},{4,6},{6,4},{8,10},{10,8},{12,14},{14,12},{16,18},{18,... | collective-permute-start | bytes 1572872 | tf_op jit(solution)/shard_map/ppermute | solution.py:28
  107.8 19.2 %collective-permute-start.23 = (f16[256,1024]{1,0:T(8,128)(2,1)S(1)}, f16[256,1024]{1,0:T(8,128)(2,1)S(1)}, u32[]{:S(2)}, u32[]{:S(2)}) collective-permute-start(f16[256,1024]{1,0:T(8,128)(2,1)S(1)} %multiply_convert_fusion.1), channel_id=1, source_target_pairs={{2,4},{4,2},{6,8},{8,6},{10,12},{12,10},{14,16},{16,14},{18,20},{2... | collective-permute-start | bytes 1572872 | tf_op jit(solution)/shard_map/ppermute | solution.py:28
  108.2 4.2 %copy-start.4 = (f32[512,1024]{1,0:T(8,128)S(1)}, f32[512,1024]{1,0:T(8,128)}, u32[]{:S(2)}) copy-start(f32[512,1024]{1,0:T(8,128)} %copy-done.2) | copy-start | bytes 6291460
  108.2 6.5 %slice-start = ((s8[6291456]{0:T(1024)(128)(4,1)}), s8[4194304]{0:T(1024)(128)(4,1)S(1)}, s32[]{:S(2)}) async-start(s8[6291456]{0:T(1024)(128)(4,1)} %bitcast.75), calls=%async_computation | async-start | bytes 8388608
  111.2 3.4 %slice-start.1 = ((s8[6291456]{0:T(1024)(128)(4,1)}), s8[2097152]{0:T(1024)(128)(4,1)S(1)}, s32[]{:S(2)}) async-start(s8[6291456]{0:T(1024)(128)(4,1)} %bitcast.75), calls=%async_computation.1 | async-start | bytes 4194304
  111.2 3.4 %copy-start.10 = (f16[256,1024]{1,0:T(8,128)(2,1)S(1)}, f16[256,1024]{1,0:T(8,128)(2,1)}, u32[]{:S(2)}) copy-start(f16[256,1024]{1,0:T(8,128)(2,1)} %copy-done.9) | copy-start | bytes 1572868
  111.3 3.4 %copy-start.12 = (f16[256,1024]{1,0:T(8,128)(2,1)S(1)}, f16[256,1024]{1,0:T(8,128)(2,1)}, u32[]{:S(2)}) copy-start(f16[256,1024]{1,0:T(8,128)(2,1)} %copy-done.11) | copy-start | bytes 1572868
  112.3 5.8 %copy-start.7 = (f16[256,1024]{1,0:T(8,128)(2,1)S(1)}, f16[256,1024]{1,0:T(8,128)(2,1)}, u32[]{:S(2)}) copy-start(f16[256,1024]{1,0:T(8,128)(2,1)} %copy-done.6) | copy-start | bytes 1572868
  124.9 3.4 %copy-start.5 = (f32[1,2048,1024]{2,1,0:T(8,128)}, f32[1,2048,1024]{2,1,0:T(8,128)S(1)}, u32[]{:S(2)}) copy-start(f32[1,2048,1024]{2,1,0:T(8,128)S(1)} %bitcast_dynamic-update-slice_fusion.1) | copy-start | bytes 25165828

commit v8 on v7

--- a/solution.py
+++ b/solution.py
@@ -86,30 +86,28 @@
         return total
 
     split = min(2, chunks)
-    early = min(AHEAD + 1, chunks)
     near = {}
     far = {}
-    terms = {chunk: for_others(shard, chunk * step, step) for chunk in range(early)}
-    arrived = {chunk: send_terms(terms[chunk]) for chunk in range(min(AHEAD, chunks))}
+    terms = {0: for_others(shard, 0, step)}
+    arrived = {0: send_terms(terms[0])}
+    rest = for_others(shard, step, rows - step) if chunks > 1 else []
+    for chunk in range(1, chunks):
+        terms[chunk] = [rows_of(term, chunk - 1) for term in rest]
+    if chunks > 1:
+        arrived[1] = send_terms(terms[1])
     base = [own_part(shard, 0, split)]
 
     arrived[0], base, terms = lax.optimization_barrier((arrived[0], base, terms))
     for chunk in range(chunks):
-        if chunk in (1, 2):
-            arrived[chunk], base, terms = lax.optimization_barrier((arrived[chunk], base, terms))
         if chunk == 1:
-            arrived[1], far[0] = lax.optimization_barrier((arrived[1], far[0]))
+            arrived[1], base = lax.optimization_barrier((arrived[1], base))
         if chunk >= 2:
             arrived[chunk], far[chunk - 2], near[chunk - 2] = lax.optimization_barrier(
                 (arrived[chunk], far[chunk - 2], near[chunk - 2])
             )
         sent = (u_of(chunk) * scale).astype(WIRE)
         sent, base, later = lax.optimization_barrier((sent, base, shard))
-        if chunk == 0 and early < chunks:
-            rest = for_others(later, early * step, rows - early * step)
-            for after in range(early, chunks):
-                terms[after] = [rows_of(term, after - early) for term in rest]
-        if chunk == 1 and split < chunks:
+        if chunk == 0 and split < chunks:
             base.append(own_part(later, split, chunks - split))
         after = chunk + AHEAD
         if after < chunks:

time: 134 us -> 130 us (0.970)
  the two profiles are of different devices: /device:TPU:1 before, /device:TPU:0 now
where the time goes in v8:
time: 130 us
  starting transfers between devices  44 us (34%)
  waiting for transfers between devices  27.9 us (21%)
  other arithmetic  26.5 us (20%)
  matrix products  19.1 us (15%)
  local copies, waits for them, and re-layouts  9.12 us (7%)
  between operations  3 us (2%)
    ppermute x16, starting transfers between devices, swapped(): return lax.ppermute(value, axis, pairs)  31.8 us
    ppermute x8, waiting for transfers between devices, from_behind(): return lax.ppermute(value, axis, pairs)  27.7 us
    dot_general x4, matrix products, partial(): lax.dot_general(block, cot_local, (((0,), (0,)), ((), ())), preferred_ele...  19 us
    dynamic_update_slice x7, other arithmetic, on_device(): out = lax.dynamic_update_slice_in_dim(out, mixed, chunk * step, axis=0)  14.1 us
    ppermute x8, starting transfers between devices, from_behind(): return lax.ppermute(value, axis, pairs)  12.3 us
    convert_element_type x8, other arithmetic, on_device(): sent = (u_of(chunk) * scale).astype(WIRE)  9.36 us
    unnamed x46, local copies, waits for them, and re-layouts  5.16 us
    add x1, other arithmetic, on_device(): c_near * near[chunk].astype(jnp.float32) + c_self * u_of(chunk)  3.07 us
  transfers between devices with their start and end apart: 24, of which 7 were waited for; matrix products, arithmetic and copies ran while one was open for 35% of the time, Pallas kernels for 0%

profile of v8, /device:TPU:0, one launch (start us, length us, event | category | flops | bytes accessed | tf_op | source)
XLA Modules:
  0.0 129.7 jit_solution(10827743858312976024)
XLA Ops:
  0.0 1.5 %copy-done = bf16[1,896,1024]{2,1,0:T(8,128)(2,1)S(1)} copy-done((bf16[1,896,1024]{2,1,0:T(8,128)(2,1)S(1)}, bf16[1,896,1024]{2,1,0:T(8,128)(2,1)}, u32[]{:S(2)}) %copy-start) | copy-done | bytes 1835032
  1.5 1.7 %fusion.15 = f16[256,1024]{1,0:T(8,128)(2,1)S(1)} fusion(bf16[1,896,1024]{2,1,0:T(8,128)(2,1)S(1)} %copy-done, bf16[1,896,4096]{2,1,0:T(8,128)(2,1)} %param.5, s32[]{:T(128)S(6)} %select_n.33), kind=kOutput, calls=%fused_computation.15 | convolution fusion | flops 470286336 | bytes 2818052 | tf_op jit(solution)/shard_map/dot_general | solution.py:56
  3.3 3.0 %collective-permute-start = (f16[256,1024]{1,0:T(8,128)(2,1)S(1)}, f16[256,1024]{1,0:T(8,128)(2,1)S(1)}, u32[]{:S(2)}, u32[]{:S(2)}) collective-permute-start(f16[256,1024]{1,0:T(8,128)(2,1)S(1)} %fusion.15), channel_id=1, source_target_pairs={{0,1},{1,0},{2,3},{3,2},{4,5},{5,4},{6,7},{7,6},{8,9},{9,8},{10,11... | collective-permute-start | bytes 1572872 | tf_op jit(solution)/shard_map/ppermute | solution.py:19
  6.3 6.2 %multiply_convert_fusion = f16[1792,1024]{1,0:T(8,128)(2,1)S(1)} fusion(bf16[1,896,4096]{2,1,0:T(8,128)(2,1)} %param.5, s32[]{:T(128)S(6)} %select_n.35, bf16[1,896,1024]{2,1,0:T(8,128)(2,1)S(1)} %copy-done), kind=kOutput, calls=%fused_computation.1 | convolution fusion | flops 3292004352 | bytes 8716292 | tf_op jit(solution)/shard_map/dot_general | solution.py:56
  12.4 2.2 %fusion.32 = (f16[256,1024]{1,0:T(8,128)(2,1)}, f16[256,1024]{1,0:T(8,128)(2,1)}, f16[256,1024]{1,0:T(8,128)(2,1)}, f16[256,1024]{1,0:T(8,128)(2,1)}, f16[256,10...) fusion(f16[1792,1024]{1,0:T(8,128)(2,1)S(1)} %multiply_convert_fusion), kind=kLoop, calls=%fused_computation.55 | loop fusion | bytes 7340032 | tf_op jit(solution)/shard_map/slice | solution.py:74
  14.7 0.0 collective-permute-start.4
  14.7 3.2 %bitcast_subtract_fusion.1 = f32[512,1024]{1,0:T(8,128)S(1)} fusion(f32[1,2048,1024]{2,1,0:T(8,128)} %param.4, bf16[1,896,1024]{2,1,0:T(8,128)(2,1)S(1)} %copy-done, bf16[1,896,4096]{2,1,0:T(8,128)(2,1)} %param.5, s32[]{:T(128)S(6)} %select_n.34), kind=kOutput, calls=%fused_computation.7 | convolution fusion | flops 940572672 | bytes 6946820 | tf_op jit(solution)/shard_map/dot_general | solution.py:56
  17.9 1.1 collective-permute-done
  19.0 0.2 copy-done.2
  19.2 1.1 multiply_convert_fusion.8
  20.3 3.9 %collective-permute-start.2 = (f16[256,1024]{1,0:T(8,128)(2,1)}, f16[256,1024]{1,0:T(8,128)(2,1)}, u32[]{:S(2)}, u32[]{:S(2)}) collective-permute-start(f16[256,1024]{1,0:T(8,128)(2,1)} %multiply_convert_fusion.8), channel_id=1, source_target_pairs={{2,4},{4,2},{6,8},{8,6},{10,12},{12,10},{14,16},{16,14},{18,20},{2... | collective-permute-start | bytes 1572872 | tf_op jit(solution)/shard_map/ppermute | solution.py:28
  24.2 0.0 collective-permute-start.3
  24.2 1.5 %collective-permute-start.1 = (f16[256,1024]{1,0:T(8,128)(2,1)}, f16[256,1024]{1,0:T(8,128)(2,1)S(1)}, u32[]{:S(2)}, u32[]{:S(2)}) collective-permute-start(f16[256,1024]{1,0:T(8,128)(2,1)} %get-tuple-element.77), channel_id=1, source_target_pairs={{0,1},{1,0},{2,3},{3,2},{4,5},{5,4},{6,7},{7,6},{8,9},{9,8},{10,11... | collective-permute-start | bytes 1572872 | tf_op jit(solution)/shard_map/ppermute | solution.py:19
  25.7 7.9 %bitcast_subtract_fusion = f32[1536,1024]{1,0:T(8,128)S(1)} fusion(f32[1,2048,1024]{2,1,0:T(8,128)} %param.4, bf16[1,896,4096]{2,1,0:T(8,128)(2,1)} %param.5, s32[]{:T(128)S(6)} %select_n.36, bf16[1,896,1024]{2,1,0:T(8,128)(2,1)S(1)} %copy-done), kind=kOutput, calls=%fused_computation.2 | convolution fusion | flops 2821718016 | bytes 17170436 | tf_op jit(solution)/shard_map/dot_general | solution.py:56
  33.6 0.0 copy-start.1
  33.6 0.0 copy-start.20
  33.6 0.0 collective-permute-done.4
  33.7 0.2 multiply_convert_fusion.7
  33.9 0.6 collective-permute-start.5
  34.5 0.7 collective-permute-start.6
  35.2 6.3 %collective-permute-done.1 = f16[256,1024]{1,0:T(8,128)(2,1)S(1)} collective-permute-done((f16[256,1024]{1,0:T(8,128)(2,1)}, f16[256,1024]{1,0:T(8,128)(2,1)S(1)}, u32[]{:S(2)}, u32[]{:S(2)}) %collective-permute-start.1) | collective-permute-done | bytes 524320 | tf_op jit(solution)/shard_map/ppermute | solution.py:19
  41.5 0.0 collective-permute-start.7
  41.5 0.0 collective-permute-done.2
  41.5 0.0 collective-permute-done.3
  41.5 0.2 multiply_convert_fusion.6
  41.8 0.6 collective-permute-start.10
  42.3 2.1 %collective-permute-start.8 = (f16[256,1024]{1,0:T(8,128)(2,1)S(1)}, f16[256,1024]{1,0:T(8,128)(2,1)S(1)}, u32[]{:S(2)}, u32[]{:S(2)}) collective-permute-start(f16[256,1024]{1,0:T(8,128)(2,1)S(1)} %copy-done.10), channel_id=1, source_target_pairs={{0,1},{1,0},{2,3},{3,2},{4,5},{5,4},{6,7},{7,6},{8,9},{9,8},{10,11... | collective-permute-start | bytes 1572872 | tf_op jit(solution)/shard_map/ppermute | solution.py:19
  44.4 8.4 %collective-permute-done.5 = f16[256,1024]{1,0:T(8,128)(2,1)S(1)} collective-permute-done((f16[256,1024]{1,0:T(8,128)(2,1)S(1)}, f16[256,1024]{1,0:T(8,128)(2,1)S(1)}, u32[]{:S(2)}, u32[]{:S(2)}) %collective-permute-start.5) | collective-permute-done | bytes 524320 | tf_op jit(solution)/shard_map/ppermute | solution.py:19
  52.7 2.5 %collective-permute-start.9 = (f16[256,1024]{1,0:T(8,128)(2,1)S(1)}, f16[256,1024]{1,0:T(8,128)(2,1)S(1)}, u32[]{:S(2)}, u32[]{:S(2)}) collective-permute-start(f16[256,1024]{1,0:T(8,128)(2,1)S(1)} %multiply_convert_fusion.6), channel_id=1, source_target_pairs={{2,4},{4,2},{6,8},{8,6},{10,12},{12,10},{14,16},{16,14},{18,20},{2... | collective-permute-start | bytes 1572872 | tf_op jit(solution)/shard_map/ppermute | solution.py:28
  55.2 0.0 collective-permute-done.6
  55.3 1.2 multiply_convert_fusion.5
  56.5 1.5 %collective-permute-start.11 = (f16[256,1024]{1,0:T(8,128)(2,1)}, f16[256,1024]{1,0:T(8,128)(2,1)}, u32[]{:S(2)}, u32[]{:S(2)}) collective-permute-start(f16[256,1024]{1,0:T(8,128)(2,1)} %get-tuple-element.106), channel_id=1, source_target_pairs={{0,1},{1,0},{2,3},{3,2},{4,5},{5,4},{6,7},{7,6},{8,9},{9,8},{10,11... | collective-permute-start | bytes 1572872 | tf_op jit(solution)/shard_map/ppermute | solution.py:19
  58.0 2.2 %collective-permute-start.12 = (f16[256,1024]{1,0:T(8,128)(2,1)}, f16[256,1024]{1,0:T(8,128)(2,1)}, u32[]{:S(2)}, u32[]{:S(2)}) collective-permute-start(f16[256,1024]{1,0:T(8,128)(2,1)} %multiply_convert_fusion.5), channel_id=1, source_target_pairs={{2,4},{4,2},{6,8},{8,6},{10,12},{12,10},{14,16},{16,14},{18,20},{2... | collective-permute-start | bytes 1572872 | tf_op jit(solution)/shard_map/ppermute | solution.py:28
  60.2 3.8 %collective-permute-done.8 = f16[256,1024]{1,0:T(8,128)(2,1)S(1)} collective-permute-done((f16[256,1024]{1,0:T(8,128)(2,1)S(1)}, f16[256,1024]{1,0:T(8,128)(2,1)S(1)}, u32[]{:S(2)}, u32[]{:S(2)}) %collective-permute-start.8) | collective-permute-done | bytes 524320 | tf_op jit(solution)/shard_map/ppermute | solution.py:19
  64.0 0.2 collective-permute-done.9
  64.2 1.0 multiply_convert_fusion.4
  65.2 2.1 %collective-permute-start.14 = (f16[256,1024]{1,0:T(8,128)(2,1)}, f16[256,1024]{1,0:T(8,128)(2,1)}, u32[]{:S(2)}, u32[]{:S(2)}) collective-permute-start(f16[256,1024]{1,0:T(8,128)(2,1)} %get-tuple-element.113), channel_id=1, source_target_pairs={{0,1},{1,0},{2,3},{3,2},{4,5},{5,4},{6,7},{7,6},{8,9},{9,8},{10,11... | collective-permute-start | bytes 1572872 | tf_op jit(solution)/shard_map/ppermute | solution.py:19
  67.3 1.7 %collective-permute-start.15 = (f16[256,1024]{1,0:T(8,128)(2,1)}, f16[256,1024]{1,0:T(8,128)(2,1)}, u32[]{:S(2)}, u32[]{:S(2)}) collective-permute-start(f16[256,1024]{1,0:T(8,128)(2,1)} %multiply_convert_fusion.4), channel_id=1, source_target_pairs={{2,4},{4,2},{6,8},{8,6},{10,12},{12,10},{14,16},{16,14},{18,20},{2... | collective-permute-start | bytes 1572872 | tf_op jit(solution)/shard_map/ppermute | solution.py:28
  69.0 5.5 %collective-permute-done.11 = f16[256,1024]{1,0:T(8,128)(2,1)} collective-permute-done((f16[256,1024]{1,0:T(8,128)(2,1)}, f16[256,1024]{1,0:T(8,128)(2,1)}, u32[]{:S(2)}, u32[]{:S(2)}) %collective-permute-start.11) | collective-permute-done | bytes 524320 | tf_op jit(solution)/shard_map/ppermute | solution.py:19
  74.5 8.5 %collective-permute-start.16 = (f16[256,1024]{1,0:T(8,128)(2,1)}, f16[256,1024]{1,0:T(8,128)(2,1)}, u32[]{:S(2)}, u32[]{:S(2)}) collective-permute-start(f16[256,1024]{1,0:T(8,128)(2,1)} %multiply_convert_fusion.4), channel_id=1, source_target_pairs={{0,2},{2,0},{4,6},{6,4},{8,10},{10,8},{12,14},{14,12},{16,18},{18,... | collective-permute-start | bytes 1572872 | tf_op jit(solution)/shard_map/ppermute | solution.py:28
  83.0 2.4 %multiply_convert_fusion.3 = f16[256,1024]{1,0:T(8,128)(2,1)} fusion(f16[256,1024]{1,0:T(8,128)(2,1)} %collective-permute-done.11, f32[1536,1024]{1,0:T(8,128)} %copy-done.1), kind=kLoop, calls=%fused_computation.30 | loop fusion | flops 1310720 | bytes 2097152 | tf_op jit(solution)/shard_map/convert_element_type | solution.py:108
  85.4 3.2 %collective-permute-start.18 = (f16[256,1024]{1,0:T(8,128)(2,1)}, f16[256,1024]{1,0:T(8,128)(2,1)}, u32[]{:S(2)}, u32[]{:S(2)}) collective-permute-start(f16[256,1024]{1,0:T(8,128)(2,1)} %multiply_convert_fusion.3), channel_id=1, source_target_pairs={{2,4},{4,2},{6,8},{8,6},{10,12},{12,10},{14,16},{16,14},{18,20},{2... | collective-permute-start | bytes 1572872 | tf_op jit(solution)/shard_map/ppermute | solution.py:28
  88.6 1.4 %collective-permute-start.17 = (f16[256,1024]{1,0:T(8,128)(2,1)}, f16[256,1024]{1,0:T(8,128)(2,1)}, u32[]{:S(2)}, u32[]{:S(2)}) collective-permute-start(f16[256,1024]{1,0:T(8,128)(2,1)} %get-tuple-element.120), channel_id=1, source_target_pairs={{0,1},{1,0},{2,3},{3,2},{4,5},{5,4},{6,7},{7,6},{8,9},{9,8},{10,11... | collective-permute-start | bytes 1572872 | tf_op jit(solution)/shard_map/ppermute | solution.py:19
  90.0 0.1 fusion.18
  90.1 0.7 fusion.33
  93.5 1.6 %multiply_convert_fusion.2 = f16[256,1024]{1,0:T(8,128)(2,1)S(1)} fusion(f16[256,1024]{1,0:T(8,128)(2,1)} %collective-permute-done.14, f32[1536,1024]{1,0:T(8,128)} %copy-done.1), kind=kLoop, calls=%fused_computation.28 | loop fusion | flops 1310720 | bytes 2097152 | tf_op jit(solution)/shard_map/convert_element_type | solution.py:108
  95.0 1.7 %collective-permute-start.20 = (f16[256,1024]{1,0:T(8,128)(2,1)S(1)}, f16[256,1024]{1,0:T(8,128)(2,1)S(1)}, u32[]{:S(2)}, u32[]{:S(2)}) collective-permute-start(f16[256,1024]{1,0:T(8,128)(2,1)S(1)} %multiply_convert_fusion.2), channel_id=1, source_target_pairs={{0,2},{2,0},{4,6},{6,4},{8,10},{10,8},{12,14},{14,12},{16,18},{18,... | collective-permute-start | bytes 1572872 | tf_op jit(solution)/shard_map/ppermute | solution.py:28
  96.7 3.9 %collective-permute-start.21 = (f16[256,1024]{1,0:T(8,128)(2,1)S(1)}, f16[256,1024]{1,0:T(8,128)(2,1)S(1)}, u32[]{:S(2)}, u32[]{:S(2)}) collective-permute-start(f16[256,1024]{1,0:T(8,128)(2,1)S(1)} %multiply_convert_fusion.2), channel_id=1, source_target_pairs={{2,4},{4,2},{6,8},{8,6},{10,12},{12,10},{14,16},{16,14},{18,20},{2... | collective-permute-start | bytes 1572872 | tf_op jit(solution)/shard_map/ppermute | solution.py:28
  100.6 2.6 %collective-permute-done.17 = f16[256,1024]{1,0:T(8,128)(2,1)} collective-permute-done((f16[256,1024]{1,0:T(8,128)(2,1)}, f16[256,1024]{1,0:T(8,128)(2,1)}, u32[]{:S(2)}, u32[]{:S(2)}) %collective-permute-start.17) | collective-permute-done | bytes 524320 | tf_op jit(solution)/shard_map/ppermute | solution.py:19
  103.3 1.6 %multiply_convert_fusion.1 = f16[256,1024]{1,0:T(8,128)(2,1)S(1)} fusion(f16[256,1024]{1,0:T(8,128)(2,1)} %collective-permute-done.17, f32[1536,1024]{1,0:T(8,128)} %copy-done.1), kind=kLoop, calls=%fused_computation.26 | loop fusion | flops 1310720 | bytes 2097152 | tf_op jit(solution)/shard_map/convert_element_type | solution.py:108
  104.9 0.1 collective-permute-start.22
  104.9 2.9 %collective-permute-start.23 = (f16[256,1024]{1,0:T(8,128)(2,1)S(1)}, f16[256,1024]{1,0:T(8,128)(2,1)S(1)}, u32[]{:S(2)}, u32[]{:S(2)}) collective-permute-start(f16[256,1024]{1,0:T(8,128)(2,1)S(1)} %multiply_convert_fusion.1), channel_id=1, source_target_pairs={{2,4},{4,2},{6,8},{8,6},{10,12},{12,10},{14,16},{16,14},{18,20},{2... | collective-permute-start | bytes 1572872 | tf_op jit(solution)/shard_map/ppermute | solution.py:28
  107.9 3.1 %multiply_add_fusion = f32[256,1024]{1,0:T(8,128)S(1)} fusion(f16[256,1024]{1,0:T(8,128)(2,1)} %collective-permute-done.2, f32[512,1024]{1,0:T(8,128)} %copy-done.2, f16[256,1024]{1,0:T(8,128)(2,1)} %collective-permute-done.3, f16[256,1024]{1,0:T(8,128)(2,1)S(1)} %collective-permute-done, f32[]{:T(128)S(6)} %div.51, f32[]{:T(128)} %bitcast.11, f32[]{:T(128)S(6)} %div.42), kind=kLoop, calls=%fused_computation.25 | loop fusion | flops 2621440 | bytes 3670028 | tf_op jit(solution)/shard_map/add | solution.py:124
  111.0 0.0 slice-start.1
  111.0 1.1 pad_bitcast_fusion
  112.1 1.1 bitcast_dynamic-update-slice_fusion.6
  113.2 1.0 bitcast_dynamic-update-slice_fusion.5
  114.3 2.2 %bitcast_dynamic-update-slice_fusion.4 = f32[1,2048,1024]{2,1,0:T(8,128)S(1)} fusion(f32[1,2048,1024]{2,1,0:T(8,128)S(1)} %bitcast_dynamic-update-slice_fusion.5, f16[256,1024]{1,0:T(8,128)(2,1)} %collective-permute-done.12, f32[1536,1024]{1,0:T(8,128)S(1)} %bitcast.58, f16[256,1024]{1,0:T(8,128)(2,1)} %collective-permute-done.13, ...), kind=kLoop, calls=%fused_computation.22 | loop fusion | flops 2621440 | bytes 3670028 | tf_op jit(solution)/shard_map/dynamic_update_slice | solution.py:128
  116.5 2.2 %bitcast_dynamic-update-slice_fusion.3 = f32[1,2048,1024]{2,1,0:T(8,128)S(1)} fusion(f32[1,2048,1024]{2,1,0:T(8,128)S(1)} %bitcast_dynamic-update-slice_fusion.4, f16[256,1024]{1,0:T(8,128)(2,1)} %collective-permute-done.15, f32[1536,1024]{1,0:T(8,128)S(1)} %bitcast.58, f16[256,1024]{1,0:T(8,128)(2,1)} %collective-permute-done.16, ...), kind=kLoop, calls=%fused_computation.21 | loop fusion | flops 2621440 | bytes 3670028 | tf_op jit(solution)/shard_map/dynamic_update_slice | solution.py:128
  118.8 2.4 %bitcast_dynamic-update-slice_fusion.2 = f32[1,2048,1024]{2,1,0:T(8,128)S(1)} fusion(f32[1,2048,1024]{2,1,0:T(8,128)S(1)} %bitcast_dynamic-update-slice_fusion.3, f16[256,1024]{1,0:T(8,128)(2,1)} %collective-permute-done.18, f32[1536,1024]{1,0:T(8,128)S(1)} %bitcast.58, f16[256,1024]{1,0:T(8,128)(2,1)} %collective-permute-done.19, ...), kind=kLoop, calls=%fused_computation.20 | loop fusion | flops 2621440 | bytes 3670028 | tf_op jit(solution)/shard_map/dynamic_update_slice | solution.py:128
  121.2 2.1 %bitcast_dynamic-update-slice_fusion.1 = f32[1,2048,1024]{2,1,0:T(8,128)S(1)} fusion(f32[1,2048,1024]{2,1,0:T(8,128)S(1)} %bitcast_dynamic-update-slice_fusion.2, f16[256,1024]{1,0:T(8,128)(2,1)S(1)} %collective-permute-done.21, f32[1536,1024]{1,0:T(8,128)S(1)} %bitcast.58, f16[256,1024]{1,0:T(8,128)(2,1)S(1)} %collective-permute-done.20, ...), kind=kLoop, calls=%fused_computation.19 | loop fusion | flops 2621440 | bytes 3670028 | tf_op jit(solution)/shard_map/dynamic_update_slice | solution.py:128
  123.2 0.0 copy-start.5
  123.3 3.4 %copy-done.5 = f32[1,2048,1024]{2,1,0:T(8,128)} copy-done((f32[1,2048,1024]{2,1,0:T(8,128)}, f32[1,2048,1024]{2,1,0:T(8,128)S(1)}, u32[]{:S(2)}) %copy-start.5) | copy-done | bytes 8388632
  126.6 3.0 %bitcast_dynamic-update-slice_fusion = f32[1,2048,1024]{2,1,0:T(8,128)} fusion(f32[1,2048,1024]{2,1,0:T(8,128)} %copy-done.5, f16[256,1024]{1,0:T(8,128)(2,1)S(1)} %collective-permute-done.23, f32[1536,1024]{1,0:T(8,128)S(1)} %bitcast.58, f16[256,1024]{1,0:T(8,128)(2,1)S(1)} %collective-permute-done.22, f16[256,1024]{1,0:T(8,128)(2,1)} %collective-permute-done.17, ...), kind=kLoop, calls=%fused_computation.18 | loop fusion | flops 2621440 | bytes 3670536 | tf_op jit(solution)/shard_map/dynamic_update_slice | solution.py:128
  (55 shorter events, 0.1 us)
Async XLA Ops:
  0.0 1.5 %copy-start = (bf16[1,896,1024]{2,1,0:T(8,128)(2,1)S(1)}, bf16[1,896,1024]{2,1,0:T(8,128)(2,1)}, u32[]{:S(2)}) copy-start(bf16[1,896,1024]{2,1,0:T(8,128)(2,1)} %param.6) | copy-start | bytes 5505028
  3.3 15.8 %collective-permute-start = (f16[256,1024]{1,0:T(8,128)(2,1)S(1)}, f16[256,1024]{1,0:T(8,128)(2,1)S(1)}, u32[]{:S(2)}, u32[]{:S(2)}) collective-permute-start(f16[256,1024]{1,0:T(8,128)(2,1)S(1)} %fusion.15), channel_id=1, source_target_pairs={{0,1},{1,0},{2,3},{3,2},{4,5},{5,4},{6,7},{7,6},{8,9},{9,8},{10,11... | collective-permute-start | bytes 1572872 | tf_op jit(solution)/shard_map/ppermute | solution.py:19
  14.7 19.0 %collective-permute-start.4 = (f16[256,1024]{1,0:T(8,128)(2,1)}, f16[256,1024]{1,0:T(8,128)(2,1)S(1)}, u32[]{:S(2)}, u32[]{:S(2)}) collective-permute-start(f16[256,1024]{1,0:T(8,128)(2,1)} %get-tuple-element.147), channel_id=1, source_target_pairs={{0,1},{1,0},{2,3},{3,2},{4,5},{5,4},{6,7},{7,6},{8,9},{9,8},{10,11... | collective-permute-start | bytes 1572872 | tf_op jit(solution)/shard_map/ppermute | solution.py:19
  17.9 1.3 %copy-start.2 = (f32[512,1024]{1,0:T(8,128)}, f32[512,1024]{1,0:T(8,128)S(1)}, u32[]{:S(2)}) copy-start(f32[512,1024]{1,0:T(8,128)S(1)} %bitcast_subtract_fusion.1) | copy-start | bytes 6291460
  20.3 21.2 %collective-permute-start.2 = (f16[256,1024]{1,0:T(8,128)(2,1)}, f16[256,1024]{1,0:T(8,128)(2,1)}, u32[]{:S(2)}, u32[]{:S(2)}) collective-permute-start(f16[256,1024]{1,0:T(8,128)(2,1)} %multiply_convert_fusion.8), channel_id=1, source_target_pairs={{2,4},{4,2},{6,8},{8,6},{10,12},{12,10},{14,16},{16,14},{18,20},{2... | collective-permute-start | bytes 1572872 | tf_op jit(solution)/shard_map/ppermute | solution.py:28
  24.2 17.3 %collective-permute-start.3 = (f16[256,1024]{1,0:T(8,128)(2,1)}, f16[256,1024]{1,0:T(8,128)(2,1)}, u32[]{:S(2)}, u32[]{:S(2)}) collective-permute-start(f16[256,1024]{1,0:T(8,128)(2,1)} %multiply_convert_fusion.8), channel_id=1, source_target_pairs={{0,2},{2,0},{4,6},{6,4},{8,10},{10,8},{12,14},{14,12},{16,18},{18,... | collective-permute-start | bytes 1572872 | tf_op jit(solution)/shard_map/ppermute | solution.py:28
  24.2 17.3 %collective-permute-start.1 = (f16[256,1024]{1,0:T(8,128)(2,1)}, f16[256,1024]{1,0:T(8,128)(2,1)S(1)}, u32[]{:S(2)}, u32[]{:S(2)}) collective-permute-start(f16[256,1024]{1,0:T(8,128)(2,1)} %get-tuple-element.77), channel_id=1, source_target_pairs={{0,1},{1,0},{2,3},{3,2},{4,5},{5,4},{6,7},{7,6},{8,9},{9,8},{10,11... | collective-permute-start | bytes 1572872 | tf_op jit(solution)/shard_map/ppermute | solution.py:19
  25.7 8.0 %copy-start.3 = (f32[512,1024]{1,0:T(8,128)S(1)}, f32[512,1024]{1,0:T(8,128)}, u32[]{:S(2)}) copy-start(f32[512,1024]{1,0:T(8,128)} %copy-done.2) | copy-start | bytes 6291460
  25.7 8.2 %copy-start.11 = (f16[256,1024]{1,0:T(8,128)(2,1)S(1)}, f16[256,1024]{1,0:T(8,128)(2,1)}, u32[]{:S(2)}) copy-start(f16[256,1024]{1,0:T(8,128)(2,1)} %get-tuple-element.92) | copy-start | bytes 1572868
  25.7 16.6 %copy-start.10 = (f16[256,1024]{1,0:T(8,128)(2,1)S(1)}, f16[256,1024]{1,0:T(8,128)(2,1)}, u32[]{:S(2)}) copy-start(f16[256,1024]{1,0:T(8,128)(2,1)} %get-tuple-element.99) | copy-start | bytes 1572868
  33.6 30.5 %copy-start.1 = (f32[1536,1024]{1,0:T(8,128)}, f32[1536,1024]{1,0:T(8,128)S(1)}, u32[]{:S(2)}) copy-start(f32[1536,1024]{1,0:T(8,128)S(1)} %bitcast_subtract_fusion) | copy-start | bytes 18874372
  33.6 56.4 %copy-start.20 = (s32[16,3]{0,1:T(4,128)S(1)}, s32[16,3]{0,1:T(4,128)}, u32[]{:S(2)}) copy-start(s32[16,3]{0,1:T(4,128)} %param.7) | copy-start | bytes 580
  33.9 18.8 %collective-permute-start.5 = (f16[256,1024]{1,0:T(8,128)(2,1)S(1)}, f16[256,1024]{1,0:T(8,128)(2,1)S(1)}, u32[]{:S(2)}, u32[]{:S(2)}) collective-permute-start(f16[256,1024]{1,0:T(8,128)(2,1)S(1)} %copy-done.11), channel_id=1, source_target_pairs={{0,1},{1,0},{2,3},{3,2},{4,5},{5,4},{6,7},{7,6},{8,9},{9,8},{10,11... | collective-permute-start | bytes 1572872 | tf_op jit(solution)/shard_map/ppermute | solution.py:19
  34.5 20.8 %collective-permute-start.6 = (f16[256,1024]{1,0:T(8,128)(2,1)S(1)}, f16[256,1024]{1,0:T(8,128)(2,1)S(1)}, u32[]{:S(2)}, u32[]{:S(2)}) collective-permute-start(f16[256,1024]{1,0:T(8,128)(2,1)S(1)} %multiply_convert_fusion.7), channel_id=1, source_target_pairs={{2,4},{4,2},{6,8},{8,6},{10,12},{12,10},{14,16},{16,14},{18,20},{2... | collective-permute-start | bytes 1572872 | tf_op jit(solution)/shard_map/ppermute | solution.py:28
  41.5 13.7 %collective-permute-start.7 = (f16[256,1024]{1,0:T(8,128)(2,1)S(1)}, f16[256,1024]{1,0:T(8,128)(2,1)S(1)}, u32[]{:S(2)}, u32[]{:S(2)}) collective-permute-start(f16[256,1024]{1,0:T(8,128)(2,1)S(1)} %multiply_convert_fusion.7), channel_id=1, source_target_pairs={{0,2},{2,0},{4,6},{6,4},{8,10},{10,8},{12,14},{14,12},{16,18},{18,... | collective-permute-start | bytes 1572872 | tf_op jit(solution)/shard_map/ppermute | solution.py:28
  41.8 18.4 %collective-permute-start.10 = (f16[256,1024]{1,0:T(8,128)(2,1)S(1)}, f16[256,1024]{1,0:T(8,128)(2,1)S(1)}, u32[]{:S(2)}, u32[]{:S(2)}) collective-permute-start(f16[256,1024]{1,0:T(8,128)(2,1)S(1)} %multiply_convert_fusion.6), channel_id=1, source_target_pairs={{0,2},{2,0},{4,6},{6,4},{8,10},{10,8},{12,14},{14,12},{16,18},{18,... | collective-permute-start | bytes 1572872 | tf_op jit(solution)/shard_map/ppermute | solution.py:28
  42.3 21.7 %collective-permute-start.8 = (f16[256,1024]{1,0:T(8,128)(2,1)S(1)}, f16[256,1024]{1,0:T(8,128)(2,1)S(1)}, u32[]{:S(2)}, u32[]{:S(2)}) collective-permute-start(f16[256,1024]{1,0:T(8,128)(2,1)S(1)} %copy-done.10), channel_id=1, source_target_pairs={{0,1},{1,0},{2,3},{3,2},{4,5},{5,4},{6,7},{7,6},{8,9},{9,8},{10,11... | collective-permute-start | bytes 1572872 | tf_op jit(solution)/shard_map/ppermute | solution.py:19
  52.7 12.5 %copy-start.6 = (f16[256,1024]{1,0:T(8,128)(2,1)}, f16[256,1024]{1,0:T(8,128)(2,1)S(1)}, u32[]{:S(2)}) copy-start(f16[256,1024]{1,0:T(8,128)(2,1)S(1)} %collective-permute-done.5) | copy-start | bytes 1572868
  52.7 11.4 %collective-permute-start.9 = (f16[256,1024]{1,0:T(8,128)(2,1)S(1)}, f16[256,1024]{1,0:T(8,128)(2,1)S(1)}, u32[]{:S(2)}, u32[]{:S(2)}) collective-permute-start(f16[256,1024]{1,0:T(8,128)(2,1)S(1)} %multiply_convert_fusion.6), channel_id=1, source_target_pairs={{2,4},{4,2},{6,8},{8,6},{10,12},{12,10},{14,16},{16,14},{18,20},{2... | collective-permute-start | bytes 1572872 | tf_op jit(solution)/shard_map/ppermute | solution.py:28
  55.2 10.0 %copy-start.12 = (f16[256,1024]{1,0:T(8,128)(2,1)}, f16[256,1024]{1,0:T(8,128)(2,1)S(1)}, u32[]{:S(2)}) copy-start(f16[256,1024]{1,0:T(8,128)(2,1)S(1)} %collective-permute-done.6) | copy-start | bytes 1572868
  55.2 10.0 %copy-start.14 = (f16[256,1024]{1,0:T(8,128)(2,1)}, f16[256,1024]{1,0:T(8,128)(2,1)S(1)}, u32[]{:S(2)}) copy-start(f16[256,1024]{1,0:T(8,128)(2,1)S(1)} %collective-permute-done.7) | copy-start | bytes 1572868
  56.5 18.0 %collective-permute-start.11 = (f16[256,1024]{1,0:T(8,128)(2,1)}, f16[256,1024]{1,0:T(8,128)(2,1)}, u32[]{:S(2)}, u32[]{:S(2)}) collective-permute-start(f16[256,1024]{1,0:T(8,128)(2,1)} %get-tuple-element.106), channel_id=1, source_target_pairs={{0,1},{1,0},{2,3},{3,2},{4,5},{5,4},{6,7},{7,6},{8,9},{9,8},{10,11... | collective-permute-start | bytes 1572872 | tf_op jit(solution)/shard_map/ppermute | solution.py:19
  58.0 25.0 %collective-permute-start.12 = (f16[256,1024]{1,0:T(8,128)(2,1)}, f16[256,1024]{1,0:T(8,128)(2,1)}, u32[]{:S(2)}, u32[]{:S(2)}) collective-permute-start(f16[256,1024]{1,0:T(8,128)(2,1)} %multiply_convert_fusion.5), channel_id=1, source_target_pairs={{2,4},{4,2},{6,8},{8,6},{10,12},{12,10},{14,16},{16,14},{18,20},{2... | collective-permute-start | bytes 1572872 | tf_op jit(solution)/shard_map/ppermute | solution.py:28
  60.2 5.0 %copy-start.16 = (f16[256,1024]{1,0:T(8,128)(2,1)}, f16[256,1024]{1,0:T(8,128)(2,1)S(1)}, u32[]{:S(2)}) copy-start(f16[256,1024]{1,0:T(8,128)(2,1)S(1)} %collective-permute-done.10) | copy-start | bytes 1572868
  60.2 22.8 %collective-permute-start.13 = (f16[256,1024]{1,0:T(8,128)(2,1)}, f16[256,1024]{1,0:T(8,128)(2,1)}, u32[]{:S(2)}, u32[]{:S(2)}) collective-permute-start(f16[256,1024]{1,0:T(8,128)(2,1)} %multiply_convert_fusion.5), channel_id=1, source_target_pairs={{0,2},{2,0},{4,6},{6,4},{8,10},{10,8},{12,14},{14,12},{16,18},{18,... | collective-permute-start | bytes 1572872 | tf_op jit(solution)/shard_map/ppermute | solution.py:28
  64.0 1.2 copy-start.8
  64.2 1.1 copy-start.18
  65.2 23.4 %collective-permute-start.14 = (f16[256,1024]{1,0:T(8,128)(2,1)}, f16[256,1024]{1,0:T(8,128)(2,1)}, u32[]{:S(2)}, u32[]{:S(2)}) collective-permute-start(f16[256,1024]{1,0:T(8,128)(2,1)} %get-tuple-element.113), channel_id=1, source_target_pairs={{0,1},{1,0},{2,3},{3,2},{4,5},{5,4},{6,7},{7,6},{8,9},{9,8},{10,11... | collective-permute-start | bytes 1572872 | tf_op jit(solution)/shard_map/ppermute | solution.py:19
  67.3 26.1 %collective-permute-start.15 = (f16[256,1024]{1,0:T(8,128)(2,1)}, f16[256,1024]{1,0:T(8,128)(2,1)}, u32[]{:S(2)}, u32[]{:S(2)}) collective-permute-start(f16[256,1024]{1,0:T(8,128)(2,1)} %multiply_convert_fusion.4), channel_id=1, source_target_pairs={{2,4},{4,2},{6,8},{8,6},{10,12},{12,10},{14,16},{16,14},{18,20},{2... | collective-permute-start | bytes 1572872 | tf_op jit(solution)/shard_map/ppermute | solution.py:28
  74.5 19.0 %collective-permute-start.16 = (f16[256,1024]{1,0:T(8,128)(2,1)}, f16[256,1024]{1,0:T(8,128)(2,1)}, u32[]{:S(2)}, u32[]{:S(2)}) collective-permute-start(f16[256,1024]{1,0:T(8,128)(2,1)} %multiply_convert_fusion.4), channel_id=1, source_target_pairs={{0,2},{2,0},{4,6},{6,4},{8,10},{10,8},{12,14},{14,12},{16,18},{18,... | collective-permute-start | bytes 1572872 | tf_op jit(solution)/shard_map/ppermute | solution.py:28
  85.4 17.8 %collective-permute-start.18 = (f16[256,1024]{1,0:T(8,128)(2,1)}, f16[256,1024]{1,0:T(8,128)(2,1)}, u32[]{:S(2)}, u32[]{:S(2)}) collective-permute-start(f16[256,1024]{1,0:T(8,128)(2,1)} %multiply_convert_fusion.3), channel_id=1, source_target_pairs={{2,4},{4,2},{6,8},{8,6},{10,12},{12,10},{14,16},{16,14},{18,20},{2... | collective-permute-start | bytes 1572872 | tf_op jit(solution)/shard_map/ppermute | solution.py:28
  88.6 14.7 %collective-permute-start.19 = (f16[256,1024]{1,0:T(8,128)(2,1)}, f16[256,1024]{1,0:T(8,128)(2,1)}, u32[]{:S(2)}, u32[]{:S(2)}) collective-permute-start(f16[256,1024]{1,0:T(8,128)(2,1)} %multiply_convert_fusion.3), channel_id=1, source_target_pairs={{0,2},{2,0},{4,6},{6,4},{8,10},{10,8},{12,14},{14,12},{16,18},{18,... | collective-permute-start | bytes 1572872 | tf_op jit(solution)/shard_map/ppermute | solution.py:28
  88.6 14.7 %collective-permute-start.17 = (f16[256,1024]{1,0:T(8,128)(2,1)}, f16[256,1024]{1,0:T(8,128)(2,1)}, u32[]{:S(2)}, u32[]{:S(2)}) collective-permute-start(f16[256,1024]{1,0:T(8,128)(2,1)} %get-tuple-element.120), channel_id=1, source_target_pairs={{0,1},{1,0},{2,3},{3,2},{4,5},{5,4},{6,7},{7,6},{8,9},{9,8},{10,11... | collective-permute-start | bytes 1572872 | tf_op jit(solution)/shard_map/ppermute | solution.py:19
  95.0 26.1 %collective-permute-start.20 = (f16[256,1024]{1,0:T(8,128)(2,1)S(1)}, f16[256,1024]{1,0:T(8,128)(2,1)S(1)}, u32[]{:S(2)}, u32[]{:S(2)}) collective-permute-start(f16[256,1024]{1,0:T(8,128)(2,1)S(1)} %multiply_convert_fusion.2), channel_id=1, source_target_pairs={{0,2},{2,0},{4,6},{6,4},{8,10},{10,8},{12,14},{14,12},{16,18},{18,... | collective-permute-start | bytes 1572872 | tf_op jit(solution)/shard_map/ppermute | solution.py:28
  96.7 24.4 %collective-permute-start.21 = (f16[256,1024]{1,0:T(8,128)(2,1)S(1)}, f16[256,1024]{1,0:T(8,128)(2,1)S(1)}, u32[]{:S(2)}, u32[]{:S(2)}) collective-permute-start(f16[256,1024]{1,0:T(8,128)(2,1)S(1)} %multiply_convert_fusion.2), channel_id=1, source_target_pairs={{2,4},{4,2},{6,8},{8,6},{10,12},{12,10},{14,16},{16,14},{18,20},{2... | collective-permute-start | bytes 1572872 | tf_op jit(solution)/shard_map/ppermute | solution.py:28
  104.9 18.4 %collective-permute-start.22 = (f16[256,1024]{1,0:T(8,128)(2,1)S(1)}, f16[256,1024]{1,0:T(8,128)(2,1)S(1)}, u32[]{:S(2)}, u32[]{:S(2)}) collective-permute-start(f16[256,1024]{1,0:T(8,128)(2,1)S(1)} %multiply_convert_fusion.1), channel_id=1, source_target_pairs={{0,2},{2,0},{4,6},{6,4},{8,10},{10,8},{12,14},{14,12},{16,18},{18,... | collective-permute-start | bytes 1572872 | tf_op jit(solution)/shard_map/ppermute | solution.py:28
  104.9 18.3 %collective-permute-start.23 = (f16[256,1024]{1,0:T(8,128)(2,1)S(1)}, f16[256,1024]{1,0:T(8,128)(2,1)S(1)}, u32[]{:S(2)}, u32[]{:S(2)}) collective-permute-start(f16[256,1024]{1,0:T(8,128)(2,1)S(1)} %multiply_convert_fusion.1), channel_id=1, source_target_pairs={{2,4},{4,2},{6,8},{8,6},{10,12},{12,10},{14,16},{16,14},{18,20},{2... | collective-permute-start | bytes 1572872 | tf_op jit(solution)/shard_map/ppermute | solution.py:28
  107.9 4.2 %copy-start.4 = (f32[512,1024]{1,0:T(8,128)S(1)}, f32[512,1024]{1,0:T(8,128)}, u32[]{:S(2)}) copy-start(f32[512,1024]{1,0:T(8,128)} %copy-done.2) | copy-start | bytes 6291460
  107.9 4.2 %copy-start.13 = (f16[256,1024]{1,0:T(8,128)(2,1)S(1)}, f16[256,1024]{1,0:T(8,128)(2,1)}, u32[]{:S(2)}) copy-start(f16[256,1024]{1,0:T(8,128)(2,1)} %copy-done.12) | copy-start | bytes 1572868
  107.9 4.2 %copy-start.15 = (f16[256,1024]{1,0:T(8,128)(2,1)S(1)}, f16[256,1024]{1,0:T(8,128)(2,1)}, u32[]{:S(2)}) copy-start(f16[256,1024]{1,0:T(8,128)(2,1)} %copy-done.14) | copy-start | bytes 1572868
  107.9 5.3 %slice-start = ((s8[6291456]{0:T(1024)(128)(4,1)}), s8[4194304]{0:T(1024)(128)(4,1)S(1)}, s32[]{:S(2)}) async-start(s8[6291456]{0:T(1024)(128)(4,1)} %bitcast.57), calls=%async_computation | async-start | bytes 8388608
  111.0 2.2 %slice-start.1 = ((s8[6291456]{0:T(1024)(128)(4,1)}), s8[2097152]{0:T(1024)(128)(4,1)S(1)}, s32[]{:S(2)}) async-start(s8[6291456]{0:T(1024)(128)(4,1)} %bitcast.57), calls=%async_computation.1 | async-start | bytes 4194304
  111.0 2.2 %copy-start.17 = (f16[256,1024]{1,0:T(8,128)(2,1)S(1)}, f16[256,1024]{1,0:T(8,128)(2,1)}, u32[]{:S(2)}) copy-start(f16[256,1024]{1,0:T(8,128)(2,1)} %copy-done.16) | copy-start | bytes 1572868
  111.0 2.2 %copy-start.19 = (f16[256,1024]{1,0:T(8,128)(2,1)S(1)}, f16[256,1024]{1,0:T(8,128)(2,1)}, u32[]{:S(2)}) copy-start(f16[256,1024]{1,0:T(8,128)(2,1)} %copy-done.18) | copy-start | bytes 1572868
  111.0 3.3 %copy-start.7 = (f16[256,1024]{1,0:T(8,128)(2,1)S(1)}, f16[256,1024]{1,0:T(8,128)(2,1)}, u32[]{:S(2)}) copy-start(f16[256,1024]{1,0:T(8,128)(2,1)} %copy-done.6) | copy-start | bytes 1572868
  112.1 4.4 %copy-start.9 = (f16[256,1024]{1,0:T(8,128)(2,1)S(1)}, f16[256,1024]{1,0:T(8,128)(2,1)}, u32[]{:S(2)}) copy-start(f16[256,1024]{1,0:T(8,128)(2,1)} %copy-done.8) | copy-start | bytes 1572868
  123.2 3.4 %copy-start.5 = (f32[1,2048,1024]{2,1,0:T(8,128)}, f32[1,2048,1024]{2,1,0:T(8,128)S(1)}, u32[]{:S(2)}) copy-start(f32[1,2048,1024]{2,1,0:T(8,128)S(1)} %bitcast_dynamic-update-slice_fusion.1) | copy-start | bytes 25165828

commit v9 on v8

--- a/solution.py
+++ b/solution.py
@@ -10,7 +10,9 @@
 LARGEST = 6.0
 WIRE = jnp.float16
 STEP = 256
-AHEAD = 2
+AHEAD = 3
+LAG = 2
+NLAG = 1
 
 
 def from_behind(value, axis, steps):
@@ -93,18 +95,18 @@
     rest = for_others(shard, step, rows - step) if chunks > 1 else []
     for chunk in range(1, chunks):
         terms[chunk] = [rows_of(term, chunk - 1) for term in rest]
-    if chunks > 1:
-        arrived[1] = send_terms(terms[1])
+    for chunk in range(1, min(AHEAD, chunks)):
+        arrived[chunk] = send_terms(terms[chunk])
     base = [own_part(shard, 0, split)]
 
     arrived[0], base, terms = lax.optimization_barrier((arrived[0], base, terms))
     for chunk in range(chunks):
         if chunk == 1:
             arrived[1], base = lax.optimization_barrier((arrived[1], base))
-        if chunk >= 2:
-            arrived[chunk], far[chunk - 2], near[chunk - 2] = lax.optimization_barrier(
-                (arrived[chunk], far[chunk - 2], near[chunk - 2])
-            )
+        if chunk >= LAG:
+            arrived[chunk], far[chunk - LAG] = lax.optimization_barrier((arrived[chunk], far[chunk - LAG]))
+        if chunk >= NLAG:
+            arrived[chunk], near[chunk - NLAG] = lax.optimization_barrier((arrived[chunk], near[chunk - NLAG]))
         sent = (u_of(chunk) * scale).astype(WIRE)
         sent, base, later = lax.optimization_barrier((sent, base, shard))
         if chunk == 0 and split < chunks:

time: 130 us -> 124 us (0.954)
  waiting for transfers between devices: 27.9 us -> 19 us
  other arithmetic: 26.5 us -> 20.3 us
  local copies, waits for them, and re-layouts: 9.12 us -> 14 us
  starting transfers between devices: 44 us -> 47.8 us
    ppermute x8, waiting for transfers between devices: 27.7 us -> 18.9 us  [from_behind(): return lax.ppermute(value, axis, pairs)]
    ppermute x8, starting transfers between devices: 12.3 us -> 17.6 us  [from_behind(): return lax.ppermute(value, axis, pairs)]
    unnamed x46 -> x78, local copies, waits for them, and re-layouts: 5.16 us -> 10.1 us
    convert_element_type x8, other arithmetic: 9.36 us -> 5.6 us  [on_device(): sent = (u_of(chunk) * scale).astype(WIRE)]
    dynamic_update_slice x7, other arithmetic: 14.1 us -> 11.7 us  [on_device(): out = lax.dynamic_update_slice_in_dim(out, mixed, chunk * step, axis=0)]
    ppermute x16, starting transfers between devices: 31.8 us -> 30.2 us  [swapped(): return lax.ppermute(value, axis, pairs)]
  transfers between devices with their start and end apart: 24 -> 24, of which waited for: 7 -> 6; matrix products, arithmetic and copies ran while one was open for 35% -> 31% of each run, Pallas kernels for 0% -> 0%
where the time goes in v9:
time: 124 us
  starting transfers between devices  47.8 us (39%)
  other arithmetic  20.3 us (16%)
  matrix products  19.9 us (16%)
  waiting for transfers between devices  19 us (15%)
  local copies, waits for them, and re-layouts  14 us (11%)
  between operations  3 us (2%)
    ppermute x16, starting transfers between devices, swapped(): return lax.ppermute(value, axis, pairs)  30.2 us
    dot_general x4, matrix products, partial(): lax.dot_general(block, cot_local, (((0,), (0,)), ((), ())), preferred_ele...  19.8 us
    ppermute x8, waiting for transfers between devices, from_behind(): return lax.ppermute(value, axis, pairs)  18.9 us
    ppermute x8, starting transfers between devices, from_behind(): return lax.ppermute(value, axis, pairs)  17.6 us
    dynamic_update_slice x7, other arithmetic, on_device(): out = lax.dynamic_update_slice_in_dim(out, mixed, chunk * step, axis=0)  11.7 us
    unnamed x78, local copies, waits for them, and re-layouts  10.1 us
    convert_element_type x8, other arithmetic, on_device(): sent = (u_of(chunk) * scale).astype(WIRE)  5.6 us
    add x1, other arithmetic, on_device(): c_near * near[chunk].astype(jnp.float32) + c_self * u_of(chunk)  3.07 us
  transfers between devices with their start and end apart: 24, of which 6 were waited for; matrix products, arithmetic and copies ran while one was open for 31% of the time, Pallas kernels for 0%

profile of v9, /device:TPU:0, one launch (start us, length us, event | category | flops | bytes accessed | tf_op | source)
XLA Modules:
  0.0 124.0 jit_solution(2649670840886934626)
XLA Ops:
  0.0 1.5 %copy-done = bf16[1,896,1024]{2,1,0:T(8,128)(2,1)S(1)} copy-done((bf16[1,896,1024]{2,1,0:T(8,128)(2,1)S(1)}, bf16[1,896,1024]{2,1,0:T(8,128)(2,1)}, u32[]{:S(2)}) %copy-start) | copy-done | bytes 1835032
  1.5 2.5 %fusion.15 = f16[256,1024]{1,0:T(8,128)(2,1)} fusion(bf16[1,896,1024]{2,1,0:T(8,128)(2,1)S(1)} %copy-done, bf16[1,896,4096]{2,1,0:T(8,128)(2,1)} %param.5, s32[]{:T(128)S(6)} %select_n.34), kind=kOutput, calls=%fused_computation.15 | convolution fusion | flops 470286336 | bytes 2818052 | tf_op jit(solution)/shard_map/dot_general | solution.py:58
  4.0 3.0 %collective-permute-start.1 = (f16[256,1024]{1,0:T(8,128)(2,1)}, f16[256,1024]{1,0:T(8,128)(2,1)S(1)}, u32[]{:S(2)}, u32[]{:S(2)}) collective-permute-start(f16[256,1024]{1,0:T(8,128)(2,1)} %fusion.15), channel_id=1, source_target_pairs={{0,1},{1,0},{2,3},{3,2},{4,5},{5,4},{6,7},{7,6},{8,9},{9,8},{10,11... | collective-permute-start | bytes 1572872 | tf_op jit(solution)/shard_map/ppermute | solution.py:21
  7.0 6.2 %multiply_convert_fusion = f16[1792,1024]{1,0:T(8,128)(2,1)S(1)} fusion(bf16[1,896,4096]{2,1,0:T(8,128)(2,1)} %param.5, s32[]{:T(128)S(6)} %select_n.33, bf16[1,896,1024]{2,1,0:T(8,128)(2,1)S(1)} %copy-done), kind=kOutput, calls=%fused_computation.1 | convolution fusion | flops 3292004352 | bytes 8716292 | tf_op jit(solution)/shard_map/dot_general | solution.py:58
  13.2 2.2 %fusion.32 = (f16[256,1024]{1,0:T(8,128)(2,1)}, f16[256,1024]{1,0:T(8,128)(2,1)}, f16[256,1024]{1,0:T(8,128)(2,1)}, f16[256,1024]{1,0:T(8,128)(2,1)}, f16[256,10...) fusion(f16[1792,1024]{1,0:T(8,128)(2,1)S(1)} %multiply_convert_fusion), kind=kLoop, calls=%fused_computation.55 | loop fusion | bytes 7340032 | tf_op jit(solution)/shard_map/slice | solution.py:76
  15.4 0.0 collective-permute-start.3
  15.4 2.0 %collective-permute-start = (f16[256,1024]{1,0:T(8,128)(2,1)}, f16[256,1024]{1,0:T(8,128)(2,1)S(1)}, u32[]{:S(2)}, u32[]{:S(2)}) collective-permute-start(f16[256,1024]{1,0:T(8,128)(2,1)} %get-tuple-element.157), channel_id=1, source_target_pairs={{0,1},{1,0},{2,3},{3,2},{4,5},{5,4},{6,7},{7,6},{8,9},{9,8},{10,11... | collective-permute-start | bytes 1572872 | tf_op jit(solution)/shard_map/ppermute | solution.py:21
  17.4 3.2 %bitcast_subtract_fusion.1 = f32[512,1024]{1,0:T(8,128)S(1)} fusion(f32[1,2048,1024]{2,1,0:T(8,128)} %param.4, bf16[1,896,1024]{2,1,0:T(8,128)(2,1)S(1)} %copy-done, bf16[1,896,4096]{2,1,0:T(8,128)(2,1)} %param.5, s32[]{:T(128)S(6)} %select_n.35), kind=kOutput, calls=%fused_computation.7 | convolution fusion | flops 940572672 | bytes 6946820 | tf_op jit(solution)/shard_map/dot_general | solution.py:58
  20.6 0.0 collective-permute-done.1
  20.6 1.3 %copy-done.2 = f32[512,1024]{1,0:T(8,128)} copy-done((f32[512,1024]{1,0:T(8,128)}, f32[512,1024]{1,0:T(8,128)S(1)}, u32[]{:S(2)}) %copy-start.2) | copy-done | bytes 2097176
  21.9 1.1 multiply_convert_fusion.8
  23.0 4.6 %collective-permute-start.2 = (f16[256,1024]{1,0:T(8,128)(2,1)}, f16[256,1024]{1,0:T(8,128)(2,1)}, u32[]{:S(2)}, u32[]{:S(2)}) collective-permute-start(f16[256,1024]{1,0:T(8,128)(2,1)} %multiply_convert_fusion.8), channel_id=1, source_target_pairs={{2,4},{4,2},{6,8},{8,6},{10,12},{12,10},{14,16},{16,14},{18,20},{2... | collective-permute-start | bytes 1572872 | tf_op jit(solution)/shard_map/ppermute | solution.py:30
  27.6 7.9 %bitcast_subtract_fusion = f32[1536,1024]{1,0:T(8,128)S(1)} fusion(f32[1,2048,1024]{2,1,0:T(8,128)} %param.4, bf16[1,896,4096]{2,1,0:T(8,128)(2,1)} %param.5, s32[]{:T(128)S(6)} %select_n.36, bf16[1,896,1024]{2,1,0:T(8,128)(2,1)S(1)} %copy-done), kind=kOutput, calls=%fused_computation.2 | convolution fusion | flops 2821718016 | bytes 17170436 | tf_op jit(solution)/shard_map/dot_general | solution.py:58
  35.5 0.0 copy-start.1
  35.6 0.0 copy-start.36
  35.6 0.2 multiply_convert_fusion.7
  35.9 0.1 collective-permute-start.5
  35.9 0.6 collective-permute-start.6
  36.5 1.4 %collective-permute-start.7 = (f16[256,1024]{1,0:T(8,128)(2,1)S(1)}, f16[256,1024]{1,0:T(8,128)(2,1)S(1)}, u32[]{:S(2)}, u32[]{:S(2)}) collective-permute-start(f16[256,1024]{1,0:T(8,128)(2,1)S(1)} %multiply_convert_fusion.7), channel_id=1, source_target_pairs={{2,4},{4,2},{6,8},{8,6},{10,12},{12,10},{14,16},{16,14},{18,20},{2... | collective-permute-start | bytes 1572872 | tf_op jit(solution)/shard_map/ppermute | solution.py:30
  38.0 4.5 %collective-permute-done = f16[256,1024]{1,0:T(8,128)(2,1)S(1)} collective-permute-done((f16[256,1024]{1,0:T(8,128)(2,1)}, f16[256,1024]{1,0:T(8,128)(2,1)S(1)}, u32[]{:S(2)}, u32[]{:S(2)}) %collective-permute-start) | collective-permute-done | bytes 524320 | tf_op jit(solution)/shard_map/ppermute | solution.py:21
  42.5 0.2 multiply_convert_fusion.6
  42.7 0.6 copy-done.18
  43.3 2.1 %collective-permute-start.9 = (f16[256,1024]{1,0:T(8,128)(2,1)S(1)}, f16[256,1024]{1,0:T(8,128)(2,1)S(1)}, u32[]{:S(2)}, u32[]{:S(2)}) collective-permute-start(f16[256,1024]{1,0:T(8,128)(2,1)S(1)} %copy-done.16), channel_id=1, source_target_pairs={{0,1},{1,0},{2,3},{3,2},{4,5},{5,4},{6,7},{7,6},{8,9},{9,8},{10,11... | collective-permute-start | bytes 1572872 | tf_op jit(solution)/shard_map/ppermute | solution.py:21
  45.3 4.4 %collective-permute-start.10 = (f16[256,1024]{1,0:T(8,128)(2,1)S(1)}, f16[256,1024]{1,0:T(8,128)(2,1)S(1)}, u32[]{:S(2)}, u32[]{:S(2)}) collective-permute-start(f16[256,1024]{1,0:T(8,128)(2,1)S(1)} %multiply_convert_fusion.6), channel_id=1, source_target_pairs={{2,4},{4,2},{6,8},{8,6},{10,12},{12,10},{14,16},{16,14},{18,20},{2... | collective-permute-start | bytes 1572872 | tf_op jit(solution)/shard_map/ppermute | solution.py:30
  49.7 4.0 %collective-permute-done.6 = f16[256,1024]{1,0:T(8,128)(2,1)S(1)} collective-permute-done((f16[256,1024]{1,0:T(8,128)(2,1)S(1)}, f16[256,1024]{1,0:T(8,128)(2,1)S(1)}, u32[]{:S(2)}, u32[]{:S(2)}) %collective-permute-start.6) | collective-permute-done | bytes 524320 | tf_op jit(solution)/shard_map/ppermute | solution.py:21
  53.7 0.8 copy-done.6
  54.5 0.2 multiply_convert_fusion.5
  54.7 0.1 collective-permute-start.11
  54.8 3.8 %collective-permute-start.12 = (f16[256,1024]{1,0:T(8,128)(2,1)S(1)}, f16[256,1024]{1,0:T(8,128)(2,1)S(1)}, u32[]{:S(2)}, u32[]{:S(2)}) collective-permute-start(f16[256,1024]{1,0:T(8,128)(2,1)S(1)} %copy-done.15), channel_id=1, source_target_pairs={{0,1},{1,0},{2,3},{3,2},{4,5},{5,4},{6,7},{7,6},{8,9},{9,8},{10,11... | collective-permute-start | bytes 1572872 | tf_op jit(solution)/shard_map/ppermute | solution.py:21
  58.6 2.6 %collective-permute-start.13 = (f16[256,1024]{1,0:T(8,128)(2,1)S(1)}, f16[256,1024]{1,0:T(8,128)(2,1)S(1)}, u32[]{:S(2)}, u32[]{:S(2)}) collective-permute-start(f16[256,1024]{1,0:T(8,128)(2,1)S(1)} %multiply_convert_fusion.5), channel_id=1, source_target_pairs={{2,4},{4,2},{6,8},{8,6},{10,12},{12,10},{14,16},{16,14},{18,20},{2... | collective-permute-start | bytes 1572872 | tf_op jit(solution)/shard_map/ppermute | solution.py:30
  61.2 3.7 %collective-permute-done.9 = f16[256,1024]{1,0:T(8,128)(2,1)S(1)} collective-permute-done((f16[256,1024]{1,0:T(8,128)(2,1)S(1)}, f16[256,1024]{1,0:T(8,128)(2,1)S(1)}, u32[]{:S(2)}, u32[]{:S(2)}) %collective-permute-start.9) | collective-permute-done | bytes 524320 | tf_op jit(solution)/shard_map/ppermute | solution.py:21
  64.9 0.8 copy-done.8
  65.7 0.2 multiply_convert_fusion.4
  65.9 0.1 collective-permute-start.14
  66.0 2.1 %collective-permute-start.15 = (f16[256,1024]{1,0:T(8,128)(2,1)S(1)}, f16[256,1024]{1,0:T(8,128)(2,1)S(1)}, u32[]{:S(2)}, u32[]{:S(2)}) collective-permute-start(f16[256,1024]{1,0:T(8,128)(2,1)S(1)} %copy-done.14), channel_id=1, source_target_pairs={{0,1},{1,0},{2,3},{3,2},{4,5},{5,4},{6,7},{7,6},{8,9},{9,8},{10,11... | collective-permute-start | bytes 1572872 | tf_op jit(solution)/shard_map/ppermute | solution.py:21
  68.2 4.3 %collective-permute-start.16 = (f16[256,1024]{1,0:T(8,128)(2,1)S(1)}, f16[256,1024]{1,0:T(8,128)(2,1)S(1)}, u32[]{:S(2)}, u32[]{:S(2)}) collective-permute-start(f16[256,1024]{1,0:T(8,128)(2,1)S(1)} %multiply_convert_fusion.4), channel_id=1, source_target_pairs={{2,4},{4,2},{6,8},{8,6},{10,12},{12,10},{14,16},{16,14},{18,20},{2... | collective-permute-start | bytes 1572872 | tf_op jit(solution)/shard_map/ppermute | solution.py:30
  72.5 3.7 %collective-permute-done.12 = f16[256,1024]{1,0:T(8,128)(2,1)S(1)} collective-permute-done((f16[256,1024]{1,0:T(8,128)(2,1)S(1)}, f16[256,1024]{1,0:T(8,128)(2,1)S(1)}, u32[]{:S(2)}, u32[]{:S(2)}) %collective-permute-start.12) | collective-permute-done | bytes 524320 | tf_op jit(solution)/shard_map/ppermute | solution.py:21
  76.2 0.8 copy-done.10
  77.0 1.0 multiply_convert_fusion.3
  78.0 4.0 %collective-permute-start.18 = (f16[256,1024]{1,0:T(8,128)(2,1)}, f16[256,1024]{1,0:T(8,128)(2,1)}, u32[]{:S(2)}, u32[]{:S(2)}) collective-permute-start(f16[256,1024]{1,0:T(8,128)(2,1)} %get-tuple-element.129), channel_id=1, source_target_pairs={{0,1},{1,0},{2,3},{3,2},{4,5},{5,4},{6,7},{7,6},{8,9},{9,8},{10,11... | collective-permute-start | bytes 1572872 | tf_op jit(solution)/shard_map/ppermute | solution.py:21
  82.0 2.4 %collective-permute-start.19 = (f16[256,1024]{1,0:T(8,128)(2,1)}, f16[256,1024]{1,0:T(8,128)(2,1)}, u32[]{:S(2)}, u32[]{:S(2)}) collective-permute-start(f16[256,1024]{1,0:T(8,128)(2,1)} %multiply_convert_fusion.3), channel_id=1, source_target_pairs={{2,4},{4,2},{6,8},{8,6},{10,12},{12,10},{14,16},{16,14},{18,20},{2... | collective-permute-start | bytes 1572872 | tf_op jit(solution)/shard_map/ppermute | solution.py:30
  84.4 3.0 %collective-permute-done.15 = f16[256,1024]{1,0:T(8,128)(2,1)S(1)} collective-permute-done((f16[256,1024]{1,0:T(8,128)(2,1)S(1)}, f16[256,1024]{1,0:T(8,128)(2,1)S(1)}, u32[]{:S(2)}, u32[]{:S(2)}) %collective-permute-start.15) | collective-permute-done | bytes 524320 | tf_op jit(solution)/shard_map/ppermute | solution.py:21
  87.4 0.8 copy-done.12
  88.2 1.0 multiply_convert_fusion.2
  89.3 0.1 collective-permute-start.20
  89.4 0.1 fusion.18
  89.5 0.7 fusion.33
  92.6 5.2 %collective-permute-start.21 = (f16[256,1024]{1,0:T(8,128)(2,1)}, f16[256,1024]{1,0:T(8,128)(2,1)S(1)}, u32[]{:S(2)}, u32[]{:S(2)}) collective-permute-start(f16[256,1024]{1,0:T(8,128)(2,1)} %multiply_convert_fusion.2), channel_id=1, source_target_pairs={{2,4},{4,2},{6,8},{8,6},{10,12},{12,10},{14,16},{16,14},{18,20},{2... | collective-permute-start | bytes 1572872 | tf_op jit(solution)/shard_map/ppermute | solution.py:30
  97.8 0.1 collective-permute-done.18
  97.9 1.6 %multiply_convert_fusion.1 = f16[256,1024]{1,0:T(8,128)(2,1)S(1)} fusion(f16[256,1024]{1,0:T(8,128)(2,1)} %collective-permute-done.18, f32[1536,1024]{1,0:T(8,128)} %copy-done.1), kind=kLoop, calls=%fused_computation.26 | loop fusion | flops 1310720 | bytes 2097152 | tf_op jit(solution)/shard_map/convert_element_type | solution.py:110
  99.5 0.1 collective-permute-start.22
  99.6 4.9 %collective-permute-start.23 = (f16[256,1024]{1,0:T(8,128)(2,1)S(1)}, f16[256,1024]{1,0:T(8,128)(2,1)S(1)}, u32[]{:S(2)}, u32[]{:S(2)}) collective-permute-start(f16[256,1024]{1,0:T(8,128)(2,1)S(1)} %multiply_convert_fusion.1), channel_id=1, source_target_pairs={{2,4},{4,2},{6,8},{8,6},{10,12},{12,10},{14,16},{16,14},{18,20},{2... | collective-permute-start | bytes 1572872 | tf_op jit(solution)/shard_map/ppermute | solution.py:30
  104.4 3.1 %multiply_add_fusion = f32[256,1024]{1,0:T(8,128)S(1)} fusion(f16[256,1024]{1,0:T(8,128)(2,1)} %collective-permute-done.2, f32[512,1024]{1,0:T(8,128)} %copy-done.2, f16[256,1024]{1,0:T(8,128)(2,1)} %collective-permute-done.4, f16[256,1024]{1,0:T(8,128)(2,1)S(1)} %collective-permute-done.1, f32[]{:T(128)S(6)} %div.51, f32[]{:T(128)} %bitcast.11, f32[]{:T(128)S(6)} %div.42), kind=kLoop, calls=%fused_computation.25 | loop fusion | flops 2621440 | bytes 3670028 | tf_op jit(solution)/shard_map/add | solution.py:126
  107.5 0.0 slice-start.1
  107.6 1.1 pad_bitcast_fusion
  108.7 1.2 %bitcast_dynamic-update-slice_fusion.6 = f32[1,2048,1024]{2,1,0:T(8,128)S(1)} fusion(f32[1,2048,1024]{2,1,0:T(8,128)S(1)} %pad_bitcast_fusion, f16[256,1024]{1,0:T(8,128)(2,1)S(1)} %copy-done.21, f32[512,1024]{1,0:T(8,128)S(1)} %copy-done.4, f16[256,1024]{1,0:T(8,128)(2,1)S(1)} %copy-done.19, f16[256,1024]{1,0:T(8,128)(2,1)S(1)} %collective-permute-done.3, ...), kind=kLoop, calls=%fused_computation.24 | loop fusion | flops 2621440 | bytes 3670028 | tf_op jit(solution)/shard_map/dynamic_update_slice | solution.py:130
  110.0 1.1 bitcast_dynamic-update-slice_fusion.5
  111.2 1.1 bitcast_dynamic-update-slice_fusion.4
  112.3 1.1 bitcast_dynamic-update-slice_fusion.3
  113.4 2.1 %bitcast_dynamic-update-slice_fusion.2 = f32[1,2048,1024]{2,1,0:T(8,128)S(1)} fusion(f32[1,2048,1024]{2,1,0:T(8,128)S(1)} %bitcast_dynamic-update-slice_fusion.3, f16[256,1024]{1,0:T(8,128)(2,1)} %collective-permute-done.19, f32[1536,1024]{1,0:T(8,128)S(1)} %bitcast.58, f16[256,1024]{1,0:T(8,128)(2,1)S(1)} %copy-done.35, f16[256,1024]{1,0:T(8,128)(2,1)S(1)} %copy-done.11, ...), kind=kLoop, calls=%fused_computation.20 | loop fusion | flops 2621440 | bytes 3670028 | tf_op jit(solution)/shard_map/dynamic_update_slice | solution.py:130
  115.5 2.1 %bitcast_dynamic-update-slice_fusion.1 = f32[1,2048,1024]{2,1,0:T(8,128)S(1)} fusion(f32[1,2048,1024]{2,1,0:T(8,128)S(1)} %bitcast_dynamic-update-slice_fusion.2, f16[256,1024]{1,0:T(8,128)(2,1)S(1)} %collective-permute-done.21, f32[1536,1024]{1,0:T(8,128)S(1)} %bitcast.58, f16[256,1024]{1,0:T(8,128)(2,1)} %collective-permute-done.20, ...), kind=kLoop, calls=%fused_computation.19 | loop fusion | flops 2621440 | bytes 3670028 | tf_op jit(solution)/shard_map/dynamic_update_slice | solution.py:130
  117.5 0.0 copy-start.5
  117.6 3.4 %copy-done.5 = f32[1,2048,1024]{2,1,0:T(8,128)} copy-done((f32[1,2048,1024]{2,1,0:T(8,128)}, f32[1,2048,1024]{2,1,0:T(8,128)S(1)}, u32[]{:S(2)}) %copy-start.5) | copy-done | bytes 8388632
  120.9 3.0 %bitcast_dynamic-update-slice_fusion = f32[1,2048,1024]{2,1,0:T(8,128)} fusion(f32[1,2048,1024]{2,1,0:T(8,128)} %copy-done.5, f16[256,1024]{1,0:T(8,128)(2,1)S(1)} %collective-permute-done.23, f32[1536,1024]{1,0:T(8,128)S(1)} %bitcast.58, f16[256,1024]{1,0:T(8,128)(2,1)S(1)} %collective-permute-done.22, f16[256,1024]{1,0:T(8,128)(2,1)} %collective-permute-done.18, ...), kind=kLoop, calls=%fused_computation.18 | loop fusion | flops 2621440 | bytes 3670536 | tf_op jit(solution)/shard_map/dynamic_update_slice | solution.py:130
  (87 shorter events, 0.2 us)
Async XLA Ops:
  0.0 1.5 %copy-start = (bf16[1,896,1024]{2,1,0:T(8,128)(2,1)S(1)}, bf16[1,896,1024]{2,1,0:T(8,128)(2,1)}, u32[]{:S(2)}) copy-start(bf16[1,896,1024]{2,1,0:T(8,128)(2,1)} %param.6) | copy-start | bytes 5505028
  4.0 16.5 %collective-permute-start.1 = (f16[256,1024]{1,0:T(8,128)(2,1)}, f16[256,1024]{1,0:T(8,128)(2,1)S(1)}, u32[]{:S(2)}, u32[]{:S(2)}) collective-permute-start(f16[256,1024]{1,0:T(8,128)(2,1)} %fusion.15), channel_id=1, source_target_pairs={{0,1},{1,0},{2,3},{3,2},{4,5},{5,4},{6,7},{7,6},{8,9},{9,8},{10,11... | collective-permute-start | bytes 1572872 | tf_op jit(solution)/shard_map/ppermute | solution.py:21
  15.4 20.2 %collective-permute-start.3 = (f16[256,1024]{1,0:T(8,128)(2,1)}, f16[256,1024]{1,0:T(8,128)(2,1)S(1)}, u32[]{:S(2)}, u32[]{:S(2)}) collective-permute-start(f16[256,1024]{1,0:T(8,128)(2,1)} %get-tuple-element.156), channel_id=1, source_target_pairs={{0,1},{1,0},{2,3},{3,2},{4,5},{5,4},{6,7},{7,6},{8,9},{9,8},{10,11... | collective-permute-start | bytes 1572872 | tf_op jit(solution)/shard_map/ppermute | solution.py:21
  15.4 27.1 %collective-permute-start = (f16[256,1024]{1,0:T(8,128)(2,1)}, f16[256,1024]{1,0:T(8,128)(2,1)S(1)}, u32[]{:S(2)}, u32[]{:S(2)}) collective-permute-start(f16[256,1024]{1,0:T(8,128)(2,1)} %get-tuple-element.157), channel_id=1, source_target_pairs={{0,1},{1,0},{2,3},{3,2},{4,5},{5,4},{6,7},{7,6},{8,9},{9,8},{10,11... | collective-permute-start | bytes 1572872 | tf_op jit(solution)/shard_map/ppermute | solution.py:21
  20.6 1.3 %copy-start.2 = (f32[512,1024]{1,0:T(8,128)}, f32[512,1024]{1,0:T(8,128)S(1)}, u32[]{:S(2)}) copy-start(f32[512,1024]{1,0:T(8,128)S(1)} %bitcast_subtract_fusion.1) | copy-start | bytes 6291460
  23.0 12.6 %collective-permute-start.4 = (f16[256,1024]{1,0:T(8,128)(2,1)}, f16[256,1024]{1,0:T(8,128)(2,1)}, u32[]{:S(2)}, u32[]{:S(2)}) collective-permute-start(f16[256,1024]{1,0:T(8,128)(2,1)} %multiply_convert_fusion.8), channel_id=1, source_target_pairs={{0,2},{2,0},{4,6},{6,4},{8,10},{10,8},{12,14},{14,12},{16,18},{18,... | collective-permute-start | bytes 1572872 | tf_op jit(solution)/shard_map/ppermute | solution.py:30
  23.0 19.5 %collective-permute-start.2 = (f16[256,1024]{1,0:T(8,128)(2,1)}, f16[256,1024]{1,0:T(8,128)(2,1)}, u32[]{:S(2)}, u32[]{:S(2)}) collective-permute-start(f16[256,1024]{1,0:T(8,128)(2,1)} %multiply_convert_fusion.8), channel_id=1, source_target_pairs={{2,4},{4,2},{6,8},{8,6},{10,12},{12,10},{14,16},{16,14},{18,20},{2... | collective-permute-start | bytes 1572872 | tf_op jit(solution)/shard_map/ppermute | solution.py:30
  27.6 8.0 %copy-start.3 = (f32[512,1024]{1,0:T(8,128)S(1)}, f32[512,1024]{1,0:T(8,128)}, u32[]{:S(2)}) copy-start(f32[512,1024]{1,0:T(8,128)} %copy-done.2) | copy-start | bytes 6291460
  27.6 8.3 %copy-start.17 = (f16[256,1024]{1,0:T(8,128)(2,1)S(1)}, f16[256,1024]{1,0:T(8,128)(2,1)}, u32[]{:S(2)}) copy-start(f16[256,1024]{1,0:T(8,128)(2,1)} %get-tuple-element.99) | copy-start | bytes 1572868
  27.6 15.6 %copy-start.16 = (f16[256,1024]{1,0:T(8,128)(2,1)S(1)}, f16[256,1024]{1,0:T(8,128)(2,1)}, u32[]{:S(2)}) copy-start(f16[256,1024]{1,0:T(8,128)(2,1)} %get-tuple-element.107) | copy-start | bytes 1572868
  35.5 53.7 %copy-start.1 = (f32[1536,1024]{1,0:T(8,128)}, f32[1536,1024]{1,0:T(8,128)S(1)}, u32[]{:S(2)}) copy-start(f32[1536,1024]{1,0:T(8,128)S(1)} %bitcast_subtract_fusion) | copy-start | bytes 18874372
  35.6 19.3 %copy-start.15 = (f16[256,1024]{1,0:T(8,128)(2,1)S(1)}, f16[256,1024]{1,0:T(8,128)(2,1)}, u32[]{:S(2)}) copy-start(f16[256,1024]{1,0:T(8,128)(2,1)} %get-tuple-element.115) | copy-start | bytes 1572868
  35.6 30.5 %copy-start.14 = (f16[256,1024]{1,0:T(8,128)(2,1)S(1)}, f16[256,1024]{1,0:T(8,128)(2,1)}, u32[]{:S(2)}) copy-start(f16[256,1024]{1,0:T(8,128)(2,1)} %get-tuple-element.123) | copy-start | bytes 1572868
  35.6 53.8 %copy-start.36 = (s32[16,3]{0,1:T(4,128)S(1)}, s32[16,3]{0,1:T(4,128)}, u32[]{:S(2)}) copy-start(s32[16,3]{0,1:T(4,128)} %param.7) | copy-start | bytes 580
  35.9 6.6 %collective-permute-start.5 = (f16[256,1024]{1,0:T(8,128)(2,1)S(1)}, f16[256,1024]{1,0:T(8,128)(2,1)S(1)}, u32[]{:S(2)}, u32[]{:S(2)}) collective-permute-start(f16[256,1024]{1,0:T(8,128)(2,1)S(1)} %multiply_convert_fusion.7), channel_id=1, source_target_pairs={{0,2},{2,0},{4,6},{6,4},{8,10},{10,8},{12,14},{14,12},{16,18},{18,... | collective-permute-start | bytes 1572872 | tf_op jit(solution)/shard_map/ppermute | solution.py:30
  35.9 17.7 %collective-permute-start.6 = (f16[256,1024]{1,0:T(8,128)(2,1)S(1)}, f16[256,1024]{1,0:T(8,128)(2,1)S(1)}, u32[]{:S(2)}, u32[]{:S(2)}) collective-permute-start(f16[256,1024]{1,0:T(8,128)(2,1)S(1)} %copy-done.17), channel_id=1, source_target_pairs={{0,1},{1,0},{2,3},{3,2},{4,5},{5,4},{6,7},{7,6},{8,9},{9,8},{10,11... | collective-permute-start | bytes 1572872 | tf_op jit(solution)/shard_map/ppermute | solution.py:21
  36.5 17.2 %collective-permute-start.7 = (f16[256,1024]{1,0:T(8,128)(2,1)S(1)}, f16[256,1024]{1,0:T(8,128)(2,1)S(1)}, u32[]{:S(2)}, u32[]{:S(2)}) collective-permute-start(f16[256,1024]{1,0:T(8,128)(2,1)S(1)} %multiply_convert_fusion.7), channel_id=1, source_target_pairs={{2,4},{4,2},{6,8},{8,6},{10,12},{12,10},{14,16},{16,14},{18,20},{2... | collective-permute-start | bytes 1572872 | tf_op jit(solution)/shard_map/ppermute | solution.py:30
  42.4 0.8 copy-start.18
  43.2 10.4 %collective-permute-start.8 = (f16[256,1024]{1,0:T(8,128)(2,1)S(1)}, f16[256,1024]{1,0:T(8,128)(2,1)S(1)}, u32[]{:S(2)}, u32[]{:S(2)}) collective-permute-start(f16[256,1024]{1,0:T(8,128)(2,1)S(1)} %multiply_convert_fusion.6), channel_id=1, source_target_pairs={{0,2},{2,0},{4,6},{6,4},{8,10},{10,8},{12,14},{14,12},{16,18},{18,... | collective-permute-start | bytes 1572872 | tf_op jit(solution)/shard_map/ppermute | solution.py:30
  43.3 21.7 %collective-permute-start.9 = (f16[256,1024]{1,0:T(8,128)(2,1)S(1)}, f16[256,1024]{1,0:T(8,128)(2,1)S(1)}, u32[]{:S(2)}, u32[]{:S(2)}) collective-permute-start(f16[256,1024]{1,0:T(8,128)(2,1)S(1)} %copy-done.16), channel_id=1, source_target_pairs={{0,1},{1,0},{2,3},{3,2},{4,5},{5,4},{6,7},{7,6},{8,9},{9,8},{10,11... | collective-permute-start | bytes 1572872 | tf_op jit(solution)/shard_map/ppermute | solution.py:21
  45.3 19.6 %collective-permute-start.10 = (f16[256,1024]{1,0:T(8,128)(2,1)S(1)}, f16[256,1024]{1,0:T(8,128)(2,1)S(1)}, u32[]{:S(2)}, u32[]{:S(2)}) collective-permute-start(f16[256,1024]{1,0:T(8,128)(2,1)S(1)} %multiply_convert_fusion.6), channel_id=1, source_target_pairs={{2,4},{4,2},{6,8},{8,6},{10,12},{12,10},{14,16},{16,14},{18,20},{2... | collective-permute-start | bytes 1572872 | tf_op jit(solution)/shard_map/ppermute | solution.py:30
  53.7 0.8 copy-start.6
  53.7 35.6 %copy-start.20 = (f16[256,1024]{1,0:T(8,128)(2,1)}, f16[256,1024]{1,0:T(8,128)(2,1)S(1)}, u32[]{:S(2)}) copy-start(f16[256,1024]{1,0:T(8,128)(2,1)S(1)} %collective-permute-done.7) | copy-start | bytes 1572868
  54.5 34.8 %copy-start.22 = (f16[256,1024]{1,0:T(8,128)(2,1)}, f16[256,1024]{1,0:T(8,128)(2,1)S(1)}, u32[]{:S(2)}) copy-start(f16[256,1024]{1,0:T(8,128)(2,1)S(1)} %collective-permute-done.8) | copy-start | bytes 1572868
  54.7 10.2 %collective-permute-start.11 = (f16[256,1024]{1,0:T(8,128)(2,1)S(1)}, f16[256,1024]{1,0:T(8,128)(2,1)S(1)}, u32[]{:S(2)}, u32[]{:S(2)}) collective-permute-start(f16[256,1024]{1,0:T(8,128)(2,1)S(1)} %multiply_convert_fusion.5), channel_id=1, source_target_pairs={{0,2},{2,0},{4,6},{6,4},{8,10},{10,8},{12,14},{14,12},{16,18},{18,... | collective-permute-start | bytes 1572872 | tf_op jit(solution)/shard_map/ppermute | solution.py:30
  54.8 21.3 %collective-permute-start.12 = (f16[256,1024]{1,0:T(8,128)(2,1)S(1)}, f16[256,1024]{1,0:T(8,128)(2,1)S(1)}, u32[]{:S(2)}, u32[]{:S(2)}) collective-permute-start(f16[256,1024]{1,0:T(8,128)(2,1)S(1)} %copy-done.15), channel_id=1, source_target_pairs={{0,1},{1,0},{2,3},{3,2},{4,5},{5,4},{6,7},{7,6},{8,9},{9,8},{10,11... | collective-permute-start | bytes 1572872 | tf_op jit(solution)/shard_map/ppermute | solution.py:21
  58.6 17.5 %collective-permute-start.13 = (f16[256,1024]{1,0:T(8,128)(2,1)S(1)}, f16[256,1024]{1,0:T(8,128)(2,1)S(1)}, u32[]{:S(2)}, u32[]{:S(2)}) collective-permute-start(f16[256,1024]{1,0:T(8,128)(2,1)S(1)} %multiply_convert_fusion.5), channel_id=1, source_target_pairs={{2,4},{4,2},{6,8},{8,6},{10,12},{12,10},{14,16},{16,14},{18,20},{2... | collective-permute-start | bytes 1572872 | tf_op jit(solution)/shard_map/ppermute | solution.py:30
  64.9 0.8 copy-start.8
  64.9 24.3 %copy-start.24 = (f16[256,1024]{1,0:T(8,128)(2,1)}, f16[256,1024]{1,0:T(8,128)(2,1)S(1)}, u32[]{:S(2)}) copy-start(f16[256,1024]{1,0:T(8,128)(2,1)S(1)} %collective-permute-done.10) | copy-start | bytes 1572868
  65.7 23.6 %copy-start.26 = (f16[256,1024]{1,0:T(8,128)(2,1)}, f16[256,1024]{1,0:T(8,128)(2,1)S(1)}, u32[]{:S(2)}) copy-start(f16[256,1024]{1,0:T(8,128)(2,1)S(1)} %collective-permute-done.11) | copy-start | bytes 1572868
  65.9 10.2 %collective-permute-start.14 = (f16[256,1024]{1,0:T(8,128)(2,1)S(1)}, f16[256,1024]{1,0:T(8,128)(2,1)S(1)}, u32[]{:S(2)}, u32[]{:S(2)}) collective-permute-start(f16[256,1024]{1,0:T(8,128)(2,1)S(1)} %multiply_convert_fusion.4), channel_id=1, source_target_pairs={{0,2},{2,0},{4,6},{6,4},{8,10},{10,8},{12,14},{14,12},{16,18},{18,... | collective-permute-start | bytes 1572872 | tf_op jit(solution)/shard_map/ppermute | solution.py:30
  66.0 21.3 %collective-permute-start.15 = (f16[256,1024]{1,0:T(8,128)(2,1)S(1)}, f16[256,1024]{1,0:T(8,128)(2,1)S(1)}, u32[]{:S(2)}, u32[]{:S(2)}) collective-permute-start(f16[256,1024]{1,0:T(8,128)(2,1)S(1)} %copy-done.14), channel_id=1, source_target_pairs={{0,1},{1,0},{2,3},{3,2},{4,5},{5,4},{6,7},{7,6},{8,9},{9,8},{10,11... | collective-permute-start | bytes 1572872 | tf_op jit(solution)/shard_map/ppermute | solution.py:21
  68.2 19.2 %collective-permute-start.16 = (f16[256,1024]{1,0:T(8,128)(2,1)S(1)}, f16[256,1024]{1,0:T(8,128)(2,1)S(1)}, u32[]{:S(2)}, u32[]{:S(2)}) collective-permute-start(f16[256,1024]{1,0:T(8,128)(2,1)S(1)} %multiply_convert_fusion.4), channel_id=1, source_target_pairs={{2,4},{4,2},{6,8},{8,6},{10,12},{12,10},{14,16},{16,14},{18,20},{2... | collective-permute-start | bytes 1572872 | tf_op jit(solution)/shard_map/ppermute | solution.py:30
  76.1 0.8 copy-start.10
  76.2 13.1 %copy-start.28 = (f16[256,1024]{1,0:T(8,128)(2,1)}, f16[256,1024]{1,0:T(8,128)(2,1)S(1)}, u32[]{:S(2)}) copy-start(f16[256,1024]{1,0:T(8,128)(2,1)S(1)} %collective-permute-done.13) | copy-start | bytes 1572868
  77.0 12.3 %copy-start.30 = (f16[256,1024]{1,0:T(8,128)(2,1)}, f16[256,1024]{1,0:T(8,128)(2,1)S(1)}, u32[]{:S(2)}) copy-start(f16[256,1024]{1,0:T(8,128)(2,1)S(1)} %collective-permute-done.14) | copy-start | bytes 1572868
  78.0 9.4 %collective-permute-start.17 = (f16[256,1024]{1,0:T(8,128)(2,1)}, f16[256,1024]{1,0:T(8,128)(2,1)S(1)}, u32[]{:S(2)}, u32[]{:S(2)}) collective-permute-start(f16[256,1024]{1,0:T(8,128)(2,1)} %multiply_convert_fusion.3), channel_id=1, source_target_pairs={{0,2},{2,0},{4,6},{6,4},{8,10},{10,8},{12,14},{14,12},{16,18},{18,... | collective-permute-start | bytes 1572872 | tf_op jit(solution)/shard_map/ppermute | solution.py:30
  78.0 19.9 %collective-permute-start.18 = (f16[256,1024]{1,0:T(8,128)(2,1)}, f16[256,1024]{1,0:T(8,128)(2,1)}, u32[]{:S(2)}, u32[]{:S(2)}) collective-permute-start(f16[256,1024]{1,0:T(8,128)(2,1)} %get-tuple-element.129), channel_id=1, source_target_pairs={{0,1},{1,0},{2,3},{3,2},{4,5},{5,4},{6,7},{7,6},{8,9},{9,8},{10,11... | collective-permute-start | bytes 1572872 | tf_op jit(solution)/shard_map/ppermute | solution.py:21
  82.0 15.9 %collective-permute-start.19 = (f16[256,1024]{1,0:T(8,128)(2,1)}, f16[256,1024]{1,0:T(8,128)(2,1)}, u32[]{:S(2)}, u32[]{:S(2)}) collective-permute-start(f16[256,1024]{1,0:T(8,128)(2,1)} %multiply_convert_fusion.3), channel_id=1, source_target_pairs={{2,4},{4,2},{6,8},{8,6},{10,12},{12,10},{14,16},{16,14},{18,20},{2... | collective-permute-start | bytes 1572872 | tf_op jit(solution)/shard_map/ppermute | solution.py:30
  87.4 0.8 copy-start.12
  87.4 1.9 %copy-start.32 = (f16[256,1024]{1,0:T(8,128)(2,1)}, f16[256,1024]{1,0:T(8,128)(2,1)S(1)}, u32[]{:S(2)}) copy-start(f16[256,1024]{1,0:T(8,128)(2,1)S(1)} %collective-permute-done.16) | copy-start | bytes 1572868
  88.2 1.1 copy-start.34
  89.3 8.6 %collective-permute-start.20 = (f16[256,1024]{1,0:T(8,128)(2,1)}, f16[256,1024]{1,0:T(8,128)(2,1)}, u32[]{:S(2)}, u32[]{:S(2)}) collective-permute-start(f16[256,1024]{1,0:T(8,128)(2,1)} %multiply_convert_fusion.2), channel_id=1, source_target_pairs={{0,2},{2,0},{4,6},{6,4},{8,10},{10,8},{12,14},{14,12},{16,18},{18,... | collective-permute-start | bytes 1572872 | tf_op jit(solution)/shard_map/ppermute | solution.py:30
  92.6 22.9 %collective-permute-start.21 = (f16[256,1024]{1,0:T(8,128)(2,1)}, f16[256,1024]{1,0:T(8,128)(2,1)S(1)}, u32[]{:S(2)}, u32[]{:S(2)}) collective-permute-start(f16[256,1024]{1,0:T(8,128)(2,1)} %multiply_convert_fusion.2), channel_id=1, source_target_pairs={{2,4},{4,2},{6,8},{8,6},{10,12},{12,10},{14,16},{16,14},{18,20},{2... | collective-permute-start | bytes 1572872 | tf_op jit(solution)/shard_map/ppermute | solution.py:30
  99.5 18.1 %collective-permute-start.22 = (f16[256,1024]{1,0:T(8,128)(2,1)S(1)}, f16[256,1024]{1,0:T(8,128)(2,1)S(1)}, u32[]{:S(2)}, u32[]{:S(2)}) collective-permute-start(f16[256,1024]{1,0:T(8,128)(2,1)S(1)} %multiply_convert_fusion.1), channel_id=1, source_target_pairs={{0,2},{2,0},{4,6},{6,4},{8,10},{10,8},{12,14},{14,12},{16,18},{18,... | collective-permute-start | bytes 1572872 | tf_op jit(solution)/shard_map/ppermute | solution.py:30
  99.6 18.0 %collective-permute-start.23 = (f16[256,1024]{1,0:T(8,128)(2,1)S(1)}, f16[256,1024]{1,0:T(8,128)(2,1)S(1)}, u32[]{:S(2)}, u32[]{:S(2)}) collective-permute-start(f16[256,1024]{1,0:T(8,128)(2,1)S(1)} %multiply_convert_fusion.1), channel_id=1, source_target_pairs={{2,4},{4,2},{6,8},{8,6},{10,12},{12,10},{14,16},{16,14},{18,20},{2... | collective-permute-start | bytes 1572872 | tf_op jit(solution)/shard_map/ppermute | solution.py:30
  104.4 4.2 %copy-start.4 = (f32[512,1024]{1,0:T(8,128)S(1)}, f32[512,1024]{1,0:T(8,128)}, u32[]{:S(2)}) copy-start(f32[512,1024]{1,0:T(8,128)} %copy-done.2) | copy-start | bytes 6291460
  104.4 4.2 %copy-start.19 = (f16[256,1024]{1,0:T(8,128)(2,1)S(1)}, f16[256,1024]{1,0:T(8,128)(2,1)}, u32[]{:S(2)}) copy-start(f16[256,1024]{1,0:T(8,128)(2,1)} %copy-done.18) | copy-start | bytes 1572868
  104.4 4.2 %copy-start.21 = (f16[256,1024]{1,0:T(8,128)(2,1)S(1)}, f16[256,1024]{1,0:T(8,128)(2,1)}, u32[]{:S(2)}) copy-start(f16[256,1024]{1,0:T(8,128)(2,1)} %copy-done.20) | copy-start | bytes 1572868
  104.4 5.5 %slice-start = ((s8[6291456]{0:T(1024)(128)(4,1)}), s8[4194304]{0:T(1024)(128)(4,1)S(1)}, s32[]{:S(2)}) async-start(s8[6291456]{0:T(1024)(128)(4,1)} %bitcast.57), calls=%async_computation | async-start | bytes 8388608
  107.5 2.4 %slice-start.1 = ((s8[6291456]{0:T(1024)(128)(4,1)}), s8[2097152]{0:T(1024)(128)(4,1)S(1)}, s32[]{:S(2)}) async-start(s8[6291456]{0:T(1024)(128)(4,1)} %bitcast.57), calls=%async_computation.1 | async-start | bytes 4194304
  107.5 2.4 %copy-start.23 = (f16[256,1024]{1,0:T(8,128)(2,1)S(1)}, f16[256,1024]{1,0:T(8,128)(2,1)}, u32[]{:S(2)}) copy-start(f16[256,1024]{1,0:T(8,128)(2,1)} %copy-done.22) | copy-start | bytes 1572868
  107.5 2.4 %copy-start.25 = (f16[256,1024]{1,0:T(8,128)(2,1)S(1)}, f16[256,1024]{1,0:T(8,128)(2,1)}, u32[]{:S(2)}) copy-start(f16[256,1024]{1,0:T(8,128)(2,1)} %copy-done.24) | copy-start | bytes 1572868
  107.5 3.6 %copy-start.7 = (f16[256,1024]{1,0:T(8,128)(2,1)S(1)}, f16[256,1024]{1,0:T(8,128)(2,1)}, u32[]{:S(2)}) copy-start(f16[256,1024]{1,0:T(8,128)(2,1)} %copy-done.6) | copy-start | bytes 1572868
  107.6 3.6 %copy-start.27 = (f16[256,1024]{1,0:T(8,128)(2,1)S(1)}, f16[256,1024]{1,0:T(8,128)(2,1)}, u32[]{:S(2)}) copy-start(f16[256,1024]{1,0:T(8,128)(2,1)} %copy-done.26) | copy-start | bytes 1572868
  107.6 3.6 %copy-start.29 = (f16[256,1024]{1,0:T(8,128)(2,1)S(1)}, f16[256,1024]{1,0:T(8,128)(2,1)}, u32[]{:S(2)}) copy-start(f16[256,1024]{1,0:T(8,128)(2,1)} %copy-done.28) | copy-start | bytes 1572868
  108.7 3.6 %copy-start.9 = (f16[256,1024]{1,0:T(8,128)(2,1)S(1)}, f16[256,1024]{1,0:T(8,128)(2,1)}, u32[]{:S(2)}) copy-start(f16[256,1024]{1,0:T(8,128)(2,1)} %copy-done.8) | copy-start | bytes 1572868
  108.7 3.6 %copy-start.31 = (f16[256,1024]{1,0:T(8,128)(2,1)S(1)}, f16[256,1024]{1,0:T(8,128)(2,1)}, u32[]{:S(2)}) copy-start(f16[256,1024]{1,0:T(8,128)(2,1)} %copy-done.30) | copy-start | bytes 1572868
  108.7 3.6 %copy-start.33 = (f16[256,1024]{1,0:T(8,128)(2,1)S(1)}, f16[256,1024]{1,0:T(8,128)(2,1)}, u32[]{:S(2)}) copy-start(f16[256,1024]{1,0:T(8,128)(2,1)} %copy-done.32) | copy-start | bytes 1572868
  110.0 3.4 %copy-start.11 = (f16[256,1024]{1,0:T(8,128)(2,1)S(1)}, f16[256,1024]{1,0:T(8,128)(2,1)}, u32[]{:S(2)}) copy-start(f16[256,1024]{1,0:T(8,128)(2,1)} %copy-done.10) | copy-start | bytes 1572868
  110.0 3.4 %copy-start.35 = (f16[256,1024]{1,0:T(8,128)(2,1)S(1)}, f16[256,1024]{1,0:T(8,128)(2,1)}, u32[]{:S(2)}) copy-start(f16[256,1024]{1,0:T(8,128)(2,1)} %copy-done.34) | copy-start | bytes 1572868
  111.2 4.3 %copy-start.13 = (f16[256,1024]{1,0:T(8,128)(2,1)S(1)}, f16[256,1024]{1,0:T(8,128)(2,1)}, u32[]{:S(2)}) copy-start(f16[256,1024]{1,0:T(8,128)(2,1)} %copy-done.12) | copy-start | bytes 1572868
  117.5 3.4 %copy-start.5 = (f32[1,2048,1024]{2,1,0:T(8,128)}, f32[1,2048,1024]{2,1,0:T(8,128)S(1)}, u32[]{:S(2)}) copy-start(f32[1,2048,1024]{2,1,0:T(8,128)S(1)} %bitcast_dynamic-update-slice_fusion.1) | copy-start | bytes 25165828

commit v10 on v9

--- a/solution.py
+++ b/solution.py
@@ -13,6 +13,8 @@
 AHEAD = 3
 LAG = 2
 NLAG = 1
+MIXLAG = 3
+EARLY = 1
 
 
 def from_behind(value, axis, steps):
@@ -90,13 +92,26 @@
     split = min(2, chunks)
     near = {}
     far = {}
-    terms = {0: for_others(shard, 0, step)}
-    arrived = {0: send_terms(terms[0])}
-    rest = for_others(shard, step, rows - step) if chunks > 1 else []
-    for chunk in range(1, chunks):
-        terms[chunk] = [rows_of(term, chunk - 1) for term in rest]
-    for chunk in range(1, min(AHEAD, chunks)):
-        arrived[chunk] = send_terms(terms[chunk])
+    out = jnp.zeros_like(weights)
+    mixed = 0
+
+    def mix_into(out, chunk):
+        value = (
+            c_near * near[chunk].astype(jnp.float32)
+            + c_self * u_of(chunk)
+            + c_far * far[chunk].astype(jnp.float32)
+        )
+        return lax.dynamic_update_slice_in_dim(out, value, chunk * step, axis=0)
+
+    early = min(EARLY, chunks)
+    terms = {chunk: for_others(shard, chunk * step, step) for chunk in range(early)}
+    arrived = {chunk: send_terms(terms[chunk]) for chunk in range(min(AHEAD, early))}
+    if early < chunks:
+        rest = for_others(shard, early * step, rows - early * step)
+        for after in range(early, chunks):
+            terms[after] = [rows_of(term, after - early) for term in rest]
+        for after in range(early, min(AHEAD, chunks)):
+            arrived[after] = send_terms(terms[after])
     base = [own_part(shard, 0, split)]
 
     arrived[0], base, terms = lax.optimization_barrier((arrived[0], base, terms))
@@ -107,27 +122,24 @@
             arrived[chunk], far[chunk - LAG] = lax.optimization_barrier((arrived[chunk], far[chunk - LAG]))
         if chunk >= NLAG:
             arrived[chunk], near[chunk - NLAG] = lax.optimization_barrier((arrived[chunk], near[chunk - NLAG]))
+        if mixed:
+            arrived[chunk], out = lax.optimization_barrier((arrived[chunk], out))
         sent = (u_of(chunk) * scale).astype(WIRE)
-        sent, base, later = lax.optimization_barrier((sent, base, shard))
+        sent, base, out, later = lax.optimization_barrier((sent, base, out, shard))
         if chunk == 0 and split < chunks:
             base.append(own_part(later, split, chunks - split))
         after = chunk + AHEAD
         if after < chunks:
             terms[after], sent = lax.optimization_barrier((terms[after], sent))
             arrived[after] = send_terms(terms[after])
-        if chunk == chunks - 1:
-            far[0], near[0], sent = lax.optimization_barrier((far[0], near[0], sent))
         far[chunk] = swapped(sent, "blk", 1)
         near[chunk] = swapped(sent, "blk", 0)
+        if chunk >= MIXLAG:
+            out = mix_into(out, mixed)
+            mixed += 1
 
-    out = jnp.zeros_like(weights)
-    for chunk in range(chunks):
-        mixed = (
-            c_near * near[chunk].astype(jnp.float32)
-            + c_self * u_of(chunk)
-            + c_far * far[chunk].astype(jnp.float32)
-        )
-        out = lax.dynamic_update_slice_in_dim(out, mixed, chunk * step, axis=0)
+    for chunk in range(mixed, chunks):
+        out = mix_into(out, chunk)
     return out[None]
 
 

time: 124 us -> 127 us (1.024)
  the two profiles are of different devices: /device:TPU:0 before, /device:TPU:1 now
where the time goes in v10:
time: 127 us; the launch traced here: 126 us
  waiting for transfers between devices  52.8 us (42%)
  other arithmetic  23 us (18%)
  starting transfers between devices  20.9 us (16%)
  matrix products  19.9 us (16%)
  local copies, waits for them, and re-layouts  6.84 us (5%)
  between operations  2.72 us (2%)
    ppermute x16, waiting for transfers between devices, swapped(): return lax.ppermute(value, axis, pairs)  31.9 us
    ppermute x8, waiting for transfers between devices, from_behind(): return lax.ppermute(value, axis, pairs)  20.9 us
    dot_general x4, matrix products, partial(): lax.dot_general(block, cot_local, (((0,), (0,)), ((), ())), preferred_ele...  19.8 us
    dynamic_update_slice x8, other arithmetic, mix_into(): return lax.dynamic_update_slice_in_dim(out, value, chunk * step, axis=0)  15.2 us
    ppermute x16, starting transfers between devices, swapped(): return lax.ppermute(value, axis, pairs)  13.5 us
    convert_element_type x8, other arithmetic, on_device(): sent = (u_of(chunk) * scale).astype(WIRE)  7.81 us
    ppermute x8, starting transfers between devices, from_behind(): return lax.ppermute(value, axis, pairs)  7.37 us
    unnamed x30, local copies, waits for them, and re-layouts  2.9 us
  transfers between devices with their start and end apart: 24, of which 9 were waited for; matrix products, arithmetic and copies ran while one was open for 34% of the time, Pallas kernels for 0%

profile of v10, /device:TPU:1, one launch (start us, length us, event | category | flops | bytes accessed | tf_op | source)
XLA Modules:
  0.0 126.1 jit_solution(14941903241191224173)
XLA Ops:
  0.0 1.5 %copy-done = bf16[1,896,1024]{2,1,0:T(8,128)(2,1)S(1)} copy-done((bf16[1,896,1024]{2,1,0:T(8,128)(2,1)S(1)}, bf16[1,896,1024]{2,1,0:T(8,128)(2,1)}, u32[]{:S(2)}) %copy-start) | copy-done | bytes 1835032
  1.5 2.5 %fusion.15 = f16[256,1024]{1,0:T(8,128)(2,1)} fusion(bf16[1,896,1024]{2,1,0:T(8,128)(2,1)S(1)} %copy-done, bf16[1,896,4096]{2,1,0:T(8,128)(2,1)} %param.5, s32[]{:T(128)S(6)} %select_n.32), kind=kOutput, calls=%fused_computation.14 | convolution fusion | flops 470286336 | bytes 2818052 | tf_op jit(solution)/shard_map/dot_general | solution.py:60
  4.0 2.1 %collective-permute-start.1 = (f16[256,1024]{1,0:T(8,128)(2,1)}, f16[256,1024]{1,0:T(8,128)(2,1)S(1)}, u32[]{:S(2)}, u32[]{:S(2)}) collective-permute-start(f16[256,1024]{1,0:T(8,128)(2,1)} %fusion.15), channel_id=1, source_target_pairs={{0,1},{1,0},{2,3},{3,2},{4,5},{5,4},{6,7},{7,6},{8,9},{9,8},{10,11... | collective-permute-start | bytes 1572872 | tf_op jit(solution)/shard_map/ppermute | solution.py:23
  6.1 6.2 %multiply_convert_fusion = f16[1792,1024]{1,0:T(8,128)(2,1)S(1)} fusion(bf16[1,896,4096]{2,1,0:T(8,128)(2,1)} %param.5, s32[]{:T(128)S(6)} %select_n.31, bf16[1,896,1024]{2,1,0:T(8,128)(2,1)S(1)} %copy-done), kind=kOutput, calls=%fused_computation | convolution fusion | flops 3292004352 | bytes 8716292 | tf_op jit(solution)/shard_map/dot_general | solution.py:60
  12.3 2.3 %fusion.32 = (f16[256,1024]{1,0:T(8,128)(2,1)}, f16[256,1024]{1,0:T(8,128)(2,1)}, f16[256,1024]{1,0:T(8,128)(2,1)}, f16[256,1024]{1,0:T(8,128)(2,1)}, f16[256,10...) fusion(f16[1792,1024]{1,0:T(8,128)(2,1)S(1)} %multiply_convert_fusion), kind=kLoop, calls=%fused_computation.54 | loop fusion | bytes 7340032 | tf_op jit(solution)/shard_map/slice | solution.py:78
  14.5 0.0 collective-permute-start
  14.5 1.5 %collective-permute-start.3 = (f16[256,1024]{1,0:T(8,128)(2,1)}, f16[256,1024]{1,0:T(8,128)(2,1)S(1)}, u32[]{:S(2)}, u32[]{:S(2)}) collective-permute-start(f16[256,1024]{1,0:T(8,128)(2,1)} %get-tuple-element.176), channel_id=1, source_target_pairs={{0,1},{1,0},{2,3},{3,2},{4,5},{5,4},{6,7},{7,6},{8,9},{9,8},{10,11... | collective-permute-start | bytes 1572872 | tf_op jit(solution)/shard_map/ppermute | solution.py:23
  16.0 3.2 %bitcast_subtract_fusion.1 = f32[512,1024]{1,0:T(8,128)S(1)} fusion(f32[1,2048,1024]{2,1,0:T(8,128)} %param.4, bf16[1,896,1024]{2,1,0:T(8,128)(2,1)S(1)} %copy-done, bf16[1,896,4096]{2,1,0:T(8,128)(2,1)} %param.5, s32[]{:T(128)S(6)} %select_n.33), kind=kOutput, calls=%fused_computation.6 | convolution fusion | flops 940572672 | bytes 6946820 | tf_op jit(solution)/shard_map/dot_general | solution.py:60
  19.2 1.3 %copy-done.2 = f32[512,1024]{1,0:T(8,128)} copy-done((f32[512,1024]{1,0:T(8,128)}, f32[512,1024]{1,0:T(8,128)S(1)}, u32[]{:S(2)}) %copy-start.2) | copy-done | bytes 2097176
  20.5 1.0 multiply_convert_fusion.8
  21.6 1.5 %collective-permute-start.2 = (f16[256,1024]{1,0:T(8,128)(2,1)}, f16[256,1024]{1,0:T(8,128)(2,1)}, u32[]{:S(2)}, u32[]{:S(2)}) collective-permute-start(f16[256,1024]{1,0:T(8,128)(2,1)} %multiply_convert_fusion.8), channel_id=1, source_target_pairs={{0,2},{2,0},{4,6},{6,4},{8,10},{10,8},{12,14},{14,12},{16,18},{18,... | collective-permute-start | bytes 1572872 | tf_op jit(solution)/shard_map/ppermute | solution.py:32
  23.1 1.1 collective-permute-start.4
  24.2 7.9 %bitcast_subtract_fusion = f32[1536,1024]{1,0:T(8,128)S(1)} fusion(f32[1,2048,1024]{2,1,0:T(8,128)} %param.4, bf16[1,896,4096]{2,1,0:T(8,128)(2,1)} %param.5, s32[]{:T(128)S(6)} %select_n.34, bf16[1,896,1024]{2,1,0:T(8,128)(2,1)S(1)} %copy-done), kind=kOutput, calls=%fused_computation.1 | convolution fusion | flops 2821718016 | bytes 17170436 | tf_op jit(solution)/shard_map/dot_general | solution.py:60
  32.1 0.0 copy-start.1
  32.1 0.0 copy-start.12
  32.2 0.0 collective-permute-done.2
  32.2 1.3 %multiply_convert_fusion.7 = f16[256,1024]{1,0:T(8,128)(2,1)} fusion(f16[256,1024]{1,0:T(8,128)(2,1)S(1)} %collective-permute-done, f32[512,1024]{1,0:T(8,128)S(1)} %copy-done.3), kind=kLoop, calls=%fused_computation.37 | loop fusion | flops 1310720 | bytes 2097152 | tf_op jit(solution)/shard_map/convert_element_type | solution.py:127
  33.5 3.6 %collective-permute-start.5 = (f16[256,1024]{1,0:T(8,128)(2,1)}, f16[256,1024]{1,0:T(8,128)(2,1)S(1)}, u32[]{:S(2)}, u32[]{:S(2)}) collective-permute-start(f16[256,1024]{1,0:T(8,128)(2,1)} %multiply_convert_fusion.7), channel_id=1, source_target_pairs={{0,2},{2,0},{4,6},{6,4},{8,10},{10,8},{12,14},{14,12},{16,18},{18,... | collective-permute-start | bytes 1572872 | tf_op jit(solution)/shard_map/ppermute | solution.py:32
  37.0 0.2 collective-permute-start.6
  37.2 0.0 collective-permute-start.7
  37.2 3.2 %collective-permute-done.3 = f16[256,1024]{1,0:T(8,128)(2,1)S(1)} collective-permute-done((f16[256,1024]{1,0:T(8,128)(2,1)}, f16[256,1024]{1,0:T(8,128)(2,1)S(1)}, u32[]{:S(2)}, u32[]{:S(2)}) %collective-permute-start.3) | collective-permute-done | bytes 524320 | tf_op jit(solution)/shard_map/ppermute | solution.py:23
  40.4 0.0 collective-permute-done.4
  40.4 0.0 collective-permute-done.5
  40.5 1.0 multiply_convert_fusion.6
  41.5 2.1 %collective-permute-start.8 = (f16[256,1024]{1,0:T(8,128)(2,1)}, f16[256,1024]{1,0:T(8,128)(2,1)}, u32[]{:S(2)}, u32[]{:S(2)}) collective-permute-start(f16[256,1024]{1,0:T(8,128)(2,1)} %multiply_convert_fusion.6), channel_id=1, source_target_pairs={{0,2},{2,0},{4,6},{6,4},{8,10},{10,8},{12,14},{14,12},{16,18},{18,... | collective-permute-start | bytes 1572872 | tf_op jit(solution)/shard_map/ppermute | solution.py:32
  43.6 1.8 %collective-permute-start.9 = (f16[256,1024]{1,0:T(8,128)(2,1)}, f16[256,1024]{1,0:T(8,128)(2,1)}, u32[]{:S(2)}, u32[]{:S(2)}) collective-permute-start(f16[256,1024]{1,0:T(8,128)(2,1)} %get-tuple-element.118), channel_id=1, source_target_pairs={{0,1},{1,0},{2,3},{3,2},{4,5},{5,4},{6,7},{7,6},{8,9},{9,8},{10,11... | collective-permute-start | bytes 1572872 | tf_op jit(solution)/shard_map/ppermute | solution.py:23
  45.3 1.4 %collective-permute-start.10 = (f16[256,1024]{1,0:T(8,128)(2,1)}, f16[256,1024]{1,0:T(8,128)(2,1)}, u32[]{:S(2)}, u32[]{:S(2)}) collective-permute-start(f16[256,1024]{1,0:T(8,128)(2,1)} %multiply_convert_fusion.6), channel_id=1, source_target_pairs={{2,4},{4,2},{6,8},{8,6},{10,12},{12,10},{14,16},{16,14},{18,20},{2... | collective-permute-start | bytes 1572872 | tf_op jit(solution)/shard_map/ppermute | solution.py:32
  46.7 5.1 %collective-permute-done.6 = f16[256,1024]{1,0:T(8,128)(2,1)S(1)} collective-permute-done((f16[256,1024]{1,0:T(8,128)(2,1)}, f16[256,1024]{1,0:T(8,128)(2,1)S(1)}, u32[]{:S(2)}, u32[]{:S(2)}) %collective-permute-start.6) | collective-permute-done | bytes 524320 | tf_op jit(solution)/shard_map/ppermute | solution.py:23
  51.8 5.9 %collective-permute-done.7 = f16[256,1024]{1,0:T(8,128)(2,1)} collective-permute-done((f16[256,1024]{1,0:T(8,128)(2,1)}, f16[256,1024]{1,0:T(8,128)(2,1)}, u32[]{:S(2)}, u32[]{:S(2)}) %collective-permute-start.7) | collective-permute-done | bytes 524320 | tf_op jit(solution)/shard_map/ppermute | solution.py:32
  57.7 2.2 %multiply_convert_fusion.5 = f16[256,1024]{1,0:T(8,128)(2,1)} fusion(f16[256,1024]{1,0:T(8,128)(2,1)S(1)} %collective-permute-done.6, f32[1536,1024]{1,0:T(8,128)} %copy-done.1), kind=kLoop, calls=%fused_computation.33 | loop fusion | flops 1310720 | bytes 2097152 | tf_op jit(solution)/shard_map/convert_element_type | solution.py:127
  59.9 0.1 fusion.18
  60.0 0.6 fusion.33
  63.1 1.3 %collective-permute-start.12 = (f16[256,1024]{1,0:T(8,128)(2,1)}, f16[256,1024]{1,0:T(8,128)(2,1)S(1)}, u32[]{:S(2)}, u32[]{:S(2)}) collective-permute-start(f16[256,1024]{1,0:T(8,128)(2,1)} %get-tuple-element.131), channel_id=1, source_target_pairs={{0,1},{1,0},{2,3},{3,2},{4,5},{5,4},{6,7},{7,6},{8,9},{9,8},{10,11... | collective-permute-start | bytes 1572872 | tf_op jit(solution)/shard_map/ppermute | solution.py:23
  64.4 1.1 broadcast_in_dim.14
  65.5 0.0 slice-start.1
  65.5 2.7 %add_dynamic-update-slice_fusion.3 = f32[2048,1024]{1,0:T(8,128)S(1)} fusion(f32[2048,1024]{1,0:T(8,128)S(1)} %broadcast_in_dim.14, f16[256,1024]{1,0:T(8,128)(2,1)} %collective-permute-done.4, f32[512,1024]{1,0:T(8,128)S(1)} %copy-done.4, f16[256,1024]{1,0:T(8,128)(2,1)} %collective-permute-done.2, f16[256,1024]{1,0:T(8,128)(2,1)S(1)} %copy-done.7, ...), kind=kLoop, calls=%fused_computation.32 | loop fusion | flops 2621440 | bytes 3670028 | tf_op jit(solution)/shard_map/dynamic_update_slice | solution.py:104
  68.2 1.6 %multiply_convert_fusion.4 = f16[256,1024]{1,0:T(8,128)(2,1)S(1)} fusion(f16[256,1024]{1,0:T(8,128)(2,1)} %collective-permute-done.9, f32[1536,1024]{1,0:T(8,128)} %copy-done.1), kind=kLoop, calls=%fused_computation.30 | loop fusion | flops 1310720 | bytes 2097152 | tf_op jit(solution)/shard_map/convert_element_type | solution.py:127
  69.8 1.3 %collective-permute-start.14 = (f16[256,1024]{1,0:T(8,128)(2,1)S(1)}, f16[256,1024]{1,0:T(8,128)(2,1)S(1)}, u32[]{:S(2)}, u32[]{:S(2)}) collective-permute-start(f16[256,1024]{1,0:T(8,128)(2,1)S(1)} %multiply_convert_fusion.4), channel_id=1, source_target_pairs={{0,2},{2,0},{4,6},{6,4},{8,10},{10,8},{12,14},{14,12},{16,18},{18,... | collective-permute-start | bytes 1572872 | tf_op jit(solution)/shard_map/ppermute | solution.py:32
  71.1 0.2 collective-permute-start.15
  71.3 0.9 collective-permute-start.16
  72.2 4.1 %collective-permute-done.12 = f16[256,1024]{1,0:T(8,128)(2,1)S(1)} collective-permute-done((f16[256,1024]{1,0:T(8,128)(2,1)}, f16[256,1024]{1,0:T(8,128)(2,1)S(1)}, u32[]{:S(2)}, u32[]{:S(2)}) %collective-permute-start.12) | collective-permute-done | bytes 524320 | tf_op jit(solution)/shard_map/ppermute | solution.py:23
  76.3 8.4 %collective-permute-done.13 = f16[256,1024]{1,0:T(8,128)(2,1)S(1)} collective-permute-done((f16[256,1024]{1,0:T(8,128)(2,1)}, f16[256,1024]{1,0:T(8,128)(2,1)S(1)}, u32[]{:S(2)}, u32[]{:S(2)}) %collective-permute-start.13) | collective-permute-done | bytes 524320 | tf_op jit(solution)/shard_map/ppermute | solution.py:32
  84.7 2.1 %add_dynamic-update-slice_fusion.2 = f32[2048,1024]{1,0:T(8,128)S(1)} fusion(f32[2048,1024]{1,0:T(8,128)S(1)} %add_dynamic-update-slice_fusion.3, f16[256,1024]{1,0:T(8,128)(2,1)} %collective-permute-done.7, f32[512,1024]{1,0:T(8,128)S(1)} %copy-done.4, f16[256,1024]{1,0:T(8,128)(2,1)S(1)} %copy-done.11, f16[256,1024]{1,0:T(8,128)(2,1)S(1)} %collective-permute-done, ...), kind=kLoop, calls=%fused_computation.29 | loop fusion | flops 2621440 | bytes 3670028 | tf_op jit(solution)/shard_map/dynamic_update_slice | solution.py:104
  86.8 0.2 multiply_convert_fusion.3
  87.0 0.1 collective-permute-start.17
  87.1 0.3 collective-permute-start.18
  87.4 2.2 %add_dynamic-update-slice_fusion.1 = f32[2048,1024]{1,0:T(8,128)S(1)} fusion(f32[2048,1024]{1,0:T(8,128)S(1)} %add_dynamic-update-slice_fusion.2, f16[256,1024]{1,0:T(8,128)(2,1)} %collective-permute-done.10, f32[1536,1024]{1,0:T(8,128)S(1)} %bitcast.51, f16[256,1024]{1,0:T(8,128)(2,1)} %collective-permute-done.8, ...), kind=kLoop, calls=%fused_computation.26 | loop fusion | flops 2621440 | bytes 3670028 | tf_op jit(solution)/shard_map/dynamic_update_slice | solution.py:104
  89.6 0.4 collective-permute-done.16
  90.0 0.2 multiply_convert_fusion.2
  90.3 0.4 collective-permute-start.20
  90.7 1.1 collective-permute-start.21
  91.8 8.5 %collective-permute-done.18 = f16[256,1024]{1,0:T(8,128)(2,1)S(1)} collective-permute-done((f16[256,1024]{1,0:T(8,128)(2,1)S(1)}, f16[256,1024]{1,0:T(8,128)(2,1)S(1)}, u32[]{:S(2)}, u32[]{:S(2)}) %collective-permute-start.18) | collective-permute-done | bytes 524320 | tf_op jit(solution)/shard_map/ppermute | solution.py:23
  100.3 7.0 %collective-permute-done.19 = f16[256,1024]{1,0:T(8,128)(2,1)S(1)} collective-permute-done((f16[256,1024]{1,0:T(8,128)(2,1)S(1)}, f16[256,1024]{1,0:T(8,128)(2,1)S(1)}, u32[]{:S(2)}, u32[]{:S(2)}) %collective-permute-start.19) | collective-permute-done | bytes 524320 | tf_op jit(solution)/shard_map/ppermute | solution.py:32
  107.2 2.1 %add_dynamic-update-slice_fusion = f32[2048,1024]{1,0:T(8,128)S(1)} fusion(f32[2048,1024]{1,0:T(8,128)S(1)} %add_dynamic-update-slice_fusion.1, f16[256,1024]{1,0:T(8,128)(2,1)S(1)} %collective-permute-done.13, f32[1536,1024]{1,0:T(8,128)S(1)} %bitcast.51, f16[256,1024]{1,0:T(8,128)(2,1)} %collective-permute-done.11, ...), kind=kLoop, calls=%fused_computation.23 | loop fusion | flops 2621440 | bytes 3670028 | tf_op jit(solution)/shard_map/dynamic_update_slice | solution.py:104
  109.3 0.2 multiply_convert_fusion.1
  109.5 0.1 collective-permute-start.22
  109.6 0.1 collective-permute-start.23
  109.7 2.1 %bitcast_dynamic-update-slice_fusion.3 = f32[1,2048,1024]{2,1,0:T(8,128)S(1)} fusion(f32[1,2048,1024]{2,1,0:T(8,128)S(1)} %bitcast.52, f16[256,1024]{1,0:T(8,128)(2,1)S(1)} %collective-permute-done.16, f32[1536,1024]{1,0:T(8,128)S(1)} %bitcast.51, f16[256,1024]{1,0:T(8,128)(2,1)S(1)} %collective-permute-done.14, f16[256,1024]{1,0:T(8,128)(2,1)} %collective-permute-done.9, ...), kind=kLoop, calls=%fused_computation.20 | loop fusion | flops 2621440 | bytes 3670028 | tf_op jit(solution)/shard_map/dynamic_update_slice | solution.py:104
  111.8 1.0 bitcast_dynamic-update-slice_fusion.2
  112.8 0.0 collective-permute-done.21
  112.9 1.0 bitcast_dynamic-update-slice_fusion.1
  113.9 0.0 copy-start.5
  113.9 10.2 %collective-permute-done.23 = f16[256,1024]{1,0:T(8,128)(2,1)S(1)} collective-permute-done((f16[256,1024]{1,0:T(8,128)(2,1)S(1)}, f16[256,1024]{1,0:T(8,128)(2,1)S(1)}, u32[]{:S(2)}, u32[]{:S(2)}) %collective-permute-start.23) | collective-permute-done | bytes 524320 | tf_op jit(solution)/shard_map/ppermute | solution.py:32
  124.1 2.0 %bitcast_dynamic-update-slice_fusion = f32[1,2048,1024]{2,1,0:T(8,128)} fusion(f32[1,2048,1024]{2,1,0:T(8,128)} %copy-done.5, f16[256,1024]{1,0:T(8,128)(2,1)S(1)} %collective-permute-done.23, f32[1536,1024]{1,0:T(8,128)S(1)} %bitcast.51, f16[256,1024]{1,0:T(8,128)(2,1)S(1)} %collective-permute-done.22, f16[256,1024]{1,0:T(8,128)(2,1)S(1)} %collective-permute-done.18, ...), kind=kLoop, calls=%fused_computation.17 | loop fusion | flops 2621440 | bytes 3670536 | tf_op jit(solution)/shard_map/dynamic_update_slice | solution.py:104
  (39 shorter events, 0.1 us)
Async XLA Ops:
  0.0 1.5 %copy-start = (bf16[1,896,1024]{2,1,0:T(8,128)(2,1)S(1)}, bf16[1,896,1024]{2,1,0:T(8,128)(2,1)}, u32[]{:S(2)}) copy-start(bf16[1,896,1024]{2,1,0:T(8,128)(2,1)} %param.6) | copy-start | bytes 5505028
  4.0 15.1 %collective-permute-start.1 = (f16[256,1024]{1,0:T(8,128)(2,1)}, f16[256,1024]{1,0:T(8,128)(2,1)S(1)}, u32[]{:S(2)}, u32[]{:S(2)}) collective-permute-start(f16[256,1024]{1,0:T(8,128)(2,1)} %fusion.15), channel_id=1, source_target_pairs={{0,1},{1,0},{2,3},{3,2},{4,5},{5,4},{6,7},{7,6},{8,9},{9,8},{10,11... | collective-permute-start | bytes 1572872 | tf_op jit(solution)/shard_map/ppermute | solution.py:23
  14.5 17.6 %collective-permute-start = (f16[256,1024]{1,0:T(8,128)(2,1)}, f16[256,1024]{1,0:T(8,128)(2,1)S(1)}, u32[]{:S(2)}, u32[]{:S(2)}) collective-permute-start(f16[256,1024]{1,0:T(8,128)(2,1)} %get-tuple-element.177), channel_id=1, source_target_pairs={{0,1},{1,0},{2,3},{3,2},{4,5},{5,4},{6,7},{7,6},{8,9},{9,8},{10,11... | collective-permute-start | bytes 1572872 | tf_op jit(solution)/shard_map/ppermute | solution.py:23
  14.5 25.9 %collective-permute-start.3 = (f16[256,1024]{1,0:T(8,128)(2,1)}, f16[256,1024]{1,0:T(8,128)(2,1)S(1)}, u32[]{:S(2)}, u32[]{:S(2)}) collective-permute-start(f16[256,1024]{1,0:T(8,128)(2,1)} %get-tuple-element.176), channel_id=1, source_target_pairs={{0,1},{1,0},{2,3},{3,2},{4,5},{5,4},{6,7},{7,6},{8,9},{9,8},{10,11... | collective-permute-start | bytes 1572872 | tf_op jit(solution)/shard_map/ppermute | solution.py:23
  19.2 1.4 %copy-start.2 = (f32[512,1024]{1,0:T(8,128)}, f32[512,1024]{1,0:T(8,128)S(1)}, u32[]{:S(2)}) copy-start(f32[512,1024]{1,0:T(8,128)S(1)} %bitcast_subtract_fusion.1) | copy-start | bytes 6291460
  19.2 12.9 %copy-start.6 = (f16[256,1024]{1,0:T(8,128)(2,1)}, f16[256,1024]{1,0:T(8,128)(2,1)S(1)}, u32[]{:S(2)}) copy-start(f16[256,1024]{1,0:T(8,128)(2,1)S(1)} %collective-permute-done.1) | copy-start | bytes 1572868
  21.6 10.6 %collective-permute-start.2 = (f16[256,1024]{1,0:T(8,128)(2,1)}, f16[256,1024]{1,0:T(8,128)(2,1)}, u32[]{:S(2)}, u32[]{:S(2)}) collective-permute-start(f16[256,1024]{1,0:T(8,128)(2,1)} %multiply_convert_fusion.8), channel_id=1, source_target_pairs={{0,2},{2,0},{4,6},{6,4},{8,10},{10,8},{12,14},{14,12},{16,18},{18,... | collective-permute-start | bytes 1572872 | tf_op jit(solution)/shard_map/ppermute | solution.py:32
  23.1 17.3 %collective-permute-start.4 = (f16[256,1024]{1,0:T(8,128)(2,1)}, f16[256,1024]{1,0:T(8,128)(2,1)}, u32[]{:S(2)}, u32[]{:S(2)}) collective-permute-start(f16[256,1024]{1,0:T(8,128)(2,1)} %multiply_convert_fusion.8), channel_id=1, source_target_pairs={{2,4},{4,2},{6,8},{8,6},{10,12},{12,10},{14,16},{16,14},{18,20},{2... | collective-permute-start | bytes 1572872 | tf_op jit(solution)/shard_map/ppermute | solution.py:32
  24.2 8.0 %copy-start.3 = (f32[512,1024]{1,0:T(8,128)S(1)}, f32[512,1024]{1,0:T(8,128)}, u32[]{:S(2)}) copy-start(f32[512,1024]{1,0:T(8,128)} %copy-done.2) | copy-start | bytes 6291460
  32.1 8.3 %copy-start.1 = (f32[1536,1024]{1,0:T(8,128)}, f32[1536,1024]{1,0:T(8,128)S(1)}, u32[]{:S(2)}) copy-start(f32[1536,1024]{1,0:T(8,128)S(1)} %bitcast_subtract_fusion) | copy-start | bytes 18874372
  32.1 27.8 %copy-start.12 = (s32[16,3]{0,1:T(4,128)S(1)}, s32[16,3]{0,1:T(4,128)}, u32[]{:S(2)}) copy-start(s32[16,3]{0,1:T(4,128)} %param.7) | copy-start | bytes 580
  33.5 7.0 %collective-permute-start.5 = (f16[256,1024]{1,0:T(8,128)(2,1)}, f16[256,1024]{1,0:T(8,128)(2,1)S(1)}, u32[]{:S(2)}, u32[]{:S(2)}) collective-permute-start(f16[256,1024]{1,0:T(8,128)(2,1)} %multiply_convert_fusion.7), channel_id=1, source_target_pairs={{0,2},{2,0},{4,6},{6,4},{8,10},{10,8},{12,14},{14,12},{16,18},{18,... | collective-permute-start | bytes 1572872 | tf_op jit(solution)/shard_map/ppermute | solution.py:32
  37.0 14.8 %collective-permute-start.6 = (f16[256,1024]{1,0:T(8,128)(2,1)}, f16[256,1024]{1,0:T(8,128)(2,1)S(1)}, u32[]{:S(2)}, u32[]{:S(2)}) collective-permute-start(f16[256,1024]{1,0:T(8,128)(2,1)} %get-tuple-element.109), channel_id=1, source_target_pairs={{0,1},{1,0},{2,3},{3,2},{4,5},{5,4},{6,7},{7,6},{8,9},{9,8},{10,11... | collective-permute-start | bytes 1572872 | tf_op jit(solution)/shard_map/ppermute | solution.py:23
  37.2 20.5 %collective-permute-start.7 = (f16[256,1024]{1,0:T(8,128)(2,1)}, f16[256,1024]{1,0:T(8,128)(2,1)}, u32[]{:S(2)}, u32[]{:S(2)}) collective-permute-start(f16[256,1024]{1,0:T(8,128)(2,1)} %multiply_convert_fusion.7), channel_id=1, source_target_pairs={{2,4},{4,2},{6,8},{8,6},{10,12},{12,10},{14,16},{16,14},{18,20},{2... | collective-permute-start | bytes 1572872 | tf_op jit(solution)/shard_map/ppermute | solution.py:32
  40.5 1.0 copy-start.10
  41.5 16.2 %collective-permute-start.8 = (f16[256,1024]{1,0:T(8,128)(2,1)}, f16[256,1024]{1,0:T(8,128)(2,1)}, u32[]{:S(2)}, u32[]{:S(2)}) collective-permute-start(f16[256,1024]{1,0:T(8,128)(2,1)} %multiply_convert_fusion.6), channel_id=1, source_target_pairs={{0,2},{2,0},{4,6},{6,4},{8,10},{10,8},{12,14},{14,12},{16,18},{18,... | collective-permute-start | bytes 1572872 | tf_op jit(solution)/shard_map/ppermute | solution.py:32
  43.6 24.6 %collective-permute-start.9 = (f16[256,1024]{1,0:T(8,128)(2,1)}, f16[256,1024]{1,0:T(8,128)(2,1)}, u32[]{:S(2)}, u32[]{:S(2)}) collective-permute-start(f16[256,1024]{1,0:T(8,128)(2,1)} %get-tuple-element.118), channel_id=1, source_target_pairs={{0,1},{1,0},{2,3},{3,2},{4,5},{5,4},{6,7},{7,6},{8,9},{9,8},{10,11... | collective-permute-start | bytes 1572872 | tf_op jit(solution)/shard_map/ppermute | solution.py:23
  45.3 22.9 %collective-permute-start.10 = (f16[256,1024]{1,0:T(8,128)(2,1)}, f16[256,1024]{1,0:T(8,128)(2,1)}, u32[]{:S(2)}, u32[]{:S(2)}) collective-permute-start(f16[256,1024]{1,0:T(8,128)(2,1)} %multiply_convert_fusion.6), channel_id=1, source_target_pairs={{2,4},{4,2},{6,8},{8,6},{10,12},{12,10},{14,16},{16,14},{18,20},{2... | collective-permute-start | bytes 1572872 | tf_op jit(solution)/shard_map/ppermute | solution.py:32
  59.9 8.3 %collective-permute-start.11 = (f16[256,1024]{1,0:T(8,128)(2,1)}, f16[256,1024]{1,0:T(8,128)(2,1)}, u32[]{:S(2)}, u32[]{:S(2)}) collective-permute-start(f16[256,1024]{1,0:T(8,128)(2,1)} %multiply_convert_fusion.5), channel_id=1, source_target_pairs={{0,2},{2,0},{4,6},{6,4},{8,10},{10,8},{12,14},{14,12},{16,18},{18,... | collective-permute-start | bytes 1572872 | tf_op jit(solution)/shard_map/ppermute | solution.py:32
  63.0 2.4 %copy-start.4 = (f32[512,1024]{1,0:T(8,128)S(1)}, f32[512,1024]{1,0:T(8,128)}, u32[]{:S(2)}) copy-start(f32[512,1024]{1,0:T(8,128)} %copy-done.2) | copy-start | bytes 6291460
  63.0 2.4 %copy-start.7 = (f16[256,1024]{1,0:T(8,128)(2,1)S(1)}, f16[256,1024]{1,0:T(8,128)(2,1)}, u32[]{:S(2)}) copy-start(f16[256,1024]{1,0:T(8,128)(2,1)} %copy-done.6) | copy-start | bytes 1572868
  63.1 13.3 %collective-permute-start.12 = (f16[256,1024]{1,0:T(8,128)(2,1)}, f16[256,1024]{1,0:T(8,128)(2,1)S(1)}, u32[]{:S(2)}, u32[]{:S(2)}) collective-permute-start(f16[256,1024]{1,0:T(8,128)(2,1)} %get-tuple-element.131), channel_id=1, source_target_pairs={{0,1},{1,0},{2,3},{3,2},{4,5},{5,4},{6,7},{7,6},{8,9},{9,8},{10,11... | collective-permute-start | bytes 1572872 | tf_op jit(solution)/shard_map/ppermute | solution.py:23
  64.4 20.3 %collective-permute-start.13 = (f16[256,1024]{1,0:T(8,128)(2,1)}, f16[256,1024]{1,0:T(8,128)(2,1)S(1)}, u32[]{:S(2)}, u32[]{:S(2)}) collective-permute-start(f16[256,1024]{1,0:T(8,128)(2,1)} %multiply_convert_fusion.5), channel_id=1, source_target_pairs={{2,4},{4,2},{6,8},{8,6},{10,12},{12,10},{14,16},{16,14},{18,20},{2... | collective-permute-start | bytes 1572872 | tf_op jit(solution)/shard_map/ppermute | solution.py:32
  64.4 6.7 %copy-start.9 = (f16[256,1024]{1,0:T(8,128)(2,1)S(1)}, f16[256,1024]{1,0:T(8,128)(2,1)}, u32[]{:S(2)}) copy-start(f16[256,1024]{1,0:T(8,128)(2,1)} %get-tuple-element.144) | copy-start | bytes 1572868
  64.4 20.3 %copy-start.11 = (f16[256,1024]{1,0:T(8,128)(2,1)S(1)}, f16[256,1024]{1,0:T(8,128)(2,1)}, u32[]{:S(2)}) copy-start(f16[256,1024]{1,0:T(8,128)(2,1)} %copy-done.10) | copy-start | bytes 1572868
  64.4 22.4 %slice-start = ((s8[6291456]{0:T(1024)(128)(4,1)}), s8[2097152]{0:T(1024)(128)(4,1)S(1)}, s32[]{:S(2)}) async-start(s8[6291456]{0:T(1024)(128)(4,1)} %bitcast.50), calls=%async_computation | async-start | bytes 4194304
  65.5 21.3 %slice-start.1 = ((s8[6291456]{0:T(1024)(128)(4,1)}), s8[4194304]{0:T(1024)(128)(4,1)S(1)}, s32[]{:S(2)}) async-start(s8[6291456]{0:T(1024)(128)(4,1)} %bitcast.50), calls=%async_computation.1 | async-start | bytes 8388608
  65.5 21.6 %copy-start.8 = (f16[256,1024]{1,0:T(8,128)(2,1)S(1)}, f16[256,1024]{1,0:T(8,128)(2,1)}, u32[]{:S(2)}) copy-start(f16[256,1024]{1,0:T(8,128)(2,1)} %get-tuple-element.154) | copy-start | bytes 1572868
  69.8 17.0 %collective-permute-start.14 = (f16[256,1024]{1,0:T(8,128)(2,1)S(1)}, f16[256,1024]{1,0:T(8,128)(2,1)S(1)}, u32[]{:S(2)}, u32[]{:S(2)}) collective-permute-start(f16[256,1024]{1,0:T(8,128)(2,1)S(1)} %multiply_convert_fusion.4), channel_id=1, source_target_pairs={{0,2},{2,0},{4,6},{6,4},{8,10},{10,8},{12,14},{14,12},{16,18},{18,... | collective-permute-start | bytes 1572872 | tf_op jit(solution)/shard_map/ppermute | solution.py:32
  71.1 18.5 %collective-permute-start.15 = (f16[256,1024]{1,0:T(8,128)(2,1)S(1)}, f16[256,1024]{1,0:T(8,128)(2,1)S(1)}, u32[]{:S(2)}, u32[]{:S(2)}) collective-permute-start(f16[256,1024]{1,0:T(8,128)(2,1)S(1)} %copy-done.9), channel_id=1, source_target_pairs={{0,1},{1,0},{2,3},{3,2},{4,5},{5,4},{6,7},{7,6},{8,9},{9,8},{10,11... | collective-permute-start | bytes 1572872 | tf_op jit(solution)/shard_map/ppermute | solution.py:23
  71.3 18.7 %collective-permute-start.16 = (f16[256,1024]{1,0:T(8,128)(2,1)S(1)}, f16[256,1024]{1,0:T(8,128)(2,1)S(1)}, u32[]{:S(2)}, u32[]{:S(2)}) collective-permute-start(f16[256,1024]{1,0:T(8,128)(2,1)S(1)} %multiply_convert_fusion.4), channel_id=1, source_target_pairs={{2,4},{4,2},{6,8},{8,6},{10,12},{12,10},{14,16},{16,14},{18,20},{2... | collective-permute-start | bytes 1572872 | tf_op jit(solution)/shard_map/ppermute | solution.py:32
  87.0 3.0 %collective-permute-start.17 = (f16[256,1024]{1,0:T(8,128)(2,1)S(1)}, f16[256,1024]{1,0:T(8,128)(2,1)S(1)}, u32[]{:S(2)}, u32[]{:S(2)}) collective-permute-start(f16[256,1024]{1,0:T(8,128)(2,1)S(1)} %multiply_convert_fusion.3), channel_id=1, source_target_pairs={{0,2},{2,0},{4,6},{6,4},{8,10},{10,8},{12,14},{14,12},{16,18},{18,... | collective-permute-start | bytes 1572872 | tf_op jit(solution)/shard_map/ppermute | solution.py:32
  87.1 13.1 %collective-permute-start.18 = (f16[256,1024]{1,0:T(8,128)(2,1)S(1)}, f16[256,1024]{1,0:T(8,128)(2,1)S(1)}, u32[]{:S(2)}, u32[]{:S(2)}) collective-permute-start(f16[256,1024]{1,0:T(8,128)(2,1)S(1)} %copy-done.8), channel_id=1, source_target_pairs={{0,1},{1,0},{2,3},{3,2},{4,5},{5,4},{6,7},{7,6},{8,9},{9,8},{10,11... | collective-permute-start | bytes 1572872 | tf_op jit(solution)/shard_map/ppermute | solution.py:23
  87.4 19.8 %collective-permute-start.19 = (f16[256,1024]{1,0:T(8,128)(2,1)S(1)}, f16[256,1024]{1,0:T(8,128)(2,1)S(1)}, u32[]{:S(2)}, u32[]{:S(2)}) collective-permute-start(f16[256,1024]{1,0:T(8,128)(2,1)S(1)} %multiply_convert_fusion.3), channel_id=1, source_target_pairs={{2,4},{4,2},{6,8},{8,6},{10,12},{12,10},{14,16},{16,14},{18,20},{2... | collective-permute-start | bytes 1572872 | tf_op jit(solution)/shard_map/ppermute | solution.py:32
  90.3 19.0 %collective-permute-start.20 = (f16[256,1024]{1,0:T(8,128)(2,1)S(1)}, f16[256,1024]{1,0:T(8,128)(2,1)S(1)}, u32[]{:S(2)}, u32[]{:S(2)}) collective-permute-start(f16[256,1024]{1,0:T(8,128)(2,1)S(1)} %multiply_convert_fusion.2), channel_id=1, source_target_pairs={{0,2},{2,0},{4,6},{6,4},{8,10},{10,8},{12,14},{14,12},{16,18},{18,... | collective-permute-start | bytes 1572872 | tf_op jit(solution)/shard_map/ppermute | solution.py:32
  90.7 22.2 %collective-permute-start.21 = (f16[256,1024]{1,0:T(8,128)(2,1)S(1)}, f16[256,1024]{1,0:T(8,128)(2,1)S(1)}, u32[]{:S(2)}, u32[]{:S(2)}) collective-permute-start(f16[256,1024]{1,0:T(8,128)(2,1)S(1)} %multiply_convert_fusion.2), channel_id=1, source_target_pairs={{2,4},{4,2},{6,8},{8,6},{10,12},{12,10},{14,16},{16,14},{18,20},{2... | collective-permute-start | bytes 1572872 | tf_op jit(solution)/shard_map/ppermute | solution.py:32
  109.5 4.4 %collective-permute-start.22 = (f16[256,1024]{1,0:T(8,128)(2,1)S(1)}, f16[256,1024]{1,0:T(8,128)(2,1)S(1)}, u32[]{:S(2)}, u32[]{:S(2)}) collective-permute-start(f16[256,1024]{1,0:T(8,128)(2,1)S(1)} %multiply_convert_fusion.1), channel_id=1, source_target_pairs={{0,2},{2,0},{4,6},{6,4},{8,10},{10,8},{12,14},{14,12},{16,18},{18,... | collective-permute-start | bytes 1572872 | tf_op jit(solution)/shard_map/ppermute | solution.py:32
  109.6 14.5 %collective-permute-start.23 = (f16[256,1024]{1,0:T(8,128)(2,1)S(1)}, f16[256,1024]{1,0:T(8,128)(2,1)S(1)}, u32[]{:S(2)}, u32[]{:S(2)}) collective-permute-start(f16[256,1024]{1,0:T(8,128)(2,1)S(1)} %multiply_convert_fusion.1), channel_id=1, source_target_pairs={{2,4},{4,2},{6,8},{8,6},{10,12},{12,10},{14,16},{16,14},{18,20},{2... | collective-permute-start | bytes 1572872 | tf_op jit(solution)/shard_map/ppermute | solution.py:32
  113.9 10.2 %copy-start.5 = (f32[1,2048,1024]{2,1,0:T(8,128)}, f32[1,2048,1024]{2,1,0:T(8,128)S(1)}, u32[]{:S(2)}) copy-start(f32[1,2048,1024]{2,1,0:T(8,128)S(1)} %bitcast_dynamic-update-slice_fusion.1) | copy-start | bytes 25165828

commit v11 on v10

v11 whole, which is shorter than its diff:
```python
import math

import jax
import jax.numpy as jnp
from jax import lax
from jax.sharding import PartitionSpec as P

MIX_DENOM = 64
RATE = 0.03
LARGEST = 6.0
WIRE = jnp.float16
STEP = 256
FIRST = 256
AHEAD = 3
MIXLAG = 5


def from_behind(value, axis, steps):
    count = lax.axis_size(axis)
    pairs = [(source, (source + steps) % count) for source in range(count)]
    return lax.ppermute(value, axis, pairs)


def swapped(value, axis, first):
    count = lax.axis_size(axis)
    pairs = []
    for source in range(first, count, 2):
        partner = (source + 1) % count
        pairs += [(source, partner), (partner, source)]
    return lax.ppermute(value, axis, pairs)


def wire_scale(tokens):
    bound = LARGEST + RATE * LARGEST * LARGEST * tokens
    return 2.0 ** math.floor(math.log2(float(jnp.finfo(WIRE).max) / bound))


def on_device(params, inputs, cotangent, mix):
    weights = params[0]
    features = inputs[0]
    cot_local = cotangent[0]
    rows = weights.shape[0]
    shards = lax.axis_size("fsdp")
    scale = wire_scale(features.shape[0] * shards)
    replica = lax.axis_index("blk")
    shard = lax.axis_index("fsdp")
    row = lax.dynamic_slice_in_dim(mix, replica, 1, axis=0).astype(jnp.float32) / MIX_DENOM
    left, own, right = row[:, 0:1], row[:, 1:2], row[:, 2:3]
    even = replica % 2 == 0
    sides = [jnp.where(even, right, left) / scale, own, jnp.where(even, left, right) / scale]
    coeff = jnp.broadcast_to(jnp.concatenate(sides, axis=0), (3, weights.shape[1]))
    first = min(FIRST, rows // 2)
    main = rows - first
    cuts = list(range(0, main, STEP)) + [main]
    chunks = len(cuts) - 1

    def owner(away, shard=shard):
        other = shard + away
        return jnp.where(other < shards, other, other - shards)

    def partial(owner, start, size):
        block = lax.dynamic_slice_in_dim(features, owner * rows + start, size, axis=1)
        return lax.dot_general(
            block, cot_local, (((0,), (0,)), ((), ())), preferred_element_type=jnp.float32
        )

    def for_others(start, stop):
        return [
            (partial(owner(away), start, stop - start) * (RATE * scale)).astype(WIRE)
            for away in range(1, shards)
        ]

    def own_part(shard, start, stop):
        return weights[start:stop] - RATE * partial(shard, start, stop - start)

    def add_over_fsdp(terms):
        return [from_behind(term, "fsdp", away) for away, term in zip(range(1, shards), terms)]

    def u_of(chunk):
        start, stop = cuts[chunk], cuts[chunk + 1]
        total = base[0][start:stop] if stop <= split else base[1][start - split:stop - split]
        for term in arrived[chunk]:
            total = total - term.astype(jnp.float32) / scale
        return total

    def mixture(near, own, far):
        return (
            coeff[0:1] * near.astype(jnp.float32) + coeff[1:2] * own + coeff[2:3] * far.astype(jnp.float32)
        )

    def mix_into(out, chunk):
        value = mixture(near[chunk], u_of(chunk), far[chunk])
        return lax.dynamic_update_slice_in_dim(out, value, cuts[chunk], axis=0)

    near = {}
    far = {}
    mixed = 0
    out = jnp.zeros_like(weights)
    split = cuts[min(2, chunks)]
    terms = {0: for_others(0, cuts[1])}
    arrived = {0: add_over_fsdp(terms[0])}

    parts = [own_part(shard, main, rows)]
    parts += [-RATE * partial(owner(away), main, first) for away in range(1, shards)]
    parts = jnp.concatenate(parts, axis=0)
    parts, sent = lax.optimization_barrier((parts, (parts * scale).astype(WIRE)))
    far[-1] = swapped(sent, "blk", 1)
    near[-1] = swapped(sent, "blk", 0)

    if chunks > 1:
        parts, later = lax.optimization_barrier((parts, shard))
        rest = [
            (partial(owner(away, later), cuts[1], main - cuts[1]) * (RATE * scale)).astype(WIRE)
            for away in range(1, shards)
        ]
        for chunk in range(1, chunks):
            terms[chunk] = [term[cuts[chunk] - cuts[1]:cuts[chunk + 1] - cuts[1]] for term in rest]
        for chunk in range(1, min(AHEAD, chunks)):
            if chunk == 2:
                terms[chunk], near[-1] = lax.optimization_barrier((terms[chunk], near[-1]))
            arrived[chunk] = add_over_fsdp(terms[chunk])
    base = [own_part(shard, 0, split)]

    arrived[0], base, terms = lax.optimization_barrier((arrived[0], base, terms))
    for chunk in range(chunks):
        if chunk == 1:
            arrived[1], base = lax.optimization_barrier((arrived[1], base))
        if chunk >= 1:
            arrived[chunk], far[chunk - 2] = lax.optimization_barrier((arrived[chunk], far[chunk - 2]))
        arrived[chunk], near[chunk - 1] = lax.optimization_barrier((arrived[chunk], near[chunk - 1]))
        if mixed:
            arrived[chunk], out = lax.optimization_barrier((arrived[chunk], out))
        if chunk == 3:
            arrived[chunk], parts = lax.optimization_barrier((arrived[chunk], parts))
        sent = (u_of(chunk) * scale).astype(WIRE)
        sent, base, out, later = lax.optimization_barrier((sent, base, out, shard))
        if chunk == 0 and split < main:
            base.append(own_part(later, split, main))
        if chunk == min(1, chunks - 1):
            coeff, parts, sent = lax.optimization_barrier((coeff, parts, sent))
            parts = mixture(near[-1], parts, far[-1])
            back = [
                (parts[away * first:(away + 1) * first] * scale).astype(WIRE) for away in range(1, shards)
            ]
            parts = parts[:first]
        after = chunk + AHEAD
        if after < chunks:
            terms[after], sent = lax.optimization_barrier((terms[after], sent))
            arrived[after] = add_over_fsdp(terms[after])
        if after == max(chunks, AHEAD):
            back, sent = lax.optimization_barrier((back, sent))
            back = add_over_fsdp(back)
        far[chunk] = swapped(sent, "blk", 1)
        near[chunk] = swapped(sent, "blk", 0)
        if chunk >= MIXLAG:
            out = mix_into(out, mixed)
            mixed += 1

    for term in back:
        parts = parts + term.astype(jnp.float32) / scale
    out = lax.dynamic_update_slice_in_dim(out, parts, main, axis=0)
    for chunk in range(mixed, chunks):
        out = mix_into(out, chunk)
    return out[None]


def solution(mesh):
    return jax.shard_map(
        on_device,
        mesh=mesh,
        in_specs=(P("blk", "fsdp", None), P("blk", "fsdp", None), P("blk", "fsdp", None), P()),
        out_specs=P("blk", "fsdp", None),
        check_vma=False,
    )
```

time: 127 us -> 119 us (0.937)
  other arithmetic: 23 us -> 13.2 us
  starting transfers between devices: 20.9 us -> 23.9 us
  matrix products: 19.9 us -> 21.5 us
  local copies, waits for them, and re-layouts: 6.84 us -> 5.48 us
  waiting for transfers between devices: 52.8 us -> 51.5 us
    ppermute x16, waiting for transfers between devices: 31.9 us -> 13.7 us  [swapped(): return lax.ppermute(value, axis, pairs)]
    ppermute x8, waiting for transfers between devices: 20.9 us -> 37.8 us  [from_behind(): return lax.ppermute(value, axis, pairs)]
    dynamic_update_slice x8, other arithmetic: 15.2 us -> 5.44 us  [the longest x7 5.23 us: mix_into(): return lax.dynamic_update_slice_in_dim(out, value, cuts[chunk], axis=0)]
    convert_element_type x8 -> x7, other arithmetic: 7.81 us -> 2.32 us  [on_device(): sent = (u_of(chunk) * scale).astype(WIRE)]
    ppermute x16, starting transfers between devices: 13.5 us -> 15.9 us  [swapped(): return lax.ppermute(value, axis, pairs)]
    convert_element_type x0 -> x2, other arithmetic: none -> 2.34 us  [the longest x1 2.09 us: on_device(): (parts * scale).astype(WIRE)]
    add x0 -> x1, other arithmetic: none -> 2.24 us  [mixture(): coeff[0:1] * near.astype(jnp.float32) + coeff[1:2] * own]
    dot_general x4 -> x6, matrix products: 19.8 us -> 21.5 us  [partial(): lax.dot_general(block, cot_local, (((0,), (0,)), ((), ())), preferred_ele...]
  transfers between devices with their start and end apart: 24 -> 24, of which waited for: 9 -> 9; matrix products, arithmetic and copies ran while one was open for 34% -> 26% of each run, Pallas kernels for 0% -> 0%
where the time goes in v11:
time: 119 us; the launch traced here: 118 us
  waiting for transfers between devices  51.5 us (43%)
  starting transfers between devices  23.9 us (20%)
  matrix products  21.5 us (18%)
  other arithmetic  13.2 us (11%)
  local copies, waits for them, and re-layouts  5.48 us (5%)
  between operations  2.92 us (2%)
    ppermute x8, waiting for transfers between devices, from_behind(): return lax.ppermute(value, axis, pairs)  37.8 us
    dot_general x6, matrix products, partial(): lax.dot_general(block, cot_local, (((0,), (0,)), ((), ())), preferred_ele...  21.5 us
    ppermute x16, starting transfers between devices, swapped(): return lax.ppermute(value, axis, pairs)  15.9 us
    ppermute x16, waiting for transfers between devices, swapped(): return lax.ppermute(value, axis, pairs)  13.7 us
    ppermute x8, starting transfers between devices, from_behind(): return lax.ppermute(value, axis, pairs)  7.98 us
    dynamic_update_slice x7, other arithmetic, mix_into(): return lax.dynamic_update_slice_in_dim(out, value, cuts[chunk], axis=0)  5.23 us
  transfers between devices with their start and end apart: 24, of which 9 were waited for; matrix products, arithmetic and copies ran while one was open for 26% of the time, Pallas kernels for 0%

profile of v11, /device:TPU:1, one launch (start us, length us, event | category | flops | bytes accessed | tf_op | source)
XLA Modules:
  0.0 118.5 jit_solution(5432394128358333105)
XLA Ops:
  0.0 1.5 %copy-done = bf16[1,896,1024]{2,1,0:T(8,128)(2,1)S(1)} copy-done((bf16[1,896,1024]{2,1,0:T(8,128)(2,1)S(1)}, bf16[1,896,1024]{2,1,0:T(8,128)(2,1)}, u32[]{:S(2)}) %copy-start) | copy-done | bytes 1835032
  1.5 1.7 %fusion.22 = f32[256,1024]{1,0:T(8,128)S(1)} fusion(bf16[1,896,1024]{2,1,0:T(8,128)(2,1)S(1)} %copy-done, bf16[1,896,4096]{2,1,0:T(8,128)(2,1)} %param.5, s32[]{:T(128)S(6)} %select_n.49), kind=kOutput, calls=%fused_computation.22 | convolution fusion | flops 470024192 | bytes 3342340 | tf_op jit(solution)/shard_map/dot_general | solution.py:63
  3.2 2.1 %fusion.19 = f32[256,1024]{1,0:T(8,128)S(1)} fusion(bf16[1,896,1024]{2,1,0:T(8,128)(2,1)S(1)} %copy-done, f32[1,2048,1024]{2,1,0:T(8,128)} %param.4, bf16[1,896,4096]{2,1,0:T(8,128)(2,1)} %param.5, s32[]{:T(128)S(6)} %select_n.47), kind=kOutput, calls=%fused_computation.21 | convolution fusion | flops 470286336 | bytes 4390916 | tf_op jit(solution)/shard_map/dot_general | solution.py:63
  5.4 2.1 %multiply_convert_fusion.1 = (f16[512,1024]{1,0:T(8,128)(2,1)}, f32[512,1024]{1,0:T(8,128)}) fusion(f32[256,1024]{1,0:T(8,128)S(1)} %fusion.22, f32[256,1024]{1,0:T(8,128)S(1)} %fusion.19), kind=kLoop, calls=%fused_computation.9 | loop fusion | flops 1572864 | bytes 5242880 | tf_op jit(solution)/shard_map/convert_element_type | solution.py:106
  7.5 2.6 %collective-permute-start.3 = (f16[512,1024]{1,0:T(8,128)(2,1)}, f16[512,1024]{1,0:T(8,128)(2,1)}, u32[]{:S(2)}, u32[]{:S(2)}) collective-permute-start(f16[512,1024]{1,0:T(8,128)(2,1)} %get-tuple-element.93), channel_id=1, source_target_pairs={{2,4},{4,2},{6,8},{8,6},{10,12},{12,10},{14,16},{16,14},{18,20},{2... | collective-permute-start | bytes 3145736 | tf_op jit(solution)/shard_map/ppermute | solution.py:30
  10.1 2.9 %collective-permute-start.2 = (f16[512,1024]{1,0:T(8,128)(2,1)}, f16[512,1024]{1,0:T(8,128)(2,1)}, u32[]{:S(2)}, u32[]{:S(2)}) collective-permute-start(f16[512,1024]{1,0:T(8,128)(2,1)} %get-tuple-element.93), channel_id=1, source_target_pairs={{0,2},{2,0},{4,6},{6,4},{8,10},{10,8},{12,14},{14,12},{16,18},{18,... | collective-permute-start | bytes 3145736 | tf_op jit(solution)/shard_map/ppermute | solution.py:30
  12.9 2.6 %fusion.28 = f16[256,1024]{1,0:T(8,128)(2,1)} fusion(bf16[1,896,1024]{2,1,0:T(8,128)(2,1)S(1)} %copy-done, bf16[1,896,4096]{2,1,0:T(8,128)(2,1)} %param.5, s32[]{:T(128)S(6)} %select_n.52), kind=kOutput, calls=%fused_computation.24 | convolution fusion | flops 470286336 | bytes 2818052 | tf_op jit(solution)/shard_map/dot_general | solution.py:63
  15.5 1.2 %collective-permute-start.1 = (f16[256,1024]{1,0:T(8,128)(2,1)}, f16[256,1024]{1,0:T(8,128)(2,1)S(1)}, u32[]{:S(2)}, u32[]{:S(2)}) collective-permute-start(f16[256,1024]{1,0:T(8,128)(2,1)} %fusion.28), channel_id=1, source_target_pairs={{0,1},{1,0},{2,3},{3,2},{4,5},{5,4},{6,7},{7,6},{8,9},{9,8},{10,11... | collective-permute-start | bytes 1572872 | tf_op jit(solution)/shard_map/ppermute | solution.py:21
  16.8 5.5 %multiply_convert_fusion = f16[1536,1024]{1,0:T(8,128)(2,1)S(1)} fusion(bf16[1,896,4096]{2,1,0:T(8,128)(2,1)} %param.5, s32[]{:T(128)S(6)} %select_n.51, bf16[1,896,1024]{2,1,0:T(8,128)(2,1)S(1)} %copy-done), kind=kOutput, calls=%fused_computation | convolution fusion | flops 2821718016 | bytes 7733252 | tf_op jit(solution)/shard_map/dot_general | solution.py:63
  22.2 2.2 %fusion.48 = (f16[256,1024]{1,0:T(8,128)(2,1)}, f16[256,1024]{1,0:T(8,128)(2,1)}, f16[256,1024]{1,0:T(8,128)(2,1)}, f16[256,1024]{1,0:T(8,128)(2,1)}, f16[256,1024]{1,0:T(8,128)(2,1)}, /*index=5*/f16[256,1024]{1,0:T(8,128)(2,1)}) fusion(f16[1536,1024]{1,0:T(8,128)(2,1)S(1)} %multiply_convert_fusion), kind=kLoop, calls=%fused_computation.67 | loop fusion | bytes 6291456 | tf_op jit(solution)/shard_map/slice | solution.py:117
  24.5 0.2 collective-permute-start
  24.7 0.1 fusion.47
  24.8 0.6 fusion.50
  28.0 3.2 %bitcast_subtract_fusion.1 = f32[512,1024]{1,0:T(8,128)S(1)} fusion(f32[1,2048,1024]{2,1,0:T(8,128)} %param.4, bf16[1,896,1024]{2,1,0:T(8,128)(2,1)S(1)} %copy-done, bf16[1,896,4096]{2,1,0:T(8,128)(2,1)} %param.5, s32[]{:T(128)S(6)} %select_n.53), kind=kOutput, calls=%fused_computation.7 | convolution fusion | flops 940572672 | bytes 6946820 | tf_op jit(solution)/shard_map/dot_general | solution.py:63
  31.2 0.8 maximum_bitcast_fusion
  31.9 1.3 %collective-permute-start.5 = (f16[256,1024]{1,0:T(8,128)(2,1)}, f16[256,1024]{1,0:T(8,128)(2,1)S(1)}, u32[]{:S(2)}, u32[]{:S(2)}) collective-permute-start(f16[256,1024]{1,0:T(8,128)(2,1)} %get-tuple-element.94), channel_id=1, source_target_pairs={{0,1},{1,0},{2,3},{3,2},{4,5},{5,4},{6,7},{7,6},{8,9},{9,8},{10,11... | collective-permute-start | bytes 1572872 | tf_op jit(solution)/shard_map/ppermute | solution.py:21
  33.2 1.0 multiply_convert_fusion.8
  34.2 0.8 collective-permute-start.4
  35.1 6.5 %bitcast_subtract_fusion = f32[1280,1024]{1,0:T(8,128)S(1)} fusion(f32[1,2048,1024]{2,1,0:T(8,128)} %param.4, bf16[1,896,4096]{2,1,0:T(8,128)(2,1)} %param.5, s32[]{:T(128)S(6)} %select_n.54, bf16[1,896,1024]{2,1,0:T(8,128)(2,1)S(1)} %copy-done), kind=kOutput, calls=%fused_computation.1 | convolution fusion | flops 2351431680 | bytes 14614532 | tf_op jit(solution)/shard_map/dot_general | solution.py:63
  41.6 0.2 multiply_convert_fusion.7
  41.8 0.1 broadcast_in_dim.29
  41.9 0.1 collective-permute-start.7
  42.0 1.3 %collective-permute-start.8 = (f16[256,1024]{1,0:T(8,128)(2,1)S(1)}, f16[256,1024]{1,0:T(8,128)(2,1)S(1)}, u32[]{:S(2)}, u32[]{:S(2)}) collective-permute-start(f16[256,1024]{1,0:T(8,128)(2,1)S(1)} %copy-done.8), channel_id=1, source_target_pairs={{0,1},{1,0},{2,3},{3,2},{4,5},{5,4},{6,7},{7,6},{8,9},{9,8},{10,11... | collective-permute-start | bytes 1572872 | tf_op jit(solution)/shard_map/ppermute | solution.py:21
  43.2 0.8 collective-permute-start.9
  44.1 7.7 %collective-permute-done.5 = f16[256,1024]{1,0:T(8,128)(2,1)S(1)} collective-permute-done((f16[256,1024]{1,0:T(8,128)(2,1)}, f16[256,1024]{1,0:T(8,128)(2,1)S(1)}, u32[]{:S(2)}, u32[]{:S(2)}) %collective-permute-start.5) | collective-permute-done | bytes 524320 | tf_op jit(solution)/shard_map/ppermute | solution.py:21
  51.8 0.0 collective-permute-done.6
  51.8 1.2 %collective-permute-start.11 = (f16[256,1024]{1,0:T(8,128)(2,1)S(1)}, f16[256,1024]{1,0:T(8,128)(2,1)S(1)}, u32[]{:S(2)}, u32[]{:S(2)}) collective-permute-start(f16[256,1024]{1,0:T(8,128)(2,1)S(1)} %copy-done.7), channel_id=1, source_target_pairs={{0,1},{1,0},{2,3},{3,2},{4,5},{5,4},{6,7},{7,6},{8,9},{9,8},{10,11... | collective-permute-start | bytes 1572872 | tf_op jit(solution)/shard_map/ppermute | solution.py:21
  53.0 0.2 multiply_convert_fusion.6
  53.2 1.5 %collective-permute-start.10 = (f16[256,1024]{1,0:T(8,128)(2,1)S(1)}, f16[256,1024]{1,0:T(8,128)(2,1)S(1)}, u32[]{:S(2)}, u32[]{:S(2)}) collective-permute-start(f16[256,1024]{1,0:T(8,128)(2,1)S(1)} %multiply_convert_fusion.6), channel_id=1, source_target_pairs={{0,2},{2,0},{4,6},{6,4},{8,10},{10,8},{12,14},{14,12},{16,18},{18,... | collective-permute-start | bytes 1572872 | tf_op jit(solution)/shard_map/ppermute | solution.py:30
  54.8 2.2 %multiply_add_fusion = f32[512,1024]{1,0:T(8,128)S(1)} fusion(f16[512,1024]{1,0:T(8,128)(2,1)} %collective-permute-done.3, f32[512,1024]{1,0:T(8,128)S(1)} %copy-done.2, f16[512,1024]{1,0:T(8,128)(2,1)} %collective-permute-done.2, f32[1024]{0:T(1024)S(1)} %bitcast.79, f32[1024]{0:T(1024)S(1)} %bitcast.87, f32[1024]{0:T(1024)S(1)} %bitcast.71), kind=kLoop, calls=%fused_computation.8 | loop fusion | flops 3670016 | bytes 6303744 | tf_op jit(solution)/shard_map/add | solution.py:88
  57.0 0.2 fusion.31
  57.3 0.7 collective-permute-start.12
  58.0 5.0 %collective-permute-done.8 = f16[256,1024]{1,0:T(8,128)(2,1)S(1)} collective-permute-done((f16[256,1024]{1,0:T(8,128)(2,1)S(1)}, f16[256,1024]{1,0:T(8,128)(2,1)S(1)}, u32[]{:S(2)}, u32[]{:S(2)}) %collective-permute-start.8) | collective-permute-done | bytes 524320 | tf_op jit(solution)/shard_map/ppermute | solution.py:21
  63.0 0.2 multiply_convert_fusion.5
  63.2 1.2 %collective-permute-start.13 = (f16[256,1024]{1,0:T(8,128)(2,1)S(1)}, f16[256,1024]{1,0:T(8,128)(2,1)S(1)}, u32[]{:S(2)}, u32[]{:S(2)}) collective-permute-start(f16[256,1024]{1,0:T(8,128)(2,1)S(1)} %multiply_convert_fusion.5), channel_id=1, source_target_pairs={{0,2},{2,0},{4,6},{6,4},{8,10},{10,8},{12,14},{14,12},{16,18},{18,... | collective-permute-start | bytes 1572872 | tf_op jit(solution)/shard_map/ppermute | solution.py:30
  64.5 1.3 %collective-permute-start.14 = (f16[256,1024]{1,0:T(8,128)(2,1)S(1)}, f16[256,1024]{1,0:T(8,128)(2,1)S(1)}, u32[]{:S(2)}, u32[]{:S(2)}) collective-permute-start(f16[256,1024]{1,0:T(8,128)(2,1)S(1)} %copy-done.6), channel_id=1, source_target_pairs={{0,1},{1,0},{2,3},{3,2},{4,5},{5,4},{6,7},{7,6},{8,9},{9,8},{10,11... | collective-permute-start | bytes 1572872 | tf_op jit(solution)/shard_map/ppermute | solution.py:21
  65.7 8.5 %collective-permute-done.11 = f16[256,1024]{1,0:T(8,128)(2,1)S(1)} collective-permute-done((f16[256,1024]{1,0:T(8,128)(2,1)S(1)}, f16[256,1024]{1,0:T(8,128)(2,1)S(1)}, u32[]{:S(2)}, u32[]{:S(2)}) %collective-permute-start.11) | collective-permute-done | bytes 524320 | tf_op jit(solution)/shard_map/ppermute | solution.py:21
  74.2 3.2 %collective-permute-done.12 = f16[256,1024]{1,0:T(8,128)(2,1)S(1)} collective-permute-done((f16[256,1024]{1,0:T(8,128)(2,1)S(1)}, f16[256,1024]{1,0:T(8,128)(2,1)S(1)}, u32[]{:S(2)}, u32[]{:S(2)}) %collective-permute-start.12) | collective-permute-done | bytes 524320 | tf_op jit(solution)/shard_map/ppermute | solution.py:30
  77.5 0.2 multiply_convert_fusion.4
  77.7 0.1 collective-permute-start.16
  77.8 0.3 collective-permute-start.17
  78.1 1.3 %collective-permute-start.18 = (f16[256,1024]{1,0:T(8,128)(2,1)S(1)}, f16[256,1024]{1,0:T(8,128)(2,1)S(1)}, u32[]{:S(2)}, u32[]{:S(2)}) collective-permute-start(f16[256,1024]{1,0:T(8,128)(2,1)S(1)} %multiply_convert_fusion.4), channel_id=1, source_target_pairs={{2,4},{4,2},{6,8},{8,6},{10,12},{12,10},{14,16},{16,14},{18,20},{2... | collective-permute-start | bytes 1572872 | tf_op jit(solution)/shard_map/ppermute | solution.py:30
  79.4 6.1 %collective-permute-done.14 = f16[256,1024]{1,0:T(8,128)(2,1)S(1)} collective-permute-done((f16[256,1024]{1,0:T(8,128)(2,1)S(1)}, f16[256,1024]{1,0:T(8,128)(2,1)S(1)}, u32[]{:S(2)}, u32[]{:S(2)}) %collective-permute-start.14) | collective-permute-done | bytes 524320 | tf_op jit(solution)/shard_map/ppermute | solution.py:21
  85.5 0.2 multiply_convert_fusion.3
  85.7 1.2 %collective-permute-start.19 = (f16[256,1024]{1,0:T(8,128)(2,1)S(1)}, f16[256,1024]{1,0:T(8,128)(2,1)S(1)}, u32[]{:S(2)}, u32[]{:S(2)}) collective-permute-start(f16[256,1024]{1,0:T(8,128)(2,1)S(1)} %multiply_convert_fusion.3), channel_id=1, source_target_pairs={{0,2},{2,0},{4,6},{6,4},{8,10},{10,8},{12,14},{14,12},{16,18},{18,... | collective-permute-start | bytes 1572872 | tf_op jit(solution)/shard_map/ppermute | solution.py:30
  86.9 1.3 %collective-permute-start.20 = (f16[256,1024]{1,0:T(8,128)(2,1)S(1)}, f16[256,1024]{1,0:T(8,128)(2,1)S(1)}, u32[]{:S(2)}, u32[]{:S(2)}) collective-permute-start(f16[256,1024]{1,0:T(8,128)(2,1)S(1)} %get-tuple-element.167), channel_id=1, source_target_pairs={{0,1},{1,0},{2,3},{3,2},{4,5},{5,4},{6,7},{7,6},{8,9},{9,8},{10,11... | collective-permute-start | bytes 1572872 | tf_op jit(solution)/shard_map/ppermute | solution.py:21
  88.2 2.4 %collective-permute-start.21 = (f16[256,1024]{1,0:T(8,128)(2,1)S(1)}, f16[256,1024]{1,0:T(8,128)(2,1)S(1)}, u32[]{:S(2)}, u32[]{:S(2)}) collective-permute-start(f16[256,1024]{1,0:T(8,128)(2,1)S(1)} %multiply_convert_fusion.3), channel_id=1, source_target_pairs={{2,4},{4,2},{6,8},{8,6},{10,12},{12,10},{14,16},{16,14},{18,20},{2... | collective-permute-start | bytes 1572872 | tf_op jit(solution)/shard_map/ppermute | solution.py:30
  90.6 6.1 %collective-permute-done.17 = f16[256,1024]{1,0:T(8,128)(2,1)S(1)} collective-permute-done((f16[256,1024]{1,0:T(8,128)(2,1)S(1)}, f16[256,1024]{1,0:T(8,128)(2,1)S(1)}, u32[]{:S(2)}, u32[]{:S(2)}) %collective-permute-start.17) | collective-permute-done | bytes 524320 | tf_op jit(solution)/shard_map/ppermute | solution.py:21
  96.7 3.2 %collective-permute-done.18 = f16[256,1024]{1,0:T(8,128)(2,1)S(1)} collective-permute-done((f16[256,1024]{1,0:T(8,128)(2,1)S(1)}, f16[256,1024]{1,0:T(8,128)(2,1)S(1)}, u32[]{:S(2)}, u32[]{:S(2)}) %collective-permute-start.18) | collective-permute-done | bytes 524320 | tf_op jit(solution)/shard_map/ppermute | solution.py:30
  99.9 1.1 broadcast_in_dim.27
  101.0 1.6 %add_dynamic-update-slice_fusion = f32[2048,1024]{1,0:T(8,128)S(1)} fusion(f32[2048,1024]{1,0:T(8,128)S(1)} %broadcast_in_dim.27, f16[256,1024]{1,0:T(8,128)(2,1)} %collective-permute-done.6, f32[512,1024]{1,0:T(8,128)S(1)} %copy-done.4, f16[256,1024]{1,0:T(8,128)(2,1)} %collective-permute-done.4, f16[256,1024]{1,0:T(8,128)(2,1)S(1)} %collective-permute-done.1, ...), kind=kLoop, calls=%fused_computation.36 | loop fusion | flops 2621440 | bytes 3682304 | tf_op jit(solution)/shard_map/dynamic_update_slice | solution.py:93
  102.6 0.2 multiply_convert_fusion.2
  102.9 0.1 collective-permute-start.23
  102.9 0.1 collective-permute-start.22
  103.0 0.4 bitcast_dynamic-update-slice_fusion.6
  103.5 4.5 %collective-permute-done.20 = f16[256,1024]{1,0:T(8,128)(2,1)S(1)} collective-permute-done((f16[256,1024]{1,0:T(8,128)(2,1)S(1)}, f16[256,1024]{1,0:T(8,128)(2,1)S(1)}, u32[]{:S(2)}, u32[]{:S(2)}) %collective-permute-start.20) | collective-permute-done | bytes 524320 | tf_op jit(solution)/shard_map/ppermute | solution.py:21
  107.9 0.2 bitcast_dynamic-update-slice_fusion.5
  108.2 0.4 bitcast_dynamic-update-slice_fusion.4
  108.6 0.4 bitcast_dynamic-update-slice_fusion.3
  109.0 0.4 bitcast_dynamic-update-slice_fusion.2
  109.5 0.4 bitcast_dynamic-update-slice_fusion.1
  110.0 0.0 copy-start.1
  110.0 7.1 %collective-permute-done.23 = f16[256,1024]{1,0:T(8,128)(2,1)S(1)} collective-permute-done((f16[256,1024]{1,0:T(8,128)(2,1)S(1)}, f16[256,1024]{1,0:T(8,128)(2,1)S(1)}, u32[]{:S(2)}, u32[]{:S(2)}) %collective-permute-start.23) | collective-permute-done | bytes 524320 | tf_op jit(solution)/shard_map/ppermute | solution.py:30
  117.1 1.4 %bitcast_dynamic-update-slice_fusion = f32[1,2048,1024]{2,1,0:T(8,128)} fusion(f32[1,2048,1024]{2,1,0:T(8,128)} %copy-done.1, f16[256,1024]{1,0:T(8,128)(2,1)S(1)} %collective-permute-done.23, f32[1280,1024]{1,0:T(8,128)S(1)} %bitcast_subtract_fusion, f16[256,1024]{1,0:T(8,128)(2,1)S(1)} %collective-permute-done.22, ...), kind=kLoop, calls=%fused_computation.27 | loop fusion | flops 2621440 | bytes 3682304 | tf_op jit(solution)/shard_map/dynamic_update_slice | solution.py:93
  (35 shorter events, 0.1 us)
Async XLA Ops:
  0.0 1.5 %copy-start = (bf16[1,896,1024]{2,1,0:T(8,128)(2,1)S(1)}, bf16[1,896,1024]{2,1,0:T(8,128)(2,1)}, u32[]{:S(2)}) copy-start(bf16[1,896,1024]{2,1,0:T(8,128)(2,1)} %param.6) | copy-start | bytes 5505028
  7.5 34.1 %collective-permute-start.3 = (f16[512,1024]{1,0:T(8,128)(2,1)}, f16[512,1024]{1,0:T(8,128)(2,1)}, u32[]{:S(2)}, u32[]{:S(2)}) collective-permute-start(f16[512,1024]{1,0:T(8,128)(2,1)} %get-tuple-element.93), channel_id=1, source_target_pairs={{2,4},{4,2},{6,8},{8,6},{10,12},{12,10},{14,16},{16,14},{18,20},{2... | collective-permute-start | bytes 3145736 | tf_op jit(solution)/shard_map/ppermute | solution.py:30
  10.1 21.9 %collective-permute-start.2 = (f16[512,1024]{1,0:T(8,128)(2,1)}, f16[512,1024]{1,0:T(8,128)(2,1)}, u32[]{:S(2)}, u32[]{:S(2)}) collective-permute-start(f16[512,1024]{1,0:T(8,128)(2,1)} %get-tuple-element.93), channel_id=1, source_target_pairs={{0,2},{2,0},{4,6},{6,4},{8,10},{10,8},{12,14},{14,12},{16,18},{18,... | collective-permute-start | bytes 3145736 | tf_op jit(solution)/shard_map/ppermute | solution.py:30
  15.5 17.7 %collective-permute-start.1 = (f16[256,1024]{1,0:T(8,128)(2,1)}, f16[256,1024]{1,0:T(8,128)(2,1)S(1)}, u32[]{:S(2)}, u32[]{:S(2)}) collective-permute-start(f16[256,1024]{1,0:T(8,128)(2,1)} %fusion.28), channel_id=1, source_target_pairs={{0,1},{1,0},{2,3},{3,2},{4,5},{5,4},{6,7},{7,6},{8,9},{9,8},{10,11... | collective-permute-start | bytes 1572872 | tf_op jit(solution)/shard_map/ppermute | solution.py:21
  22.2 2.5 %copy-start.9 = (s32[16,3]{0,1:T(4,128)S(1)}, s32[16,3]{0,1:T(4,128)}, u32[]{:S(2)}) copy-start(s32[16,3]{0,1:T(4,128)} %param.7) | copy-start | bytes 580
  24.5 17.1 %collective-permute-start = (f16[256,1024]{1,0:T(8,128)(2,1)}, f16[256,1024]{1,0:T(8,128)(2,1)S(1)}, u32[]{:S(2)}, u32[]{:S(2)}) collective-permute-start(f16[256,1024]{1,0:T(8,128)(2,1)} %get-tuple-element.182), channel_id=1, source_target_pairs={{0,1},{1,0},{2,3},{3,2},{4,5},{5,4},{6,7},{7,6},{8,9},{9,8},{10,11... | collective-permute-start | bytes 1572872 | tf_op jit(solution)/shard_map/ppermute | solution.py:21
  31.2 2.0 %copy-start.3 = (f32[512,1024]{1,0:T(8,128)}, f32[512,1024]{1,0:T(8,128)S(1)}, u32[]{:S(2)}) copy-start(f32[512,1024]{1,0:T(8,128)S(1)} %bitcast_subtract_fusion.1) | copy-start | bytes 6291460
  31.9 19.8 %collective-permute-start.5 = (f16[256,1024]{1,0:T(8,128)(2,1)}, f16[256,1024]{1,0:T(8,128)(2,1)S(1)}, u32[]{:S(2)}, u32[]{:S(2)}) collective-permute-start(f16[256,1024]{1,0:T(8,128)(2,1)} %get-tuple-element.94), channel_id=1, source_target_pairs={{0,1},{1,0},{2,3},{3,2},{4,5},{5,4},{6,7},{7,6},{8,9},{9,8},{10,11... | collective-permute-start | bytes 1572872 | tf_op jit(solution)/shard_map/ppermute | solution.py:21
  34.2 17.6 %collective-permute-start.6 = (f16[256,1024]{1,0:T(8,128)(2,1)}, f16[256,1024]{1,0:T(8,128)(2,1)}, u32[]{:S(2)}, u32[]{:S(2)}) collective-permute-start(f16[256,1024]{1,0:T(8,128)(2,1)} %multiply_convert_fusion.8), channel_id=1, source_target_pairs={{2,4},{4,2},{6,8},{8,6},{10,12},{12,10},{14,16},{16,14},{18,20},{2... | collective-permute-start | bytes 1572872 | tf_op jit(solution)/shard_map/ppermute | solution.py:30
  34.2 7.3 %collective-permute-start.4 = (f16[256,1024]{1,0:T(8,128)(2,1)}, f16[256,1024]{1,0:T(8,128)(2,1)}, u32[]{:S(2)}, u32[]{:S(2)}) collective-permute-start(f16[256,1024]{1,0:T(8,128)(2,1)} %multiply_convert_fusion.8), channel_id=1, source_target_pairs={{0,2},{2,0},{4,6},{6,4},{8,10},{10,8},{12,14},{14,12},{16,18},{18,... | collective-permute-start | bytes 1572872 | tf_op jit(solution)/shard_map/ppermute | solution.py:30
  35.1 6.5 %copy-start.4 = (f32[512,1024]{1,0:T(8,128)S(1)}, f32[512,1024]{1,0:T(8,128)}, u32[]{:S(2)}) copy-start(f32[512,1024]{1,0:T(8,128)} %copy-done.3) | copy-start | bytes 6291460
  35.1 6.9 %copy-start.8 = (f16[256,1024]{1,0:T(8,128)(2,1)S(1)}, f16[256,1024]{1,0:T(8,128)(2,1)}, u32[]{:S(2)}) copy-start(f16[256,1024]{1,0:T(8,128)(2,1)} %get-tuple-element.121) | copy-start | bytes 1572868
  35.1 16.7 %copy-start.7 = (f16[256,1024]{1,0:T(8,128)(2,1)S(1)}, f16[256,1024]{1,0:T(8,128)(2,1)}, u32[]{:S(2)}) copy-start(f16[256,1024]{1,0:T(8,128)(2,1)} %get-tuple-element.135) | copy-start | bytes 1572868
  41.5 13.2 %copy-start.2 = (f32[512,1024]{1,0:T(8,128)S(1)}, f32[512,1024]{1,0:T(8,128)}, u32[]{:S(2)}) copy-start(f32[512,1024]{1,0:T(8,128)} %get-tuple-element.129) | copy-start | bytes 6291460
  41.9 11.2 %collective-permute-start.7 = (f16[256,1024]{1,0:T(8,128)(2,1)S(1)}, f16[256,1024]{1,0:T(8,128)(2,1)S(1)}, u32[]{:S(2)}, u32[]{:S(2)}) collective-permute-start(f16[256,1024]{1,0:T(8,128)(2,1)S(1)} %multiply_convert_fusion.7), channel_id=1, source_target_pairs={{0,2},{2,0},{4,6},{6,4},{8,10},{10,8},{12,14},{14,12},{16,18},{18,... | collective-permute-start | bytes 1572872 | tf_op jit(solution)/shard_map/ppermute | solution.py:30
  42.0 21.0 %collective-permute-start.8 = (f16[256,1024]{1,0:T(8,128)(2,1)S(1)}, f16[256,1024]{1,0:T(8,128)(2,1)S(1)}, u32[]{:S(2)}, u32[]{:S(2)}) collective-permute-start(f16[256,1024]{1,0:T(8,128)(2,1)S(1)} %copy-done.8), channel_id=1, source_target_pairs={{0,1},{1,0},{2,3},{3,2},{4,5},{5,4},{6,7},{7,6},{8,9},{9,8},{10,11... | collective-permute-start | bytes 1572872 | tf_op jit(solution)/shard_map/ppermute | solution.py:21
  43.2 19.7 %collective-permute-start.9 = (f16[256,1024]{1,0:T(8,128)(2,1)S(1)}, f16[256,1024]{1,0:T(8,128)(2,1)S(1)}, u32[]{:S(2)}, u32[]{:S(2)}) collective-permute-start(f16[256,1024]{1,0:T(8,128)(2,1)S(1)} %multiply_convert_fusion.7), channel_id=1, source_target_pairs={{2,4},{4,2},{6,8},{8,6},{10,12},{12,10},{14,16},{16,14},{18,20},{2... | collective-permute-start | bytes 1572872 | tf_op jit(solution)/shard_map/ppermute | solution.py:30
  51.8 22.4 %collective-permute-start.11 = (f16[256,1024]{1,0:T(8,128)(2,1)S(1)}, f16[256,1024]{1,0:T(8,128)(2,1)S(1)}, u32[]{:S(2)}, u32[]{:S(2)}) collective-permute-start(f16[256,1024]{1,0:T(8,128)(2,1)S(1)} %copy-done.7), channel_id=1, source_target_pairs={{0,1},{1,0},{2,3},{3,2},{4,5},{5,4},{6,7},{7,6},{8,9},{9,8},{10,11... | collective-permute-start | bytes 1572872 | tf_op jit(solution)/shard_map/ppermute | solution.py:21
  53.2 9.8 %collective-permute-start.10 = (f16[256,1024]{1,0:T(8,128)(2,1)S(1)}, f16[256,1024]{1,0:T(8,128)(2,1)S(1)}, u32[]{:S(2)}, u32[]{:S(2)}) collective-permute-start(f16[256,1024]{1,0:T(8,128)(2,1)S(1)} %multiply_convert_fusion.6), channel_id=1, source_target_pairs={{0,2},{2,0},{4,6},{6,4},{8,10},{10,8},{12,14},{14,12},{16,18},{18,... | collective-permute-start | bytes 1572872 | tf_op jit(solution)/shard_map/ppermute | solution.py:30
  54.8 9.7 %copy-start.6 = (f16[256,1024]{1,0:T(8,128)(2,1)S(1)}, f16[256,1024]{1,0:T(8,128)(2,1)}, u32[]{:S(2)}) copy-start(f16[256,1024]{1,0:T(8,128)(2,1)} %get-tuple-element.144) | copy-start | bytes 1572868
  57.0 20.8 %copy-start.5 = (f16[256,1024]{1,0:T(8,128)(2,1)S(1)}, f16[256,1024]{1,0:T(8,128)(2,1)}, u32[]{:S(2)}) copy-start(f16[256,1024]{1,0:T(8,128)(2,1)} %get-tuple-element.152) | copy-start | bytes 1572868
  57.3 20.2 %collective-permute-start.12 = (f16[256,1024]{1,0:T(8,128)(2,1)S(1)}, f16[256,1024]{1,0:T(8,128)(2,1)S(1)}, u32[]{:S(2)}, u32[]{:S(2)}) collective-permute-start(f16[256,1024]{1,0:T(8,128)(2,1)S(1)} %multiply_convert_fusion.6), channel_id=1, source_target_pairs={{2,4},{4,2},{6,8},{8,6},{10,12},{12,10},{14,16},{16,14},{18,20},{2... | collective-permute-start | bytes 1572872 | tf_op jit(solution)/shard_map/ppermute | solution.py:30
  63.2 14.2 %collective-permute-start.13 = (f16[256,1024]{1,0:T(8,128)(2,1)S(1)}, f16[256,1024]{1,0:T(8,128)(2,1)S(1)}, u32[]{:S(2)}, u32[]{:S(2)}) collective-permute-start(f16[256,1024]{1,0:T(8,128)(2,1)S(1)} %multiply_convert_fusion.5), channel_id=1, source_target_pairs={{0,2},{2,0},{4,6},{6,4},{8,10},{10,8},{12,14},{14,12},{16,18},{18,... | collective-permute-start | bytes 1572872 | tf_op jit(solution)/shard_map/ppermute | solution.py:30
  64.5 21.0 %collective-permute-start.14 = (f16[256,1024]{1,0:T(8,128)(2,1)S(1)}, f16[256,1024]{1,0:T(8,128)(2,1)S(1)}, u32[]{:S(2)}, u32[]{:S(2)}) collective-permute-start(f16[256,1024]{1,0:T(8,128)(2,1)S(1)} %copy-done.6), channel_id=1, source_target_pairs={{0,1},{1,0},{2,3},{3,2},{4,5},{5,4},{6,7},{7,6},{8,9},{9,8},{10,11... | collective-permute-start | bytes 1572872 | tf_op jit(solution)/shard_map/ppermute | solution.py:21
  65.7 19.7 %collective-permute-start.15 = (f16[256,1024]{1,0:T(8,128)(2,1)S(1)}, f16[256,1024]{1,0:T(8,128)(2,1)S(1)}, u32[]{:S(2)}, u32[]{:S(2)}) collective-permute-start(f16[256,1024]{1,0:T(8,128)(2,1)S(1)} %multiply_convert_fusion.5), channel_id=1, source_target_pairs={{2,4},{4,2},{6,8},{8,6},{10,12},{12,10},{14,16},{16,14},{18,20},{2... | collective-permute-start | bytes 1572872 | tf_op jit(solution)/shard_map/ppermute | solution.py:30
  77.7 7.8 %collective-permute-start.16 = (f16[256,1024]{1,0:T(8,128)(2,1)S(1)}, f16[256,1024]{1,0:T(8,128)(2,1)S(1)}, u32[]{:S(2)}, u32[]{:S(2)}) collective-permute-start(f16[256,1024]{1,0:T(8,128)(2,1)S(1)} %multiply_convert_fusion.4), channel_id=1, source_target_pairs={{0,2},{2,0},{4,6},{6,4},{8,10},{10,8},{12,14},{14,12},{16,18},{18,... | collective-permute-start | bytes 1572872 | tf_op jit(solution)/shard_map/ppermute | solution.py:30
  77.8 18.9 %collective-permute-start.17 = (f16[256,1024]{1,0:T(8,128)(2,1)S(1)}, f16[256,1024]{1,0:T(8,128)(2,1)S(1)}, u32[]{:S(2)}, u32[]{:S(2)}) collective-permute-start(f16[256,1024]{1,0:T(8,128)(2,1)S(1)} %copy-done.5), channel_id=1, source_target_pairs={{0,1},{1,0},{2,3},{3,2},{4,5},{5,4},{6,7},{7,6},{8,9},{9,8},{10,11... | collective-permute-start | bytes 1572872 | tf_op jit(solution)/shard_map/ppermute | solution.py:21
  78.1 21.9 %collective-permute-start.18 = (f16[256,1024]{1,0:T(8,128)(2,1)S(1)}, f16[256,1024]{1,0:T(8,128)(2,1)S(1)}, u32[]{:S(2)}, u32[]{:S(2)}) collective-permute-start(f16[256,1024]{1,0:T(8,128)(2,1)S(1)} %multiply_convert_fusion.4), channel_id=1, source_target_pairs={{2,4},{4,2},{6,8},{8,6},{10,12},{12,10},{14,16},{16,14},{18,20},{2... | collective-permute-start | bytes 1572872 | tf_op jit(solution)/shard_map/ppermute | solution.py:30
  85.7 16.9 %collective-permute-start.19 = (f16[256,1024]{1,0:T(8,128)(2,1)S(1)}, f16[256,1024]{1,0:T(8,128)(2,1)S(1)}, u32[]{:S(2)}, u32[]{:S(2)}) collective-permute-start(f16[256,1024]{1,0:T(8,128)(2,1)S(1)} %multiply_convert_fusion.3), channel_id=1, source_target_pairs={{0,2},{2,0},{4,6},{6,4},{8,10},{10,8},{12,14},{14,12},{16,18},{18,... | collective-permute-start | bytes 1572872 | tf_op jit(solution)/shard_map/ppermute | solution.py:30
  86.9 21.0 %collective-permute-start.20 = (f16[256,1024]{1,0:T(8,128)(2,1)S(1)}, f16[256,1024]{1,0:T(8,128)(2,1)S(1)}, u32[]{:S(2)}, u32[]{:S(2)}) collective-permute-start(f16[256,1024]{1,0:T(8,128)(2,1)S(1)} %get-tuple-element.167), channel_id=1, source_target_pairs={{0,1},{1,0},{2,3},{3,2},{4,5},{5,4},{6,7},{7,6},{8,9},{9,8},{10,11... | collective-permute-start | bytes 1572872 | tf_op jit(solution)/shard_map/ppermute | solution.py:21
  88.2 21.3 %collective-permute-start.21 = (f16[256,1024]{1,0:T(8,128)(2,1)S(1)}, f16[256,1024]{1,0:T(8,128)(2,1)S(1)}, u32[]{:S(2)}, u32[]{:S(2)}) collective-permute-start(f16[256,1024]{1,0:T(8,128)(2,1)S(1)} %multiply_convert_fusion.3), channel_id=1, source_target_pairs={{2,4},{4,2},{6,8},{8,6},{10,12},{12,10},{14,16},{16,14},{18,20},{2... | collective-permute-start | bytes 1572872 | tf_op jit(solution)/shard_map/ppermute | solution.py:30
  102.9 14.2 %collective-permute-start.23 = (f16[256,1024]{1,0:T(8,128)(2,1)S(1)}, f16[256,1024]{1,0:T(8,128)(2,1)S(1)}, u32[]{:S(2)}, u32[]{:S(2)}) collective-permute-start(f16[256,1024]{1,0:T(8,128)(2,1)S(1)} %multiply_convert_fusion.2), channel_id=1, source_target_pairs={{2,4},{4,2},{6,8},{8,6},{10,12},{12,10},{14,16},{16,14},{18,20},{2... | collective-permute-start | bytes 1572872 | tf_op jit(solution)/shard_map/ppermute | solution.py:30
  102.9 14.2 %collective-permute-start.22 = (f16[256,1024]{1,0:T(8,128)(2,1)S(1)}, f16[256,1024]{1,0:T(8,128)(2,1)S(1)}, u32[]{:S(2)}, u32[]{:S(2)}) collective-permute-start(f16[256,1024]{1,0:T(8,128)(2,1)S(1)} %multiply_convert_fusion.2), channel_id=1, source_target_pairs={{0,2},{2,0},{4,6},{6,4},{8,10},{10,8},{12,14},{14,12},{16,18},{18,... | collective-permute-start | bytes 1572872 | tf_op jit(solution)/shard_map/ppermute | solution.py:30
  110.0 7.1 %copy-start.1 = (f32[1,2048,1024]{2,1,0:T(8,128)}, f32[1,2048,1024]{2,1,0:T(8,128)S(1)}, u32[]{:S(2)}) copy-start(f32[1,2048,1024]{2,1,0:T(8,128)S(1)} %bitcast_dynamic-update-slice_fusion.1) | copy-start | bytes 25165828

commit v12 on v11

--- a/solution.py
+++ b/solution.py
@@ -9,8 +9,8 @@
 RATE = 0.03
 LARGEST = 6.0
 WIRE = jnp.float16
-STEP = 256
-FIRST = 256
+STEP = 240
+FIRST = 192
 AHEAD = 3
 MIXLAG = 5
 
@@ -44,15 +44,18 @@
     scale = wire_scale(features.shape[0] * shards)
     replica = lax.axis_index("blk")
     shard = lax.axis_index("fsdp")
-    row = lax.dynamic_slice_in_dim(mix, replica, 1, axis=0).astype(jnp.float32) / MIX_DENOM
-    left, own, right = row[:, 0:1], row[:, 1:2], row[:, 2:3]
-    even = replica % 2 == 0
-    sides = [jnp.where(even, right, left) / scale, own, jnp.where(even, left, right) / scale]
-    coeff = jnp.broadcast_to(jnp.concatenate(sides, axis=0), (3, weights.shape[1]))
+    def coefficients(mix):
+        row = lax.dynamic_slice_in_dim(mix, replica, 1, axis=0).astype(jnp.float32) / MIX_DENOM
+        left, own, right = row[:, 0:1], row[:, 1:2], row[:, 2:3]
+        even = replica % 2 == 0
+        sides = [jnp.where(even, right, left) / scale, own, jnp.where(even, left, right) / scale]
+        return jnp.broadcast_to(jnp.concatenate(sides, axis=0), (3, weights.shape[1]))
+
     first = min(FIRST, rows // 2)
     main = rows - first
     cuts = list(range(0, main, STEP)) + [main]
     chunks = len(cuts) - 1
+    middle = min(1, chunks - 1)
 
     def owner(away, shard=shard):
         other = shard + away
@@ -98,10 +101,11 @@
     out = jnp.zeros_like(weights)
     split = cuts[min(2, chunks)]
     terms = {0: for_others(0, cuts[1])}
+
+    terms[0], later = lax.optimization_barrier((terms[0], shard))
     arrived = {0: add_over_fsdp(terms[0])}
-
-    parts = [own_part(shard, main, rows)]
-    parts += [-RATE * partial(owner(away), main, first) for away in range(1, shards)]
+    parts = [own_part(later, main, rows)]
+    parts += [-RATE * partial(owner(away, later), main, first) for away in range(1, shards)]
     parts = jnp.concatenate(parts, axis=0)
     parts, sent = lax.optimization_barrier((parts, (parts * scale).astype(WIRE)))
     far[-1] = swapped(sent, "blk", 1)
@@ -136,8 +140,9 @@
         sent, base, out, later = lax.optimization_barrier((sent, base, out, shard))
         if chunk == 0 and split < main:
             base.append(own_part(later, split, main))
-        if chunk == min(1, chunks - 1):
-            coeff, parts, sent = lax.optimization_barrier((coeff, parts, sent))
+        if chunk == middle:
+            mix, parts, sent = lax.optimization_barrier((mix, parts, sent))
+            coeff = lax.optimization_barrier(coefficients(mix))
             parts = mixture(near[-1], parts, far[-1])
             back = [
                 (parts[away * first:(away + 1) * first] * scale).astype(WIRE) for away in range(1, shards)
@@ -147,7 +152,7 @@
         if after < chunks:
             terms[after], sent = lax.optimization_barrier((terms[after], sent))
             arrived[after] = add_over_fsdp(terms[after])
-        if after == max(chunks, AHEAD):
+        if chunk == max(chunks - AHEAD, middle):
             back, sent = lax.optimization_barrier((back, sent))
             back = add_over_fsdp(back)
         far[chunk] = swapped(sent, "blk", 1)

time: 119 us -> 129 us (1.084)
  waiting for transfers between devices: 51.5 us -> 33.5 us
  starting transfers between devices: 23.9 us -> 38.9 us
  matrix products: 21.5 us -> 27.9 us
  other arithmetic: 13.2 us -> 17.9 us
  local copies, waits for them, and re-layouts: 5.48 us -> 7.44 us
    ppermute x8 -> x9, waiting for transfers between devices: 37.8 us -> 0.02 us  [from_behind(): return lax.ppermute(value, axis, pairs)]
    ppermute x16 -> x18, waiting for transfers between devices: 13.7 us -> 33.5 us  [swapped(): return lax.ppermute(value, axis, pairs)]
    ppermute x16 -> x18, starting transfers between devices: 15.9 us -> 26.9 us  [swapped(): return lax.ppermute(value, axis, pairs)]
    dot_general x6, matrix products: 21.5 us -> 27.9 us  [partial(): lax.dot_general(block, cot_local, (((0,), (0,)), ((), ())), preferred_ele...]
    ppermute x8 -> x9, starting transfers between devices: 7.98 us -> 12 us  [from_behind(): return lax.ppermute(value, axis, pairs)]
    convert_element_type x7 -> x8, other arithmetic: 2.32 us -> 5.49 us  [on_device(): sent = (u_of(chunk) * scale).astype(WIRE)]
    dynamic_update_slice x7 -> x8, other arithmetic: 5.23 us -> 7.21 us  [mix_into(): return lax.dynamic_update_slice_in_dim(out, value, cuts[chunk], axis=0)]
    slice x1 -> x2, local copies, waits for them, and re-layouts: 2.21 us -> 2.94 us  [on_device(): term[cuts[chunk] - cuts[1]:cuts[chunk + 1] - cuts[1]]]
  transfers between devices with their start and end apart: 24 -> 27, of which waited for: 9 -> 6; matrix products, arithmetic and copies ran while one was open for 26% -> 31% of each run, Pallas kernels for 0% -> 0%
where the time goes in v12:
time: 129 us
  starting transfers between devices  38.9 us (30%)
  waiting for transfers between devices  33.5 us (26%)
  matrix products  27.9 us (22%)
  other arithmetic  17.9 us (14%)
  local copies, waits for them, and re-layouts  7.44 us (6%)
  between operations  2.93 us (2%)
    ppermute x18, waiting for transfers between devices, swapped(): return lax.ppermute(value, axis, pairs)  33.5 us
    dot_general x6, matrix products, partial(): lax.dot_general(block, cot_local, (((0,), (0,)), ((), ())), preferred_ele...  27.9 us
    ppermute x18, starting transfers between devices, swapped(): return lax.ppermute(value, axis, pairs)  26.9 us
    ppermute x9, starting transfers between devices, from_behind(): return lax.ppermute(value, axis, pairs)  12 us
    dynamic_update_slice x8, other arithmetic, mix_into(): return lax.dynamic_update_slice_in_dim(out, value, cuts[chunk], axis=0)  7.21 us
    convert_element_type x8, other arithmetic, on_device(): sent = (u_of(chunk) * scale).astype(WIRE)  5.49 us
    slice x2, local copies, waits for them, and re-layouts, on_device(): term[cuts[chunk] - cuts[1]:cuts[chunk + 1] - cuts[1]]  2.94 us
    unnamed x20, local copies, waits for them, and re-layouts  2.78 us
  transfers between devices with their start and end apart: 27, of which 6 were waited for; matrix products, arithmetic and copies ran while one was open for 31% of the time, Pallas kernels for 0%

profile of v12, /device:TPU:1, one launch (start us, length us, event | category | flops | bytes accessed | tf_op | source)
XLA Modules:
  0.0 128.6 jit_solution(4172878038306951611)
XLA Ops:
  0.0 1.5 %copy-done = bf16[1,896,1024]{2,1,0:T(8,128)(2,1)S(1)} copy-done((bf16[1,896,1024]{2,1,0:T(8,128)(2,1)S(1)}, bf16[1,896,1024]{2,1,0:T(8,128)(2,1)}, u32[]{:S(2)}) %copy-start) | copy-done | bytes 1835032
  1.5 2.7 %fusion.28 = f16[240,1024]{1,0:T(8,128)(2,1)} fusion(bf16[1,896,1024]{2,1,0:T(8,128)(2,1)S(1)} %copy-done, bf16[1,896,4096]{2,1,0:T(8,128)(2,1)} %param.5, s32[]{:T(128)S(6)} %select_n.50), kind=kOutput, calls=%fused_computation.24 | convolution fusion | flops 440893440 | bytes 2785284 | tf_op jit(solution)/shard_map/dot_general | solution.py:66
  4.2 2.6 %fusion.25 = f32[192,1024]{1,0:T(8,128)} fusion(bf16[1,896,1024]{2,1,0:T(8,128)(2,1)S(1)} %copy-done, bf16[1,896,4096]{2,1,0:T(8,128)(2,1)} %param.5, s32[]{:T(128)S(6)} %select_n.53), kind=kOutput, calls=%fused_computation.23 | convolution fusion | flops 352518144 | bytes 3080196 | tf_op jit(solution)/shard_map/dot_general | solution.py:66
  6.7 2.0 %fusion.22 = f32[192,1024]{1,0:T(8,128)S(1)} fusion(bf16[1,896,1024]{2,1,0:T(8,128)(2,1)S(1)} %copy-done, f32[1,2048,1024]{2,1,0:T(8,128)} %param.4, bf16[1,896,4096]{2,1,0:T(8,128)(2,1)} %param.5, s32[]{:T(128)S(6)} %select_n.51), kind=kOutput, calls=%fused_computation.22 | convolution fusion | flops 352714752 | bytes 3866628 | tf_op jit(solution)/shard_map/dot_general | solution.py:66
  8.8 2.3 %multiply_convert_fusion.1 = (f16[384,1024]{1,0:T(8,128)(2,1)}, f32[384,1024]{1,0:T(8,128)S(1)}) fusion(f32[192,1024]{1,0:T(8,128)} %fusion.25, f32[192,1024]{1,0:T(8,128)S(1)} %fusion.22), kind=kLoop, calls=%fused_computation.19 | loop fusion | flops 1179648 | bytes 3932160 | tf_op jit(solution)/shard_map/convert_element_type | solution.py:110
  11.2 2.5 %collective-permute-start.3 = (f16[384,1024]{1,0:T(8,128)(2,1)}, f16[384,1024]{1,0:T(8,128)(2,1)}, u32[]{:S(2)}, u32[]{:S(2)}) collective-permute-start(f16[384,1024]{1,0:T(8,128)(2,1)} %get-tuple-element.109), channel_id=1, source_target_pairs={{2,4},{4,2},{6,8},{8,6},{10,12},{12,10},{14,16},{16,14},{18,20},{2... | collective-permute-start | bytes 2359304 | tf_op jit(solution)/shard_map/ppermute | solution.py:30
  13.7 1.2 collective-permute-start.1
  15.0 7.8 %multiply_convert_fusion = f16[1616,1024]{1,0:T(8,128)(2,1)S(1)} fusion(bf16[1,896,4096]{2,1,0:T(8,128)(2,1)} %param.5, s32[]{:T(128)S(6)} %select_n.55, bf16[1,896,1024]{2,1,0:T(8,128)(2,1)S(1)} %copy-done), kind=kOutput, calls=%fused_computation | convolution fusion | flops 2968682496 | bytes 8126468 | tf_op jit(solution)/shard_map/dot_general | solution.py:66
  22.8 2.1 %fusion.48 = (f16[240,1024]{1,0:T(8,128)(2,1)}, f16[240,1024]{1,0:T(8,128)(2,1)}, f16[240,1024]{1,0:T(8,128)(2,1)}, f16[240,1024]{1,0:T(8,128)(2,1)}, f16[240,1024]{1,0:T(8,128)(2,1)}, /*index=5*/f16[240,1024]{1,0:T(8,128)(2,1)}) fusion(f16[1616,1024]{1,0:T(8,128)(2,1)S(1)} %multiply_convert_fusion), kind=kLoop, calls=%fused_computation.70 | loop fusion | bytes 5898240 | tf_op jit(solution)/shard_map/slice | solution.py:121
  24.9 0.2 collective-permute-start
  25.1 0.8 slice.178
  26.0 3.2 %bitcast_subtract_fusion.1 = f32[480,1024]{1,0:T(8,128)S(1)} fusion(f32[1,2048,1024]{2,1,0:T(8,128)} %param.4, bf16[1,896,1024]{2,1,0:T(8,128)(2,1)S(1)} %copy-done, bf16[1,896,4096]{2,1,0:T(8,128)(2,1)} %param.5, s32[]{:T(128)S(6)} %select_n.56), kind=kOutput, calls=%fused_computation.6 | convolution fusion | flops 881786880 | bytes 6684676 | tf_op jit(solution)/shard_map/dot_general | solution.py:66
  29.3 1.2 copy-done.2
  30.5 2.1 %multiply_convert_fusion.8 = f16[240,1024]{1,0:T(8,128)(2,1)} fusion(f16[240,1024]{1,0:T(8,128)(2,1)} %collective-permute-done.1, f32[480,1024]{1,0:T(8,128)S(1)} %bitcast_subtract_fusion.1), kind=kLoop, calls=%fused_computation.44 | loop fusion | flops 1228800 | bytes 1966080 | tf_op jit(solution)/shard_map/convert_element_type | solution.py:139
  32.6 4.1 %collective-permute-start.4 = (f16[240,1024]{1,0:T(8,128)(2,1)}, f16[240,1024]{1,0:T(8,128)(2,1)}, u32[]{:S(2)}, u32[]{:S(2)}) collective-permute-start(f16[240,1024]{1,0:T(8,128)(2,1)} %multiply_convert_fusion.8), channel_id=1, source_target_pairs={{0,2},{2,0},{4,6},{6,4},{8,10},{10,8},{12,14},{14,12},{16,18},{18,... | collective-permute-start | bytes 1474568 | tf_op jit(solution)/shard_map/ppermute | solution.py:30
  36.7 1.2 collective-permute-start.5
  37.9 9.5 %bitcast_subtract_fusion = f32[1376,1024]{1,0:T(8,128)S(1)} fusion(f32[1,2048,1024]{2,1,0:T(8,128)} %param.4, bf16[1,896,4096]{2,1,0:T(8,128)(2,1)} %param.5, s32[]{:T(128)S(6)} %select_n.57, bf16[1,896,1024]{2,1,0:T(8,128)(2,1)S(1)} %copy-done), kind=kOutput, calls=%fused_computation.1 | convolution fusion | flops 2527789056 | bytes 15630340 | tf_op jit(solution)/shard_map/dot_general | solution.py:66
  47.5 0.3 collective-permute-start.8
  47.8 1.2 multiply_convert_fusion.7
  49.0 1.3 collective-permute-start.7
  50.3 0.1 fusion.47
  50.3 0.6 fusion.50
  53.5 1.2 collective-permute-start.9
  54.7 0.7 maximum_bitcast_fusion
  55.4 0.1 broadcast_in_dim.29
  55.5 1.3 %collective-permute-start.11 = (f16[240,1024]{1,0:T(8,128)(2,1)S(1)}, f16[240,1024]{1,0:T(8,128)(2,1)S(1)}, u32[]{:S(2)}, u32[]{:S(2)}) collective-permute-start(f16[240,1024]{1,0:T(8,128)(2,1)S(1)} %copy-done.6), channel_id=1, source_target_pairs={{0,1},{1,0},{2,3},{3,2},{4,5},{5,4},{6,7},{7,6},{8,9},{9,8},{10,11... | collective-permute-start | bytes 1474568 | tf_op jit(solution)/shard_map/ppermute | solution.py:21
  56.9 1.3 multiply_convert_fusion.6
  58.1 2.5 %collective-permute-start.10 = (f16[240,1024]{1,0:T(8,128)(2,1)S(1)}, f16[240,1024]{1,0:T(8,128)(2,1)S(1)}, u32[]{:S(2)}, u32[]{:S(2)}) collective-permute-start(f16[240,1024]{1,0:T(8,128)(2,1)S(1)} %multiply_convert_fusion.6), channel_id=1, source_target_pairs={{0,2},{2,0},{4,6},{6,4},{8,10},{10,8},{12,14},{14,12},{16,18},{18,... | collective-permute-start | bytes 1474568 | tf_op jit(solution)/shard_map/ppermute | solution.py:30
  60.6 1.9 %multiply_add_fusion = f32[384,1024]{1,0:T(8,128)S(1)} fusion(f16[384,1024]{1,0:T(8,128)(2,1)} %collective-permute-done.3, f32[384,1024]{1,0:T(8,128)S(1)} %get-tuple-element.145, f16[384,1024]{1,0:T(8,128)(2,1)} %collective-permute-done.2, f32[1024]{0:T(1024)S(1)} %bitcast.80, f32[1024]{0:T(1024)S(1)} %bitcast.89, f32[1024]{0:T(1024)S(1)} %bitcast.71), kind=kLoop, calls=%fused_computation.18 | loop fusion | flops 2752512 | bytes 4730880 | tf_op jit(solution)/shard_map/add | solution.py:91
  62.5 0.1 fusion.33
  62.6 0.1 collective-permute-start.12
  62.7 8.3 %collective-permute-done.9 = f16[240,1024]{1,0:T(8,128)(2,1)S(1)} collective-permute-done((f16[240,1024]{1,0:T(8,128)(2,1)S(1)}, f16[240,1024]{1,0:T(8,128)(2,1)S(1)}, u32[]{:S(2)}, u32[]{:S(2)}) %collective-permute-start.9) | collective-permute-done | bytes 491552 | tf_op jit(solution)/shard_map/ppermute | solution.py:30
  71.0 0.2 multiply_convert_fusion.5
  71.2 0.1 collective-permute-start.13
  71.3 2.7 %collective-permute-start.14 = (f16[240,1024]{1,0:T(8,128)(2,1)S(1)}, f16[240,1024]{1,0:T(8,128)(2,1)S(1)}, u32[]{:S(2)}, u32[]{:S(2)}) collective-permute-start(f16[240,1024]{1,0:T(8,128)(2,1)S(1)} %copy-done.5), channel_id=1, source_target_pairs={{0,1},{1,0},{2,3},{3,2},{4,5},{5,4},{6,7},{7,6},{8,9},{9,8},{10,11... | collective-permute-start | bytes 1474568 | tf_op jit(solution)/shard_map/ppermute | solution.py:21
  74.0 1.4 %collective-permute-start.15 = (f16[240,1024]{1,0:T(8,128)(2,1)S(1)}, f16[240,1024]{1,0:T(8,128)(2,1)S(1)}, u32[]{:S(2)}, u32[]{:S(2)}) collective-permute-start(f16[240,1024]{1,0:T(8,128)(2,1)S(1)} %multiply_convert_fusion.5), channel_id=1, source_target_pairs={{2,4},{4,2},{6,8},{8,6},{10,12},{12,10},{14,16},{16,14},{18,20},{2... | collective-permute-start | bytes 1474568 | tf_op jit(solution)/shard_map/ppermute | solution.py:30
  75.4 2.6 %collective-permute-done.12 = f16[240,1024]{1,0:T(8,128)(2,1)S(1)} collective-permute-done((f16[240,1024]{1,0:T(8,128)(2,1)S(1)}, f16[240,1024]{1,0:T(8,128)(2,1)S(1)}, u32[]{:S(2)}, u32[]{:S(2)}) %collective-permute-start.12) | collective-permute-done | bytes 491552 | tf_op jit(solution)/shard_map/ppermute | solution.py:30
  77.9 0.2 multiply_convert_fusion.4
  78.2 1.3 %collective-permute-start.17 = (f16[240,1024]{1,0:T(8,128)(2,1)S(1)}, f16[240,1024]{1,0:T(8,128)(2,1)S(1)}, u32[]{:S(2)}, u32[]{:S(2)}) collective-permute-start(f16[240,1024]{1,0:T(8,128)(2,1)S(1)} %copy-done.4), channel_id=1, source_target_pairs={{0,1},{1,0},{2,3},{3,2},{4,5},{5,4},{6,7},{7,6},{8,9},{9,8},{10,11... | collective-permute-start | bytes 1474568 | tf_op jit(solution)/shard_map/ppermute | solution.py:21
  79.6 6.4 %collective-permute-start.18 = (f16[240,1024]{1,0:T(8,128)(2,1)S(1)}, f16[240,1024]{1,0:T(8,128)(2,1)S(1)}, u32[]{:S(2)}, u32[]{:S(2)}) collective-permute-start(f16[240,1024]{1,0:T(8,128)(2,1)S(1)} %multiply_convert_fusion.4), channel_id=1, source_target_pairs={{2,4},{4,2},{6,8},{8,6},{10,12},{12,10},{14,16},{16,14},{18,20},{2... | collective-permute-start | bytes 1474568 | tf_op jit(solution)/shard_map/ppermute | solution.py:30
  85.9 7.8 %collective-permute-done.15 = f16[240,1024]{1,0:T(8,128)(2,1)S(1)} collective-permute-done((f16[240,1024]{1,0:T(8,128)(2,1)S(1)}, f16[240,1024]{1,0:T(8,128)(2,1)S(1)}, u32[]{:S(2)}, u32[]{:S(2)}) %collective-permute-start.15) | collective-permute-done | bytes 491552 | tf_op jit(solution)/shard_map/ppermute | solution.py:30
  93.7 0.2 multiply_convert_fusion.3
  93.9 0.1 collective-permute-start.19
  94.0 1.3 %collective-permute-start.20 = (f16[176,1024]{1,0:T(8,128)(2,1)S(1)}, f16[176,1024]{1,0:T(8,128)(2,1)S(1)}, u32[]{:S(2)}, u32[]{:S(2)}) collective-permute-start(f16[176,1024]{1,0:T(8,128)(2,1)S(1)} %copy-done.8), channel_id=1, source_target_pairs={{0,1},{1,0},{2,3},{3,2},{4,5},{5,4},{6,7},{7,6},{8,9},{9,8},{10,11... | collective-permute-start | bytes 1081352 | tf_op jit(solution)/shard_map/ppermute | solution.py:21
  95.4 1.1 collective-permute-start.21
  96.4 1.1 broadcast_in_dim.27
  97.5 1.7 %add_dynamic-update-slice_fusion.1 = f32[2048,1024]{1,0:T(8,128)S(1)} fusion(f32[2048,1024]{1,0:T(8,128)S(1)} %broadcast_in_dim.27, f16[240,1024]{1,0:T(8,128)(2,1)} %collective-permute-done.6, f32[480,1024]{1,0:T(8,128)S(1)} %copy-done.3, f16[240,1024]{1,0:T(8,128)(2,1)} %collective-permute-done.4, f16[240,1024]{1,0:T(8,128)(2,1)} %collective-permute-done.1, ...), kind=kLoop, calls=%fused_computation.33 | loop fusion | flops 2457600 | bytes 3452928 | tf_op jit(solution)/shard_map/dynamic_update_slice | solution.py:96
  99.2 0.2 multiply_convert_fusion.2
  99.4 2.3 %collective-permute-start.22 = (f16[240,1024]{1,0:T(8,128)(2,1)S(1)}, f16[240,1024]{1,0:T(8,128)(2,1)S(1)}, u32[]{:S(2)}, u32[]{:S(2)}) collective-permute-start(f16[240,1024]{1,0:T(8,128)(2,1)S(1)} %multiply_convert_fusion.2), channel_id=1, source_target_pairs={{0,2},{2,0},{4,6},{6,4},{8,10},{10,8},{12,14},{14,12},{16,18},{18,... | collective-permute-start | bytes 1474568 | tf_op jit(solution)/shard_map/ppermute | solution.py:30
  101.8 2.4 %collective-permute-start.23 = (f16[192,1024]{1,0:T(8,128)(2,1)S(1)}, f16[192,1024]{1,0:T(8,128)(2,1)S(1)}, u32[]{:S(2)}, u32[]{:S(2)}) collective-permute-start(f16[192,1024]{1,0:T(8,128)(2,1)S(1)} %get-tuple-element.196), channel_id=1, source_target_pairs={{0,1},{1,0},{2,3},{3,2},{4,5},{5,4},{6,7},{7,6},{8,9},{9,8},{10,11... | collective-permute-start | bytes 1179656 | tf_op jit(solution)/shard_map/ppermute | solution.py:21
  104.2 2.8 %collective-permute-start.24 = (f16[240,1024]{1,0:T(8,128)(2,1)S(1)}, f16[240,1024]{1,0:T(8,128)(2,1)S(1)}, u32[]{:S(2)}, u32[]{:S(2)}) collective-permute-start(f16[240,1024]{1,0:T(8,128)(2,1)S(1)} %multiply_convert_fusion.2), channel_id=1, source_target_pairs={{2,4},{4,2},{6,8},{8,6},{10,12},{12,10},{14,16},{16,14},{18,20},{2... | collective-permute-start | bytes 1474568 | tf_op jit(solution)/shard_map/ppermute | solution.py:30
  107.0 2.6 %collective-permute-done.21 = f16[240,1024]{1,0:T(8,128)(2,1)S(1)} collective-permute-done((f16[240,1024]{1,0:T(8,128)(2,1)S(1)}, f16[240,1024]{1,0:T(8,128)(2,1)S(1)}, u32[]{:S(2)}, u32[]{:S(2)}) %collective-permute-start.21) | collective-permute-done | bytes 491552 | tf_op jit(solution)/shard_map/ppermute | solution.py:30
  109.5 1.4 %add_dynamic-update-slice_fusion = f32[2048,1024]{1,0:T(8,128)S(1)} fusion(f32[2048,1024]{1,0:T(8,128)S(1)} %add_dynamic-update-slice_fusion.1, f16[240,1024]{1,0:T(8,128)(2,1)S(1)} %collective-permute-done.9, f32[480,1024]{1,0:T(8,128)S(1)} %copy-done.3, f16[240,1024]{1,0:T(8,128)(2,1)S(1)} %collective-permute-done.7, ...), kind=kLoop, calls=%fused_computation.30 | loop fusion | flops 2457600 | bytes 3452928 | tf_op jit(solution)/shard_map/dynamic_update_slice | solution.py:96
  111.0 0.1 multiply_convert_fusion.9
  111.2 0.9 collective-permute-start.26
  112.1 1.4 %bitcast_dynamic-update-slice_fusion.4 = f32[1,2048,1024]{2,1,0:T(8,128)S(1)} fusion(f32[1,2048,1024]{2,1,0:T(8,128)S(1)} %bitcast.70, f16[240,1024]{1,0:T(8,128)(2,1)S(1)} %collective-permute-done.12, f32[1376,1024]{1,0:T(8,128)S(1)} %bitcast_subtract_fusion, f16[240,1024]{1,0:T(8,128)(2,1)S(1)} %collective-permute-done.10, ...), kind=kLoop, calls=%fused_computation.29 | loop fusion | flops 2457600 | bytes 3452928 | tf_op jit(solution)/shard_map/dynamic_update_slice | solution.py:96
  113.5 0.1 bitcast_dynamic-update-slice_fusion.5
  113.7 0.4 bitcast_dynamic-update-slice_fusion.3
  114.0 0.4 bitcast_dynamic-update-slice_fusion.2
  114.4 0.4 bitcast_dynamic-update-slice_fusion.1
  114.8 7.5 %collective-permute-done.24 = f16[240,1024]{1,0:T(8,128)(2,1)S(1)} collective-permute-done((f16[240,1024]{1,0:T(8,128)(2,1)S(1)}, f16[240,1024]{1,0:T(8,128)(2,1)S(1)}, u32[]{:S(2)}, u32[]{:S(2)}) %collective-permute-start.24) | collective-permute-done | bytes 491552 | tf_op jit(solution)/shard_map/ppermute | solution.py:30
  122.3 0.4 bitcast_dynamic-update-slice_fusion
  122.7 4.8 %collective-permute-done.26 = f16[176,1024]{1,0:T(8,128)(2,1)S(1)} collective-permute-done((f16[176,1024]{1,0:T(8,128)(2,1)S(1)}, f16[176,1024]{1,0:T(8,128)(2,1)S(1)}, u32[]{:S(2)}, u32[]{:S(2)}) %collective-permute-start.26) | collective-permute-done | bytes 360480 | tf_op jit(solution)/shard_map/ppermute | solution.py:30
  127.5 1.1 bitcast_dynamic-update-slice_fusion.6
  (44 shorter events, 0.3 us)
Async XLA Ops:
  0.0 1.5 %copy-start = (bf16[1,896,1024]{2,1,0:T(8,128)(2,1)S(1)}, bf16[1,896,1024]{2,1,0:T(8,128)(2,1)}, u32[]{:S(2)}) copy-start(bf16[1,896,1024]{2,1,0:T(8,128)(2,1)} %param.6) | copy-start | bytes 5505028
  11.1 18.1 %collective-permute-start.2 = (f16[384,1024]{1,0:T(8,128)(2,1)}, f16[384,1024]{1,0:T(8,128)(2,1)}, u32[]{:S(2)}, u32[]{:S(2)}) collective-permute-start(f16[384,1024]{1,0:T(8,128)(2,1)} %get-tuple-element.109), channel_id=1, source_target_pairs={{0,2},{2,0},{4,6},{6,4},{8,10},{10,8},{12,14},{14,12},{16,18},{18,... | collective-permute-start | bytes 2359304 | tf_op jit(solution)/shard_map/ppermute | solution.py:30
  11.2 36.3 %collective-permute-start.3 = (f16[384,1024]{1,0:T(8,128)(2,1)}, f16[384,1024]{1,0:T(8,128)(2,1)}, u32[]{:S(2)}, u32[]{:S(2)}) collective-permute-start(f16[384,1024]{1,0:T(8,128)(2,1)} %get-tuple-element.109), channel_id=1, source_target_pairs={{2,4},{4,2},{6,8},{8,6},{10,12},{12,10},{14,16},{16,14},{18,20},{2... | collective-permute-start | bytes 2359304 | tf_op jit(solution)/shard_map/ppermute | solution.py:30
  13.7 15.5 %collective-permute-start.1 = (f16[240,1024]{1,0:T(8,128)(2,1)}, f16[240,1024]{1,0:T(8,128)(2,1)}, u32[]{:S(2)}, u32[]{:S(2)}) collective-permute-start(f16[240,1024]{1,0:T(8,128)(2,1)} %fusion.28), channel_id=1, source_target_pairs={{0,1},{1,0},{2,3},{3,2},{4,5},{5,4},{6,7},{7,6},{8,9},{9,8},{10,11... | collective-permute-start | bytes 1474568 | tf_op jit(solution)/shard_map/ppermute | solution.py:21
  24.9 22.5 %collective-permute-start = (f16[240,1024]{1,0:T(8,128)(2,1)}, f16[240,1024]{1,0:T(8,128)(2,1)}, u32[]{:S(2)}, u32[]{:S(2)}) collective-permute-start(f16[240,1024]{1,0:T(8,128)(2,1)} %get-tuple-element.210), channel_id=1, source_target_pairs={{0,1},{1,0},{2,3},{3,2},{4,5},{5,4},{6,7},{7,6},{8,9},{9,8},{10,11... | collective-permute-start | bytes 1474568 | tf_op jit(solution)/shard_map/ppermute | solution.py:21
  29.2 1.3 copy-start.2
  32.6 15.2 %collective-permute-start.4 = (f16[240,1024]{1,0:T(8,128)(2,1)}, f16[240,1024]{1,0:T(8,128)(2,1)}, u32[]{:S(2)}, u32[]{:S(2)}) collective-permute-start(f16[240,1024]{1,0:T(8,128)(2,1)} %multiply_convert_fusion.8), channel_id=1, source_target_pairs={{0,2},{2,0},{4,6},{6,4},{8,10},{10,8},{12,14},{14,12},{16,18},{18,... | collective-permute-start | bytes 1474568 | tf_op jit(solution)/shard_map/ppermute | solution.py:30
  36.7 18.8 %collective-permute-start.6 = (f16[240,1024]{1,0:T(8,128)(2,1)}, f16[240,1024]{1,0:T(8,128)(2,1)}, u32[]{:S(2)}, u32[]{:S(2)}) collective-permute-start(f16[240,1024]{1,0:T(8,128)(2,1)} %multiply_convert_fusion.8), channel_id=1, source_target_pairs={{2,4},{4,2},{6,8},{8,6},{10,12},{12,10},{14,16},{16,14},{18,20},{2... | collective-permute-start | bytes 1474568 | tf_op jit(solution)/shard_map/ppermute | solution.py:30
  36.7 18.8 %collective-permute-start.5 = (f16[240,1024]{1,0:T(8,128)(2,1)}, f16[240,1024]{1,0:T(8,128)(2,1)}, u32[]{:S(2)}, u32[]{:S(2)}) collective-permute-start(f16[240,1024]{1,0:T(8,128)(2,1)} %get-tuple-element.110), channel_id=1, source_target_pairs={{0,1},{1,0},{2,3},{3,2},{4,5},{5,4},{6,7},{7,6},{8,9},{9,8},{10,11... | collective-permute-start | bytes 1474568 | tf_op jit(solution)/shard_map/ppermute | solution.py:21
  37.9 9.6 %copy-start.7 = (f16[240,1024]{1,0:T(8,128)(2,1)S(1)}, f16[240,1024]{1,0:T(8,128)(2,1)}, u32[]{:S(2)}) copy-start(f16[240,1024]{1,0:T(8,128)(2,1)} %get-tuple-element.137) | copy-start | bytes 1474564
  37.9 9.9 %copy-start.3 = (f32[480,1024]{1,0:T(8,128)S(1)}, f32[480,1024]{1,0:T(8,128)}, u32[]{:S(2)}) copy-start(f32[480,1024]{1,0:T(8,128)} %copy-done.2) | copy-start | bytes 5898244
  37.9 12.4 %copy-start.9 = (s32[16,3]{0,1:T(4,128)S(1)}, s32[16,3]{0,1:T(4,128)}, u32[]{:S(2)}) copy-start(s32[16,3]{0,1:T(4,128)} %param.7) | copy-start | bytes 580
  37.9 17.6 %copy-start.6 = (f16[240,1024]{1,0:T(8,128)(2,1)S(1)}, f16[240,1024]{1,0:T(8,128)(2,1)}, u32[]{:S(2)}) copy-start(f16[240,1024]{1,0:T(8,128)(2,1)} %get-tuple-element.151) | copy-start | bytes 1474564
  47.5 15.2 %collective-permute-start.8 = (f16[240,1024]{1,0:T(8,128)(2,1)S(1)}, f16[240,1024]{1,0:T(8,128)(2,1)S(1)}, u32[]{:S(2)}, u32[]{:S(2)}) collective-permute-start(f16[240,1024]{1,0:T(8,128)(2,1)S(1)} %copy-done.7), channel_id=1, source_target_pairs={{0,1},{1,0},{2,3},{3,2},{4,5},{5,4},{6,7},{7,6},{8,9},{9,8},{10,11... | collective-permute-start | bytes 1474568 | tf_op jit(solution)/shard_map/ppermute | solution.py:21
  49.0 7.8 %collective-permute-start.7 = (f16[240,1024]{1,0:T(8,128)(2,1)S(1)}, f16[240,1024]{1,0:T(8,128)(2,1)S(1)}, u32[]{:S(2)}, u32[]{:S(2)}) collective-permute-start(f16[240,1024]{1,0:T(8,128)(2,1)S(1)} %multiply_convert_fusion.7), channel_id=1, source_target_pairs={{0,2},{2,0},{4,6},{6,4},{8,10},{10,8},{12,14},{14,12},{16,18},{18,... | collective-permute-start | bytes 1474568 | tf_op jit(solution)/shard_map/ppermute | solution.py:30
  53.5 17.5 %collective-permute-start.9 = (f16[240,1024]{1,0:T(8,128)(2,1)S(1)}, f16[240,1024]{1,0:T(8,128)(2,1)S(1)}, u32[]{:S(2)}, u32[]{:S(2)}) collective-permute-start(f16[240,1024]{1,0:T(8,128)(2,1)S(1)} %multiply_convert_fusion.7), channel_id=1, source_target_pairs={{2,4},{4,2},{6,8},{8,6},{10,12},{12,10},{14,16},{16,14},{18,20},{2... | collective-permute-start | bytes 1474568 | tf_op jit(solution)/shard_map/ppermute | solution.py:30
  55.5 19.8 %collective-permute-start.11 = (f16[240,1024]{1,0:T(8,128)(2,1)S(1)}, f16[240,1024]{1,0:T(8,128)(2,1)S(1)}, u32[]{:S(2)}, u32[]{:S(2)}) collective-permute-start(f16[240,1024]{1,0:T(8,128)(2,1)S(1)} %copy-done.6), channel_id=1, source_target_pairs={{0,1},{1,0},{2,3},{3,2},{4,5},{5,4},{6,7},{7,6},{8,9},{9,8},{10,11... | collective-permute-start | bytes 1474568 | tf_op jit(solution)/shard_map/ppermute | solution.py:21
  56.8 14.5 %copy-start.5 = (f16[240,1024]{1,0:T(8,128)(2,1)S(1)}, f16[240,1024]{1,0:T(8,128)(2,1)}, u32[]{:S(2)}) copy-start(f16[240,1024]{1,0:T(8,128)(2,1)} %get-tuple-element.160) | copy-start | bytes 1474564
  58.1 12.9 %collective-permute-start.10 = (f16[240,1024]{1,0:T(8,128)(2,1)S(1)}, f16[240,1024]{1,0:T(8,128)(2,1)S(1)}, u32[]{:S(2)}, u32[]{:S(2)}) collective-permute-start(f16[240,1024]{1,0:T(8,128)(2,1)S(1)} %multiply_convert_fusion.6), channel_id=1, source_target_pairs={{0,2},{2,0},{4,6},{6,4},{8,10},{10,8},{12,14},{14,12},{16,18},{18,... | collective-permute-start | bytes 1474568 | tf_op jit(solution)/shard_map/ppermute | solution.py:30
  60.6 17.6 %copy-start.4 = (f16[240,1024]{1,0:T(8,128)(2,1)S(1)}, f16[240,1024]{1,0:T(8,128)(2,1)}, u32[]{:S(2)}) copy-start(f16[240,1024]{1,0:T(8,128)(2,1)} %get-tuple-element.169) | copy-start | bytes 1474564
  60.6 33.4 %copy-start.8 = (f16[176,1024]{1,0:T(8,128)(2,1)S(1)}, f16[176,1024]{1,0:T(8,128)(2,1)}, u32[]{:S(2)}) copy-start(f16[176,1024]{1,0:T(8,128)(2,1)} %slice.178) | copy-start | bytes 1081348
  62.6 15.3 %collective-permute-start.12 = (f16[240,1024]{1,0:T(8,128)(2,1)S(1)}, f16[240,1024]{1,0:T(8,128)(2,1)S(1)}, u32[]{:S(2)}, u32[]{:S(2)}) collective-permute-start(f16[240,1024]{1,0:T(8,128)(2,1)S(1)} %multiply_convert_fusion.6), channel_id=1, source_target_pairs={{2,4},{4,2},{6,8},{8,6},{10,12},{12,10},{14,16},{16,14},{18,20},{2... | collective-permute-start | bytes 1474568 | tf_op jit(solution)/shard_map/ppermute | solution.py:30
  71.2 6.7 %collective-permute-start.13 = (f16[240,1024]{1,0:T(8,128)(2,1)S(1)}, f16[240,1024]{1,0:T(8,128)(2,1)S(1)}, u32[]{:S(2)}, u32[]{:S(2)}) collective-permute-start(f16[240,1024]{1,0:T(8,128)(2,1)S(1)} %multiply_convert_fusion.5), channel_id=1, source_target_pairs={{0,2},{2,0},{4,6},{6,4},{8,10},{10,8},{12,14},{14,12},{16,18},{18,... | collective-permute-start | bytes 1474568 | tf_op jit(solution)/shard_map/ppermute | solution.py:30
  71.3 14.6 %collective-permute-start.14 = (f16[240,1024]{1,0:T(8,128)(2,1)S(1)}, f16[240,1024]{1,0:T(8,128)(2,1)S(1)}, u32[]{:S(2)}, u32[]{:S(2)}) collective-permute-start(f16[240,1024]{1,0:T(8,128)(2,1)S(1)} %copy-done.5), channel_id=1, source_target_pairs={{0,1},{1,0},{2,3},{3,2},{4,5},{5,4},{6,7},{7,6},{8,9},{9,8},{10,11... | collective-permute-start | bytes 1474568 | tf_op jit(solution)/shard_map/ppermute | solution.py:21
  74.0 19.7 %collective-permute-start.15 = (f16[240,1024]{1,0:T(8,128)(2,1)S(1)}, f16[240,1024]{1,0:T(8,128)(2,1)S(1)}, u32[]{:S(2)}, u32[]{:S(2)}) collective-permute-start(f16[240,1024]{1,0:T(8,128)(2,1)S(1)} %multiply_convert_fusion.5), channel_id=1, source_target_pairs={{2,4},{4,2},{6,8},{8,6},{10,12},{12,10},{14,16},{16,14},{18,20},{2... | collective-permute-start | bytes 1474568 | tf_op jit(solution)/shard_map/ppermute | solution.py:30
  78.2 15.6 %collective-permute-start.16 = (f16[240,1024]{1,0:T(8,128)(2,1)S(1)}, f16[240,1024]{1,0:T(8,128)(2,1)S(1)}, u32[]{:S(2)}, u32[]{:S(2)}) collective-permute-start(f16[240,1024]{1,0:T(8,128)(2,1)S(1)} %multiply_convert_fusion.4), channel_id=1, source_target_pairs={{0,2},{2,0},{4,6},{6,4},{8,10},{10,8},{12,14},{14,12},{16,18},{18,... | collective-permute-start | bytes 1474568 | tf_op jit(solution)/shard_map/ppermute | solution.py:30
  78.2 21.0 %collective-permute-start.17 = (f16[240,1024]{1,0:T(8,128)(2,1)S(1)}, f16[240,1024]{1,0:T(8,128)(2,1)S(1)}, u32[]{:S(2)}, u32[]{:S(2)}) collective-permute-start(f16[240,1024]{1,0:T(8,128)(2,1)S(1)} %copy-done.4), channel_id=1, source_target_pairs={{0,1},{1,0},{2,3},{3,2},{4,5},{5,4},{6,7},{7,6},{8,9},{9,8},{10,11... | collective-permute-start | bytes 1474568 | tf_op jit(solution)/shard_map/ppermute | solution.py:21
  79.6 19.7 %collective-permute-start.18 = (f16[240,1024]{1,0:T(8,128)(2,1)S(1)}, f16[240,1024]{1,0:T(8,128)(2,1)S(1)}, u32[]{:S(2)}, u32[]{:S(2)}) collective-permute-start(f16[240,1024]{1,0:T(8,128)(2,1)S(1)} %multiply_convert_fusion.4), channel_id=1, source_target_pairs={{2,4},{4,2},{6,8},{8,6},{10,12},{12,10},{14,16},{16,14},{18,20},{2... | collective-permute-start | bytes 1474568 | tf_op jit(solution)/shard_map/ppermute | solution.py:30
  93.9 5.3 %collective-permute-start.19 = (f16[240,1024]{1,0:T(8,128)(2,1)S(1)}, f16[240,1024]{1,0:T(8,128)(2,1)S(1)}, u32[]{:S(2)}, u32[]{:S(2)}) collective-permute-start(f16[240,1024]{1,0:T(8,128)(2,1)S(1)} %multiply_convert_fusion.3), channel_id=1, source_target_pairs={{0,2},{2,0},{4,6},{6,4},{8,10},{10,8},{12,14},{14,12},{16,18},{18,... | collective-permute-start | bytes 1474568 | tf_op jit(solution)/shard_map/ppermute | solution.py:30
  94.0 12.9 %collective-permute-start.20 = (f16[176,1024]{1,0:T(8,128)(2,1)S(1)}, f16[176,1024]{1,0:T(8,128)(2,1)S(1)}, u32[]{:S(2)}, u32[]{:S(2)}) collective-permute-start(f16[176,1024]{1,0:T(8,128)(2,1)S(1)} %copy-done.8), channel_id=1, source_target_pairs={{0,1},{1,0},{2,3},{3,2},{4,5},{5,4},{6,7},{7,6},{8,9},{9,8},{10,11... | collective-permute-start | bytes 1081352 | tf_op jit(solution)/shard_map/ppermute | solution.py:21
  95.4 14.2 %collective-permute-start.21 = (f16[240,1024]{1,0:T(8,128)(2,1)S(1)}, f16[240,1024]{1,0:T(8,128)(2,1)S(1)}, u32[]{:S(2)}, u32[]{:S(2)}) collective-permute-start(f16[240,1024]{1,0:T(8,128)(2,1)S(1)} %multiply_convert_fusion.3), channel_id=1, source_target_pairs={{2,4},{4,2},{6,8},{8,6},{10,12},{12,10},{14,16},{16,14},{18,20},{2... | collective-permute-start | bytes 1474568 | tf_op jit(solution)/shard_map/ppermute | solution.py:30
  99.4 11.5 %collective-permute-start.22 = (f16[240,1024]{1,0:T(8,128)(2,1)S(1)}, f16[240,1024]{1,0:T(8,128)(2,1)S(1)}, u32[]{:S(2)}, u32[]{:S(2)}) collective-permute-start(f16[240,1024]{1,0:T(8,128)(2,1)S(1)} %multiply_convert_fusion.2), channel_id=1, source_target_pairs={{0,2},{2,0},{4,6},{6,4},{8,10},{10,8},{12,14},{14,12},{16,18},{18,... | collective-permute-start | bytes 1474568 | tf_op jit(solution)/shard_map/ppermute | solution.py:30
  101.8 11.7 %collective-permute-start.23 = (f16[192,1024]{1,0:T(8,128)(2,1)S(1)}, f16[192,1024]{1,0:T(8,128)(2,1)S(1)}, u32[]{:S(2)}, u32[]{:S(2)}) collective-permute-start(f16[192,1024]{1,0:T(8,128)(2,1)S(1)} %get-tuple-element.196), channel_id=1, source_target_pairs={{0,1},{1,0},{2,3},{3,2},{4,5},{5,4},{6,7},{7,6},{8,9},{9,8},{10,11... | collective-permute-start | bytes 1179656 | tf_op jit(solution)/shard_map/ppermute | solution.py:21
  104.2 18.1 %collective-permute-start.24 = (f16[240,1024]{1,0:T(8,128)(2,1)S(1)}, f16[240,1024]{1,0:T(8,128)(2,1)S(1)}, u32[]{:S(2)}, u32[]{:S(2)}) collective-permute-start(f16[240,1024]{1,0:T(8,128)(2,1)S(1)} %multiply_convert_fusion.2), channel_id=1, source_target_pairs={{2,4},{4,2},{6,8},{8,6},{10,12},{12,10},{14,16},{16,14},{18,20},{2... | collective-permute-start | bytes 1474568 | tf_op jit(solution)/shard_map/ppermute | solution.py:30
  111.1 11.6 %collective-permute-start.25 = (f16[176,1024]{1,0:T(8,128)(2,1)S(1)}, f16[176,1024]{1,0:T(8,128)(2,1)S(1)}, u32[]{:S(2)}, u32[]{:S(2)}) collective-permute-start(f16[176,1024]{1,0:T(8,128)(2,1)S(1)} %multiply_convert_fusion.9), channel_id=1, source_target_pairs={{0,2},{2,0},{4,6},{6,4},{8,10},{10,8},{12,14},{14,12},{16,18},{18,... | collective-permute-start | bytes 1081352 | tf_op jit(solution)/shard_map/ppermute | solution.py:30
  111.2 16.3 %collective-permute-start.26 = (f16[176,1024]{1,0:T(8,128)(2,1)S(1)}, f16[176,1024]{1,0:T(8,128)(2,1)S(1)}, u32[]{:S(2)}, u32[]{:S(2)}) collective-permute-start(f16[176,1024]{1,0:T(8,128)(2,1)S(1)} %multiply_convert_fusion.9), channel_id=1, source_target_pairs={{2,4},{4,2},{6,8},{8,6},{10,12},{12,10},{14,16},{16,14},{18,20},{2... | collective-permute-start | bytes 1081352 | tf_op jit(solution)/shard_map/ppermute | solution.py:30
  122.7 4.8 %copy-start.1 = (f32[1,2048,1024]{2,1,0:T(8,128)}, f32[1,2048,1024]{2,1,0:T(8,128)S(1)}, u32[]{:S(2)}) copy-start(f32[1,2048,1024]{2,1,0:T(8,128)S(1)} %bitcast_dynamic-update-slice_fusion) | copy-start | bytes 25165828

commit v13 on v12

--- a/solution.py
+++ b/solution.py
@@ -9,10 +9,10 @@
 RATE = 0.03
 LARGEST = 6.0
 WIRE = jnp.float16
-STEP = 240
-FIRST = 192
+STEP = 256
+FIRST = 128
 AHEAD = 3
-MIXLAG = 5
+MIXLAG = 99
 
 
 def from_behind(value, axis, steps):
@@ -45,11 +45,10 @@
     replica = lax.axis_index("blk")
     shard = lax.axis_index("fsdp")
     def coefficients(mix):
-        row = lax.dynamic_slice_in_dim(mix, replica, 1, axis=0).astype(jnp.float32) / MIX_DENOM
-        left, own, right = row[:, 0:1], row[:, 1:2], row[:, 2:3]
-        even = replica % 2 == 0
-        sides = [jnp.where(even, right, left) / scale, own, jnp.where(even, left, right) / scale]
-        return jnp.broadcast_to(jnp.concatenate(sides, axis=0), (3, weights.shape[1]))
+        row = lax.dynamic_slice_in_dim(mix, replica, 1, axis=0).astype(jnp.float32)
+        row = jnp.where(replica % 2 == 0, row[:, ::-1], row)
+        column = jnp.reshape(row, (3, 1)) / MIX_DENOM
+        return jnp.broadcast_to(column, (3, weights.shape[1]))
 
     first = min(FIRST, rows // 2)
     main = rows - first
@@ -88,7 +87,9 @@
 
     def mixture(near, own, far):
         return (
-            coeff[0:1] * near.astype(jnp.float32) + coeff[1:2] * own + coeff[2:3] * far.astype(jnp.float32)
+            coeff[0:1] * (near.astype(jnp.float32) / scale)
+            + coeff[1:2] * own
+            + coeff[2:3] * (far.astype(jnp.float32) / scale)
         )
 
     def mix_into(out, chunk):
@@ -114,7 +115,7 @@
     if chunks > 1:
         parts, later = lax.optimization_barrier((parts, shard))
         rest = [
-            (partial(owner(away, later), cuts[1], main - cuts[1]) * (RATE * scale)).astype(WIRE)
+            (partial(owner(away, later), cuts[1], rows - cuts[1]) * (RATE * scale)).astype(WIRE)
             for away in range(1, shards)
         ]
         for chunk in range(1, chunks):
@@ -139,7 +140,7 @@
         sent = (u_of(chunk) * scale).astype(WIRE)
         sent, base, out, later = lax.optimization_barrier((sent, base, out, shard))
         if chunk == 0 and split < main:
-            base.append(own_part(later, split, main))
+            base.append(own_part(later, split, rows))
         if chunk == middle:
             mix, parts, sent = lax.optimization_barrier((mix, parts, sent))
             coeff = lax.optimization_barrier(coefficients(mix))

time: 129 us -> 126 us (0.977)
  starting transfers between devices: 38.9 us -> 30.7 us
  waiting for transfers between devices: 33.5 us -> 41.6 us
  matrix products: 27.9 us -> 23.1 us
  local copies, waits for them, and re-layouts: 7.44 us -> 10.1 us
  between operations: 2.93 us -> 0.29 us
    ppermute x9, waiting for transfers between devices: 0.02 us -> 28.5 us  [from_behind(): return lax.ppermute(value, axis, pairs)]
    ppermute x18, waiting for transfers between devices: 33.5 us -> 13.1 us  [swapped(): return lax.ppermute(value, axis, pairs)]
    dot_general x6, matrix products: 27.9 us -> 23.1 us  [partial(): lax.dot_general(block, cot_local, (((0,), (0,)), ((), ())), preferred_ele...]
    ppermute x9, starting transfers between devices: 12 us -> 7.88 us  [from_behind(): return lax.ppermute(value, axis, pairs)]
    ppermute x18, starting transfers between devices: 26.9 us -> 22.9 us  [swapped(): return lax.ppermute(value, axis, pairs)]
    unnamed x20 -> x22, local copies, waits for them, and re-layouts: 2.78 us -> 5.1 us
    convert_element_type x8, other arithmetic: 5.49 us -> 7.04 us  [on_device(): sent = (u_of(chunk) * scale).astype(WIRE)]
    dynamic_update_slice x8, other arithmetic: 7.21 us -> 8.53 us  [mix_into(): return lax.dynamic_update_slice_in_dim(out, value, cuts[chunk], axis=0)]
  transfers between devices with their start and end apart: 27 -> 27, of which waited for: 6 -> 11; matrix products, arithmetic and copies ran while one was open for 31% -> 31% of each run, Pallas kernels for 0% -> 0%
where the time goes in v13:
time: 126 us; the launch traced here: 124 us
  waiting for transfers between devices  41.6 us (33%)
  starting transfers between devices  30.7 us (24%)
  matrix products  23.1 us (18%)
  other arithmetic  18.6 us (15%)
  local copies, waits for them, and re-layouts  10.1 us (8%)
    ppermute x9, waiting for transfers between devices, from_behind(): return lax.ppermute(value, axis, pairs)  28.5 us
    dot_general x6, matrix products, partial(): lax.dot_general(block, cot_local, (((0,), (0,)), ((), ())), preferred_ele...  23.1 us
    ppermute x18, starting transfers between devices, swapped(): return lax.ppermute(value, axis, pairs)  22.9 us
    ppermute x18, waiting for transfers between devices, swapped(): return lax.ppermute(value, axis, pairs)  13.1 us
    dynamic_update_slice x8, other arithmetic, mix_into(): return lax.dynamic_update_slice_in_dim(out, value, cuts[chunk], axis=0)  8.53 us
    ppermute x9, starting transfers between devices, from_behind(): return lax.ppermute(value, axis, pairs)  7.88 us
    convert_element_type x8, other arithmetic, on_device(): sent = (u_of(chunk) * scale).astype(WIRE)  7.04 us
    unnamed x22, local copies, waits for them, and re-layouts  5.1 us
  transfers between devices with their start and end apart: 27, of which 11 were waited for; matrix products, arithmetic and copies ran while one was open for 31% of the time, Pallas kernels for 0%

profile of v13, /device:TPU:1, one launch (start us, length us, event | category | flops | bytes accessed | tf_op | source)
XLA Modules:
  0.0 124.5 jit_solution(2645625952917771432)
XLA Ops:
  0.0 1.5 %copy-done = bf16[1,896,1024]{2,1,0:T(8,128)(2,1)S(1)} copy-done((bf16[1,896,1024]{2,1,0:T(8,128)(2,1)S(1)}, bf16[1,896,1024]{2,1,0:T(8,128)(2,1)}, u32[]{:S(2)}) %copy-start) | copy-done | bytes 1835032
  1.5 2.5 %fusion.19 = f16[256,1024]{1,0:T(8,128)(2,1)} fusion(bf16[1,896,1024]{2,1,0:T(8,128)(2,1)S(1)} %copy-done, bf16[1,896,4096]{2,1,0:T(8,128)(2,1)} %param.5, s32[]{:T(128)S(6)} %select_n.46), kind=kOutput, calls=%fused_computation.18 | convolution fusion | flops 470286336 | bytes 2818052 | tf_op jit(solution)/shard_map/dot_general | solution.py:65
  4.0 1.4 %fusion.25 = f32[128,1024]{1,0:T(8,128)S(1)} fusion(bf16[1,896,1024]{2,1,0:T(8,128)(2,1)S(1)} %copy-done, bf16[1,896,4096]{2,1,0:T(8,128)(2,1)} %param.5, s32[]{:T(128)S(6)} %select_n.49), kind=kOutput, calls=%fused_computation.20 | convolution fusion | flops 235012096 | bytes 2588676 | tf_op jit(solution)/shard_map/dot_general | solution.py:65
  5.5 1.6 %fusion.28 = f32[128,1024]{1,0:T(8,128)S(1)} fusion(bf16[1,896,1024]{2,1,0:T(8,128)(2,1)S(1)} %copy-done, f32[1,2048,1024]{2,1,0:T(8,128)} %param.4, bf16[1,896,4096]{2,1,0:T(8,128)(2,1)} %param.5, s32[]{:T(128)S(6)} %select_n.47), kind=kOutput, calls=%fused_computation.21 | convolution fusion | flops 235143168 | bytes 3112964 | tf_op jit(solution)/shard_map/dot_general | solution.py:65
  7.1 1.0 multiply_convert_fusion.8
  8.2 2.6 %collective-permute-start.3 = (f16[256,1024]{1,0:T(8,128)(2,1)}, f16[256,1024]{1,0:T(8,128)(2,1)}, u32[]{:S(2)}, u32[]{:S(2)}) collective-permute-start(f16[256,1024]{1,0:T(8,128)(2,1)} %get-tuple-element.106), channel_id=1, source_target_pairs={{2,4},{4,2},{6,8},{8,6},{10,12},{12,10},{14,16},{16,14},{18,20},{2... | collective-permute-start | bytes 1572872 | tf_op jit(solution)/shard_map/ppermute | solution.py:30
  10.8 2.9 %collective-permute-start.2 = (f16[256,1024]{1,0:T(8,128)(2,1)}, f16[256,1024]{1,0:T(8,128)(2,1)}, u32[]{:S(2)}, u32[]{:S(2)}) collective-permute-start(f16[256,1024]{1,0:T(8,128)(2,1)} %get-tuple-element.106), channel_id=1, source_target_pairs={{0,2},{2,0},{4,6},{6,4},{8,10},{10,8},{12,14},{14,12},{16,18},{18,... | collective-permute-start | bytes 1572872 | tf_op jit(solution)/shard_map/ppermute | solution.py:30
  13.6 1.2 collective-permute-start.1
  14.9 6.2 %multiply_convert_fusion = f16[1792,1024]{1,0:T(8,128)(2,1)S(1)} fusion(bf16[1,896,4096]{2,1,0:T(8,128)(2,1)} %param.5, s32[]{:T(128)S(6)} %select_n.51, bf16[1,896,1024]{2,1,0:T(8,128)(2,1)S(1)} %copy-done), kind=kOutput, calls=%fused_computation | convolution fusion | flops 3292004352 | bytes 8716292 | tf_op jit(solution)/shard_map/dot_general | solution.py:65
  21.1 1.8 %copy-done.6 = f16[1792,1024]{1,0:T(8,128)(2,1)} copy-done((f16[1792,1024]{1,0:T(8,128)(2,1)}, f16[1792,1024]{1,0:T(8,128)(2,1)S(1)}, u32[]{:S(2)}) %copy-start.6) | copy-done | bytes 3670040
  22.9 2.1 %fusion.47 = (f16[256,1024]{1,0:T(8,128)(2,1)}, f16[256,1024]{1,0:T(8,128)(2,1)}, f16[256,1024]{1,0:T(8,128)(2,1)}, f16[256,1024]{1,0:T(8,128)(2,1)}, f16[256,1024]{1,0:T(8,128)(2,1)}, /*index=5*/f16[256,1024]{1,0:T(8,128)(2,1)}) fusion(f16[1792,1024]{1,0:T(8,128)(2,1)S(1)} %multiply_convert_fusion), kind=kLoop, calls=%fused_computation.71 | loop fusion | bytes 6291456 | tf_op jit(solution)/shard_map/slice | solution.py:122
  25.0 0.2 collective-permute-start
  25.3 1.7 %slice.166 = f16[128,1024]{1,0:T(8,128)(2,1)} slice(f16[1792,1024]{1,0:T(8,128)(2,1)} %copy-done.6), slice={[1536:1664], [0:1024]} | slice | bytes 524288 | tf_op jit(solution)/shard_map/slice | solution.py:122
  27.0 3.2 %bitcast_subtract_fusion.1 = f32[512,1024]{1,0:T(8,128)S(1)} fusion(f32[1,2048,1024]{2,1,0:T(8,128)} %param.4, bf16[1,896,1024]{2,1,0:T(8,128)(2,1)S(1)} %copy-done, bf16[1,896,4096]{2,1,0:T(8,128)(2,1)} %param.5, s32[]{:T(128)S(6)} %select_n.52), kind=kOutput, calls=%fused_computation.6 | convolution fusion | flops 940572672 | bytes 6946820 | tf_op jit(solution)/shard_map/dot_general | solution.py:65
  30.1 1.3 %collective-permute-start.5 = (f16[256,1024]{1,0:T(8,128)(2,1)}, f16[256,1024]{1,0:T(8,128)(2,1)}, u32[]{:S(2)}, u32[]{:S(2)}) collective-permute-start(f16[256,1024]{1,0:T(8,128)(2,1)} %get-tuple-element.107), channel_id=1, source_target_pairs={{0,1},{1,0},{2,3},{3,2},{4,5},{5,4},{6,7},{7,6},{8,9},{9,8},{10,11... | collective-permute-start | bytes 1572872 | tf_op jit(solution)/shard_map/ppermute | solution.py:21
  31.5 1.0 multiply_convert_fusion.7
  32.5 0.8 collective-permute-start.4
  33.3 8.2 %bitcast_subtract_fusion = f32[1536,1024]{1,0:T(8,128)} fusion(f32[1,2048,1024]{2,1,0:T(8,128)} %param.4, bf16[1,896,4096]{2,1,0:T(8,128)(2,1)} %param.5, s32[]{:T(128)S(6)} %select_n.53, bf16[1,896,1024]{2,1,0:T(8,128)(2,1)S(1)} %copy-done), kind=kOutput, calls=%fused_computation.1 | convolution fusion | flops 2821718016 | bytes 17170436 | tf_op jit(solution)/shard_map/dot_general | solution.py:65
  41.6 2.1 %multiply_convert_fusion.6 = f16[256,1024]{1,0:T(8,128)(2,1)} fusion(f16[256,1024]{1,0:T(8,128)(2,1)} %collective-permute-done, f32[512,1024]{1,0:T(8,128)S(1)} %copy-done.4), kind=kLoop, calls=%fused_computation.41 | loop fusion | flops 1310720 | bytes 2097152 | tf_op jit(solution)/shard_map/convert_element_type | solution.py:140
  43.7 1.1 collective-permute-start.8
  44.8 1.9 %collective-permute-start.9 = (f16[256,1024]{1,0:T(8,128)(2,1)}, f16[256,1024]{1,0:T(8,128)(2,1)}, u32[]{:S(2)}, u32[]{:S(2)}) collective-permute-start(f16[256,1024]{1,0:T(8,128)(2,1)} %multiply_convert_fusion.6), channel_id=1, source_target_pairs={{2,4},{4,2},{6,8},{8,6},{10,12},{12,10},{14,16},{16,14},{18,20},{2... | collective-permute-start | bytes 1572872 | tf_op jit(solution)/shard_map/ppermute | solution.py:30
  46.6 3.2 %collective-permute-done.5 = f16[256,1024]{1,0:T(8,128)(2,1)} collective-permute-done((f16[256,1024]{1,0:T(8,128)(2,1)}, f16[256,1024]{1,0:T(8,128)(2,1)}, u32[]{:S(2)}, u32[]{:S(2)}) %collective-permute-start.5) | collective-permute-done | bytes 524320 | tf_op jit(solution)/shard_map/ppermute | solution.py:21
  49.8 0.1 fusion.46
  50.0 0.2 multiply_reduce_fusion
  50.1 0.1 broadcast_in_dim.30
  50.2 1.4 %collective-permute-start.11 = (f16[256,1024]{1,0:T(8,128)(2,1)}, f16[256,1024]{1,0:T(8,128)(2,1)S(1)}, u32[]{:S(2)}, u32[]{:S(2)}) collective-permute-start(f16[256,1024]{1,0:T(8,128)(2,1)} %get-tuple-element.148), channel_id=1, source_target_pairs={{0,1},{1,0},{2,3},{3,2},{4,5},{5,4},{6,7},{7,6},{8,9},{9,8},{10,11... | collective-permute-start | bytes 1572872 | tf_op jit(solution)/shard_map/ppermute | solution.py:21
  51.6 2.0 %multiply_convert_fusion.5 = f16[256,1024]{1,0:T(8,128)(2,1)S(1)} fusion(f16[256,1024]{1,0:T(8,128)(2,1)} %collective-permute-done.5, f32[1536,1024]{1,0:T(8,128)} %bitcast_subtract_fusion), kind=kLoop, calls=%fused_computation.39 | loop fusion | flops 1310720 | bytes 2097152 | tf_op jit(solution)/shard_map/convert_element_type | solution.py:140
  53.6 1.7 %collective-permute-start.10 = (f16[256,1024]{1,0:T(8,128)(2,1)S(1)}, f16[256,1024]{1,0:T(8,128)(2,1)S(1)}, u32[]{:S(2)}, u32[]{:S(2)}) collective-permute-start(f16[256,1024]{1,0:T(8,128)(2,1)S(1)} %multiply_convert_fusion.5), channel_id=1, source_target_pairs={{0,2},{2,0},{4,6},{6,4},{8,10},{10,8},{12,14},{14,12},{16,18},{18,... | collective-permute-start | bytes 1572872 | tf_op jit(solution)/shard_map/ppermute | solution.py:30
  55.3 1.5 %multiply_add_fusion = f32[256,1024]{1,0:T(8,128)S(1)} fusion(f16[256,1024]{1,0:T(8,128)(2,1)} %collective-permute-done.3, f32[256,1024]{1,0:T(8,128)S(1)} %get-tuple-element.142, f16[256,1024]{1,0:T(8,128)(2,1)} %collective-permute-done.2, f32[1024]{0:T(1024)S(1)} %bitcast.81, f32[1024]{0:T(1024)S(1)} %bitcast.90, f32[1024]{0:T(1024)S(1)} %bitcast.72), kind=kLoop, calls=%fused_computation.38 | loop fusion | flops 1835008 | bytes 3158016 | tf_op jit(solution)/shard_map/add | solution.py:90
  57.0 4.1 %collective-permute-done.8 = f16[256,1024]{1,0:T(8,128)(2,1)} collective-permute-done((f16[256,1024]{1,0:T(8,128)(2,1)}, f16[256,1024]{1,0:T(8,128)(2,1)}, u32[]{:S(2)}, u32[]{:S(2)}) %collective-permute-start.8) | collective-permute-done | bytes 524320 | tf_op jit(solution)/shard_map/ppermute | solution.py:21
  61.1 3.2 %collective-permute-done.9 = f16[256,1024]{1,0:T(8,128)(2,1)} collective-permute-done((f16[256,1024]{1,0:T(8,128)(2,1)}, f16[256,1024]{1,0:T(8,128)(2,1)}, u32[]{:S(2)}, u32[]{:S(2)}) %collective-permute-start.9) | collective-permute-done | bytes 524320 | tf_op jit(solution)/shard_map/ppermute | solution.py:30
  64.3 1.2 multiply_convert_fusion.4
  65.7 0.3 collective-permute-start.14
  66.0 2.7 %collective-permute-start.15 = (f16[256,1024]{1,0:T(8,128)(2,1)S(1)}, f16[256,1024]{1,0:T(8,128)(2,1)S(1)}, u32[]{:S(2)}, u32[]{:S(2)}) collective-permute-start(f16[256,1024]{1,0:T(8,128)(2,1)S(1)} %multiply_convert_fusion.4), channel_id=1, source_target_pairs={{2,4},{4,2},{6,8},{8,6},{10,12},{12,10},{14,16},{16,14},{18,20},{2... | collective-permute-start | bytes 1572872 | tf_op jit(solution)/shard_map/ppermute | solution.py:30
  68.7 3.5 %collective-permute-done.11 = f16[256,1024]{1,0:T(8,128)(2,1)S(1)} collective-permute-done((f16[256,1024]{1,0:T(8,128)(2,1)}, f16[256,1024]{1,0:T(8,128)(2,1)S(1)}, u32[]{:S(2)}, u32[]{:S(2)}) %collective-permute-start.11) | collective-permute-done | bytes 524320 | tf_op jit(solution)/shard_map/ppermute | solution.py:21
  72.2 0.2 multiply_convert_fusion.3
  72.4 1.9 %collective-permute-start.16 = (f16[256,1024]{1,0:T(8,128)(2,1)S(1)}, f16[256,1024]{1,0:T(8,128)(2,1)S(1)}, u32[]{:S(2)}, u32[]{:S(2)}) collective-permute-start(f16[256,1024]{1,0:T(8,128)(2,1)S(1)} %multiply_convert_fusion.3), channel_id=1, source_target_pairs={{0,2},{2,0},{4,6},{6,4},{8,10},{10,8},{12,14},{14,12},{16,18},{18,... | collective-permute-start | bytes 1572872 | tf_op jit(solution)/shard_map/ppermute | solution.py:30
  74.3 0.8 collective-permute-start.17
  75.1 8.4 %collective-permute-done.14 = f16[256,1024]{1,0:T(8,128)(2,1)S(1)} collective-permute-done((f16[256,1024]{1,0:T(8,128)(2,1)S(1)}, f16[256,1024]{1,0:T(8,128)(2,1)S(1)}, u32[]{:S(2)}, u32[]{:S(2)}) %collective-permute-start.14) | collective-permute-done | bytes 524320 | tf_op jit(solution)/shard_map/ppermute | solution.py:21
  83.4 4.9 %collective-permute-done.15 = f16[256,1024]{1,0:T(8,128)(2,1)S(1)} collective-permute-done((f16[256,1024]{1,0:T(8,128)(2,1)S(1)}, f16[256,1024]{1,0:T(8,128)(2,1)S(1)}, u32[]{:S(2)}, u32[]{:S(2)}) %collective-permute-start.15) | collective-permute-done | bytes 524320 | tf_op jit(solution)/shard_map/ppermute | solution.py:30
  88.4 0.2 multiply_convert_fusion.2
  88.7 0.9 collective-permute-start.21
  89.5 5.1 %collective-permute-done.17 = f16[256,1024]{1,0:T(8,128)(2,1)S(1)} collective-permute-done((f16[256,1024]{1,0:T(8,128)(2,1)S(1)}, f16[256,1024]{1,0:T(8,128)(2,1)S(1)}, u32[]{:S(2)}, u32[]{:S(2)}) %collective-permute-start.17) | collective-permute-done | bytes 524320 | tf_op jit(solution)/shard_map/ppermute | solution.py:21
  94.7 3.2 %collective-permute-done.18 = f16[256,1024]{1,0:T(8,128)(2,1)S(1)} collective-permute-done((f16[256,1024]{1,0:T(8,128)(2,1)S(1)}, f16[256,1024]{1,0:T(8,128)(2,1)S(1)}, u32[]{:S(2)}, u32[]{:S(2)}) %collective-permute-start.18) | collective-permute-done | bytes 524320 | tf_op jit(solution)/shard_map/ppermute | solution.py:30
  97.9 0.2 multiply_convert_fusion.1
  98.2 0.7 collective-permute-start.20
  98.9 0.8 collective-permute-start.23
  99.7 3.0 %collective-permute-start.24 = (f16[256,1024]{1,0:T(8,128)(2,1)S(1)}, f16[256,1024]{1,0:T(8,128)(2,1)S(1)}, u32[]{:S(2)}, u32[]{:S(2)}) collective-permute-start(f16[256,1024]{1,0:T(8,128)(2,1)S(1)} %multiply_convert_fusion.1), channel_id=1, source_target_pairs={{2,4},{4,2},{6,8},{8,6},{10,12},{12,10},{14,16},{16,14},{18,20},{2... | collective-permute-start | bytes 1572872 | tf_op jit(solution)/shard_map/ppermute | solution.py:30
  102.8 2.9 %collective-permute-done.20 = f16[128,1024]{1,0:T(8,128)(2,1)S(1)} collective-permute-done((f16[128,1024]{1,0:T(8,128)(2,1)S(1)}, f16[128,1024]{1,0:T(8,128)(2,1)S(1)}, u32[]{:S(2)}, u32[]{:S(2)}) %collective-permute-start.20) | collective-permute-done | bytes 262176 | tf_op jit(solution)/shard_map/ppermute | solution.py:21
  105.7 0.1 multiply_convert_fusion.9
  105.8 4.2 %collective-permute-start.26 = (f16[128,1024]{1,0:T(8,128)(2,1)S(1)}, f16[128,1024]{1,0:T(8,128)(2,1)S(1)}, u32[]{:S(2)}, u32[]{:S(2)}) collective-permute-start(f16[128,1024]{1,0:T(8,128)(2,1)S(1)} %multiply_convert_fusion.9), channel_id=1, source_target_pairs={{2,4},{4,2},{6,8},{8,6},{10,12},{12,10},{14,16},{16,14},{18,20},{2... | collective-permute-start | bytes 786440 | tf_op jit(solution)/shard_map/ppermute | solution.py:30
  110.1 1.3 %collective-permute-done.23 = f16[128,1024]{1,0:T(8,128)(2,1)S(1)} collective-permute-done((f16[128,1024]{1,0:T(8,128)(2,1)S(1)}, f16[128,1024]{1,0:T(8,128)(2,1)S(1)}, u32[]{:S(2)}, u32[]{:S(2)}) %collective-permute-start.23) | collective-permute-done | bytes 262176 | tf_op jit(solution)/shard_map/ppermute | solution.py:21
  111.4 1.1 broadcast_in_dim.29
  112.4 0.1 bitcast_dynamic-update-slice_fusion.8
  112.5 1.6 %bitcast_dynamic-update-slice_fusion.6 = f32[1,2048,1024]{2,1,0:T(8,128)S(1)} fusion(f32[1,2048,1024]{2,1,0:T(8,128)S(1)} %bitcast_dynamic-update-slice_fusion.8, f16[256,1024]{1,0:T(8,128)(2,1)} %collective-permute-done.6, f32[512,1024]{1,0:T(8,128)S(1)} %copy-done.5, f16[256,1024]{1,0:T(8,128)(2,1)} %collective-permute-done.4, ...), kind=kLoop, calls=%fused_computation.29 | loop fusion | flops 2621440 | bytes 3682304 | tf_op jit(solution)/shard_map/dynamic_update_slice | solution.py:97
  114.1 1.8 %bitcast_dynamic-update-slice_fusion.5 = f32[1,2048,1024]{2,1,0:T(8,128)S(1)} fusion(f32[1,2048,1024]{2,1,0:T(8,128)S(1)} %bitcast_dynamic-update-slice_fusion.6, f16[256,1024]{1,0:T(8,128)(2,1)} %collective-permute-done.9, f32[512,1024]{1,0:T(8,128)S(1)} %copy-done.5, f16[256,1024]{1,0:T(8,128)(2,1)} %collective-permute-done.7, ...), kind=kLoop, calls=%fused_computation.28 | loop fusion | flops 2621440 | bytes 3682304 | tf_op jit(solution)/shard_map/dynamic_update_slice | solution.py:97
  115.9 1.5 %bitcast_dynamic-update-slice_fusion.4 = f32[1,2048,1024]{2,1,0:T(8,128)S(1)} fusion(f32[1,2048,1024]{2,1,0:T(8,128)S(1)} %bitcast_dynamic-update-slice_fusion.5, f16[256,1024]{1,0:T(8,128)(2,1)S(1)} %collective-permute-done.12, f32[1536,1024]{1,0:T(8,128)S(1)} %copy-done.1, f16[256,1024]{1,0:T(8,128)(2,1)S(1)} %collective-permute-done.10, ...), kind=kLoop, calls=%fused_computation.27 | loop fusion | flops 2621440 | bytes 3682304 | tf_op jit(solution)/shard_map/dynamic_update_slice | solution.py:97
  117.4 1.5 %bitcast_dynamic-update-slice_fusion.3 = f32[1,2048,1024]{2,1,0:T(8,128)S(1)} fusion(f32[1,2048,1024]{2,1,0:T(8,128)S(1)} %bitcast_dynamic-update-slice_fusion.4, f16[256,1024]{1,0:T(8,128)(2,1)S(1)} %collective-permute-done.15, f32[1536,1024]{1,0:T(8,128)S(1)} %copy-done.1, f16[256,1024]{1,0:T(8,128)(2,1)S(1)} %collective-permute-done.13, ...), kind=kLoop, calls=%fused_computation.26 | loop fusion | flops 2621440 | bytes 3682304 | tf_op jit(solution)/shard_map/dynamic_update_slice | solution.py:97
  118.8 0.4 bitcast_dynamic-update-slice_fusion.2
  119.2 0.4 bitcast_dynamic-update-slice_fusion.1
  119.7 0.4 bitcast_dynamic-update-slice_fusion
  120.1 1.7 %collective-permute-done.26 = f16[128,1024]{1,0:T(8,128)(2,1)S(1)} collective-permute-done((f16[128,1024]{1,0:T(8,128)(2,1)S(1)}, f16[128,1024]{1,0:T(8,128)(2,1)S(1)}, u32[]{:S(2)}, u32[]{:S(2)}) %collective-permute-start.26) | collective-permute-done | bytes 262176 | tf_op jit(solution)/shard_map/ppermute | solution.py:30
  121.8 1.7 %copy-done.2 = f32[1,2048,1024]{2,1,0:T(8,128)} copy-done((f32[1,2048,1024]{2,1,0:T(8,128)}, f32[1,2048,1024]{2,1,0:T(8,128)S(1)}, u32[]{:S(2)}) %copy-start.2) | copy-done | bytes 8388632
  123.5 1.0 bitcast_dynamic-update-slice_fusion.7
  (46 shorter events, 0.5 us)
Async XLA Ops:
  0.0 1.5 %copy-start = (bf16[1,896,1024]{2,1,0:T(8,128)(2,1)S(1)}, bf16[1,896,1024]{2,1,0:T(8,128)(2,1)}, u32[]{:S(2)}) copy-start(bf16[1,896,1024]{2,1,0:T(8,128)(2,1)} %param.6) | copy-start | bytes 5505028
  8.2 33.4 %collective-permute-start.3 = (f16[256,1024]{1,0:T(8,128)(2,1)}, f16[256,1024]{1,0:T(8,128)(2,1)}, u32[]{:S(2)}, u32[]{:S(2)}) collective-permute-start(f16[256,1024]{1,0:T(8,128)(2,1)} %get-tuple-element.106), channel_id=1, source_target_pairs={{2,4},{4,2},{6,8},{8,6},{10,12},{12,10},{14,16},{16,14},{18,20},{2... | collective-permute-start | bytes 1572872 | tf_op jit(solution)/shard_map/ppermute | solution.py:30
  10.8 19.4 %collective-permute-start.2 = (f16[256,1024]{1,0:T(8,128)(2,1)}, f16[256,1024]{1,0:T(8,128)(2,1)}, u32[]{:S(2)}, u32[]{:S(2)}) collective-permute-start(f16[256,1024]{1,0:T(8,128)(2,1)} %get-tuple-element.106), channel_id=1, source_target_pairs={{0,2},{2,0},{4,6},{6,4},{8,10},{10,8},{12,14},{14,12},{16,18},{18,... | collective-permute-start | bytes 1572872 | tf_op jit(solution)/shard_map/ppermute | solution.py:30
  13.6 17.8 %collective-permute-start.1 = (f16[256,1024]{1,0:T(8,128)(2,1)}, f16[256,1024]{1,0:T(8,128)(2,1)S(1)}, u32[]{:S(2)}, u32[]{:S(2)}) collective-permute-start(f16[256,1024]{1,0:T(8,128)(2,1)} %fusion.19), channel_id=1, source_target_pairs={{0,1},{1,0},{2,3},{3,2},{4,5},{5,4},{6,7},{7,6},{8,9},{9,8},{10,11... | collective-permute-start | bytes 1572872 | tf_op jit(solution)/shard_map/ppermute | solution.py:21
  21.0 1.8 %copy-start.6 = (f16[1792,1024]{1,0:T(8,128)(2,1)}, f16[1792,1024]{1,0:T(8,128)(2,1)S(1)}, u32[]{:S(2)}) copy-start(f16[1792,1024]{1,0:T(8,128)(2,1)S(1)} %multiply_convert_fusion) | copy-start | bytes 11010052
  25.0 16.5 %collective-permute-start = (f16[256,1024]{1,0:T(8,128)(2,1)}, f16[256,1024]{1,0:T(8,128)(2,1)}, u32[]{:S(2)}, u32[]{:S(2)}) collective-permute-start(f16[256,1024]{1,0:T(8,128)(2,1)} %get-tuple-element.204), channel_id=1, source_target_pairs={{0,1},{1,0},{2,3},{3,2},{4,5},{5,4},{6,7},{7,6},{8,9},{9,8},{10,11... | collective-permute-start | bytes 1572872 | tf_op jit(solution)/shard_map/ppermute | solution.py:21
  30.1 1.4 %copy-start.3 = (f32[512,1024]{1,0:T(8,128)}, f32[512,1024]{1,0:T(8,128)S(1)}, u32[]{:S(2)}) copy-start(f32[512,1024]{1,0:T(8,128)S(1)} %bitcast_subtract_fusion.1) | copy-start | bytes 6291460
  30.1 19.7 %collective-permute-start.5 = (f16[256,1024]{1,0:T(8,128)(2,1)}, f16[256,1024]{1,0:T(8,128)(2,1)}, u32[]{:S(2)}, u32[]{:S(2)}) collective-permute-start(f16[256,1024]{1,0:T(8,128)(2,1)} %get-tuple-element.107), channel_id=1, source_target_pairs={{0,1},{1,0},{2,3},{3,2},{4,5},{5,4},{6,7},{7,6},{8,9},{9,8},{10,11... | collective-permute-start | bytes 1572872 | tf_op jit(solution)/shard_map/ppermute | solution.py:21
  32.5 17.3 %collective-permute-start.6 = (f16[256,1024]{1,0:T(8,128)(2,1)}, f16[256,1024]{1,0:T(8,128)(2,1)}, u32[]{:S(2)}, u32[]{:S(2)}) collective-permute-start(f16[256,1024]{1,0:T(8,128)(2,1)} %multiply_convert_fusion.7), channel_id=1, source_target_pairs={{2,4},{4,2},{6,8},{8,6},{10,12},{12,10},{14,16},{16,14},{18,20},{2... | collective-permute-start | bytes 1572872 | tf_op jit(solution)/shard_map/ppermute | solution.py:30
  32.5 9.1 %collective-permute-start.4 = (f16[256,1024]{1,0:T(8,128)(2,1)}, f16[256,1024]{1,0:T(8,128)(2,1)}, u32[]{:S(2)}, u32[]{:S(2)}) collective-permute-start(f16[256,1024]{1,0:T(8,128)(2,1)} %multiply_convert_fusion.7), channel_id=1, source_target_pairs={{0,2},{2,0},{4,6},{6,4},{8,10},{10,8},{12,14},{14,12},{16,18},{18,... | collective-permute-start | bytes 1572872 | tf_op jit(solution)/shard_map/ppermute | solution.py:30
  33.3 8.2 %copy-start.4 = (f32[512,1024]{1,0:T(8,128)S(1)}, f32[512,1024]{1,0:T(8,128)}, u32[]{:S(2)}) copy-start(f32[512,1024]{1,0:T(8,128)} %copy-done.3) | copy-start | bytes 6291460
  33.3 16.5 %copy-start.10 = (s32[16,3]{0,1:T(4,128)S(1)}, s32[16,3]{0,1:T(4,128)}, u32[]{:S(2)}) copy-start(s32[16,3]{0,1:T(4,128)} %param.7) | copy-start | bytes 580
  43.7 8.0 %collective-permute-start.7 = (f16[256,1024]{1,0:T(8,128)(2,1)}, f16[256,1024]{1,0:T(8,128)(2,1)}, u32[]{:S(2)}, u32[]{:S(2)}) collective-permute-start(f16[256,1024]{1,0:T(8,128)(2,1)} %multiply_convert_fusion.6), channel_id=1, source_target_pairs={{0,2},{2,0},{4,6},{6,4},{8,10},{10,8},{12,14},{14,12},{16,18},{18,... | collective-permute-start | bytes 1572872 | tf_op jit(solution)/shard_map/ppermute | solution.py:30
  43.7 17.4 %collective-permute-start.8 = (f16[256,1024]{1,0:T(8,128)(2,1)}, f16[256,1024]{1,0:T(8,128)(2,1)}, u32[]{:S(2)}, u32[]{:S(2)}) collective-permute-start(f16[256,1024]{1,0:T(8,128)(2,1)} %get-tuple-element.134), channel_id=1, source_target_pairs={{0,1},{1,0},{2,3},{3,2},{4,5},{5,4},{6,7},{7,6},{8,9},{9,8},{10,11... | collective-permute-start | bytes 1572872 | tf_op jit(solution)/shard_map/ppermute | solution.py:21
  44.8 19.5 %collective-permute-start.9 = (f16[256,1024]{1,0:T(8,128)(2,1)}, f16[256,1024]{1,0:T(8,128)(2,1)}, u32[]{:S(2)}, u32[]{:S(2)}) collective-permute-start(f16[256,1024]{1,0:T(8,128)(2,1)} %multiply_convert_fusion.6), channel_id=1, source_target_pairs={{2,4},{4,2},{6,8},{8,6},{10,12},{12,10},{14,16},{16,14},{18,20},{2... | collective-permute-start | bytes 1572872 | tf_op jit(solution)/shard_map/ppermute | solution.py:30
  49.9 14.4 %copy-start.1 = (f32[1536,1024]{1,0:T(8,128)S(1)}, f32[1536,1024]{1,0:T(8,128)}, u32[]{:S(2)}) copy-start(f32[1536,1024]{1,0:T(8,128)} %bitcast_subtract_fusion) | copy-start | bytes 18874372
  49.9 15.7 %copy-start.8 = (f16[256,1024]{1,0:T(8,128)(2,1)S(1)}, f16[256,1024]{1,0:T(8,128)(2,1)}, u32[]{:S(2)}) copy-start(f16[256,1024]{1,0:T(8,128)(2,1)} %get-tuple-element.157) | copy-start | bytes 1572868
  49.9 24.3 %copy-start.7 = (f16[256,1024]{1,0:T(8,128)(2,1)S(1)}, f16[256,1024]{1,0:T(8,128)(2,1)}, u32[]{:S(2)}) copy-start(f16[256,1024]{1,0:T(8,128)(2,1)} %get-tuple-element.166) | copy-start | bytes 1572868
  50.2 22.0 %collective-permute-start.11 = (f16[256,1024]{1,0:T(8,128)(2,1)}, f16[256,1024]{1,0:T(8,128)(2,1)S(1)}, u32[]{:S(2)}, u32[]{:S(2)}) collective-permute-start(f16[256,1024]{1,0:T(8,128)(2,1)} %get-tuple-element.148), channel_id=1, source_target_pairs={{0,1},{1,0},{2,3},{3,2},{4,5},{5,4},{6,7},{7,6},{8,9},{9,8},{10,11... | collective-permute-start | bytes 1572872 | tf_op jit(solution)/shard_map/ppermute | solution.py:21
  53.6 10.7 %collective-permute-start.10 = (f16[256,1024]{1,0:T(8,128)(2,1)S(1)}, f16[256,1024]{1,0:T(8,128)(2,1)S(1)}, u32[]{:S(2)}, u32[]{:S(2)}) collective-permute-start(f16[256,1024]{1,0:T(8,128)(2,1)S(1)} %multiply_convert_fusion.5), channel_id=1, source_target_pairs={{0,2},{2,0},{4,6},{6,4},{8,10},{10,8},{12,14},{14,12},{16,18},{18,... | collective-permute-start | bytes 1572872 | tf_op jit(solution)/shard_map/ppermute | solution.py:30
  55.3 42.9 %copy-start.9 = (f16[128,1024]{1,0:T(8,128)(2,1)S(1)}, f16[128,1024]{1,0:T(8,128)(2,1)}, u32[]{:S(2)}) copy-start(f16[128,1024]{1,0:T(8,128)(2,1)} %slice.166) | copy-start | bytes 786436
  56.9 15.3 %collective-permute-start.12 = (f16[256,1024]{1,0:T(8,128)(2,1)S(1)}, f16[256,1024]{1,0:T(8,128)(2,1)S(1)}, u32[]{:S(2)}, u32[]{:S(2)}) collective-permute-start(f16[256,1024]{1,0:T(8,128)(2,1)S(1)} %multiply_convert_fusion.5), channel_id=1, source_target_pairs={{2,4},{4,2},{6,8},{8,6},{10,12},{12,10},{14,16},{16,14},{18,20},{2... | collective-permute-start | bytes 1572872 | tf_op jit(solution)/shard_map/ppermute | solution.py:30
  65.6 6.6 %collective-permute-start.13 = (f16[256,1024]{1,0:T(8,128)(2,1)S(1)}, f16[256,1024]{1,0:T(8,128)(2,1)S(1)}, u32[]{:S(2)}, u32[]{:S(2)}) collective-permute-start(f16[256,1024]{1,0:T(8,128)(2,1)S(1)} %multiply_convert_fusion.4), channel_id=1, source_target_pairs={{0,2},{2,0},{4,6},{6,4},{8,10},{10,8},{12,14},{14,12},{16,18},{18,... | collective-permute-start | bytes 1572872 | tf_op jit(solution)/shard_map/ppermute | solution.py:30
  65.7 17.8 %collective-permute-start.14 = (f16[256,1024]{1,0:T(8,128)(2,1)S(1)}, f16[256,1024]{1,0:T(8,128)(2,1)S(1)}, u32[]{:S(2)}, u32[]{:S(2)}) collective-permute-start(f16[256,1024]{1,0:T(8,128)(2,1)S(1)} %copy-done.8), channel_id=1, source_target_pairs={{0,1},{1,0},{2,3},{3,2},{4,5},{5,4},{6,7},{7,6},{8,9},{9,8},{10,11... | collective-permute-start | bytes 1572872 | tf_op jit(solution)/shard_map/ppermute | solution.py:21
  66.0 22.4 %collective-permute-start.15 = (f16[256,1024]{1,0:T(8,128)(2,1)S(1)}, f16[256,1024]{1,0:T(8,128)(2,1)S(1)}, u32[]{:S(2)}, u32[]{:S(2)}) collective-permute-start(f16[256,1024]{1,0:T(8,128)(2,1)S(1)} %multiply_convert_fusion.4), channel_id=1, source_target_pairs={{2,4},{4,2},{6,8},{8,6},{10,12},{12,10},{14,16},{16,14},{18,20},{2... | collective-permute-start | bytes 1572872 | tf_op jit(solution)/shard_map/ppermute | solution.py:30
  72.4 16.0 %collective-permute-start.16 = (f16[256,1024]{1,0:T(8,128)(2,1)S(1)}, f16[256,1024]{1,0:T(8,128)(2,1)S(1)}, u32[]{:S(2)}, u32[]{:S(2)}) collective-permute-start(f16[256,1024]{1,0:T(8,128)(2,1)S(1)} %multiply_convert_fusion.3), channel_id=1, source_target_pairs={{0,2},{2,0},{4,6},{6,4},{8,10},{10,8},{12,14},{14,12},{16,18},{18,... | collective-permute-start | bytes 1572872 | tf_op jit(solution)/shard_map/ppermute | solution.py:30
  74.3 20.4 %collective-permute-start.17 = (f16[256,1024]{1,0:T(8,128)(2,1)S(1)}, f16[256,1024]{1,0:T(8,128)(2,1)S(1)}, u32[]{:S(2)}, u32[]{:S(2)}) collective-permute-start(f16[256,1024]{1,0:T(8,128)(2,1)S(1)} %copy-done.7), channel_id=1, source_target_pairs={{0,1},{1,0},{2,3},{3,2},{4,5},{5,4},{6,7},{7,6},{8,9},{9,8},{10,11... | collective-permute-start | bytes 1572872 | tf_op jit(solution)/shard_map/ppermute | solution.py:21
  75.1 22.9 %collective-permute-start.18 = (f16[256,1024]{1,0:T(8,128)(2,1)S(1)}, f16[256,1024]{1,0:T(8,128)(2,1)S(1)}, u32[]{:S(2)}, u32[]{:S(2)}) collective-permute-start(f16[256,1024]{1,0:T(8,128)(2,1)S(1)} %multiply_convert_fusion.3), channel_id=1, source_target_pairs={{2,4},{4,2},{6,8},{8,6},{10,12},{12,10},{14,16},{16,14},{18,20},{2... | collective-permute-start | bytes 1572872 | tf_op jit(solution)/shard_map/ppermute | solution.py:30
  88.6 23.9 %copy-start.5 = (f32[512,1024]{1,0:T(8,128)S(1)}, f32[512,1024]{1,0:T(8,128)}, u32[]{:S(2)}) copy-start(f32[512,1024]{1,0:T(8,128)} %copy-done.3) | copy-start | bytes 6291460
  88.6 9.3 %collective-permute-start.19 = (f16[256,1024]{1,0:T(8,128)(2,1)S(1)}, f16[256,1024]{1,0:T(8,128)(2,1)S(1)}, u32[]{:S(2)}, u32[]{:S(2)}) collective-permute-start(f16[256,1024]{1,0:T(8,128)(2,1)S(1)} %multiply_convert_fusion.2), channel_id=1, source_target_pairs={{0,2},{2,0},{4,6},{6,4},{8,10},{10,8},{12,14},{14,12},{16,18},{18,... | collective-permute-start | bytes 1572872 | tf_op jit(solution)/shard_map/ppermute | solution.py:30
  88.7 17.1 %collective-permute-start.21 = (f16[256,1024]{1,0:T(8,128)(2,1)S(1)}, f16[256,1024]{1,0:T(8,128)(2,1)S(1)}, u32[]{:S(2)}, u32[]{:S(2)}) collective-permute-start(f16[256,1024]{1,0:T(8,128)(2,1)S(1)} %multiply_convert_fusion.2), channel_id=1, source_target_pairs={{2,4},{4,2},{6,8},{8,6},{10,12},{12,10},{14,16},{16,14},{18,20},{2... | collective-permute-start | bytes 1572872 | tf_op jit(solution)/shard_map/ppermute | solution.py:30
  98.1 7.6 %collective-permute-start.22 = (f16[256,1024]{1,0:T(8,128)(2,1)S(1)}, f16[256,1024]{1,0:T(8,128)(2,1)S(1)}, u32[]{:S(2)}, u32[]{:S(2)}) collective-permute-start(f16[256,1024]{1,0:T(8,128)(2,1)S(1)} %multiply_convert_fusion.1), channel_id=1, source_target_pairs={{0,2},{2,0},{4,6},{6,4},{8,10},{10,8},{12,14},{14,12},{16,18},{18,... | collective-permute-start | bytes 1572872 | tf_op jit(solution)/shard_map/ppermute | solution.py:30
  98.2 7.5 %collective-permute-start.20 = (f16[128,1024]{1,0:T(8,128)(2,1)S(1)}, f16[128,1024]{1,0:T(8,128)(2,1)S(1)}, u32[]{:S(2)}, u32[]{:S(2)}) collective-permute-start(f16[128,1024]{1,0:T(8,128)(2,1)S(1)} %copy-done.9), channel_id=1, source_target_pairs={{0,1},{1,0},{2,3},{3,2},{4,5},{5,4},{6,7},{7,6},{8,9},{9,8},{10,11... | collective-permute-start | bytes 786440 | tf_op jit(solution)/shard_map/ppermute | solution.py:21
  98.9 12.4 %collective-permute-start.23 = (f16[128,1024]{1,0:T(8,128)(2,1)S(1)}, f16[128,1024]{1,0:T(8,128)(2,1)S(1)}, u32[]{:S(2)}, u32[]{:S(2)}) collective-permute-start(f16[128,1024]{1,0:T(8,128)(2,1)S(1)} %get-tuple-element.182), channel_id=1, source_target_pairs={{0,1},{1,0},{2,3},{3,2},{4,5},{5,4},{6,7},{7,6},{8,9},{9,8},{10,11... | collective-permute-start | bytes 786440 | tf_op jit(solution)/shard_map/ppermute | solution.py:21
  99.7 19.9 %collective-permute-start.24 = (f16[256,1024]{1,0:T(8,128)(2,1)S(1)}, f16[256,1024]{1,0:T(8,128)(2,1)S(1)}, u32[]{:S(2)}, u32[]{:S(2)}) collective-permute-start(f16[256,1024]{1,0:T(8,128)(2,1)S(1)} %multiply_convert_fusion.1), channel_id=1, source_target_pairs={{2,4},{4,2},{6,8},{8,6},{10,12},{12,10},{14,16},{16,14},{18,20},{2... | collective-permute-start | bytes 1572872 | tf_op jit(solution)/shard_map/ppermute | solution.py:30
  105.8 15.9 %collective-permute-start.26 = (f16[128,1024]{1,0:T(8,128)(2,1)S(1)}, f16[128,1024]{1,0:T(8,128)(2,1)S(1)}, u32[]{:S(2)}, u32[]{:S(2)}) collective-permute-start(f16[128,1024]{1,0:T(8,128)(2,1)S(1)} %multiply_convert_fusion.9), channel_id=1, source_target_pairs={{2,4},{4,2},{6,8},{8,6},{10,12},{12,10},{14,16},{16,14},{18,20},{2... | collective-permute-start | bytes 786440 | tf_op jit(solution)/shard_map/ppermute | solution.py:30
  110.0 11.7 %collective-permute-start.25 = (f16[128,1024]{1,0:T(8,128)(2,1)S(1)}, f16[128,1024]{1,0:T(8,128)(2,1)S(1)}, u32[]{:S(2)}, u32[]{:S(2)}) collective-permute-start(f16[128,1024]{1,0:T(8,128)(2,1)S(1)} %multiply_convert_fusion.9), channel_id=1, source_target_pairs={{0,2},{2,0},{4,6},{6,4},{8,10},{10,8},{12,14},{14,12},{16,18},{18,... | collective-permute-start | bytes 786440 | tf_op jit(solution)/shard_map/ppermute | solution.py:30
  120.1 3.4 %copy-start.2 = (f32[1,2048,1024]{2,1,0:T(8,128)}, f32[1,2048,1024]{2,1,0:T(8,128)S(1)}, u32[]{:S(2)}) copy-start(f32[1,2048,1024]{2,1,0:T(8,128)S(1)} %bitcast_dynamic-update-slice_fusion) | copy-start | bytes 25165828

commit v14 on v13

--- a/solution.py
+++ b/solution.py
@@ -10,7 +10,7 @@
 LARGEST = 6.0
 WIRE = jnp.float16
 STEP = 256
-FIRST = 128
+FIRST = 256
 AHEAD = 3
 MIXLAG = 99
 
@@ -102,11 +102,10 @@
     out = jnp.zeros_like(weights)
     split = cuts[min(2, chunks)]
     terms = {0: for_others(0, cuts[1])}
+    arrived = {0: add_over_fsdp(terms[0])}
 
-    terms[0], later = lax.optimization_barrier((terms[0], shard))
-    arrived = {0: add_over_fsdp(terms[0])}
-    parts = [own_part(later, main, rows)]
-    parts += [-RATE * partial(owner(away, later), main, first) for away in range(1, shards)]
+    parts = [own_part(shard, main, rows)]
+    parts += [-RATE * partial(owner(away), main, first) for away in range(1, shards)]
     parts = jnp.concatenate(parts, axis=0)
     parts, sent = lax.optimization_barrier((parts, (parts * scale).astype(WIRE)))
     far[-1] = swapped(sent, "blk", 1)
@@ -115,7 +114,7 @@
     if chunks > 1:
         parts, later = lax.optimization_barrier((parts, shard))
         rest = [
-            (partial(owner(away, later), cuts[1], rows - cuts[1]) * (RATE * scale)).astype(WIRE)
+            (partial(owner(away, later), cuts[1], main - cuts[1]) * (RATE * scale)).astype(WIRE)
             for away in range(1, shards)
         ]
         for chunk in range(1, chunks):
@@ -140,7 +139,7 @@
         sent = (u_of(chunk) * scale).astype(WIRE)
         sent, base, out, later = lax.optimization_barrier((sent, base, out, shard))
         if chunk == 0 and split < main:
-            base.append(own_part(later, split, rows))
+            base.append(own_part(later, split, main))
         if chunk == middle:
             mix, parts, sent = lax.optimization_barrier((mix, parts, sent))
             coeff = lax.optimization_barrier(coefficients(mix))

time: 126 us -> 121 us (0.960)
  waiting for transfers between devices: 41.6 us -> 51.8 us
  starting transfers between devices: 30.7 us -> 22.6 us
  local copies, waits for them, and re-layouts: 10.1 us -> 4.87 us
    ppermute x18 -> x16, starting transfers between devices: 22.9 us -> 15.7 us  [swapped(): return lax.ppermute(value, axis, pairs)]
    ppermute x18 -> x16, waiting for transfers between devices: 13.1 us -> 19.9 us  [swapped(): return lax.ppermute(value, axis, pairs)]
    unnamed x22 -> x20, local copies, waits for them, and re-layouts: 5.1 us -> 1.54 us
    ppermute x9 -> x8, waiting for transfers between devices: 28.5 us -> 31.9 us  [from_behind(): return lax.ppermute(value, axis, pairs)]
    convert_element_type x8 -> x7, other arithmetic: 7.04 us -> 5.33 us  [on_device(): sent = (u_of(chunk) * scale).astype(WIRE)]
    slice x2 -> x1, local copies, waits for them, and re-layouts: 3.85 us -> 2.18 us  [on_device(): term[cuts[chunk] - cuts[1]:cuts[chunk + 1] - cuts[1]]]
    add x1, other arithmetic: 1.52 us -> 2.87 us  [mixture(): coeff[0:1] * (near.astype(jnp.float32) / scale) + coeff[1:2] * own]
    dynamic_update_slice x8 -> x7, other arithmetic: 8.53 us -> 7.3 us  [mix_into(): return lax.dynamic_update_slice_in_dim(out, value, cuts[chunk], axis=0)]
  transfers between devices with their start and end apart: 27 -> 24, of which waited for: 11 -> 12; matrix products, arithmetic and copies ran while one was open for 31% -> 30% of each run, Pallas kernels for 0% -> 0%
where the time goes in v14:
time: 121 us; the launch traced here: 120 us
  waiting for transfers between devices  51.8 us (43%)
  starting transfers between devices  22.6 us (19%)
  matrix products  22.2 us (18%)
  other arithmetic  18.3 us (15%)
  local copies, waits for them, and re-layouts  4.87 us (4%)
    ppermute x8, waiting for transfers between devices, from_behind(): return lax.ppermute(value, axis, pairs)  31.9 us
    dot_general x6, matrix products, partial(): lax.dot_general(block, cot_local, (((0,), (0,)), ((), ())), preferred_ele...  22.2 us
    ppermute x16, waiting for transfers between devices, swapped(): return lax.ppermute(value, axis, pairs)  19.9 us
    ppermute x16, starting transfers between devices, swapped(): return lax.ppermute(value, axis, pairs)  15.7 us
    dynamic_update_slice x7, other arithmetic, mix_into(): return lax.dynamic_update_slice_in_dim(out, value, cuts[chunk], axis=0)  7.3 us
    ppermute x8, starting transfers between devices, from_behind(): return lax.ppermute(value, axis, pairs)  6.87 us
    convert_element_type x7, other arithmetic, on_device(): sent = (u_of(chunk) * scale).astype(WIRE)  5.33 us
    add x1, other arithmetic, mixture(): coeff[0:1] * (near.astype(jnp.float32) / scale) + coeff[1:2] * own  2.87 us
  transfers between devices with their start and end apart: 24, of which 12 were waited for; matrix products, arithmetic and copies ran while one was open for 30% of the time, Pallas kernels for 0%

profile of v14, /device:TPU:1, one launch (start us, length us, event | category | flops | bytes accessed | tf_op | source)
XLA Modules:
  0.0 120.1 jit_solution(6594578023051495686)
XLA Ops:
  0.0 1.5 %copy-done = bf16[1,896,1024]{2,1,0:T(8,128)(2,1)S(1)} copy-done((bf16[1,896,1024]{2,1,0:T(8,128)(2,1)S(1)}, bf16[1,896,1024]{2,1,0:T(8,128)(2,1)}, u32[]{:S(2)}) %copy-start) | copy-done | bytes 1835032
  1.5 1.7 %fusion.22 = f32[256,1024]{1,0:T(8,128)S(1)} fusion(bf16[1,896,1024]{2,1,0:T(8,128)(2,1)S(1)} %copy-done, bf16[1,896,4096]{2,1,0:T(8,128)(2,1)} %param.5, s32[]{:T(128)S(6)} %select_n.45), kind=kOutput, calls=%fused_computation.22 | convolution fusion | flops 470024192 | bytes 3342340 | tf_op jit(solution)/shard_map/dot_general | solution.py:65
  3.2 2.1 %fusion.19 = f32[256,1024]{1,0:T(8,128)S(1)} fusion(bf16[1,896,1024]{2,1,0:T(8,128)(2,1)S(1)} %copy-done, f32[1,2048,1024]{2,1,0:T(8,128)} %param.4, bf16[1,896,4096]{2,1,0:T(8,128)(2,1)} %param.5, s32[]{:T(128)S(6)} %select_n.43), kind=kOutput, calls=%fused_computation.21 | convolution fusion | flops 470286336 | bytes 4390916 | tf_op jit(solution)/shard_map/dot_general | solution.py:65
  5.4 2.1 %multiply_convert_fusion.1 = (f16[512,1024]{1,0:T(8,128)(2,1)}, f32[512,1024]{1,0:T(8,128)}) fusion(f32[256,1024]{1,0:T(8,128)S(1)} %fusion.22, f32[256,1024]{1,0:T(8,128)S(1)} %fusion.19), kind=kLoop, calls=%fused_computation.9 | loop fusion | flops 1572864 | bytes 5242880 | tf_op jit(solution)/shard_map/convert_element_type | solution.py:110
  7.5 2.6 %collective-permute-start.3 = (f16[512,1024]{1,0:T(8,128)(2,1)}, f16[512,1024]{1,0:T(8,128)(2,1)}, u32[]{:S(2)}, u32[]{:S(2)}) collective-permute-start(f16[512,1024]{1,0:T(8,128)(2,1)} %get-tuple-element.91), channel_id=1, source_target_pairs={{2,4},{4,2},{6,8},{8,6},{10,12},{12,10},{14,16},{16,14},{18,20},{2... | collective-permute-start | bytes 3145736 | tf_op jit(solution)/shard_map/ppermute | solution.py:30
  10.1 2.9 %collective-permute-start.2 = (f16[512,1024]{1,0:T(8,128)(2,1)}, f16[512,1024]{1,0:T(8,128)(2,1)}, u32[]{:S(2)}, u32[]{:S(2)}) collective-permute-start(f16[512,1024]{1,0:T(8,128)(2,1)} %get-tuple-element.91), channel_id=1, source_target_pairs={{0,2},{2,0},{4,6},{6,4},{8,10},{10,8},{12,14},{14,12},{16,18},{18,... | collective-permute-start | bytes 3145736 | tf_op jit(solution)/shard_map/ppermute | solution.py:30
  13.0 2.5 %fusion.28 = f16[256,1024]{1,0:T(8,128)(2,1)} fusion(bf16[1,896,1024]{2,1,0:T(8,128)(2,1)S(1)} %copy-done, bf16[1,896,4096]{2,1,0:T(8,128)(2,1)} %param.5, s32[]{:T(128)S(6)} %select_n.48), kind=kOutput, calls=%fused_computation.24 | convolution fusion | flops 470286336 | bytes 2818052 | tf_op jit(solution)/shard_map/dot_general | solution.py:65
  15.5 1.2 %collective-permute-start.1 = (f16[256,1024]{1,0:T(8,128)(2,1)}, f16[256,1024]{1,0:T(8,128)(2,1)S(1)}, u32[]{:S(2)}, u32[]{:S(2)}) collective-permute-start(f16[256,1024]{1,0:T(8,128)(2,1)} %fusion.28), channel_id=1, source_target_pairs={{0,1},{1,0},{2,3},{3,2},{4,5},{5,4},{6,7},{7,6},{8,9},{9,8},{10,11... | collective-permute-start | bytes 1572872 | tf_op jit(solution)/shard_map/ppermute | solution.py:21
  16.8 5.5 %multiply_convert_fusion = f16[1536,1024]{1,0:T(8,128)(2,1)S(1)} fusion(bf16[1,896,4096]{2,1,0:T(8,128)(2,1)} %param.5, s32[]{:T(128)S(6)} %select_n.47, bf16[1,896,1024]{2,1,0:T(8,128)(2,1)S(1)} %copy-done), kind=kOutput, calls=%fused_computation | convolution fusion | flops 2821718016 | bytes 7733252 | tf_op jit(solution)/shard_map/dot_general | solution.py:65
  22.2 2.2 %fusion.47 = (f16[256,1024]{1,0:T(8,128)(2,1)}, f16[256,1024]{1,0:T(8,128)(2,1)}, f16[256,1024]{1,0:T(8,128)(2,1)}, f16[256,1024]{1,0:T(8,128)(2,1)}, f16[256,1024]{1,0:T(8,128)(2,1)}, /*index=5*/f16[256,1024]{1,0:T(8,128)(2,1)}) fusion(f16[1536,1024]{1,0:T(8,128)(2,1)S(1)} %multiply_convert_fusion), kind=kLoop, calls=%fused_computation.68 | loop fusion | bytes 6291456 | tf_op jit(solution)/shard_map/slice | solution.py:121
  24.4 0.2 collective-permute-start
  24.6 3.2 %bitcast_subtract_fusion.1 = f32[512,1024]{1,0:T(8,128)S(1)} fusion(f32[1,2048,1024]{2,1,0:T(8,128)} %param.4, bf16[1,896,1024]{2,1,0:T(8,128)(2,1)S(1)} %copy-done, bf16[1,896,4096]{2,1,0:T(8,128)(2,1)} %param.5, s32[]{:T(128)S(6)} %select_n.49), kind=kOutput, calls=%fused_computation.7 | convolution fusion | flops 940572672 | bytes 6946820 | tf_op jit(solution)/shard_map/dot_general | solution.py:65
  27.8 1.3 %collective-permute-start.5 = (f16[256,1024]{1,0:T(8,128)(2,1)}, f16[256,1024]{1,0:T(8,128)(2,1)S(1)}, u32[]{:S(2)}, u32[]{:S(2)}) collective-permute-start(f16[256,1024]{1,0:T(8,128)(2,1)} %get-tuple-element.92), channel_id=1, source_target_pairs={{0,1},{1,0},{2,3},{3,2},{4,5},{5,4},{6,7},{7,6},{8,9},{9,8},{10,11... | collective-permute-start | bytes 1572872 | tf_op jit(solution)/shard_map/ppermute | solution.py:21
  29.1 0.2 collective-permute-done.1
  29.3 1.0 multiply_convert_fusion.8
  30.3 0.0 collective-permute-start.6
  30.3 1.1 collective-permute-start.4
  31.5 7.2 %bitcast_subtract_fusion = f32[1280,1024]{1,0:T(8,128)} fusion(f32[1,2048,1024]{2,1,0:T(8,128)} %param.4, bf16[1,896,4096]{2,1,0:T(8,128)(2,1)} %param.5, s32[]{:T(128)S(6)} %select_n.50, bf16[1,896,1024]{2,1,0:T(8,128)(2,1)S(1)} %copy-done), kind=kOutput, calls=%fused_computation.1 | convolution fusion | flops 2351431680 | bytes 14614532 | tf_op jit(solution)/shard_map/dot_general | solution.py:65
  38.7 1.9 %collective-permute-done = f16[256,1024]{1,0:T(8,128)(2,1)S(1)} collective-permute-done((f16[256,1024]{1,0:T(8,128)(2,1)}, f16[256,1024]{1,0:T(8,128)(2,1)S(1)}, u32[]{:S(2)}, u32[]{:S(2)}) %collective-permute-start) | collective-permute-done | bytes 524320 | tf_op jit(solution)/shard_map/ppermute | solution.py:21
  40.6 1.0 multiply_convert_fusion.7
  41.7 1.1 collective-permute-start.7
  42.7 1.2 %collective-permute-start.8 = (f16[256,1024]{1,0:T(8,128)(2,1)}, f16[256,1024]{1,0:T(8,128)(2,1)}, u32[]{:S(2)}, u32[]{:S(2)}) collective-permute-start(f16[256,1024]{1,0:T(8,128)(2,1)} %get-tuple-element.119), channel_id=1, source_target_pairs={{0,1},{1,0},{2,3},{3,2},{4,5},{5,4},{6,7},{7,6},{8,9},{9,8},{10,11... | collective-permute-start | bytes 1572872 | tf_op jit(solution)/shard_map/ppermute | solution.py:21
  44.0 0.1 collective-permute-start.9
  44.0 7.8 %collective-permute-done.5 = f16[256,1024]{1,0:T(8,128)(2,1)S(1)} collective-permute-done((f16[256,1024]{1,0:T(8,128)(2,1)}, f16[256,1024]{1,0:T(8,128)(2,1)S(1)}, u32[]{:S(2)}, u32[]{:S(2)}) %collective-permute-start.5) | collective-permute-done | bytes 524320 | tf_op jit(solution)/shard_map/ppermute | solution.py:21
  51.9 0.1 fusion.46
  52.0 0.2 multiply_reduce_fusion
  52.2 0.1 broadcast_in_dim.28
  52.2 1.2 %collective-permute-start.11 = (f16[256,1024]{1,0:T(8,128)(2,1)}, f16[256,1024]{1,0:T(8,128)(2,1)S(1)}, u32[]{:S(2)}, u32[]{:S(2)}) collective-permute-start(f16[256,1024]{1,0:T(8,128)(2,1)} %get-tuple-element.133), channel_id=1, source_target_pairs={{0,1},{1,0},{2,3},{3,2},{4,5},{5,4},{6,7},{7,6},{8,9},{9,8},{10,11... | collective-permute-start | bytes 1572872 | tf_op jit(solution)/shard_map/ppermute | solution.py:21
  53.5 1.4 %multiply_convert_fusion.6 = f16[256,1024]{1,0:T(8,128)(2,1)S(1)} fusion(f16[256,1024]{1,0:T(8,128)(2,1)S(1)} %collective-permute-done.5, f32[1280,1024]{1,0:T(8,128)} %bitcast_subtract_fusion), kind=kLoop, calls=%fused_computation.43 | loop fusion | flops 1310720 | bytes 2097152 | tf_op jit(solution)/shard_map/convert_element_type | solution.py:139
  54.9 1.4 %collective-permute-start.10 = (f16[256,1024]{1,0:T(8,128)(2,1)S(1)}, f16[256,1024]{1,0:T(8,128)(2,1)S(1)}, u32[]{:S(2)}, u32[]{:S(2)}) collective-permute-start(f16[256,1024]{1,0:T(8,128)(2,1)S(1)} %multiply_convert_fusion.6), channel_id=1, source_target_pairs={{0,2},{2,0},{4,6},{6,4},{8,10},{10,8},{12,14},{14,12},{16,18},{18,... | collective-permute-start | bytes 1572872 | tf_op jit(solution)/shard_map/ppermute | solution.py:30
  56.4 2.9 %multiply_add_fusion = f32[512,1024]{1,0:T(8,128)S(1)} fusion(f16[512,1024]{1,0:T(8,128)(2,1)} %collective-permute-done.3, f32[512,1024]{1,0:T(8,128)} %get-tuple-element.127, f16[512,1024]{1,0:T(8,128)(2,1)} %collective-permute-done.2, f32[1024]{0:T(1024)S(1)} %bitcast.80, f32[1024]{0:T(1024)S(1)} %bitcast.88, f32[1024]{0:T(1024)S(1)} %bitcast.72), kind=kLoop, calls=%fused_computation.8 | loop fusion | flops 3670016 | bytes 6303744 | tf_op jit(solution)/shard_map/add | solution.py:90
  59.2 0.2 fusion.31
  59.4 0.1 collective-permute-start.12
  59.5 3.6 %collective-permute-done.8 = f16[256,1024]{1,0:T(8,128)(2,1)} collective-permute-done((f16[256,1024]{1,0:T(8,128)(2,1)}, f16[256,1024]{1,0:T(8,128)(2,1)}, u32[]{:S(2)}, u32[]{:S(2)}) %collective-permute-start.8) | collective-permute-done | bytes 524320 | tf_op jit(solution)/shard_map/ppermute | solution.py:21
  63.1 1.2 %multiply_convert_fusion.5 = f16[256,1024]{1,0:T(8,128)(2,1)S(1)} fusion(f16[256,1024]{1,0:T(8,128)(2,1)} %collective-permute-done.8, f32[1280,1024]{1,0:T(8,128)S(1)} %bitcast.70), kind=kLoop, calls=%fused_computation.41 | loop fusion | flops 1310720 | bytes 2097152 | tf_op jit(solution)/shard_map/convert_element_type | solution.py:139
  64.4 1.2 %collective-permute-start.13 = (f16[256,1024]{1,0:T(8,128)(2,1)S(1)}, f16[256,1024]{1,0:T(8,128)(2,1)S(1)}, u32[]{:S(2)}, u32[]{:S(2)}) collective-permute-start(f16[256,1024]{1,0:T(8,128)(2,1)S(1)} %multiply_convert_fusion.5), channel_id=1, source_target_pairs={{0,2},{2,0},{4,6},{6,4},{8,10},{10,8},{12,14},{14,12},{16,18},{18,... | collective-permute-start | bytes 1572872 | tf_op jit(solution)/shard_map/ppermute | solution.py:30
  65.6 1.3 %collective-permute-start.14 = (f16[256,1024]{1,0:T(8,128)(2,1)S(1)}, f16[256,1024]{1,0:T(8,128)(2,1)S(1)}, u32[]{:S(2)}, u32[]{:S(2)}) collective-permute-start(f16[256,1024]{1,0:T(8,128)(2,1)S(1)} %copy-done.6), channel_id=1, source_target_pairs={{0,1},{1,0},{2,3},{3,2},{4,5},{5,4},{6,7},{7,6},{8,9},{9,8},{10,11... | collective-permute-start | bytes 1572872 | tf_op jit(solution)/shard_map/ppermute | solution.py:21
  66.9 7.4 %collective-permute-done.11 = f16[256,1024]{1,0:T(8,128)(2,1)S(1)} collective-permute-done((f16[256,1024]{1,0:T(8,128)(2,1)}, f16[256,1024]{1,0:T(8,128)(2,1)S(1)}, u32[]{:S(2)}, u32[]{:S(2)}) %collective-permute-start.11) | collective-permute-done | bytes 524320 | tf_op jit(solution)/shard_map/ppermute | solution.py:21
  74.2 5.4 %collective-permute-done.12 = f16[256,1024]{1,0:T(8,128)(2,1)S(1)} collective-permute-done((f16[256,1024]{1,0:T(8,128)(2,1)S(1)}, f16[256,1024]{1,0:T(8,128)(2,1)S(1)}, u32[]{:S(2)}, u32[]{:S(2)}) %collective-permute-start.12) | collective-permute-done | bytes 524320 | tf_op jit(solution)/shard_map/ppermute | solution.py:30
  79.6 0.2 multiply_convert_fusion.4
  79.9 0.1 collective-permute-start.16
  79.9 0.3 collective-permute-start.17
  80.2 5.2 %collective-permute-done.14 = f16[256,1024]{1,0:T(8,128)(2,1)S(1)} collective-permute-done((f16[256,1024]{1,0:T(8,128)(2,1)S(1)}, f16[256,1024]{1,0:T(8,128)(2,1)S(1)}, u32[]{:S(2)}, u32[]{:S(2)}) %collective-permute-start.14) | collective-permute-done | bytes 524320 | tf_op jit(solution)/shard_map/ppermute | solution.py:21
  85.5 2.7 %collective-permute-done.15 = f16[256,1024]{1,0:T(8,128)(2,1)S(1)} collective-permute-done((f16[256,1024]{1,0:T(8,128)(2,1)S(1)}, f16[256,1024]{1,0:T(8,128)(2,1)S(1)}, u32[]{:S(2)}, u32[]{:S(2)}) %collective-permute-start.15) | collective-permute-done | bytes 524320 | tf_op jit(solution)/shard_map/ppermute | solution.py:30
  88.1 0.2 multiply_convert_fusion.3
  88.3 0.1 collective-permute-start.19
  88.4 0.1 collective-permute-start.20
  88.5 2.5 %collective-permute-start.21 = (f16[256,1024]{1,0:T(8,128)(2,1)S(1)}, f16[256,1024]{1,0:T(8,128)(2,1)S(1)}, u32[]{:S(2)}, u32[]{:S(2)}) collective-permute-start(f16[256,1024]{1,0:T(8,128)(2,1)S(1)} %multiply_convert_fusion.3), channel_id=1, source_target_pairs={{2,4},{4,2},{6,8},{8,6},{10,12},{12,10},{14,16},{16,14},{18,20},{2... | collective-permute-start | bytes 1572872 | tf_op jit(solution)/shard_map/ppermute | solution.py:30
  91.0 5.7 %collective-permute-done.17 = f16[256,1024]{1,0:T(8,128)(2,1)S(1)} collective-permute-done((f16[256,1024]{1,0:T(8,128)(2,1)S(1)}, f16[256,1024]{1,0:T(8,128)(2,1)S(1)}, u32[]{:S(2)}, u32[]{:S(2)}) %collective-permute-start.17) | collective-permute-done | bytes 524320 | tf_op jit(solution)/shard_map/ppermute | solution.py:21
  96.7 8.3 %collective-permute-done.18 = f16[256,1024]{1,0:T(8,128)(2,1)S(1)} collective-permute-done((f16[256,1024]{1,0:T(8,128)(2,1)S(1)}, f16[256,1024]{1,0:T(8,128)(2,1)S(1)}, u32[]{:S(2)}, u32[]{:S(2)}) %collective-permute-start.18) | collective-permute-done | bytes 524320 | tf_op jit(solution)/shard_map/ppermute | solution.py:30
  105.0 0.2 multiply_convert_fusion.2
  105.2 2.5 %collective-permute-start.23 = (f16[256,1024]{1,0:T(8,128)(2,1)S(1)}, f16[256,1024]{1,0:T(8,128)(2,1)S(1)}, u32[]{:S(2)}, u32[]{:S(2)}) collective-permute-start(f16[256,1024]{1,0:T(8,128)(2,1)S(1)} %multiply_convert_fusion.2), channel_id=1, source_target_pairs={{2,4},{4,2},{6,8},{8,6},{10,12},{12,10},{14,16},{16,14},{18,20},{2... | collective-permute-start | bytes 1572872 | tf_op jit(solution)/shard_map/ppermute | solution.py:30
  107.7 0.2 collective-permute-done.20
  107.9 1.1 broadcast_in_dim.27
  109.0 0.2 bitcast_dynamic-update-slice_fusion.7
  109.2 1.6 %bitcast_dynamic-update-slice_fusion.6 = f32[1,2048,1024]{2,1,0:T(8,128)S(1)} fusion(f32[1,2048,1024]{2,1,0:T(8,128)S(1)} %bitcast_dynamic-update-slice_fusion.7, f16[256,1024]{1,0:T(8,128)(2,1)} %collective-permute-done.6, f32[512,1024]{1,0:T(8,128)S(1)} %copy-done.4, f16[256,1024]{1,0:T(8,128)(2,1)} %collective-permute-done.4, ...), kind=kLoop, calls=%fused_computation.33 | loop fusion | flops 2621440 | bytes 3682304 | tf_op jit(solution)/shard_map/dynamic_update_slice | solution.py:97
  110.8 1.6 %bitcast_dynamic-update-slice_fusion.5 = f32[1,2048,1024]{2,1,0:T(8,128)S(1)} fusion(f32[1,2048,1024]{2,1,0:T(8,128)S(1)} %bitcast_dynamic-update-slice_fusion.6, f16[256,1024]{1,0:T(8,128)(2,1)} %collective-permute-done.9, f32[512,1024]{1,0:T(8,128)S(1)} %copy-done.4, f16[256,1024]{1,0:T(8,128)(2,1)} %collective-permute-done.7, ...), kind=kLoop, calls=%fused_computation.32 | loop fusion | flops 2621440 | bytes 3682304 | tf_op jit(solution)/shard_map/dynamic_update_slice | solution.py:97
  112.4 0.4 bitcast_dynamic-update-slice_fusion.4
  112.9 1.5 %bitcast_dynamic-update-slice_fusion.3 = f32[1,2048,1024]{2,1,0:T(8,128)S(1)} fusion(f32[1,2048,1024]{2,1,0:T(8,128)S(1)} %bitcast_dynamic-update-slice_fusion.4, f16[256,1024]{1,0:T(8,128)(2,1)S(1)} %collective-permute-done.15, f32[1280,1024]{1,0:T(8,128)S(1)} %bitcast.70, f16[256,1024]{1,0:T(8,128)(2,1)S(1)} %collective-permute-done.13, ...), kind=kLoop, calls=%fused_computation.30 | loop fusion | flops 2621440 | bytes 3682304 | tf_op jit(solution)/shard_map/dynamic_update_slice | solution.py:97
  114.3 0.4 bitcast_dynamic-update-slice_fusion.2
  114.7 0.4 bitcast_dynamic-update-slice_fusion.1
  115.2 0.0 copy-start.1
  115.2 3.5 %collective-permute-done.23 = f16[256,1024]{1,0:T(8,128)(2,1)S(1)} collective-permute-done((f16[256,1024]{1,0:T(8,128)(2,1)S(1)}, f16[256,1024]{1,0:T(8,128)(2,1)S(1)}, u32[]{:S(2)}, u32[]{:S(2)}) %collective-permute-start.23) | collective-permute-done | bytes 524320 | tf_op jit(solution)/shard_map/ppermute | solution.py:30
  118.7 1.4 %bitcast_dynamic-update-slice_fusion = f32[1,2048,1024]{2,1,0:T(8,128)} fusion(f32[1,2048,1024]{2,1,0:T(8,128)} %copy-done.1, f16[256,1024]{1,0:T(8,128)(2,1)S(1)} %collective-permute-done.23, f32[1280,1024]{1,0:T(8,128)S(1)} %bitcast.70, f16[256,1024]{1,0:T(8,128)(2,1)S(1)} %collective-permute-done.22, f16[256,1024]{1,0:T(8,128)(2,1)S(1)} %collective-permute-done.17, ...), kind=kLoop, calls=%fused_computation.27 | loop fusion | flops 2621440 | bytes 3682304 | tf_op jit(solution)/shard_map/dynamic_update_slice | solution.py:97
  (36 shorter events, 0.1 us)
Async XLA Ops:
  0.0 1.5 %copy-start = (bf16[1,896,1024]{2,1,0:T(8,128)(2,1)S(1)}, bf16[1,896,1024]{2,1,0:T(8,128)(2,1)}, u32[]{:S(2)}) copy-start(bf16[1,896,1024]{2,1,0:T(8,128)(2,1)} %param.6) | copy-start | bytes 5505028
  7.5 33.1 %collective-permute-start.3 = (f16[512,1024]{1,0:T(8,128)(2,1)}, f16[512,1024]{1,0:T(8,128)(2,1)}, u32[]{:S(2)}, u32[]{:S(2)}) collective-permute-start(f16[512,1024]{1,0:T(8,128)(2,1)} %get-tuple-element.91), channel_id=1, source_target_pairs={{2,4},{4,2},{6,8},{8,6},{10,12},{12,10},{14,16},{16,14},{18,20},{2... | collective-permute-start | bytes 3145736 | tf_op jit(solution)/shard_map/ppermute | solution.py:30
  10.1 17.7 %collective-permute-start.2 = (f16[512,1024]{1,0:T(8,128)(2,1)}, f16[512,1024]{1,0:T(8,128)(2,1)}, u32[]{:S(2)}, u32[]{:S(2)}) collective-permute-start(f16[512,1024]{1,0:T(8,128)(2,1)} %get-tuple-element.91), channel_id=1, source_target_pairs={{0,2},{2,0},{4,6},{6,4},{8,10},{10,8},{12,14},{14,12},{16,18},{18,... | collective-permute-start | bytes 3145736 | tf_op jit(solution)/shard_map/ppermute | solution.py:30
  15.5 13.8 %collective-permute-start.1 = (f16[256,1024]{1,0:T(8,128)(2,1)}, f16[256,1024]{1,0:T(8,128)(2,1)S(1)}, u32[]{:S(2)}, u32[]{:S(2)}) collective-permute-start(f16[256,1024]{1,0:T(8,128)(2,1)} %fusion.28), channel_id=1, source_target_pairs={{0,1},{1,0},{2,3},{3,2},{4,5},{5,4},{6,7},{7,6},{8,9},{9,8},{10,11... | collective-permute-start | bytes 1572872 | tf_op jit(solution)/shard_map/ppermute | solution.py:21
  24.4 16.2 %collective-permute-start = (f16[256,1024]{1,0:T(8,128)(2,1)}, f16[256,1024]{1,0:T(8,128)(2,1)S(1)}, u32[]{:S(2)}, u32[]{:S(2)}) collective-permute-start(f16[256,1024]{1,0:T(8,128)(2,1)} %get-tuple-element.178), channel_id=1, source_target_pairs={{0,1},{1,0},{2,3},{3,2},{4,5},{5,4},{6,7},{7,6},{8,9},{9,8},{10,11... | collective-permute-start | bytes 1572872 | tf_op jit(solution)/shard_map/ppermute | solution.py:21
  27.8 1.5 %copy-start.2 = (f32[512,1024]{1,0:T(8,128)}, f32[512,1024]{1,0:T(8,128)S(1)}, u32[]{:S(2)}) copy-start(f32[512,1024]{1,0:T(8,128)S(1)} %bitcast_subtract_fusion.1) | copy-start | bytes 6291460
  27.8 24.0 %collective-permute-start.5 = (f16[256,1024]{1,0:T(8,128)(2,1)}, f16[256,1024]{1,0:T(8,128)(2,1)S(1)}, u32[]{:S(2)}, u32[]{:S(2)}) collective-permute-start(f16[256,1024]{1,0:T(8,128)(2,1)} %get-tuple-element.92), channel_id=1, source_target_pairs={{0,1},{1,0},{2,3},{3,2},{4,5},{5,4},{6,7},{7,6},{8,9},{9,8},{10,11... | collective-permute-start | bytes 1572872 | tf_op jit(solution)/shard_map/ppermute | solution.py:21
  30.3 21.5 %collective-permute-start.6 = (f16[256,1024]{1,0:T(8,128)(2,1)}, f16[256,1024]{1,0:T(8,128)(2,1)}, u32[]{:S(2)}, u32[]{:S(2)}) collective-permute-start(f16[256,1024]{1,0:T(8,128)(2,1)} %multiply_convert_fusion.8), channel_id=1, source_target_pairs={{2,4},{4,2},{6,8},{8,6},{10,12},{12,10},{14,16},{16,14},{18,20},{2... | collective-permute-start | bytes 1572872 | tf_op jit(solution)/shard_map/ppermute | solution.py:30
  30.3 10.3 %collective-permute-start.4 = (f16[256,1024]{1,0:T(8,128)(2,1)}, f16[256,1024]{1,0:T(8,128)(2,1)}, u32[]{:S(2)}, u32[]{:S(2)}) collective-permute-start(f16[256,1024]{1,0:T(8,128)(2,1)} %multiply_convert_fusion.8), channel_id=1, source_target_pairs={{0,2},{2,0},{4,6},{6,4},{8,10},{10,8},{12,14},{14,12},{16,18},{18,... | collective-permute-start | bytes 1572872 | tf_op jit(solution)/shard_map/ppermute | solution.py:30
  31.5 9.1 %copy-start.3 = (f32[512,1024]{1,0:T(8,128)S(1)}, f32[512,1024]{1,0:T(8,128)}, u32[]{:S(2)}) copy-start(f32[512,1024]{1,0:T(8,128)} %copy-done.2) | copy-start | bytes 6291460
  31.5 20.4 %copy-start.7 = (s32[16,3]{0,1:T(4,128)S(1)}, s32[16,3]{0,1:T(4,128)}, u32[]{:S(2)}) copy-start(s32[16,3]{0,1:T(4,128)} %param.7) | copy-start | bytes 580
  41.7 11.8 %collective-permute-start.7 = (f16[256,1024]{1,0:T(8,128)(2,1)}, f16[256,1024]{1,0:T(8,128)(2,1)}, u32[]{:S(2)}, u32[]{:S(2)}) collective-permute-start(f16[256,1024]{1,0:T(8,128)(2,1)} %multiply_convert_fusion.7), channel_id=1, source_target_pairs={{0,2},{2,0},{4,6},{6,4},{8,10},{10,8},{12,14},{14,12},{16,18},{18,... | collective-permute-start | bytes 1572872 | tf_op jit(solution)/shard_map/ppermute | solution.py:30
  42.7 20.4 %collective-permute-start.8 = (f16[256,1024]{1,0:T(8,128)(2,1)}, f16[256,1024]{1,0:T(8,128)(2,1)}, u32[]{:S(2)}, u32[]{:S(2)}) collective-permute-start(f16[256,1024]{1,0:T(8,128)(2,1)} %get-tuple-element.119), channel_id=1, source_target_pairs={{0,1},{1,0},{2,3},{3,2},{4,5},{5,4},{6,7},{7,6},{8,9},{9,8},{10,11... | collective-permute-start | bytes 1572872 | tf_op jit(solution)/shard_map/ppermute | solution.py:21
  44.0 19.1 %collective-permute-start.9 = (f16[256,1024]{1,0:T(8,128)(2,1)}, f16[256,1024]{1,0:T(8,128)(2,1)}, u32[]{:S(2)}, u32[]{:S(2)}) collective-permute-start(f16[256,1024]{1,0:T(8,128)(2,1)} %multiply_convert_fusion.7), channel_id=1, source_target_pairs={{2,4},{4,2},{6,8},{8,6},{10,12},{12,10},{14,16},{16,14},{18,20},{2... | collective-permute-start | bytes 1572872 | tf_op jit(solution)/shard_map/ppermute | solution.py:30
  52.2 22.0 %collective-permute-start.11 = (f16[256,1024]{1,0:T(8,128)(2,1)}, f16[256,1024]{1,0:T(8,128)(2,1)S(1)}, u32[]{:S(2)}, u32[]{:S(2)}) collective-permute-start(f16[256,1024]{1,0:T(8,128)(2,1)} %get-tuple-element.133), channel_id=1, source_target_pairs={{0,1},{1,0},{2,3},{3,2},{4,5},{5,4},{6,7},{7,6},{8,9},{9,8},{10,11... | collective-permute-start | bytes 1572872 | tf_op jit(solution)/shard_map/ppermute | solution.py:21
  54.9 8.2 %slice-start = ((s8[5242880]{0:T(1024)(128)(4,1)}), s8[4194304]{0:T(1024)(128)(4,1)S(1)}, s32[]{:S(2)}) async-start(s8[5242880]{0:T(1024)(128)(4,1)} %bitcast.69), calls=%async_computation | async-start | bytes 8388608
  54.9 8.2 %collective-permute-start.10 = (f16[256,1024]{1,0:T(8,128)(2,1)S(1)}, f16[256,1024]{1,0:T(8,128)(2,1)S(1)}, u32[]{:S(2)}, u32[]{:S(2)}) collective-permute-start(f16[256,1024]{1,0:T(8,128)(2,1)S(1)} %multiply_convert_fusion.6), channel_id=1, source_target_pairs={{0,2},{2,0},{4,6},{6,4},{8,10},{10,8},{12,14},{14,12},{16,18},{18,... | collective-permute-start | bytes 1572872 | tf_op jit(solution)/shard_map/ppermute | solution.py:30
  56.4 6.8 %slice-start.1 = ((s8[5242880]{0:T(1024)(128)(4,1)}), s8[1048576]{0:T(1024)(128)(4,1)S(1)}, s32[]{:S(2)}) async-start(s8[5242880]{0:T(1024)(128)(4,1)} %bitcast.69), calls=%async_computation.1 | async-start | bytes 2097152
  56.4 9.3 %copy-start.6 = (f16[256,1024]{1,0:T(8,128)(2,1)S(1)}, f16[256,1024]{1,0:T(8,128)(2,1)}, u32[]{:S(2)}) copy-start(f16[256,1024]{1,0:T(8,128)(2,1)} %get-tuple-element.142) | copy-start | bytes 1572868
  59.2 20.7 %copy-start.5 = (f16[256,1024]{1,0:T(8,128)(2,1)S(1)}, f16[256,1024]{1,0:T(8,128)(2,1)}, u32[]{:S(2)}) copy-start(f16[256,1024]{1,0:T(8,128)(2,1)} %get-tuple-element.150) | copy-start | bytes 1572868
  59.4 20.2 %collective-permute-start.12 = (f16[256,1024]{1,0:T(8,128)(2,1)S(1)}, f16[256,1024]{1,0:T(8,128)(2,1)S(1)}, u32[]{:S(2)}, u32[]{:S(2)}) collective-permute-start(f16[256,1024]{1,0:T(8,128)(2,1)S(1)} %multiply_convert_fusion.6), channel_id=1, source_target_pairs={{2,4},{4,2},{6,8},{8,6},{10,12},{12,10},{14,16},{16,14},{18,20},{2... | collective-permute-start | bytes 1572872 | tf_op jit(solution)/shard_map/ppermute | solution.py:30
  64.4 15.3 %collective-permute-start.13 = (f16[256,1024]{1,0:T(8,128)(2,1)S(1)}, f16[256,1024]{1,0:T(8,128)(2,1)S(1)}, u32[]{:S(2)}, u32[]{:S(2)}) collective-permute-start(f16[256,1024]{1,0:T(8,128)(2,1)S(1)} %multiply_convert_fusion.5), channel_id=1, source_target_pairs={{0,2},{2,0},{4,6},{6,4},{8,10},{10,8},{12,14},{14,12},{16,18},{18,... | collective-permute-start | bytes 1572872 | tf_op jit(solution)/shard_map/ppermute | solution.py:30
  65.6 19.9 %collective-permute-start.14 = (f16[256,1024]{1,0:T(8,128)(2,1)S(1)}, f16[256,1024]{1,0:T(8,128)(2,1)S(1)}, u32[]{:S(2)}, u32[]{:S(2)}) collective-permute-start(f16[256,1024]{1,0:T(8,128)(2,1)S(1)} %copy-done.6), channel_id=1, source_target_pairs={{0,1},{1,0},{2,3},{3,2},{4,5},{5,4},{6,7},{7,6},{8,9},{9,8},{10,11... | collective-permute-start | bytes 1572872 | tf_op jit(solution)/shard_map/ppermute | solution.py:21
  66.9 21.3 %collective-permute-start.15 = (f16[256,1024]{1,0:T(8,128)(2,1)S(1)}, f16[256,1024]{1,0:T(8,128)(2,1)S(1)}, u32[]{:S(2)}, u32[]{:S(2)}) collective-permute-start(f16[256,1024]{1,0:T(8,128)(2,1)S(1)} %multiply_convert_fusion.5), channel_id=1, source_target_pairs={{2,4},{4,2},{6,8},{8,6},{10,12},{12,10},{14,16},{16,14},{18,20},{2... | collective-permute-start | bytes 1572872 | tf_op jit(solution)/shard_map/ppermute | solution.py:30
  79.9 8.3 %collective-permute-start.16 = (f16[256,1024]{1,0:T(8,128)(2,1)S(1)}, f16[256,1024]{1,0:T(8,128)(2,1)S(1)}, u32[]{:S(2)}, u32[]{:S(2)}) collective-permute-start(f16[256,1024]{1,0:T(8,128)(2,1)S(1)} %multiply_convert_fusion.4), channel_id=1, source_target_pairs={{0,2},{2,0},{4,6},{6,4},{8,10},{10,8},{12,14},{14,12},{16,18},{18,... | collective-permute-start | bytes 1572872 | tf_op jit(solution)/shard_map/ppermute | solution.py:30
  79.9 16.7 %collective-permute-start.17 = (f16[256,1024]{1,0:T(8,128)(2,1)S(1)}, f16[256,1024]{1,0:T(8,128)(2,1)S(1)}, u32[]{:S(2)}, u32[]{:S(2)}) collective-permute-start(f16[256,1024]{1,0:T(8,128)(2,1)S(1)} %copy-done.5), channel_id=1, source_target_pairs={{0,1},{1,0},{2,3},{3,2},{4,5},{5,4},{6,7},{7,6},{8,9},{9,8},{10,11... | collective-permute-start | bytes 1572872 | tf_op jit(solution)/shard_map/ppermute | solution.py:21
  80.2 24.7 %collective-permute-start.18 = (f16[256,1024]{1,0:T(8,128)(2,1)S(1)}, f16[256,1024]{1,0:T(8,128)(2,1)S(1)}, u32[]{:S(2)}, u32[]{:S(2)}) collective-permute-start(f16[256,1024]{1,0:T(8,128)(2,1)S(1)} %multiply_convert_fusion.4), channel_id=1, source_target_pairs={{2,4},{4,2},{6,8},{8,6},{10,12},{12,10},{14,16},{16,14},{18,20},{2... | collective-permute-start | bytes 1572872 | tf_op jit(solution)/shard_map/ppermute | solution.py:30
  88.3 16.6 %collective-permute-start.19 = (f16[256,1024]{1,0:T(8,128)(2,1)S(1)}, f16[256,1024]{1,0:T(8,128)(2,1)S(1)}, u32[]{:S(2)}, u32[]{:S(2)}) collective-permute-start(f16[256,1024]{1,0:T(8,128)(2,1)S(1)} %multiply_convert_fusion.3), channel_id=1, source_target_pairs={{0,2},{2,0},{4,6},{6,4},{8,10},{10,8},{12,14},{14,12},{16,18},{18,... | collective-permute-start | bytes 1572872 | tf_op jit(solution)/shard_map/ppermute | solution.py:30
  88.4 19.5 %collective-permute-start.20 = (f16[256,1024]{1,0:T(8,128)(2,1)S(1)}, f16[256,1024]{1,0:T(8,128)(2,1)S(1)}, u32[]{:S(2)}, u32[]{:S(2)}) collective-permute-start(f16[256,1024]{1,0:T(8,128)(2,1)S(1)} %get-tuple-element.158), channel_id=1, source_target_pairs={{0,1},{1,0},{2,3},{3,2},{4,5},{5,4},{6,7},{7,6},{8,9},{9,8},{10,11... | collective-permute-start | bytes 1572872 | tf_op jit(solution)/shard_map/ppermute | solution.py:21
  88.5 26.3 %collective-permute-start.21 = (f16[256,1024]{1,0:T(8,128)(2,1)S(1)}, f16[256,1024]{1,0:T(8,128)(2,1)S(1)}, u32[]{:S(2)}, u32[]{:S(2)}) collective-permute-start(f16[256,1024]{1,0:T(8,128)(2,1)S(1)} %multiply_convert_fusion.3), channel_id=1, source_target_pairs={{2,4},{4,2},{6,8},{8,6},{10,12},{12,10},{14,16},{16,14},{18,20},{2... | collective-permute-start | bytes 1572872 | tf_op jit(solution)/shard_map/ppermute | solution.py:30
  105.2 4.0 %copy-start.4 = (f32[512,1024]{1,0:T(8,128)S(1)}, f32[512,1024]{1,0:T(8,128)}, u32[]{:S(2)}) copy-start(f32[512,1024]{1,0:T(8,128)} %copy-done.2) | copy-start | bytes 6291460
  105.2 13.5 %collective-permute-start.23 = (f16[256,1024]{1,0:T(8,128)(2,1)S(1)}, f16[256,1024]{1,0:T(8,128)(2,1)S(1)}, u32[]{:S(2)}, u32[]{:S(2)}) collective-permute-start(f16[256,1024]{1,0:T(8,128)(2,1)S(1)} %multiply_convert_fusion.2), channel_id=1, source_target_pairs={{2,4},{4,2},{6,8},{8,6},{10,12},{12,10},{14,16},{16,14},{18,20},{2... | collective-permute-start | bytes 1572872 | tf_op jit(solution)/shard_map/ppermute | solution.py:30
  107.7 10.9 %collective-permute-start.22 = (f16[256,1024]{1,0:T(8,128)(2,1)S(1)}, f16[256,1024]{1,0:T(8,128)(2,1)S(1)}, u32[]{:S(2)}, u32[]{:S(2)}) collective-permute-start(f16[256,1024]{1,0:T(8,128)(2,1)S(1)} %multiply_convert_fusion.2), channel_id=1, source_target_pairs={{0,2},{2,0},{4,6},{6,4},{8,10},{10,8},{12,14},{14,12},{16,18},{18,... | collective-permute-start | bytes 1572872 | tf_op jit(solution)/shard_map/ppermute | solution.py:30
  115.2 3.5 %copy-start.1 = (f32[1,2048,1024]{2,1,0:T(8,128)}, f32[1,2048,1024]{2,1,0:T(8,128)S(1)}, u32[]{:S(2)}) copy-start(f32[1,2048,1024]{2,1,0:T(8,128)S(1)} %bitcast_dynamic-update-slice_fusion.1) | copy-start | bytes 25165828

commit v15 on v13

--- a/solution.py
+++ b/solution.py
@@ -12,7 +12,7 @@
 STEP = 256
 FIRST = 128
 AHEAD = 3
-MIXLAG = 99
+MIXLAG = 5
 
 
 def from_behind(value, axis, steps):
@@ -100,8 +100,10 @@
     far = {}
     mixed = 0
     out = jnp.zeros_like(weights)
-    split = cuts[min(2, chunks)]
-    terms = {0: for_others(0, cuts[1])}
+    split = cuts[min(3, chunks)]
+    begun = min(2, chunks)
+    made = for_others(0, cuts[begun])
+    terms = {chunk: [term[cuts[chunk]:cuts[chunk + 1]] for term in made] for chunk in range(begun)}
 
     terms[0], later = lax.optimization_barrier((terms[0], shard))
     arrived = {0: add_over_fsdp(terms[0])}
@@ -112,24 +114,14 @@
     far[-1] = swapped(sent, "blk", 1)
     near[-1] = swapped(sent, "blk", 0)
 
-    if chunks > 1:
-        parts, later = lax.optimization_barrier((parts, shard))
-        rest = [
-            (partial(owner(away, later), cuts[1], rows - cuts[1]) * (RATE * scale)).astype(WIRE)
-            for away in range(1, shards)
-        ]
-        for chunk in range(1, chunks):
-            terms[chunk] = [term[cuts[chunk] - cuts[1]:cuts[chunk + 1] - cuts[1]] for term in rest]
-        for chunk in range(1, min(AHEAD, chunks)):
-            if chunk == 2:
-                terms[chunk], near[-1] = lax.optimization_barrier((terms[chunk], near[-1]))
-            arrived[chunk] = add_over_fsdp(terms[chunk])
+    if begun > 1:
+        arrived[1] = add_over_fsdp(terms[1])
     base = [own_part(shard, 0, split)]
 
     arrived[0], base, terms = lax.optimization_barrier((arrived[0], base, terms))
     for chunk in range(chunks):
-        if chunk == 1:
-            arrived[1], base = lax.optimization_barrier((arrived[1], base))
+        if chunk in (1, 3):
+            arrived[chunk], base, terms = lax.optimization_barrier((arrived[chunk], base, terms))
         if chunk >= 1:
             arrived[chunk], far[chunk - 2] = lax.optimization_barrier((arrived[chunk], far[chunk - 2]))
         arrived[chunk], near[chunk - 1] = lax.optimization_barrier((arrived[chunk], near[chunk - 1]))
@@ -139,7 +131,17 @@
             arrived[chunk], parts = lax.optimization_barrier((arrived[chunk], parts))
         sent = (u_of(chunk) * scale).astype(WIRE)
         sent, base, out, later = lax.optimization_barrier((sent, base, out, shard))
-        if chunk == 0 and split < main:
+        if chunk == 0 and begun < chunks:
+            start = cuts[begun]
+            rest = [
+                (partial(owner(away, later), start, rows - start) * (RATE * scale)).astype(WIRE)
+                for away in range(1, shards)
+            ]
+            for after in range(begun, chunks):
+                terms[after] = [term[cuts[after] - start:cuts[after + 1] - start] for term in rest]
+            for after in range(begun, min(AHEAD, chunks)):
+                arrived[after] = add_over_fsdp(terms[after])
+        if chunk == 2 and split < main:
             base.append(own_part(later, split, rows))
         if chunk == middle:
             mix, parts, sent = lax.optimization_barrier((mix, parts, sent))
@@ -150,7 +152,7 @@
             ]
             parts = parts[:first]
         after = chunk + AHEAD
-        if after < chunks:
+        if chunk > 0 and after < chunks:
             terms[after], sent = lax.optimization_barrier((terms[after], sent))
             arrived[after] = add_over_fsdp(terms[after])
         if chunk == max(chunks - AHEAD, middle):
@@ -158,14 +160,18 @@
             back = add_over_fsdp(back)
         far[chunk] = swapped(sent, "blk", 1)
         near[chunk] = swapped(sent, "blk", 0)
+        if chunk == 0 and after < chunks:
+            terms[after], near[0] = lax.optimization_barrier((terms[after], near[0]))
+            arrived[after] = add_over_fsdp(terms[after])
         if chunk >= MIXLAG:
             out = mix_into(out, mixed)
             mixed += 1
 
-    for term in back:
-        parts = parts + term.astype(jnp.float32) / scale
-    out = lax.dynamic_update_slice_in_dim(out, parts, main, axis=0)
     for chunk in range(mixed, chunks):
+        if chunk == chunks - 1:
+            for term in back:
+                parts = parts + term.astype(jnp.float32) / scale
+            out = lax.dynamic_update_slice_in_dim(out, parts, main, axis=0)
         out = mix_into(out, chunk)
     return out[None]
 

time: 126 us -> 126 us (level)
  other arithmetic: 18.6 us -> 23.1 us
  starting transfers between devices: 30.7 us -> 33.2 us
  local copies, waits for them, and re-layouts: 10.1 us -> 7.77 us
  waiting for transfers between devices: 41.6 us -> 39.3 us
  matrix products: 23.1 us -> 21.3 us
    ppermute x9, waiting for transfers between devices: 28.5 us -> 8.85 us  [from_behind(): return lax.ppermute(value, axis, pairs)]
    ppermute x18, waiting for transfers between devices: 13.1 us -> 30.5 us  [swapped(): return lax.ppermute(value, axis, pairs)]
    ppermute x18, starting transfers between devices: 22.9 us -> 26.9 us  [swapped(): return lax.ppermute(value, axis, pairs)]
    convert_element_type x8, other arithmetic: 7.04 us -> 9.79 us  [on_device(): sent = (u_of(chunk) * scale).astype(WIRE)]
    unnamed x22 -> x18, local copies, waits for them, and re-layouts: 5.1 us -> 2.88 us
    dot_general x6, matrix products: 23.1 us -> 21.3 us  [partial(): lax.dot_general(block, cot_local, (((0,), (0,)), ((), ())), preferred_ele...]
    ppermute x9, starting transfers between devices: 7.88 us -> 6.22 us  [from_behind(): return lax.ppermute(value, axis, pairs)]
    slice x2 -> x3, local copies, waits for them, and re-layouts: 3.85 us -> 3.74 us  [the longest x2 2.5 us: on_device(): term[cuts[after] - start:cuts[after + 1] - start]]
  transfers between devices with their start and end apart: 27 -> 27, of which waited for: 11 -> 10; matrix products, arithmetic and copies ran while one was open for 31% -> 36% of each run, Pallas kernels for 0% -> 0%
where the time goes in v15:
time: 126 us; the launch traced here: 125 us
  waiting for transfers between devices  39.3 us (31%)
  starting transfers between devices  33.2 us (26%)
  other arithmetic  23.1 us (18%)
  matrix products  21.3 us (17%)
  local copies, waits for them, and re-layouts  7.77 us (6%)
    ppermute x18, waiting for transfers between devices, swapped(): return lax.ppermute(value, axis, pairs)  30.5 us
    ppermute x18, starting transfers between devices, swapped(): return lax.ppermute(value, axis, pairs)  26.9 us
    dot_general x6, matrix products, partial(): lax.dot_general(block, cot_local, (((0,), (0,)), ((), ())), preferred_ele...  21.3 us
    convert_element_type x8, other arithmetic, on_device(): sent = (u_of(chunk) * scale).astype(WIRE)  9.79 us
    dynamic_update_slice x8, other arithmetic, mix_into(): return lax.dynamic_update_slice_in_dim(out, value, cuts[chunk], axis=0)  9.71 us
    ppermute x9, waiting for transfers between devices, from_behind(): return lax.ppermute(value, axis, pairs)  8.85 us
    ppermute x9, starting transfers between devices, from_behind(): return lax.ppermute(value, axis, pairs)  6.22 us
    unnamed x18, local copies, waits for them, and re-layouts  2.88 us
  transfers between devices with their start and end apart: 27, of which 10 were waited for; matrix products, arithmetic and copies ran while one was open for 36% of the time, Pallas kernels for 0%

profile of v15, /device:TPU:1, one launch (start us, length us, event | category | flops | bytes accessed | tf_op | source)
XLA Modules:
  0.0 125.0 jit_solution(3151259111429273733)
XLA Ops:
  0.0 1.5 %copy-done = bf16[1,896,1024]{2,1,0:T(8,128)(2,1)S(1)} copy-done((bf16[1,896,1024]{2,1,0:T(8,128)(2,1)S(1)}, bf16[1,896,1024]{2,1,0:T(8,128)(2,1)}, u32[]{:S(2)}) %copy-start) | copy-done | bytes 1835032
  1.5 2.4 %multiply_convert_fusion.1 = f16[512,1024]{1,0:T(8,128)(2,1)S(1)} fusion(bf16[1,896,1024]{2,1,0:T(8,128)(2,1)S(1)} %copy-done, bf16[1,896,4096]{2,1,0:T(8,128)(2,1)} %param.5, s32[]{:T(128)S(6)} %select_n.46), kind=kOutput, calls=%fused_computation.7 | convolution fusion | flops 940572672 | bytes 3801092 | tf_op jit(solution)/shard_map/dot_general | solution.py:65
  4.0 1.2 fusion.41
  5.2 2.1 %collective-permute-start = (f16[256,1024]{1,0:T(8,128)(2,1)}, f16[256,1024]{1,0:T(8,128)(2,1)}, u32[]{:S(2)}, u32[]{:S(2)}) collective-permute-start(f16[256,1024]{1,0:T(8,128)(2,1)} %get-tuple-element.104), channel_id=1, source_target_pairs={{0,1},{1,0},{2,3},{3,2},{4,5},{5,4},{6,7},{7,6},{8,9},{9,8},{10,11... | collective-permute-start | bytes 1572872 | tf_op jit(solution)/shard_map/ppermute | solution.py:21
  7.3 1.4 %fusion.20 = f32[128,1024]{1,0:T(8,128)S(1)} fusion(bf16[1,896,1024]{2,1,0:T(8,128)(2,1)S(1)} %copy-done, bf16[1,896,4096]{2,1,0:T(8,128)(2,1)} %param.5, s32[]{:T(128)S(6)} %select_n.50), kind=kOutput, calls=%fused_computation.20 | convolution fusion | flops 235012096 | bytes 2588676 | tf_op jit(solution)/shard_map/dot_general | solution.py:65
  8.7 1.7 %fusion.23 = f32[128,1024]{1,0:T(8,128)S(1)} fusion(bf16[1,896,1024]{2,1,0:T(8,128)(2,1)S(1)} %copy-done, f32[1,2048,1024]{2,1,0:T(8,128)} %param.4, bf16[1,896,4096]{2,1,0:T(8,128)(2,1)} %param.5, s32[]{:T(128)S(6)} %select_n.48), kind=kOutput, calls=%fused_computation.21 | convolution fusion | flops 235143168 | bytes 3112964 | tf_op jit(solution)/shard_map/dot_general | solution.py:65
  10.3 1.0 multiply_convert_fusion.9
  11.3 1.0 collective-permute-start.1
  12.3 1.1 collective-permute-start.5
  13.4 0.2 collective-permute-start.4
  13.6 4.2 %bitcast_subtract_fusion.1 = f32[768,1024]{1,0:T(8,128)S(1)} fusion(f32[1,2048,1024]{2,1,0:T(8,128)} %param.4, bf16[1,896,1024]{2,1,0:T(8,128)(2,1)S(1)} %copy-done, bf16[1,896,4096]{2,1,0:T(8,128)(2,1)} %param.5, s32[]{:T(128)S(6)} %select_n.47), kind=kOutput, calls=%fused_computation.2 | convolution fusion | flops 1410859008 | bytes 9502724 | tf_op jit(solution)/shard_map/dot_general | solution.py:65
  17.8 1.4 %collective-permute-done = f16[256,1024]{1,0:T(8,128)(2,1)} collective-permute-done((f16[256,1024]{1,0:T(8,128)(2,1)}, f16[256,1024]{1,0:T(8,128)(2,1)}, u32[]{:S(2)}, u32[]{:S(2)}) %collective-permute-start) | collective-permute-done | bytes 524320 | tf_op jit(solution)/shard_map/ppermute | solution.py:21
  19.2 0.2 copy-done.1
  19.5 2.1 %multiply_convert_fusion.8 = f16[256,1024]{1,0:T(8,128)(2,1)} fusion(f16[256,1024]{1,0:T(8,128)(2,1)} %collective-permute-done, f32[768,1024]{1,0:T(8,128)S(1)} %bitcast_subtract_fusion.1), kind=kLoop, calls=%fused_computation.43 | loop fusion | flops 1310720 | bytes 2097152 | tf_op jit(solution)/shard_map/convert_element_type | solution.py:132
  21.6 3.8 %collective-permute-start.2 = (f16[256,1024]{1,0:T(8,128)(2,1)}, f16[256,1024]{1,0:T(8,128)(2,1)}, u32[]{:S(2)}, u32[]{:S(2)}) collective-permute-start(f16[256,1024]{1,0:T(8,128)(2,1)} %multiply_convert_fusion.8), channel_id=1, source_target_pairs={{0,2},{2,0},{4,6},{6,4},{8,10},{10,8},{12,14},{14,12},{16,18},{18,... | collective-permute-start | bytes 1572872 | tf_op jit(solution)/shard_map/ppermute | solution.py:30
  25.4 5.5 %multiply_convert_fusion = f16[1536,1024]{1,0:T(8,128)(2,1)S(1)} fusion(bf16[1,896,4096]{2,1,0:T(8,128)(2,1)} %param.5, s32[]{:T(128)S(6)} %select_n.52, bf16[1,896,1024]{2,1,0:T(8,128)(2,1)S(1)} %copy-done), kind=kOutput, calls=%fused_computation | convolution fusion | flops 2821718016 | bytes 7733252 | tf_op jit(solution)/shard_map/dot_general | solution.py:65
  30.9 0.7 slice.171
  31.6 1.8 %fusion.40 = (f16[256,1024]{1,0:T(8,128)(2,1)}, f16[256,1024]{1,0:T(8,128)(2,1)}, f16[256,1024]{1,0:T(8,128)(2,1)}, f16[256,1024]{1,0:T(8,128)(2,1)}, f16[256,1024]{1,0:T(8,128)(2,1)}) fusion(f16[1536,1024]{1,0:T(8,128)(2,1)S(1)} %multiply_convert_fusion), kind=kLoop, calls=%fused_computation.69 | loop fusion | bytes 5242880 | tf_op jit(solution)/shard_map/slice | solution.py:141
  33.4 1.2 collective-permute-start.6
  34.6 0.2 collective-permute-start.3
  34.8 2.3 %multiply_convert_fusion.7 = f16[256,1024]{1,0:T(8,128)(2,1)} fusion(f16[256,1024]{1,0:T(8,128)(2,1)S(1)} %collective-permute-done.4, f32[768,1024]{1,0:T(8,128)} %copy-done.1), kind=kLoop, calls=%fused_computation.41 | loop fusion | flops 1310720 | bytes 2097152 | tf_op jit(solution)/shard_map/convert_element_type | solution.py:132
  37.1 3.8 %collective-permute-start.8 = (f16[256,1024]{1,0:T(8,128)(2,1)}, f16[256,1024]{1,0:T(8,128)(2,1)}, u32[]{:S(2)}, u32[]{:S(2)}) collective-permute-start(f16[256,1024]{1,0:T(8,128)(2,1)} %multiply_convert_fusion.7), channel_id=1, source_target_pairs={{0,2},{2,0},{4,6},{6,4},{8,10},{10,8},{12,14},{14,12},{16,18},{18,... | collective-permute-start | bytes 1572872 | tf_op jit(solution)/shard_map/ppermute | solution.py:30
  40.9 0.1 fusion.39
  41.0 0.2 multiply_reduce_fusion
  41.2 0.1 broadcast_in_dim.26
  41.3 2.6 %collective-permute-done.6 = f16[256,1024]{1,0:T(8,128)(2,1)} collective-permute-done((f16[256,1024]{1,0:T(8,128)(2,1)}, f16[256,1024]{1,0:T(8,128)(2,1)}, u32[]{:S(2)}, u32[]{:S(2)}) %collective-permute-start.6) | collective-permute-done | bytes 524320 | tf_op jit(solution)/shard_map/ppermute | solution.py:21
  43.9 1.2 collective-permute-start.11
  45.2 1.5 %multiply_add_fusion = f32[256,1024]{1,0:T(8,128)S(1)} fusion(f16[256,1024]{1,0:T(8,128)(2,1)} %collective-permute-done.5, f32[256,1024]{1,0:T(8,128)S(1)} %get-tuple-element.144, f16[256,1024]{1,0:T(8,128)(2,1)} %collective-permute-done.1, f32[1024]{0:T(1024)S(1)} %bitcast.73, f32[1024]{0:T(1024)S(1)} %bitcast.82, f32[1024]{0:T(1024)S(1)} %bitcast.64), kind=kLoop, calls=%fused_computation.38 | loop fusion | flops 1835008 | bytes 3158016 | tf_op jit(solution)/shard_map/add | solution.py:90
  46.6 0.8 fusion.28
  47.4 2.4 %multiply_convert_fusion.6 = f16[256,1024]{1,0:T(8,128)(2,1)} fusion(f16[256,1024]{1,0:T(8,128)(2,1)} %collective-permute-done.6, f32[768,1024]{1,0:T(8,128)} %copy-done.1), kind=kLoop, calls=%fused_computation.39 | loop fusion | flops 1310720 | bytes 2097152 | tf_op jit(solution)/shard_map/convert_element_type | solution.py:132
  49.8 8.1 %collective-permute-start.10 = (f16[256,1024]{1,0:T(8,128)(2,1)}, f16[256,1024]{1,0:T(8,128)(2,1)S(1)}, u32[]{:S(2)}, u32[]{:S(2)}) collective-permute-start(f16[256,1024]{1,0:T(8,128)(2,1)} %multiply_convert_fusion.6), channel_id=1, source_target_pairs={{0,2},{2,0},{4,6},{6,4},{8,10},{10,8},{12,14},{14,12},{16,18},{18,... | collective-permute-start | bytes 1572872 | tf_op jit(solution)/shard_map/ppermute | solution.py:30
  57.9 6.2 %bitcast_subtract_fusion = f32[1280,1024]{1,0:T(8,128)S(1)} fusion(f32[1,2048,1024]{2,1,0:T(8,128)} %param.4, bf16[1,896,4096]{2,1,0:T(8,128)(2,1)} %param.5, s32[]{:T(128)S(6)} %select_n.53, bf16[1,896,1024]{2,1,0:T(8,128)(2,1)S(1)} %copy-done), kind=kOutput, calls=%fused_computation.1 | convolution fusion | flops 2351431680 | bytes 14614532 | tf_op jit(solution)/shard_map/dot_general | solution.py:65
  64.2 1.3 %multiply_convert_fusion.5 = f16[256,1024]{1,0:T(8,128)(2,1)S(1)} fusion(f16[256,1024]{1,0:T(8,128)(2,1)} %collective-permute-done.3, f32[1280,1024]{1,0:T(8,128)S(1)} %bitcast_subtract_fusion), kind=kLoop, calls=%fused_computation.36 | loop fusion | flops 1310720 | bytes 2097152 | tf_op jit(solution)/shard_map/convert_element_type | solution.py:132
  65.5 0.5 collective-permute-start.13
  66.0 0.2 collective-permute-start.14
  66.3 1.6 %collective-permute-start.15 = (f16[256,1024]{1,0:T(8,128)(2,1)S(1)}, f16[256,1024]{1,0:T(8,128)(2,1)S(1)}, u32[]{:S(2)}, u32[]{:S(2)}) collective-permute-start(f16[256,1024]{1,0:T(8,128)(2,1)S(1)} %multiply_convert_fusion.5), channel_id=1, source_target_pairs={{2,4},{4,2},{6,8},{8,6},{10,12},{12,10},{14,16},{16,14},{18,20},{2... | collective-permute-start | bytes 1572872 | tf_op jit(solution)/shard_map/ppermute | solution.py:30
  67.9 10.4 %collective-permute-done.12 = f16[256,1024]{1,0:T(8,128)(2,1)} collective-permute-done((f16[256,1024]{1,0:T(8,128)(2,1)}, f16[256,1024]{1,0:T(8,128)(2,1)}, u32[]{:S(2)}, u32[]{:S(2)}) %collective-permute-start.12) | collective-permute-done | bytes 524320 | tf_op jit(solution)/shard_map/ppermute | solution.py:30
  78.3 1.2 multiply_convert_fusion.4
  79.8 0.3 collective-permute-done.14
  80.0 3.9 %collective-permute-done.15 = f16[256,1024]{1,0:T(8,128)(2,1)S(1)} collective-permute-done((f16[256,1024]{1,0:T(8,128)(2,1)S(1)}, f16[256,1024]{1,0:T(8,128)(2,1)S(1)}, u32[]{:S(2)}, u32[]{:S(2)}) %collective-permute-start.15) | collective-permute-done | bytes 524320 | tf_op jit(solution)/shard_map/ppermute | solution.py:30
  83.9 0.2 multiply_convert_fusion.3
  84.2 0.3 collective-permute-start.20
  84.5 0.9 collective-permute-start.21
  85.4 1.1 broadcast_in_dim.25
  86.5 1.8 %add_dynamic-update-slice_fusion.1 = f32[2048,1024]{1,0:T(8,128)S(1)} fusion(f32[2048,1024]{1,0:T(8,128)S(1)} %broadcast_in_dim.25, f16[256,1024]{1,0:T(8,128)(2,1)} %collective-permute-done.7, f32[768,1024]{1,0:T(8,128)S(1)} %copy-done.2, f16[256,1024]{1,0:T(8,128)(2,1)} %collective-permute-done.2, f16[256,1024]{1,0:T(8,128)(2,1)} %collective-permute-done, ...), kind=kLoop, calls=%fused_computation.31 | loop fusion | flops 2621440 | bytes 3682304 | tf_op jit(solution)/shard_map/dynamic_update_slice | solution.py:97
  88.2 4.5 %collective-permute-done.17 = f16[256,1024]{1,0:T(8,128)(2,1)S(1)} collective-permute-done((f16[256,1024]{1,0:T(8,128)(2,1)S(1)}, f16[256,1024]{1,0:T(8,128)(2,1)S(1)}, u32[]{:S(2)}, u32[]{:S(2)}) %collective-permute-start.17) | collective-permute-done | bytes 524320 | tf_op jit(solution)/shard_map/ppermute | solution.py:21
  92.8 7.7 %collective-permute-done.18 = f16[256,1024]{1,0:T(8,128)(2,1)S(1)} collective-permute-done((f16[256,1024]{1,0:T(8,128)(2,1)S(1)}, f16[256,1024]{1,0:T(8,128)(2,1)S(1)}, u32[]{:S(2)}, u32[]{:S(2)}) %collective-permute-start.18) | collective-permute-done | bytes 524320 | tf_op jit(solution)/shard_map/ppermute | solution.py:30
  100.5 0.2 multiply_convert_fusion.2
  100.8 0.6 collective-permute-start.24
  101.4 0.4 collective-permute-start.23
  101.7 4.6 %collective-permute-done.21 = f16[256,1024]{1,0:T(8,128)(2,1)S(1)} collective-permute-done((f16[256,1024]{1,0:T(8,128)(2,1)S(1)}, f16[256,1024]{1,0:T(8,128)(2,1)S(1)}, u32[]{:S(2)}, u32[]{:S(2)}) %collective-permute-start.21) | collective-permute-done | bytes 524320 | tf_op jit(solution)/shard_map/ppermute | solution.py:30
  106.4 1.6 %add_dynamic-update-slice_fusion = f32[2048,1024]{1,0:T(8,128)S(1)} fusion(f32[2048,1024]{1,0:T(8,128)S(1)} %add_dynamic-update-slice_fusion.1, f16[256,1024]{1,0:T(8,128)(2,1)} %collective-permute-done.9, f32[768,1024]{1,0:T(8,128)S(1)} %copy-done.2, f16[256,1024]{1,0:T(8,128)(2,1)} %collective-permute-done.8, ...), kind=kLoop, calls=%fused_computation.28 | loop fusion | flops 2621440 | bytes 3682304 | tf_op jit(solution)/shard_map/dynamic_update_slice | solution.py:97
  108.0 0.1 multiply_convert_fusion.10
  108.2 5.4 %collective-permute-start.26 = (f16[128,1024]{1,0:T(8,128)(2,1)S(1)}, f16[128,1024]{1,0:T(8,128)(2,1)S(1)}, u32[]{:S(2)}, u32[]{:S(2)}) collective-permute-start(f16[128,1024]{1,0:T(8,128)(2,1)S(1)} %multiply_convert_fusion.10), channel_id=1, source_target_pairs={{2,4},{4,2},{6,8},{8,6},{10,12},{12,10},{14,16},{16,14},{18,20},{2... | collective-permute-start | bytes 786440 | tf_op jit(solution)/shard_map/ppermute | solution.py:30
  113.6 1.6 %bitcast_dynamic-update-slice_fusion.4 = f32[1,2048,1024]{2,1,0:T(8,128)S(1)} fusion(f32[1,2048,1024]{2,1,0:T(8,128)S(1)} %bitcast.63, f16[256,1024]{1,0:T(8,128)(2,1)} %collective-permute-done.12, f32[768,1024]{1,0:T(8,128)S(1)} %copy-done.2, f16[256,1024]{1,0:T(8,128)(2,1)S(1)} %collective-permute-done.10, f16[256,1024]{1,0:T(8,128)(2,1)} %collective-permute-done.6, ...), kind=kLoop, calls=%fused_computation.27 | loop fusion | flops 2621440 | bytes 3682304 | tf_op jit(solution)/shard_map/dynamic_update_slice | solution.py:97
  115.2 1.5 %bitcast_dynamic-update-slice_fusion.3 = f32[1,2048,1024]{2,1,0:T(8,128)S(1)} fusion(f32[1,2048,1024]{2,1,0:T(8,128)S(1)} %bitcast_dynamic-update-slice_fusion.4, f16[256,1024]{1,0:T(8,128)(2,1)S(1)} %collective-permute-done.15, f32[1280,1024]{1,0:T(8,128)S(1)} %bitcast_subtract_fusion, f16[256,1024]{1,0:T(8,128)(2,1)S(1)} %collective-permute-done.13, ...), kind=kLoop, calls=%fused_computation.26 | loop fusion | flops 2621440 | bytes 3682304 | tf_op jit(solution)/shard_map/dynamic_update_slice | solution.py:97
  116.6 1.5 %bitcast_dynamic-update-slice_fusion.2 = f32[1,2048,1024]{2,1,0:T(8,128)S(1)} fusion(f32[1,2048,1024]{2,1,0:T(8,128)S(1)} %bitcast_dynamic-update-slice_fusion.3, f16[256,1024]{1,0:T(8,128)(2,1)S(1)} %collective-permute-done.18, f32[1280,1024]{1,0:T(8,128)S(1)} %bitcast_subtract_fusion, f16[256,1024]{1,0:T(8,128)(2,1)S(1)} %collective-permute-done.16, ...), kind=kLoop, calls=%fused_computation.25 | loop fusion | flops 2621440 | bytes 3682304 | tf_op jit(solution)/shard_map/dynamic_update_slice | solution.py:97
  118.1 0.4 bitcast_dynamic-update-slice_fusion.1
  118.5 1.6 %collective-permute-done.23 = f16[256,1024]{1,0:T(8,128)(2,1)S(1)} collective-permute-done((f16[256,1024]{1,0:T(8,128)(2,1)S(1)}, f16[256,1024]{1,0:T(8,128)(2,1)S(1)}, u32[]{:S(2)}, u32[]{:S(2)}) %collective-permute-start.23) | collective-permute-done | bytes 524320 | tf_op jit(solution)/shard_map/ppermute | solution.py:30
  120.1 0.4 bitcast_dynamic-update-slice_fusion
  120.5 0.1 bitcast_dynamic-update-slice_fusion.6
  120.7 2.3 %collective-permute-done.26 = f16[128,1024]{1,0:T(8,128)(2,1)S(1)} collective-permute-done((f16[128,1024]{1,0:T(8,128)(2,1)S(1)}, f16[128,1024]{1,0:T(8,128)(2,1)S(1)}, u32[]{:S(2)}, u32[]{:S(2)}) %collective-permute-start.26) | collective-permute-done | bytes 262176 | tf_op jit(solution)/shard_map/ppermute | solution.py:30
  122.9 1.1 copy-done.3
  124.0 1.0 bitcast_dynamic-update-slice_fusion.5
  (43 shorter events, 0.6 us)
Async XLA Ops:
  0.0 1.5 %copy-start = (bf16[1,896,1024]{2,1,0:T(8,128)(2,1)S(1)}, bf16[1,896,1024]{2,1,0:T(8,128)(2,1)}, u32[]{:S(2)}) copy-start(bf16[1,896,1024]{2,1,0:T(8,128)(2,1)} %param.6) | copy-start | bytes 5505028
  5.2 14.0 %collective-permute-start = (f16[256,1024]{1,0:T(8,128)(2,1)}, f16[256,1024]{1,0:T(8,128)(2,1)}, u32[]{:S(2)}, u32[]{:S(2)}) collective-permute-start(f16[256,1024]{1,0:T(8,128)(2,1)} %get-tuple-element.104), channel_id=1, source_target_pairs={{0,1},{1,0},{2,3},{3,2},{4,5},{5,4},{6,7},{7,6},{8,9},{9,8},{10,11... | collective-permute-start | bytes 1572872 | tf_op jit(solution)/shard_map/ppermute | solution.py:21
  11.3 7.9 %collective-permute-start.1 = (f16[256,1024]{1,0:T(8,128)(2,1)}, f16[256,1024]{1,0:T(8,128)(2,1)}, u32[]{:S(2)}, u32[]{:S(2)}) collective-permute-start(f16[256,1024]{1,0:T(8,128)(2,1)} %get-tuple-element.108), channel_id=1, source_target_pairs={{0,2},{2,0},{4,6},{6,4},{8,10},{10,8},{12,14},{14,12},{16,18},{18,... | collective-permute-start | bytes 1572872 | tf_op jit(solution)/shard_map/ppermute | solution.py:30
  12.3 22.5 %collective-permute-start.5 = (f16[256,1024]{1,0:T(8,128)(2,1)}, f16[256,1024]{1,0:T(8,128)(2,1)}, u32[]{:S(2)}, u32[]{:S(2)}) collective-permute-start(f16[256,1024]{1,0:T(8,128)(2,1)} %get-tuple-element.108), channel_id=1, source_target_pairs={{2,4},{4,2},{6,8},{8,6},{10,12},{12,10},{14,16},{16,14},{18,20},{2... | collective-permute-start | bytes 1572872 | tf_op jit(solution)/shard_map/ppermute | solution.py:30
  13.4 21.4 %collective-permute-start.4 = (f16[256,1024]{1,0:T(8,128)(2,1)}, f16[256,1024]{1,0:T(8,128)(2,1)S(1)}, u32[]{:S(2)}, u32[]{:S(2)}) collective-permute-start(f16[256,1024]{1,0:T(8,128)(2,1)} %get-tuple-element.212), channel_id=1, source_target_pairs={{0,1},{1,0},{2,3},{3,2},{4,5},{5,4},{6,7},{7,6},{8,9},{9,8},{10,11... | collective-permute-start | bytes 1572872 | tf_op jit(solution)/shard_map/ppermute | solution.py:21
  17.8 1.7 %copy-start.1 = (f32[768,1024]{1,0:T(8,128)}, f32[768,1024]{1,0:T(8,128)S(1)}, u32[]{:S(2)}) copy-start(f32[768,1024]{1,0:T(8,128)S(1)} %bitcast_subtract_fusion.1) | copy-start | bytes 9437188
  21.6 13.1 %collective-permute-start.2 = (f16[256,1024]{1,0:T(8,128)(2,1)}, f16[256,1024]{1,0:T(8,128)(2,1)}, u32[]{:S(2)}, u32[]{:S(2)}) collective-permute-start(f16[256,1024]{1,0:T(8,128)(2,1)} %multiply_convert_fusion.8), channel_id=1, source_target_pairs={{0,2},{2,0},{4,6},{6,4},{8,10},{10,8},{12,14},{14,12},{16,18},{18,... | collective-permute-start | bytes 1572872 | tf_op jit(solution)/shard_map/ppermute | solution.py:30
  25.4 18.5 %collective-permute-start.7 = (f16[256,1024]{1,0:T(8,128)(2,1)}, f16[256,1024]{1,0:T(8,128)(2,1)}, u32[]{:S(2)}, u32[]{:S(2)}) collective-permute-start(f16[256,1024]{1,0:T(8,128)(2,1)} %multiply_convert_fusion.8), channel_id=1, source_target_pairs={{2,4},{4,2},{6,8},{8,6},{10,12},{12,10},{14,16},{16,14},{18,20},{2... | collective-permute-start | bytes 1572872 | tf_op jit(solution)/shard_map/ppermute | solution.py:30
  30.9 10.0 %copy-start.8 = (s32[16,3]{0,1:T(4,128)S(1)}, s32[16,3]{0,1:T(4,128)}, u32[]{:S(2)}) copy-start(s32[16,3]{0,1:T(4,128)} %param.7) | copy-start | bytes 580
  33.4 10.5 %collective-permute-start.6 = (f16[256,1024]{1,0:T(8,128)(2,1)}, f16[256,1024]{1,0:T(8,128)(2,1)}, u32[]{:S(2)}, u32[]{:S(2)}) collective-permute-start(f16[256,1024]{1,0:T(8,128)(2,1)} %get-tuple-element.206), channel_id=1, source_target_pairs={{0,1},{1,0},{2,3},{3,2},{4,5},{5,4},{6,7},{7,6},{8,9},{9,8},{10,11... | collective-permute-start | bytes 1572872 | tf_op jit(solution)/shard_map/ppermute | solution.py:21
  34.6 29.6 %collective-permute-start.3 = (f16[256,1024]{1,0:T(8,128)(2,1)}, f16[256,1024]{1,0:T(8,128)(2,1)}, u32[]{:S(2)}, u32[]{:S(2)}) collective-permute-start(f16[256,1024]{1,0:T(8,128)(2,1)} %get-tuple-element.112), channel_id=1, source_target_pairs={{0,1},{1,0},{2,3},{3,2},{4,5},{5,4},{6,7},{7,6},{8,9},{9,8},{10,11... | collective-permute-start | bytes 1572872 | tf_op jit(solution)/shard_map/ppermute | solution.py:21
  37.1 10.3 %collective-permute-start.8 = (f16[256,1024]{1,0:T(8,128)(2,1)}, f16[256,1024]{1,0:T(8,128)(2,1)}, u32[]{:S(2)}, u32[]{:S(2)}) collective-permute-start(f16[256,1024]{1,0:T(8,128)(2,1)} %multiply_convert_fusion.7), channel_id=1, source_target_pairs={{0,2},{2,0},{4,6},{6,4},{8,10},{10,8},{12,14},{14,12},{16,18},{18,... | collective-permute-start | bytes 1572872 | tf_op jit(solution)/shard_map/ppermute | solution.py:30
  40.9 23.3 %collective-permute-start.9 = (f16[256,1024]{1,0:T(8,128)(2,1)}, f16[256,1024]{1,0:T(8,128)(2,1)}, u32[]{:S(2)}, u32[]{:S(2)}) collective-permute-start(f16[256,1024]{1,0:T(8,128)(2,1)} %multiply_convert_fusion.7), channel_id=1, source_target_pairs={{2,4},{4,2},{6,8},{8,6},{10,12},{12,10},{14,16},{16,14},{18,20},{2... | collective-permute-start | bytes 1572872 | tf_op jit(solution)/shard_map/ppermute | solution.py:30
  43.9 24.0 %collective-permute-start.11 = (f16[256,1024]{1,0:T(8,128)(2,1)}, f16[256,1024]{1,0:T(8,128)(2,1)}, u32[]{:S(2)}, u32[]{:S(2)}) collective-permute-start(f16[256,1024]{1,0:T(8,128)(2,1)} %get-tuple-element.131), channel_id=1, source_target_pairs={{0,1},{1,0},{2,3},{3,2},{4,5},{5,4},{6,7},{7,6},{8,9},{9,8},{10,11... | collective-permute-start | bytes 1572872 | tf_op jit(solution)/shard_map/ppermute | solution.py:21
  49.8 14.4 %collective-permute-start.10 = (f16[256,1024]{1,0:T(8,128)(2,1)}, f16[256,1024]{1,0:T(8,128)(2,1)S(1)}, u32[]{:S(2)}, u32[]{:S(2)}) collective-permute-start(f16[256,1024]{1,0:T(8,128)(2,1)} %multiply_convert_fusion.6), channel_id=1, source_target_pairs={{0,2},{2,0},{4,6},{6,4},{8,10},{10,8},{12,14},{14,12},{16,18},{18,... | collective-permute-start | bytes 1572872 | tf_op jit(solution)/shard_map/ppermute | solution.py:30
  57.9 20.3 %collective-permute-start.12 = (f16[256,1024]{1,0:T(8,128)(2,1)}, f16[256,1024]{1,0:T(8,128)(2,1)}, u32[]{:S(2)}, u32[]{:S(2)}) collective-permute-start(f16[256,1024]{1,0:T(8,128)(2,1)} %multiply_convert_fusion.6), channel_id=1, source_target_pairs={{2,4},{4,2},{6,8},{8,6},{10,12},{12,10},{14,16},{16,14},{18,20},{2... | collective-permute-start | bytes 1572872 | tf_op jit(solution)/shard_map/ppermute | solution.py:30
  57.9 8.1 %copy-start.5 = (f16[256,1024]{1,0:T(8,128)(2,1)S(1)}, f16[256,1024]{1,0:T(8,128)(2,1)}, u32[]{:S(2)}) copy-start(f16[256,1024]{1,0:T(8,128)(2,1)} %get-tuple-element.134) | copy-start | bytes 1572868
  57.9 21.7 %copy-start.4 = (f16[256,1024]{1,0:T(8,128)(2,1)S(1)}, f16[256,1024]{1,0:T(8,128)(2,1)}, u32[]{:S(2)}) copy-start(f16[256,1024]{1,0:T(8,128)(2,1)} %get-tuple-element.166) | copy-start | bytes 1572868
  64.2 20.0 %copy-start.7 = (f16[128,1024]{1,0:T(8,128)(2,1)S(1)}, f16[128,1024]{1,0:T(8,128)(2,1)}, u32[]{:S(2)}) copy-start(f16[128,1024]{1,0:T(8,128)(2,1)} %slice.171) | copy-start | bytes 786436
  65.5 12.8 %collective-permute-start.13 = (f16[256,1024]{1,0:T(8,128)(2,1)S(1)}, f16[256,1024]{1,0:T(8,128)(2,1)S(1)}, u32[]{:S(2)}, u32[]{:S(2)}) collective-permute-start(f16[256,1024]{1,0:T(8,128)(2,1)S(1)} %multiply_convert_fusion.5), channel_id=1, source_target_pairs={{0,2},{2,0},{4,6},{6,4},{8,10},{10,8},{12,14},{14,12},{16,18},{18,... | collective-permute-start | bytes 1572872 | tf_op jit(solution)/shard_map/ppermute | solution.py:30
  66.0 14.0 %collective-permute-start.14 = (f16[256,1024]{1,0:T(8,128)(2,1)S(1)}, f16[256,1024]{1,0:T(8,128)(2,1)S(1)}, u32[]{:S(2)}, u32[]{:S(2)}) collective-permute-start(f16[256,1024]{1,0:T(8,128)(2,1)S(1)} %copy-done.5), channel_id=1, source_target_pairs={{0,1},{1,0},{2,3},{3,2},{4,5},{5,4},{6,7},{7,6},{8,9},{9,8},{10,11... | collective-permute-start | bytes 1572872 | tf_op jit(solution)/shard_map/ppermute | solution.py:21
  66.3 17.6 %collective-permute-start.15 = (f16[256,1024]{1,0:T(8,128)(2,1)S(1)}, f16[256,1024]{1,0:T(8,128)(2,1)S(1)}, u32[]{:S(2)}, u32[]{:S(2)}) collective-permute-start(f16[256,1024]{1,0:T(8,128)(2,1)S(1)} %multiply_convert_fusion.5), channel_id=1, source_target_pairs={{2,4},{4,2},{6,8},{8,6},{10,12},{12,10},{14,16},{16,14},{18,20},{2... | collective-permute-start | bytes 1572872 | tf_op jit(solution)/shard_map/ppermute | solution.py:30
  79.5 6.9 %copy-start.2 = (f32[768,1024]{1,0:T(8,128)S(1)}, f32[768,1024]{1,0:T(8,128)}, u32[]{:S(2)}) copy-start(f32[768,1024]{1,0:T(8,128)} %copy-done.1) | copy-start | bytes 9437188
  79.5 4.4 %collective-permute-start.16 = (f16[256,1024]{1,0:T(8,128)(2,1)S(1)}, f16[256,1024]{1,0:T(8,128)(2,1)S(1)}, u32[]{:S(2)}, u32[]{:S(2)}) collective-permute-start(f16[256,1024]{1,0:T(8,128)(2,1)S(1)} %multiply_convert_fusion.4), channel_id=1, source_target_pairs={{0,2},{2,0},{4,6},{6,4},{8,10},{10,8},{12,14},{14,12},{16,18},{18,... | collective-permute-start | bytes 1572872 | tf_op jit(solution)/shard_map/ppermute | solution.py:30
  79.6 13.1 %collective-permute-start.17 = (f16[256,1024]{1,0:T(8,128)(2,1)S(1)}, f16[256,1024]{1,0:T(8,128)(2,1)S(1)}, u32[]{:S(2)}, u32[]{:S(2)}) collective-permute-start(f16[256,1024]{1,0:T(8,128)(2,1)S(1)} %copy-done.4), channel_id=1, source_target_pairs={{0,1},{1,0},{2,3},{3,2},{4,5},{5,4},{6,7},{7,6},{8,9},{9,8},{10,11... | collective-permute-start | bytes 1572872 | tf_op jit(solution)/shard_map/ppermute | solution.py:21
  79.7 20.7 %collective-permute-start.18 = (f16[256,1024]{1,0:T(8,128)(2,1)S(1)}, f16[256,1024]{1,0:T(8,128)(2,1)S(1)}, u32[]{:S(2)}, u32[]{:S(2)}) collective-permute-start(f16[256,1024]{1,0:T(8,128)(2,1)S(1)} %multiply_convert_fusion.4), channel_id=1, source_target_pairs={{2,4},{4,2},{6,8},{8,6},{10,12},{12,10},{14,16},{16,14},{18,20},{2... | collective-permute-start | bytes 1572872 | tf_op jit(solution)/shard_map/ppermute | solution.py:30
  84.1 16.6 %copy-start.6 = (f16[128,1024]{1,0:T(8,128)(2,1)S(1)}, f16[128,1024]{1,0:T(8,128)(2,1)}, u32[]{:S(2)}) copy-start(f16[128,1024]{1,0:T(8,128)(2,1)} %get-tuple-element.201) | copy-start | bytes 786436
  84.1 16.3 %collective-permute-start.19 = (f16[256,1024]{1,0:T(8,128)(2,1)S(1)}, f16[256,1024]{1,0:T(8,128)(2,1)S(1)}, u32[]{:S(2)}, u32[]{:S(2)}) collective-permute-start(f16[256,1024]{1,0:T(8,128)(2,1)S(1)} %multiply_convert_fusion.3), channel_id=1, source_target_pairs={{0,2},{2,0},{4,6},{6,4},{8,10},{10,8},{12,14},{14,12},{16,18},{18,... | collective-permute-start | bytes 1572872 | tf_op jit(solution)/shard_map/ppermute | solution.py:30
  84.2 17.5 %collective-permute-start.20 = (f16[128,1024]{1,0:T(8,128)(2,1)S(1)}, f16[128,1024]{1,0:T(8,128)(2,1)S(1)}, u32[]{:S(2)}, u32[]{:S(2)}) collective-permute-start(f16[128,1024]{1,0:T(8,128)(2,1)S(1)} %copy-done.7), channel_id=1, source_target_pairs={{0,1},{1,0},{2,3},{3,2},{4,5},{5,4},{6,7},{7,6},{8,9},{9,8},{10,11... | collective-permute-start | bytes 786440 | tf_op jit(solution)/shard_map/ppermute | solution.py:21
  84.5 21.9 %collective-permute-start.21 = (f16[256,1024]{1,0:T(8,128)(2,1)S(1)}, f16[256,1024]{1,0:T(8,128)(2,1)S(1)}, u32[]{:S(2)}, u32[]{:S(2)}) collective-permute-start(f16[256,1024]{1,0:T(8,128)(2,1)S(1)} %multiply_convert_fusion.3), channel_id=1, source_target_pairs={{2,4},{4,2},{6,8},{8,6},{10,12},{12,10},{14,16},{16,14},{18,20},{2... | collective-permute-start | bytes 1572872 | tf_op jit(solution)/shard_map/ppermute | solution.py:30
  100.7 7.3 %collective-permute-start.22 = (f16[256,1024]{1,0:T(8,128)(2,1)S(1)}, f16[256,1024]{1,0:T(8,128)(2,1)S(1)}, u32[]{:S(2)}, u32[]{:S(2)}) collective-permute-start(f16[256,1024]{1,0:T(8,128)(2,1)S(1)} %multiply_convert_fusion.2), channel_id=1, source_target_pairs={{0,2},{2,0},{4,6},{6,4},{8,10},{10,8},{12,14},{14,12},{16,18},{18,... | collective-permute-start | bytes 1572872 | tf_op jit(solution)/shard_map/ppermute | solution.py:30
  100.8 19.8 %collective-permute-start.24 = (f16[128,1024]{1,0:T(8,128)(2,1)S(1)}, f16[128,1024]{1,0:T(8,128)(2,1)S(1)}, u32[]{:S(2)}, u32[]{:S(2)}) collective-permute-start(f16[128,1024]{1,0:T(8,128)(2,1)S(1)} %copy-done.6), channel_id=1, source_target_pairs={{0,1},{1,0},{2,3},{3,2},{4,5},{5,4},{6,7},{7,6},{8,9},{9,8},{10,11... | collective-permute-start | bytes 786440 | tf_op jit(solution)/shard_map/ppermute | solution.py:21
  101.4 18.7 %collective-permute-start.23 = (f16[256,1024]{1,0:T(8,128)(2,1)S(1)}, f16[256,1024]{1,0:T(8,128)(2,1)S(1)}, u32[]{:S(2)}, u32[]{:S(2)}) collective-permute-start(f16[256,1024]{1,0:T(8,128)(2,1)S(1)} %multiply_convert_fusion.2), channel_id=1, source_target_pairs={{2,4},{4,2},{6,8},{8,6},{10,12},{12,10},{14,16},{16,14},{18,20},{2... | collective-permute-start | bytes 1572872 | tf_op jit(solution)/shard_map/ppermute | solution.py:30
  108.1 12.5 %collective-permute-start.25 = (f16[128,1024]{1,0:T(8,128)(2,1)S(1)}, f16[128,1024]{1,0:T(8,128)(2,1)S(1)}, u32[]{:S(2)}, u32[]{:S(2)}) collective-permute-start(f16[128,1024]{1,0:T(8,128)(2,1)S(1)} %multiply_convert_fusion.10), channel_id=1, source_target_pairs={{0,2},{2,0},{4,6},{6,4},{8,10},{10,8},{12,14},{14,12},{16,18},{18,... | collective-permute-start | bytes 786440 | tf_op jit(solution)/shard_map/ppermute | solution.py:30
  108.2 14.7 %collective-permute-start.26 = (f16[128,1024]{1,0:T(8,128)(2,1)S(1)}, f16[128,1024]{1,0:T(8,128)(2,1)S(1)}, u32[]{:S(2)}, u32[]{:S(2)}) collective-permute-start(f16[128,1024]{1,0:T(8,128)(2,1)S(1)} %multiply_convert_fusion.10), channel_id=1, source_target_pairs={{2,4},{4,2},{6,8},{8,6},{10,12},{12,10},{14,16},{16,14},{18,20},{2... | collective-permute-start | bytes 786440 | tf_op jit(solution)/shard_map/ppermute | solution.py:30
  120.6 3.4 %copy-start.3 = (f32[1,2048,1024]{2,1,0:T(8,128)}, f32[1,2048,1024]{2,1,0:T(8,128)S(1)}, u32[]{:S(2)}) copy-start(f32[1,2048,1024]{2,1,0:T(8,128)S(1)} %bitcast_dynamic-update-slice_fusion.6) | copy-start | bytes 25165828

commit v16 on v15

--- a/solution.py
+++ b/solution.py
@@ -101,7 +101,7 @@
     mixed = 0
     out = jnp.zeros_like(weights)
     split = cuts[min(3, chunks)]
-    begun = min(2, chunks)
+    begun = min(3, chunks)
     made = for_others(0, cuts[begun])
     terms = {chunk: [term[cuts[chunk]:cuts[chunk + 1]] for term in made] for chunk in range(begun)}
 
@@ -114,8 +114,8 @@
     far[-1] = swapped(sent, "blk", 1)
     near[-1] = swapped(sent, "blk", 0)
 
-    if begun > 1:
-        arrived[1] = add_over_fsdp(terms[1])
+    for chunk in range(1, begun):
+        arrived[chunk] = add_over_fsdp(terms[chunk])
     base = [own_part(shard, 0, split)]
 
     arrived[0], base, terms = lax.optimization_barrier((arrived[0], base, terms))

time: 126 us -> 121 us (0.960); the launches traced: 125 us -> 118 us
  starting transfers between devices: 33.2 us -> 29.3 us
  waiting for transfers between devices: 39.3 us -> 35.9 us
    ppermute x18, starting transfers between devices: 26.9 us -> 21.6 us  [swapped(): return lax.ppermute(value, axis, pairs)]
    ppermute x9, waiting for transfers between devices: 8.85 us -> 6.95 us  [from_behind(): return lax.ppermute(value, axis, pairs)]
    ppermute x9, starting transfers between devices: 6.22 us -> 7.74 us  [from_behind(): return lax.ppermute(value, axis, pairs)]
    ppermute x18, waiting for transfers between devices: 30.5 us -> 29 us  [swapped(): return lax.ppermute(value, axis, pairs)]
    unnamed x18 -> x22, local copies, waits for them, and re-layouts: 2.88 us -> 3.01 us
  transfers between devices with their start and end apart: 27 -> 27, of which waited for: 10 -> 10; matrix products, arithmetic and copies ran while one was open for 36% -> 37% of each run, Pallas kernels for 0% -> 0%
where the time goes in v16:
time: 121 us; the launch traced here: 118 us
  waiting for transfers between devices  35.9 us (30%)
  starting transfers between devices  29.3 us (24%)
  other arithmetic  23.4 us (19%)
  matrix products  21.4 us (18%)
  local copies, waits for them, and re-layouts  7.95 us (7%)
    ppermute x18, waiting for transfers between devices, swapped(): return lax.ppermute(value, axis, pairs)  29 us
    ppermute x18, starting transfers between devices, swapped(): return lax.ppermute(value, axis, pairs)  21.6 us
    dot_general x6, matrix products, partial(): lax.dot_general(block, cot_local, (((0,), (0,)), ((), ())), preferred_ele...  21.4 us
    convert_element_type x8, other arithmetic, on_device(): sent = (u_of(chunk) * scale).astype(WIRE)  10 us
    dynamic_update_slice x8, other arithmetic, mix_into(): return lax.dynamic_update_slice_in_dim(out, value, cuts[chunk], axis=0)  9.79 us
    ppermute x9, starting transfers between devices, from_behind(): return lax.ppermute(value, axis, pairs)  7.74 us
    ppermute x9, waiting for transfers between devices, from_behind(): return lax.ppermute(value, axis, pairs)  6.95 us
    unnamed x22, local copies, waits for them, and re-layouts  3.01 us
  transfers between devices with their start and end apart: 27, of which 10 were waited for; matrix products, arithmetic and copies ran while one was open for 37% of the time, Pallas kernels for 0%

profile of v16, /device:TPU:1, one launch (start us, length us, event | category | flops | bytes accessed | tf_op | source)
XLA Modules:
  0.0 118.3 jit_solution(4056177386725941478)
XLA Ops:
  0.0 1.5 %copy-done = bf16[1,896,1024]{2,1,0:T(8,128)(2,1)S(1)} copy-done((bf16[1,896,1024]{2,1,0:T(8,128)(2,1)S(1)}, bf16[1,896,1024]{2,1,0:T(8,128)(2,1)}, u32[]{:S(2)}) %copy-start) | copy-done | bytes 1835032
  1.5 3.2 %multiply_convert_fusion.1 = f16[768,1024]{1,0:T(8,128)(2,1)S(1)} fusion(bf16[1,896,1024]{2,1,0:T(8,128)(2,1)S(1)} %copy-done, bf16[1,896,4096]{2,1,0:T(8,128)(2,1)} %param.5, s32[]{:T(128)S(6)} %select_n.46), kind=kOutput, calls=%fused_computation.3 | convolution fusion | flops 1410859008 | bytes 4784132 | tf_op jit(solution)/shard_map/dot_general | solution.py:65
  4.7 1.4 %fusion.38 = (f16[256,1024]{1,0:T(8,128)(2,1)}, f16[256,1024]{1,0:T(8,128)(2,1)}, f16[256,1024]{1,0:T(8,128)(2,1)}) fusion(f16[768,1024]{1,0:T(8,128)(2,1)S(1)} %multiply_convert_fusion.1), kind=kLoop, calls=%fused_computation.69 | loop fusion | bytes 3145728 | tf_op jit(solution)/shard_map/slice | solution.py:106
  6.1 2.1 %collective-permute-start = (f16[256,1024]{1,0:T(8,128)(2,1)}, f16[256,1024]{1,0:T(8,128)(2,1)}, u32[]{:S(2)}, u32[]{:S(2)}) collective-permute-start(f16[256,1024]{1,0:T(8,128)(2,1)} %get-tuple-element.104), channel_id=1, source_target_pairs={{0,1},{1,0},{2,3},{3,2},{4,5},{5,4},{6,7},{7,6},{8,9},{9,8},{10,11... | collective-permute-start | bytes 1572872 | tf_op jit(solution)/shard_map/ppermute | solution.py:21
  8.1 1.4 %fusion.19 = f32[128,1024]{1,0:T(8,128)S(1)} fusion(bf16[1,896,1024]{2,1,0:T(8,128)(2,1)S(1)} %copy-done, bf16[1,896,4096]{2,1,0:T(8,128)(2,1)} %param.5, s32[]{:T(128)S(6)} %select_n.50), kind=kOutput, calls=%fused_computation.21 | convolution fusion | flops 235012096 | bytes 2588676 | tf_op jit(solution)/shard_map/dot_general | solution.py:65
  9.5 1.7 %fusion.22 = f32[128,1024]{1,0:T(8,128)S(1)} fusion(bf16[1,896,1024]{2,1,0:T(8,128)(2,1)S(1)} %copy-done, f32[1,2048,1024]{2,1,0:T(8,128)} %param.4, bf16[1,896,4096]{2,1,0:T(8,128)(2,1)} %param.5, s32[]{:T(128)S(6)} %select_n.48), kind=kOutput, calls=%fused_computation.22 | convolution fusion | flops 235143168 | bytes 3112964 | tf_op jit(solution)/shard_map/dot_general | solution.py:65
  11.2 1.0 multiply_convert_fusion.9
  12.2 1.0 collective-permute-start.1
  13.2 1.1 collective-permute-start.5
  14.3 0.2 collective-permute-start.4
  14.5 1.2 %collective-permute-start.6 = (f16[256,1024]{1,0:T(8,128)(2,1)}, f16[256,1024]{1,0:T(8,128)(2,1)S(1)}, u32[]{:S(2)}, u32[]{:S(2)}) collective-permute-start(f16[256,1024]{1,0:T(8,128)(2,1)} %get-tuple-element.207), channel_id=1, source_target_pairs={{0,1},{1,0},{2,3},{3,2},{4,5},{5,4},{6,7},{7,6},{8,9},{9,8},{10,11... | collective-permute-start | bytes 1572872 | tf_op jit(solution)/shard_map/ppermute | solution.py:21
  15.7 4.2 %bitcast_subtract_fusion.1 = f32[768,1024]{1,0:T(8,128)S(1)} fusion(f32[1,2048,1024]{2,1,0:T(8,128)} %param.4, bf16[1,896,1024]{2,1,0:T(8,128)(2,1)S(1)} %copy-done, bf16[1,896,4096]{2,1,0:T(8,128)(2,1)} %param.5, s32[]{:T(128)S(6)} %select_n.47), kind=kOutput, calls=%fused_computation.2 | convolution fusion | flops 1410859008 | bytes 9502724 | tf_op jit(solution)/shard_map/dot_general | solution.py:65
  19.9 0.2 collective-permute-done
  20.1 1.5 %copy-done.1 = f32[768,1024]{1,0:T(8,128)} copy-done((f32[768,1024]{1,0:T(8,128)}, f32[768,1024]{1,0:T(8,128)S(1)}, u32[]{:S(2)}) %copy-start.1) | copy-done | bytes 3145752
  21.6 2.1 %multiply_convert_fusion.8 = f16[256,1024]{1,0:T(8,128)(2,1)} fusion(f16[256,1024]{1,0:T(8,128)(2,1)} %collective-permute-done, f32[768,1024]{1,0:T(8,128)S(1)} %bitcast_subtract_fusion.1), kind=kLoop, calls=%fused_computation.44 | loop fusion | flops 1310720 | bytes 2097152 | tf_op jit(solution)/shard_map/convert_element_type | solution.py:132
  23.7 4.1 %collective-permute-start.2 = (f16[256,1024]{1,0:T(8,128)(2,1)}, f16[256,1024]{1,0:T(8,128)(2,1)}, u32[]{:S(2)}, u32[]{:S(2)}) collective-permute-start(f16[256,1024]{1,0:T(8,128)(2,1)} %multiply_convert_fusion.8), channel_id=1, source_target_pairs={{0,2},{2,0},{4,6},{6,4},{8,10},{10,8},{12,14},{14,12},{16,18},{18,... | collective-permute-start | bytes 1572872 | tf_op jit(solution)/shard_map/ppermute | solution.py:30
  27.8 4.8 %multiply_convert_fusion = f16[1280,1024]{1,0:T(8,128)(2,1)S(1)} fusion(bf16[1,896,4096]{2,1,0:T(8,128)(2,1)} %param.5, s32[]{:T(128)S(6)} %select_n.52, bf16[1,896,1024]{2,1,0:T(8,128)(2,1)S(1)} %copy-done), kind=kOutput, calls=%fused_computation.1 | convolution fusion | flops 2351431680 | bytes 6750212 | tf_op jit(solution)/shard_map/dot_general | solution.py:65
  32.6 0.8 slice.171
  33.3 1.7 %fusion.37 = (f16[256,1024]{1,0:T(8,128)(2,1)}, f16[256,1024]{1,0:T(8,128)(2,1)}, f16[256,1024]{1,0:T(8,128)(2,1)}, f16[256,1024]{1,0:T(8,128)(2,1)}) fusion(f16[1280,1024]{1,0:T(8,128)(2,1)S(1)} %multiply_convert_fusion), kind=kLoop, calls=%fused_computation.68 | loop fusion | bytes 4194304 | tf_op jit(solution)/shard_map/slice | solution.py:141
  35.0 0.2 collective-permute-start.3
  35.2 2.5 %multiply_convert_fusion.7 = f16[256,1024]{1,0:T(8,128)(2,1)} fusion(f16[256,1024]{1,0:T(8,128)(2,1)} %collective-permute-done.4, f32[768,1024]{1,0:T(8,128)} %copy-done.1), kind=kLoop, calls=%fused_computation.42 | loop fusion | flops 1310720 | bytes 2097152 | tf_op jit(solution)/shard_map/convert_element_type | solution.py:132
  37.7 3.0 %collective-permute-start.8 = (f16[256,1024]{1,0:T(8,128)(2,1)}, f16[256,1024]{1,0:T(8,128)(2,1)}, u32[]{:S(2)}, u32[]{:S(2)}) collective-permute-start(f16[256,1024]{1,0:T(8,128)(2,1)} %multiply_convert_fusion.7), channel_id=1, source_target_pairs={{0,2},{2,0},{4,6},{6,4},{8,10},{10,8},{12,14},{14,12},{16,18},{18,... | collective-permute-start | bytes 1572872 | tf_op jit(solution)/shard_map/ppermute | solution.py:30
  40.7 0.1 fusion.36
  40.8 0.2 multiply_reduce_fusion
  40.9 0.1 broadcast_in_dim.26
  41.0 1.4 %collective-permute-done.6 = f16[256,1024]{1,0:T(8,128)(2,1)S(1)} collective-permute-done((f16[256,1024]{1,0:T(8,128)(2,1)}, f16[256,1024]{1,0:T(8,128)(2,1)S(1)}, u32[]{:S(2)}, u32[]{:S(2)}) %collective-permute-start.6) | collective-permute-done | bytes 524320 | tf_op jit(solution)/shard_map/ppermute | solution.py:21
  42.5 1.1 collective-permute-start.11
  43.6 1.5 %multiply_add_fusion = f32[256,1024]{1,0:T(8,128)S(1)} fusion(f16[256,1024]{1,0:T(8,128)(2,1)} %collective-permute-done.5, f32[256,1024]{1,0:T(8,128)S(1)} %get-tuple-element.144, f16[256,1024]{1,0:T(8,128)(2,1)} %collective-permute-done.1, f32[1024]{0:T(1024)S(1)} %bitcast.71, f32[1024]{0:T(1024)S(1)} %bitcast.80, f32[1024]{0:T(1024)S(1)} %bitcast.62), kind=kLoop, calls=%fused_computation.39 | loop fusion | flops 1835008 | bytes 3158016 | tf_op jit(solution)/shard_map/add | solution.py:90
  45.1 0.8 fusion.25
  45.9 2.3 %multiply_convert_fusion.6 = f16[256,1024]{1,0:T(8,128)(2,1)} fusion(f16[256,1024]{1,0:T(8,128)(2,1)S(1)} %collective-permute-done.6, f32[768,1024]{1,0:T(8,128)} %copy-done.1), kind=kLoop, calls=%fused_computation.40 | loop fusion | flops 1310720 | bytes 2097152 | tf_op jit(solution)/shard_map/convert_element_type | solution.py:132
  48.1 3.0 %collective-permute-start.10 = (f16[256,1024]{1,0:T(8,128)(2,1)}, f16[256,1024]{1,0:T(8,128)(2,1)S(1)}, u32[]{:S(2)}, u32[]{:S(2)}) collective-permute-start(f16[256,1024]{1,0:T(8,128)(2,1)} %multiply_convert_fusion.6), channel_id=1, source_target_pairs={{0,2},{2,0},{4,6},{6,4},{8,10},{10,8},{12,14},{14,12},{16,18},{18,... | collective-permute-start | bytes 1572872 | tf_op jit(solution)/shard_map/ppermute | solution.py:30
  51.1 1.1 collective-permute-start.12
  52.2 6.2 %bitcast_subtract_fusion = f32[1280,1024]{1,0:T(8,128)S(1)} fusion(f32[1,2048,1024]{2,1,0:T(8,128)} %param.4, bf16[1,896,4096]{2,1,0:T(8,128)(2,1)} %param.5, s32[]{:T(128)S(6)} %select_n.53, bf16[1,896,1024]{2,1,0:T(8,128)(2,1)S(1)} %copy-done), kind=kOutput, calls=%fused_computation | convolution fusion | flops 2351431680 | bytes 14614532 | tf_op jit(solution)/shard_map/dot_general | solution.py:65
  58.5 1.5 %multiply_convert_fusion.5 = f16[256,1024]{1,0:T(8,128)(2,1)S(1)} fusion(f16[256,1024]{1,0:T(8,128)(2,1)} %collective-permute-done.3, f32[1280,1024]{1,0:T(8,128)S(1)} %bitcast_subtract_fusion), kind=kLoop, calls=%fused_computation.37 | loop fusion | flops 1310720 | bytes 2097152 | tf_op jit(solution)/shard_map/convert_element_type | solution.py:132
  59.9 3.6 %collective-permute-start.13 = (f16[256,1024]{1,0:T(8,128)(2,1)S(1)}, f16[256,1024]{1,0:T(8,128)(2,1)S(1)}, u32[]{:S(2)}, u32[]{:S(2)}) collective-permute-start(f16[256,1024]{1,0:T(8,128)(2,1)S(1)} %multiply_convert_fusion.5), channel_id=1, source_target_pairs={{0,2},{2,0},{4,6},{6,4},{8,10},{10,8},{12,14},{14,12},{16,18},{18,... | collective-permute-start | bytes 1572872 | tf_op jit(solution)/shard_map/ppermute | solution.py:30
  63.6 0.2 collective-permute-start.14
  63.8 1.2 %collective-permute-done.11 = f16[256,1024]{1,0:T(8,128)(2,1)} collective-permute-done((f16[256,1024]{1,0:T(8,128)(2,1)}, f16[256,1024]{1,0:T(8,128)(2,1)}, u32[]{:S(2)}, u32[]{:S(2)}) %collective-permute-start.11) | collective-permute-done | bytes 524320 | tf_op jit(solution)/shard_map/ppermute | solution.py:21
  65.0 4.9 %collective-permute-done.12 = f16[256,1024]{1,0:T(8,128)(2,1)} collective-permute-done((f16[256,1024]{1,0:T(8,128)(2,1)}, f16[256,1024]{1,0:T(8,128)(2,1)}, u32[]{:S(2)}, u32[]{:S(2)}) %collective-permute-start.12) | collective-permute-done | bytes 524320 | tf_op jit(solution)/shard_map/ppermute | solution.py:30
  69.9 1.2 %multiply_convert_fusion.4 = f16[256,1024]{1,0:T(8,128)(2,1)S(1)} fusion(f16[256,1024]{1,0:T(8,128)(2,1)} %collective-permute-done.11, f32[1280,1024]{1,0:T(8,128)S(1)} %bitcast_subtract_fusion), kind=kLoop, calls=%fused_computation.35 | loop fusion | flops 1310720 | bytes 2097152 | tf_op jit(solution)/shard_map/convert_element_type | solution.py:132
  71.3 0.1 collective-permute-start.17
  71.3 2.5 %collective-permute-start.18 = (f16[256,1024]{1,0:T(8,128)(2,1)S(1)}, f16[256,1024]{1,0:T(8,128)(2,1)S(1)}, u32[]{:S(2)}, u32[]{:S(2)}) collective-permute-start(f16[256,1024]{1,0:T(8,128)(2,1)S(1)} %multiply_convert_fusion.4), channel_id=1, source_target_pairs={{2,4},{4,2},{6,8},{8,6},{10,12},{12,10},{14,16},{16,14},{18,20},{2... | collective-permute-start | bytes 1572872 | tf_op jit(solution)/shard_map/ppermute | solution.py:30
  73.8 3.2 %collective-permute-done.14 = f16[256,1024]{1,0:T(8,128)(2,1)S(1)} collective-permute-done((f16[256,1024]{1,0:T(8,128)(2,1)S(1)}, f16[256,1024]{1,0:T(8,128)(2,1)S(1)}, u32[]{:S(2)}, u32[]{:S(2)}) %collective-permute-start.14) | collective-permute-done | bytes 524320 | tf_op jit(solution)/shard_map/ppermute | solution.py:21
  77.0 6.9 %collective-permute-done.15 = f16[256,1024]{1,0:T(8,128)(2,1)S(1)} collective-permute-done((f16[256,1024]{1,0:T(8,128)(2,1)S(1)}, f16[256,1024]{1,0:T(8,128)(2,1)S(1)}, u32[]{:S(2)}, u32[]{:S(2)}) %collective-permute-start.15) | collective-permute-done | bytes 524320 | tf_op jit(solution)/shard_map/ppermute | solution.py:30
  83.9 0.2 multiply_convert_fusion.3
  84.2 1.3 %collective-permute-start.20 = (f16[128,1024]{1,0:T(8,128)(2,1)S(1)}, f16[128,1024]{1,0:T(8,128)(2,1)S(1)}, u32[]{:S(2)}, u32[]{:S(2)}) collective-permute-start(f16[128,1024]{1,0:T(8,128)(2,1)S(1)} %copy-done.9), channel_id=1, source_target_pairs={{0,1},{1,0},{2,3},{3,2},{4,5},{5,4},{6,7},{7,6},{8,9},{9,8},{10,11... | collective-permute-start | bytes 786440 | tf_op jit(solution)/shard_map/ppermute | solution.py:21
  85.5 1.1 broadcast_in_dim.25
  86.6 1.8 %add_dynamic-update-slice_fusion.1 = f32[2048,1024]{1,0:T(8,128)S(1)} fusion(f32[2048,1024]{1,0:T(8,128)S(1)} %broadcast_in_dim.25, f16[256,1024]{1,0:T(8,128)(2,1)} %collective-permute-done.7, f32[768,1024]{1,0:T(8,128)S(1)} %copy-done.2, f16[256,1024]{1,0:T(8,128)(2,1)} %collective-permute-done.2, f16[256,1024]{1,0:T(8,128)(2,1)} %collective-permute-done, ...), kind=kLoop, calls=%fused_computation.32 | loop fusion | flops 2621440 | bytes 3682304 | tf_op jit(solution)/shard_map/dynamic_update_slice | solution.py:97
  88.5 1.1 collective-permute-done.18
  89.6 0.2 multiply_convert_fusion.2
  89.8 0.1 collective-permute-start.22
  89.9 1.3 %collective-permute-start.24 = (f16[128,1024]{1,0:T(8,128)(2,1)S(1)}, f16[128,1024]{1,0:T(8,128)(2,1)S(1)}, u32[]{:S(2)}, u32[]{:S(2)}) collective-permute-start(f16[128,1024]{1,0:T(8,128)(2,1)S(1)} %copy-done.8), channel_id=1, source_target_pairs={{0,1},{1,0},{2,3},{3,2},{4,5},{5,4},{6,7},{7,6},{8,9},{9,8},{10,11... | collective-permute-start | bytes 786440 | tf_op jit(solution)/shard_map/ppermute | solution.py:21
  91.2 1.8 %collective-permute-start.23 = (f16[256,1024]{1,0:T(8,128)(2,1)S(1)}, f16[256,1024]{1,0:T(8,128)(2,1)S(1)}, u32[]{:S(2)}, u32[]{:S(2)}) collective-permute-start(f16[256,1024]{1,0:T(8,128)(2,1)S(1)} %multiply_convert_fusion.2), channel_id=1, source_target_pairs={{2,4},{4,2},{6,8},{8,6},{10,12},{12,10},{14,16},{16,14},{18,20},{2... | collective-permute-start | bytes 1572872 | tf_op jit(solution)/shard_map/ppermute | solution.py:30
  93.0 0.9 collective-permute-done.20
  93.9 12.2 %collective-permute-done.21 = f16[256,1024]{1,0:T(8,128)(2,1)S(1)} collective-permute-done((f16[256,1024]{1,0:T(8,128)(2,1)S(1)}, f16[256,1024]{1,0:T(8,128)(2,1)S(1)}, u32[]{:S(2)}, u32[]{:S(2)}) %collective-permute-start.21) | collective-permute-done | bytes 524320 | tf_op jit(solution)/shard_map/ppermute | solution.py:30
  106.1 1.8 %add_dynamic-update-slice_fusion = f32[2048,1024]{1,0:T(8,128)S(1)} fusion(f32[2048,1024]{1,0:T(8,128)S(1)} %add_dynamic-update-slice_fusion.1, f16[256,1024]{1,0:T(8,128)(2,1)} %collective-permute-done.9, f32[768,1024]{1,0:T(8,128)S(1)} %copy-done.2, f16[256,1024]{1,0:T(8,128)(2,1)} %collective-permute-done.8, f16[256,1024]{1,0:T(8,128)(2,1)} %collective-permute-done.4, ...), kind=kLoop, calls=%fused_computation.29 | loop fusion | flops 2621440 | bytes 3682304 | tf_op jit(solution)/shard_map/dynamic_update_slice | solution.py:97
  107.9 0.1 multiply_convert_fusion.10
  108.2 1.5 %bitcast_dynamic-update-slice_fusion.4 = f32[1,2048,1024]{2,1,0:T(8,128)S(1)} fusion(f32[1,2048,1024]{2,1,0:T(8,128)S(1)} %bitcast.61, f16[256,1024]{1,0:T(8,128)(2,1)} %collective-permute-done.12, f32[768,1024]{1,0:T(8,128)S(1)} %copy-done.2, f16[256,1024]{1,0:T(8,128)(2,1)S(1)} %copy-done.5, f16[256,1024]{1,0:T(8,128)(2,1)S(1)} %collective-permute-done.6, ...), kind=kLoop, calls=%fused_computation.28 | loop fusion | flops 2621440 | bytes 3682304 | tf_op jit(solution)/shard_map/dynamic_update_slice | solution.py:97
  109.6 1.5 %bitcast_dynamic-update-slice_fusion.3 = f32[1,2048,1024]{2,1,0:T(8,128)S(1)} fusion(f32[1,2048,1024]{2,1,0:T(8,128)S(1)} %bitcast_dynamic-update-slice_fusion.4, f16[256,1024]{1,0:T(8,128)(2,1)S(1)} %collective-permute-done.15, f32[1280,1024]{1,0:T(8,128)S(1)} %bitcast_subtract_fusion, f16[256,1024]{1,0:T(8,128)(2,1)S(1)} %collective-permute-done.13, ...), kind=kLoop, calls=%fused_computation.27 | loop fusion | flops 2621440 | bytes 3682304 | tf_op jit(solution)/shard_map/dynamic_update_slice | solution.py:97
  111.1 1.5 %bitcast_dynamic-update-slice_fusion.2 = f32[1,2048,1024]{2,1,0:T(8,128)S(1)} fusion(f32[1,2048,1024]{2,1,0:T(8,128)S(1)} %bitcast_dynamic-update-slice_fusion.3, f16[256,1024]{1,0:T(8,128)(2,1)S(1)} %collective-permute-done.18, f32[1280,1024]{1,0:T(8,128)S(1)} %bitcast_subtract_fusion, f16[256,1024]{1,0:T(8,128)(2,1)S(1)} %collective-permute-done.16, ...), kind=kLoop, calls=%fused_computation.26 | loop fusion | flops 2621440 | bytes 3682304 | tf_op jit(solution)/shard_map/dynamic_update_slice | solution.py:97
  112.5 0.4 bitcast_dynamic-update-slice_fusion.1
  113.0 0.4 bitcast_dynamic-update-slice_fusion
  113.4 0.1 bitcast_dynamic-update-slice_fusion.6
  113.5 3.8 %collective-permute-done.26 = f16[128,1024]{1,0:T(8,128)(2,1)S(1)} collective-permute-done((f16[128,1024]{1,0:T(8,128)(2,1)S(1)}, f16[128,1024]{1,0:T(8,128)(2,1)S(1)}, u32[]{:S(2)}, u32[]{:S(2)}) %collective-permute-start.26) | collective-permute-done | bytes 262176 | tf_op jit(solution)/shard_map/ppermute | solution.py:30
  117.3 1.0 bitcast_dynamic-update-slice_fusion.5
  (47 shorter events, 0.5 us)
Async XLA Ops:
  0.0 1.5 %copy-start = (bf16[1,896,1024]{2,1,0:T(8,128)(2,1)S(1)}, bf16[1,896,1024]{2,1,0:T(8,128)(2,1)}, u32[]{:S(2)}) copy-start(bf16[1,896,1024]{2,1,0:T(8,128)(2,1)} %param.6) | copy-start | bytes 5505028
  6.1 14.0 %collective-permute-start = (f16[256,1024]{1,0:T(8,128)(2,1)}, f16[256,1024]{1,0:T(8,128)(2,1)}, u32[]{:S(2)}, u32[]{:S(2)}) collective-permute-start(f16[256,1024]{1,0:T(8,128)(2,1)} %get-tuple-element.104), channel_id=1, source_target_pairs={{0,1},{1,0},{2,3},{3,2},{4,5},{5,4},{6,7},{7,6},{8,9},{9,8},{10,11... | collective-permute-start | bytes 1572872 | tf_op jit(solution)/shard_map/ppermute | solution.py:21
  12.2 7.9 %collective-permute-start.1 = (f16[256,1024]{1,0:T(8,128)(2,1)}, f16[256,1024]{1,0:T(8,128)(2,1)}, u32[]{:S(2)}, u32[]{:S(2)}) collective-permute-start(f16[256,1024]{1,0:T(8,128)(2,1)} %get-tuple-element.108), channel_id=1, source_target_pairs={{0,2},{2,0},{4,6},{6,4},{8,10},{10,8},{12,14},{14,12},{16,18},{18,... | collective-permute-start | bytes 1572872 | tf_op jit(solution)/shard_map/ppermute | solution.py:30
  13.2 22.1 %collective-permute-start.5 = (f16[256,1024]{1,0:T(8,128)(2,1)}, f16[256,1024]{1,0:T(8,128)(2,1)}, u32[]{:S(2)}, u32[]{:S(2)}) collective-permute-start(f16[256,1024]{1,0:T(8,128)(2,1)} %get-tuple-element.108), channel_id=1, source_target_pairs={{2,4},{4,2},{6,8},{8,6},{10,12},{12,10},{14,16},{16,14},{18,20},{2... | collective-permute-start | bytes 1572872 | tf_op jit(solution)/shard_map/ppermute | solution.py:30
  14.3 21.0 %collective-permute-start.4 = (f16[256,1024]{1,0:T(8,128)(2,1)}, f16[256,1024]{1,0:T(8,128)(2,1)}, u32[]{:S(2)}, u32[]{:S(2)}) collective-permute-start(f16[256,1024]{1,0:T(8,128)(2,1)} %get-tuple-element.208), channel_id=1, source_target_pairs={{0,1},{1,0},{2,3},{3,2},{4,5},{5,4},{6,7},{7,6},{8,9},{9,8},{10,11... | collective-permute-start | bytes 1572872 | tf_op jit(solution)/shard_map/ppermute | solution.py:21
  14.5 28.0 %collective-permute-start.6 = (f16[256,1024]{1,0:T(8,128)(2,1)}, f16[256,1024]{1,0:T(8,128)(2,1)S(1)}, u32[]{:S(2)}, u32[]{:S(2)}) collective-permute-start(f16[256,1024]{1,0:T(8,128)(2,1)} %get-tuple-element.207), channel_id=1, source_target_pairs={{0,1},{1,0},{2,3},{3,2},{4,5},{5,4},{6,7},{7,6},{8,9},{9,8},{10,11... | collective-permute-start | bytes 1572872 | tf_op jit(solution)/shard_map/ppermute | solution.py:21
  19.9 1.7 %copy-start.1 = (f32[768,1024]{1,0:T(8,128)}, f32[768,1024]{1,0:T(8,128)S(1)}, u32[]{:S(2)}) copy-start(f32[768,1024]{1,0:T(8,128)S(1)} %bitcast_subtract_fusion.1) | copy-start | bytes 9437188
  23.7 11.3 %collective-permute-start.2 = (f16[256,1024]{1,0:T(8,128)(2,1)}, f16[256,1024]{1,0:T(8,128)(2,1)}, u32[]{:S(2)}, u32[]{:S(2)}) collective-permute-start(f16[256,1024]{1,0:T(8,128)(2,1)} %multiply_convert_fusion.8), channel_id=1, source_target_pairs={{0,2},{2,0},{4,6},{6,4},{8,10},{10,8},{12,14},{14,12},{16,18},{18,... | collective-permute-start | bytes 1572872 | tf_op jit(solution)/shard_map/ppermute | solution.py:30
  27.8 14.7 %collective-permute-start.7 = (f16[256,1024]{1,0:T(8,128)(2,1)}, f16[256,1024]{1,0:T(8,128)(2,1)}, u32[]{:S(2)}, u32[]{:S(2)}) collective-permute-start(f16[256,1024]{1,0:T(8,128)(2,1)} %multiply_convert_fusion.8), channel_id=1, source_target_pairs={{2,4},{4,2},{6,8},{8,6},{10,12},{12,10},{14,16},{16,14},{18,20},{2... | collective-permute-start | bytes 1572872 | tf_op jit(solution)/shard_map/ppermute | solution.py:30
  32.6 8.1 %copy-start.10 = (s32[16,3]{0,1:T(4,128)S(1)}, s32[16,3]{0,1:T(4,128)}, u32[]{:S(2)}) copy-start(s32[16,3]{0,1:T(4,128)} %param.7) | copy-start | bytes 580
  35.0 23.4 %collective-permute-start.3 = (f16[256,1024]{1,0:T(8,128)(2,1)}, f16[256,1024]{1,0:T(8,128)(2,1)}, u32[]{:S(2)}, u32[]{:S(2)}) collective-permute-start(f16[256,1024]{1,0:T(8,128)(2,1)} %get-tuple-element.112), channel_id=1, source_target_pairs={{0,1},{1,0},{2,3},{3,2},{4,5},{5,4},{6,7},{7,6},{8,9},{9,8},{10,11... | collective-permute-start | bytes 1572872 | tf_op jit(solution)/shard_map/ppermute | solution.py:21
  37.7 8.2 %collective-permute-start.8 = (f16[256,1024]{1,0:T(8,128)(2,1)}, f16[256,1024]{1,0:T(8,128)(2,1)}, u32[]{:S(2)}, u32[]{:S(2)}) collective-permute-start(f16[256,1024]{1,0:T(8,128)(2,1)} %multiply_convert_fusion.7), channel_id=1, source_target_pairs={{0,2},{2,0},{4,6},{6,4},{8,10},{10,8},{12,14},{14,12},{16,18},{18,... | collective-permute-start | bytes 1572872 | tf_op jit(solution)/shard_map/ppermute | solution.py:30
  40.6 17.8 %collective-permute-start.9 = (f16[256,1024]{1,0:T(8,128)(2,1)}, f16[256,1024]{1,0:T(8,128)(2,1)}, u32[]{:S(2)}, u32[]{:S(2)}) collective-permute-start(f16[256,1024]{1,0:T(8,128)(2,1)} %multiply_convert_fusion.7), channel_id=1, source_target_pairs={{2,4},{4,2},{6,8},{8,6},{10,12},{12,10},{14,16},{16,14},{18,20},{2... | collective-permute-start | bytes 1572872 | tf_op jit(solution)/shard_map/ppermute | solution.py:30
  42.5 22.5 %collective-permute-start.11 = (f16[256,1024]{1,0:T(8,128)(2,1)}, f16[256,1024]{1,0:T(8,128)(2,1)}, u32[]{:S(2)}, u32[]{:S(2)}) collective-permute-start(f16[256,1024]{1,0:T(8,128)(2,1)} %get-tuple-element.131), channel_id=1, source_target_pairs={{0,1},{1,0},{2,3},{3,2},{4,5},{5,4},{6,7},{7,6},{8,9},{9,8},{10,11... | collective-permute-start | bytes 1572872 | tf_op jit(solution)/shard_map/ppermute | solution.py:21
  48.1 10.3 %collective-permute-start.10 = (f16[256,1024]{1,0:T(8,128)(2,1)}, f16[256,1024]{1,0:T(8,128)(2,1)S(1)}, u32[]{:S(2)}, u32[]{:S(2)}) collective-permute-start(f16[256,1024]{1,0:T(8,128)(2,1)} %multiply_convert_fusion.6), channel_id=1, source_target_pairs={{0,2},{2,0},{4,6},{6,4},{8,10},{10,8},{12,14},{14,12},{16,18},{18,... | collective-permute-start | bytes 1572872 | tf_op jit(solution)/shard_map/ppermute | solution.py:30
  51.1 18.8 %collective-permute-start.12 = (f16[256,1024]{1,0:T(8,128)(2,1)}, f16[256,1024]{1,0:T(8,128)(2,1)}, u32[]{:S(2)}, u32[]{:S(2)}) collective-permute-start(f16[256,1024]{1,0:T(8,128)(2,1)} %multiply_convert_fusion.6), channel_id=1, source_target_pairs={{2,4},{4,2},{6,8},{8,6},{10,12},{12,10},{14,16},{16,14},{18,20},{2... | collective-permute-start | bytes 1572872 | tf_op jit(solution)/shard_map/ppermute | solution.py:30
  52.2 11.4 %copy-start.7 = (f16[256,1024]{1,0:T(8,128)(2,1)S(1)}, f16[256,1024]{1,0:T(8,128)(2,1)}, u32[]{:S(2)}) copy-start(f16[256,1024]{1,0:T(8,128)(2,1)} %get-tuple-element.134) | copy-start | bytes 1572868
  52.2 19.1 %copy-start.6 = (f16[256,1024]{1,0:T(8,128)(2,1)S(1)}, f16[256,1024]{1,0:T(8,128)(2,1)}, u32[]{:S(2)}) copy-start(f16[256,1024]{1,0:T(8,128)(2,1)} %get-tuple-element.166) | copy-start | bytes 1572868
  58.4 25.8 %copy-start.9 = (f16[128,1024]{1,0:T(8,128)(2,1)S(1)}, f16[128,1024]{1,0:T(8,128)(2,1)}, u32[]{:S(2)}) copy-start(f16[128,1024]{1,0:T(8,128)(2,1)} %slice.171) | copy-start | bytes 786436
  58.5 1.5 %copy-start.4 = (f16[256,1024]{1,0:T(8,128)(2,1)}, f16[256,1024]{1,0:T(8,128)(2,1)S(1)}, u32[]{:S(2)}) copy-start(f16[256,1024]{1,0:T(8,128)(2,1)S(1)} %collective-permute-done.10) | copy-start | bytes 1572868
  59.9 10.0 %collective-permute-start.13 = (f16[256,1024]{1,0:T(8,128)(2,1)S(1)}, f16[256,1024]{1,0:T(8,128)(2,1)S(1)}, u32[]{:S(2)}, u32[]{:S(2)}) collective-permute-start(f16[256,1024]{1,0:T(8,128)(2,1)S(1)} %multiply_convert_fusion.5), channel_id=1, source_target_pairs={{0,2},{2,0},{4,6},{6,4},{8,10},{10,8},{12,14},{14,12},{16,18},{18,... | collective-permute-start | bytes 1572872 | tf_op jit(solution)/shard_map/ppermute | solution.py:30
  63.6 13.5 %collective-permute-start.14 = (f16[256,1024]{1,0:T(8,128)(2,1)S(1)}, f16[256,1024]{1,0:T(8,128)(2,1)S(1)}, u32[]{:S(2)}, u32[]{:S(2)}) collective-permute-start(f16[256,1024]{1,0:T(8,128)(2,1)S(1)} %copy-done.7), channel_id=1, source_target_pairs={{0,1},{1,0},{2,3},{3,2},{4,5},{5,4},{6,7},{7,6},{8,9},{9,8},{10,11... | collective-permute-start | bytes 1572872 | tf_op jit(solution)/shard_map/ppermute | solution.py:21
  63.8 20.1 %collective-permute-start.15 = (f16[256,1024]{1,0:T(8,128)(2,1)S(1)}, f16[256,1024]{1,0:T(8,128)(2,1)S(1)}, u32[]{:S(2)}, u32[]{:S(2)}) collective-permute-start(f16[256,1024]{1,0:T(8,128)(2,1)S(1)} %multiply_convert_fusion.5), channel_id=1, source_target_pairs={{2,4},{4,2},{6,8},{8,6},{10,12},{12,10},{14,16},{16,14},{18,20},{2... | collective-permute-start | bytes 1572872 | tf_op jit(solution)/shard_map/ppermute | solution.py:30
  71.2 15.5 %copy-start.2 = (f32[768,1024]{1,0:T(8,128)S(1)}, f32[768,1024]{1,0:T(8,128)}, u32[]{:S(2)}) copy-start(f32[768,1024]{1,0:T(8,128)} %copy-done.1) | copy-start | bytes 9437188
  71.2 12.8 %collective-permute-start.16 = (f16[256,1024]{1,0:T(8,128)(2,1)S(1)}, f16[256,1024]{1,0:T(8,128)(2,1)S(1)}, u32[]{:S(2)}, u32[]{:S(2)}) collective-permute-start(f16[256,1024]{1,0:T(8,128)(2,1)S(1)} %multiply_convert_fusion.4), channel_id=1, source_target_pairs={{0,2},{2,0},{4,6},{6,4},{8,10},{10,8},{12,14},{14,12},{16,18},{18,... | collective-permute-start | bytes 1572872 | tf_op jit(solution)/shard_map/ppermute | solution.py:30
  71.3 17.2 %collective-permute-start.17 = (f16[256,1024]{1,0:T(8,128)(2,1)S(1)}, f16[256,1024]{1,0:T(8,128)(2,1)S(1)}, u32[]{:S(2)}, u32[]{:S(2)}) collective-permute-start(f16[256,1024]{1,0:T(8,128)(2,1)S(1)} %copy-done.6), channel_id=1, source_target_pairs={{0,1},{1,0},{2,3},{3,2},{4,5},{5,4},{6,7},{7,6},{8,9},{9,8},{10,11... | collective-permute-start | bytes 1572872 | tf_op jit(solution)/shard_map/ppermute | solution.py:21
  71.3 18.2 %collective-permute-start.18 = (f16[256,1024]{1,0:T(8,128)(2,1)S(1)}, f16[256,1024]{1,0:T(8,128)(2,1)S(1)}, u32[]{:S(2)}, u32[]{:S(2)}) collective-permute-start(f16[256,1024]{1,0:T(8,128)(2,1)S(1)} %multiply_convert_fusion.4), channel_id=1, source_target_pairs={{2,4},{4,2},{6,8},{8,6},{10,12},{12,10},{14,16},{16,14},{18,20},{2... | collective-permute-start | bytes 1572872 | tf_op jit(solution)/shard_map/ppermute | solution.py:30
  84.1 5.7 %copy-start.8 = (f16[128,1024]{1,0:T(8,128)(2,1)S(1)}, f16[128,1024]{1,0:T(8,128)(2,1)}, u32[]{:S(2)}) copy-start(f16[128,1024]{1,0:T(8,128)(2,1)} %get-tuple-element.201) | copy-start | bytes 786436
  84.2 5.4 %collective-permute-start.19 = (f16[256,1024]{1,0:T(8,128)(2,1)S(1)}, f16[256,1024]{1,0:T(8,128)(2,1)S(1)}, u32[]{:S(2)}, u32[]{:S(2)}) collective-permute-start(f16[256,1024]{1,0:T(8,128)(2,1)S(1)} %multiply_convert_fusion.3), channel_id=1, source_target_pairs={{0,2},{2,0},{4,6},{6,4},{8,10},{10,8},{12,14},{14,12},{16,18},{18,... | collective-permute-start | bytes 1572872 | tf_op jit(solution)/shard_map/ppermute | solution.py:30
  84.2 9.7 %collective-permute-start.20 = (f16[128,1024]{1,0:T(8,128)(2,1)S(1)}, f16[128,1024]{1,0:T(8,128)(2,1)S(1)}, u32[]{:S(2)}, u32[]{:S(2)}) collective-permute-start(f16[128,1024]{1,0:T(8,128)(2,1)S(1)} %copy-done.9), channel_id=1, source_target_pairs={{0,1},{1,0},{2,3},{3,2},{4,5},{5,4},{6,7},{7,6},{8,9},{9,8},{10,11... | collective-permute-start | bytes 786440 | tf_op jit(solution)/shard_map/ppermute | solution.py:21
  85.5 20.6 %collective-permute-start.21 = (f16[256,1024]{1,0:T(8,128)(2,1)S(1)}, f16[256,1024]{1,0:T(8,128)(2,1)S(1)}, u32[]{:S(2)}, u32[]{:S(2)}) collective-permute-start(f16[256,1024]{1,0:T(8,128)(2,1)S(1)} %multiply_convert_fusion.3), channel_id=1, source_target_pairs={{2,4},{4,2},{6,8},{8,6},{10,12},{12,10},{14,16},{16,14},{18,20},{2... | collective-permute-start | bytes 1572872 | tf_op jit(solution)/shard_map/ppermute | solution.py:30
  86.6 21.5 %copy-start.5 = (f16[256,1024]{1,0:T(8,128)(2,1)S(1)}, f16[256,1024]{1,0:T(8,128)(2,1)}, u32[]{:S(2)}) copy-start(f16[256,1024]{1,0:T(8,128)(2,1)} %copy-done.4) | copy-start | bytes 1572868
  89.8 18.1 %collective-permute-start.22 = (f16[256,1024]{1,0:T(8,128)(2,1)S(1)}, f16[256,1024]{1,0:T(8,128)(2,1)S(1)}, u32[]{:S(2)}, u32[]{:S(2)}) collective-permute-start(f16[256,1024]{1,0:T(8,128)(2,1)S(1)} %multiply_convert_fusion.2), channel_id=1, source_target_pairs={{0,2},{2,0},{4,6},{6,4},{8,10},{10,8},{12,14},{14,12},{16,18},{18,... | collective-permute-start | bytes 1572872 | tf_op jit(solution)/shard_map/ppermute | solution.py:30
  89.9 23.5 %collective-permute-start.24 = (f16[128,1024]{1,0:T(8,128)(2,1)S(1)}, f16[128,1024]{1,0:T(8,128)(2,1)S(1)}, u32[]{:S(2)}, u32[]{:S(2)}) collective-permute-start(f16[128,1024]{1,0:T(8,128)(2,1)S(1)} %copy-done.8), channel_id=1, source_target_pairs={{0,1},{1,0},{2,3},{3,2},{4,5},{5,4},{6,7},{7,6},{8,9},{9,8},{10,11... | collective-permute-start | bytes 786440 | tf_op jit(solution)/shard_map/ppermute | solution.py:21
  91.2 21.8 %collective-permute-start.23 = (f16[256,1024]{1,0:T(8,128)(2,1)S(1)}, f16[256,1024]{1,0:T(8,128)(2,1)S(1)}, u32[]{:S(2)}, u32[]{:S(2)}) collective-permute-start(f16[256,1024]{1,0:T(8,128)(2,1)S(1)} %multiply_convert_fusion.2), channel_id=1, source_target_pairs={{2,4},{4,2},{6,8},{8,6},{10,12},{12,10},{14,16},{16,14},{18,20},{2... | collective-permute-start | bytes 1572872 | tf_op jit(solution)/shard_map/ppermute | solution.py:30
  108.0 5.5 %collective-permute-start.25 = (f16[128,1024]{1,0:T(8,128)(2,1)S(1)}, f16[128,1024]{1,0:T(8,128)(2,1)S(1)}, u32[]{:S(2)}, u32[]{:S(2)}) collective-permute-start(f16[128,1024]{1,0:T(8,128)(2,1)S(1)} %multiply_convert_fusion.10), channel_id=1, source_target_pairs={{0,2},{2,0},{4,6},{6,4},{8,10},{10,8},{12,14},{14,12},{16,18},{18,... | collective-permute-start | bytes 786440 | tf_op jit(solution)/shard_map/ppermute | solution.py:30
  108.1 9.3 %collective-permute-start.26 = (f16[128,1024]{1,0:T(8,128)(2,1)S(1)}, f16[128,1024]{1,0:T(8,128)(2,1)S(1)}, u32[]{:S(2)}, u32[]{:S(2)}) collective-permute-start(f16[128,1024]{1,0:T(8,128)(2,1)S(1)} %multiply_convert_fusion.10), channel_id=1, source_target_pairs={{2,4},{4,2},{6,8},{8,6},{10,12},{12,10},{14,16},{16,14},{18,20},{2... | collective-permute-start | bytes 786440 | tf_op jit(solution)/shard_map/ppermute | solution.py:30
  113.5 3.9 %copy-start.3 = (f32[1,2048,1024]{2,1,0:T(8,128)}, f32[1,2048,1024]{2,1,0:T(8,128)S(1)}, u32[]{:S(2)}) copy-start(f32[1,2048,1024]{2,1,0:T(8,128)S(1)} %bitcast_dynamic-update-slice_fusion.6) | copy-start | bytes 25165828

commit v17 on v16

--- a/solution.py
+++ b/solution.py
@@ -54,7 +54,7 @@
     main = rows - first
     cuts = list(range(0, main, STEP)) + [main]
     chunks = len(cuts) - 1
-    middle = min(1, chunks - 1)
+    middle = min(3, chunks - 1)
 
     def owner(away, shard=shard):
         other = shard + away
@@ -127,7 +127,7 @@
         arrived[chunk], near[chunk - 1] = lax.optimization_barrier((arrived[chunk], near[chunk - 1]))
         if mixed:
             arrived[chunk], out = lax.optimization_barrier((arrived[chunk], out))
-        if chunk == 3:
+        if chunk == middle + 2:
             arrived[chunk], parts = lax.optimization_barrier((arrived[chunk], parts))
         sent = (u_of(chunk) * scale).astype(WIRE)
         sent, base, out, later = lax.optimization_barrier((sent, base, out, shard))

time: 121 us -> 121 us (level)
  other arithmetic: 23.4 us -> 25 us
    ppermute x18, starting transfers between devices: 21.6 us -> 18.4 us  [swapped(): return lax.ppermute(value, axis, pairs)]
    ppermute x18, waiting for transfers between devices: 29 us -> 25.9 us  [swapped(): return lax.ppermute(value, axis, pairs)]
    ppermute x9, starting transfers between devices: 7.74 us -> 9.93 us  [from_behind(): return lax.ppermute(value, axis, pairs)]
    ppermute x9, waiting for transfers between devices: 6.95 us -> 9.07 us  [from_behind(): return lax.ppermute(value, axis, pairs)]
    dynamic_update_slice x8, other arithmetic: 9.79 us -> 11.2 us  [mix_into(): return lax.dynamic_update_slice_in_dim(out, value, cuts[chunk], axis=0)]
    unnamed x22 -> x18, local copies, waits for them, and re-layouts: 3.01 us -> 4.09 us
  transfers between devices with their start and end apart: 27 -> 27, of which waited for: 10 -> 12; matrix products, arithmetic and copies ran while one was open for 37% -> 38% of each run, Pallas kernels for 0% -> 0%
where the time goes in v17:
time: 121 us; the launch traced here: 119 us
  waiting for transfers between devices  35 us (29%)
  starting transfers between devices  28.4 us (23%)
  other arithmetic  25 us (21%)
  matrix products  21.3 us (18%)
  local copies, waits for them, and re-layouts  9 us (7%)
    ppermute x18, waiting for transfers between devices, swapped(): return lax.ppermute(value, axis, pairs)  25.9 us
    dot_general x6, matrix products, partial(): lax.dot_general(block, cot_local, (((0,), (0,)), ((), ())), preferred_ele...  21.3 us
    ppermute x18, starting transfers between devices, swapped(): return lax.ppermute(value, axis, pairs)  18.4 us
    dynamic_update_slice x8, other arithmetic, mix_into(): return lax.dynamic_update_slice_in_dim(out, value, cuts[chunk], axis=0)  11.2 us
    convert_element_type x8, other arithmetic, on_device(): sent = (u_of(chunk) * scale).astype(WIRE)  10.8 us
    ppermute x9, starting transfers between devices, from_behind(): return lax.ppermute(value, axis, pairs)  9.93 us
    ppermute x9, waiting for transfers between devices, from_behind(): return lax.ppermute(value, axis, pairs)  9.07 us
    unnamed x18, local copies, waits for them, and re-layouts  4.09 us
  transfers between devices with their start and end apart: 27, of which 12 were waited for; matrix products, arithmetic and copies ran while one was open for 38% of the time, Pallas kernels for 0%

profile of v17, /device:TPU:1, one launch (start us, length us, event | category | flops | bytes accessed | tf_op | source)
XLA Modules:
  0.0 118.9 jit_solution(948957796173366088)
XLA Ops:
  0.0 1.5 %copy-done = bf16[1,896,1024]{2,1,0:T(8,128)(2,1)S(1)} copy-done((bf16[1,896,1024]{2,1,0:T(8,128)(2,1)S(1)}, bf16[1,896,1024]{2,1,0:T(8,128)(2,1)}, u32[]{:S(2)}) %copy-start) | copy-done | bytes 1835032
  1.5 3.2 %multiply_convert_fusion.1 = f16[768,1024]{1,0:T(8,128)(2,1)S(1)} fusion(bf16[1,896,1024]{2,1,0:T(8,128)(2,1)S(1)} %copy-done, bf16[1,896,4096]{2,1,0:T(8,128)(2,1)} %param.5, s32[]{:T(128)S(6)} %select_n.46), kind=kOutput, calls=%fused_computation.3 | convolution fusion | flops 1410859008 | bytes 4784132 | tf_op jit(solution)/shard_map/dot_general | solution.py:65
  4.7 1.3 %fusion.38 = (f16[256,1024]{1,0:T(8,128)(2,1)}, f16[256,1024]{1,0:T(8,128)(2,1)}, f16[256,1024]{1,0:T(8,128)(2,1)}) fusion(f16[768,1024]{1,0:T(8,128)(2,1)S(1)} %multiply_convert_fusion.1), kind=kLoop, calls=%fused_computation.69 | loop fusion | bytes 3145728 | tf_op jit(solution)/shard_map/slice | solution.py:106
  6.0 2.1 %collective-permute-start = (f16[256,1024]{1,0:T(8,128)(2,1)}, f16[256,1024]{1,0:T(8,128)(2,1)}, u32[]{:S(2)}, u32[]{:S(2)}) collective-permute-start(f16[256,1024]{1,0:T(8,128)(2,1)} %get-tuple-element.104), channel_id=1, source_target_pairs={{0,1},{1,0},{2,3},{3,2},{4,5},{5,4},{6,7},{7,6},{8,9},{9,8},{10,11... | collective-permute-start | bytes 1572872 | tf_op jit(solution)/shard_map/ppermute | solution.py:21
  8.1 1.4 %fusion.19 = f32[128,1024]{1,0:T(8,128)S(1)} fusion(bf16[1,896,1024]{2,1,0:T(8,128)(2,1)S(1)} %copy-done, bf16[1,896,4096]{2,1,0:T(8,128)(2,1)} %param.5, s32[]{:T(128)S(6)} %select_n.50), kind=kOutput, calls=%fused_computation.21 | convolution fusion | flops 235012096 | bytes 2588676 | tf_op jit(solution)/shard_map/dot_general | solution.py:65
  9.5 1.7 %fusion.22 = f32[128,1024]{1,0:T(8,128)S(1)} fusion(bf16[1,896,1024]{2,1,0:T(8,128)(2,1)S(1)} %copy-done, f32[1,2048,1024]{2,1,0:T(8,128)} %param.4, bf16[1,896,4096]{2,1,0:T(8,128)(2,1)} %param.5, s32[]{:T(128)S(6)} %select_n.48), kind=kOutput, calls=%fused_computation.22 | convolution fusion | flops 235143168 | bytes 3112964 | tf_op jit(solution)/shard_map/dot_general | solution.py:65
  11.2 1.0 multiply_convert_fusion.9
  12.2 1.0 collective-permute-start.1
  13.1 1.1 collective-permute-start.5
  14.2 0.2 collective-permute-start.4
  14.4 1.2 %collective-permute-start.6 = (f16[256,1024]{1,0:T(8,128)(2,1)}, f16[256,1024]{1,0:T(8,128)(2,1)S(1)}, u32[]{:S(2)}, u32[]{:S(2)}) collective-permute-start(f16[256,1024]{1,0:T(8,128)(2,1)} %get-tuple-element.207), channel_id=1, source_target_pairs={{0,1},{1,0},{2,3},{3,2},{4,5},{5,4},{6,7},{7,6},{8,9},{9,8},{10,11... | collective-permute-start | bytes 1572872 | tf_op jit(solution)/shard_map/ppermute | solution.py:21
  15.7 4.2 %bitcast_subtract_fusion.1 = f32[768,1024]{1,0:T(8,128)S(1)} fusion(f32[1,2048,1024]{2,1,0:T(8,128)} %param.4, bf16[1,896,1024]{2,1,0:T(8,128)(2,1)S(1)} %copy-done, bf16[1,896,4096]{2,1,0:T(8,128)(2,1)} %param.5, s32[]{:T(128)S(6)} %select_n.47), kind=kOutput, calls=%fused_computation.2 | convolution fusion | flops 1410859008 | bytes 9502724 | tf_op jit(solution)/shard_map/dot_general | solution.py:65
  19.9 0.2 collective-permute-done
  20.0 1.4 %copy-done.3 = f32[768,1024]{1,0:T(8,128)} copy-done((f32[768,1024]{1,0:T(8,128)}, f32[768,1024]{1,0:T(8,128)S(1)}, u32[]{:S(2)}) %copy-start.3) | copy-done | bytes 3145752
  21.5 2.0 %multiply_convert_fusion.8 = f16[256,1024]{1,0:T(8,128)(2,1)} fusion(f16[256,1024]{1,0:T(8,128)(2,1)} %collective-permute-done, f32[768,1024]{1,0:T(8,128)S(1)} %bitcast_subtract_fusion.1), kind=kLoop, calls=%fused_computation.44 | loop fusion | flops 1310720 | bytes 2097152 | tf_op jit(solution)/shard_map/convert_element_type | solution.py:132
  23.5 4.1 %collective-permute-start.2 = (f16[256,1024]{1,0:T(8,128)(2,1)}, f16[256,1024]{1,0:T(8,128)(2,1)}, u32[]{:S(2)}, u32[]{:S(2)}) collective-permute-start(f16[256,1024]{1,0:T(8,128)(2,1)} %multiply_convert_fusion.8), channel_id=1, source_target_pairs={{0,2},{2,0},{4,6},{6,4},{8,10},{10,8},{12,14},{14,12},{16,18},{18,... | collective-permute-start | bytes 1572872 | tf_op jit(solution)/shard_map/ppermute | solution.py:30
  27.6 4.8 %multiply_convert_fusion = f16[1280,1024]{1,0:T(8,128)(2,1)S(1)} fusion(bf16[1,896,4096]{2,1,0:T(8,128)(2,1)} %param.5, s32[]{:T(128)S(6)} %select_n.52, bf16[1,896,1024]{2,1,0:T(8,128)(2,1)S(1)} %copy-done), kind=kOutput, calls=%fused_computation.1 | convolution fusion | flops 2351431680 | bytes 6750212 | tf_op jit(solution)/shard_map/dot_general | solution.py:65
  32.4 0.7 slice.171
  33.2 1.7 %fusion.37 = (f16[256,1024]{1,0:T(8,128)(2,1)}, f16[256,1024]{1,0:T(8,128)(2,1)}, f16[256,1024]{1,0:T(8,128)(2,1)}, f16[256,1024]{1,0:T(8,128)(2,1)}) fusion(f16[1280,1024]{1,0:T(8,128)(2,1)S(1)} %multiply_convert_fusion), kind=kLoop, calls=%fused_computation.68 | loop fusion | bytes 4194304 | tf_op jit(solution)/shard_map/slice | solution.py:141
  34.9 2.1 %multiply_convert_fusion.7 = f16[256,1024]{1,0:T(8,128)(2,1)} fusion(f16[256,1024]{1,0:T(8,128)(2,1)} %collective-permute-done.4, f32[768,1024]{1,0:T(8,128)S(1)} %copy-done.4), kind=kLoop, calls=%fused_computation.42 | loop fusion | flops 1310720 | bytes 2097152 | tf_op jit(solution)/shard_map/convert_element_type | solution.py:132
  37.0 1.7 %collective-permute-start.8 = (f16[256,1024]{1,0:T(8,128)(2,1)}, f16[256,1024]{1,0:T(8,128)(2,1)}, u32[]{:S(2)}, u32[]{:S(2)}) collective-permute-start(f16[256,1024]{1,0:T(8,128)(2,1)} %multiply_convert_fusion.7), channel_id=1, source_target_pairs={{0,2},{2,0},{4,6},{6,4},{8,10},{10,8},{12,14},{14,12},{16,18},{18,... | collective-permute-start | bytes 1572872 | tf_op jit(solution)/shard_map/ppermute | solution.py:30
  38.7 1.2 %collective-permute-start.3 = (f16[256,1024]{1,0:T(8,128)(2,1)}, f16[256,1024]{1,0:T(8,128)(2,1)}, u32[]{:S(2)}, u32[]{:S(2)}) collective-permute-start(f16[256,1024]{1,0:T(8,128)(2,1)} %get-tuple-element.112), channel_id=1, source_target_pairs={{0,1},{1,0},{2,3},{3,2},{4,5},{5,4},{6,7},{7,6},{8,9},{9,8},{10,11... | collective-permute-start | bytes 1572872 | tf_op jit(solution)/shard_map/ppermute | solution.py:21
  39.9 2.5 %collective-permute-done.6 = f16[256,1024]{1,0:T(8,128)(2,1)S(1)} collective-permute-done((f16[256,1024]{1,0:T(8,128)(2,1)}, f16[256,1024]{1,0:T(8,128)(2,1)S(1)}, u32[]{:S(2)}, u32[]{:S(2)}) %collective-permute-start.6) | collective-permute-done | bytes 524320 | tf_op jit(solution)/shard_map/ppermute | solution.py:21
  42.4 1.1 collective-permute-start.11
  43.6 1.0 multiply_convert_fusion.6
  44.6 3.0 %collective-permute-start.10 = (f16[256,1024]{1,0:T(8,128)(2,1)}, f16[256,1024]{1,0:T(8,128)(2,1)}, u32[]{:S(2)}, u32[]{:S(2)}) collective-permute-start(f16[256,1024]{1,0:T(8,128)(2,1)} %multiply_convert_fusion.6), channel_id=1, source_target_pairs={{0,2},{2,0},{4,6},{6,4},{8,10},{10,8},{12,14},{14,12},{16,18},{18,... | collective-permute-start | bytes 1572872 | tf_op jit(solution)/shard_map/ppermute | solution.py:30
  47.6 1.1 collective-permute-start.12
  48.7 6.1 %bitcast_subtract_fusion = f32[1280,1024]{1,0:T(8,128)S(1)} fusion(f32[1,2048,1024]{2,1,0:T(8,128)} %param.4, bf16[1,896,4096]{2,1,0:T(8,128)(2,1)} %param.5, s32[]{:T(128)S(6)} %select_n.53, bf16[1,896,1024]{2,1,0:T(8,128)(2,1)S(1)} %copy-done), kind=kOutput, calls=%fused_computation | convolution fusion | flops 2351431680 | bytes 14614532 | tf_op jit(solution)/shard_map/dot_general | solution.py:65
  54.8 5.5 %collective-permute-done.9 = f16[256,1024]{1,0:T(8,128)(2,1)} collective-permute-done((f16[256,1024]{1,0:T(8,128)(2,1)}, f16[256,1024]{1,0:T(8,128)(2,1)}, u32[]{:S(2)}, u32[]{:S(2)}) %collective-permute-start.9) | collective-permute-done | bytes 524320 | tf_op jit(solution)/shard_map/ppermute | solution.py:30
  60.4 2.0 %multiply_convert_fusion.5 = f16[256,1024]{1,0:T(8,128)(2,1)} fusion(f16[256,1024]{1,0:T(8,128)(2,1)} %collective-permute-done.3, f32[1280,1024]{1,0:T(8,128)S(1)} %bitcast_subtract_fusion), kind=kLoop, calls=%fused_computation.38 | loop fusion | flops 1310720 | bytes 2097152 | tf_op jit(solution)/shard_map/convert_element_type | solution.py:132
  62.4 0.4 collective-permute-start.13
  62.8 0.2 collective-permute-start.14
  63.0 2.0 %collective-permute-done.11 = f16[256,1024]{1,0:T(8,128)(2,1)} collective-permute-done((f16[256,1024]{1,0:T(8,128)(2,1)}, f16[256,1024]{1,0:T(8,128)(2,1)}, u32[]{:S(2)}, u32[]{:S(2)}) %collective-permute-start.11) | collective-permute-done | bytes 524320 | tf_op jit(solution)/shard_map/ppermute | solution.py:21
  65.0 0.8 collective-permute-done.12
  65.9 0.2 multiply_reduce_fusion
  66.2 0.4 collective-permute-start.17
  66.6 1.9 %multiply_convert_fusion.4 = f16[256,1024]{1,0:T(8,128)(2,1)S(1)} fusion(f16[256,1024]{1,0:T(8,128)(2,1)} %collective-permute-done.11, f32[1280,1024]{1,0:T(8,128)} %copy-done.1), kind=kLoop, calls=%fused_computation.36 | loop fusion | flops 1310720 | bytes 2097152 | tf_op jit(solution)/shard_map/convert_element_type | solution.py:132
  68.5 2.6 %collective-permute-start.16 = (f16[256,1024]{1,0:T(8,128)(2,1)S(1)}, f16[256,1024]{1,0:T(8,128)(2,1)S(1)}, u32[]{:S(2)}, u32[]{:S(2)}) collective-permute-start(f16[256,1024]{1,0:T(8,128)(2,1)S(1)} %multiply_convert_fusion.4), channel_id=1, source_target_pairs={{0,2},{2,0},{4,6},{6,4},{8,10},{10,8},{12,14},{14,12},{16,18},{18,... | collective-permute-start | bytes 1572872 | tf_op jit(solution)/shard_map/ppermute | solution.py:30
  71.2 1.5 %multiply_add_fusion = f32[256,1024]{1,0:T(8,128)S(1)} fusion(f16[256,1024]{1,0:T(8,128)(2,1)} %collective-permute-done.5, f32[256,1024]{1,0:T(8,128)S(1)} %get-tuple-element.160, f16[256,1024]{1,0:T(8,128)(2,1)} %collective-permute-done.1, f32[1024]{0:T(1024)S(1)} %bitcast.71, f32[1024]{0:T(1024)S(1)} %bitcast.80, f32[1024]{0:T(1024)S(1)} %bitcast.62), kind=kLoop, calls=%fused_computation.35 | loop fusion | flops 1835008 | bytes 3158016 | tf_op jit(solution)/shard_map/add | solution.py:90
  72.7 1.2 collective-permute-start.18
  73.9 2.6 %collective-permute-done.14 = f16[256,1024]{1,0:T(8,128)(2,1)} collective-permute-done((f16[256,1024]{1,0:T(8,128)(2,1)}, f16[256,1024]{1,0:T(8,128)(2,1)}, u32[]{:S(2)}, u32[]{:S(2)}) %collective-permute-start.14) | collective-permute-done | bytes 524320 | tf_op jit(solution)/shard_map/ppermute | solution.py:21
  76.5 1.2 %collective-permute-done.15 = f16[256,1024]{1,0:T(8,128)(2,1)} collective-permute-done((f16[256,1024]{1,0:T(8,128)(2,1)}, f16[256,1024]{1,0:T(8,128)(2,1)}, u32[]{:S(2)}, u32[]{:S(2)}) %collective-permute-start.15) | collective-permute-done | bytes 524320 | tf_op jit(solution)/shard_map/ppermute | solution.py:30
  77.7 1.4 %multiply_convert_fusion.3 = f16[256,1024]{1,0:T(8,128)(2,1)S(1)} fusion(f16[256,1024]{1,0:T(8,128)(2,1)} %collective-permute-done.14, f32[1280,1024]{1,0:T(8,128)S(1)} %copy-done.2), kind=kLoop, calls=%fused_computation.33 | loop fusion | flops 1310720 | bytes 2097152 | tf_op jit(solution)/shard_map/convert_element_type | solution.py:132
  79.1 0.3 collective-permute-start.19
  79.5 2.1 %collective-permute-start.20 = (f16[128,1024]{1,0:T(8,128)(2,1)S(1)}, f16[128,1024]{1,0:T(8,128)(2,1)S(1)}, u32[]{:S(2)}, u32[]{:S(2)}) collective-permute-start(f16[128,1024]{1,0:T(8,128)(2,1)S(1)} %copy-done.7), channel_id=1, source_target_pairs={{0,1},{1,0},{2,3},{3,2},{4,5},{5,4},{6,7},{7,6},{8,9},{9,8},{10,11... | collective-permute-start | bytes 786440 | tf_op jit(solution)/shard_map/ppermute | solution.py:21
  81.6 1.4 %collective-permute-start.21 = (f16[256,1024]{1,0:T(8,128)(2,1)S(1)}, f16[256,1024]{1,0:T(8,128)(2,1)S(1)}, u32[]{:S(2)}, u32[]{:S(2)}) collective-permute-start(f16[256,1024]{1,0:T(8,128)(2,1)S(1)} %multiply_convert_fusion.3), channel_id=1, source_target_pairs={{2,4},{4,2},{6,8},{8,6},{10,12},{12,10},{14,16},{16,14},{18,20},{2... | collective-permute-start | bytes 1572872 | tf_op jit(solution)/shard_map/ppermute | solution.py:30
  83.0 1.1 broadcast_in_dim.25
  84.1 1.8 %add_dynamic-update-slice_fusion.1 = f32[2048,1024]{1,0:T(8,128)S(1)} fusion(f32[2048,1024]{1,0:T(8,128)S(1)} %broadcast_in_dim.25, f16[256,1024]{1,0:T(8,128)(2,1)} %collective-permute-done.7, f32[768,1024]{1,0:T(8,128)S(1)} %copy-done.5, f16[256,1024]{1,0:T(8,128)(2,1)} %collective-permute-done.2, f16[256,1024]{1,0:T(8,128)(2,1)} %collective-permute-done, ...), kind=kLoop, calls=%fused_computation.32 | loop fusion | flops 2621440 | bytes 3682304 | tf_op jit(solution)/shard_map/dynamic_update_slice | solution.py:97
  85.9 1.8 %collective-permute-done.17 = f16[256,1024]{1,0:T(8,128)(2,1)S(1)} collective-permute-done((f16[256,1024]{1,0:T(8,128)(2,1)}, f16[256,1024]{1,0:T(8,128)(2,1)S(1)}, u32[]{:S(2)}, u32[]{:S(2)}) %collective-permute-start.17) | collective-permute-done | bytes 524320 | tf_op jit(solution)/shard_map/ppermute | solution.py:21
  87.6 6.6 %collective-permute-done.18 = f16[256,1024]{1,0:T(8,128)(2,1)S(1)} collective-permute-done((f16[256,1024]{1,0:T(8,128)(2,1)S(1)}, f16[256,1024]{1,0:T(8,128)(2,1)S(1)}, u32[]{:S(2)}, u32[]{:S(2)}) %collective-permute-start.18) | collective-permute-done | bytes 524320 | tf_op jit(solution)/shard_map/ppermute | solution.py:30
  94.3 0.2 multiply_convert_fusion.2
  94.6 1.3 %collective-permute-start.24 = (f16[128,1024]{1,0:T(8,128)(2,1)S(1)}, f16[128,1024]{1,0:T(8,128)(2,1)S(1)}, u32[]{:S(2)}, u32[]{:S(2)}) collective-permute-start(f16[128,1024]{1,0:T(8,128)(2,1)S(1)} %get-tuple-element.201), channel_id=1, source_target_pairs={{0,1},{1,0},{2,3},{3,2},{4,5},{5,4},{6,7},{7,6},{8,9},{9,8},{10,11... | collective-permute-start | bytes 786440 | tf_op jit(solution)/shard_map/ppermute | solution.py:21
  95.9 0.3 collective-permute-start.23
  96.2 4.0 %collective-permute-done.21 = f16[256,1024]{1,0:T(8,128)(2,1)S(1)} collective-permute-done((f16[256,1024]{1,0:T(8,128)(2,1)S(1)}, f16[256,1024]{1,0:T(8,128)(2,1)S(1)}, u32[]{:S(2)}, u32[]{:S(2)}) %collective-permute-start.21) | collective-permute-done | bytes 524320 | tf_op jit(solution)/shard_map/ppermute | solution.py:30
  100.2 1.8 %add_dynamic-update-slice_fusion = f32[2048,1024]{1,0:T(8,128)S(1)} fusion(f32[2048,1024]{1,0:T(8,128)S(1)} %add_dynamic-update-slice_fusion.1, f16[256,1024]{1,0:T(8,128)(2,1)} %collective-permute-done.9, f32[768,1024]{1,0:T(8,128)S(1)} %copy-done.5, f16[256,1024]{1,0:T(8,128)(2,1)} %collective-permute-done.8, f16[256,1024]{1,0:T(8,128)(2,1)} %collective-permute-done.4, ...), kind=kLoop, calls=%fused_computation.29 | loop fusion | flops 2621440 | bytes 3682304 | tf_op jit(solution)/shard_map/dynamic_update_slice | solution.py:97
  102.2 1.6 %bitcast_dynamic-update-slice_fusion.4 = f32[1,2048,1024]{2,1,0:T(8,128)S(1)} fusion(f32[1,2048,1024]{2,1,0:T(8,128)S(1)} %bitcast.61, f16[256,1024]{1,0:T(8,128)(2,1)} %collective-permute-done.12, f32[768,1024]{1,0:T(8,128)S(1)} %copy-done.5, f16[256,1024]{1,0:T(8,128)(2,1)} %collective-permute-done.10, f16[256,1024]{1,0:T(8,128)(2,1)S(1)} %collective-permute-done.6, ...), kind=kLoop, calls=%fused_computation.28 | loop fusion | flops 2621440 | bytes 3682304 | tf_op jit(solution)/shard_map/dynamic_update_slice | solution.py:97
  103.9 1.8 %bitcast_dynamic-update-slice_fusion.3 = f32[1,2048,1024]{2,1,0:T(8,128)S(1)} fusion(f32[1,2048,1024]{2,1,0:T(8,128)S(1)} %bitcast_dynamic-update-slice_fusion.4, f16[256,1024]{1,0:T(8,128)(2,1)} %collective-permute-done.15, f32[1280,1024]{1,0:T(8,128)S(1)} %copy-done.2, f16[256,1024]{1,0:T(8,128)(2,1)} %collective-permute-done.13, ...), kind=kLoop, calls=%fused_computation.27 | loop fusion | flops 2621440 | bytes 3682304 | tf_op jit(solution)/shard_map/dynamic_update_slice | solution.py:97
  105.6 1.5 %bitcast_dynamic-update-slice_fusion.2 = f32[1,2048,1024]{2,1,0:T(8,128)S(1)} fusion(f32[1,2048,1024]{2,1,0:T(8,128)S(1)} %bitcast_dynamic-update-slice_fusion.3, f16[256,1024]{1,0:T(8,128)(2,1)S(1)} %collective-permute-done.18, f32[1280,1024]{1,0:T(8,128)S(1)} %copy-done.2, f16[256,1024]{1,0:T(8,128)(2,1)S(1)} %collective-permute-done.16, ...), kind=kLoop, calls=%fused_computation.26 | loop fusion | flops 2621440 | bytes 3682304 | tf_op jit(solution)/shard_map/dynamic_update_slice | solution.py:97
  107.1 1.5 %bitcast_dynamic-update-slice_fusion.1 = f32[1,2048,1024]{2,1,0:T(8,128)S(1)} fusion(f32[1,2048,1024]{2,1,0:T(8,128)S(1)} %bitcast_dynamic-update-slice_fusion.2, f16[256,1024]{1,0:T(8,128)(2,1)S(1)} %collective-permute-done.21, f32[1280,1024]{1,0:T(8,128)S(1)} %copy-done.2, f16[256,1024]{1,0:T(8,128)(2,1)S(1)} %collective-permute-done.19, ...), kind=kLoop, calls=%fused_computation.25 | loop fusion | flops 2621440 | bytes 3682304 | tf_op jit(solution)/shard_map/dynamic_update_slice | solution.py:97
  108.5 5.4 %collective-permute-done.23 = f16[256,1024]{1,0:T(8,128)(2,1)S(1)} collective-permute-done((f16[256,1024]{1,0:T(8,128)(2,1)S(1)}, f16[256,1024]{1,0:T(8,128)(2,1)S(1)}, u32[]{:S(2)}, u32[]{:S(2)}) %collective-permute-start.23) | collective-permute-done | bytes 524320 | tf_op jit(solution)/shard_map/ppermute | solution.py:30
  113.9 0.4 bitcast_dynamic-update-slice_fusion
  114.5 2.3 %collective-permute-done.26 = f16[128,1024]{1,0:T(8,128)(2,1)S(1)} collective-permute-done((f16[128,1024]{1,0:T(8,128)(2,1)S(1)}, f16[128,1024]{1,0:T(8,128)(2,1)S(1)}, u32[]{:S(2)}, u32[]{:S(2)}) %collective-permute-start.26) | collective-permute-done | bytes 262176 | tf_op jit(solution)/shard_map/ppermute | solution.py:30
  116.8 1.1 copy-done.6
  117.9 1.0 bitcast_dynamic-update-slice_fusion.5
  (43 shorter events, 0.8 us)
Async XLA Ops:
  0.0 1.5 %copy-start = (bf16[1,896,1024]{2,1,0:T(8,128)(2,1)S(1)}, bf16[1,896,1024]{2,1,0:T(8,128)(2,1)}, u32[]{:S(2)}) copy-start(bf16[1,896,1024]{2,1,0:T(8,128)(2,1)} %param.6) | copy-start | bytes 5505028
  6.0 14.0 %collective-permute-start = (f16[256,1024]{1,0:T(8,128)(2,1)}, f16[256,1024]{1,0:T(8,128)(2,1)}, u32[]{:S(2)}, u32[]{:S(2)}) collective-permute-start(f16[256,1024]{1,0:T(8,128)(2,1)} %get-tuple-element.104), channel_id=1, source_target_pairs={{0,1},{1,0},{2,3},{3,2},{4,5},{5,4},{6,7},{7,6},{8,9},{9,8},{10,11... | collective-permute-start | bytes 1572872 | tf_op jit(solution)/shard_map/ppermute | solution.py:21
  12.2 7.9 %collective-permute-start.1 = (f16[256,1024]{1,0:T(8,128)(2,1)}, f16[256,1024]{1,0:T(8,128)(2,1)}, u32[]{:S(2)}, u32[]{:S(2)}) collective-permute-start(f16[256,1024]{1,0:T(8,128)(2,1)} %get-tuple-element.108), channel_id=1, source_target_pairs={{0,2},{2,0},{4,6},{6,4},{8,10},{10,8},{12,14},{14,12},{16,18},{18,... | collective-permute-start | bytes 1572872 | tf_op jit(solution)/shard_map/ppermute | solution.py:30
  13.1 21.7 %collective-permute-start.5 = (f16[256,1024]{1,0:T(8,128)(2,1)}, f16[256,1024]{1,0:T(8,128)(2,1)}, u32[]{:S(2)}, u32[]{:S(2)}) collective-permute-start(f16[256,1024]{1,0:T(8,128)(2,1)} %get-tuple-element.108), channel_id=1, source_target_pairs={{2,4},{4,2},{6,8},{8,6},{10,12},{12,10},{14,16},{16,14},{18,20},{2... | collective-permute-start | bytes 1572872 | tf_op jit(solution)/shard_map/ppermute | solution.py:30
  14.2 20.6 %collective-permute-start.4 = (f16[256,1024]{1,0:T(8,128)(2,1)}, f16[256,1024]{1,0:T(8,128)(2,1)}, u32[]{:S(2)}, u32[]{:S(2)}) collective-permute-start(f16[256,1024]{1,0:T(8,128)(2,1)} %get-tuple-element.208), channel_id=1, source_target_pairs={{0,1},{1,0},{2,3},{3,2},{4,5},{5,4},{6,7},{7,6},{8,9},{9,8},{10,11... | collective-permute-start | bytes 1572872 | tf_op jit(solution)/shard_map/ppermute | solution.py:21
  14.4 28.0 %collective-permute-start.6 = (f16[256,1024]{1,0:T(8,128)(2,1)}, f16[256,1024]{1,0:T(8,128)(2,1)S(1)}, u32[]{:S(2)}, u32[]{:S(2)}) collective-permute-start(f16[256,1024]{1,0:T(8,128)(2,1)} %get-tuple-element.207), channel_id=1, source_target_pairs={{0,1},{1,0},{2,3},{3,2},{4,5},{5,4},{6,7},{7,6},{8,9},{9,8},{10,11... | collective-permute-start | bytes 1572872 | tf_op jit(solution)/shard_map/ppermute | solution.py:21
  19.8 1.6 %copy-start.3 = (f32[768,1024]{1,0:T(8,128)}, f32[768,1024]{1,0:T(8,128)S(1)}, u32[]{:S(2)}) copy-start(f32[768,1024]{1,0:T(8,128)S(1)} %bitcast_subtract_fusion.1) | copy-start | bytes 9437188
  23.5 11.3 %collective-permute-start.2 = (f16[256,1024]{1,0:T(8,128)(2,1)}, f16[256,1024]{1,0:T(8,128)(2,1)}, u32[]{:S(2)}, u32[]{:S(2)}) collective-permute-start(f16[256,1024]{1,0:T(8,128)(2,1)} %multiply_convert_fusion.8), channel_id=1, source_target_pairs={{0,2},{2,0},{4,6},{6,4},{8,10},{10,8},{12,14},{14,12},{16,18},{18,... | collective-permute-start | bytes 1572872 | tf_op jit(solution)/shard_map/ppermute | solution.py:30
  27.6 14.8 %collective-permute-start.7 = (f16[256,1024]{1,0:T(8,128)(2,1)}, f16[256,1024]{1,0:T(8,128)(2,1)}, u32[]{:S(2)}, u32[]{:S(2)}) collective-permute-start(f16[256,1024]{1,0:T(8,128)(2,1)} %multiply_convert_fusion.8), channel_id=1, source_target_pairs={{2,4},{4,2},{6,8},{8,6},{10,12},{12,10},{14,16},{16,14},{18,20},{2... | collective-permute-start | bytes 1572872 | tf_op jit(solution)/shard_map/ppermute | solution.py:30
  32.4 2.4 %copy-start.4 = (f32[768,1024]{1,0:T(8,128)S(1)}, f32[768,1024]{1,0:T(8,128)}, u32[]{:S(2)}) copy-start(f32[768,1024]{1,0:T(8,128)} %copy-done.3) | copy-start | bytes 9437188
  37.0 6.6 %collective-permute-start.8 = (f16[256,1024]{1,0:T(8,128)(2,1)}, f16[256,1024]{1,0:T(8,128)(2,1)}, u32[]{:S(2)}, u32[]{:S(2)}) collective-permute-start(f16[256,1024]{1,0:T(8,128)(2,1)} %multiply_convert_fusion.7), channel_id=1, source_target_pairs={{0,2},{2,0},{4,6},{6,4},{8,10},{10,8},{12,14},{14,12},{16,18},{18,... | collective-permute-start | bytes 1572872 | tf_op jit(solution)/shard_map/ppermute | solution.py:30
  38.7 16.2 %collective-permute-start.3 = (f16[256,1024]{1,0:T(8,128)(2,1)}, f16[256,1024]{1,0:T(8,128)(2,1)}, u32[]{:S(2)}, u32[]{:S(2)}) collective-permute-start(f16[256,1024]{1,0:T(8,128)(2,1)} %get-tuple-element.112), channel_id=1, source_target_pairs={{0,1},{1,0},{2,3},{3,2},{4,5},{5,4},{6,7},{7,6},{8,9},{9,8},{10,11... | collective-permute-start | bytes 1572872 | tf_op jit(solution)/shard_map/ppermute | solution.py:21
  39.9 20.5 %collective-permute-start.9 = (f16[256,1024]{1,0:T(8,128)(2,1)}, f16[256,1024]{1,0:T(8,128)(2,1)}, u32[]{:S(2)}, u32[]{:S(2)}) collective-permute-start(f16[256,1024]{1,0:T(8,128)(2,1)} %multiply_convert_fusion.7), channel_id=1, source_target_pairs={{2,4},{4,2},{6,8},{8,6},{10,12},{12,10},{14,16},{16,14},{18,20},{2... | collective-permute-start | bytes 1572872 | tf_op jit(solution)/shard_map/ppermute | solution.py:30
  42.4 22.6 %collective-permute-start.11 = (f16[256,1024]{1,0:T(8,128)(2,1)}, f16[256,1024]{1,0:T(8,128)(2,1)}, u32[]{:S(2)}, u32[]{:S(2)}) collective-permute-start(f16[256,1024]{1,0:T(8,128)(2,1)} %get-tuple-element.129), channel_id=1, source_target_pairs={{0,1},{1,0},{2,3},{3,2},{4,5},{5,4},{6,7},{7,6},{8,9},{9,8},{10,11... | collective-permute-start | bytes 1572872 | tf_op jit(solution)/shard_map/ppermute | solution.py:21
  44.6 15.8 %collective-permute-start.10 = (f16[256,1024]{1,0:T(8,128)(2,1)}, f16[256,1024]{1,0:T(8,128)(2,1)}, u32[]{:S(2)}, u32[]{:S(2)}) collective-permute-start(f16[256,1024]{1,0:T(8,128)(2,1)} %multiply_convert_fusion.6), channel_id=1, source_target_pairs={{0,2},{2,0},{4,6},{6,4},{8,10},{10,8},{12,14},{14,12},{16,18},{18,... | collective-permute-start | bytes 1572872 | tf_op jit(solution)/shard_map/ppermute | solution.py:30
  47.6 18.2 %collective-permute-start.12 = (f16[256,1024]{1,0:T(8,128)(2,1)}, f16[256,1024]{1,0:T(8,128)(2,1)}, u32[]{:S(2)}, u32[]{:S(2)}) collective-permute-start(f16[256,1024]{1,0:T(8,128)(2,1)} %multiply_convert_fusion.6), channel_id=1, source_target_pairs={{2,4},{4,2},{6,8},{8,6},{10,12},{12,10},{14,16},{16,14},{18,20},{2... | collective-permute-start | bytes 1572872 | tf_op jit(solution)/shard_map/ppermute | solution.py:30
  48.7 17.1 %copy-start.8 = (s32[16,3]{0,1:T(4,128)S(1)}, s32[16,3]{0,1:T(4,128)}, u32[]{:S(2)}) copy-start(s32[16,3]{0,1:T(4,128)} %param.7) | copy-start | bytes 580
  54.8 5.5 %copy-start.1 = (f32[1280,1024]{1,0:T(8,128)}, f32[1280,1024]{1,0:T(8,128)S(1)}, u32[]{:S(2)}) copy-start(f32[1280,1024]{1,0:T(8,128)S(1)} %bitcast_subtract_fusion) | copy-start | bytes 15728644
  62.4 4.2 %collective-permute-start.13 = (f16[256,1024]{1,0:T(8,128)(2,1)}, f16[256,1024]{1,0:T(8,128)(2,1)}, u32[]{:S(2)}, u32[]{:S(2)}) collective-permute-start(f16[256,1024]{1,0:T(8,128)(2,1)} %multiply_convert_fusion.5), channel_id=1, source_target_pairs={{0,2},{2,0},{4,6},{6,4},{8,10},{10,8},{12,14},{14,12},{16,18},{18,... | collective-permute-start | bytes 1572872 | tf_op jit(solution)/shard_map/ppermute | solution.py:30
  62.8 13.8 %collective-permute-start.14 = (f16[256,1024]{1,0:T(8,128)(2,1)}, f16[256,1024]{1,0:T(8,128)(2,1)}, u32[]{:S(2)}, u32[]{:S(2)}) collective-permute-start(f16[256,1024]{1,0:T(8,128)(2,1)} %get-tuple-element.132), channel_id=1, source_target_pairs={{0,1},{1,0},{2,3},{3,2},{4,5},{5,4},{6,7},{7,6},{8,9},{9,8},{10,11... | collective-permute-start | bytes 1572872 | tf_op jit(solution)/shard_map/ppermute | solution.py:21
  63.0 14.7 %collective-permute-start.15 = (f16[256,1024]{1,0:T(8,128)(2,1)}, f16[256,1024]{1,0:T(8,128)(2,1)}, u32[]{:S(2)}, u32[]{:S(2)}) collective-permute-start(f16[256,1024]{1,0:T(8,128)(2,1)} %multiply_convert_fusion.5), channel_id=1, source_target_pairs={{2,4},{4,2},{6,8},{8,6},{10,12},{12,10},{14,16},{16,14},{18,20},{2... | collective-permute-start | bytes 1572872 | tf_op jit(solution)/shard_map/ppermute | solution.py:30
  65.9 11.8 %copy-start.2 = (f32[1280,1024]{1,0:T(8,128)S(1)}, f32[1280,1024]{1,0:T(8,128)}, u32[]{:S(2)}) copy-start(f32[1280,1024]{1,0:T(8,128)} %copy-done.1) | copy-start | bytes 15728644
  65.9 13.5 %copy-start.7 = (f16[128,1024]{1,0:T(8,128)(2,1)S(1)}, f16[128,1024]{1,0:T(8,128)(2,1)}, u32[]{:S(2)}) copy-start(f16[128,1024]{1,0:T(8,128)(2,1)} %slice.171) | copy-start | bytes 786436
  66.2 21.5 %collective-permute-start.17 = (f16[256,1024]{1,0:T(8,128)(2,1)}, f16[256,1024]{1,0:T(8,128)(2,1)S(1)}, u32[]{:S(2)}, u32[]{:S(2)}) collective-permute-start(f16[256,1024]{1,0:T(8,128)(2,1)} %get-tuple-element.166), channel_id=1, source_target_pairs={{0,1},{1,0},{2,3},{3,2},{4,5},{5,4},{6,7},{7,6},{8,9},{9,8},{10,11... | collective-permute-start | bytes 1572872 | tf_op jit(solution)/shard_map/ppermute | solution.py:21
  68.5 9.2 %collective-permute-start.16 = (f16[256,1024]{1,0:T(8,128)(2,1)S(1)}, f16[256,1024]{1,0:T(8,128)(2,1)S(1)}, u32[]{:S(2)}, u32[]{:S(2)}) collective-permute-start(f16[256,1024]{1,0:T(8,128)(2,1)S(1)} %multiply_convert_fusion.4), channel_id=1, source_target_pairs={{0,2},{2,0},{4,6},{6,4},{8,10},{10,8},{12,14},{14,12},{16,18},{18,... | collective-permute-start | bytes 1572872 | tf_op jit(solution)/shard_map/ppermute | solution.py:30
  72.7 21.5 %collective-permute-start.18 = (f16[256,1024]{1,0:T(8,128)(2,1)S(1)}, f16[256,1024]{1,0:T(8,128)(2,1)S(1)}, u32[]{:S(2)}, u32[]{:S(2)}) collective-permute-start(f16[256,1024]{1,0:T(8,128)(2,1)S(1)} %multiply_convert_fusion.4), channel_id=1, source_target_pairs={{2,4},{4,2},{6,8},{8,6},{10,12},{12,10},{14,16},{16,14},{18,20},{2... | collective-permute-start | bytes 1572872 | tf_op jit(solution)/shard_map/ppermute | solution.py:30
  77.7 6.3 %copy-start.5 = (f32[768,1024]{1,0:T(8,128)S(1)}, f32[768,1024]{1,0:T(8,128)}, u32[]{:S(2)}) copy-start(f32[768,1024]{1,0:T(8,128)} %copy-done.3) | copy-start | bytes 9437188
  79.1 15.2 %collective-permute-start.19 = (f16[256,1024]{1,0:T(8,128)(2,1)S(1)}, f16[256,1024]{1,0:T(8,128)(2,1)S(1)}, u32[]{:S(2)}, u32[]{:S(2)}) collective-permute-start(f16[256,1024]{1,0:T(8,128)(2,1)S(1)} %multiply_convert_fusion.3), channel_id=1, source_target_pairs={{0,2},{2,0},{4,6},{6,4},{8,10},{10,8},{12,14},{14,12},{16,18},{18,... | collective-permute-start | bytes 1572872 | tf_op jit(solution)/shard_map/ppermute | solution.py:30
  79.5 16.7 %collective-permute-start.20 = (f16[128,1024]{1,0:T(8,128)(2,1)S(1)}, f16[128,1024]{1,0:T(8,128)(2,1)S(1)}, u32[]{:S(2)}, u32[]{:S(2)}) collective-permute-start(f16[128,1024]{1,0:T(8,128)(2,1)S(1)} %copy-done.7), channel_id=1, source_target_pairs={{0,1},{1,0},{2,3},{3,2},{4,5},{5,4},{6,7},{7,6},{8,9},{9,8},{10,11... | collective-permute-start | bytes 786440 | tf_op jit(solution)/shard_map/ppermute | solution.py:21
  81.6 18.6 %collective-permute-start.21 = (f16[256,1024]{1,0:T(8,128)(2,1)S(1)}, f16[256,1024]{1,0:T(8,128)(2,1)S(1)}, u32[]{:S(2)}, u32[]{:S(2)}) collective-permute-start(f16[256,1024]{1,0:T(8,128)(2,1)S(1)} %multiply_convert_fusion.3), channel_id=1, source_target_pairs={{2,4},{4,2},{6,8},{8,6},{10,12},{12,10},{14,16},{16,14},{18,20},{2... | collective-permute-start | bytes 1572872 | tf_op jit(solution)/shard_map/ppermute | solution.py:30
  94.5 7.5 %collective-permute-start.22 = (f16[256,1024]{1,0:T(8,128)(2,1)S(1)}, f16[256,1024]{1,0:T(8,128)(2,1)S(1)}, u32[]{:S(2)}, u32[]{:S(2)}) collective-permute-start(f16[256,1024]{1,0:T(8,128)(2,1)S(1)} %multiply_convert_fusion.2), channel_id=1, source_target_pairs={{0,2},{2,0},{4,6},{6,4},{8,10},{10,8},{12,14},{14,12},{16,18},{18,... | collective-permute-start | bytes 1572872 | tf_op jit(solution)/shard_map/ppermute | solution.py:30
  94.6 19.8 %collective-permute-start.24 = (f16[128,1024]{1,0:T(8,128)(2,1)S(1)}, f16[128,1024]{1,0:T(8,128)(2,1)S(1)}, u32[]{:S(2)}, u32[]{:S(2)}) collective-permute-start(f16[128,1024]{1,0:T(8,128)(2,1)S(1)} %get-tuple-element.201), channel_id=1, source_target_pairs={{0,1},{1,0},{2,3},{3,2},{4,5},{5,4},{6,7},{7,6},{8,9},{9,8},{10,11... | collective-permute-start | bytes 786440 | tf_op jit(solution)/shard_map/ppermute | solution.py:21
  95.9 18.1 %collective-permute-start.23 = (f16[256,1024]{1,0:T(8,128)(2,1)S(1)}, f16[256,1024]{1,0:T(8,128)(2,1)S(1)}, u32[]{:S(2)}, u32[]{:S(2)}) collective-permute-start(f16[256,1024]{1,0:T(8,128)(2,1)S(1)} %multiply_convert_fusion.2), channel_id=1, source_target_pairs={{2,4},{4,2},{6,8},{8,6},{10,12},{12,10},{14,16},{16,14},{18,20},{2... | collective-permute-start | bytes 1572872 | tf_op jit(solution)/shard_map/ppermute | solution.py:30
  102.1 12.4 %collective-permute-start.25 = (f16[128,1024]{1,0:T(8,128)(2,1)S(1)}, f16[128,1024]{1,0:T(8,128)(2,1)S(1)}, u32[]{:S(2)}, u32[]{:S(2)}) collective-permute-start(f16[128,1024]{1,0:T(8,128)(2,1)S(1)} %multiply_convert_fusion.10), channel_id=1, source_target_pairs={{0,2},{2,0},{4,6},{6,4},{8,10},{10,8},{12,14},{14,12},{16,18},{18,... | collective-permute-start | bytes 786440 | tf_op jit(solution)/shard_map/ppermute | solution.py:30
  102.2 14.6 %collective-permute-start.26 = (f16[128,1024]{1,0:T(8,128)(2,1)S(1)}, f16[128,1024]{1,0:T(8,128)(2,1)S(1)}, u32[]{:S(2)}, u32[]{:S(2)}) collective-permute-start(f16[128,1024]{1,0:T(8,128)(2,1)S(1)} %multiply_convert_fusion.10), channel_id=1, source_target_pairs={{2,4},{4,2},{6,8},{8,6},{10,12},{12,10},{14,16},{16,14},{18,20},{2... | collective-permute-start | bytes 786440 | tf_op jit(solution)/shard_map/ppermute | solution.py:30
  114.5 3.4 %copy-start.6 = (f32[1,2048,1024]{2,1,0:T(8,128)}, f32[1,2048,1024]{2,1,0:T(8,128)S(1)}, u32[]{:S(2)}) copy-start(f32[1,2048,1024]{2,1,0:T(8,128)S(1)} %bitcast_dynamic-update-slice_fusion.6) | copy-start | bytes 25165828

commit v18 on v17

--- a/solution.py
+++ b/solution.py
@@ -12,7 +12,7 @@
 STEP = 256
 FIRST = 128
 AHEAD = 3
-MIXLAG = 5
+MIXLAG = 3
 
 
 def from_behind(value, axis, steps):
@@ -54,7 +54,7 @@
     main = rows - first
     cuts = list(range(0, main, STEP)) + [main]
     chunks = len(cuts) - 1
-    middle = min(3, chunks - 1)
+    middle = min(2, chunks - 1)
 
     def owner(away, shard=shard):
         other = shard + away

time: 121 us -> 120 us (level); the launches traced: 119 us -> 119 us
  other arithmetic: 25 us -> 22.6 us
  matrix products: 21.3 us -> 23 us
  waiting for transfers between devices: 35 us -> 36.6 us
    ppermute x18, waiting for transfers between devices: 25.9 us -> 33 us  [swapped(): return lax.ppermute(value, axis, pairs)]
    ppermute x9, waiting for transfers between devices: 9.07 us -> 3.59 us  [from_behind(): return lax.ppermute(value, axis, pairs)]
    ppermute x18, starting transfers between devices: 18.4 us -> 22.6 us  [swapped(): return lax.ppermute(value, axis, pairs)]
    ppermute x9, starting transfers between devices: 9.93 us -> 5.92 us  [from_behind(): return lax.ppermute(value, axis, pairs)]
    dynamic_update_slice x8 -> x7, other arithmetic: 11.2 us -> 8.35 us  [mix_into(): return lax.dynamic_update_slice_in_dim(out, value, cuts[chunk], axis=0)]
    dot_general x6, matrix products: 21.3 us -> 23 us  [partial(): lax.dot_general(block, cot_local, (((0,), (0,)), ((), ())), preferred_ele...]
    convert_element_type x8, other arithmetic: 10.8 us -> 9.34 us  [on_device(): sent = (u_of(chunk) * scale).astype(WIRE)]
  transfers between devices with their start and end apart: 27 -> 27, of which waited for: 12 -> 10; matrix products, arithmetic and copies ran while one was open for 38% -> 38% of each run, Pallas kernels for 0% -> 0%
where the time goes in v18:
time: 120 us; the launch traced here: 119 us
  waiting for transfers between devices  36.6 us (30%)
  starting transfers between devices  28.5 us (24%)
  matrix products  23 us (19%)
  other arithmetic  22.6 us (19%)
  local copies, waits for them, and re-layouts  8.09 us (7%)
    ppermute x18, waiting for transfers between devices, swapped(): return lax.ppermute(value, axis, pairs)  33 us
    dot_general x6, matrix products, partial(): lax.dot_general(block, cot_local, (((0,), (0,)), ((), ())), preferred_ele...  23 us
    ppermute x18, starting transfers between devices, swapped(): return lax.ppermute(value, axis, pairs)  22.6 us
    convert_element_type x8, other arithmetic, on_device(): sent = (u_of(chunk) * scale).astype(WIRE)  9.34 us
    dynamic_update_slice x7, other arithmetic, mix_into(): return lax.dynamic_update_slice_in_dim(out, value, cuts[chunk], axis=0)  8.35 us
    ppermute x9, starting transfers between devices, from_behind(): return lax.ppermute(value, axis, pairs)  5.92 us
    ppermute x9, waiting for transfers between devices, from_behind(): return lax.ppermute(value, axis, pairs)  3.59 us
    unnamed x18, local copies, waits for them, and re-layouts  3.14 us
  transfers between devices with their start and end apart: 27, of which 10 were waited for; matrix products, arithmetic and copies ran while one was open for 38% of the time, Pallas kernels for 0%

profile of v18, /device:TPU:1, one launch (start us, length us, event | category | flops | bytes accessed | tf_op | source)
XLA Modules:
  0.0 119.1 jit_solution(187465911675996104)
XLA Ops:
  0.0 1.5 %copy-done = bf16[1,896,1024]{2,1,0:T(8,128)(2,1)S(1)} copy-done((bf16[1,896,1024]{2,1,0:T(8,128)(2,1)S(1)}, bf16[1,896,1024]{2,1,0:T(8,128)(2,1)}, u32[]{:S(2)}) %copy-start) | copy-done | bytes 1835032
  1.5 3.2 %multiply_convert_fusion.1 = f16[768,1024]{1,0:T(8,128)(2,1)S(1)} fusion(bf16[1,896,1024]{2,1,0:T(8,128)(2,1)S(1)} %copy-done, bf16[1,896,4096]{2,1,0:T(8,128)(2,1)} %param.5, s32[]{:T(128)S(6)} %select_n.46), kind=kOutput, calls=%fused_computation.3 | convolution fusion | flops 1410859008 | bytes 4784132 | tf_op jit(solution)/shard_map/dot_general | solution.py:65
  4.7 1.3 %fusion.38 = (f16[256,1024]{1,0:T(8,128)(2,1)}, f16[256,1024]{1,0:T(8,128)(2,1)}, f16[256,1024]{1,0:T(8,128)(2,1)}) fusion(f16[768,1024]{1,0:T(8,128)(2,1)S(1)} %multiply_convert_fusion.1), kind=kLoop, calls=%fused_computation.69 | loop fusion | bytes 3145728 | tf_op jit(solution)/shard_map/slice | solution.py:106
  6.0 2.1 %collective-permute-start = (f16[256,1024]{1,0:T(8,128)(2,1)}, f16[256,1024]{1,0:T(8,128)(2,1)S(1)}, u32[]{:S(2)}, u32[]{:S(2)}) collective-permute-start(f16[256,1024]{1,0:T(8,128)(2,1)} %get-tuple-element.106), channel_id=1, source_target_pairs={{0,1},{1,0},{2,3},{3,2},{4,5},{5,4},{6,7},{7,6},{8,9},{9,8},{10,11... | collective-permute-start | bytes 1572872 | tf_op jit(solution)/shard_map/ppermute | solution.py:21
  8.1 2.2 %fusion.19 = f32[128,1024]{1,0:T(8,128)} fusion(bf16[1,896,1024]{2,1,0:T(8,128)(2,1)S(1)} %copy-done, bf16[1,896,4096]{2,1,0:T(8,128)(2,1)} %param.5, s32[]{:T(128)S(6)} %select_n.50), kind=kOutput, calls=%fused_computation.21 | convolution fusion | flops 235012096 | bytes 2588676 | tf_op jit(solution)/shard_map/dot_general | solution.py:65
  10.3 1.6 %fusion.22 = f32[128,1024]{1,0:T(8,128)S(1)} fusion(bf16[1,896,1024]{2,1,0:T(8,128)(2,1)S(1)} %copy-done, f32[1,2048,1024]{2,1,0:T(8,128)} %param.4, bf16[1,896,4096]{2,1,0:T(8,128)(2,1)} %param.5, s32[]{:T(128)S(6)} %select_n.48), kind=kOutput, calls=%fused_computation.22 | convolution fusion | flops 235143168 | bytes 3112964 | tf_op jit(solution)/shard_map/dot_general | solution.py:65
  11.9 2.0 %multiply_convert_fusion.9 = (f16[256,1024]{1,0:T(8,128)(2,1)}, f32[256,1024]{1,0:T(8,128)S(1)}) fusion(f32[128,1024]{1,0:T(8,128)} %fusion.19, f32[128,1024]{1,0:T(8,128)S(1)} %fusion.22), kind=kLoop, calls=%fused_computation.46 | loop fusion | flops 786432 | bytes 2621440 | tf_op jit(solution)/shard_map/convert_element_type | solution.py:113
  14.0 1.0 collective-permute-start.1
  14.9 1.1 collective-permute-start.5
  16.0 0.2 collective-permute-start.4
  16.3 1.2 %collective-permute-start.6 = (f16[256,1024]{1,0:T(8,128)(2,1)}, f16[256,1024]{1,0:T(8,128)(2,1)}, u32[]{:S(2)}, u32[]{:S(2)}) collective-permute-start(f16[256,1024]{1,0:T(8,128)(2,1)} %get-tuple-element.211), channel_id=1, source_target_pairs={{0,1},{1,0},{2,3},{3,2},{4,5},{5,4},{6,7},{7,6},{8,9},{9,8},{10,11... | collective-permute-start | bytes 1572872 | tf_op jit(solution)/shard_map/ppermute | solution.py:21
  17.5 4.2 %bitcast_subtract_fusion.1 = f32[768,1024]{1,0:T(8,128)S(1)} fusion(f32[1,2048,1024]{2,1,0:T(8,128)} %param.4, bf16[1,896,1024]{2,1,0:T(8,128)(2,1)S(1)} %copy-done, bf16[1,896,4096]{2,1,0:T(8,128)(2,1)} %param.5, s32[]{:T(128)S(6)} %select_n.47), kind=kOutput, calls=%fused_computation.2 | convolution fusion | flops 1410859008 | bytes 9502724 | tf_op jit(solution)/shard_map/dot_general | solution.py:65
  21.7 1.6 %copy-done.1 = f32[768,1024]{1,0:T(8,128)} copy-done((f32[768,1024]{1,0:T(8,128)}, f32[768,1024]{1,0:T(8,128)S(1)}, u32[]{:S(2)}) %copy-start.1) | copy-done | bytes 3145752
  23.3 1.0 multiply_convert_fusion.8
  24.3 4.1 %collective-permute-start.2 = (f16[256,1024]{1,0:T(8,128)(2,1)}, f16[256,1024]{1,0:T(8,128)(2,1)}, u32[]{:S(2)}, u32[]{:S(2)}) collective-permute-start(f16[256,1024]{1,0:T(8,128)(2,1)} %multiply_convert_fusion.8), channel_id=1, source_target_pairs={{0,2},{2,0},{4,6},{6,4},{8,10},{10,8},{12,14},{14,12},{16,18},{18,... | collective-permute-start | bytes 1572872 | tf_op jit(solution)/shard_map/ppermute | solution.py:30
  28.4 4.8 %multiply_convert_fusion = f16[1280,1024]{1,0:T(8,128)(2,1)S(1)} fusion(bf16[1,896,4096]{2,1,0:T(8,128)(2,1)} %param.5, s32[]{:T(128)S(6)} %select_n.52, bf16[1,896,1024]{2,1,0:T(8,128)(2,1)S(1)} %copy-done), kind=kOutput, calls=%fused_computation.1 | convolution fusion | flops 2351431680 | bytes 6750212 | tf_op jit(solution)/shard_map/dot_general | solution.py:65
  33.2 0.8 slice.171
  34.0 1.7 %fusion.37 = (f16[256,1024]{1,0:T(8,128)(2,1)}, f16[256,1024]{1,0:T(8,128)(2,1)}, f16[256,1024]{1,0:T(8,128)(2,1)}, f16[256,1024]{1,0:T(8,128)(2,1)}) fusion(f16[1280,1024]{1,0:T(8,128)(2,1)S(1)} %multiply_convert_fusion), kind=kLoop, calls=%fused_computation.68 | loop fusion | bytes 4194304 | tf_op jit(solution)/shard_map/slice | solution.py:141
  35.7 2.4 %multiply_convert_fusion.7 = f16[256,1024]{1,0:T(8,128)(2,1)} fusion(f16[256,1024]{1,0:T(8,128)(2,1)} %collective-permute-done.4, f32[768,1024]{1,0:T(8,128)} %copy-done.1), kind=kLoop, calls=%fused_computation.42 | loop fusion | flops 1310720 | bytes 2097152 | tf_op jit(solution)/shard_map/convert_element_type | solution.py:132
  38.1 0.7 collective-permute-start.8
  38.8 0.4 collective-permute-start.3
  39.1 1.2 %collective-permute-start.9 = (f16[256,1024]{1,0:T(8,128)(2,1)}, f16[256,1024]{1,0:T(8,128)(2,1)}, u32[]{:S(2)}, u32[]{:S(2)}) collective-permute-start(f16[256,1024]{1,0:T(8,128)(2,1)} %multiply_convert_fusion.7), channel_id=1, source_target_pairs={{2,4},{4,2},{6,8},{8,6},{10,12},{12,10},{14,16},{16,14},{18,20},{2... | collective-permute-start | bytes 1572872 | tf_op jit(solution)/shard_map/ppermute | solution.py:30
  40.4 1.1 collective-permute-done.6
  41.5 1.8 %collective-permute-done.7 = f16[256,1024]{1,0:T(8,128)(2,1)} collective-permute-done((f16[256,1024]{1,0:T(8,128)(2,1)}, f16[256,1024]{1,0:T(8,128)(2,1)}, u32[]{:S(2)}, u32[]{:S(2)}) %collective-permute-start.7) | collective-permute-done | bytes 524320 | tf_op jit(solution)/shard_map/ppermute | solution.py:30
  43.3 0.4 collective-permute-start.11
  43.7 2.4 %multiply_convert_fusion.6 = f16[256,1024]{1,0:T(8,128)(2,1)} fusion(f16[256,1024]{1,0:T(8,128)(2,1)} %collective-permute-done.6, f32[768,1024]{1,0:T(8,128)} %copy-done.1), kind=kLoop, calls=%fused_computation.40 | loop fusion | flops 1310720 | bytes 2097152 | tf_op jit(solution)/shard_map/convert_element_type | solution.py:132
  46.1 3.0 %collective-permute-start.10 = (f16[256,1024]{1,0:T(8,128)(2,1)}, f16[256,1024]{1,0:T(8,128)(2,1)}, u32[]{:S(2)}, u32[]{:S(2)}) collective-permute-start(f16[256,1024]{1,0:T(8,128)(2,1)} %multiply_convert_fusion.6), channel_id=1, source_target_pairs={{0,2},{2,0},{4,6},{6,4},{8,10},{10,8},{12,14},{14,12},{16,18},{18,... | collective-permute-start | bytes 1572872 | tf_op jit(solution)/shard_map/ppermute | solution.py:30
  49.0 1.1 collective-permute-start.12
  50.1 7.1 %bitcast_subtract_fusion = f32[1280,1024]{1,0:T(8,128)} fusion(f32[1,2048,1024]{2,1,0:T(8,128)} %param.4, bf16[1,896,4096]{2,1,0:T(8,128)(2,1)} %param.5, s32[]{:T(128)S(6)} %select_n.53, bf16[1,896,1024]{2,1,0:T(8,128)(2,1)S(1)} %copy-done), kind=kOutput, calls=%fused_computation | convolution fusion | flops 2351431680 | bytes 14614532 | tf_op jit(solution)/shard_map/dot_general | solution.py:65
  57.2 0.1 fusion.36
  57.3 0.2 multiply_reduce_fusion
  57.5 0.1 broadcast_in_dim.22
  57.6 0.2 collective-permute-start.14
  57.9 1.7 %multiply_convert_fusion.5 = f16[256,1024]{1,0:T(8,128)(2,1)S(1)} fusion(f16[256,1024]{1,0:T(8,128)(2,1)} %collective-permute-done.3, f32[1280,1024]{1,0:T(8,128)} %bitcast_subtract_fusion), kind=kLoop, calls=%fused_computation.38 | loop fusion | flops 1310720 | bytes 2097152 | tf_op jit(solution)/shard_map/convert_element_type | solution.py:132
  59.6 3.9 %collective-permute-start.13 = (f16[256,1024]{1,0:T(8,128)(2,1)S(1)}, f16[256,1024]{1,0:T(8,128)(2,1)S(1)}, u32[]{:S(2)}, u32[]{:S(2)}) collective-permute-start(f16[256,1024]{1,0:T(8,128)(2,1)S(1)} %multiply_convert_fusion.5), channel_id=1, source_target_pairs={{0,2},{2,0},{4,6},{6,4},{8,10},{10,8},{12,14},{14,12},{16,18},{18,... | collective-permute-start | bytes 1572872 | tf_op jit(solution)/shard_map/ppermute | solution.py:30
  63.5 1.1 broadcast_in_dim.21
  64.6 2.4 %multiply_add_fusion = (f32[256,1024]{1,0:T(8,128)S(1)}, f32[2048,1024]{1,0:T(8,128)S(1)}) fusion(f16[256,1024]{1,0:T(8,128)(2,1)} %collective-permute-done.5, f32[256,1024]{1,0:T(8,128)S(1)} %get-tuple-element.159, f16[256,1024]{1,0:T(8,128)(2,1)} %collective-permute-done.1, f32[1024]{0:T(1024)S(1)} %bitcast.68, f32[1024]{0:T(1024)S(1)} %bitcast.76, ...), kind=kLoop, calls=%fused_computation.36 | loop fusion | flops 4456448 | bytes 6828032 | tf_op jit(solution)/shard_map/add | solution.py:90
  67.0 0.1 fusion.25
  67.1 2.2 %collective-permute-done.12 = f16[256,1024]{1,0:T(8,128)(2,1)} collective-permute-done((f16[256,1024]{1,0:T(8,128)(2,1)}, f16[256,1024]{1,0:T(8,128)(2,1)}, u32[]{:S(2)}, u32[]{:S(2)}) %collective-permute-start.12) | collective-permute-done | bytes 524320 | tf_op jit(solution)/shard_map/ppermute | solution.py:30
  69.3 1.2 %multiply_convert_fusion.4 = f16[256,1024]{1,0:T(8,128)(2,1)S(1)} fusion(f16[256,1024]{1,0:T(8,128)(2,1)} %collective-permute-done.11, f32[1280,1024]{1,0:T(8,128)S(1)} %bitcast.58), kind=kLoop, calls=%fused_computation.34 | loop fusion | flops 1310720 | bytes 2097152 | tf_op jit(solution)/shard_map/convert_element_type | solution.py:132
  70.6 0.1 collective-permute-start.16
  70.7 2.5 %collective-permute-start.18 = (f16[256,1024]{1,0:T(8,128)(2,1)S(1)}, f16[256,1024]{1,0:T(8,128)(2,1)S(1)}, u32[]{:S(2)}, u32[]{:S(2)}) collective-permute-start(f16[256,1024]{1,0:T(8,128)(2,1)S(1)} %multiply_convert_fusion.4), channel_id=1, source_target_pairs={{2,4},{4,2},{6,8},{8,6},{10,12},{12,10},{14,16},{16,14},{18,20},{2... | collective-permute-start | bytes 1572872 | tf_op jit(solution)/shard_map/ppermute | solution.py:30
  73.3 2.2 %collective-permute-done.14 = f16[256,1024]{1,0:T(8,128)(2,1)S(1)} collective-permute-done((f16[256,1024]{1,0:T(8,128)(2,1)}, f16[256,1024]{1,0:T(8,128)(2,1)S(1)}, u32[]{:S(2)}, u32[]{:S(2)}) %collective-permute-start.14) | collective-permute-done | bytes 524320 | tf_op jit(solution)/shard_map/ppermute | solution.py:21
  75.5 8.2 %collective-permute-done.15 = f16[256,1024]{1,0:T(8,128)(2,1)S(1)} collective-permute-done((f16[256,1024]{1,0:T(8,128)(2,1)S(1)}, f16[256,1024]{1,0:T(8,128)(2,1)S(1)}, u32[]{:S(2)}, u32[]{:S(2)}) %collective-permute-start.15) | collective-permute-done | bytes 524320 | tf_op jit(solution)/shard_map/ppermute | solution.py:30
  83.6 1.8 %add_dynamic-update-slice_fusion.2 = f32[2048,1024]{1,0:T(8,128)S(1)} fusion(f32[2048,1024]{1,0:T(8,128)S(1)} %get-tuple-element.169, f16[256,1024]{1,0:T(8,128)(2,1)} %collective-permute-done.9, f32[768,1024]{1,0:T(8,128)S(1)} %copy-done.2, f16[256,1024]{1,0:T(8,128)(2,1)} %collective-permute-done.8, f16[256,1024]{1,0:T(8,128)(2,1)} %collective-permute-done.4, ...), kind=kLoop, calls=%fused_computation.33 | loop fusion | flops 2621440 | bytes 3682304 | tf_op jit(solution)/shard_map/dynamic_update_slice | solution.py:97
  85.4 0.2 multiply_convert_fusion.3
  85.7 1.3 %collective-permute-start.20 = (f16[128,1024]{1,0:T(8,128)(2,1)S(1)}, f16[128,1024]{1,0:T(8,128)(2,1)S(1)}, u32[]{:S(2)}, u32[]{:S(2)}) collective-permute-start(f16[128,1024]{1,0:T(8,128)(2,1)S(1)} %copy-done.5), channel_id=1, source_target_pairs={{0,1},{1,0},{2,3},{3,2},{4,5},{5,4},{6,7},{7,6},{8,9},{9,8},{10,11... | collective-permute-start | bytes 786440 | tf_op jit(solution)/shard_map/ppermute | solution.py:21
  87.0 1.8 %add_dynamic-update-slice_fusion.1 = f32[2048,1024]{1,0:T(8,128)S(1)} fusion(f32[2048,1024]{1,0:T(8,128)S(1)} %add_dynamic-update-slice_fusion.2, f16[256,1024]{1,0:T(8,128)(2,1)} %collective-permute-done.12, f32[768,1024]{1,0:T(8,128)S(1)} %copy-done.2, f16[256,1024]{1,0:T(8,128)(2,1)} %collective-permute-done.10, ...), kind=kLoop, calls=%fused_computation.30 | loop fusion | flops 2621440 | bytes 3682304 | tf_op jit(solution)/shard_map/dynamic_update_slice | solution.py:97
  88.8 0.2 collective-permute-done.18
  89.0 0.2 multiply_convert_fusion.2
  89.2 2.3 %collective-permute-start.22 = (f16[256,1024]{1,0:T(8,128)(2,1)S(1)}, f16[256,1024]{1,0:T(8,128)(2,1)S(1)}, u32[]{:S(2)}, u32[]{:S(2)}) collective-permute-start(f16[256,1024]{1,0:T(8,128)(2,1)S(1)} %multiply_convert_fusion.2), channel_id=1, source_target_pairs={{0,2},{2,0},{4,6},{6,4},{8,10},{10,8},{12,14},{14,12},{16,18},{18,... | collective-permute-start | bytes 1572872 | tf_op jit(solution)/shard_map/ppermute | solution.py:30
  91.5 1.4 %collective-permute-start.23 = (f16[256,1024]{1,0:T(8,128)(2,1)S(1)}, f16[256,1024]{1,0:T(8,128)(2,1)S(1)}, u32[]{:S(2)}, u32[]{:S(2)}) collective-permute-start(f16[256,1024]{1,0:T(8,128)(2,1)S(1)} %multiply_convert_fusion.2), channel_id=1, source_target_pairs={{2,4},{4,2},{6,8},{8,6},{10,12},{12,10},{14,16},{16,14},{18,20},{2... | collective-permute-start | bytes 1572872 | tf_op jit(solution)/shard_map/ppermute | solution.py:30
  93.0 0.3 collective-permute-done.20
  93.2 13.6 %collective-permute-done.21 = f16[256,1024]{1,0:T(8,128)(2,1)S(1)} collective-permute-done((f16[256,1024]{1,0:T(8,128)(2,1)S(1)}, f16[256,1024]{1,0:T(8,128)(2,1)S(1)}, u32[]{:S(2)}, u32[]{:S(2)}) %collective-permute-start.21) | collective-permute-done | bytes 524320 | tf_op jit(solution)/shard_map/ppermute | solution.py:30
  106.9 1.5 %add_dynamic-update-slice_fusion = f32[2048,1024]{1,0:T(8,128)S(1)} fusion(f32[2048,1024]{1,0:T(8,128)S(1)} %add_dynamic-update-slice_fusion.1, f16[256,1024]{1,0:T(8,128)(2,1)S(1)} %collective-permute-done.15, f32[1280,1024]{1,0:T(8,128)S(1)} %bitcast.58, f16[256,1024]{1,0:T(8,128)(2,1)S(1)} %collective-permute-done.13, ...), kind=kLoop, calls=%fused_computation.27 | loop fusion | flops 2621440 | bytes 3682304 | tf_op jit(solution)/shard_map/dynamic_update_slice | solution.py:97
  108.3 0.1 multiply_convert_fusion.10
  108.5 0.1 collective-permute-start.26
  108.6 1.5 %bitcast_dynamic-update-slice_fusion.2 = f32[1,2048,1024]{2,1,0:T(8,128)S(1)} fusion(f32[1,2048,1024]{2,1,0:T(8,128)S(1)} %bitcast.59, f16[256,1024]{1,0:T(8,128)(2,1)S(1)} %collective-permute-done.18, f32[1280,1024]{1,0:T(8,128)S(1)} %bitcast.58, f16[256,1024]{1,0:T(8,128)(2,1)S(1)} %collective-permute-done.16, ...), kind=kLoop, calls=%fused_computation.26 | loop fusion | flops 2621440 | bytes 3682304 | tf_op jit(solution)/shard_map/dynamic_update_slice | solution.py:97
  110.1 0.4 bitcast_dynamic-update-slice_fusion.1
  110.5 2.0 %collective-permute-done.23 = f16[256,1024]{1,0:T(8,128)(2,1)S(1)} collective-permute-done((f16[256,1024]{1,0:T(8,128)(2,1)S(1)}, f16[256,1024]{1,0:T(8,128)(2,1)S(1)}, u32[]{:S(2)}, u32[]{:S(2)}) %collective-permute-start.23) | collective-permute-done | bytes 524320 | tf_op jit(solution)/shard_map/ppermute | solution.py:30
  112.5 0.4 bitcast_dynamic-update-slice_fusion
  112.9 0.1 bitcast_dynamic-update-slice_fusion.4
  113.0 5.1 %collective-permute-done.26 = f16[128,1024]{1,0:T(8,128)(2,1)S(1)} collective-permute-done((f16[128,1024]{1,0:T(8,128)(2,1)S(1)}, f16[128,1024]{1,0:T(8,128)(2,1)S(1)}, u32[]{:S(2)}, u32[]{:S(2)}) %collective-permute-start.26) | collective-permute-done | bytes 262176 | tf_op jit(solution)/shard_map/ppermute | solution.py:30
  118.1 1.0 bitcast_dynamic-update-slice_fusion.3
  (43 shorter events, 0.3 us)
Async XLA Ops:
  0.0 1.5 %copy-start = (bf16[1,896,1024]{2,1,0:T(8,128)(2,1)S(1)}, bf16[1,896,1024]{2,1,0:T(8,128)(2,1)}, u32[]{:S(2)}) copy-start(bf16[1,896,1024]{2,1,0:T(8,128)(2,1)} %param.6) | copy-start | bytes 5505028
  6.0 15.7 %collective-permute-start = (f16[256,1024]{1,0:T(8,128)(2,1)}, f16[256,1024]{1,0:T(8,128)(2,1)S(1)}, u32[]{:S(2)}, u32[]{:S(2)}) collective-permute-start(f16[256,1024]{1,0:T(8,128)(2,1)} %get-tuple-element.106), channel_id=1, source_target_pairs={{0,1},{1,0},{2,3},{3,2},{4,5},{5,4},{6,7},{7,6},{8,9},{9,8},{10,11... | collective-permute-start | bytes 1572872 | tf_op jit(solution)/shard_map/ppermute | solution.py:21
  14.0 7.7 %collective-permute-start.1 = (f16[256,1024]{1,0:T(8,128)(2,1)}, f16[256,1024]{1,0:T(8,128)(2,1)}, u32[]{:S(2)}, u32[]{:S(2)}) collective-permute-start(f16[256,1024]{1,0:T(8,128)(2,1)} %get-tuple-element.110), channel_id=1, source_target_pairs={{0,2},{2,0},{4,6},{6,4},{8,10},{10,8},{12,14},{14,12},{16,18},{18,... | collective-permute-start | bytes 1572872 | tf_op jit(solution)/shard_map/ppermute | solution.py:30
  14.9 20.8 %collective-permute-start.5 = (f16[256,1024]{1,0:T(8,128)(2,1)}, f16[256,1024]{1,0:T(8,128)(2,1)}, u32[]{:S(2)}, u32[]{:S(2)}) collective-permute-start(f16[256,1024]{1,0:T(8,128)(2,1)} %get-tuple-element.110), channel_id=1, source_target_pairs={{2,4},{4,2},{6,8},{8,6},{10,12},{12,10},{14,16},{16,14},{18,20},{2... | collective-permute-start | bytes 1572872 | tf_op jit(solution)/shard_map/ppermute | solution.py:30
  16.0 19.6 %collective-permute-start.4 = (f16[256,1024]{1,0:T(8,128)(2,1)}, f16[256,1024]{1,0:T(8,128)(2,1)}, u32[]{:S(2)}, u32[]{:S(2)}) collective-permute-start(f16[256,1024]{1,0:T(8,128)(2,1)} %get-tuple-element.212), channel_id=1, source_target_pairs={{0,1},{1,0},{2,3},{3,2},{4,5},{5,4},{6,7},{7,6},{8,9},{9,8},{10,11... | collective-permute-start | bytes 1572872 | tf_op jit(solution)/shard_map/ppermute | solution.py:21
  16.3 25.2 %collective-permute-start.6 = (f16[256,1024]{1,0:T(8,128)(2,1)}, f16[256,1024]{1,0:T(8,128)(2,1)}, u32[]{:S(2)}, u32[]{:S(2)}) collective-permute-start(f16[256,1024]{1,0:T(8,128)(2,1)} %get-tuple-element.211), channel_id=1, source_target_pairs={{0,1},{1,0},{2,3},{3,2},{4,5},{5,4},{6,7},{7,6},{8,9},{9,8},{10,11... | collective-permute-start | bytes 1572872 | tf_op jit(solution)/shard_map/ppermute | solution.py:21
  21.7 1.6 %copy-start.1 = (f32[768,1024]{1,0:T(8,128)}, f32[768,1024]{1,0:T(8,128)S(1)}, u32[]{:S(2)}) copy-start(f32[768,1024]{1,0:T(8,128)S(1)} %bitcast_subtract_fusion.1) | copy-start | bytes 9437188
  24.3 11.4 %collective-permute-start.2 = (f16[256,1024]{1,0:T(8,128)(2,1)}, f16[256,1024]{1,0:T(8,128)(2,1)}, u32[]{:S(2)}, u32[]{:S(2)}) collective-permute-start(f16[256,1024]{1,0:T(8,128)(2,1)} %multiply_convert_fusion.8), channel_id=1, source_target_pairs={{0,2},{2,0},{4,6},{6,4},{8,10},{10,8},{12,14},{14,12},{16,18},{18,... | collective-permute-start | bytes 1572872 | tf_op jit(solution)/shard_map/ppermute | solution.py:30
  28.4 14.8 %collective-permute-start.7 = (f16[256,1024]{1,0:T(8,128)(2,1)}, f16[256,1024]{1,0:T(8,128)(2,1)}, u32[]{:S(2)}, u32[]{:S(2)}) collective-permute-start(f16[256,1024]{1,0:T(8,128)(2,1)} %multiply_convert_fusion.8), channel_id=1, source_target_pairs={{2,4},{4,2},{6,8},{8,6},{10,12},{12,10},{14,16},{16,14},{18,20},{2... | collective-permute-start | bytes 1572872 | tf_op jit(solution)/shard_map/ppermute | solution.py:30
  38.1 5.6 %collective-permute-start.8 = (f16[256,1024]{1,0:T(8,128)(2,1)}, f16[256,1024]{1,0:T(8,128)(2,1)}, u32[]{:S(2)}, u32[]{:S(2)}) collective-permute-start(f16[256,1024]{1,0:T(8,128)(2,1)} %multiply_convert_fusion.7), channel_id=1, source_target_pairs={{0,2},{2,0},{4,6},{6,4},{8,10},{10,8},{12,14},{14,12},{16,18},{18,... | collective-permute-start | bytes 1572872 | tf_op jit(solution)/shard_map/ppermute | solution.py:30
  38.8 18.8 %collective-permute-start.3 = (f16[256,1024]{1,0:T(8,128)(2,1)}, f16[256,1024]{1,0:T(8,128)(2,1)}, u32[]{:S(2)}, u32[]{:S(2)}) collective-permute-start(f16[256,1024]{1,0:T(8,128)(2,1)} %get-tuple-element.114), channel_id=1, source_target_pairs={{0,1},{1,0},{2,3},{3,2},{4,5},{5,4},{6,7},{7,6},{8,9},{9,8},{10,11... | collective-permute-start | bytes 1572872 | tf_op jit(solution)/shard_map/ppermute | solution.py:21
  39.1 18.7 %collective-permute-start.9 = (f16[256,1024]{1,0:T(8,128)(2,1)}, f16[256,1024]{1,0:T(8,128)(2,1)}, u32[]{:S(2)}, u32[]{:S(2)}) collective-permute-start(f16[256,1024]{1,0:T(8,128)(2,1)} %multiply_convert_fusion.7), channel_id=1, source_target_pairs={{2,4},{4,2},{6,8},{8,6},{10,12},{12,10},{14,16},{16,14},{18,20},{2... | collective-permute-start | bytes 1572872 | tf_op jit(solution)/shard_map/ppermute | solution.py:30
  43.3 23.8 %collective-permute-start.11 = (f16[256,1024]{1,0:T(8,128)(2,1)}, f16[256,1024]{1,0:T(8,128)(2,1)}, u32[]{:S(2)}, u32[]{:S(2)}) collective-permute-start(f16[256,1024]{1,0:T(8,128)(2,1)} %get-tuple-element.131), channel_id=1, source_target_pairs={{0,1},{1,0},{2,3},{3,2},{4,5},{5,4},{6,7},{7,6},{8,9},{9,8},{10,11... | collective-permute-start | bytes 1572872 | tf_op jit(solution)/shard_map/ppermute | solution.py:21
  46.1 11.8 %collective-permute-start.10 = (f16[256,1024]{1,0:T(8,128)(2,1)}, f16[256,1024]{1,0:T(8,128)(2,1)}, u32[]{:S(2)}, u32[]{:S(2)}) collective-permute-start(f16[256,1024]{1,0:T(8,128)(2,1)} %multiply_convert_fusion.6), channel_id=1, source_target_pairs={{0,2},{2,0},{4,6},{6,4},{8,10},{10,8},{12,14},{14,12},{16,18},{18,... | collective-permute-start | bytes 1572872 | tf_op jit(solution)/shard_map/ppermute | solution.py:30
  49.0 20.3 %collective-permute-start.12 = (f16[256,1024]{1,0:T(8,128)(2,1)}, f16[256,1024]{1,0:T(8,128)(2,1)}, u32[]{:S(2)}, u32[]{:S(2)}) collective-permute-start(f16[256,1024]{1,0:T(8,128)(2,1)} %multiply_convert_fusion.6), channel_id=1, source_target_pairs={{2,4},{4,2},{6,8},{8,6},{10,12},{12,10},{14,16},{16,14},{18,20},{2... | collective-permute-start | bytes 1572872 | tf_op jit(solution)/shard_map/ppermute | solution.py:30
  50.1 7.1 %copy-start.6 = (s32[16,3]{0,1:T(4,128)S(1)}, s32[16,3]{0,1:T(4,128)}, u32[]{:S(2)}) copy-start(s32[16,3]{0,1:T(4,128)} %param.7) | copy-start | bytes 580
  57.6 17.9 %collective-permute-start.14 = (f16[256,1024]{1,0:T(8,128)(2,1)}, f16[256,1024]{1,0:T(8,128)(2,1)S(1)}, u32[]{:S(2)}, u32[]{:S(2)}) collective-permute-start(f16[256,1024]{1,0:T(8,128)(2,1)} %get-tuple-element.136), channel_id=1, source_target_pairs={{0,1},{1,0},{2,3},{3,2},{4,5},{5,4},{6,7},{7,6},{8,9},{9,8},{10,11... | collective-permute-start | bytes 1572872 | tf_op jit(solution)/shard_map/ppermute | solution.py:21
  57.8 6.7 %copy-start.2 = (f32[768,1024]{1,0:T(8,128)S(1)}, f32[768,1024]{1,0:T(8,128)}, u32[]{:S(2)}) copy-start(f32[768,1024]{1,0:T(8,128)} %copy-done.1) | copy-start | bytes 9437188
  59.6 9.7 %collective-permute-start.13 = (f16[256,1024]{1,0:T(8,128)(2,1)S(1)}, f16[256,1024]{1,0:T(8,128)(2,1)S(1)}, u32[]{:S(2)}, u32[]{:S(2)}) collective-permute-start(f16[256,1024]{1,0:T(8,128)(2,1)S(1)} %multiply_convert_fusion.5), channel_id=1, source_target_pairs={{0,2},{2,0},{4,6},{6,4},{8,10},{10,8},{12,14},{14,12},{16,18},{18,... | collective-permute-start | bytes 1572872 | tf_op jit(solution)/shard_map/ppermute | solution.py:30
  63.5 20.1 %collective-permute-start.15 = (f16[256,1024]{1,0:T(8,128)(2,1)S(1)}, f16[256,1024]{1,0:T(8,128)(2,1)S(1)}, u32[]{:S(2)}, u32[]{:S(2)}) collective-permute-start(f16[256,1024]{1,0:T(8,128)(2,1)S(1)} %multiply_convert_fusion.5), channel_id=1, source_target_pairs={{2,4},{4,2},{6,8},{8,6},{10,12},{12,10},{14,16},{16,14},{18,20},{2... | collective-permute-start | bytes 1572872 | tf_op jit(solution)/shard_map/ppermute | solution.py:30
  63.5 5.8 %slice-start = ((s8[5242880]{0:T(1024)(128)(4,1)}), s8[1048576]{0:T(1024)(128)(4,1)S(1)}, s32[]{:S(2)}) async-start(s8[5242880]{0:T(1024)(128)(4,1)} %bitcast.57), calls=%async_computation | async-start | bytes 2097152
  64.6 4.7 %slice-start.1 = ((s8[5242880]{0:T(1024)(128)(4,1)}), s8[4194304]{0:T(1024)(128)(4,1)S(1)}, s32[]{:S(2)}) async-start(s8[5242880]{0:T(1024)(128)(4,1)} %bitcast.57), calls=%async_computation.1 | async-start | bytes 8388608
  64.6 6.1 %copy-start.4 = (f16[256,1024]{1,0:T(8,128)(2,1)S(1)}, f16[256,1024]{1,0:T(8,128)(2,1)}, u32[]{:S(2)}) copy-start(f16[256,1024]{1,0:T(8,128)(2,1)} %get-tuple-element.176) | copy-start | bytes 1572868
  67.0 18.7 %copy-start.5 = (f16[128,1024]{1,0:T(8,128)(2,1)S(1)}, f16[128,1024]{1,0:T(8,128)(2,1)}, u32[]{:S(2)}) copy-start(f16[128,1024]{1,0:T(8,128)(2,1)} %slice.171) | copy-start | bytes 786436
  70.6 14.8 %collective-permute-start.16 = (f16[256,1024]{1,0:T(8,128)(2,1)S(1)}, f16[256,1024]{1,0:T(8,128)(2,1)S(1)}, u32[]{:S(2)}, u32[]{:S(2)}) collective-permute-start(f16[256,1024]{1,0:T(8,128)(2,1)S(1)} %multiply_convert_fusion.4), channel_id=1, source_target_pairs={{0,2},{2,0},{4,6},{6,4},{8,10},{10,8},{12,14},{14,12},{16,18},{18,... | collective-permute-start | bytes 1572872 | tf_op jit(solution)/shard_map/ppermute | solution.py:30
  70.7 18.1 %collective-permute-start.17 = (f16[256,1024]{1,0:T(8,128)(2,1)S(1)}, f16[256,1024]{1,0:T(8,128)(2,1)S(1)}, u32[]{:S(2)}, u32[]{:S(2)}) collective-permute-start(f16[256,1024]{1,0:T(8,128)(2,1)S(1)} %copy-done.4), channel_id=1, source_target_pairs={{0,1},{1,0},{2,3},{3,2},{4,5},{5,4},{6,7},{7,6},{8,9},{9,8},{10,11... | collective-permute-start | bytes 1572872 | tf_op jit(solution)/shard_map/ppermute | solution.py:21
  70.7 18.2 %collective-permute-start.18 = (f16[256,1024]{1,0:T(8,128)(2,1)S(1)}, f16[256,1024]{1,0:T(8,128)(2,1)S(1)}, u32[]{:S(2)}, u32[]{:S(2)}) collective-permute-start(f16[256,1024]{1,0:T(8,128)(2,1)S(1)} %multiply_convert_fusion.4), channel_id=1, source_target_pairs={{2,4},{4,2},{6,8},{8,6},{10,12},{12,10},{14,16},{16,14},{18,20},{2... | collective-permute-start | bytes 1572872 | tf_op jit(solution)/shard_map/ppermute | solution.py:30
  85.6 3.3 %collective-permute-start.19 = (f16[256,1024]{1,0:T(8,128)(2,1)S(1)}, f16[256,1024]{1,0:T(8,128)(2,1)S(1)}, u32[]{:S(2)}, u32[]{:S(2)}) collective-permute-start(f16[256,1024]{1,0:T(8,128)(2,1)S(1)} %multiply_convert_fusion.3), channel_id=1, source_target_pairs={{0,2},{2,0},{4,6},{6,4},{8,10},{10,8},{12,14},{14,12},{16,18},{18,... | collective-permute-start | bytes 1572872 | tf_op jit(solution)/shard_map/ppermute | solution.py:30
  85.7 7.5 %collective-permute-start.20 = (f16[128,1024]{1,0:T(8,128)(2,1)S(1)}, f16[128,1024]{1,0:T(8,128)(2,1)S(1)}, u32[]{:S(2)}, u32[]{:S(2)}) collective-permute-start(f16[128,1024]{1,0:T(8,128)(2,1)S(1)} %copy-done.5), channel_id=1, source_target_pairs={{0,1},{1,0},{2,3},{3,2},{4,5},{5,4},{6,7},{7,6},{8,9},{9,8},{10,11... | collective-permute-start | bytes 786440 | tf_op jit(solution)/shard_map/ppermute | solution.py:21
  87.0 19.8 %collective-permute-start.21 = (f16[256,1024]{1,0:T(8,128)(2,1)S(1)}, f16[256,1024]{1,0:T(8,128)(2,1)S(1)}, u32[]{:S(2)}, u32[]{:S(2)}) collective-permute-start(f16[256,1024]{1,0:T(8,128)(2,1)S(1)} %multiply_convert_fusion.3), channel_id=1, source_target_pairs={{2,4},{4,2},{6,8},{8,6},{10,12},{12,10},{14,16},{16,14},{18,20},{2... | collective-permute-start | bytes 1572872 | tf_op jit(solution)/shard_map/ppermute | solution.py:30
  89.2 19.1 %collective-permute-start.22 = (f16[256,1024]{1,0:T(8,128)(2,1)S(1)}, f16[256,1024]{1,0:T(8,128)(2,1)S(1)}, u32[]{:S(2)}, u32[]{:S(2)}) collective-permute-start(f16[256,1024]{1,0:T(8,128)(2,1)S(1)} %multiply_convert_fusion.2), channel_id=1, source_target_pairs={{0,2},{2,0},{4,6},{6,4},{8,10},{10,8},{12,14},{14,12},{16,18},{18,... | collective-permute-start | bytes 1572872 | tf_op jit(solution)/shard_map/ppermute | solution.py:30
  91.5 21.4 %collective-permute-start.24 = (f16[128,1024]{1,0:T(8,128)(2,1)S(1)}, f16[128,1024]{1,0:T(8,128)(2,1)S(1)}, u32[]{:S(2)}, u32[]{:S(2)}) collective-permute-start(f16[128,1024]{1,0:T(8,128)(2,1)S(1)} %get-tuple-element.205), channel_id=1, source_target_pairs={{0,1},{1,0},{2,3},{3,2},{4,5},{5,4},{6,7},{7,6},{8,9},{9,8},{10,11... | collective-permute-start | bytes 786440 | tf_op jit(solution)/shard_map/ppermute | solution.py:21
  91.5 21.0 %collective-permute-start.23 = (f16[256,1024]{1,0:T(8,128)(2,1)S(1)}, f16[256,1024]{1,0:T(8,128)(2,1)S(1)}, u32[]{:S(2)}, u32[]{:S(2)}) collective-permute-start(f16[256,1024]{1,0:T(8,128)(2,1)S(1)} %multiply_convert_fusion.2), channel_id=1, source_target_pairs={{2,4},{4,2},{6,8},{8,6},{10,12},{12,10},{14,16},{16,14},{18,20},{2... | collective-permute-start | bytes 1572872 | tf_op jit(solution)/shard_map/ppermute | solution.py:30
  108.4 4.6 %collective-permute-start.25 = (f16[128,1024]{1,0:T(8,128)(2,1)S(1)}, f16[128,1024]{1,0:T(8,128)(2,1)S(1)}, u32[]{:S(2)}, u32[]{:S(2)}) collective-permute-start(f16[128,1024]{1,0:T(8,128)(2,1)S(1)} %multiply_convert_fusion.10), channel_id=1, source_target_pairs={{0,2},{2,0},{4,6},{6,4},{8,10},{10,8},{12,14},{14,12},{16,18},{18,... | collective-permute-start | bytes 786440 | tf_op jit(solution)/shard_map/ppermute | solution.py:30
  108.5 9.6 %collective-permute-start.26 = (f16[128,1024]{1,0:T(8,128)(2,1)S(1)}, f16[128,1024]{1,0:T(8,128)(2,1)S(1)}, u32[]{:S(2)}, u32[]{:S(2)}) collective-permute-start(f16[128,1024]{1,0:T(8,128)(2,1)S(1)} %multiply_convert_fusion.10), channel_id=1, source_target_pairs={{2,4},{4,2},{6,8},{8,6},{10,12},{12,10},{14,16},{16,14},{18,20},{2... | collective-permute-start | bytes 786440 | tf_op jit(solution)/shard_map/ppermute | solution.py:30
  113.0 5.1 %copy-start.3 = (f32[1,2048,1024]{2,1,0:T(8,128)}, f32[1,2048,1024]{2,1,0:T(8,128)S(1)}, u32[]{:S(2)}) copy-start(f32[1,2048,1024]{2,1,0:T(8,128)S(1)} %bitcast_dynamic-update-slice_fusion.4) | copy-start | bytes 25165828

commit v19 on v18

--- a/solution.py
+++ b/solution.py
@@ -102,8 +102,7 @@
     out = jnp.zeros_like(weights)
     split = cuts[min(3, chunks)]
     begun = min(3, chunks)
-    made = for_others(0, cuts[begun])
-    terms = {chunk: [term[cuts[chunk]:cuts[chunk + 1]] for term in made] for chunk in range(begun)}
+    terms = {0: for_others(0, cuts[1])}
 
     terms[0], later = lax.optimization_barrier((terms[0], shard))
     arrived = {0: add_over_fsdp(terms[0])}
@@ -114,8 +113,16 @@
     far[-1] = swapped(sent, "blk", 1)
     near[-1] = swapped(sent, "blk", 0)
 
-    for chunk in range(1, begun):
-        arrived[chunk] = add_over_fsdp(terms[chunk])
+    if begun > 1:
+        parts, later = lax.optimization_barrier((parts, shard))
+        size = cuts[begun] - cuts[1]
+        made = [
+            (partial(owner(away, later), cuts[1], size) * (RATE * scale)).astype(WIRE)
+            for away in range(1, shards)
+        ]
+        for chunk in range(1, begun):
+            terms[chunk] = [term[cuts[chunk] - cuts[1]:cuts[chunk + 1] - cuts[1]] for term in made]
+            arrived[chunk] = add_over_fsdp(terms[chunk])
     base = [own_part(shard, 0, split)]
 
     arrived[0], base, terms = lax.optimization_barrier((arrived[0], base, terms))

time: 120 us -> 122 us (1.017)
  waiting for transfers between devices: 36.6 us -> 39.1 us
    ppermute x9, starting transfers between devices: 5.92 us -> 9.22 us  [from_behind(): return lax.ppermute(value, axis, pairs)]
    ppermute x18, starting transfers between devices: 22.6 us -> 19.4 us  [swapped(): return lax.ppermute(value, axis, pairs)]
    ppermute x9, waiting for transfers between devices: 3.59 us -> 6.51 us  [from_behind(): return lax.ppermute(value, axis, pairs)]
    dot_general x6 -> x7, matrix products: 23 us -> 24.1 us  [partial(): lax.dot_general(block, cot_local, (((0,), (0,)), ((), ())), preferred_ele...]
  transfers between devices with their start and end apart: 27 -> 27, of which waited for: 10 -> 10; matrix products, arithmetic and copies ran while one was open for 38% -> 35% of each run, Pallas kernels for 0% -> 0%
where the time goes in v19:
time: 122 us
  waiting for transfers between devices  39.1 us (32%)
  starting transfers between devices  28.6 us (23%)
  matrix products  24.1 us (20%)
  other arithmetic  21.5 us (18%)
  local copies, waits for them, and re-layouts  8.25 us (7%)
    ppermute x18, waiting for transfers between devices, swapped(): return lax.ppermute(value, axis, pairs)  32.6 us
    dot_general x7, matrix products, partial(): lax.dot_general(block, cot_local, (((0,), (0,)), ((), ())), preferred_ele...  24.1 us
    ppermute x18, starting transfers between devices, swapped(): return lax.ppermute(value, axis, pairs)  19.4 us
    convert_element_type x8, other arithmetic, on_device(): sent = (u_of(chunk) * scale).astype(WIRE)  9.33 us
    ppermute x9, starting transfers between devices, from_behind(): return lax.ppermute(value, axis, pairs)  9.22 us
    dynamic_update_slice x7, other arithmetic, mix_into(): return lax.dynamic_update_slice_in_dim(out, value, cuts[chunk], axis=0)  8.33 us
    ppermute x9, waiting for transfers between devices, from_behind(): return lax.ppermute(value, axis, pairs)  6.51 us
    unnamed x18, local copies, waits for them, and re-layouts  3.41 us
  transfers between devices with their start and end apart: 27, of which 10 were waited for; matrix products, arithmetic and copies ran while one was open for 35% of the time, Pallas kernels for 0%

profile of v19, /device:TPU:1, one launch (start us, length us, event | category | flops | bytes accessed | tf_op | source)
XLA Modules:
  0.0 121.9 jit_solution(13858466511854712050)
XLA Ops:
  0.0 1.5 %copy-done = bf16[1,896,1024]{2,1,0:T(8,128)(2,1)S(1)} copy-done((bf16[1,896,1024]{2,1,0:T(8,128)(2,1)S(1)}, bf16[1,896,1024]{2,1,0:T(8,128)(2,1)}, u32[]{:S(2)}) %copy-start) | copy-done | bytes 1835032
  1.5 2.6 %fusion.22 = f16[256,1024]{1,0:T(8,128)(2,1)} fusion(bf16[1,896,1024]{2,1,0:T(8,128)(2,1)S(1)} %copy-done, bf16[1,896,4096]{2,1,0:T(8,128)(2,1)} %param.5, s32[]{:T(128)S(6)} %select_n.52), kind=kOutput, calls=%fused_computation.22 | convolution fusion | flops 470286336 | bytes 2818052 | tf_op jit(solution)/shard_map/dot_general | solution.py:65
  4.1 1.4 %fusion.28 = f32[128,1024]{1,0:T(8,128)S(1)} fusion(bf16[1,896,1024]{2,1,0:T(8,128)(2,1)S(1)} %copy-done, bf16[1,896,4096]{2,1,0:T(8,128)(2,1)} %param.5, s32[]{:T(128)S(6)} %select_n.56), kind=kOutput, calls=%fused_computation.24 | convolution fusion | flops 235012096 | bytes 2588676 | tf_op jit(solution)/shard_map/dot_general | solution.py:65
  5.5 1.6 %fusion.31 = f32[128,1024]{1,0:T(8,128)S(1)} fusion(bf16[1,896,1024]{2,1,0:T(8,128)(2,1)S(1)} %copy-done, f32[1,2048,1024]{2,1,0:T(8,128)} %param.4, bf16[1,896,4096]{2,1,0:T(8,128)(2,1)} %param.5, s32[]{:T(128)S(6)} %select_n.54), kind=kOutput, calls=%fused_computation.25 | convolution fusion | flops 235143168 | bytes 3112964 | tf_op jit(solution)/shard_map/dot_general | solution.py:65
  7.1 1.0 multiply_convert_fusion.9
  8.2 2.5 %collective-permute-start.5 = (f16[256,1024]{1,0:T(8,128)(2,1)}, f16[256,1024]{1,0:T(8,128)(2,1)}, u32[]{:S(2)}, u32[]{:S(2)}) collective-permute-start(f16[256,1024]{1,0:T(8,128)(2,1)} %get-tuple-element.114), channel_id=1, source_target_pairs={{2,4},{4,2},{6,8},{8,6},{10,12},{12,10},{14,16},{16,14},{18,20},{2... | collective-permute-start | bytes 1572872 | tf_op jit(solution)/shard_map/ppermute | solution.py:30
  10.7 1.2 %collective-permute-start = (f16[256,1024]{1,0:T(8,128)(2,1)}, f16[256,1024]{1,0:T(8,128)(2,1)S(1)}, u32[]{:S(2)}, u32[]{:S(2)}) collective-permute-start(f16[256,1024]{1,0:T(8,128)(2,1)} %fusion.22), channel_id=1, source_target_pairs={{0,1},{1,0},{2,3},{3,2},{4,5},{5,4},{6,7},{7,6},{8,9},{9,8},{10,11... | collective-permute-start | bytes 1572872 | tf_op jit(solution)/shard_map/ppermute | solution.py:21
  12.0 2.4 %multiply_convert_fusion.1 = f16[512,1024]{1,0:T(8,128)(2,1)S(1)} fusion(bf16[1,896,1024]{2,1,0:T(8,128)(2,1)S(1)} %copy-done, bf16[1,896,4096]{2,1,0:T(8,128)(2,1)} %param.5, s32[]{:T(128)S(6)} %select_n.58), kind=kOutput, calls=%fused_computation.7 | convolution fusion | flops 940572672 | bytes 3801092 | tf_op jit(solution)/shard_map/dot_general | solution.py:65
  14.4 1.2 %fusion.52 = (f16[256,1024]{1,0:T(8,128)(2,1)}, f16[256,1024]{1,0:T(8,128)(2,1)}) fusion(f16[512,1024]{1,0:T(8,128)(2,1)S(1)} %multiply_convert_fusion.1), kind=kLoop, calls=%fused_computation.77 | loop fusion | bytes 2097152 | tf_op jit(solution)/shard_map/slice | solution.py:124
  15.7 0.2 collective-permute-start.4
  15.9 1.2 %collective-permute-start.6 = (f16[256,1024]{1,0:T(8,128)(2,1)}, f16[256,1024]{1,0:T(8,128)(2,1)}, u32[]{:S(2)}, u32[]{:S(2)}) collective-permute-start(f16[256,1024]{1,0:T(8,128)(2,1)} %get-tuple-element.217), channel_id=1, source_target_pairs={{0,1},{1,0},{2,3},{3,2},{4,5},{5,4},{6,7},{7,6},{8,9},{9,8},{10,11... | collective-permute-start | bytes 1572872 | tf_op jit(solution)/shard_map/ppermute | solution.py:21
  17.1 4.2 %bitcast_subtract_fusion.1 = f32[768,1024]{1,0:T(8,128)S(1)} fusion(f32[1,2048,1024]{2,1,0:T(8,128)} %param.4, bf16[1,896,1024]{2,1,0:T(8,128)(2,1)S(1)} %copy-done, bf16[1,896,4096]{2,1,0:T(8,128)(2,1)} %param.5, s32[]{:T(128)S(6)} %select_n.53), kind=kOutput, calls=%fused_computation.2 | convolution fusion | flops 1410859008 | bytes 9502724 | tf_op jit(solution)/shard_map/dot_general | solution.py:65
  21.3 1.6 %copy-done.1 = f32[768,1024]{1,0:T(8,128)} copy-done((f32[768,1024]{1,0:T(8,128)}, f32[768,1024]{1,0:T(8,128)S(1)}, u32[]{:S(2)}) %copy-start.1) | copy-done | bytes 3145752
  22.9 1.0 multiply_convert_fusion.8
  24.0 6.4 %collective-permute-start.2 = (f16[256,1024]{1,0:T(8,128)(2,1)}, f16[256,1024]{1,0:T(8,128)(2,1)}, u32[]{:S(2)}, u32[]{:S(2)}) collective-permute-start(f16[256,1024]{1,0:T(8,128)(2,1)} %multiply_convert_fusion.8), channel_id=1, source_target_pairs={{0,2},{2,0},{4,6},{6,4},{8,10},{10,8},{12,14},{14,12},{16,18},{18,... | collective-permute-start | bytes 1572872 | tf_op jit(solution)/shard_map/ppermute | solution.py:30
  30.4 4.8 %multiply_convert_fusion = f16[1280,1024]{1,0:T(8,128)(2,1)S(1)} fusion(bf16[1,896,4096]{2,1,0:T(8,128)(2,1)} %param.5, s32[]{:T(128)S(6)} %select_n.60, bf16[1,896,1024]{2,1,0:T(8,128)(2,1)S(1)} %copy-done), kind=kOutput, calls=%fused_computation.1 | convolution fusion | flops 2351431680 | bytes 6750212 | tf_op jit(solution)/shard_map/dot_general | solution.py:65
  35.2 0.8 slice.166
  36.0 1.7 %fusion.51 = (f16[256,1024]{1,0:T(8,128)(2,1)}, f16[256,1024]{1,0:T(8,128)(2,1)}, f16[256,1024]{1,0:T(8,128)(2,1)}, f16[256,1024]{1,0:T(8,128)(2,1)}) fusion(f16[1280,1024]{1,0:T(8,128)(2,1)S(1)} %multiply_convert_fusion), kind=kLoop, calls=%fused_computation.76 | loop fusion | bytes 4194304 | tf_op jit(solution)/shard_map/slice | solution.py:148
  37.7 2.4 %multiply_convert_fusion.7 = f16[256,1024]{1,0:T(8,128)(2,1)} fusion(f16[256,1024]{1,0:T(8,128)(2,1)} %collective-permute-done.4, f32[768,1024]{1,0:T(8,128)} %copy-done.1), kind=kLoop, calls=%fused_computation.45 | loop fusion | flops 1310720 | bytes 2097152 | tf_op jit(solution)/shard_map/convert_element_type | solution.py:139
  40.1 3.0 %collective-permute-start.8 = (f16[256,1024]{1,0:T(8,128)(2,1)}, f16[256,1024]{1,0:T(8,128)(2,1)}, u32[]{:S(2)}, u32[]{:S(2)}) collective-permute-start(f16[256,1024]{1,0:T(8,128)(2,1)} %multiply_convert_fusion.7), channel_id=1, source_target_pairs={{0,2},{2,0},{4,6},{6,4},{8,10},{10,8},{12,14},{14,12},{16,18},{18,... | collective-permute-start | bytes 1572872 | tf_op jit(solution)/shard_map/ppermute | solution.py:30
  43.1 1.2 %collective-permute-start.3 = (f16[256,1024]{1,0:T(8,128)(2,1)}, f16[256,1024]{1,0:T(8,128)(2,1)}, u32[]{:S(2)}, u32[]{:S(2)}) collective-permute-start(f16[256,1024]{1,0:T(8,128)(2,1)} %get-tuple-element.118), channel_id=1, source_target_pairs={{0,1},{1,0},{2,3},{3,2},{4,5},{5,4},{6,7},{7,6},{8,9},{9,8},{10,11... | collective-permute-start | bytes 1572872 | tf_op jit(solution)/shard_map/ppermute | solution.py:21
  44.3 0.9 collective-permute-done.7
  45.2 1.2 %collective-permute-start.11 = (f16[256,1024]{1,0:T(8,128)(2,1)}, f16[256,1024]{1,0:T(8,128)(2,1)}, u32[]{:S(2)}, u32[]{:S(2)}) collective-permute-start(f16[256,1024]{1,0:T(8,128)(2,1)} %get-tuple-element.135), channel_id=1, source_target_pairs={{0,1},{1,0},{2,3},{3,2},{4,5},{5,4},{6,7},{7,6},{8,9},{9,8},{10,11... | collective-permute-start | bytes 1572872 | tf_op jit(solution)/shard_map/ppermute | solution.py:21
  46.5 2.4 %multiply_convert_fusion.6 = f16[256,1024]{1,0:T(8,128)(2,1)} fusion(f16[256,1024]{1,0:T(8,128)(2,1)} %collective-permute-done.6, f32[768,1024]{1,0:T(8,128)} %copy-done.1), kind=kLoop, calls=%fused_computation.43 | loop fusion | flops 1310720 | bytes 2097152 | tf_op jit(solution)/shard_map/convert_element_type | solution.py:139
  48.9 4.2 %collective-permute-start.10 = (f16[256,1024]{1,0:T(8,128)(2,1)}, f16[256,1024]{1,0:T(8,128)(2,1)}, u32[]{:S(2)}, u32[]{:S(2)}) collective-permute-start(f16[256,1024]{1,0:T(8,128)(2,1)} %multiply_convert_fusion.6), channel_id=1, source_target_pairs={{0,2},{2,0},{4,6},{6,4},{8,10},{10,8},{12,14},{14,12},{16,18},{18,... | collective-permute-start | bytes 1572872 | tf_op jit(solution)/shard_map/ppermute | solution.py:30
  53.1 7.1 %bitcast_subtract_fusion = f32[1280,1024]{1,0:T(8,128)} fusion(f32[1,2048,1024]{2,1,0:T(8,128)} %param.4, bf16[1,896,4096]{2,1,0:T(8,128)(2,1)} %param.5, s32[]{:T(128)S(6)} %select_n.61, bf16[1,896,1024]{2,1,0:T(8,128)(2,1)S(1)} %copy-done), kind=kOutput, calls=%fused_computation | convolution fusion | flops 2351431680 | bytes 14614532 | tf_op jit(solution)/shard_map/dot_general | solution.py:65
  60.2 0.1 fusion.50
  60.3 0.2 multiply_reduce_fusion
  60.5 0.1 broadcast_in_dim.22
  60.6 0.2 collective-permute-start.14
  60.8 4.0 %collective-permute-done.9 = f16[256,1024]{1,0:T(8,128)(2,1)} collective-permute-done((f16[256,1024]{1,0:T(8,128)(2,1)}, f16[256,1024]{1,0:T(8,128)(2,1)}, u32[]{:S(2)}, u32[]{:S(2)}) %collective-permute-start.9) | collective-permute-done | bytes 524320 | tf_op jit(solution)/shard_map/ppermute | solution.py:30
  64.8 1.7 %multiply_convert_fusion.5 = f16[256,1024]{1,0:T(8,128)(2,1)S(1)} fusion(f16[256,1024]{1,0:T(8,128)(2,1)} %collective-permute-done.3, f32[1280,1024]{1,0:T(8,128)} %bitcast_subtract_fusion), kind=kLoop, calls=%fused_computation.41 | loop fusion | flops 1310720 | bytes 2097152 | tf_op jit(solution)/shard_map/convert_element_type | solution.py:139
  66.6 0.1 collective-permute-start.13
  66.6 0.1 collective-permute-start.15
  66.7 1.1 broadcast_in_dim.21
  67.8 2.4 %multiply_add_fusion = (f32[256,1024]{1,0:T(8,128)S(1)}, f32[2048,1024]{1,0:T(8,128)S(1)}) fusion(f16[256,1024]{1,0:T(8,128)(2,1)} %collective-permute-done.5, f32[256,1024]{1,0:T(8,128)S(1)} %get-tuple-element.163, f16[256,1024]{1,0:T(8,128)(2,1)} %collective-permute-done.1, f32[1024]{0:T(1024)S(1)} %bitcast.79, f32[1024]{0:T(1024)S(1)} %bitcast.87, ...), kind=kLoop, calls=%fused_computation.39 | loop fusion | flops 4456448 | bytes 6828032 | tf_op jit(solution)/shard_map/add | solution.py:90
  70.2 0.1 fusion.36
  70.4 0.3 slice-done.1
  70.7 1.2 %multiply_convert_fusion.4 = f16[256,1024]{1,0:T(8,128)(2,1)S(1)} fusion(f16[256,1024]{1,0:T(8,128)(2,1)} %collective-permute-done.11, f32[1280,1024]{1,0:T(8,128)S(1)} %bitcast.69), kind=kLoop, calls=%fused_computation.37 | loop fusion | flops 1310720 | bytes 2097152 | tf_op jit(solution)/shard_map/convert_element_type | solution.py:139
  71.9 1.1 collective-permute-start.16
  73.0 1.2 %collective-permute-start.17 = (f16[256,1024]{1,0:T(8,128)(2,1)S(1)}, f16[256,1024]{1,0:T(8,128)(2,1)S(1)}, u32[]{:S(2)}, u32[]{:S(2)}) collective-permute-start(f16[256,1024]{1,0:T(8,128)(2,1)S(1)} %copy-done.4), channel_id=1, source_target_pairs={{0,1},{1,0},{2,3},{3,2},{4,5},{5,4},{6,7},{7,6},{8,9},{9,8},{10,11... | collective-permute-start | bytes 1572872 | tf_op jit(solution)/shard_map/ppermute | solution.py:21
  74.2 0.7 collective-permute-start.18
  74.9 4.9 %collective-permute-done.14 = f16[256,1024]{1,0:T(8,128)(2,1)S(1)} collective-permute-done((f16[256,1024]{1,0:T(8,128)(2,1)}, f16[256,1024]{1,0:T(8,128)(2,1)S(1)}, u32[]{:S(2)}, u32[]{:S(2)}) %collective-permute-start.14) | collective-permute-done | bytes 524320 | tf_op jit(solution)/shard_map/ppermute | solution.py:21
  79.8 7.4 %collective-permute-done.15 = f16[256,1024]{1,0:T(8,128)(2,1)S(1)} collective-permute-done((f16[256,1024]{1,0:T(8,128)(2,1)S(1)}, f16[256,1024]{1,0:T(8,128)(2,1)S(1)}, u32[]{:S(2)}, u32[]{:S(2)}) %collective-permute-start.15) | collective-permute-done | bytes 524320 | tf_op jit(solution)/shard_map/ppermute | solution.py:30
  87.1 1.8 %add_dynamic-update-slice_fusion.2 = f32[2048,1024]{1,0:T(8,128)S(1)} fusion(f32[2048,1024]{1,0:T(8,128)S(1)} %get-tuple-element.173, f16[256,1024]{1,0:T(8,128)(2,1)} %collective-permute-done.9, f32[768,1024]{1,0:T(8,128)S(1)} %copy-done.2, f16[256,1024]{1,0:T(8,128)(2,1)} %collective-permute-done.8, f16[256,1024]{1,0:T(8,128)(2,1)} %collective-permute-done.4, ...), kind=kLoop, calls=%fused_computation.36 | loop fusion | flops 2621440 | bytes 3682304 | tf_op jit(solution)/shard_map/dynamic_update_slice | solution.py:97
  88.9 0.2 multiply_convert_fusion.3
  89.2 0.6 collective-permute-start.20
  89.8 1.8 %add_dynamic-update-slice_fusion.1 = f32[2048,1024]{1,0:T(8,128)S(1)} fusion(f32[2048,1024]{1,0:T(8,128)S(1)} %add_dynamic-update-slice_fusion.2, f16[256,1024]{1,0:T(8,128)(2,1)} %collective-permute-done.12, f32[768,1024]{1,0:T(8,128)S(1)} %copy-done.2, f16[256,1024]{1,0:T(8,128)(2,1)} %collective-permute-done.10, ...), kind=kLoop, calls=%fused_computation.33 | loop fusion | flops 2621440 | bytes 3682304 | tf_op jit(solution)/shard_map/dynamic_update_slice | solution.py:97
  91.6 0.9 collective-permute-done.18
  92.5 0.2 multiply_convert_fusion.2
  92.8 0.5 collective-permute-start.22
  93.2 2.0 %collective-permute-start.24 = (f16[128,1024]{1,0:T(8,128)(2,1)S(1)}, f16[128,1024]{1,0:T(8,128)(2,1)S(1)}, u32[]{:S(2)}, u32[]{:S(2)}) collective-permute-start(f16[128,1024]{1,0:T(8,128)(2,1)S(1)} %get-tuple-element.209), channel_id=1, source_target_pairs={{0,1},{1,0},{2,3},{3,2},{4,5},{5,4},{6,7},{7,6},{8,9},{9,8},{10,11... | collective-permute-start | bytes 786440 | tf_op jit(solution)/shard_map/ppermute | solution.py:21
  95.2 0.6 collective-permute-start.23
  95.8 1.6 %collective-permute-done.20 = f16[128,1024]{1,0:T(8,128)(2,1)S(1)} collective-permute-done((f16[128,1024]{1,0:T(8,128)(2,1)S(1)}, f16[128,1024]{1,0:T(8,128)(2,1)S(1)}, u32[]{:S(2)}, u32[]{:S(2)}) %collective-permute-start.20) | collective-permute-done | bytes 262176 | tf_op jit(solution)/shard_map/ppermute | solution.py:21
  97.4 12.3 %collective-permute-done.21 = f16[256,1024]{1,0:T(8,128)(2,1)S(1)} collective-permute-done((f16[256,1024]{1,0:T(8,128)(2,1)S(1)}, f16[256,1024]{1,0:T(8,128)(2,1)S(1)}, u32[]{:S(2)}, u32[]{:S(2)}) %collective-permute-start.21) | collective-permute-done | bytes 524320 | tf_op jit(solution)/shard_map/ppermute | solution.py:30
  109.7 1.5 %add_dynamic-update-slice_fusion = f32[2048,1024]{1,0:T(8,128)S(1)} fusion(f32[2048,1024]{1,0:T(8,128)S(1)} %add_dynamic-update-slice_fusion.1, f16[256,1024]{1,0:T(8,128)(2,1)S(1)} %collective-permute-done.15, f32[1280,1024]{1,0:T(8,128)S(1)} %bitcast.69, f16[256,1024]{1,0:T(8,128)(2,1)S(1)} %collective-permute-done.13, ...), kind=kLoop, calls=%fused_computation.30 | loop fusion | flops 2621440 | bytes 3682304 | tf_op jit(solution)/shard_map/dynamic_update_slice | solution.py:97
  111.1 0.1 multiply_convert_fusion.10
  111.4 1.5 %bitcast_dynamic-update-slice_fusion.2 = f32[1,2048,1024]{2,1,0:T(8,128)S(1)} fusion(f32[1,2048,1024]{2,1,0:T(8,128)S(1)} %bitcast.70, f16[256,1024]{1,0:T(8,128)(2,1)S(1)} %collective-permute-done.18, f32[1280,1024]{1,0:T(8,128)S(1)} %bitcast.69, f16[256,1024]{1,0:T(8,128)(2,1)S(1)} %collective-permute-done.16, ...), kind=kLoop, calls=%fused_computation.29 | loop fusion | flops 2621440 | bytes 3682304 | tf_op jit(solution)/shard_map/dynamic_update_slice | solution.py:97
  112.9 0.4 bitcast_dynamic-update-slice_fusion.1
  113.3 2.0 %collective-permute-done.23 = f16[256,1024]{1,0:T(8,128)(2,1)S(1)} collective-permute-done((f16[256,1024]{1,0:T(8,128)(2,1)S(1)}, f16[256,1024]{1,0:T(8,128)(2,1)S(1)}, u32[]{:S(2)}, u32[]{:S(2)}) %collective-permute-start.23) | collective-permute-done | bytes 524320 | tf_op jit(solution)/shard_map/ppermute | solution.py:30
  115.3 0.4 bitcast_dynamic-update-slice_fusion
  115.7 0.1 bitcast_dynamic-update-slice_fusion.4
  115.8 5.1 %collective-permute-done.26 = f16[128,1024]{1,0:T(8,128)(2,1)S(1)} collective-permute-done((f16[128,1024]{1,0:T(8,128)(2,1)S(1)}, f16[128,1024]{1,0:T(8,128)(2,1)S(1)}, u32[]{:S(2)}, u32[]{:S(2)}) %collective-permute-start.26) | collective-permute-done | bytes 262176 | tf_op jit(solution)/shard_map/ppermute | solution.py:30
  120.9 1.0 bitcast_dynamic-update-slice_fusion.3
  (44 shorter events, 0.5 us)
Async XLA Ops:
  0.0 1.5 %copy-start = (bf16[1,896,1024]{2,1,0:T(8,128)(2,1)S(1)}, bf16[1,896,1024]{2,1,0:T(8,128)(2,1)}, u32[]{:S(2)}) copy-start(bf16[1,896,1024]{2,1,0:T(8,128)(2,1)} %param.6) | copy-start | bytes 5505028
  8.1 13.2 %collective-permute-start.1 = (f16[256,1024]{1,0:T(8,128)(2,1)}, f16[256,1024]{1,0:T(8,128)(2,1)}, u32[]{:S(2)}, u32[]{:S(2)}) collective-permute-start(f16[256,1024]{1,0:T(8,128)(2,1)} %get-tuple-element.114), channel_id=1, source_target_pairs={{0,2},{2,0},{4,6},{6,4},{8,10},{10,8},{12,14},{14,12},{16,18},{18,... | collective-permute-start | bytes 1572872 | tf_op jit(solution)/shard_map/ppermute | solution.py:30
  8.2 29.5 %collective-permute-start.5 = (f16[256,1024]{1,0:T(8,128)(2,1)}, f16[256,1024]{1,0:T(8,128)(2,1)}, u32[]{:S(2)}, u32[]{:S(2)}) collective-permute-start(f16[256,1024]{1,0:T(8,128)(2,1)} %get-tuple-element.114), channel_id=1, source_target_pairs={{2,4},{4,2},{6,8},{8,6},{10,12},{12,10},{14,16},{16,14},{18,20},{2... | collective-permute-start | bytes 1572872 | tf_op jit(solution)/shard_map/ppermute | solution.py:30
  10.7 10.6 %collective-permute-start = (f16[256,1024]{1,0:T(8,128)(2,1)}, f16[256,1024]{1,0:T(8,128)(2,1)S(1)}, u32[]{:S(2)}, u32[]{:S(2)}) collective-permute-start(f16[256,1024]{1,0:T(8,128)(2,1)} %fusion.22), channel_id=1, source_target_pairs={{0,1},{1,0},{2,3},{3,2},{4,5},{5,4},{6,7},{7,6},{8,9},{9,8},{10,11... | collective-permute-start | bytes 1572872 | tf_op jit(solution)/shard_map/ppermute | solution.py:21
  15.7 22.0 %collective-permute-start.4 = (f16[256,1024]{1,0:T(8,128)(2,1)}, f16[256,1024]{1,0:T(8,128)(2,1)}, u32[]{:S(2)}, u32[]{:S(2)}) collective-permute-start(f16[256,1024]{1,0:T(8,128)(2,1)} %get-tuple-element.218), channel_id=1, source_target_pairs={{0,1},{1,0},{2,3},{3,2},{4,5},{5,4},{6,7},{7,6},{8,9},{9,8},{10,11... | collective-permute-start | bytes 1572872 | tf_op jit(solution)/shard_map/ppermute | solution.py:21
  15.9 28.4 %collective-permute-start.6 = (f16[256,1024]{1,0:T(8,128)(2,1)}, f16[256,1024]{1,0:T(8,128)(2,1)}, u32[]{:S(2)}, u32[]{:S(2)}) collective-permute-start(f16[256,1024]{1,0:T(8,128)(2,1)} %get-tuple-element.217), channel_id=1, source_target_pairs={{0,1},{1,0},{2,3},{3,2},{4,5},{5,4},{6,7},{7,6},{8,9},{9,8},{10,11... | collective-permute-start | bytes 1572872 | tf_op jit(solution)/shard_map/ppermute | solution.py:21
  21.3 1.6 %copy-start.1 = (f32[768,1024]{1,0:T(8,128)}, f32[768,1024]{1,0:T(8,128)S(1)}, u32[]{:S(2)}) copy-start(f32[768,1024]{1,0:T(8,128)S(1)} %bitcast_subtract_fusion.1) | copy-start | bytes 9437188
  24.0 13.7 %collective-permute-start.2 = (f16[256,1024]{1,0:T(8,128)(2,1)}, f16[256,1024]{1,0:T(8,128)(2,1)}, u32[]{:S(2)}, u32[]{:S(2)}) collective-permute-start(f16[256,1024]{1,0:T(8,128)(2,1)} %multiply_convert_fusion.8), channel_id=1, source_target_pairs={{0,2},{2,0},{4,6},{6,4},{8,10},{10,8},{12,14},{14,12},{16,18},{18,... | collective-permute-start | bytes 1572872 | tf_op jit(solution)/shard_map/ppermute | solution.py:30
  30.4 14.8 %collective-permute-start.7 = (f16[256,1024]{1,0:T(8,128)(2,1)}, f16[256,1024]{1,0:T(8,128)(2,1)}, u32[]{:S(2)}, u32[]{:S(2)}) collective-permute-start(f16[256,1024]{1,0:T(8,128)(2,1)} %multiply_convert_fusion.8), channel_id=1, source_target_pairs={{2,4},{4,2},{6,8},{8,6},{10,12},{12,10},{14,16},{16,14},{18,20},{2... | collective-permute-start | bytes 1572872 | tf_op jit(solution)/shard_map/ppermute | solution.py:30
  40.1 6.4 %collective-permute-start.8 = (f16[256,1024]{1,0:T(8,128)(2,1)}, f16[256,1024]{1,0:T(8,128)(2,1)}, u32[]{:S(2)}, u32[]{:S(2)}) collective-permute-start(f16[256,1024]{1,0:T(8,128)(2,1)} %multiply_convert_fusion.7), channel_id=1, source_target_pairs={{0,2},{2,0},{4,6},{6,4},{8,10},{10,8},{12,14},{14,12},{16,18},{18,... | collective-permute-start | bytes 1572872 | tf_op jit(solution)/shard_map/ppermute | solution.py:30
  43.1 17.5 %collective-permute-start.3 = (f16[256,1024]{1,0:T(8,128)(2,1)}, f16[256,1024]{1,0:T(8,128)(2,1)}, u32[]{:S(2)}, u32[]{:S(2)}) collective-permute-start(f16[256,1024]{1,0:T(8,128)(2,1)} %get-tuple-element.118), channel_id=1, source_target_pairs={{0,1},{1,0},{2,3},{3,2},{4,5},{5,4},{6,7},{7,6},{8,9},{9,8},{10,11... | collective-permute-start | bytes 1572872 | tf_op jit(solution)/shard_map/ppermute | solution.py:21
  44.3 20.5 %collective-permute-start.9 = (f16[256,1024]{1,0:T(8,128)(2,1)}, f16[256,1024]{1,0:T(8,128)(2,1)}, u32[]{:S(2)}, u32[]{:S(2)}) collective-permute-start(f16[256,1024]{1,0:T(8,128)(2,1)} %multiply_convert_fusion.7), channel_id=1, source_target_pairs={{2,4},{4,2},{6,8},{8,6},{10,12},{12,10},{14,16},{16,14},{18,20},{2... | collective-permute-start | bytes 1572872 | tf_op jit(solution)/shard_map/ppermute | solution.py:30
  45.2 25.1 %collective-permute-start.11 = (f16[256,1024]{1,0:T(8,128)(2,1)}, f16[256,1024]{1,0:T(8,128)(2,1)}, u32[]{:S(2)}, u32[]{:S(2)}) collective-permute-start(f16[256,1024]{1,0:T(8,128)(2,1)} %get-tuple-element.135), channel_id=1, source_target_pairs={{0,1},{1,0},{2,3},{3,2},{4,5},{5,4},{6,7},{7,6},{8,9},{9,8},{10,11... | collective-permute-start | bytes 1572872 | tf_op jit(solution)/shard_map/ppermute | solution.py:21
  48.9 15.9 %collective-permute-start.10 = (f16[256,1024]{1,0:T(8,128)(2,1)}, f16[256,1024]{1,0:T(8,128)(2,1)}, u32[]{:S(2)}, u32[]{:S(2)}) collective-permute-start(f16[256,1024]{1,0:T(8,128)(2,1)} %multiply_convert_fusion.6), channel_id=1, source_target_pairs={{0,2},{2,0},{4,6},{6,4},{8,10},{10,8},{12,14},{14,12},{16,18},{18,... | collective-permute-start | bytes 1572872 | tf_op jit(solution)/shard_map/ppermute | solution.py:30
  53.1 17.3 %collective-permute-start.12 = (f16[256,1024]{1,0:T(8,128)(2,1)}, f16[256,1024]{1,0:T(8,128)(2,1)}, u32[]{:S(2)}, u32[]{:S(2)}) collective-permute-start(f16[256,1024]{1,0:T(8,128)(2,1)} %multiply_convert_fusion.6), channel_id=1, source_target_pairs={{2,4},{4,2},{6,8},{8,6},{10,12},{12,10},{14,16},{16,14},{18,20},{2... | collective-permute-start | bytes 1572872 | tf_op jit(solution)/shard_map/ppermute | solution.py:30
  53.1 7.1 %copy-start.6 = (s32[16,3]{0,1:T(4,128)S(1)}, s32[16,3]{0,1:T(4,128)}, u32[]{:S(2)}) copy-start(s32[16,3]{0,1:T(4,128)} %param.7) | copy-start | bytes 580
  60.6 19.2 %collective-permute-start.14 = (f16[256,1024]{1,0:T(8,128)(2,1)}, f16[256,1024]{1,0:T(8,128)(2,1)S(1)}, u32[]{:S(2)}, u32[]{:S(2)}) collective-permute-start(f16[256,1024]{1,0:T(8,128)(2,1)} %get-tuple-element.140), channel_id=1, source_target_pairs={{0,1},{1,0},{2,3},{3,2},{4,5},{5,4},{6,7},{7,6},{8,9},{9,8},{10,11... | collective-permute-start | bytes 1572872 | tf_op jit(solution)/shard_map/ppermute | solution.py:21
  64.8 3.0 %copy-start.2 = (f32[768,1024]{1,0:T(8,128)S(1)}, f32[768,1024]{1,0:T(8,128)}, u32[]{:S(2)}) copy-start(f32[768,1024]{1,0:T(8,128)} %copy-done.1) | copy-start | bytes 9437188
  66.6 3.8 %collective-permute-start.13 = (f16[256,1024]{1,0:T(8,128)(2,1)S(1)}, f16[256,1024]{1,0:T(8,128)(2,1)S(1)}, u32[]{:S(2)}, u32[]{:S(2)}) collective-permute-start(f16[256,1024]{1,0:T(8,128)(2,1)S(1)} %multiply_convert_fusion.5), channel_id=1, source_target_pairs={{0,2},{2,0},{4,6},{6,4},{8,10},{10,8},{12,14},{14,12},{16,18},{18,... | collective-permute-start | bytes 1572872 | tf_op jit(solution)/shard_map/ppermute | solution.py:30
  66.6 20.5 %collective-permute-start.15 = (f16[256,1024]{1,0:T(8,128)(2,1)S(1)}, f16[256,1024]{1,0:T(8,128)(2,1)S(1)}, u32[]{:S(2)}, u32[]{:S(2)}) collective-permute-start(f16[256,1024]{1,0:T(8,128)(2,1)S(1)} %multiply_convert_fusion.5), channel_id=1, source_target_pairs={{2,4},{4,2},{6,8},{8,6},{10,12},{12,10},{14,16},{16,14},{18,20},{2... | collective-permute-start | bytes 1572872 | tf_op jit(solution)/shard_map/ppermute | solution.py:30
  66.7 3.7 %slice-start = ((s8[5242880]{0:T(1024)(128)(4,1)}), s8[1048576]{0:T(1024)(128)(4,1)S(1)}, s32[]{:S(2)}) async-start(s8[5242880]{0:T(1024)(128)(4,1)} %bitcast.68), calls=%async_computation | async-start | bytes 2097152
  67.8 2.9 %slice-start.1 = ((s8[5242880]{0:T(1024)(128)(4,1)}), s8[4194304]{0:T(1024)(128)(4,1)S(1)}, s32[]{:S(2)}) async-start(s8[5242880]{0:T(1024)(128)(4,1)} %bitcast.68), calls=%async_computation.1 | async-start | bytes 8388608
  67.8 5.2 %copy-start.4 = (f16[256,1024]{1,0:T(8,128)(2,1)S(1)}, f16[256,1024]{1,0:T(8,128)(2,1)}, u32[]{:S(2)}) copy-start(f16[256,1024]{1,0:T(8,128)(2,1)} %get-tuple-element.180) | copy-start | bytes 1572868
  70.2 19.0 %copy-start.5 = (f16[128,1024]{1,0:T(8,128)(2,1)S(1)}, f16[128,1024]{1,0:T(8,128)(2,1)}, u32[]{:S(2)}) copy-start(f16[128,1024]{1,0:T(8,128)(2,1)} %slice.166) | copy-start | bytes 786436
  71.9 17.0 %collective-permute-start.16 = (f16[256,1024]{1,0:T(8,128)(2,1)S(1)}, f16[256,1024]{1,0:T(8,128)(2,1)S(1)}, u32[]{:S(2)}, u32[]{:S(2)}) collective-permute-start(f16[256,1024]{1,0:T(8,128)(2,1)S(1)} %multiply_convert_fusion.4), channel_id=1, source_target_pairs={{0,2},{2,0},{4,6},{6,4},{8,10},{10,8},{12,14},{14,12},{16,18},{18,... | collective-permute-start | bytes 1572872 | tf_op jit(solution)/shard_map/ppermute | solution.py:30
  73.0 18.6 %collective-permute-start.17 = (f16[256,1024]{1,0:T(8,128)(2,1)S(1)}, f16[256,1024]{1,0:T(8,128)(2,1)S(1)}, u32[]{:S(2)}, u32[]{:S(2)}) collective-permute-start(f16[256,1024]{1,0:T(8,128)(2,1)S(1)} %copy-done.4), channel_id=1, source_target_pairs={{0,1},{1,0},{2,3},{3,2},{4,5},{5,4},{6,7},{7,6},{8,9},{9,8},{10,11... | collective-permute-start | bytes 1572872 | tf_op jit(solution)/shard_map/ppermute | solution.py:21
  74.2 18.3 %collective-permute-start.18 = (f16[256,1024]{1,0:T(8,128)(2,1)S(1)}, f16[256,1024]{1,0:T(8,128)(2,1)S(1)}, u32[]{:S(2)}, u32[]{:S(2)}) collective-permute-start(f16[256,1024]{1,0:T(8,128)(2,1)S(1)} %multiply_convert_fusion.4), channel_id=1, source_target_pairs={{2,4},{4,2},{6,8},{8,6},{10,12},{12,10},{14,16},{16,14},{18,20},{2... | collective-permute-start | bytes 1572872 | tf_op jit(solution)/shard_map/ppermute | solution.py:30
  89.1 3.4 %collective-permute-start.19 = (f16[256,1024]{1,0:T(8,128)(2,1)S(1)}, f16[256,1024]{1,0:T(8,128)(2,1)S(1)}, u32[]{:S(2)}, u32[]{:S(2)}) collective-permute-start(f16[256,1024]{1,0:T(8,128)(2,1)S(1)} %multiply_convert_fusion.3), channel_id=1, source_target_pairs={{0,2},{2,0},{4,6},{6,4},{8,10},{10,8},{12,14},{14,12},{16,18},{18,... | collective-permute-start | bytes 1572872 | tf_op jit(solution)/shard_map/ppermute | solution.py:30
  89.2 8.1 %collective-permute-start.20 = (f16[128,1024]{1,0:T(8,128)(2,1)S(1)}, f16[128,1024]{1,0:T(8,128)(2,1)S(1)}, u32[]{:S(2)}, u32[]{:S(2)}) collective-permute-start(f16[128,1024]{1,0:T(8,128)(2,1)S(1)} %copy-done.5), channel_id=1, source_target_pairs={{0,1},{1,0},{2,3},{3,2},{4,5},{5,4},{6,7},{7,6},{8,9},{9,8},{10,11... | collective-permute-start | bytes 786440 | tf_op jit(solution)/shard_map/ppermute | solution.py:21
  89.8 19.8 %collective-permute-start.21 = (f16[256,1024]{1,0:T(8,128)(2,1)S(1)}, f16[256,1024]{1,0:T(8,128)(2,1)S(1)}, u32[]{:S(2)}, u32[]{:S(2)}) collective-permute-start(f16[256,1024]{1,0:T(8,128)(2,1)S(1)} %multiply_convert_fusion.3), channel_id=1, source_target_pairs={{2,4},{4,2},{6,8},{8,6},{10,12},{12,10},{14,16},{16,14},{18,20},{2... | collective-permute-start | bytes 1572872 | tf_op jit(solution)/shard_map/ppermute | solution.py:30
  92.8 18.4 %collective-permute-start.22 = (f16[256,1024]{1,0:T(8,128)(2,1)S(1)}, f16[256,1024]{1,0:T(8,128)(2,1)S(1)}, u32[]{:S(2)}, u32[]{:S(2)}) collective-permute-start(f16[256,1024]{1,0:T(8,128)(2,1)S(1)} %multiply_convert_fusion.2), channel_id=1, source_target_pairs={{0,2},{2,0},{4,6},{6,4},{8,10},{10,8},{12,14},{14,12},{16,18},{18,... | collective-permute-start | bytes 1572872 | tf_op jit(solution)/shard_map/ppermute | solution.py:30
  93.2 22.5 %collective-permute-start.24 = (f16[128,1024]{1,0:T(8,128)(2,1)S(1)}, f16[128,1024]{1,0:T(8,128)(2,1)S(1)}, u32[]{:S(2)}, u32[]{:S(2)}) collective-permute-start(f16[128,1024]{1,0:T(8,128)(2,1)S(1)} %get-tuple-element.209), channel_id=1, source_target_pairs={{0,1},{1,0},{2,3},{3,2},{4,5},{5,4},{6,7},{7,6},{8,9},{9,8},{10,11... | collective-permute-start | bytes 786440 | tf_op jit(solution)/shard_map/ppermute | solution.py:21
  95.2 20.1 %collective-permute-start.23 = (f16[256,1024]{1,0:T(8,128)(2,1)S(1)}, f16[256,1024]{1,0:T(8,128)(2,1)S(1)}, u32[]{:S(2)}, u32[]{:S(2)}) collective-permute-start(f16[256,1024]{1,0:T(8,128)(2,1)S(1)} %multiply_convert_fusion.2), channel_id=1, source_target_pairs={{2,4},{4,2},{6,8},{8,6},{10,12},{12,10},{14,16},{16,14},{18,20},{2... | collective-permute-start | bytes 1572872 | tf_op jit(solution)/shard_map/ppermute | solution.py:30
  111.2 4.6 %collective-permute-start.25 = (f16[128,1024]{1,0:T(8,128)(2,1)S(1)}, f16[128,1024]{1,0:T(8,128)(2,1)S(1)}, u32[]{:S(2)}, u32[]{:S(2)}) collective-permute-start(f16[128,1024]{1,0:T(8,128)(2,1)S(1)} %multiply_convert_fusion.10), channel_id=1, source_target_pairs={{0,2},{2,0},{4,6},{6,4},{8,10},{10,8},{12,14},{14,12},{16,18},{18,... | collective-permute-start | bytes 786440 | tf_op jit(solution)/shard_map/ppermute | solution.py:30
  111.3 9.6 %collective-permute-start.26 = (f16[128,1024]{1,0:T(8,128)(2,1)S(1)}, f16[128,1024]{1,0:T(8,128)(2,1)S(1)}, u32[]{:S(2)}, u32[]{:S(2)}) collective-permute-start(f16[128,1024]{1,0:T(8,128)(2,1)S(1)} %multiply_convert_fusion.10), channel_id=1, source_target_pairs={{2,4},{4,2},{6,8},{8,6},{10,12},{12,10},{14,16},{16,14},{18,20},{2... | collective-permute-start | bytes 786440 | tf_op jit(solution)/shard_map/ppermute | solution.py:30
  115.8 5.1 %copy-start.3 = (f32[1,2048,1024]{2,1,0:T(8,128)}, f32[1,2048,1024]{2,1,0:T(8,128)S(1)}, u32[]{:S(2)}) copy-start(f32[1,2048,1024]{2,1,0:T(8,128)S(1)} %bitcast_dynamic-update-slice_fusion.4) | copy-start | bytes 25165828

commit v20 on v14

--- a/solution.py
+++ b/solution.py
@@ -12,7 +12,7 @@
 STEP = 256
 FIRST = 256
 AHEAD = 3
-MIXLAG = 99
+MIXLAG = 5
 
 
 def from_behind(value, axis, steps):

time: 121 us -> 121 us (level)
  waiting for transfers between devices: 51.8 us -> 54.2 us
  starting transfers between devices: 22.6 us -> 20.2 us
    ppermute x16, starting transfers between devices: 15.7 us -> 13.3 us  [swapped(): return lax.ppermute(value, axis, pairs)]
    ppermute x16, waiting for transfers between devices: 19.9 us -> 21.4 us  [swapped(): return lax.ppermute(value, axis, pairs)]
  transfers between devices with their start and end apart: 24 -> 24, of which waited for: 12 -> 13; matrix products, arithmetic and copies ran while one was open for 30% -> 30% of each run, Pallas kernels for 0% -> 0%
where the time goes in v20:
time: 121 us; the launch traced here: 120 us
  waiting for transfers between devices  54.2 us (45%)
  matrix products  22.2 us (18%)
  starting transfers between devices  20.2 us (17%)
  other arithmetic  18.3 us (15%)
  local copies, waits for them, and re-layouts  4.87 us (4%)
    ppermute x8, waiting for transfers between devices, from_behind(): return lax.ppermute(value, axis, pairs)  32.8 us
    dot_general x6, matrix products, partial(): lax.dot_general(block, cot_local, (((0,), (0,)), ((), ())), preferred_ele...  22.2 us
    ppermute x16, waiting for transfers between devices, swapped(): return lax.ppermute(value, axis, pairs)  21.4 us
    ppermute x16, starting transfers between devices, swapped(): return lax.ppermute(value, axis, pairs)  13.3 us
    dynamic_update_slice x7, other arithmetic, mix_into(): return lax.dynamic_update_slice_in_dim(out, value, cuts[chunk], axis=0)  7.31 us
    ppermute x8, starting transfers between devices, from_behind(): return lax.ppermute(value, axis, pairs)  6.87 us
    convert_element_type x7, other arithmetic, on_device(): sent = (u_of(chunk) * scale).astype(WIRE)  5.33 us
    add x1, other arithmetic, mixture(): coeff[0:1] * (near.astype(jnp.float32) / scale) + coeff[1:2] * own  2.87 us
  transfers between devices with their start and end apart: 24, of which 13 were waited for; matrix products, arithmetic and copies ran while one was open for 30% of the time, Pallas kernels for 0%

profile of v20, /device:TPU:1, one launch (start us, length us, event | category | flops | bytes accessed | tf_op | source)
XLA Modules:
  0.0 120.1 jit_solution(3520732776285793075)
XLA Ops:
  0.0 1.5 %copy-done = bf16[1,896,1024]{2,1,0:T(8,128)(2,1)S(1)} copy-done((bf16[1,896,1024]{2,1,0:T(8,128)(2,1)S(1)}, bf16[1,896,1024]{2,1,0:T(8,128)(2,1)}, u32[]{:S(2)}) %copy-start) | copy-done | bytes 1835032
  1.5 1.7 %fusion.22 = f32[256,1024]{1,0:T(8,128)S(1)} fusion(bf16[1,896,1024]{2,1,0:T(8,128)(2,1)S(1)} %copy-done, bf16[1,896,4096]{2,1,0:T(8,128)(2,1)} %param.5, s32[]{:T(128)S(6)} %select_n.45), kind=kOutput, calls=%fused_computation.22 | convolution fusion | flops 470024192 | bytes 3342340 | tf_op jit(solution)/shard_map/dot_general | solution.py:65
  3.2 2.1 %fusion.19 = f32[256,1024]{1,0:T(8,128)S(1)} fusion(bf16[1,896,1024]{2,1,0:T(8,128)(2,1)S(1)} %copy-done, f32[1,2048,1024]{2,1,0:T(8,128)} %param.4, bf16[1,896,4096]{2,1,0:T(8,128)(2,1)} %param.5, s32[]{:T(128)S(6)} %select_n.43), kind=kOutput, calls=%fused_computation.21 | convolution fusion | flops 470286336 | bytes 4390916 | tf_op jit(solution)/shard_map/dot_general | solution.py:65
  5.4 2.1 %multiply_convert_fusion.1 = (f16[512,1024]{1,0:T(8,128)(2,1)}, f32[512,1024]{1,0:T(8,128)}) fusion(f32[256,1024]{1,0:T(8,128)S(1)} %fusion.22, f32[256,1024]{1,0:T(8,128)S(1)} %fusion.19), kind=kLoop, calls=%fused_computation.9 | loop fusion | flops 1572864 | bytes 5242880 | tf_op jit(solution)/shard_map/convert_element_type | solution.py:110
  7.5 2.6 %collective-permute-start.3 = (f16[512,1024]{1,0:T(8,128)(2,1)}, f16[512,1024]{1,0:T(8,128)(2,1)}, u32[]{:S(2)}, u32[]{:S(2)}) collective-permute-start(f16[512,1024]{1,0:T(8,128)(2,1)} %get-tuple-element.93), channel_id=1, source_target_pairs={{2,4},{4,2},{6,8},{8,6},{10,12},{12,10},{14,16},{16,14},{18,20},{2... | collective-permute-start | bytes 3145736 | tf_op jit(solution)/shard_map/ppermute | solution.py:30
  10.1 2.9 %collective-permute-start.2 = (f16[512,1024]{1,0:T(8,128)(2,1)}, f16[512,1024]{1,0:T(8,128)(2,1)}, u32[]{:S(2)}, u32[]{:S(2)}) collective-permute-start(f16[512,1024]{1,0:T(8,128)(2,1)} %get-tuple-element.93), channel_id=1, source_target_pairs={{0,2},{2,0},{4,6},{6,4},{8,10},{10,8},{12,14},{14,12},{16,18},{18,... | collective-permute-start | bytes 3145736 | tf_op jit(solution)/shard_map/ppermute | solution.py:30
  13.0 2.5 %fusion.28 = f16[256,1024]{1,0:T(8,128)(2,1)} fusion(bf16[1,896,1024]{2,1,0:T(8,128)(2,1)S(1)} %copy-done, bf16[1,896,4096]{2,1,0:T(8,128)(2,1)} %param.5, s32[]{:T(128)S(6)} %select_n.48), kind=kOutput, calls=%fused_computation.24 | convolution fusion | flops 470286336 | bytes 2818052 | tf_op jit(solution)/shard_map/dot_general | solution.py:65
  15.5 1.2 %collective-permute-start.1 = (f16[256,1024]{1,0:T(8,128)(2,1)}, f16[256,1024]{1,0:T(8,128)(2,1)S(1)}, u32[]{:S(2)}, u32[]{:S(2)}) collective-permute-start(f16[256,1024]{1,0:T(8,128)(2,1)} %fusion.28), channel_id=1, source_target_pairs={{0,1},{1,0},{2,3},{3,2},{4,5},{5,4},{6,7},{7,6},{8,9},{9,8},{10,11... | collective-permute-start | bytes 1572872 | tf_op jit(solution)/shard_map/ppermute | solution.py:21
  16.8 5.5 %multiply_convert_fusion = f16[1536,1024]{1,0:T(8,128)(2,1)S(1)} fusion(bf16[1,896,4096]{2,1,0:T(8,128)(2,1)} %param.5, s32[]{:T(128)S(6)} %select_n.47, bf16[1,896,1024]{2,1,0:T(8,128)(2,1)S(1)} %copy-done), kind=kOutput, calls=%fused_computation | convolution fusion | flops 2821718016 | bytes 7733252 | tf_op jit(solution)/shard_map/dot_general | solution.py:65
  22.2 2.2 %fusion.47 = (f16[256,1024]{1,0:T(8,128)(2,1)}, f16[256,1024]{1,0:T(8,128)(2,1)}, f16[256,1024]{1,0:T(8,128)(2,1)}, f16[256,1024]{1,0:T(8,128)(2,1)}, f16[256,1024]{1,0:T(8,128)(2,1)}, /*index=5*/f16[256,1024]{1,0:T(8,128)(2,1)}) fusion(f16[1536,1024]{1,0:T(8,128)(2,1)S(1)} %multiply_convert_fusion), kind=kLoop, calls=%fused_computation.68 | loop fusion | bytes 6291456 | tf_op jit(solution)/shard_map/slice | solution.py:121
  24.4 0.2 collective-permute-start
  24.6 3.2 %bitcast_subtract_fusion.1 = f32[512,1024]{1,0:T(8,128)S(1)} fusion(f32[1,2048,1024]{2,1,0:T(8,128)} %param.4, bf16[1,896,1024]{2,1,0:T(8,128)(2,1)S(1)} %copy-done, bf16[1,896,4096]{2,1,0:T(8,128)(2,1)} %param.5, s32[]{:T(128)S(6)} %select_n.49), kind=kOutput, calls=%fused_computation.7 | convolution fusion | flops 940572672 | bytes 6946820 | tf_op jit(solution)/shard_map/dot_general | solution.py:65
  27.8 1.3 %collective-permute-start.5 = (f16[256,1024]{1,0:T(8,128)(2,1)}, f16[256,1024]{1,0:T(8,128)(2,1)S(1)}, u32[]{:S(2)}, u32[]{:S(2)}) collective-permute-start(f16[256,1024]{1,0:T(8,128)(2,1)} %get-tuple-element.94), channel_id=1, source_target_pairs={{0,1},{1,0},{2,3},{3,2},{4,5},{5,4},{6,7},{7,6},{8,9},{9,8},{10,11... | collective-permute-start | bytes 1572872 | tf_op jit(solution)/shard_map/ppermute | solution.py:21
  29.1 0.2 collective-permute-done.1
  29.3 1.0 multiply_convert_fusion.8
  30.3 1.1 collective-permute-start.4
  31.5 7.2 %bitcast_subtract_fusion = f32[1280,1024]{1,0:T(8,128)} fusion(f32[1,2048,1024]{2,1,0:T(8,128)} %param.4, bf16[1,896,4096]{2,1,0:T(8,128)(2,1)} %param.5, s32[]{:T(128)S(6)} %select_n.50, bf16[1,896,1024]{2,1,0:T(8,128)(2,1)S(1)} %copy-done), kind=kOutput, calls=%fused_computation.1 | convolution fusion | flops 2351431680 | bytes 14614532 | tf_op jit(solution)/shard_map/dot_general | solution.py:65
  38.7 1.9 %collective-permute-done = f16[256,1024]{1,0:T(8,128)(2,1)S(1)} collective-permute-done((f16[256,1024]{1,0:T(8,128)(2,1)}, f16[256,1024]{1,0:T(8,128)(2,1)S(1)}, u32[]{:S(2)}, u32[]{:S(2)}) %collective-permute-start) | collective-permute-done | bytes 524320 | tf_op jit(solution)/shard_map/ppermute | solution.py:21
  40.6 1.0 multiply_convert_fusion.7
  41.7 1.1 collective-permute-start.7
  42.7 1.2 %collective-permute-start.8 = (f16[256,1024]{1,0:T(8,128)(2,1)}, f16[256,1024]{1,0:T(8,128)(2,1)}, u32[]{:S(2)}, u32[]{:S(2)}) collective-permute-start(f16[256,1024]{1,0:T(8,128)(2,1)} %get-tuple-element.121), channel_id=1, source_target_pairs={{0,1},{1,0},{2,3},{3,2},{4,5},{5,4},{6,7},{7,6},{8,9},{9,8},{10,11... | collective-permute-start | bytes 1572872 | tf_op jit(solution)/shard_map/ppermute | solution.py:21
  44.0 0.1 collective-permute-start.9
  44.0 7.8 %collective-permute-done.5 = f16[256,1024]{1,0:T(8,128)(2,1)S(1)} collective-permute-done((f16[256,1024]{1,0:T(8,128)(2,1)}, f16[256,1024]{1,0:T(8,128)(2,1)S(1)}, u32[]{:S(2)}, u32[]{:S(2)}) %collective-permute-start.5) | collective-permute-done | bytes 524320 | tf_op jit(solution)/shard_map/ppermute | solution.py:21
  51.9 0.1 fusion.46
  52.0 0.2 multiply_reduce_fusion
  52.2 0.1 broadcast_in_dim.26
  52.2 1.2 %collective-permute-start.11 = (f16[256,1024]{1,0:T(8,128)(2,1)}, f16[256,1024]{1,0:T(8,128)(2,1)S(1)}, u32[]{:S(2)}, u32[]{:S(2)}) collective-permute-start(f16[256,1024]{1,0:T(8,128)(2,1)} %get-tuple-element.135), channel_id=1, source_target_pairs={{0,1},{1,0},{2,3},{3,2},{4,5},{5,4},{6,7},{7,6},{8,9},{9,8},{10,11... | collective-permute-start | bytes 1572872 | tf_op jit(solution)/shard_map/ppermute | solution.py:21
  53.5 1.4 %multiply_convert_fusion.6 = f16[256,1024]{1,0:T(8,128)(2,1)S(1)} fusion(f16[256,1024]{1,0:T(8,128)(2,1)S(1)} %collective-permute-done.5, f32[1280,1024]{1,0:T(8,128)} %bitcast_subtract_fusion), kind=kLoop, calls=%fused_computation.43 | loop fusion | flops 1310720 | bytes 2097152 | tf_op jit(solution)/shard_map/convert_element_type | solution.py:139
  54.9 1.4 %collective-permute-start.10 = (f16[256,1024]{1,0:T(8,128)(2,1)S(1)}, f16[256,1024]{1,0:T(8,128)(2,1)S(1)}, u32[]{:S(2)}, u32[]{:S(2)}) collective-permute-start(f16[256,1024]{1,0:T(8,128)(2,1)S(1)} %multiply_convert_fusion.6), channel_id=1, source_target_pairs={{0,2},{2,0},{4,6},{6,4},{8,10},{10,8},{12,14},{14,12},{16,18},{18,... | collective-permute-start | bytes 1572872 | tf_op jit(solution)/shard_map/ppermute | solution.py:30
  56.4 2.9 %multiply_add_fusion = f32[512,1024]{1,0:T(8,128)S(1)} fusion(f16[512,1024]{1,0:T(8,128)(2,1)} %collective-permute-done.3, f32[512,1024]{1,0:T(8,128)} %get-tuple-element.129, f16[512,1024]{1,0:T(8,128)(2,1)} %collective-permute-done.2, f32[1024]{0:T(1024)S(1)} %bitcast.78, f32[1024]{0:T(1024)S(1)} %bitcast.86, f32[1024]{0:T(1024)S(1)} %bitcast.70), kind=kLoop, calls=%fused_computation.8 | loop fusion | flops 3670016 | bytes 6303744 | tf_op jit(solution)/shard_map/add | solution.py:90
  59.2 0.2 fusion.31
  59.5 0.1 collective-permute-start.12
  59.5 3.6 %collective-permute-done.8 = f16[256,1024]{1,0:T(8,128)(2,1)} collective-permute-done((f16[256,1024]{1,0:T(8,128)(2,1)}, f16[256,1024]{1,0:T(8,128)(2,1)}, u32[]{:S(2)}, u32[]{:S(2)}) %collective-permute-start.8) | collective-permute-done | bytes 524320 | tf_op jit(solution)/shard_map/ppermute | solution.py:21
  63.1 1.2 %multiply_convert_fusion.5 = f16[256,1024]{1,0:T(8,128)(2,1)S(1)} fusion(f16[256,1024]{1,0:T(8,128)(2,1)} %collective-permute-done.8, f32[1280,1024]{1,0:T(8,128)S(1)} %bitcast.68), kind=kLoop, calls=%fused_computation.41 | loop fusion | flops 1310720 | bytes 2097152 | tf_op jit(solution)/shard_map/convert_element_type | solution.py:139
  64.4 1.2 %collective-permute-start.13 = (f16[256,1024]{1,0:T(8,128)(2,1)S(1)}, f16[256,1024]{1,0:T(8,128)(2,1)S(1)}, u32[]{:S(2)}, u32[]{:S(2)}) collective-permute-start(f16[256,1024]{1,0:T(8,128)(2,1)S(1)} %multiply_convert_fusion.5), channel_id=1, source_target_pairs={{0,2},{2,0},{4,6},{6,4},{8,10},{10,8},{12,14},{14,12},{16,18},{18,... | collective-permute-start | bytes 1572872 | tf_op jit(solution)/shard_map/ppermute | solution.py:30
  65.6 1.3 %collective-permute-start.14 = (f16[256,1024]{1,0:T(8,128)(2,1)S(1)}, f16[256,1024]{1,0:T(8,128)(2,1)S(1)}, u32[]{:S(2)}, u32[]{:S(2)}) collective-permute-start(f16[256,1024]{1,0:T(8,128)(2,1)S(1)} %copy-done.6), channel_id=1, source_target_pairs={{0,1},{1,0},{2,3},{3,2},{4,5},{5,4},{6,7},{7,6},{8,9},{9,8},{10,11... | collective-permute-start | bytes 1572872 | tf_op jit(solution)/shard_map/ppermute | solution.py:21
  66.9 7.4 %collective-permute-done.11 = f16[256,1024]{1,0:T(8,128)(2,1)S(1)} collective-permute-done((f16[256,1024]{1,0:T(8,128)(2,1)}, f16[256,1024]{1,0:T(8,128)(2,1)S(1)}, u32[]{:S(2)}, u32[]{:S(2)}) %collective-permute-start.11) | collective-permute-done | bytes 524320 | tf_op jit(solution)/shard_map/ppermute | solution.py:21
  74.2 5.4 %collective-permute-done.12 = f16[256,1024]{1,0:T(8,128)(2,1)S(1)} collective-permute-done((f16[256,1024]{1,0:T(8,128)(2,1)S(1)}, f16[256,1024]{1,0:T(8,128)(2,1)S(1)}, u32[]{:S(2)}, u32[]{:S(2)}) %collective-permute-start.12) | collective-permute-done | bytes 524320 | tf_op jit(solution)/shard_map/ppermute | solution.py:30
  79.7 0.2 multiply_convert_fusion.4
  79.9 0.1 collective-permute-start.16
  80.0 0.3 collective-permute-start.17
  80.3 5.2 %collective-permute-done.14 = f16[256,1024]{1,0:T(8,128)(2,1)S(1)} collective-permute-done((f16[256,1024]{1,0:T(8,128)(2,1)S(1)}, f16[256,1024]{1,0:T(8,128)(2,1)S(1)}, u32[]{:S(2)}, u32[]{:S(2)}) %collective-permute-start.14) | collective-permute-done | bytes 524320 | tf_op jit(solution)/shard_map/ppermute | solution.py:21
  85.5 2.7 %collective-permute-done.15 = f16[256,1024]{1,0:T(8,128)(2,1)S(1)} collective-permute-done((f16[256,1024]{1,0:T(8,128)(2,1)S(1)}, f16[256,1024]{1,0:T(8,128)(2,1)S(1)}, u32[]{:S(2)}, u32[]{:S(2)}) %collective-permute-start.15) | collective-permute-done | bytes 524320 | tf_op jit(solution)/shard_map/ppermute | solution.py:30
  88.1 0.2 multiply_convert_fusion.3
  88.3 0.1 collective-permute-start.19
  88.4 0.1 collective-permute-start.20
  88.5 2.5 %collective-permute-start.21 = (f16[256,1024]{1,0:T(8,128)(2,1)S(1)}, f16[256,1024]{1,0:T(8,128)(2,1)S(1)}, u32[]{:S(2)}, u32[]{:S(2)}) collective-permute-start(f16[256,1024]{1,0:T(8,128)(2,1)S(1)} %multiply_convert_fusion.3), channel_id=1, source_target_pairs={{2,4},{4,2},{6,8},{8,6},{10,12},{12,10},{14,16},{16,14},{18,20},{2... | collective-permute-start | bytes 1572872 | tf_op jit(solution)/shard_map/ppermute | solution.py:30
  91.0 5.7 %collective-permute-done.17 = f16[256,1024]{1,0:T(8,128)(2,1)S(1)} collective-permute-done((f16[256,1024]{1,0:T(8,128)(2,1)S(1)}, f16[256,1024]{1,0:T(8,128)(2,1)S(1)}, u32[]{:S(2)}, u32[]{:S(2)}) %collective-permute-start.17) | collective-permute-done | bytes 524320 | tf_op jit(solution)/shard_map/ppermute | solution.py:21
  96.7 5.4 %collective-permute-done.18 = f16[256,1024]{1,0:T(8,128)(2,1)S(1)} collective-permute-done((f16[256,1024]{1,0:T(8,128)(2,1)S(1)}, f16[256,1024]{1,0:T(8,128)(2,1)S(1)}, u32[]{:S(2)}, u32[]{:S(2)}) %collective-permute-start.18) | collective-permute-done | bytes 524320 | tf_op jit(solution)/shard_map/ppermute | solution.py:30
  102.1 1.1 broadcast_in_dim.25
  103.2 1.6 %add_dynamic-update-slice_fusion = f32[2048,1024]{1,0:T(8,128)S(1)} fusion(f32[2048,1024]{1,0:T(8,128)S(1)} %broadcast_in_dim.25, f16[256,1024]{1,0:T(8,128)(2,1)} %collective-permute-done.6, f32[512,1024]{1,0:T(8,128)S(1)} %copy-done.4, f16[256,1024]{1,0:T(8,128)(2,1)} %collective-permute-done.4, f16[256,1024]{1,0:T(8,128)(2,1)S(1)} %collective-permute-done.1, ...), kind=kLoop, calls=%fused_computation.36 | loop fusion | flops 2621440 | bytes 3682304 | tf_op jit(solution)/shard_map/dynamic_update_slice | solution.py:97
  104.8 0.2 multiply_convert_fusion.2
  105.0 0.1 collective-permute-start.23
  105.1 0.1 collective-permute-start.22
  105.2 1.6 %bitcast_dynamic-update-slice_fusion.6 = f32[1,2048,1024]{2,1,0:T(8,128)S(1)} fusion(f32[1,2048,1024]{2,1,0:T(8,128)S(1)} %bitcast.69, f16[256,1024]{1,0:T(8,128)(2,1)} %collective-permute-done.9, f32[512,1024]{1,0:T(8,128)S(1)} %copy-done.4, f16[256,1024]{1,0:T(8,128)(2,1)} %collective-permute-done.7, f16[256,1024]{1,0:T(8,128)(2,1)S(1)} %collective-permute-done, ...), kind=kLoop, calls=%fused_computation.33 | loop fusion | flops 2621440 | bytes 3682304 | tf_op jit(solution)/shard_map/dynamic_update_slice | solution.py:97
  106.8 1.1 collective-permute-done.20
  107.9 0.2 bitcast_dynamic-update-slice_fusion.5
  108.1 0.4 bitcast_dynamic-update-slice_fusion.4
  108.6 1.5 %bitcast_dynamic-update-slice_fusion.3 = f32[1,2048,1024]{2,1,0:T(8,128)S(1)} fusion(f32[1,2048,1024]{2,1,0:T(8,128)S(1)} %bitcast_dynamic-update-slice_fusion.4, f16[256,1024]{1,0:T(8,128)(2,1)S(1)} %collective-permute-done.15, f32[1280,1024]{1,0:T(8,128)S(1)} %bitcast.68, f16[256,1024]{1,0:T(8,128)(2,1)S(1)} %collective-permute-done.13, ...), kind=kLoop, calls=%fused_computation.30 | loop fusion | flops 2621440 | bytes 3682304 | tf_op jit(solution)/shard_map/dynamic_update_slice | solution.py:97
  110.0 0.4 bitcast_dynamic-update-slice_fusion.2
  110.4 2.6 %collective-permute-done.21 = f16[256,1024]{1,0:T(8,128)(2,1)S(1)} collective-permute-done((f16[256,1024]{1,0:T(8,128)(2,1)S(1)}, f16[256,1024]{1,0:T(8,128)(2,1)S(1)}, u32[]{:S(2)}, u32[]{:S(2)}) %collective-permute-start.21) | collective-permute-done | bytes 524320 | tf_op jit(solution)/shard_map/ppermute | solution.py:30
  113.1 0.4 bitcast_dynamic-update-slice_fusion.1
  113.5 5.2 %collective-permute-done.23 = f16[256,1024]{1,0:T(8,128)(2,1)S(1)} collective-permute-done((f16[256,1024]{1,0:T(8,128)(2,1)S(1)}, f16[256,1024]{1,0:T(8,128)(2,1)S(1)}, u32[]{:S(2)}, u32[]{:S(2)}) %collective-permute-start.23) | collective-permute-done | bytes 524320 | tf_op jit(solution)/shard_map/ppermute | solution.py:30
  118.7 1.4 %bitcast_dynamic-update-slice_fusion = f32[1,2048,1024]{2,1,0:T(8,128)} fusion(f32[1,2048,1024]{2,1,0:T(8,128)} %copy-done.1, f16[256,1024]{1,0:T(8,128)(2,1)S(1)} %collective-permute-done.23, f32[1280,1024]{1,0:T(8,128)S(1)} %bitcast.68, f16[256,1024]{1,0:T(8,128)(2,1)S(1)} %collective-permute-done.22, f16[256,1024]{1,0:T(8,128)(2,1)S(1)} %collective-permute-done.17, ...), kind=kLoop, calls=%fused_computation.27 | loop fusion | flops 2621440 | bytes 3682304 | tf_op jit(solution)/shard_map/dynamic_update_slice | solution.py:97
  (36 shorter events, 0.1 us)
Async XLA Ops:
  0.0 1.5 %copy-start = (bf16[1,896,1024]{2,1,0:T(8,128)(2,1)S(1)}, bf16[1,896,1024]{2,1,0:T(8,128)(2,1)}, u32[]{:S(2)}) copy-start(bf16[1,896,1024]{2,1,0:T(8,128)(2,1)} %param.6) | copy-start | bytes 5505028
  7.5 33.1 %collective-permute-start.3 = (f16[512,1024]{1,0:T(8,128)(2,1)}, f16[512,1024]{1,0:T(8,128)(2,1)}, u32[]{:S(2)}, u32[]{:S(2)}) collective-permute-start(f16[512,1024]{1,0:T(8,128)(2,1)} %get-tuple-element.93), channel_id=1, source_target_pairs={{2,4},{4,2},{6,8},{8,6},{10,12},{12,10},{14,16},{16,14},{18,20},{2... | collective-permute-start | bytes 3145736 | tf_op jit(solution)/shard_map/ppermute | solution.py:30
  10.1 17.7 %collective-permute-start.2 = (f16[512,1024]{1,0:T(8,128)(2,1)}, f16[512,1024]{1,0:T(8,128)(2,1)}, u32[]{:S(2)}, u32[]{:S(2)}) collective-permute-start(f16[512,1024]{1,0:T(8,128)(2,1)} %get-tuple-element.93), channel_id=1, source_target_pairs={{0,2},{2,0},{4,6},{6,4},{8,10},{10,8},{12,14},{14,12},{16,18},{18,... | collective-permute-start | bytes 3145736 | tf_op jit(solution)/shard_map/ppermute | solution.py:30
  15.5 13.8 %collective-permute-start.1 = (f16[256,1024]{1,0:T(8,128)(2,1)}, f16[256,1024]{1,0:T(8,128)(2,1)S(1)}, u32[]{:S(2)}, u32[]{:S(2)}) collective-permute-start(f16[256,1024]{1,0:T(8,128)(2,1)} %fusion.28), channel_id=1, source_target_pairs={{0,1},{1,0},{2,3},{3,2},{4,5},{5,4},{6,7},{7,6},{8,9},{9,8},{10,11... | collective-permute-start | bytes 1572872 | tf_op jit(solution)/shard_map/ppermute | solution.py:21
  24.4 16.2 %collective-permute-start = (f16[256,1024]{1,0:T(8,128)(2,1)}, f16[256,1024]{1,0:T(8,128)(2,1)S(1)}, u32[]{:S(2)}, u32[]{:S(2)}) collective-permute-start(f16[256,1024]{1,0:T(8,128)(2,1)} %get-tuple-element.182), channel_id=1, source_target_pairs={{0,1},{1,0},{2,3},{3,2},{4,5},{5,4},{6,7},{7,6},{8,9},{9,8},{10,11... | collective-permute-start | bytes 1572872 | tf_op jit(solution)/shard_map/ppermute | solution.py:21
  27.8 1.5 %copy-start.2 = (f32[512,1024]{1,0:T(8,128)}, f32[512,1024]{1,0:T(8,128)S(1)}, u32[]{:S(2)}) copy-start(f32[512,1024]{1,0:T(8,128)S(1)} %bitcast_subtract_fusion.1) | copy-start | bytes 6291460
  27.8 24.0 %collective-permute-start.5 = (f16[256,1024]{1,0:T(8,128)(2,1)}, f16[256,1024]{1,0:T(8,128)(2,1)S(1)}, u32[]{:S(2)}, u32[]{:S(2)}) collective-permute-start(f16[256,1024]{1,0:T(8,128)(2,1)} %get-tuple-element.94), channel_id=1, source_target_pairs={{0,1},{1,0},{2,3},{3,2},{4,5},{5,4},{6,7},{7,6},{8,9},{9,8},{10,11... | collective-permute-start | bytes 1572872 | tf_op jit(solution)/shard_map/ppermute | solution.py:21
  30.3 21.5 %collective-permute-start.6 = (f16[256,1024]{1,0:T(8,128)(2,1)}, f16[256,1024]{1,0:T(8,128)(2,1)}, u32[]{:S(2)}, u32[]{:S(2)}) collective-permute-start(f16[256,1024]{1,0:T(8,128)(2,1)} %multiply_convert_fusion.8), channel_id=1, source_target_pairs={{2,4},{4,2},{6,8},{8,6},{10,12},{12,10},{14,16},{16,14},{18,20},{2... | collective-permute-start | bytes 1572872 | tf_op jit(solution)/shard_map/ppermute | solution.py:30
  30.3 10.3 %collective-permute-start.4 = (f16[256,1024]{1,0:T(8,128)(2,1)}, f16[256,1024]{1,0:T(8,128)(2,1)}, u32[]{:S(2)}, u32[]{:S(2)}) collective-permute-start(f16[256,1024]{1,0:T(8,128)(2,1)} %multiply_convert_fusion.8), channel_id=1, source_target_pairs={{0,2},{2,0},{4,6},{6,4},{8,10},{10,8},{12,14},{14,12},{16,18},{18,... | collective-permute-start | bytes 1572872 | tf_op jit(solution)/shard_map/ppermute | solution.py:30
  31.5 9.1 %copy-start.3 = (f32[512,1024]{1,0:T(8,128)S(1)}, f32[512,1024]{1,0:T(8,128)}, u32[]{:S(2)}) copy-start(f32[512,1024]{1,0:T(8,128)} %copy-done.2) | copy-start | bytes 6291460
  31.5 20.4 %copy-start.7 = (s32[16,3]{0,1:T(4,128)S(1)}, s32[16,3]{0,1:T(4,128)}, u32[]{:S(2)}) copy-start(s32[16,3]{0,1:T(4,128)} %param.7) | copy-start | bytes 580
  41.7 11.8 %collective-permute-start.7 = (f16[256,1024]{1,0:T(8,128)(2,1)}, f16[256,1024]{1,0:T(8,128)(2,1)}, u32[]{:S(2)}, u32[]{:S(2)}) collective-permute-start(f16[256,1024]{1,0:T(8,128)(2,1)} %multiply_convert_fusion.7), channel_id=1, source_target_pairs={{0,2},{2,0},{4,6},{6,4},{8,10},{10,8},{12,14},{14,12},{16,18},{18,... | collective-permute-start | bytes 1572872 | tf_op jit(solution)/shard_map/ppermute | solution.py:30
  42.7 20.4 %collective-permute-start.8 = (f16[256,1024]{1,0:T(8,128)(2,1)}, f16[256,1024]{1,0:T(8,128)(2,1)}, u32[]{:S(2)}, u32[]{:S(2)}) collective-permute-start(f16[256,1024]{1,0:T(8,128)(2,1)} %get-tuple-element.121), channel_id=1, source_target_pairs={{0,1},{1,0},{2,3},{3,2},{4,5},{5,4},{6,7},{7,6},{8,9},{9,8},{10,11... | collective-permute-start | bytes 1572872 | tf_op jit(solution)/shard_map/ppermute | solution.py:21
  44.0 19.1 %collective-permute-start.9 = (f16[256,1024]{1,0:T(8,128)(2,1)}, f16[256,1024]{1,0:T(8,128)(2,1)}, u32[]{:S(2)}, u32[]{:S(2)}) collective-permute-start(f16[256,1024]{1,0:T(8,128)(2,1)} %multiply_convert_fusion.7), channel_id=1, source_target_pairs={{2,4},{4,2},{6,8},{8,6},{10,12},{12,10},{14,16},{16,14},{18,20},{2... | collective-permute-start | bytes 1572872 | tf_op jit(solution)/shard_map/ppermute | solution.py:30
  52.2 22.0 %collective-permute-start.11 = (f16[256,1024]{1,0:T(8,128)(2,1)}, f16[256,1024]{1,0:T(8,128)(2,1)S(1)}, u32[]{:S(2)}, u32[]{:S(2)}) collective-permute-start(f16[256,1024]{1,0:T(8,128)(2,1)} %get-tuple-element.135), channel_id=1, source_target_pairs={{0,1},{1,0},{2,3},{3,2},{4,5},{5,4},{6,7},{7,6},{8,9},{9,8},{10,11... | collective-permute-start | bytes 1572872 | tf_op jit(solution)/shard_map/ppermute | solution.py:21
  54.9 8.2 %slice-start = ((s8[5242880]{0:T(1024)(128)(4,1)}), s8[4194304]{0:T(1024)(128)(4,1)S(1)}, s32[]{:S(2)}) async-start(s8[5242880]{0:T(1024)(128)(4,1)} %bitcast.67), calls=%async_computation | async-start | bytes 8388608
  54.9 8.2 %collective-permute-start.10 = (f16[256,1024]{1,0:T(8,128)(2,1)S(1)}, f16[256,1024]{1,0:T(8,128)(2,1)S(1)}, u32[]{:S(2)}, u32[]{:S(2)}) collective-permute-start(f16[256,1024]{1,0:T(8,128)(2,1)S(1)} %multiply_convert_fusion.6), channel_id=1, source_target_pairs={{0,2},{2,0},{4,6},{6,4},{8,10},{10,8},{12,14},{14,12},{16,18},{18,... | collective-permute-start | bytes 1572872 | tf_op jit(solution)/shard_map/ppermute | solution.py:30
  56.4 6.8 %slice-start.1 = ((s8[5242880]{0:T(1024)(128)(4,1)}), s8[1048576]{0:T(1024)(128)(4,1)S(1)}, s32[]{:S(2)}) async-start(s8[5242880]{0:T(1024)(128)(4,1)} %bitcast.67), calls=%async_computation.1 | async-start | bytes 2097152
  56.4 9.3 %copy-start.6 = (f16[256,1024]{1,0:T(8,128)(2,1)S(1)}, f16[256,1024]{1,0:T(8,128)(2,1)}, u32[]{:S(2)}) copy-start(f16[256,1024]{1,0:T(8,128)(2,1)} %get-tuple-element.144) | copy-start | bytes 1572868
  59.2 20.7 %copy-start.5 = (f16[256,1024]{1,0:T(8,128)(2,1)S(1)}, f16[256,1024]{1,0:T(8,128)(2,1)}, u32[]{:S(2)}) copy-start(f16[256,1024]{1,0:T(8,128)(2,1)} %get-tuple-element.152) | copy-start | bytes 1572868
  59.5 20.2 %collective-permute-start.12 = (f16[256,1024]{1,0:T(8,128)(2,1)S(1)}, f16[256,1024]{1,0:T(8,128)(2,1)S(1)}, u32[]{:S(2)}, u32[]{:S(2)}) collective-permute-start(f16[256,1024]{1,0:T(8,128)(2,1)S(1)} %multiply_convert_fusion.6), channel_id=1, source_target_pairs={{2,4},{4,2},{6,8},{8,6},{10,12},{12,10},{14,16},{16,14},{18,20},{2... | collective-permute-start | bytes 1572872 | tf_op jit(solution)/shard_map/ppermute | solution.py:30
  64.4 15.3 %collective-permute-start.13 = (f16[256,1024]{1,0:T(8,128)(2,1)S(1)}, f16[256,1024]{1,0:T(8,128)(2,1)S(1)}, u32[]{:S(2)}, u32[]{:S(2)}) collective-permute-start(f16[256,1024]{1,0:T(8,128)(2,1)S(1)} %multiply_convert_fusion.5), channel_id=1, source_target_pairs={{0,2},{2,0},{4,6},{6,4},{8,10},{10,8},{12,14},{14,12},{16,18},{18,... | collective-permute-start | bytes 1572872 | tf_op jit(solution)/shard_map/ppermute | solution.py:30
  65.6 19.9 %collective-permute-start.14 = (f16[256,1024]{1,0:T(8,128)(2,1)S(1)}, f16[256,1024]{1,0:T(8,128)(2,1)S(1)}, u32[]{:S(2)}, u32[]{:S(2)}) collective-permute-start(f16[256,1024]{1,0:T(8,128)(2,1)S(1)} %copy-done.6), channel_id=1, source_target_pairs={{0,1},{1,0},{2,3},{3,2},{4,5},{5,4},{6,7},{7,6},{8,9},{9,8},{10,11... | collective-permute-start | bytes 1572872 | tf_op jit(solution)/shard_map/ppermute | solution.py:21
  66.9 21.3 %collective-permute-start.15 = (f16[256,1024]{1,0:T(8,128)(2,1)S(1)}, f16[256,1024]{1,0:T(8,128)(2,1)S(1)}, u32[]{:S(2)}, u32[]{:S(2)}) collective-permute-start(f16[256,1024]{1,0:T(8,128)(2,1)S(1)} %multiply_convert_fusion.5), channel_id=1, source_target_pairs={{2,4},{4,2},{6,8},{8,6},{10,12},{12,10},{14,16},{16,14},{18,20},{2... | collective-permute-start | bytes 1572872 | tf_op jit(solution)/shard_map/ppermute | solution.py:30
  79.9 23.3 %copy-start.4 = (f32[512,1024]{1,0:T(8,128)S(1)}, f32[512,1024]{1,0:T(8,128)}, u32[]{:S(2)}) copy-start(f32[512,1024]{1,0:T(8,128)} %copy-done.2) | copy-start | bytes 6291460
  79.9 8.2 %collective-permute-start.16 = (f16[256,1024]{1,0:T(8,128)(2,1)S(1)}, f16[256,1024]{1,0:T(8,128)(2,1)S(1)}, u32[]{:S(2)}, u32[]{:S(2)}) collective-permute-start(f16[256,1024]{1,0:T(8,128)(2,1)S(1)} %multiply_convert_fusion.4), channel_id=1, source_target_pairs={{0,2},{2,0},{4,6},{6,4},{8,10},{10,8},{12,14},{14,12},{16,18},{18,... | collective-permute-start | bytes 1572872 | tf_op jit(solution)/shard_map/ppermute | solution.py:30
  80.0 16.7 %collective-permute-start.17 = (f16[256,1024]{1,0:T(8,128)(2,1)S(1)}, f16[256,1024]{1,0:T(8,128)(2,1)S(1)}, u32[]{:S(2)}, u32[]{:S(2)}) collective-permute-start(f16[256,1024]{1,0:T(8,128)(2,1)S(1)} %copy-done.5), channel_id=1, source_target_pairs={{0,1},{1,0},{2,3},{3,2},{4,5},{5,4},{6,7},{7,6},{8,9},{9,8},{10,11... | collective-permute-start | bytes 1572872 | tf_op jit(solution)/shard_map/ppermute | solution.py:21
  80.3 21.9 %collective-permute-start.18 = (f16[256,1024]{1,0:T(8,128)(2,1)S(1)}, f16[256,1024]{1,0:T(8,128)(2,1)S(1)}, u32[]{:S(2)}, u32[]{:S(2)}) collective-permute-start(f16[256,1024]{1,0:T(8,128)(2,1)S(1)} %multiply_convert_fusion.4), channel_id=1, source_target_pairs={{2,4},{4,2},{6,8},{8,6},{10,12},{12,10},{14,16},{16,14},{18,20},{2... | collective-permute-start | bytes 1572872 | tf_op jit(solution)/shard_map/ppermute | solution.py:30
  88.3 16.5 %collective-permute-start.19 = (f16[256,1024]{1,0:T(8,128)(2,1)S(1)}, f16[256,1024]{1,0:T(8,128)(2,1)S(1)}, u32[]{:S(2)}, u32[]{:S(2)}) collective-permute-start(f16[256,1024]{1,0:T(8,128)(2,1)S(1)} %multiply_convert_fusion.3), channel_id=1, source_target_pairs={{0,2},{2,0},{4,6},{6,4},{8,10},{10,8},{12,14},{14,12},{16,18},{18,... | collective-permute-start | bytes 1572872 | tf_op jit(solution)/shard_map/ppermute | solution.py:30
  88.4 19.5 %collective-permute-start.20 = (f16[256,1024]{1,0:T(8,128)(2,1)S(1)}, f16[256,1024]{1,0:T(8,128)(2,1)S(1)}, u32[]{:S(2)}, u32[]{:S(2)}) collective-permute-start(f16[256,1024]{1,0:T(8,128)(2,1)S(1)} %get-tuple-element.167), channel_id=1, source_target_pairs={{0,1},{1,0},{2,3},{3,2},{4,5},{5,4},{6,7},{7,6},{8,9},{9,8},{10,11... | collective-permute-start | bytes 1572872 | tf_op jit(solution)/shard_map/ppermute | solution.py:21
  88.5 24.6 %collective-permute-start.21 = (f16[256,1024]{1,0:T(8,128)(2,1)S(1)}, f16[256,1024]{1,0:T(8,128)(2,1)S(1)}, u32[]{:S(2)}, u32[]{:S(2)}) collective-permute-start(f16[256,1024]{1,0:T(8,128)(2,1)S(1)} %multiply_convert_fusion.3), channel_id=1, source_target_pairs={{2,4},{4,2},{6,8},{8,6},{10,12},{12,10},{14,16},{16,14},{18,20},{2... | collective-permute-start | bytes 1572872 | tf_op jit(solution)/shard_map/ppermute | solution.py:30
  105.0 13.7 %collective-permute-start.23 = (f16[256,1024]{1,0:T(8,128)(2,1)S(1)}, f16[256,1024]{1,0:T(8,128)(2,1)S(1)}, u32[]{:S(2)}, u32[]{:S(2)}) collective-permute-start(f16[256,1024]{1,0:T(8,128)(2,1)S(1)} %multiply_convert_fusion.2), channel_id=1, source_target_pairs={{2,4},{4,2},{6,8},{8,6},{10,12},{12,10},{14,16},{16,14},{18,20},{2... | collective-permute-start | bytes 1572872 | tf_op jit(solution)/shard_map/ppermute | solution.py:30
  105.1 13.6 %collective-permute-start.22 = (f16[256,1024]{1,0:T(8,128)(2,1)S(1)}, f16[256,1024]{1,0:T(8,128)(2,1)S(1)}, u32[]{:S(2)}, u32[]{:S(2)}) collective-permute-start(f16[256,1024]{1,0:T(8,128)(2,1)S(1)} %multiply_convert_fusion.2), channel_id=1, source_target_pairs={{0,2},{2,0},{4,6},{6,4},{8,10},{10,8},{12,14},{14,12},{16,18},{18,... | collective-permute-start | bytes 1572872 | tf_op jit(solution)/shard_map/ppermute | solution.py:30
  113.5 5.2 %copy-start.1 = (f32[1,2048,1024]{2,1,0:T(8,128)}, f32[1,2048,1024]{2,1,0:T(8,128)S(1)}, u32[]{:S(2)}) copy-start(f32[1,2048,1024]{2,1,0:T(8,128)S(1)} %bitcast_dynamic-update-slice_fusion.1) | copy-start | bytes 25165828

commit v21 on v11

--- a/solution.py
+++ b/solution.py
@@ -12,7 +12,7 @@
 STEP = 256
 FIRST = 256
 AHEAD = 3
-MIXLAG = 5
+MIXLAG = 4
 
 
 def from_behind(value, axis, steps):

time: 119 us -> 118 us (level)
  waiting for transfers between devices: 51.5 us -> 46.2 us
  starting transfers between devices: 23.9 us -> 28.6 us
    ppermute x8, waiting for transfers between devices: 37.8 us -> 11.7 us  [from_behind(): return lax.ppermute(value, axis, pairs)]
    ppermute x16, waiting for transfers between devices: 13.7 us -> 34.5 us  [swapped(): return lax.ppermute(value, axis, pairs)]
    ppermute x16, starting transfers between devices: 15.9 us -> 20.4 us  [swapped(): return lax.ppermute(value, axis, pairs)]
  transfers between devices with their start and end apart: 24 -> 24, of which waited for: 9 -> 11; matrix products, arithmetic and copies ran while one was open for 26% -> 26% of each run, Pallas kernels for 0% -> 0%
where the time goes in v21:
time: 118 us
  waiting for transfers between devices  46.2 us (39%)
  starting transfers between devices  28.6 us (24%)
  matrix products  21.5 us (18%)
  other arithmetic  13.2 us (11%)
  local copies, waits for them, and re-layouts  5.43 us (5%)
  between operations  2.94 us (2%)
    ppermute x16, waiting for transfers between devices, swapped(): return lax.ppermute(value, axis, pairs)  34.5 us
    dot_general x6, matrix products, partial(): lax.dot_general(block, cot_local, (((0,), (0,)), ((), ())), preferred_ele...  21.5 us
    ppermute x16, starting transfers between devices, swapped(): return lax.ppermute(value, axis, pairs)  20.4 us
    ppermute x8, waiting for transfers between devices, from_behind(): return lax.ppermute(value, axis, pairs)  11.7 us
    ppermute x8, starting transfers between devices, from_behind(): return lax.ppermute(value, axis, pairs)  8.2 us
    dynamic_update_slice x7, other arithmetic, mix_into(): return lax.dynamic_update_slice_in_dim(out, value, cuts[chunk], axis=0)  5.24 us
  transfers between devices with their start and end apart: 24, of which 11 were waited for; matrix products, arithmetic and copies ran while one was open for 26% of the time, Pallas kernels for 0%

profile of v21, /device:TPU:1, one launch (start us, length us, event | category | flops | bytes accessed | tf_op | source)
XLA Modules:
  0.0 117.9 jit_solution(12382359121726005866)
XLA Ops:
  0.0 1.5 %copy-done = bf16[1,896,1024]{2,1,0:T(8,128)(2,1)S(1)} copy-done((bf16[1,896,1024]{2,1,0:T(8,128)(2,1)S(1)}, bf16[1,896,1024]{2,1,0:T(8,128)(2,1)}, u32[]{:S(2)}) %copy-start) | copy-done | bytes 1835032
  1.5 1.7 %fusion.22 = f32[256,1024]{1,0:T(8,128)S(1)} fusion(bf16[1,896,1024]{2,1,0:T(8,128)(2,1)S(1)} %copy-done, bf16[1,896,4096]{2,1,0:T(8,128)(2,1)} %param.5, s32[]{:T(128)S(6)} %select_n.49), kind=kOutput, calls=%fused_computation.22 | convolution fusion | flops 470024192 | bytes 3342340 | tf_op jit(solution)/shard_map/dot_general | solution.py:63
  3.2 2.1 %fusion.19 = f32[256,1024]{1,0:T(8,128)S(1)} fusion(bf16[1,896,1024]{2,1,0:T(8,128)(2,1)S(1)} %copy-done, f32[1,2048,1024]{2,1,0:T(8,128)} %param.4, bf16[1,896,4096]{2,1,0:T(8,128)(2,1)} %param.5, s32[]{:T(128)S(6)} %select_n.47), kind=kOutput, calls=%fused_computation.21 | convolution fusion | flops 470286336 | bytes 4390916 | tf_op jit(solution)/shard_map/dot_general | solution.py:63
  5.4 2.1 %multiply_convert_fusion.1 = (f16[512,1024]{1,0:T(8,128)(2,1)}, f32[512,1024]{1,0:T(8,128)}) fusion(f32[256,1024]{1,0:T(8,128)S(1)} %fusion.22, f32[256,1024]{1,0:T(8,128)S(1)} %fusion.19), kind=kLoop, calls=%fused_computation.9 | loop fusion | flops 1572864 | bytes 5242880 | tf_op jit(solution)/shard_map/convert_element_type | solution.py:106
  7.5 0.1 collective-permute-start.2
  7.5 2.5 %collective-permute-start.3 = (f16[512,1024]{1,0:T(8,128)(2,1)}, f16[512,1024]{1,0:T(8,128)(2,1)}, u32[]{:S(2)}, u32[]{:S(2)}) collective-permute-start(f16[512,1024]{1,0:T(8,128)(2,1)} %get-tuple-element.94), channel_id=1, source_target_pairs={{2,4},{4,2},{6,8},{8,6},{10,12},{12,10},{14,16},{16,14},{18,20},{2... | collective-permute-start | bytes 3145736 | tf_op jit(solution)/shard_map/ppermute | solution.py:30
  10.1 2.6 %fusion.28 = f16[256,1024]{1,0:T(8,128)(2,1)} fusion(bf16[1,896,1024]{2,1,0:T(8,128)(2,1)S(1)} %copy-done, bf16[1,896,4096]{2,1,0:T(8,128)(2,1)} %param.5, s32[]{:T(128)S(6)} %select_n.52), kind=kOutput, calls=%fused_computation.24 | convolution fusion | flops 470286336 | bytes 2818052 | tf_op jit(solution)/shard_map/dot_general | solution.py:63
  12.7 1.2 %collective-permute-start.1 = (f16[256,1024]{1,0:T(8,128)(2,1)}, f16[256,1024]{1,0:T(8,128)(2,1)S(1)}, u32[]{:S(2)}, u32[]{:S(2)}) collective-permute-start(f16[256,1024]{1,0:T(8,128)(2,1)} %fusion.28), channel_id=1, source_target_pairs={{0,1},{1,0},{2,3},{3,2},{4,5},{5,4},{6,7},{7,6},{8,9},{9,8},{10,11... | collective-permute-start | bytes 1572872 | tf_op jit(solution)/shard_map/ppermute | solution.py:21
  13.9 5.5 %multiply_convert_fusion = f16[1536,1024]{1,0:T(8,128)(2,1)S(1)} fusion(bf16[1,896,4096]{2,1,0:T(8,128)(2,1)} %param.5, s32[]{:T(128)S(6)} %select_n.51, bf16[1,896,1024]{2,1,0:T(8,128)(2,1)S(1)} %copy-done), kind=kOutput, calls=%fused_computation | convolution fusion | flops 2821718016 | bytes 7733252 | tf_op jit(solution)/shard_map/dot_general | solution.py:63
  19.4 2.2 %fusion.48 = (f16[256,1024]{1,0:T(8,128)(2,1)}, f16[256,1024]{1,0:T(8,128)(2,1)}, f16[256,1024]{1,0:T(8,128)(2,1)}, f16[256,1024]{1,0:T(8,128)(2,1)}, f16[256,1024]{1,0:T(8,128)(2,1)}, /*index=5*/f16[256,1024]{1,0:T(8,128)(2,1)}) fusion(f16[1536,1024]{1,0:T(8,128)(2,1)S(1)} %multiply_convert_fusion), kind=kLoop, calls=%fused_computation.67 | loop fusion | bytes 6291456 | tf_op jit(solution)/shard_map/slice | solution.py:117
  21.5 0.2 collective-permute-start
  21.8 0.1 fusion.47
  21.8 0.6 fusion.50
  25.1 3.2 %bitcast_subtract_fusion.1 = f32[512,1024]{1,0:T(8,128)S(1)} fusion(f32[1,2048,1024]{2,1,0:T(8,128)} %param.4, bf16[1,896,1024]{2,1,0:T(8,128)(2,1)S(1)} %copy-done, bf16[1,896,4096]{2,1,0:T(8,128)(2,1)} %param.5, s32[]{:T(128)S(6)} %select_n.53), kind=kOutput, calls=%fused_computation.7 | convolution fusion | flops 940572672 | bytes 6946820 | tf_op jit(solution)/shard_map/dot_general | solution.py:63
  28.3 0.8 maximum_bitcast_fusion
  29.0 1.3 %collective-permute-start.5 = (f16[256,1024]{1,0:T(8,128)(2,1)}, f16[256,1024]{1,0:T(8,128)(2,1)S(1)}, u32[]{:S(2)}, u32[]{:S(2)}) collective-permute-start(f16[256,1024]{1,0:T(8,128)(2,1)} %get-tuple-element.95), channel_id=1, source_target_pairs={{0,1},{1,0},{2,3},{3,2},{4,5},{5,4},{6,7},{7,6},{8,9},{9,8},{10,11... | collective-permute-start | bytes 1572872 | tf_op jit(solution)/shard_map/ppermute | solution.py:21
  30.3 1.0 multiply_convert_fusion.8
  31.3 1.5 %collective-permute-start.6 = (f16[256,1024]{1,0:T(8,128)(2,1)}, f16[256,1024]{1,0:T(8,128)(2,1)}, u32[]{:S(2)}, u32[]{:S(2)}) collective-permute-start(f16[256,1024]{1,0:T(8,128)(2,1)} %multiply_convert_fusion.8), channel_id=1, source_target_pairs={{2,4},{4,2},{6,8},{8,6},{10,12},{12,10},{14,16},{16,14},{18,20},{2... | collective-permute-start | bytes 1572872 | tf_op jit(solution)/shard_map/ppermute | solution.py:30
  32.8 2.9 %collective-permute-start.4 = (f16[256,1024]{1,0:T(8,128)(2,1)}, f16[256,1024]{1,0:T(8,128)(2,1)}, u32[]{:S(2)}, u32[]{:S(2)}) collective-permute-start(f16[256,1024]{1,0:T(8,128)(2,1)} %multiply_convert_fusion.8), channel_id=1, source_target_pairs={{0,2},{2,0},{4,6},{6,4},{8,10},{10,8},{12,14},{14,12},{16,18},{18,... | collective-permute-start | bytes 1572872 | tf_op jit(solution)/shard_map/ppermute | solution.py:30
  35.7 6.5 %bitcast_subtract_fusion = f32[1280,1024]{1,0:T(8,128)S(1)} fusion(f32[1,2048,1024]{2,1,0:T(8,128)} %param.4, bf16[1,896,4096]{2,1,0:T(8,128)(2,1)} %param.5, s32[]{:T(128)S(6)} %select_n.54, bf16[1,896,1024]{2,1,0:T(8,128)(2,1)S(1)} %copy-done), kind=kOutput, calls=%fused_computation.1 | convolution fusion | flops 2351431680 | bytes 14614532 | tf_op jit(solution)/shard_map/dot_general | solution.py:63
  42.2 0.2 multiply_convert_fusion.7
  42.4 0.1 broadcast_in_dim.27
  42.5 0.0 collective-permute-start.7
  42.5 0.8 collective-permute-start.8
  43.3 1.6 %collective-permute-done.6 = f16[256,1024]{1,0:T(8,128)(2,1)} collective-permute-done((f16[256,1024]{1,0:T(8,128)(2,1)}, f16[256,1024]{1,0:T(8,128)(2,1)}, u32[]{:S(2)}, u32[]{:S(2)}) %collective-permute-start.6) | collective-permute-done | bytes 524320 | tf_op jit(solution)/shard_map/ppermute | solution.py:30
  44.9 2.1 %collective-permute-done.5 = f16[256,1024]{1,0:T(8,128)(2,1)S(1)} collective-permute-done((f16[256,1024]{1,0:T(8,128)(2,1)}, f16[256,1024]{1,0:T(8,128)(2,1)S(1)}, u32[]{:S(2)}, u32[]{:S(2)}) %collective-permute-start.5) | collective-permute-done | bytes 524320 | tf_op jit(solution)/shard_map/ppermute | solution.py:21
  47.0 0.4 collective-permute-start.11
  47.4 0.2 multiply_convert_fusion.6
  47.7 7.1 %collective-permute-start.10 = (f16[256,1024]{1,0:T(8,128)(2,1)S(1)}, f16[256,1024]{1,0:T(8,128)(2,1)S(1)}, u32[]{:S(2)}, u32[]{:S(2)}) collective-permute-start(f16[256,1024]{1,0:T(8,128)(2,1)S(1)} %multiply_convert_fusion.6), channel_id=1, source_target_pairs={{0,2},{2,0},{4,6},{6,4},{8,10},{10,8},{12,14},{14,12},{16,18},{18,... | collective-permute-start | bytes 1572872 | tf_op jit(solution)/shard_map/ppermute | solution.py:30
  54.8 2.2 %multiply_add_fusion = f32[512,1024]{1,0:T(8,128)S(1)} fusion(f16[512,1024]{1,0:T(8,128)(2,1)} %collective-permute-done.3, f32[512,1024]{1,0:T(8,128)S(1)} %copy-done.2, f16[512,1024]{1,0:T(8,128)(2,1)} %collective-permute-done.2, f32[1024]{0:T(1024)S(1)} %bitcast.77, f32[1024]{0:T(1024)S(1)} %bitcast.85, f32[1024]{0:T(1024)S(1)} %bitcast.69), kind=kLoop, calls=%fused_computation.8 | loop fusion | flops 3670016 | bytes 6303744 | tf_op jit(solution)/shard_map/add | solution.py:88
  57.1 0.2 fusion.31
  57.3 0.1 collective-permute-start.12
  57.3 0.9 collective-permute-done.8
  58.2 0.2 multiply_convert_fusion.5
  58.5 5.1 %collective-permute-start.13 = (f16[256,1024]{1,0:T(8,128)(2,1)S(1)}, f16[256,1024]{1,0:T(8,128)(2,1)S(1)}, u32[]{:S(2)}, u32[]{:S(2)}) collective-permute-start(f16[256,1024]{1,0:T(8,128)(2,1)S(1)} %multiply_convert_fusion.5), channel_id=1, source_target_pairs={{0,2},{2,0},{4,6},{6,4},{8,10},{10,8},{12,14},{14,12},{16,18},{18,... | collective-permute-start | bytes 1572872 | tf_op jit(solution)/shard_map/ppermute | solution.py:30
  63.6 2.2 %collective-permute-start.14 = (f16[256,1024]{1,0:T(8,128)(2,1)S(1)}, f16[256,1024]{1,0:T(8,128)(2,1)S(1)}, u32[]{:S(2)}, u32[]{:S(2)}) collective-permute-start(f16[256,1024]{1,0:T(8,128)(2,1)S(1)} %copy-done.6), channel_id=1, source_target_pairs={{0,1},{1,0},{2,3},{3,2},{4,5},{5,4},{6,7},{7,6},{8,9},{9,8},{10,11... | collective-permute-start | bytes 1572872 | tf_op jit(solution)/shard_map/ppermute | solution.py:21
  65.8 3.7 %collective-permute-done.11 = f16[256,1024]{1,0:T(8,128)(2,1)S(1)} collective-permute-done((f16[256,1024]{1,0:T(8,128)(2,1)S(1)}, f16[256,1024]{1,0:T(8,128)(2,1)S(1)}, u32[]{:S(2)}, u32[]{:S(2)}) %collective-permute-start.11) | collective-permute-done | bytes 524320 | tf_op jit(solution)/shard_map/ppermute | solution.py:21
  69.5 8.0 %collective-permute-done.12 = f16[256,1024]{1,0:T(8,128)(2,1)S(1)} collective-permute-done((f16[256,1024]{1,0:T(8,128)(2,1)S(1)}, f16[256,1024]{1,0:T(8,128)(2,1)S(1)}, u32[]{:S(2)}, u32[]{:S(2)}) %collective-permute-start.12) | collective-permute-done | bytes 524320 | tf_op jit(solution)/shard_map/ppermute | solution.py:30
  77.5 0.2 multiply_convert_fusion.4
  77.7 0.1 collective-permute-start.16
  77.8 0.1 collective-permute-start.17
  77.9 0.2 collective-permute-start.18
  78.1 1.1 broadcast_in_dim.25
  79.1 1.6 %add_dynamic-update-slice_fusion.1 = f32[2048,1024]{1,0:T(8,128)S(1)} fusion(f32[2048,1024]{1,0:T(8,128)S(1)} %broadcast_in_dim.25, f16[256,1024]{1,0:T(8,128)(2,1)} %collective-permute-done.6, f32[512,1024]{1,0:T(8,128)S(1)} %copy-done.4, f16[256,1024]{1,0:T(8,128)(2,1)} %collective-permute-done.4, f16[256,1024]{1,0:T(8,128)(2,1)S(1)} %collective-permute-done.1, ...), kind=kLoop, calls=%fused_computation.38 | loop fusion | flops 2621440 | bytes 3682304 | tf_op jit(solution)/shard_map/dynamic_update_slice | solution.py:93
  80.8 5.2 %collective-permute-done.15 = f16[256,1024]{1,0:T(8,128)(2,1)S(1)} collective-permute-done((f16[256,1024]{1,0:T(8,128)(2,1)S(1)}, f16[256,1024]{1,0:T(8,128)(2,1)S(1)}, u32[]{:S(2)}, u32[]{:S(2)}) %collective-permute-start.15) | collective-permute-done | bytes 524320 | tf_op jit(solution)/shard_map/ppermute | solution.py:30
  85.9 0.2 multiply_convert_fusion.3
  86.2 0.1 collective-permute-start.19
  86.2 2.0 %collective-permute-start.20 = (f16[256,1024]{1,0:T(8,128)(2,1)S(1)}, f16[256,1024]{1,0:T(8,128)(2,1)S(1)}, u32[]{:S(2)}, u32[]{:S(2)}) collective-permute-start(f16[256,1024]{1,0:T(8,128)(2,1)S(1)} %get-tuple-element.172), channel_id=1, source_target_pairs={{0,1},{1,0},{2,3},{3,2},{4,5},{5,4},{6,7},{7,6},{8,9},{9,8},{10,11... | collective-permute-start | bytes 1572872 | tf_op jit(solution)/shard_map/ppermute | solution.py:21
  88.2 0.6 collective-permute-start.21
  88.9 3.1 %collective-permute-done.17 = f16[256,1024]{1,0:T(8,128)(2,1)S(1)} collective-permute-done((f16[256,1024]{1,0:T(8,128)(2,1)S(1)}, f16[256,1024]{1,0:T(8,128)(2,1)S(1)}, u32[]{:S(2)}, u32[]{:S(2)}) %collective-permute-start.17) | collective-permute-done | bytes 524320 | tf_op jit(solution)/shard_map/ppermute | solution.py:21
  91.9 8.0 %collective-permute-done.18 = f16[256,1024]{1,0:T(8,128)(2,1)S(1)} collective-permute-done((f16[256,1024]{1,0:T(8,128)(2,1)S(1)}, f16[256,1024]{1,0:T(8,128)(2,1)S(1)}, u32[]{:S(2)}, u32[]{:S(2)}) %collective-permute-start.18) | collective-permute-done | bytes 524320 | tf_op jit(solution)/shard_map/ppermute | solution.py:30
  99.9 0.4 add_dynamic-update-slice_fusion
  100.4 0.2 multiply_convert_fusion.2
  100.6 0.1 collective-permute-start.22
  100.7 0.1 collective-permute-start.23
  100.8 0.4 bitcast_dynamic-update-slice_fusion.5
  101.2 2.0 %collective-permute-done.20 = f16[256,1024]{1,0:T(8,128)(2,1)S(1)} collective-permute-done((f16[256,1024]{1,0:T(8,128)(2,1)S(1)}, f16[256,1024]{1,0:T(8,128)(2,1)S(1)}, u32[]{:S(2)}, u32[]{:S(2)}) %collective-permute-start.20) | collective-permute-done | bytes 524320 | tf_op jit(solution)/shard_map/ppermute | solution.py:21
  103.2 0.2 bitcast_dynamic-update-slice_fusion.4
  103.4 0.4 bitcast_dynamic-update-slice_fusion.3
  103.8 0.4 bitcast_dynamic-update-slice_fusion.2
  104.3 1.2 collective-permute-done.21
  105.5 0.4 bitcast_dynamic-update-slice_fusion.1
  105.9 10.6 %collective-permute-done.23 = f16[256,1024]{1,0:T(8,128)(2,1)S(1)} collective-permute-done((f16[256,1024]{1,0:T(8,128)(2,1)S(1)}, f16[256,1024]{1,0:T(8,128)(2,1)S(1)}, u32[]{:S(2)}, u32[]{:S(2)}) %collective-permute-start.23) | collective-permute-done | bytes 524320 | tf_op jit(solution)/shard_map/ppermute | solution.py:30
  116.5 1.4 %bitcast_dynamic-update-slice_fusion = f32[1,2048,1024]{2,1,0:T(8,128)} fusion(f32[1,2048,1024]{2,1,0:T(8,128)} %copy-done.1, f16[256,1024]{1,0:T(8,128)(2,1)S(1)} %collective-permute-done.23, f32[1280,1024]{1,0:T(8,128)S(1)} %bitcast_subtract_fusion, f16[256,1024]{1,0:T(8,128)(2,1)S(1)} %collective-permute-done.22, ...), kind=kLoop, calls=%fused_computation.27 | loop fusion | flops 2621440 | bytes 3682304 | tf_op jit(solution)/shard_map/dynamic_update_slice | solution.py:93
  (35 shorter events, 0.1 us)
Async XLA Ops:
  0.0 1.5 %copy-start = (bf16[1,896,1024]{2,1,0:T(8,128)(2,1)S(1)}, bf16[1,896,1024]{2,1,0:T(8,128)(2,1)}, u32[]{:S(2)}) copy-start(bf16[1,896,1024]{2,1,0:T(8,128)(2,1)} %param.6) | copy-start | bytes 5505028
  7.5 21.6 %collective-permute-start.2 = (f16[512,1024]{1,0:T(8,128)(2,1)}, f16[512,1024]{1,0:T(8,128)(2,1)}, u32[]{:S(2)}, u32[]{:S(2)}) collective-permute-start(f16[512,1024]{1,0:T(8,128)(2,1)} %get-tuple-element.94), channel_id=1, source_target_pairs={{0,2},{2,0},{4,6},{6,4},{8,10},{10,8},{12,14},{14,12},{16,18},{18,... | collective-permute-start | bytes 3145736 | tf_op jit(solution)/shard_map/ppermute | solution.py:30
  7.5 34.7 %collective-permute-start.3 = (f16[512,1024]{1,0:T(8,128)(2,1)}, f16[512,1024]{1,0:T(8,128)(2,1)}, u32[]{:S(2)}, u32[]{:S(2)}) collective-permute-start(f16[512,1024]{1,0:T(8,128)(2,1)} %get-tuple-element.94), channel_id=1, source_target_pairs={{2,4},{4,2},{6,8},{8,6},{10,12},{12,10},{14,16},{16,14},{18,20},{2... | collective-permute-start | bytes 3145736 | tf_op jit(solution)/shard_map/ppermute | solution.py:30
  12.7 17.6 %collective-permute-start.1 = (f16[256,1024]{1,0:T(8,128)(2,1)}, f16[256,1024]{1,0:T(8,128)(2,1)S(1)}, u32[]{:S(2)}, u32[]{:S(2)}) collective-permute-start(f16[256,1024]{1,0:T(8,128)(2,1)} %fusion.28), channel_id=1, source_target_pairs={{0,1},{1,0},{2,3},{3,2},{4,5},{5,4},{6,7},{7,6},{8,9},{9,8},{10,11... | collective-permute-start | bytes 1572872 | tf_op jit(solution)/shard_map/ppermute | solution.py:21
  19.4 2.4 %copy-start.9 = (s32[16,3]{0,1:T(4,128)S(1)}, s32[16,3]{0,1:T(4,128)}, u32[]{:S(2)}) copy-start(s32[16,3]{0,1:T(4,128)} %param.7) | copy-start | bytes 580
  21.5 20.6 %collective-permute-start = (f16[256,1024]{1,0:T(8,128)(2,1)}, f16[256,1024]{1,0:T(8,128)(2,1)S(1)}, u32[]{:S(2)}, u32[]{:S(2)}) collective-permute-start(f16[256,1024]{1,0:T(8,128)(2,1)} %get-tuple-element.184), channel_id=1, source_target_pairs={{0,1},{1,0},{2,3},{3,2},{4,5},{5,4},{6,7},{7,6},{8,9},{9,8},{10,11... | collective-permute-start | bytes 1572872 | tf_op jit(solution)/shard_map/ppermute | solution.py:21
  28.2 2.0 %copy-start.3 = (f32[512,1024]{1,0:T(8,128)}, f32[512,1024]{1,0:T(8,128)S(1)}, u32[]{:S(2)}) copy-start(f32[512,1024]{1,0:T(8,128)S(1)} %bitcast_subtract_fusion.1) | copy-start | bytes 6291460
  29.0 18.0 %collective-permute-start.5 = (f16[256,1024]{1,0:T(8,128)(2,1)}, f16[256,1024]{1,0:T(8,128)(2,1)S(1)}, u32[]{:S(2)}, u32[]{:S(2)}) collective-permute-start(f16[256,1024]{1,0:T(8,128)(2,1)} %get-tuple-element.95), channel_id=1, source_target_pairs={{0,1},{1,0},{2,3},{3,2},{4,5},{5,4},{6,7},{7,6},{8,9},{9,8},{10,11... | collective-permute-start | bytes 1572872 | tf_op jit(solution)/shard_map/ppermute | solution.py:21
  31.3 13.6 %collective-permute-start.6 = (f16[256,1024]{1,0:T(8,128)(2,1)}, f16[256,1024]{1,0:T(8,128)(2,1)}, u32[]{:S(2)}, u32[]{:S(2)}) collective-permute-start(f16[256,1024]{1,0:T(8,128)(2,1)} %multiply_convert_fusion.8), channel_id=1, source_target_pairs={{2,4},{4,2},{6,8},{8,6},{10,12},{12,10},{14,16},{16,14},{18,20},{2... | collective-permute-start | bytes 1572872 | tf_op jit(solution)/shard_map/ppermute | solution.py:30
  32.8 9.4 %collective-permute-start.4 = (f16[256,1024]{1,0:T(8,128)(2,1)}, f16[256,1024]{1,0:T(8,128)(2,1)}, u32[]{:S(2)}, u32[]{:S(2)}) collective-permute-start(f16[256,1024]{1,0:T(8,128)(2,1)} %multiply_convert_fusion.8), channel_id=1, source_target_pairs={{0,2},{2,0},{4,6},{6,4},{8,10},{10,8},{12,14},{14,12},{16,18},{18,... | collective-permute-start | bytes 1572872 | tf_op jit(solution)/shard_map/ppermute | solution.py:30
  35.7 6.5 %copy-start.4 = (f32[512,1024]{1,0:T(8,128)S(1)}, f32[512,1024]{1,0:T(8,128)}, u32[]{:S(2)}) copy-start(f32[512,1024]{1,0:T(8,128)} %copy-done.3) | copy-start | bytes 6291460
  35.7 6.9 %copy-start.8 = (f16[256,1024]{1,0:T(8,128)(2,1)S(1)}, f16[256,1024]{1,0:T(8,128)(2,1)}, u32[]{:S(2)}) copy-start(f16[256,1024]{1,0:T(8,128)(2,1)} %get-tuple-element.122) | copy-start | bytes 1572868
  35.7 11.3 %copy-start.7 = (f16[256,1024]{1,0:T(8,128)(2,1)S(1)}, f16[256,1024]{1,0:T(8,128)(2,1)}, u32[]{:S(2)}) copy-start(f16[256,1024]{1,0:T(8,128)(2,1)} %get-tuple-element.136) | copy-start | bytes 1572868
  42.1 12.6 %copy-start.2 = (f32[512,1024]{1,0:T(8,128)S(1)}, f32[512,1024]{1,0:T(8,128)}, u32[]{:S(2)}) copy-start(f32[512,1024]{1,0:T(8,128)} %get-tuple-element.130) | copy-start | bytes 6291460
  42.5 4.9 %collective-permute-start.7 = (f16[256,1024]{1,0:T(8,128)(2,1)S(1)}, f16[256,1024]{1,0:T(8,128)(2,1)S(1)}, u32[]{:S(2)}, u32[]{:S(2)}) collective-permute-start(f16[256,1024]{1,0:T(8,128)(2,1)S(1)} %multiply_convert_fusion.7), channel_id=1, source_target_pairs={{0,2},{2,0},{4,6},{6,4},{8,10},{10,8},{12,14},{14,12},{16,18},{18,... | collective-permute-start | bytes 1572872 | tf_op jit(solution)/shard_map/ppermute | solution.py:30
  42.5 15.7 %collective-permute-start.8 = (f16[256,1024]{1,0:T(8,128)(2,1)S(1)}, f16[256,1024]{1,0:T(8,128)(2,1)S(1)}, u32[]{:S(2)}, u32[]{:S(2)}) collective-permute-start(f16[256,1024]{1,0:T(8,128)(2,1)S(1)} %copy-done.8), channel_id=1, source_target_pairs={{0,1},{1,0},{2,3},{3,2},{4,5},{5,4},{6,7},{7,6},{8,9},{9,8},{10,11... | collective-permute-start | bytes 1572872 | tf_op jit(solution)/shard_map/ppermute | solution.py:21
  43.3 14.9 %collective-permute-start.9 = (f16[256,1024]{1,0:T(8,128)(2,1)S(1)}, f16[256,1024]{1,0:T(8,128)(2,1)S(1)}, u32[]{:S(2)}, u32[]{:S(2)}) collective-permute-start(f16[256,1024]{1,0:T(8,128)(2,1)S(1)} %multiply_convert_fusion.7), channel_id=1, source_target_pairs={{2,4},{4,2},{6,8},{8,6},{10,12},{12,10},{14,16},{16,14},{18,20},{2... | collective-permute-start | bytes 1572872 | tf_op jit(solution)/shard_map/ppermute | solution.py:30
  47.0 22.5 %collective-permute-start.11 = (f16[256,1024]{1,0:T(8,128)(2,1)S(1)}, f16[256,1024]{1,0:T(8,128)(2,1)S(1)}, u32[]{:S(2)}, u32[]{:S(2)}) collective-permute-start(f16[256,1024]{1,0:T(8,128)(2,1)S(1)} %copy-done.7), channel_id=1, source_target_pairs={{0,1},{1,0},{2,3},{3,2},{4,5},{5,4},{6,7},{7,6},{8,9},{9,8},{10,11... | collective-permute-start | bytes 1572872 | tf_op jit(solution)/shard_map/ppermute | solution.py:21
  47.7 10.6 %collective-permute-start.10 = (f16[256,1024]{1,0:T(8,128)(2,1)S(1)}, f16[256,1024]{1,0:T(8,128)(2,1)S(1)}, u32[]{:S(2)}, u32[]{:S(2)}) collective-permute-start(f16[256,1024]{1,0:T(8,128)(2,1)S(1)} %multiply_convert_fusion.6), channel_id=1, source_target_pairs={{0,2},{2,0},{4,6},{6,4},{8,10},{10,8},{12,14},{14,12},{16,18},{18,... | collective-permute-start | bytes 1572872 | tf_op jit(solution)/shard_map/ppermute | solution.py:30
  54.8 8.8 %copy-start.6 = (f16[256,1024]{1,0:T(8,128)(2,1)S(1)}, f16[256,1024]{1,0:T(8,128)(2,1)}, u32[]{:S(2)}) copy-start(f16[256,1024]{1,0:T(8,128)(2,1)} %get-tuple-element.145) | copy-start | bytes 1572868
  57.0 20.7 %copy-start.5 = (f16[256,1024]{1,0:T(8,128)(2,1)S(1)}, f16[256,1024]{1,0:T(8,128)(2,1)}, u32[]{:S(2)}) copy-start(f16[256,1024]{1,0:T(8,128)(2,1)} %get-tuple-element.157) | copy-start | bytes 1572868
  57.3 20.2 %collective-permute-start.12 = (f16[256,1024]{1,0:T(8,128)(2,1)S(1)}, f16[256,1024]{1,0:T(8,128)(2,1)S(1)}, u32[]{:S(2)}, u32[]{:S(2)}) collective-permute-start(f16[256,1024]{1,0:T(8,128)(2,1)S(1)} %multiply_convert_fusion.6), channel_id=1, source_target_pairs={{2,4},{4,2},{6,8},{8,6},{10,12},{12,10},{14,16},{16,14},{18,20},{2... | collective-permute-start | bytes 1572872 | tf_op jit(solution)/shard_map/ppermute | solution.py:30
  58.5 19.0 %collective-permute-start.13 = (f16[256,1024]{1,0:T(8,128)(2,1)S(1)}, f16[256,1024]{1,0:T(8,128)(2,1)S(1)}, u32[]{:S(2)}, u32[]{:S(2)}) collective-permute-start(f16[256,1024]{1,0:T(8,128)(2,1)S(1)} %multiply_convert_fusion.5), channel_id=1, source_target_pairs={{0,2},{2,0},{4,6},{6,4},{8,10},{10,8},{12,14},{14,12},{16,18},{18,... | collective-permute-start | bytes 1572872 | tf_op jit(solution)/shard_map/ppermute | solution.py:30
  63.6 17.2 %collective-permute-start.14 = (f16[256,1024]{1,0:T(8,128)(2,1)S(1)}, f16[256,1024]{1,0:T(8,128)(2,1)S(1)}, u32[]{:S(2)}, u32[]{:S(2)}) collective-permute-start(f16[256,1024]{1,0:T(8,128)(2,1)S(1)} %copy-done.6), channel_id=1, source_target_pairs={{0,1},{1,0},{2,3},{3,2},{4,5},{5,4},{6,7},{7,6},{8,9},{9,8},{10,11... | collective-permute-start | bytes 1572872 | tf_op jit(solution)/shard_map/ppermute | solution.py:21
  65.8 20.2 %collective-permute-start.15 = (f16[256,1024]{1,0:T(8,128)(2,1)S(1)}, f16[256,1024]{1,0:T(8,128)(2,1)S(1)}, u32[]{:S(2)}, u32[]{:S(2)}) collective-permute-start(f16[256,1024]{1,0:T(8,128)(2,1)S(1)} %multiply_convert_fusion.5), channel_id=1, source_target_pairs={{2,4},{4,2},{6,8},{8,6},{10,12},{12,10},{14,16},{16,14},{18,20},{2... | collective-permute-start | bytes 1572872 | tf_op jit(solution)/shard_map/ppermute | solution.py:30
  77.7 8.2 %collective-permute-start.16 = (f16[256,1024]{1,0:T(8,128)(2,1)S(1)}, f16[256,1024]{1,0:T(8,128)(2,1)S(1)}, u32[]{:S(2)}, u32[]{:S(2)}) collective-permute-start(f16[256,1024]{1,0:T(8,128)(2,1)S(1)} %multiply_convert_fusion.4), channel_id=1, source_target_pairs={{0,2},{2,0},{4,6},{6,4},{8,10},{10,8},{12,14},{14,12},{16,18},{18,... | collective-permute-start | bytes 1572872 | tf_op jit(solution)/shard_map/ppermute | solution.py:30
  77.8 14.2 %collective-permute-start.17 = (f16[256,1024]{1,0:T(8,128)(2,1)S(1)}, f16[256,1024]{1,0:T(8,128)(2,1)S(1)}, u32[]{:S(2)}, u32[]{:S(2)}) collective-permute-start(f16[256,1024]{1,0:T(8,128)(2,1)S(1)} %copy-done.5), channel_id=1, source_target_pairs={{0,1},{1,0},{2,3},{3,2},{4,5},{5,4},{6,7},{7,6},{8,9},{9,8},{10,11... | collective-permute-start | bytes 1572872 | tf_op jit(solution)/shard_map/ppermute | solution.py:21
  77.9 22.1 %collective-permute-start.18 = (f16[256,1024]{1,0:T(8,128)(2,1)S(1)}, f16[256,1024]{1,0:T(8,128)(2,1)S(1)}, u32[]{:S(2)}, u32[]{:S(2)}) collective-permute-start(f16[256,1024]{1,0:T(8,128)(2,1)S(1)} %multiply_convert_fusion.4), channel_id=1, source_target_pairs={{2,4},{4,2},{6,8},{8,6},{10,12},{12,10},{14,16},{16,14},{18,20},{2... | collective-permute-start | bytes 1572872 | tf_op jit(solution)/shard_map/ppermute | solution.py:30
  86.2 14.2 %collective-permute-start.19 = (f16[256,1024]{1,0:T(8,128)(2,1)S(1)}, f16[256,1024]{1,0:T(8,128)(2,1)S(1)}, u32[]{:S(2)}, u32[]{:S(2)}) collective-permute-start(f16[256,1024]{1,0:T(8,128)(2,1)S(1)} %multiply_convert_fusion.3), channel_id=1, source_target_pairs={{0,2},{2,0},{4,6},{6,4},{8,10},{10,8},{12,14},{14,12},{16,18},{18,... | collective-permute-start | bytes 1572872 | tf_op jit(solution)/shard_map/ppermute | solution.py:30
  86.2 16.9 %collective-permute-start.20 = (f16[256,1024]{1,0:T(8,128)(2,1)S(1)}, f16[256,1024]{1,0:T(8,128)(2,1)S(1)}, u32[]{:S(2)}, u32[]{:S(2)}) collective-permute-start(f16[256,1024]{1,0:T(8,128)(2,1)S(1)} %get-tuple-element.172), channel_id=1, source_target_pairs={{0,1},{1,0},{2,3},{3,2},{4,5},{5,4},{6,7},{7,6},{8,9},{9,8},{10,11... | collective-permute-start | bytes 1572872 | tf_op jit(solution)/shard_map/ppermute | solution.py:21
  88.2 17.2 %collective-permute-start.21 = (f16[256,1024]{1,0:T(8,128)(2,1)S(1)}, f16[256,1024]{1,0:T(8,128)(2,1)S(1)}, u32[]{:S(2)}, u32[]{:S(2)}) collective-permute-start(f16[256,1024]{1,0:T(8,128)(2,1)S(1)} %multiply_convert_fusion.3), channel_id=1, source_target_pairs={{2,4},{4,2},{6,8},{8,6},{10,12},{12,10},{14,16},{16,14},{18,20},{2... | collective-permute-start | bytes 1572872 | tf_op jit(solution)/shard_map/ppermute | solution.py:30
  100.6 5.3 %collective-permute-start.22 = (f16[256,1024]{1,0:T(8,128)(2,1)S(1)}, f16[256,1024]{1,0:T(8,128)(2,1)S(1)}, u32[]{:S(2)}, u32[]{:S(2)}) collective-permute-start(f16[256,1024]{1,0:T(8,128)(2,1)S(1)} %multiply_convert_fusion.2), channel_id=1, source_target_pairs={{0,2},{2,0},{4,6},{6,4},{8,10},{10,8},{12,14},{14,12},{16,18},{18,... | collective-permute-start | bytes 1572872 | tf_op jit(solution)/shard_map/ppermute | solution.py:30
  100.7 15.8 %collective-permute-start.23 = (f16[256,1024]{1,0:T(8,128)(2,1)S(1)}, f16[256,1024]{1,0:T(8,128)(2,1)S(1)}, u32[]{:S(2)}, u32[]{:S(2)}) collective-permute-start(f16[256,1024]{1,0:T(8,128)(2,1)S(1)} %multiply_convert_fusion.2), channel_id=1, source_target_pairs={{2,4},{4,2},{6,8},{8,6},{10,12},{12,10},{14,16},{16,14},{18,20},{2... | collective-permute-start | bytes 1572872 | tf_op jit(solution)/shard_map/ppermute | solution.py:30
  105.9 10.6 %copy-start.1 = (f32[1,2048,1024]{2,1,0:T(8,128)}, f32[1,2048,1024]{2,1,0:T(8,128)S(1)}, u32[]{:S(2)}) copy-start(f32[1,2048,1024]{2,1,0:T(8,128)S(1)} %bitcast_dynamic-update-slice_fusion.1) | copy-start | bytes 25165828
